TPU v7x, 32 devices: a whole 2x2x4 slice. The times are simulated.
32 devices in a mesh: island: 4 (over y, x), expert: 4 (over z), tensor: 2 (over core).
Axes of the slice: x: 2, y: 2, z: 4, core: 2. Of those that a mesh axis runs over, the one named last changes fastest.
Arguments:
- tokens: bfloat16 [4, 1024, 2048], P('island', 'expert', 'tensor'), may hold values from -6 to 6
- token_grads: bfloat16 [4, 1024, 2048], P('island', 'expert', 'tensor'), may hold values from -6 to 6
- slot_token: int32 [4, 4, 4, 96], P('island', 'expert'), may hold values from 0 to 255, as said below
- slot_count: int32 [4, 4, 4], P('island', 'expert'), may hold values from 24 to 96, as said below
- slot_prob: float32 [4, 4, 4, 96], P('island', 'expert'), may hold values from 0.1 to 1
- gate_weight: bfloat16 [4, 4, 2048, 1536], P('island', 'expert', None, 'tensor'), may hold values from -0.125 to 0.125
- down_weight: bfloat16 [4, 4, 1536, 2048], P('island', 'expert', 'tensor'), may hold values from -0.15625 to 0.15625
- drift: bfloat16 [4, 4, 2048, 1536], P('island', 'expert', None, 'tensor'), may hold values from -6 to 6
- momentum: float32 [4, 2048, 1536], P('expert', None, 'tensor'), may hold values from -1.5 to 1.5
Outputs:
- new_momentum: float32 [4, 2048, 1536], P('expert', None, 'tensor')
- outer_step: bfloat16 [4, 2048, 1536], P('expert', None, 'tensor')
Inputs may be any that keep to these rules, and one draw needn't show every extreme that they name: `slot_token`: for each island, source device and expert the 96 entries are distinct tokens of that source device. `slot_count`: in every island some expert is full from every source device.
All inputs are finite; a program needn't handle non-finite values.
Results may differ from a plain program's by a relative error of at most 0.0031.
The roundings to bfloat16 on the way count: a program that leaves them out, or rounds other values in their place, can miss the bound.
Values may be sent and summed in bfloat16 or wider, within the bound.
No kernel may reach another device: no remote copies, remote signals or barrier semaphores. Data moves between devices by JAX's collectives and lax.ppermute only.
A program may use at most 128 MiB of HBM per device.

v0:
```python
import math

import jax
import jax.numpy as jnp
from jax import lax
from jax.sharding import PartitionSpec as P


def outer_update(average, old_moment, square_sum, entries):
    clip_scale = jnp.minimum(1.0, 0.25 * math.sqrt(entries) / jnp.sqrt(square_sum + 1e-06))
    clipped = clip_scale * average
    new_moment = 0.9 * old_moment + clipped
    step_value = (0.7 * (clipped + 0.9 * new_moment)).astype(jnp.bfloat16)
    return (new_moment, step_value)


def body(
    tokens,
    token_grads,
    slot_token,
    slot_count,
    slot_prob,
    gate_weight,
    down_weight,
    drift,
    momentum,
):
    index_table = slot_token[0, 0]
    filled = slot_count[0, 0]
    live_slots = lax.broadcasted_iota(jnp.int32, index_table.shape, 1) < filled[:, None]
    slot_weights = jnp.where(live_slots, slot_prob[0, 0], jnp.float32(0.0))[..., None]
    input_slots = jnp.where(
        live_slots[..., None], tokens[0][index_table], jnp.zeros((), jnp.bfloat16)
    )
    grad_slots = (slot_weights * token_grads[0][index_table].astype(jnp.float32)).astype(
        jnp.bfloat16
    )
    input_slots, grad_slots = (input_slots, grad_slots)
    part_inputs, part_grads = (
        lax.all_to_all(input_slots, "expert", split_axis=0, concat_axis=1, tiled=True),
        lax.all_to_all(grad_slots, "expert", split_axis=0, concat_axis=1, tiled=True),
    )
    inputs, out_grads = (
        lax.all_gather(part_inputs, "tensor", axis=2, tiled=True),
        lax.all_gather(part_grads, "tensor", axis=2, tiled=True),
    )
    gate_value = jnp.einsum(
        "erd,edf->erf", inputs, gate_weight[0], preferred_element_type=jnp.float32
    )
    back_grad = jnp.einsum(
        "erd,efd->erf", out_grads, down_weight[0], preferred_element_type=jnp.float32
    )
    hidden_grad = (back_grad * jax.nn.silu(gate_value)).astype(jnp.bfloat16)
    gradient = jnp.einsum("erd,erf->edf", inputs, hidden_grad, preferred_element_type=jnp.float32)
    entries = gradient.size * lax.axis_size("expert") * lax.axis_size("tensor")
    inner_square = lax.psum(jnp.sum(gradient * gradient), ("expert", "tensor"))
    inner_scale = jnp.minimum(1.0, math.sqrt(entries) / jnp.sqrt(inner_square + 1e-06))
    pseudo = drift[0].astype(jnp.float32) + inner_scale * gradient
    islands = lax.axis_size("island")
    average = lax.psum(pseudo, "island") / islands
    outer_square = lax.psum(jnp.sum(average * average), ("expert", "tensor"))
    new_momentum, outer_step = outer_update(average, momentum, outer_square, entries)
    return (new_momentum, outer_step)


def solution(mesh):
    return jax.shard_map(
        body,
        mesh=mesh,
        in_specs=(
            P("island", "expert", "tensor"),
            P("island", "expert", "tensor"),
            P("island", "expert", None, None),
            P("island", "expert", None),
            P("island", "expert", None, None),
            P("island", "expert", None, "tensor"),
            P("island", "expert", "tensor", None),
            P("island", "expert", None, "tensor"),
            P("expert", None, "tensor"),
        ),
        out_specs=(P("expert", None, "tensor"), P("expert", None, "tensor")),
        check_vma=False,
    )
```

profile of v0, /device:TPU:0, one launch (start us, length us, event | category | flops | bytes accessed | tf_op | source)
XLA Modules:
  0.0 285.4 jit_solution(13504365626897590658)
XLA Ops:
  7.2 0.0 copy-start
  7.2 0.9 iota_compare_fusion
  8.1 0.8 compare_select_fusion
  8.8 0.1 reshape.126
  8.9 4.5 %gather_fusion = bf16[384,1024]{1,0:T(8,128)(2,1)} fusion(bf16[256,1024]{1,0:T(8,128)(2,1)} %bitcast.51, s32[1024]{0:T(1024)S(1)} %pad_clamp_fusion), kind=kCustom, calls=%fused_computation | custom fusion | bytes 1574400 | tf_op jit(solution)/shard_map/gather | solution.py:33
  13.4 2.1 broadcast_select_fusion
  15.5 6.3 %all-to-all-start = ((bf16[4,96,1024]{2,1,0:T(8,128)(2,1)}), bf16[4,96,1024]{2,1,0:T(8,128)(2,1)}, u32[]{:S(2)}, u32[]{:S(2)}) async-start(bf16[4,96,1024]{2,1,0:T(8,128)(2,1)} %broadcast_select_fusion), calls=%async_computation | async-start | bytes 1572864 | tf_op jit(solution)/shard_map/all_to_all | solution.py:40
  21.9 0.0 all-gather.3.cloned.1.call-start
  21.9 0.0 copy-start.1
  21.9 0.0 copy-start.2
  21.9 4.5 %gather_fusion.1 = bf16[384,1024]{1,0:T(8,128)(2,1)} fusion(bf16[256,1024]{1,0:T(8,128)(2,1)} %bitcast.52, s32[1024]{0:T(1024)S(1)} %pad_clamp_fusion), kind=kCustom, calls=%fused_computation.1 | custom fusion | bytes 1574400 | tf_op jit(solution)/shard_map/gather | solution.py:35
  26.4 15.7 %all-to-all-done = bf16[4,96,1024]{2,1,0:T(8,128)(2,1)} async-done(((bf16[4,96,1024]{2,1,0:T(8,128)(2,1)}), bf16[4,96,1024]{2,1,0:T(8,128)(2,1)}, u32[]{:S(2)}, u32[]{:S(2)}) %all-to-all-start) | async-done | bytes 786464 | tf_op jit(solution)/shard_map/all_to_all | solution.py:40
  42.1 0.0 all-gather.3.cloned.1.call-update
  42.1 0.0 all-gather.5.cloned.1.call-start
  42.1 0.0 copy-done.1
  42.2 0.0 copy-done.2
  42.2 0.1 bitcast_select_fusion
  42.2 1.3 fusion.5
  43.6 22.7 %all_to_all.24 = bf16[4,96,1024]{2,1,0:T(8,128)(2,1)} all-to-all(bf16[4,96,1024]{2,1,0:T(8,128)(2,1)S(1)} %fusion.5), channel_id=1, replica_groups=mesh['island'=4,'expert'=4,'tensor'=2] {'expert'}, dimensions={0} | all-to-all | bytes 1572864 | tf_op jit(solution)/shard_map/all_to_all | solution.py:41
  66.3 0.0 all-gather.5.cloned.1.call-update
  66.3 0.0 all-reduce.2.cloned.1.call-start
  66.4 0.0 all-gather.3.cloned.1.call-done
  66.4 4.8 %fusion.1 = f32[384,768]{1,0:T(8,128)} fusion(bf16[1,1,2048,768]{3,2,1,0:T(8,128)(2,1)} %param.14, bf16[1,384,2048]{2,1,0:T(8,128)(2,1)} %all-gather.3.cloned.1.call-done), kind=kOutput, calls=%fused_computation.8 | convolution fusion | flops 1207959552 | bytes 5898240 | tf_op jit(solution)/shard_map/erd,edf->erf/dot_general | solution.py:47
  71.2 4.2 %all-gather.5.cloned.1.call-done = bf16[1,384,2048]{2,1,0:T(8,128)(2,1)} async-done(((bf16[1,384,1024]{2,1,0:T(8,128)(2,1)}), bf16[1,384,2048]{2,1,0:T(8,128)(2,1)}) %all-gather.5.cloned.1.call-update) | async-done | bytes 1572880 | tf_op jit(solution)/shard_map/all_gather | solution.py:45
  75.4 0.0 copy-done
  75.4 8.8 %multiply_reduce_fusion.1 = (f32[]{:T(128)}, f32[2048,768]{1,0:T(8,128)}) fusion(bf16[1,1,768,2048]{3,2,1,0:T(8,128)(2,1)S(1)} %copy-done, bf16[1,384,2048]{2,1,0:T(8,128)(2,1)} %all-gather.5.cloned.1.call-done, f32[384,768]{1,0:T(8,128)} %fusion.1, bf16[1,384,2048]{2,1,0:T(8,128)(2,1)} %all-gather.3.cloned.1.call-done), kind=kOutput, calls=%fused_computation.6 | convolution fusion | flops 2420834304 | bytes 13762564 | tf_op jit(solution)/shard_map/erd,erf->edf/dot_general | solution.py:54
  84.2 17.7 %psum.21 = f32[]{:T(128)} all-reduce(f32[]{:T(128)} %get-tuple-element.4), channel_id=1, replica_groups=mesh['island'=4,'expert'=4,'tensor'=2] {'expert','tensor'}, use_global_device_ids=true, to_apply=%region_1.2 | all-reduce | flops 1 | bytes 8 | tf_op jit(solution)/shard_map/psum | solution.py:56
  102.6 7.0 %fusion = f32[1,2048,768]{2,1,0:T(8,128)} fusion(f32[2048,768]{1,0:T(8,128)} %get-tuple-element.5, bf16[1,1,2048,768]{3,2,1,0:T(8,128)(2,1)} %param.16, f32[]{:T(128)S(6)} %min.6), kind=kLoop, calls=%fused_computation.3 | loop fusion | flops 4718592 | bytes 15728644 | tf_op jit(solution)/shard_map/add | solution.py:58
  109.6 0.0 all-reduce.2.cloned.1.call-update
  109.6 136.8 %all-reduce.2.cloned.1.call-done = f32[1,2048,768]{2,1,0:T(8,128)} async-done(((f32[1,2048,768]{2,1,0:T(8,128)}), f32[1,2048,768]{2,1,0:T(8,128)}) %all-reduce.2.cloned.1.call-update) | async-done | bytes 6291472 | tf_op jit(solution)/shard_map/psum | solution.py:60
  246.4 5.0 %multiply_reduce_fusion = f32[]{:T(128)} fusion(f32[1,2048,768]{2,1,0:T(8,128)} %all-reduce.2.cloned.1.call-done), kind=kLoop, calls=%fused_computation.5 | loop fusion | flops 4718591 | bytes 6291460 | tf_op jit(solution)/shard_map/reduce_sum | solution.py:61
  251.4 17.0 %psum.23 = f32[]{:T(128)} all-reduce(f32[]{:T(128)} %multiply_reduce_fusion), channel_id=1, replica_groups=mesh['island'=4,'expert'=4,'tensor'=2] {'expert','tensor'}, use_global_device_ids=true, to_apply=%region_4.5 | all-reduce | flops 1 | bytes 8 | tf_op jit(solution)/shard_map/psum | solution.py:61
  269.1 9.8 %multiply_convert_fusion = (bf16[1,2048,768]{2,1,0:T(8,128)(2,1)}, f32[1,2048,768]{2,1,0:T(8,128)}) fusion(f32[1,2048,768]{2,1,0:T(8,128)} %all-reduce.2.cloned.1.call-done, f32[]{:T(128)S(6)} %mul.60, f32[1,2048,768]{2,1,0:T(8,128)} %param.17), kind=kLoop, calls=%fused_computation.4 | loop fusion | flops 11010048 | bytes 22020100 | tf_op jit(solution)/shard_map/convert_element_type | solution.py:13
  (1 shorter events, 0.0 us)
Async XLA Ops:
  7.2 68.2 %copy-start = (bf16[1,1,768,2048]{3,2,1,0:T(8,128)(2,1)S(1)}, bf16[1,1,768,2048]{3,2,1,0:T(8,128)(2,1)}, u32[]{:S(2)}) copy-start(bf16[1,1,768,2048]{3,2,1,0:T(8,128)(2,1)} %param.15) | copy-start | bytes 9437188
  15.5 26.5 %all-to-all-start = ((bf16[4,96,1024]{2,1,0:T(8,128)(2,1)}), bf16[4,96,1024]{2,1,0:T(8,128)(2,1)}, u32[]{:S(2)}, u32[]{:S(2)}) async-start(bf16[4,96,1024]{2,1,0:T(8,128)(2,1)} %broadcast_select_fusion), calls=%async_computation | async-start | bytes 1572864 | tf_op jit(solution)/shard_map/all_to_all | solution.py:40
  21.9 44.5 %all-gather.3.cloned.1.call-start = ((), (), s32[]{:S(2)}) async-start(), calls=%async_computation.2 | async-start | bytes 2359296 | tf_op jit(solution)/shard_map/all_gather | solution.py:44
  21.9 20.3 %copy-start.1 = (f32[1,1,4,96]{3,2,1,0:T(4,128)S(1)}, f32[1,1,4,96]{3,2,1,0:T(4,128)}, u32[]{:S(2)}) copy-start(f32[1,1,4,96]{3,2,1,0:T(4,128)} %param.13) | copy-start | bytes 4612
  21.9 20.3 %copy-start.2 = (s32[1,1,4]{2,1,0:T(1,128)S(1)}, s32[1,1,4]{2,1,0:T(1,128)}, u32[]{:S(2)}) copy-start(s32[1,1,4]{2,1,0:T(1,128)} %param.12) | copy-start | bytes 52
  42.1 33.3 %all-gather.5.cloned.1.call-start = ((), (), s32[]{:S(2)}) async-start(), calls=%async_computation.3 | async-start | bytes 2359296 | tf_op jit(solution)/shard_map/all_gather | solution.py:45
  66.3 180.1 %all-reduce.2.cloned.1.call-start = ((), (), s32[]{:S(2)}) async-start(), calls=%async_computation.4 | async-start | bytes 12582912 | tf_op jit(solution)/shard_map/psum | solution.py:60
Sparse Core Ops, SparseCore 0:
  42.2 8.9 all-gather.2
  66.5 8.9 all-gather.4
  109.8 136.5 all-reduce.1
where the time goes:
time: 286 us; the launch traced here: 285 us
  waiting for transfers between devices  157 us (55%)
  blocking collectives  57.4 us (20%)
  other arithmetic  27 us (9%)
  between operations  15.2 us (5%)
  matrix products  13.6 us (5%)
  local copies, waits for them, and re-layouts  9.1 us (3%)
  starting transfers between devices  6.4 us (2%)
    psum x1, waiting for transfers between devices, body(): average = lax.psum(pseudo, 'island') / islands  137 us
    all_to_all x1, blocking collectives, body(): lax.all_to_all(grad_slots, 'expert', split_axis=0, concat_axis=1, tiled=T...  22.7 us
    psum x1, blocking collectives, body(): inner_square = lax.psum(jnp.sum(gradient * gradient), ('expert', 'tensor'))  17.7 us
    psum x1, blocking collectives, body(): outer_square = lax.psum(jnp.sum(average * average), ('expert', 'tensor'))  17 us
    all_to_all x1, waiting for transfers between devices, body(): lax.all_to_all(input_slots, 'expert', split_axis=0, concat_axis=1, tiled=...  15.7 us
    convert_element_type x1, other arithmetic, outer_update(): step_value = (0.7 * (clipped + 0.9 * new_moment)).astype(jnp.bfloat16)  9.79 us
    dot_general x1, matrix products, body(): jnp.einsum('erd,erf->edf', inputs, hidden_grad, preferred_element_type=jn...  8.8 us
    add x1, other arithmetic, body(): pseudo = drift[0].astype(jnp.float32) + inner_scale * gradient  7.03 us
  transfers between devices with their start and end apart: 4, of which 3 were waited for; matrix products, arithmetic and copies ran while one was open for 4% of the time, Pallas kernels for 0%

commit v1 on v0

v1 whole, which is shorter than its diff:
```python
import functools
import math

import jax
import jax.numpy as jnp
from jax import lax
from jax.experimental import pallas as pl
from jax.experimental.pallas import tpu as pltpu
from jax.sharding import PartitionSpec as P

F32 = jnp.float32
BF16 = jnp.bfloat16
WIRE = jnp.float16


def partner(at, step, size):
    return at ^ step if size & (size - 1) == 0 else (at + step) % size


def origin(at, step, size):
    return at ^ step if size & (size - 1) == 0 else (at - step) % size


def swap(value, axis, step):
    size = lax.axis_size(axis)
    return lax.ppermute(value, axis, [(at, partner(at, step, size)) for at in range(size)])


def total(value, axes):
    for axis in axes:
        size = lax.axis_size(axis)
        if size & (size - 1):
            value = lax.psum(value, axis)
            continue
        step = 1
        while step < size:
            value = value + swap(value, axis, step)
            step *= 2
    return value


def update_kernel(place, factors, block, momentum, *rest):
    new_momentum, outer_step = rest[-2:]
    clipped = factors[0] * block[...]
    moved = 0.9 * momentum[0] + clipped
    new_momentum[0] = moved
    outer_step[0] = (0.7 * (clipped + 0.9 * moved)).astype(BF16)


def update_block(place, factor, block, momentum, outs):
    rows, columns = block.shape
    tile = rows // 4
    here = pl.BlockSpec((tile, columns), lambda r, place, factors: (r, 0))
    there = pl.BlockSpec(
        (1, tile, columns), lambda r, place, factors: (0, place[0] * 4 + r, place[1])
    )
    any_spec = pl.BlockSpec(memory_space=pl.ANY)
    return pl.pallas_call(
        update_kernel,
        grid_spec=pltpu.PrefetchScalarGridSpec(
            num_scalar_prefetch=2,
            grid=(4,),
            in_specs=[here, there] + [any_spec] * len(outs),
            out_specs=[there, there],
        ),
        out_shape=[
            jax.ShapeDtypeStruct(momentum.shape, F32),
            jax.ShapeDtypeStruct(momentum.shape, BF16),
        ],
        input_output_aliases={4 + n: n for n in range(len(outs))},
        compiler_params=pltpu.CompilerParams(vmem_limit_bytes=32 << 20),
        name="update_block",
    )(place, factor, block, momentum, *outs)


def body(
    tokens,
    token_grads,
    slot_token,
    slot_count,
    slot_prob,
    gate_weight,
    down_weight,
    drift,
    momentum,
):
    islands, experts, parts = (lax.axis_size(a) for a in ("island", "expert", "tensor"))
    island, expert, part = (lax.axis_index(a) for a in ("island", "expert", "tensor"))
    features, hidden = gate_weight.shape[2:]
    half = features // parts
    down, across = parts, islands // parts
    rows, columns = features // down, hidden // across
    entries = features * hidden * experts * parts

    def block_of(value, at):
        return lax.dynamic_slice(value, ((at // across) * rows, (at % across) * columns), (rows, columns))

    drift_block = block_of(drift[0, 0], island).astype(F32)
    drift_in = [
        swap(block_of(drift[0, 0], partner(island, d, islands)), "island", d)
        for d in range(1, islands)
    ]

    order = jnp.stack([partner(expert, d, experts) for d in range(experts)])
    table = slot_token[0, 0][order]
    filled = slot_count[0, 0][order]
    weights = slot_prob[0, 0][order]
    slots = table.shape[1]
    live = lax.broadcasted_iota(jnp.int32, table.shape, 1) < filled[:, None]
    picks = (
        (table[..., None] == lax.broadcasted_iota(jnp.int32, (1, 1, tokens.shape[1]), 2))
        & live[..., None]
    ).astype(BF16)
    input_slots = jnp.einsum("est,td->esd", picks, tokens[0], preferred_element_type=F32).astype(BF16)
    picked_grads = jnp.einsum("est,td->esd", picks, token_grads[0], preferred_element_type=F32)
    grad_slots = (weights[..., None] * picked_grads).astype(BF16)

    def routed(value):
        return [value[0]] + [swap(value[d], "expert", d) for d in range(1, experts)]

    inputs_in = routed(input_slots)
    grads_in = routed(grad_slots)
    inputs = jnp.concatenate(inputs_in)
    out_grads = jnp.concatenate(grads_in)

    inputs_all = [inputs] + [
        jnp.concatenate([swap(v, "tensor", t) for v in inputs_in]) for t in range(1, parts)
    ]
    grads_all = [out_grads] + [
        jnp.concatenate([swap(v, "tensor", t) for v in grads_in]) for t in range(1, parts)
    ]

    flat = [(i, t) for i in range(islands) for t in range(parts)]

    def send_features(d):
        pairs = []
        for at, t in flat:
            to = partner(at, d, islands)
            if t == to // across:
                pairs.append((at * parts + t, to * parts + t))
        return lax.ppermute(inputs, ("island", "tensor"), pairs)

    def spread(value):
        holder = island // across
        for t in range(1, parts):
            pairs = []
            for at in range(islands):
                keep = at // across
                pairs.append((at * parts + keep, at * parts + partner(keep, t, parts)))
            moved = lax.ppermute(value, ("island", "tensor"), pairs)
            value = jnp.where(part == partner(holder, t, parts), moved, value)
        return value

    def own_features():
        value = inputs
        holder = island // across
        for t in range(1, parts):
            value = jnp.where(part == partner(holder, t, parts), inputs_all[t], value)
        return value

    features_of = [own_features()] + [spread(send_features(d)) for d in range(1, islands)]

    def rows_of(weight, t, axis):
        return lax.dynamic_slice_in_dim(weight, origin(part, t, parts) * half, half, axis)

    gate_value = sum(
        jnp.einsum("rd,df->rf", v, rows_of(gate_weight[0, 0], t, 0), preferred_element_type=F32)
        for t, v in enumerate(inputs_all)
    )
    back_grad = sum(
        jnp.einsum("rd,fd->rf", v, rows_of(down_weight[0, 0], t, 1), preferred_element_type=F32)
        for t, v in enumerate(grads_all)
    )
    hidden_grad = (back_grad * jax.nn.silu(gate_value)).astype(BF16)

    def columns_of(value, at):
        return lax.dynamic_slice_in_dim(value, (at % across) * columns, columns, 1)

    hidden_of = [columns_of(hidden_grad, island)] + [
        swap(columns_of(hidden_grad, partner(island, d, islands)), "island", d)
        for d in range(1, islands)
    ]

    input_gram = sum(
        jnp.einsum("rd,sd->rs", v, v, preferred_element_type=F32) for v in inputs_all
    )
    hidden_gram = jnp.einsum("rf,sf->rs", hidden_grad, hidden_grad, preferred_element_type=F32)
    lanes = lax.broadcasted_iota(jnp.int32, (1, 128), 1)
    squares = jnp.where(lanes == island, jnp.sum(input_gram * hidden_gram), 0.0)
    squares = total(squares, ("tensor", "expert", "island"))
    scales = jnp.minimum(1.0, math.sqrt(entries) / jnp.sqrt(squares + 1e-06))

    average = drift_block
    for v in drift_in:
        average = average + v.astype(F32)
    for d in range(islands):
        gradient = jnp.einsum(
            "rd,rf->df", features_of[d], hidden_of[d], preferred_element_type=F32
        )
        average = average + scales[0, origin(island, d, islands)] * gradient
    average = average / islands

    peak = jnp.max(jnp.abs(average))
    peak = jnp.where(peak > 0, peak, 1.0)
    sent = (average / peak).astype(WIRE)
    blocks = [sent] + [swap(sent, "island", d) for d in range(1, islands)]

    notes = jnp.where(
        lanes == island, peak, jnp.where(lanes == islands, jnp.sum(average * average), 0.0)
    )
    notes = total(notes, ("island",))
    square = total(notes[:, islands : islands + 1], ("expert", "tensor"))
    clip = jnp.minimum(1.0, 0.25 * math.sqrt(entries) / jnp.sqrt(square[0, 0] + 1e-06))

    outs = []
    for d in range(islands):
        at = origin(island, d, islands)
        place = jnp.stack([at // across, at % across]).astype(jnp.int32)
        factor = (clip * notes[0, at])[None]
        outs = update_block(place, factor, blocks[d].astype(F32), momentum, outs)
    return tuple(outs)


def solution(mesh):
    return jax.shard_map(
        body,
        mesh=mesh,
        in_specs=(
            P("island", "expert", "tensor"),
            P("island", "expert", "tensor"),
            P("island", "expert", None, None),
            P("island", "expert", None),
            P("island", "expert", None, None),
            P("island", "expert", None, "tensor"),
            P("island", "expert", "tensor", None),
            P("island", "expert", None, "tensor"),
            P("expert", None, "tensor"),
        ),
        out_specs=(P("expert", None, "tensor"), P("expert", None, "tensor")),
        check_vma=False,
    )
```

time: 286 us -> 217 us (0.76)
  waiting for transfers between devices: 157 us -> 82.9 us
  starting transfers between devices: 6.4 us -> 64.4 us
  blocking collectives: 57.4 us -> 0 us
  other arithmetic: 27 us -> 8.07 us
  matrix products: 13.6 us -> 24.9 us
  Pallas kernels: 0 us -> 10.7 us
  local copies, waits for them, and re-layouts: 9.1 us -> 17.3 us
  between operations: 15.2 us -> 7.43 us
    psum x1 -> x0, waiting for transfers between devices: 137 us -> none  [body(): average = lax.psum(pseudo, 'island') / islands]
    ppermute x0 -> x39, waiting for transfers between devices: none -> 82.9 us  [the longest x33 82.9 us: swap(): lax.ppermute(value, axis, [(at, partner(at, step, size)) for at in range(...]
    ppermute x0 -> x39, starting transfers between devices: none -> 64.4 us  [the longest x33 49.7 us: swap(): lax.ppermute(value, axis, [(at, partner(at, step, size)) for at in range(...]
    psum x2 -> x0, blocking collectives: 34.7 us -> none  [the longest x1 17.7 us: body(): inner_square = lax.psum(jnp.sum(gradient * gradient), ('expert', 'tensor'))]
    all_to_all x1 -> x0, blocking collectives: 22.7 us -> none  [body(): lax.all_to_all(grad_slots, 'expert', split_axis=0, concat_axis=1, tiled=T...]
    all_to_all x1 -> x0, waiting for transfers between devices: 15.7 us -> none  [body(): lax.all_to_all(input_slots, 'expert', split_axis=0, concat_axis=1, tiled=...]
    dot_general x2 -> x13, matrix products: 13.6 us -> 24.9 us  [the longest x4 12.7 us: body(): jnp.einsum('rd,rf->df', features_of[d], hidden_of[d], preferred_element_t...]
    pallas_call x0 -> x4, Pallas kernels: none -> 10.7 us  [update_block(): pl.pallas_call(update_kernel, grid_spec=pltpu.PrefetchScalarGridSpec(num_...]
  transfers between devices with their start and end apart: 4 -> 39, of which waited for: 3 -> 13; matrix products, arithmetic and copies ran while one was open for 4% -> 14% of each run, Pallas kernels for 0% -> 4%
where the time goes in v1:
time: 217 us; the launch traced here: 216 us
  waiting for transfers between devices  82.9 us (38%)
  starting transfers between devices  64.4 us (30%)
  matrix products  24.9 us (11%)
  local copies, waits for them, and re-layouts  17.3 us (8%)
  Pallas kernels  10.7 us (5%)
  other arithmetic  8.07 us (4%)
  between operations  7.43 us (3%)
    ppermute x33, waiting for transfers between devices, swap(): lax.ppermute(value, axis, [(at, partner(at, step, size)) for at in range(...  82.9 us
    ppermute x33, starting transfers between devices, swap(): lax.ppermute(value, axis, [(at, partner(at, step, size)) for at in range(...  49.7 us
    dot_general x4, matrix products, body(): jnp.einsum('rd,rf->df', features_of[d], hidden_of[d], preferred_element_t...  12.7 us
    pallas_call x4, Pallas kernels, update_block(): pl.pallas_call(update_kernel, grid_spec=pltpu.PrefetchScalarGridSpec(num_...  10.7 us
    ppermute x3, starting transfers between devices, spread(): moved = lax.ppermute(value, ('island', 'tensor'), pairs)  8.77 us
    unnamed x33, local copies, waits for them, and re-layouts  6.59 us
    ppermute x3, starting transfers between devices, send_features(): return lax.ppermute(inputs, ('island', 'tensor'), pairs)  5.97 us
  transfers between devices with their start and end apart: 39, of which 13 were waited for; matrix products, arithmetic and copies ran while one was open for 14% of the time, Pallas kernels for 4%

profile of v1, /device:TPU:0, one launch (start us, length us, event | category | flops | bytes accessed | tf_op | source)
XLA Modules:
  0.0 215.7 jit_solution(11792876063247210381)
XLA Ops:
  0.7 1.4 gather_fusion
  2.1 1.3 gather_fusion.1
  3.5 1.5 convolution_convert_fusion
  5.0 0.8 slice_bitcast_fusion.7
  5.8 3.0 %collective-permute-start.3 = (bf16[96,1024]{1,0:T(8,128)(2,1)}, bf16[96,1024]{1,0:T(8,128)(2,1)}, u32[]{:S(2)}, u32[]{:S(2)}) collective-permute-start(bf16[96,1024]{1,0:T(8,128)(2,1)} %get-tuple-element.24), channel_id=1, source_target_pairs={{0,2},{2,0},{4,6},{6,4},{1,3},{3,1},{5,7},{7,5},{8,10},{10,8},{12,... | collective-permute-start | bytes 589832 | tf_op jit(solution)/shard_map/ppermute | solution.py:26
  8.9 2.6 %collective-permute-start.4 = (bf16[96,1024]{1,0:T(8,128)(2,1)}, bf16[96,1024]{1,0:T(8,128)(2,1)}, u32[]{:S(2)}, u32[]{:S(2)}) collective-permute-start(bf16[96,1024]{1,0:T(8,128)(2,1)} %get-tuple-element.23), channel_id=1, source_target_pairs={{0,4},{2,6},{4,0},{6,2},{1,5},{3,7},{5,1},{7,3},{8,12},{10,14},{12... | collective-permute-start | bytes 589832 | tf_op jit(solution)/shard_map/ppermute | solution.py:26
  12.0 1.5 multiply_convert_fusion
  13.5 0.9 slice_bitcast_fusion.3
  14.4 0.9 collective-permute-start.10
  15.3 3.1 %dynamic-slice_bitcast_fusion.2 = (bf16[1024,384]{1,0:T(8,128)(2,1)}, bf16[1024,384]{1,0:T(8,128)(2,1)}, bf16[1024,384]{1,0:T(8,128)(2,1)}) fusion(bf16[1,1,2048,768]{3,2,1,0:T(8,128)(2,1)} %param.16, s32[]{:T(128)S(6)} %select_n.186, s32[]{:T(128)S(6)} %select_n.188, s32[]{:T(128)S(6)} %select_n.193, s32[]{:T(128)S(6)} %select_n.194, s32[]{:T(128)S(6)} %select_n.190, ...), kind=kLoop, calls=%fused_computation.58 | loop fusion | bytes 4718616 | tf_op jit(solution)/shard_map/dynamic_slice | solution.py:96
  18.4 3.5 %collective-permute-start.11 = (bf16[96,1024]{1,0:T(8,128)(2,1)S(1)}, bf16[96,1024]{1,0:T(8,128)(2,1)S(1)}, u32[]{:S(2)}, u32[]{:S(2)}) collective-permute-start(bf16[96,1024]{1,0:T(8,128)(2,1)S(1)} %copy-done.11), channel_id=1, source_target_pairs={{0,4},{2,6},{4,0},{6,2},{1,5},{3,7},{5,1},{7,3},{8,12},{10,14},{12... | collective-permute-start | bytes 589832 | tf_op jit(solution)/shard_map/ppermute | solution.py:26
  21.9 4.4 %collective-permute-done.4 = bf16[96,1024]{1,0:T(8,128)(2,1)} collective-permute-done((bf16[96,1024]{1,0:T(8,128)(2,1)}, bf16[96,1024]{1,0:T(8,128)(2,1)}, u32[]{:S(2)}, u32[]{:S(2)}) %collective-permute-start.4) | collective-permute-done | bytes 196640 | tf_op jit(solution)/shard_map/ppermute | solution.py:26
  26.4 2.5 %collective-permute-start.12 = (bf16[96,1024]{1,0:T(8,128)(2,1)S(1)}, bf16[96,1024]{1,0:T(8,128)(2,1)S(1)}, u32[]{:S(2)}, u32[]{:S(2)}) collective-permute-start(bf16[96,1024]{1,0:T(8,128)(2,1)S(1)} %copy-done.10), channel_id=1, source_target_pairs={{0,6},{2,4},{4,2},{6,0},{1,7},{3,5},{5,3},{7,1},{8,14},{10,12},{12... | collective-permute-start | bytes 589832 | tf_op jit(solution)/shard_map/ppermute | solution.py:26
  28.9 2.0 pad_maximum_fusion
  30.8 2.0 fusion.77
  32.8 2.1 fusion.9
  34.9 3.4 %collective-permute-start.22 = (bf16[384,1024]{1,0:T(8,128)(2,1)}, bf16[384,1024]{1,0:T(8,128)(2,1)}, u32[]{:S(2)}, u32[]{:S(2)}) collective-permute-start(bf16[384,1024]{1,0:T(8,128)(2,1)} %pad_maximum_fusion), channel_id=1, source_target_pairs={{0,8},{8,0},{17,25},{25,17},{2,10},{10,2},{19,27},{27,19},{4,12},{... | collective-permute-start | bytes 2359304 | tf_op jit(solution)/shard_map/ppermute | solution.py:141
  38.3 4.8 %collective-permute-done.11 = bf16[96,1024]{1,0:T(8,128)(2,1)S(1)} collective-permute-done((bf16[96,1024]{1,0:T(8,128)(2,1)S(1)}, bf16[96,1024]{1,0:T(8,128)(2,1)S(1)}, u32[]{:S(2)}, u32[]{:S(2)}) %collective-permute-start.11) | collective-permute-done | bytes 196640 | tf_op jit(solution)/shard_map/ppermute | solution.py:26
  43.6 1.7 fusion.13
  45.5 0.9 constant_dynamic-update-slice_fusion.3
  47.7 0.8 fusion.25
  48.5 1.3 collective-permute-start.25
  49.9 0.9 fusion.28
  51.3 1.3 fusion.57
  53.1 2.8 %collective-permute-start.17 = (f32[1,128]{1,0:T(1,128)S(1)}, f32[1,128]{1,0:T(1,128)S(1)}, u32[]{:S(2)}, u32[]{:S(2)}) collective-permute-start(f32[1,128]{1,0:T(1,128)S(1)} %compare_select_fusion.3), channel_id=1, source_target_pairs={{0,1},{1,0},{2,3},{3,2},{4,5},{5,4},{6,7},{7,6},{8,9},{9,8},{10,11... | collective-permute-start | bytes 1544 | tf_op jit(solution)/shard_map/ppermute | solution.py:26
  56.0 1.3 collective-permute-start.28
  57.8 6.2 %collective-permute-start.18 = (f32[1,128]{1,0:T(1,128)S(1)}, f32[1,128]{1,0:T(1,128)S(1)}, u32[]{:S(2)}, u32[]{:S(2)}) collective-permute-start(f32[1,128]{1,0:T(1,128)S(1)} %fusion.91), channel_id=1, source_target_pairs={{0,2},{2,0},{4,6},{6,4},{1,3},{3,1},{5,7},{7,5},{8,10},{10,8},{12,... | collective-permute-start | bytes 1544 | tf_op jit(solution)/shard_map/ppermute | solution.py:26
  64.0 4.8 %collective-permute-start.23 = (bf16[384,1024]{1,0:T(8,128)(2,1)}, bf16[384,1024]{1,0:T(8,128)(2,1)}, u32[]{:S(2)}, u32[]{:S(2)}) collective-permute-start(bf16[384,1024]{1,0:T(8,128)(2,1)} %collective-permute-done.22), channel_id=1, source_target_pairs={{0,1},{8,9},{17,16},{25,24},{2,3},{10,11},{19,18},{27,26},{4,5},{1... | collective-permute-start | bytes 2359304 | tf_op jit(solution)/shard_map/ppermute | solution.py:150
  69.4 1.4 collective-permute-start.19
  70.8 2.4 %collective-permute-start.26 = (bf16[384,1024]{1,0:T(8,128)(2,1)}, bf16[384,1024]{1,0:T(8,128)(2,1)}, u32[]{:S(2)}, u32[]{:S(2)}) collective-permute-start(bf16[384,1024]{1,0:T(8,128)(2,1)} %collective-permute-done.25), channel_id=1, source_target_pairs={{0,1},{8,9},{17,16},{25,24},{2,3},{10,11},{19,18},{27,26},{4,5},{1... | collective-permute-start | bytes 2359304 | tf_op jit(solution)/shard_map/ppermute | solution.py:150
  73.9 1.5 collective-permute-start.20
  75.4 2.0 collective-permute-done.20
  77.8 1.2 constant_dynamic-slice_fusion.8
  79.0 1.6 collective-permute-start.24
  81.0 1.3 collective-permute-start.27
  82.4 1.5 collective-permute-start.29
  83.9 0.7 constant_dynamic-slice_fusion.10
  84.6 3.9 %collective-permute-done.24 = bf16[384,384]{1,0:T(8,128)(2,1)S(1)} collective-permute-done((bf16[384,384]{1,0:T(8,128)(2,1)S(1)}, bf16[384,384]{1,0:T(8,128)(2,1)S(1)}, u32[]{:S(2)}, u32[]{:S(2)}) %collective-permute-start.24) | collective-permute-done | bytes 294944 | tf_op jit(solution)/shard_map/ppermute | solution.py:26
  88.5 1.5 collective-permute-start
  90.3 1.7 collective-permute-start.2
  92.0 1.8 fusion.50
  93.8 1.3 collective-permute-start.30
  95.1 1.8 fusion.48
  97.0 33.0 %collective-permute-done.30 = bf16[384,384]{1,0:T(8,128)(2,1)S(1)} collective-permute-done((bf16[384,384]{1,0:T(8,128)(2,1)S(1)}, bf16[384,384]{1,0:T(8,128)(2,1)S(1)}, u32[]{:S(2)}, u32[]{:S(2)}) %collective-permute-start.30) | collective-permute-done | bytes 294944 | tf_op jit(solution)/shard_map/ppermute | solution.py:26
  130.0 1.8 fusion.46
  132.0 7.2 %abs_reduce_fusion = (f32[]{:T(128)}, f32[]{:T(128)}, f32[1024,384]{1,0:T(8,128)}) fusion(f32[1024,384]{1,0:T(8,128)S(1)} %fusion.46, f32[]{:T(128)} %bitcast.33, f32[1024,384]{1,0:T(8,128)S(1)} %fusion.48, f32[]{:T(128)} %bitcast.32, f32[1024,384]{1,0:T(8,128)S(1)} %fusion.50, f32[]{:T(128)} %bitcast.31, bf16[384,768]{1,0:T(8,128)(2,1)S(1)} %copy-done.4, ...), kind=kOutput, calls=%fused_computation.21 | convolution fusion | flops 310247424 | bytes 11307032 | tf_op jit(solution)/shard_map/rd,rf->df/dot_general | solution.py:197
  140.5 1.6 fusion.76
  142.1 0.7 collective-permute-start.38
  142.8 1.8 collective-permute-start.37
  144.6 1.0 collective-permute-start.36
  146.3 0.7 collective-permute-start.31
  147.1 29.6 %collective-permute-done.31 = f32[1,128]{1,0:T(1,128)S(1)} collective-permute-done((f32[1,128]{1,0:T(1,128)S(1)}, f32[1,128]{1,0:T(1,128)S(1)}, u32[]{:S(2)}, u32[]{:S(2)}) %collective-permute-start.31) | collective-permute-done | bytes 544 | tf_op jit(solution)/shard_map/ppermute | solution.py:26
  177.4 2.9 %collective-permute-start.32 = (f32[1,128]{1,0:T(1,128)S(1)}, f32[1,128]{1,0:T(1,128)S(1)}, u32[]{:S(2)}, u32[]{:S(2)}) collective-permute-start(f32[1,128]{1,0:T(1,128)S(1)} %fusion.90), channel_id=1, source_target_pairs={{0,16},{8,24},{16,0},{24,8},{1,17},{9,25},{17,1},{25,9},{2,18},{10... | collective-permute-start | bytes 1544 | tf_op jit(solution)/shard_map/ppermute | solution.py:26
  180.4 1.4 collective-permute-done.32
  183.2 3.0 %collective-permute-start.33 = (f32[1,1]{1,0:T(1,128)}, f32[1,1]{1,0:T(1,128)}, u32[]{:S(2)}, u32[]{:S(2)}) collective-permute-start(f32[1,1]{1,0:T(1,128)} %get-tuple-element.36), channel_id=1, source_target_pairs={{0,2},{2,0},{4,6},{6,4},{1,3},{3,1},{5,7},{7,5},{8,10},{10,8},{12,... | collective-permute-start | bytes 20 | tf_op jit(solution)/shard_map/ppermute | solution.py:26
  186.1 1.8 collective-permute-done.33
  189.1 4.4 %collective-permute-start.34 = (f32[1,1]{1,0:T(1,128)}, f32[1,1]{1,0:T(1,128)}, u32[]{:S(2)}, u32[]{:S(2)}) collective-permute-start(f32[1,1]{1,0:T(1,128)} %add.202), channel_id=1, source_target_pairs={{0,4},{2,6},{4,0},{6,2},{1,5},{3,7},{5,1},{7,3},{8,12},{10,14},{12... | collective-permute-start | bytes 20 | tf_op jit(solution)/shard_map/ppermute | solution.py:26
  194.5 1.0 collective-permute-start.35
  199.1 2.8 %copy-done.1 = f32[1,2048,768]{2,1,0:T(8,128)S(1)} copy-done((f32[1,2048,768]{2,1,0:T(8,128)S(1)}, f32[1,2048,768]{2,1,0:T(8,128)}, u32[]{:S(2)}) %copy-start.1) | copy-done | bytes 6291480
  201.9 2.7 %update_block.4 = (f32[1,2048,768]{2,1,0:T(8,128)}, bf16[1,2048,768]{2,1,0:T(8,128)(2,1)}) custom-call(s32[2]{0:T(128)S(1)} %pad_add_fusion.3.place, f32[1]{0:T(128)} %bitcast.43.factors, f32[1024,384]{1,0:T(8,128)S(1)} %get-tuple-element.16.block, f32[1,2048,768]{2,1,0:T(8,128)S(1)} %copy-done.1), custom_call_target="tpu_custom_call" | custom-call | tf_op jit(solution)/shard_map/update_block/pallas_call | solution.py:58
  204.7 2.8 %copy-done.2 = f32[1,2048,768]{2,1,0:T(8,128)S(1)} copy-done((f32[1,2048,768]{2,1,0:T(8,128)S(1)}, f32[1,2048,768]{2,1,0:T(8,128)}, u32[]{:S(2)}) %copy-start.2) | copy-done | bytes 6291480
  207.5 2.7 %update_block.5 = (f32[1,2048,768]{2,1,0:T(8,128)}, bf16[1,2048,768]{2,1,0:T(8,128)(2,1)}) custom-call(s32[2]{0:T(128)S(1)} %pad_add_fusion.2.place, f32[1]{0:T(128)} %bitcast.40.factors, f32[1024,384]{1,0:T(8,128)S(1)} %convert_element_type.51.block, f32[1,2048,768]{2,1,0:T(8,128)S(1)} %copy-done.2, ...), custom_call_target="tpu_custom_call", output_to_operand_aliasing={{0}: (4, {}), {1}: (5, {})} | custom-call | tf_op jit(solution)/shard_map/update_block/pallas_call | solution.py:58
  210.2 2.7 %update_block.6 = (f32[1,2048,768]{2,1,0:T(8,128)}, bf16[1,2048,768]{2,1,0:T(8,128)(2,1)}) custom-call(s32[2]{0:T(128)S(1)} %pad_add_fusion.1.place, f32[1]{0:T(128)} %bitcast.37.factors, f32[1024,384]{1,0:T(8,128)S(1)} %convert_element_type.50.block, f32[1,2048,768]{2,1,0:T(8,128)S(1)} %copy-done.2, ...), custom_call_target="tpu_custom_call", output_to_operand_aliasing={{0}: (4, {}), {1}: (5, {})} | custom-call | tf_op jit(solution)/shard_map/update_block/pallas_call | solution.py:58
  213.0 2.7 %update_block.7 = (f32[1,2048,768]{2,1,0:T(8,128)}, bf16[1,2048,768]{2,1,0:T(8,128)(2,1)}) custom-call(s32[2]{0:T(128)S(1)} %pad_add_fusion.place, f32[1]{0:T(128)} %bitcast.34.factors, f32[1024,384]{1,0:T(8,128)S(1)} %convert_element_type.49.block, f32[1,2048,768]{2,1,0:T(8,128)S(1)} %copy-done.2, ...), custom_call_target="tpu_custom_call", output_to_operand_aliasing={{0}: (4, {}), {1}: (5, {})} | custom-call | tf_op jit(solution)/shard_map/update_block/pallas_call | solution.py:58
  (95 shorter events, 10.6 us)
Async XLA Ops:
  0.6 32.2 %copy-start = (bf16[1,1,2048,768]{3,2,1,0:T(8,128)(2,1)S(1)}, bf16[1,1,2048,768]{3,2,1,0:T(8,128)(2,1)}, u32[]{:S(2)}) copy-start(bf16[1,1,2048,768]{3,2,1,0:T(8,128)(2,1)} %param.14) | copy-start | bytes 9437188
  3.4 8.0 %copy-start.12 = (f32[1,1,4,96]{3,2,1,0:T(4,128)S(1)}, f32[1,1,4,96]{3,2,1,0:T(4,128)}, u32[]{:S(2)}) copy-start(f32[1,1,4,96]{3,2,1,0:T(4,128)} %param.13) | copy-start | bytes 4612
  3.5 7.9 %copy-start.13 = (pred[4,96]{1,0:T(4,128)(4,1)}, pred[4,96]{1,0:T(4,128)(4,1)S(1)}, u32[]{:S(2)}) copy-start(pred[4,96]{1,0:T(4,128)(4,1)S(1)} %iota_compare_fusion.1) | copy-start | bytes 1156
  5.8 12.6 %collective-permute-start.3 = (bf16[96,1024]{1,0:T(8,128)(2,1)}, bf16[96,1024]{1,0:T(8,128)(2,1)}, u32[]{:S(2)}, u32[]{:S(2)}) collective-permute-start(bf16[96,1024]{1,0:T(8,128)(2,1)} %get-tuple-element.24), channel_id=1, source_target_pairs={{0,2},{2,0},{4,6},{6,4},{1,3},{3,1},{5,7},{7,5},{8,10},{10,8},{12,... | collective-permute-start | bytes 589832 | tf_op jit(solution)/shard_map/ppermute | solution.py:26
  8.9 17.5 %collective-permute-start.4 = (bf16[96,1024]{1,0:T(8,128)(2,1)}, bf16[96,1024]{1,0:T(8,128)(2,1)}, u32[]{:S(2)}, u32[]{:S(2)}) collective-permute-start(bf16[96,1024]{1,0:T(8,128)(2,1)} %get-tuple-element.23), channel_id=1, source_target_pairs={{0,4},{2,6},{4,0},{6,2},{1,5},{3,7},{5,1},{7,3},{8,12},{10,14},{12... | collective-permute-start | bytes 589832 | tf_op jit(solution)/shard_map/ppermute | solution.py:26
  11.4 17.4 %collective-permute-start.5 = (bf16[96,1024]{1,0:T(8,128)(2,1)}, bf16[96,1024]{1,0:T(8,128)(2,1)S(1)}, u32[]{:S(2)}, u32[]{:S(2)}) collective-permute-start(bf16[96,1024]{1,0:T(8,128)(2,1)} %get-tuple-element.22), channel_id=1, source_target_pairs={{0,6},{2,4},{4,2},{6,0},{1,7},{3,5},{5,3},{7,1},{8,14},{10,12},{12... | collective-permute-start | bytes 589832 | tf_op jit(solution)/shard_map/ppermute | solution.py:26
  11.4 33.9 %collective-permute-start.6 = (bf16[96,1024]{1,0:T(8,128)(2,1)S(1)}, bf16[96,1024]{1,0:T(8,128)(2,1)}, u32[]{:S(2)}, u32[]{:S(2)}) collective-permute-start(bf16[96,1024]{1,0:T(8,128)(2,1)S(1)} %get-tuple-element.21), channel_id=1, source_target_pairs={{0,1},{1,0},{2,3},{3,2},{4,5},{5,4},{6,7},{7,6},{8,9},{9,8},{10,11... | collective-permute-start | bytes 589832 | tf_op jit(solution)/shard_map/ppermute | solution.py:26
  14.4 20.5 %collective-permute-start.10 = (bf16[96,1024]{1,0:T(8,128)(2,1)}, bf16[96,1024]{1,0:T(8,128)(2,1)}, u32[]{:S(2)}, u32[]{:S(2)}) collective-permute-start(bf16[96,1024]{1,0:T(8,128)(2,1)} %get-tuple-element.28), channel_id=1, source_target_pairs={{0,2},{2,0},{4,6},{6,4},{1,3},{3,1},{5,7},{7,5},{8,10},{10,8},{12,... | collective-permute-start | bytes 589832 | tf_op jit(solution)/shard_map/ppermute | solution.py:26
  15.3 3.1 %copy-start.11 = (bf16[96,1024]{1,0:T(8,128)(2,1)S(1)}, bf16[96,1024]{1,0:T(8,128)(2,1)}, u32[]{:S(2)}) copy-start(bf16[96,1024]{1,0:T(8,128)(2,1)} %get-tuple-element.27) | copy-start | bytes 589828
  15.3 11.1 %copy-start.10 = (bf16[96,1024]{1,0:T(8,128)(2,1)S(1)}, bf16[96,1024]{1,0:T(8,128)(2,1)}, u32[]{:S(2)}) copy-start(bf16[96,1024]{1,0:T(8,128)(2,1)} %get-tuple-element.26) | copy-start | bytes 589828
  15.3 13.6 %copy-start.9 = (bf16[96,1024]{1,0:T(8,128)(2,1)S(1)}, bf16[96,1024]{1,0:T(8,128)(2,1)}, u32[]{:S(2)}) copy-start(bf16[96,1024]{1,0:T(8,128)(2,1)} %get-tuple-element.25) | copy-start | bytes 589828
  18.4 24.7 %collective-permute-start.11 = (bf16[96,1024]{1,0:T(8,128)(2,1)S(1)}, bf16[96,1024]{1,0:T(8,128)(2,1)S(1)}, u32[]{:S(2)}, u32[]{:S(2)}) collective-permute-start(bf16[96,1024]{1,0:T(8,128)(2,1)S(1)} %copy-done.11), channel_id=1, source_target_pairs={{0,4},{2,6},{4,0},{6,2},{1,5},{3,7},{5,1},{7,3},{8,12},{10,14},{12... | collective-permute-start | bytes 589832 | tf_op jit(solution)/shard_map/ppermute | solution.py:26
  26.4 16.8 %collective-permute-start.12 = (bf16[96,1024]{1,0:T(8,128)(2,1)S(1)}, bf16[96,1024]{1,0:T(8,128)(2,1)S(1)}, u32[]{:S(2)}, u32[]{:S(2)}) collective-permute-start(bf16[96,1024]{1,0:T(8,128)(2,1)S(1)} %copy-done.10), channel_id=1, source_target_pairs={{0,6},{2,4},{4,2},{6,0},{1,7},{3,5},{5,3},{7,1},{8,14},{10,12},{12... | collective-permute-start | bytes 589832 | tf_op jit(solution)/shard_map/ppermute | solution.py:26
  28.9 19.7 %collective-permute-start.13 = (bf16[96,1024]{1,0:T(8,128)(2,1)S(1)}, bf16[96,1024]{1,0:T(8,128)(2,1)S(1)}, u32[]{:S(2)}, u32[]{:S(2)}) collective-permute-start(bf16[96,1024]{1,0:T(8,128)(2,1)S(1)} %copy-done.9), channel_id=1, source_target_pairs={{0,1},{1,0},{2,3},{3,2},{4,5},{5,4},{6,7},{7,6},{8,9},{9,8},{10,11... | collective-permute-start | bytes 589832 | tf_op jit(solution)/shard_map/ppermute | solution.py:26
  32.8 10.8 %copy-start.14 = (bf16[1,1,768,2048]{3,2,1,0:T(8,128)(2,1)S(1)}, bf16[1,1,768,2048]{3,2,1,0:T(8,128)(2,1)}, u32[]{:S(2)}) copy-start(bf16[1,1,768,2048]{3,2,1,0:T(8,128)(2,1)} %param.15) | copy-start | bytes 9437188
  34.9 29.1 %collective-permute-start.22 = (bf16[384,1024]{1,0:T(8,128)(2,1)}, bf16[384,1024]{1,0:T(8,128)(2,1)}, u32[]{:S(2)}, u32[]{:S(2)}) collective-permute-start(bf16[384,1024]{1,0:T(8,128)(2,1)} %pad_maximum_fusion), channel_id=1, source_target_pairs={{0,8},{8,0},{17,25},{25,17},{2,10},{10,2},{19,27},{27,19},{4,12},{... | collective-permute-start | bytes 2359304 | tf_op jit(solution)/shard_map/ppermute | solution.py:141
  43.1 3.3 %collective-permute-start.7 = (bf16[96,1024]{1,0:T(8,128)(2,1)}, bf16[96,1024]{1,0:T(8,128)(2,1)S(1)}, u32[]{:S(2)}, u32[]{:S(2)}) collective-permute-start(bf16[96,1024]{1,0:T(8,128)(2,1)} %collective-permute-done.3), channel_id=1, source_target_pairs={{0,1},{1,0},{2,3},{3,2},{4,5},{5,4},{6,7},{7,6},{8,9},{9,8},{10,11... | collective-permute-start | bytes 589832 | tf_op jit(solution)/shard_map/ppermute | solution.py:26
  43.1 3.9 %collective-permute-start.8 = (bf16[96,1024]{1,0:T(8,128)(2,1)}, bf16[96,1024]{1,0:T(8,128)(2,1)S(1)}, u32[]{:S(2)}, u32[]{:S(2)}) collective-permute-start(bf16[96,1024]{1,0:T(8,128)(2,1)} %collective-permute-done.4), channel_id=1, source_target_pairs={{0,1},{1,0},{2,3},{3,2},{4,5},{5,4},{6,7},{7,6},{8,9},{9,8},{10,11... | collective-permute-start | bytes 589832 | tf_op jit(solution)/shard_map/ppermute | solution.py:26
  45.4 1.7 collective-permute-start.9
  46.4 3.4 %collective-permute-start.14 = (bf16[96,1024]{1,0:T(8,128)(2,1)}, bf16[96,1024]{1,0:T(8,128)(2,1)S(1)}, u32[]{:S(2)}, u32[]{:S(2)}) collective-permute-start(bf16[96,1024]{1,0:T(8,128)(2,1)} %collective-permute-done.10), channel_id=1, source_target_pairs={{0,1},{1,0},{2,3},{3,2},{4,5},{5,4},{6,7},{7,6},{8,9},{9,8},{10,11... | collective-permute-start | bytes 589832 | tf_op jit(solution)/shard_map/ppermute | solution.py:26
  47.0 2.8 %collective-permute-start.15 = (bf16[96,1024]{1,0:T(8,128)(2,1)S(1)}, bf16[96,1024]{1,0:T(8,128)(2,1)S(1)}, u32[]{:S(2)}, u32[]{:S(2)}) collective-permute-start(bf16[96,1024]{1,0:T(8,128)(2,1)S(1)} %collective-permute-done.11), channel_id=1, source_target_pairs={{0,1},{1,0},{2,3},{3,2},{4,5},{5,4},{6,7},{7,6},{8,9},{9,8},{10,11... | collective-permute-start | bytes 589832 | tf_op jit(solution)/shard_map/ppermute | solution.py:26
  47.1 2.7 %collective-permute-start.16 = (bf16[96,1024]{1,0:T(8,128)(2,1)S(1)}, bf16[96,1024]{1,0:T(8,128)(2,1)S(1)}, u32[]{:S(2)}, u32[]{:S(2)}) collective-permute-start(bf16[96,1024]{1,0:T(8,128)(2,1)S(1)} %collective-permute-done.12), channel_id=1, source_target_pairs={{0,1},{1,0},{2,3},{3,2},{4,5},{5,4},{6,7},{7,6},{8,9},{9,8},{10,11... | collective-permute-start | bytes 589832 | tf_op jit(solution)/shard_map/ppermute | solution.py:26
  47.7 3.6 %copy-start.5 = (bf16[384,1024]{1,0:T(8,128)(2,1)}, bf16[384,1024]{1,0:T(8,128)(2,1)S(1)}, u32[]{:S(2)}) copy-start(bf16[384,1024]{1,0:T(8,128)(2,1)S(1)} %constant_dynamic-update-slice_fusion) | copy-start | bytes 2359300
  48.5 22.3 %collective-permute-start.25 = (bf16[384,1024]{1,0:T(8,128)(2,1)}, bf16[384,1024]{1,0:T(8,128)(2,1)}, u32[]{:S(2)}, u32[]{:S(2)}) collective-permute-start(bf16[384,1024]{1,0:T(8,128)(2,1)} %pad_maximum_fusion), channel_id=1, source_target_pairs={{1,17},{9,25},{16,0},{24,8},{3,19},{11,27},{18,2},{26,10},{5,21},{... | collective-permute-start | bytes 2359304 | tf_op jit(solution)/shard_map/ppermute | solution.py:141
  50.8 1.8 copy-start.3
  53.1 4.1 %collective-permute-start.17 = (f32[1,128]{1,0:T(1,128)S(1)}, f32[1,128]{1,0:T(1,128)S(1)}, u32[]{:S(2)}, u32[]{:S(2)}) collective-permute-start(f32[1,128]{1,0:T(1,128)S(1)} %compare_select_fusion.3), channel_id=1, source_target_pairs={{0,1},{1,0},{2,3},{3,2},{4,5},{5,4},{6,7},{7,6},{8,9},{9,8},{10,11... | collective-permute-start | bytes 1544 | tf_op jit(solution)/shard_map/ppermute | solution.py:26
  56.0 26.4 %collective-permute-start.28 = (bf16[384,1024]{1,0:T(8,128)(2,1)}, bf16[384,1024]{1,0:T(8,128)(2,1)}, u32[]{:S(2)}, u32[]{:S(2)}) collective-permute-start(bf16[384,1024]{1,0:T(8,128)(2,1)} %pad_maximum_fusion), channel_id=1, source_target_pairs={{1,25},{9,17},{16,8},{24,0},{3,27},{11,19},{18,10},{26,2},{5,29},{... | collective-permute-start | bytes 2359304 | tf_op jit(solution)/shard_map/ppermute | solution.py:141
  57.8 11.0 %collective-permute-start.18 = (f32[1,128]{1,0:T(1,128)S(1)}, f32[1,128]{1,0:T(1,128)S(1)}, u32[]{:S(2)}, u32[]{:S(2)}) collective-permute-start(f32[1,128]{1,0:T(1,128)S(1)} %fusion.91), channel_id=1, source_target_pairs={{0,2},{2,0},{4,6},{6,4},{1,3},{3,1},{5,7},{7,5},{8,10},{10,8},{12,... | collective-permute-start | bytes 1544 | tf_op jit(solution)/shard_map/ppermute | solution.py:26
  64.0 26.2 %collective-permute-start.23 = (bf16[384,1024]{1,0:T(8,128)(2,1)}, bf16[384,1024]{1,0:T(8,128)(2,1)}, u32[]{:S(2)}, u32[]{:S(2)}) collective-permute-start(bf16[384,1024]{1,0:T(8,128)(2,1)} %collective-permute-done.22), channel_id=1, source_target_pairs={{0,1},{8,9},{17,16},{25,24},{2,3},{10,11},{19,18},{27,26},{4,5},{1... | collective-permute-start | bytes 2359304 | tf_op jit(solution)/shard_map/ppermute | solution.py:150
  69.4 4.5 %collective-permute-start.19 = (f32[1,128]{1,0:T(1,128)S(1)}, f32[1,128]{1,0:T(1,128)S(1)}, u32[]{:S(2)}, u32[]{:S(2)}) collective-permute-start(f32[1,128]{1,0:T(1,128)S(1)} %fusion.93), channel_id=1, source_target_pairs={{0,4},{2,6},{4,0},{6,2},{1,5},{3,7},{5,1},{7,3},{8,12},{10,14},{12... | collective-permute-start | bytes 1544 | tf_op jit(solution)/shard_map/ppermute | solution.py:26
  70.8 23.0 %collective-permute-start.26 = (bf16[384,1024]{1,0:T(8,128)(2,1)}, bf16[384,1024]{1,0:T(8,128)(2,1)}, u32[]{:S(2)}, u32[]{:S(2)}) collective-permute-start(bf16[384,1024]{1,0:T(8,128)(2,1)} %collective-permute-done.25), channel_id=1, source_target_pairs={{0,1},{8,9},{17,16},{25,24},{2,3},{10,11},{19,18},{27,26},{4,5},{1... | collective-permute-start | bytes 2359304 | tf_op jit(solution)/shard_map/ppermute | solution.py:150
  73.9 3.5 %collective-permute-start.20 = (f32[1,128]{1,0:T(1,128)S(1)}, f32[1,128]{1,0:T(1,128)S(1)}, u32[]{:S(2)}, u32[]{:S(2)}) collective-permute-start(f32[1,128]{1,0:T(1,128)S(1)} %add.187), channel_id=1, source_target_pairs={{0,8},{8,0},{16,24},{24,16},{1,9},{9,1},{17,25},{25,17},{2,10},{10... | collective-permute-start | bytes 1544 | tf_op jit(solution)/shard_map/ppermute | solution.py:26
  75.4 14.6 %copy-start.8 = (bf16[1024,384]{1,0:T(8,128)(2,1)S(1)}, bf16[1024,384]{1,0:T(8,128)(2,1)}, u32[]{:S(2)}) copy-start(bf16[1024,384]{1,0:T(8,128)(2,1)} %get-tuple-element.20) | copy-start | bytes 2359300
  75.4 14.8 %copy-start.7 = (bf16[1024,384]{1,0:T(8,128)(2,1)S(1)}, bf16[1024,384]{1,0:T(8,128)(2,1)}, u32[]{:S(2)}) copy-start(bf16[1024,384]{1,0:T(8,128)(2,1)} %get-tuple-element.19) | copy-start | bytes 2359300
  77.5 3.5 %collective-permute-start.21 = (f32[1,128]{1,0:T(1,128)S(1)}, f32[1,128]{1,0:T(1,128)S(1)}, u32[]{:S(2)}, u32[]{:S(2)}) collective-permute-start(f32[1,128]{1,0:T(1,128)S(1)} %add.188), channel_id=1, source_target_pairs={{0,16},{8,24},{16,0},{24,8},{1,17},{9,25},{17,1},{25,9},{2,18},{10... | collective-permute-start | bytes 1544 | tf_op jit(solution)/shard_map/ppermute | solution.py:26
  79.0 9.4 %collective-permute-start.24 = (bf16[384,384]{1,0:T(8,128)(2,1)S(1)}, bf16[384,384]{1,0:T(8,128)(2,1)S(1)}, u32[]{:S(2)}, u32[]{:S(2)}) collective-permute-start(bf16[384,384]{1,0:T(8,128)(2,1)S(1)} %get-tuple-element.29), channel_id=1, source_target_pairs={{0,8},{8,0},{16,24},{24,16},{1,9},{9,1},{17,25},{25,17},{2,10},{10... | collective-permute-start | bytes 884744 | tf_op jit(solution)/shard_map/ppermute | solution.py:26
  81.0 9.0 %collective-permute-start.27 = (bf16[384,384]{1,0:T(8,128)(2,1)S(1)}, bf16[384,384]{1,0:T(8,128)(2,1)S(1)}, u32[]{:S(2)}, u32[]{:S(2)}) collective-permute-start(bf16[384,384]{1,0:T(8,128)(2,1)S(1)} %get-tuple-element.31), channel_id=1, source_target_pairs={{0,16},{8,24},{16,0},{24,8},{1,17},{9,25},{17,1},{25,9},{2,18},{10... | collective-permute-start | bytes 884744 | tf_op jit(solution)/shard_map/ppermute | solution.py:26
  82.4 47.6 %collective-permute-start.29 = (bf16[384,1024]{1,0:T(8,128)(2,1)}, bf16[384,1024]{1,0:T(8,128)(2,1)S(1)}, u32[]{:S(2)}, u32[]{:S(2)}) collective-permute-start(bf16[384,1024]{1,0:T(8,128)(2,1)} %collective-permute-done.28), channel_id=1, source_target_pairs={{0,1},{8,9},{17,16},{25,24},{2,3},{10,11},{19,18},{27,26},{4,5},{1... | collective-permute-start | bytes 2359304 | tf_op jit(solution)/shard_map/ppermute | solution.py:150
  88.5 43.4 %collective-permute-start = (bf16[1024,384]{1,0:T(8,128)(2,1)}, bf16[1024,384]{1,0:T(8,128)(2,1)S(1)}, u32[]{:S(2)}, u32[]{:S(2)}) collective-permute-start(bf16[1024,384]{1,0:T(8,128)(2,1)} %get-tuple-element.18), channel_id=1, source_target_pairs={{0,8},{8,0},{16,24},{24,16},{1,9},{9,1},{17,25},{25,17},{2,10},{10... | collective-permute-start | bytes 2359304 | tf_op jit(solution)/shard_map/ppermute | solution.py:26
  90.0 42.0 %collective-permute-start.1 = (bf16[1024,384]{1,0:T(8,128)(2,1)S(1)}, bf16[1024,384]{1,0:T(8,128)(2,1)S(1)}, u32[]{:S(2)}, u32[]{:S(2)}) collective-permute-start(bf16[1024,384]{1,0:T(8,128)(2,1)S(1)} %copy-done.8), channel_id=1, source_target_pairs={{0,16},{8,24},{16,0},{24,8},{1,17},{9,25},{17,1},{25,9},{2,18},{10... | collective-permute-start | bytes 2359304 | tf_op jit(solution)/shard_map/ppermute | solution.py:26
  90.3 41.7 %collective-permute-start.2 = (bf16[1024,384]{1,0:T(8,128)(2,1)S(1)}, bf16[1024,384]{1,0:T(8,128)(2,1)S(1)}, u32[]{:S(2)}, u32[]{:S(2)}) collective-permute-start(bf16[1024,384]{1,0:T(8,128)(2,1)S(1)} %copy-done.7), channel_id=1, source_target_pairs={{0,24},{8,16},{16,8},{24,0},{1,25},{9,17},{17,9},{25,1},{2,26},{10... | collective-permute-start | bytes 2359304 | tf_op jit(solution)/shard_map/ppermute | solution.py:26
  93.8 36.2 %collective-permute-start.30 = (bf16[384,384]{1,0:T(8,128)(2,1)S(1)}, bf16[384,384]{1,0:T(8,128)(2,1)S(1)}, u32[]{:S(2)}, u32[]{:S(2)}) collective-permute-start(bf16[384,384]{1,0:T(8,128)(2,1)S(1)} %get-tuple-element.30), channel_id=1, source_target_pairs={{0,24},{8,16},{16,8},{24,0},{1,25},{9,17},{17,9},{25,1},{2,26},{10... | collective-permute-start | bytes 884744 | tf_op jit(solution)/shard_map/ppermute | solution.py:26
  96.9 35.1 %copy-start.4 = (bf16[384,768]{1,0:T(8,128)(2,1)S(1)}, bf16[384,768]{1,0:T(8,128)(2,1)}, u32[]{:S(2)}) copy-start(bf16[384,768]{1,0:T(8,128)(2,1)} %copy-done.3) | copy-start | bytes 1769476
  96.9 35.1 %copy-start.6 = (bf16[384,1024]{1,0:T(8,128)(2,1)S(1)}, bf16[384,1024]{1,0:T(8,128)(2,1)}, u32[]{:S(2)}) copy-start(bf16[384,1024]{1,0:T(8,128)(2,1)} %copy-done.5) | copy-start | bytes 2359300
  142.1 62.5 %collective-permute-start.38 = (f16[1024,384]{1,0:T(8,128)(2,1)S(1)}, f16[1024,384]{1,0:T(8,128)(2,1)S(1)}, u32[]{:S(2)}, u32[]{:S(2)}) collective-permute-start(f16[1024,384]{1,0:T(8,128)(2,1)S(1)} %get-tuple-element.17), channel_id=1, source_target_pairs={{0,8},{8,0},{16,24},{24,16},{1,9},{9,1},{17,25},{25,17},{2,10},{10... | collective-permute-start | bytes 2359304 | tf_op jit(solution)/shard_map/ppermute | solution.py:26
  142.8 67.3 %collective-permute-start.37 = (f16[1024,384]{1,0:T(8,128)(2,1)S(1)}, f16[1024,384]{1,0:T(8,128)(2,1)S(1)}, u32[]{:S(2)}, u32[]{:S(2)}) collective-permute-start(f16[1024,384]{1,0:T(8,128)(2,1)S(1)} %get-tuple-element.17), channel_id=1, source_target_pairs={{0,16},{8,24},{16,0},{24,8},{1,17},{9,25},{17,1},{25,9},{2,18},{10... | collective-permute-start | bytes 2359304 | tf_op jit(solution)/shard_map/ppermute | solution.py:26
  144.6 68.3 %collective-permute-start.36 = (f16[1024,384]{1,0:T(8,128)(2,1)S(1)}, f16[1024,384]{1,0:T(8,128)(2,1)S(1)}, u32[]{:S(2)}, u32[]{:S(2)}) collective-permute-start(f16[1024,384]{1,0:T(8,128)(2,1)S(1)} %get-tuple-element.17), channel_id=1, source_target_pairs={{0,24},{8,16},{16,8},{24,0},{1,25},{9,17},{17,9},{25,1},{2,26},{10... | collective-permute-start | bytes 2359304 | tf_op jit(solution)/shard_map/ppermute | solution.py:26
  146.3 30.4 %collective-permute-start.31 = (f32[1,128]{1,0:T(1,128)S(1)}, f32[1,128]{1,0:T(1,128)S(1)}, u32[]{:S(2)}, u32[]{:S(2)}) collective-permute-start(f32[1,128]{1,0:T(1,128)S(1)} %compare_select_fusion.2), channel_id=1, source_target_pairs={{0,8},{8,0},{16,24},{24,16},{1,9},{9,1},{17,25},{25,17},{2,10},{10... | collective-permute-start | bytes 1544 | tf_op jit(solution)/shard_map/ppermute | solution.py:26
  177.4 4.4 %collective-permute-start.32 = (f32[1,128]{1,0:T(1,128)S(1)}, f32[1,128]{1,0:T(1,128)S(1)}, u32[]{:S(2)}, u32[]{:S(2)}) collective-permute-start(f32[1,128]{1,0:T(1,128)S(1)} %fusion.90), channel_id=1, source_target_pairs={{0,16},{8,24},{16,0},{24,8},{1,17},{9,25},{17,1},{25,9},{2,18},{10... | collective-permute-start | bytes 1544 | tf_op jit(solution)/shard_map/ppermute | solution.py:26
  183.2 4.8 %collective-permute-start.33 = (f32[1,1]{1,0:T(1,128)}, f32[1,1]{1,0:T(1,128)}, u32[]{:S(2)}, u32[]{:S(2)}) collective-permute-start(f32[1,1]{1,0:T(1,128)} %get-tuple-element.36), channel_id=1, source_target_pairs={{0,2},{2,0},{4,6},{6,4},{1,3},{3,1},{5,7},{7,5},{8,10},{10,8},{12,... | collective-permute-start | bytes 20 | tf_op jit(solution)/shard_map/ppermute | solution.py:26
  189.1 4.7 %collective-permute-start.34 = (f32[1,1]{1,0:T(1,128)}, f32[1,1]{1,0:T(1,128)}, u32[]{:S(2)}, u32[]{:S(2)}) collective-permute-start(f32[1,1]{1,0:T(1,128)} %add.202), channel_id=1, source_target_pairs={{0,4},{2,6},{4,0},{6,2},{1,5},{3,7},{5,1},{7,3},{8,12},{10,14},{12... | collective-permute-start | bytes 20 | tf_op jit(solution)/shard_map/ppermute | solution.py:26
  194.5 1.3 collective-permute-start.35
  199.1 2.8 %copy-start.1 = (f32[1,2048,768]{2,1,0:T(8,128)S(1)}, f32[1,2048,768]{2,1,0:T(8,128)}, u32[]{:S(2)}) copy-start(f32[1,2048,768]{2,1,0:T(8,128)} %momentum.7) | copy-start | bytes 18874372
  204.7 2.8 %copy-start.2 = (f32[1,2048,768]{2,1,0:T(8,128)S(1)}, f32[1,2048,768]{2,1,0:T(8,128)}, u32[]{:S(2)}) copy-start(f32[1,2048,768]{2,1,0:T(8,128)} %momentum.7) | copy-start | bytes 18874372

commit v2 on v0

v2 whole, which is shorter than its diff:
```python
import math

import jax
import jax.numpy as jnp
from jax import lax
from jax.experimental import pallas as pl
from jax.experimental.pallas import tpu as pltpu
from jax.sharding import PartitionSpec as P

F32 = jnp.float32
BF16 = jnp.bfloat16
WIRE = jnp.float16
AXES = ("island", "expert", "tensor")

VMEM = pl.BlockSpec(memory_space=pltpu.VMEM)
SMEM = pl.BlockSpec(memory_space=pltpu.SMEM)
ANY = pl.BlockSpec(memory_space=pl.ANY)


def params(mib):
    return pltpu.CompilerParams(vmem_limit_bytes=mib << 20)


def partner(at, step, size):
    return at ^ step if size & (size - 1) == 0 else (at + step) % size


def origin(at, step, size):
    return at ^ step if size & (size - 1) == 0 else (at - step) % size


def swap(value, axis, step):
    size = lax.axis_size(axis)
    return lax.ppermute(value, axis, [(at, partner(at, step, size)) for at in range(size)])


def dot(a, b, contract):
    return lax.dot_general(a, b, (contract, ((), ())), preferred_element_type=F32)


def pick_kernel(experts, spot, table, count, weight, tokens, grads, *outs):
    slots = table.shape[-1]
    rows = lax.broadcasted_iota(jnp.int32, (slots, slots), 0)
    lanes = lax.broadcasted_iota(jnp.int32, (slots, slots), 1)

    def column(row):
        return jnp.sum(jnp.where(rows == lanes, row, 0), axis=1, keepdims=True)

    for d in range(experts):
        to = partner(spot[0], d, experts)
        live = lax.broadcasted_iota(jnp.int32, (slots, 1), 0) < count[0, 0, to]
        token = column(table[0, 0, pl.ds(to, 1), :].astype(F32)).astype(jnp.int32)
        chance = column(weight[0, 0, pl.ds(to, 1), :])
        ids = lax.broadcasted_iota(jnp.int32, (slots, tokens.shape[1]), 1)
        picks = jnp.where((ids == token) & live, 1.0, 0.0).astype(BF16)
        outs[d][...] = dot(picks, tokens[0], ((1,), (0,))).astype(BF16)
        picked = dot(picks, grads[0], ((1,), (0,)))
        outs[experts + d][...] = (chance * picked).astype(BF16)


def gather_kernel(pieces, blocks, *refs):
    inputs, drifts = refs[:pieces], refs[pieces : pieces + blocks]
    joined, turned, drift_sum = refs[pieces + blocks :]
    slots = inputs[0].shape[0]
    for n, piece in enumerate(inputs):
        joined[n * slots : (n + 1) * slots, :] = piece[...]
    turned[...] = joined[...].T
    added = drifts[0][...].astype(F32)
    for other in drifts[1:]:
        added = added + other[...].astype(F32)
    drift_sum[...] = added


def gate_kernel(parts, spot, weight, *refs):
    inputs, (silu, gram) = refs[:parts], refs[parts:]
    half = inputs[0].shape[1]
    value = 0.0
    squares = 0.0
    for t in range(parts):
        start = pl.multiple_of(origin(spot[1], t, parts) * half, half)
        features = inputs[t][...]
        value = value + dot(features, weight[0, 0, pl.ds(start, half), :], ((1,), (0,)))
        squares = squares + dot(features, features, ((1,), (1,)))
    silu[...] = value / (1.0 + jnp.exp(-value))
    gram[...] = squares


def hidden_kernel(parts, pieces, across, spot, weight, silu, gram, *refs):
    grads = refs[: parts * pieces]
    outs = refs[-across - 2 : -2]
    norms, joined = refs[-2:]
    slots, half = grads[0].shape
    columns = silu.shape[1] // across
    for t in range(parts):
        for n in range(pieces):
            joined[t, n * slots : (n + 1) * slots, :] = grads[t * pieces + n][...]
    squares = 0.0
    for r in range(across):
        first = pl.multiple_of(partner(spot[2], r, across) * columns, columns)
        value = 0.0
        for t in range(parts):
            start = pl.multiple_of(origin(spot[1], t, parts) * half, half)
            block = weight[0, 0, pl.ds(first, columns), pl.ds(start, half)]
            value = value + dot(joined[t], block, ((1,), (1,)))
        rounded = (value * silu[:, pl.ds(first, columns)]).astype(BF16)
        outs[r][...] = rounded
        squares = squares + dot(rounded, rounded, ((1,), (1,)))
    norms[...] = jnp.full(norms.shape, jnp.sum(squares * gram[...]), F32)


def average_kernel(islands, entries, spot, norms, drift_sum, *refs):
    inputs, hiddens = refs[:islands], refs[islands : 2 * islands]
    scaled, notes, total = refs[-3:]
    group = norms.shape[0] // islands
    average = drift_sum[...]
    for d in range(islands):
        at = origin(spot[3], d, islands)
        square = jnp.sum(norms[pl.ds(at * group, group)], axis=0)[:1, :1]
        scale = jnp.minimum(1.0, math.sqrt(entries) / jnp.sqrt(square + 1e-06))
        average = average + scale * dot(inputs[d][...], hiddens[d][...], ((1,), (0,)))
    average = average / islands
    total[...] = average
    peak = jnp.max(jnp.abs(average))
    peak = jnp.where(peak > 0, peak, 1.0)
    scaled[...] = total[...] / peak
    sublane = lax.broadcasted_iota(jnp.int32, notes.shape, 1)
    notes[...] = jnp.where(sublane == 0, jnp.sum(average * average), peak)


def update_kernel(entries, place, notes, block, momentum, *rest):
    new_momentum, outer_step = rest[-2:]
    square = jnp.sum(notes[...], axis=0)[:1, :1]
    clip = jnp.minimum(1.0, 0.25 * math.sqrt(entries) / jnp.sqrt(square + 1e-06))
    peak = notes[pl.ds(place[2], 1)][0, 1:2, :1]
    clipped = (clip * peak) * block[...]
    moved = 0.9 * momentum[0] + clipped
    new_momentum[0] = moved
    outer_step[0] = (0.7 * (clipped + 0.9 * moved)).astype(BF16)


def update_block(entries, place, notes, block, momentum, outs):
    rows, columns = block.shape
    steps = 2
    tile = rows // steps
    here = pl.BlockSpec((tile, columns), lambda r, place: (r, 0))
    there = pl.BlockSpec(
        (1, tile, columns), lambda r, place: (0, place[0] * steps + r, place[1])
    )
    whole = pl.BlockSpec(notes.shape, lambda r, place: (0, 0, 0))
    return pl.pallas_call(
        lambda *refs: update_kernel(entries, *refs),
        grid_spec=pltpu.PrefetchScalarGridSpec(
            num_scalar_prefetch=1,
            grid=(steps,),
            in_specs=[whole, here, there] + [ANY] * len(outs),
            out_specs=[there, there],
        ),
        out_shape=[
            jax.ShapeDtypeStruct(momentum.shape, F32),
            jax.ShapeDtypeStruct(momentum.shape, BF16),
        ],
        input_output_aliases={4 + n: n for n in range(len(outs))},
        compiler_params=params(32),
        name="update_block",
    )(place, notes, block, momentum, *outs)


def body(
    tokens,
    token_grads,
    slot_token,
    slot_count,
    slot_prob,
    gate_weight,
    down_weight,
    drift,
    momentum,
):
    islands, experts, parts = (lax.axis_size(a) for a in AXES)
    island, expert, part = (lax.axis_index(a) for a in AXES)
    devices = islands * experts * parts
    features, hidden = gate_weight.shape[2:]
    half = features // parts
    across = islands // parts
    columns = hidden // across
    entries = features * hidden * experts * parts
    slots = slot_token.shape[3]
    routed_rows = experts * slots
    spot = jnp.stack([expert, part, island % across, island]).astype(jnp.int32)

    piece = jax.ShapeDtypeStruct((slots, half), BF16)
    picked = pl.pallas_call(
        lambda *refs: pick_kernel(experts, *refs),
        in_specs=[SMEM, VMEM, SMEM, VMEM, VMEM, VMEM],
        out_specs=[VMEM] * (2 * experts),
        out_shape=[piece] * (2 * experts),
        compiler_params=params(32),
        name="pick_slots",
    )(spot, slot_token, slot_count, slot_prob, tokens, token_grads)

    def routed(values):
        return [values[0]] + [swap(values[d], "expert", d) for d in range(1, experts)]

    inputs_in = routed(picked[:experts])

    def block_of(at):
        return lax.dynamic_slice(
            drift[0, 0], ((at // across) * half, (at % across) * columns), (half, columns)
        )

    drift_in = [block_of(island)] + [
        swap(block_of(partner(island, d, islands)), "island", d) for d in range(1, islands)
    ]
    grads_in = routed(picked[experts:])
    inputs, turned, drift_sum = pl.pallas_call(
        lambda *refs: gather_kernel(experts, islands, *refs),
        in_specs=[VMEM] * (experts + islands),
        out_specs=[VMEM] * 3,
        out_shape=[
            jax.ShapeDtypeStruct((routed_rows, half), BF16),
            jax.ShapeDtypeStruct((half, routed_rows), BF16),
            jax.ShapeDtypeStruct((half, columns), F32),
        ],
        compiler_params=params(40),
        name="join_inputs",
    )(*inputs_in, *drift_in)

    inputs_all = [inputs] + [swap(inputs, "tensor", t) for t in range(1, parts)]

    def send_features(d):
        pairs = []
        for at in range(islands):
            to = partner(at, d, islands)
            holder = to // across
            pairs.append((at * parts + holder, to * parts + holder))
        return lax.ppermute(turned, ("island", "tensor"), pairs)

    def spread(value):
        holder = island // across
        result = value
        for t in range(1, parts):
            pairs = []
            for at in range(islands):
                keep = at // across
                pairs.append((at * parts + keep, at * parts + partner(keep, t, parts)))
            moved = lax.ppermute(value, ("island", "tensor"), pairs)
            result = jnp.where(part == partner(holder, t, parts), moved, result)
        return result

    features_of = [spread(turned)] + [spread(send_features(d)) for d in range(1, islands)]

    silu, gram = pl.pallas_call(
        lambda *refs: gate_kernel(parts, *refs),
        in_specs=[SMEM] + [VMEM] * (1 + parts),
        out_specs=[VMEM] * 2,
        out_shape=[
            jax.ShapeDtypeStruct((routed_rows, hidden), F32),
            jax.ShapeDtypeStruct((routed_rows, routed_rows), F32),
        ],
        compiler_params=params(40),
        name="gate_values",
    )(spot, gate_weight, *inputs_all)

    grads_all = [g for t in range(1, parts) for g in [swap(v, "tensor", t) for v in grads_in]]
    grads_all = list(grads_in) + grads_all
    hidden_piece = jax.ShapeDtypeStruct((routed_rows, columns), BF16)
    *hidden_out, norms = pl.pallas_call(
        lambda *refs: hidden_kernel(parts, experts, across, *refs),
        in_specs=[SMEM] + [VMEM] * (3 + len(grads_all)) + [ANY] * islands,
        out_specs=[VMEM] * (across + 1),
        out_shape=[hidden_piece] * across + [jax.ShapeDtypeStruct((devices, 8, 128), F32)],
        scratch_shapes=[pltpu.VMEM((parts, routed_rows, half), BF16)],
        compiler_params=params(40),
        name="hidden_grads",
    )(spot, down_weight, silu, gram, *grads_all, *features_of)

    def hidden_for(d):
        if islands & (islands - 1) == 0:
            return hidden_out[d % across]
        at = partner(island, d, islands) % across
        step = (at - island) % across
        return lax.select_n(step, *hidden_out) if across > 2 else jnp.where(step == 0, *hidden_out)

    hidden_of = [hidden_out[0]] + [
        swap(hidden_for(d), "island", d) for d in range(1, islands)
    ]
    norms = lax.all_to_all(norms, AXES, split_axis=0, concat_axis=0, tiled=True)

    scaled, notes = pl.pallas_call(
        lambda *refs: average_kernel(islands, entries, *refs),
        in_specs=[SMEM] + [VMEM] * (2 + 2 * islands),
        out_specs=[VMEM] * 2,
        out_shape=[
            jax.ShapeDtypeStruct((half, columns), F32),
            jax.ShapeDtypeStruct((devices, 8, 128), F32),
        ],
        scratch_shapes=[pltpu.VMEM((half, columns), F32)],
        compiler_params=params(40),
        name="average_block",
    )(spot, norms, drift_sum, *features_of, *hidden_of)
    notes = lax.all_to_all(notes, AXES, split_axis=0, concat_axis=0, tiled=True)

    sent = lax.optimization_barrier([h.astype(WIRE) for h in jnp.split(scaled, 2)])
    if islands == 4:
        first = [[sent[0], swap(sent[0], "island", 1), swap(sent[0], "island", 2), None]]
        second = [[sent[1], swap(sent[1], "island", 1), swap(sent[1], "island", 2), None]]
        first[0][3] = swap(first[0][1], "island", 2)
        second[0][3] = swap(second[0][2], "island", 1)
        halves = first + second
    else:
        halves = [[h] + [swap(h, "island", d) for d in range(1, islands)] for h in sent]

    outs = []
    for d in range(islands):
        at = origin(island, d, islands)
        source = (at * experts + expert) * parts + part
        for n in range(2):
            place = jnp.stack([(at // across) * 2 + n, at % across, source]).astype(jnp.int32)
            block = halves[n][d].astype(F32)
            outs = update_block(entries, place, notes, block, momentum, outs)
    return tuple(outs)


def solution(mesh):
    return jax.shard_map(
        body,
        mesh=mesh,
        in_specs=(
            P("island", "expert", "tensor"),
            P("island", "expert", "tensor"),
            P("island", "expert", None, None),
            P("island", "expert", None),
            P("island", "expert", None, None),
            P("island", "expert", None, "tensor"),
            P("island", "expert", "tensor", None),
            P("island", "expert", None, "tensor"),
            P("expert", None, "tensor"),
        ),
        out_specs=(P("expert", None, "tensor"), P("expert", None, "tensor")),
        check_vma=False,
    )
```

time: 286 us -> 180 us (0.63)
  waiting for transfers between devices: 157 us -> 56.6 us
  starting transfers between devices: 6.4 us -> 49 us
  blocking collectives: 57.4 us -> 15.5 us
  Pallas kernels: 0 us -> 30.4 us
  other arithmetic: 27 us -> 10.2 us
  between operations: 15.2 us -> 1.13 us
  matrix products: 13.6 us -> 0 us
  local copies, waits for them, and re-layouts: 9.1 us -> 15.1 us
    psum x1 -> x0, waiting for transfers between devices: 137 us -> none  [body(): average = lax.psum(pseudo, 'island') / islands]
    ppermute x0 -> x30, waiting for transfers between devices: none -> 47.7 us  [the longest x23 35.9 us: swap(): lax.ppermute(value, axis, [(at, partner(at, step, size)) for at in range(...]
    ppermute x0 -> x30, starting transfers between devices: none -> 42.4 us  [the longest x23 29.5 us: swap(): lax.ppermute(value, axis, [(at, partner(at, step, size)) for at in range(...]
    psum x2 -> x0, blocking collectives: 34.7 us -> none  [the longest x1 17.7 us: body(): inner_square = lax.psum(jnp.sum(gradient * gradient), ('expert', 'tensor'))]
    pallas_call x0 -> x13, Pallas kernels: none -> 30.4 us  [the longest x8 15 us: update_block(): pl.pallas_call(lambda *refs: update_kernel(entries, *refs), grid_spec=plt...]
    dot_general x2 -> x0, matrix products: 13.6 us -> none  [the longest x1 8.8 us: body(): jnp.einsum('erd,erf->edf', inputs, hidden_grad, preferred_element_type=jn...]
    unnamed x6 -> x30, local copies, waits for them, and re-layouts: 0.02 us -> 11.3 us
    gather x2 -> x0, local copies, waits for them, and re-layouts: 9 us -> none  [the longest x1 4.51 us: body(): token_grads[0][index_table].astype(jnp.float32)]
  transfers between devices with their start and end apart: 4 -> 31, of which waited for: 3 -> 9; matrix products, arithmetic and copies ran while one was open for 4% -> 5% of each run, Pallas kernels for 0% -> 9%
where the time goes in v2:
time: 180 us; the launch traced here: 178 us
  waiting for transfers between devices  56.6 us (31%)
  starting transfers between devices  49 us (27%)
  Pallas kernels  30.4 us (17%)
  blocking collectives  15.5 us (9%)
  local copies, waits for them, and re-layouts  15.1 us (8%)
  other arithmetic  10.2 us (6%)
    ppermute x23, waiting for transfers between devices, swap(): lax.ppermute(value, axis, [(at, partner(at, step, size)) for at in range(...  35.9 us
    ppermute x23, starting transfers between devices, swap(): lax.ppermute(value, axis, [(at, partner(at, step, size)) for at in range(...  29.5 us
    all_to_all x1, blocking collectives, body(): norms = lax.all_to_all(norms, AXES, split_axis=0, concat_axis=0, tiled=True)  15.5 us
    pallas_call x8, Pallas kernels, update_block(): pl.pallas_call(lambda *refs: update_kernel(entries, *refs), grid_spec=plt...  15 us
    ppermute x3, waiting for transfers between devices, send_features(): return lax.ppermute(turned, ('island', 'tensor'), pairs)  11.8 us
    unnamed x30, local copies, waits for them, and re-layouts  11.3 us
    all_to_all x1, waiting for transfers between devices, body(): notes = lax.all_to_all(notes, AXES, split_axis=0, concat_axis=0, tiled=True)  8.95 us
    ppermute x4, starting transfers between devices, spread(): moved = lax.ppermute(value, ('island', 'tensor'), pairs)  7.86 us
  transfers between devices with their start and end apart: 31, of which 9 were waited for; matrix products, arithmetic and copies ran while one was open for 5% of the time, Pallas kernels for 9%

profile of v2, /device:TPU:0, one launch (start us, length us, event | category | flops | bytes accessed | tf_op | source)
XLA Modules:
  0.0 177.9 jit_solution(5692299802675943818)
XLA Ops:
  0.8 3.6 %dynamic-slice_bitcast_fusion = (bf16[1024,384]{1,0:T(8,128)(2,1)}, bf16[1024,384]{1,0:T(8,128)(2,1)}, bf16[1024,384]{1,0:T(8,128)(2,1)}, bf16[1024,384]{1,0:T(8,128)(2,1)}) fusion(bf16[1,1,2048,768]{3,2,1,0:T(8,128)(2,1)} %param.16, s32[]{:T(128)S(6)} %select_n.120, s32[]{:T(128)S(6)} %select_n.121, s32[]{:T(128)S(6)} %select_n.113, s32[]{:T(128)S(6)} %select_n.115, ...), kind=kLoop, calls=%fused_computation | loop fusion | bytes 6291488 | tf_op jit(solution)/shard_map/dynamic_slice | solution.py:207
  4.4 2.9 %collective-permute-start.3 = (bf16[1024,384]{1,0:T(8,128)(2,1)}, bf16[1024,384]{1,0:T(8,128)(2,1)}, u32[]{:S(2)}, u32[]{:S(2)}) collective-permute-start(bf16[1024,384]{1,0:T(8,128)(2,1)} %get-tuple-element.71), channel_id=1, source_target_pairs={{0,8},{8,0},{16,24},{24,16},{1,9},{9,1},{17,25},{25,17},{2,10},{10... | collective-permute-start | bytes 2359304 | tf_op jit(solution)/shard_map/ppermute | solution.py:34
  7.4 1.5 collective-permute-start.4
  9.0 1.0 copy-done.7
  10.0 1.0 copy-done.8
  11.1 1.4 pick_slots.1
  12.5 0.7 copy-done.12
  13.1 0.7 copy-done.14
  13.8 2.0 %collective-permute-start = (bf16[96,1024]{1,0:T(8,128)(2,1)S(1)}, bf16[96,1024]{1,0:T(8,128)(2,1)S(1)}, u32[]{:S(2)}, u32[]{:S(2)}) collective-permute-start(bf16[96,1024]{1,0:T(8,128)(2,1)S(1)} %get-tuple-element.37), channel_id=1, source_target_pairs={{0,2},{2,0},{4,6},{6,4},{1,3},{3,1},{5,7},{7,5},{8,10},{10,8},{12,... | collective-permute-start | bytes 589832 | tf_op jit(solution)/shard_map/ppermute | solution.py:34
  15.9 2.6 %collective-permute-start.1 = (bf16[96,1024]{1,0:T(8,128)(2,1)S(1)}, bf16[96,1024]{1,0:T(8,128)(2,1)S(1)}, u32[]{:S(2)}, u32[]{:S(2)}) collective-permute-start(bf16[96,1024]{1,0:T(8,128)(2,1)S(1)} %get-tuple-element.38), channel_id=1, source_target_pairs={{0,4},{2,6},{4,0},{6,2},{1,5},{3,7},{5,1},{7,3},{8,12},{10,14},{12... | collective-permute-start | bytes 589832 | tf_op jit(solution)/shard_map/ppermute | solution.py:34
  18.5 5.2 %collective-permute-done.refs_1_ = bf16[96,1024]{1,0:T(8,128)(2,1)S(1)} collective-permute-done((bf16[96,1024]{1,0:T(8,128)(2,1)S(1)}, bf16[96,1024]{1,0:T(8,128)(2,1)S(1)}, u32[]{:S(2)}, u32[]{:S(2)}) %collective-permute-start) | collective-permute-done | bytes 196640 | tf_op jit(solution)/shard_map/ppermute | solution.py:34
  23.7 3.0 %collective-permute-start.2 = (bf16[96,1024]{1,0:T(8,128)(2,1)S(1)}, bf16[96,1024]{1,0:T(8,128)(2,1)S(1)}, u32[]{:S(2)}, u32[]{:S(2)}) collective-permute-start(bf16[96,1024]{1,0:T(8,128)(2,1)S(1)} %get-tuple-element.39), channel_id=1, source_target_pairs={{0,6},{2,4},{4,2},{6,0},{1,7},{3,5},{5,3},{7,1},{8,14},{10,12},{12... | collective-permute-start | bytes 589832 | tf_op jit(solution)/shard_map/ppermute | solution.py:34
  26.7 2.3 %collective-permute-done.1.refs_2_ = bf16[96,1024]{1,0:T(8,128)(2,1)S(1)} collective-permute-done((bf16[96,1024]{1,0:T(8,128)(2,1)S(1)}, bf16[96,1024]{1,0:T(8,128)(2,1)S(1)}, u32[]{:S(2)}, u32[]{:S(2)}) %collective-permute-start.1) | collective-permute-done | bytes 196640 | tf_op jit(solution)/shard_map/ppermute | solution.py:34
  29.0 2.3 %collective-permute-done.2.refs_3_ = bf16[96,1024]{1,0:T(8,128)(2,1)S(1)} collective-permute-done((bf16[96,1024]{1,0:T(8,128)(2,1)S(1)}, bf16[96,1024]{1,0:T(8,128)(2,1)S(1)}, u32[]{:S(2)}, u32[]{:S(2)}) %collective-permute-start.2) | collective-permute-done | bytes 196640 | tf_op jit(solution)/shard_map/ppermute | solution.py:34
  31.3 12.3 %collective-permute-done.4.refs_6_ = bf16[1024,384]{1,0:T(8,128)(2,1)} collective-permute-done((bf16[1024,384]{1,0:T(8,128)(2,1)}, bf16[1024,384]{1,0:T(8,128)(2,1)}, u32[]{:S(2)}, u32[]{:S(2)}) %collective-permute-start.4) | collective-permute-done | bytes 786464 | tf_op jit(solution)/shard_map/ppermute | solution.py:34
  43.5 1.1 copy-done.4
  44.7 3.5 %join_inputs.1 = (bf16[384,1024]{1,0:T(8,128)(2,1)}, bf16[1024,384]{1,0:T(8,128)(2,1)}, f32[1024,384]{1,0:T(8,128)S(1)}) custom-call(bf16[96,1024]{1,0:T(8,128)(2,1)S(1)} %get-tuple-element.36.refs_0_, bf16[96,1024]{1,0:T(8,128)(2,1)S(1)} %collective-permute-done.refs_1_, bf16[96,1024]{1,0:T(8,128)(2,1)S(1)} %collective-permute-done.1.refs_2_, ...), custom_call_target="tpu_custom_call" | custom-call | tf_op jit(solution)/shard_map/join_inputs/pallas_call | solution.py:215
  48.2 1.1 copy-done.5
  49.3 1.3 collective-permute-start.19
  50.6 1.3 collective-permute-start.17
  51.9 2.3 %collective-permute-start.6 = (bf16[384,1024]{1,0:T(8,128)(2,1)}, bf16[384,1024]{1,0:T(8,128)(2,1)}, u32[]{:S(2)}, u32[]{:S(2)}) collective-permute-start(bf16[384,1024]{1,0:T(8,128)(2,1)} %get-tuple-element.40.refs_2_), channel_id=1, source_target_pairs={{0,1},{1,0},{2,3},{3,2},{4,5},{5,4},{6,7},{7,6},{8,9},{9,8},{10,11... | collective-permute-start | bytes 2359304 | tf_op jit(solution)/shard_map/ppermute | solution.py:34
  54.2 2.5 %collective-permute-start.15 = (bf16[1024,384]{1,0:T(8,128)(2,1)}, bf16[1024,384]{1,0:T(8,128)(2,1)}, u32[]{:S(2)}, u32[]{:S(2)}) collective-permute-start(bf16[1024,384]{1,0:T(8,128)(2,1)} %get-tuple-element.47), channel_id=1, source_target_pairs={{0,8},{8,0},{17,25},{25,17},{2,10},{10,2},{19,27},{27,19},{4,12},{... | collective-permute-start | bytes 2359304 | tf_op jit(solution)/shard_map/ppermute | solution.py:236
  56.7 2.2 %collective-permute-start.14 = (bf16[1024,384]{1,0:T(8,128)(2,1)}, bf16[1024,384]{1,0:T(8,128)(2,1)}, u32[]{:S(2)}, u32[]{:S(2)}) collective-permute-start(bf16[1024,384]{1,0:T(8,128)(2,1)} %get-tuple-element.47), channel_id=1, source_target_pairs={{0,1},{8,9},{17,16},{25,24},{2,3},{10,11},{19,18},{27,26},{4,5},{1... | collective-permute-start | bytes 2359304 | tf_op jit(solution)/shard_map/ppermute | solution.py:246
  58.9 8.2 %collective-permute-done.19 = bf16[1024,384]{1,0:T(8,128)(2,1)} collective-permute-done((bf16[1024,384]{1,0:T(8,128)(2,1)}, bf16[1024,384]{1,0:T(8,128)(2,1)}, u32[]{:S(2)}, u32[]{:S(2)}) %collective-permute-start.19) | collective-permute-done | bytes 786464 | tf_op jit(solution)/shard_map/ppermute | solution.py:236
  67.1 2.2 %collective-permute-start.20 = (bf16[1024,384]{1,0:T(8,128)(2,1)}, bf16[1024,384]{1,0:T(8,128)(2,1)}, u32[]{:S(2)}, u32[]{:S(2)}) collective-permute-start(bf16[1024,384]{1,0:T(8,128)(2,1)} %collective-permute-done.19), channel_id=1, source_target_pairs={{0,1},{8,9},{17,16},{25,24},{2,3},{10,11},{19,18},{27,26},{4,5},{1... | collective-permute-start | bytes 2359304 | tf_op jit(solution)/shard_map/ppermute | solution.py:246
  69.3 3.5 %collective-permute-done.17 = bf16[1024,384]{1,0:T(8,128)(2,1)} collective-permute-done((bf16[1024,384]{1,0:T(8,128)(2,1)}, bf16[1024,384]{1,0:T(8,128)(2,1)}, u32[]{:S(2)}, u32[]{:S(2)}) %collective-permute-start.17) | collective-permute-done | bytes 786464 | tf_op jit(solution)/shard_map/ppermute | solution.py:236
  72.9 2.2 %collective-permute-start.18 = (bf16[1024,384]{1,0:T(8,128)(2,1)}, bf16[1024,384]{1,0:T(8,128)(2,1)}, u32[]{:S(2)}, u32[]{:S(2)}) collective-permute-start(bf16[1024,384]{1,0:T(8,128)(2,1)} %collective-permute-done.17), channel_id=1, source_target_pairs={{0,1},{8,9},{17,16},{25,24},{2,3},{10,11},{19,18},{27,26},{4,5},{1... | collective-permute-start | bytes 2359304 | tf_op jit(solution)/shard_map/ppermute | solution.py:246
  75.0 1.6 collective-permute-start.7
  76.6 3.6 %gate_values.1 = (f32[384,768]{1,0:T(8,128)S(1)}, f32[384,384]{1,0:T(8,128)S(1)}) custom-call(s32[4]{0:T(128)S(1)} %pad_add_fusion.refs_0_, bf16[1,1,2048,768]{3,2,1,0:T(8,128)(2,1)S(1)} %copy-done.2, bf16[384,1024]{1,0:T(8,128)(2,1)} %get-tuple-element.40.refs_2_, bf16[384,1024]{1,0:T(8,128)(2,1)} %collective-permute-done.6.refs_3_), custom_call_target="tpu_custom_call" | custom-call | tf_op jit(solution)/shard_map/gate_values/pallas_call | solution.py:252
  80.3 2.7 %collective-permute-start.8 = (bf16[96,1024]{1,0:T(8,128)(2,1)S(1)}, bf16[96,1024]{1,0:T(8,128)(2,1)S(1)}, u32[]{:S(2)}, u32[]{:S(2)}) collective-permute-start(bf16[96,1024]{1,0:T(8,128)(2,1)S(1)} %copy-done.13), channel_id=1, source_target_pairs={{0,4},{2,6},{4,0},{6,2},{1,5},{3,7},{5,1},{7,3},{8,12},{10,14},{12... | collective-permute-start | bytes 589832 | tf_op jit(solution)/shard_map/ppermute | solution.py:34
  82.9 1.3 collective-permute-start.16
  84.2 1.2 broadcast_select_fusion.3.refs_12_.refs_3_
  85.8 1.4 broadcast_select_fusion.refs_15_.refs_6_
  87.3 6.1 %collective-permute-done.8.refs_6_ = bf16[96,1024]{1,0:T(8,128)(2,1)S(1)} collective-permute-done((bf16[96,1024]{1,0:T(8,128)(2,1)S(1)}, bf16[96,1024]{1,0:T(8,128)(2,1)S(1)}, u32[]{:S(2)}, u32[]{:S(2)}) %collective-permute-start.8) | collective-permute-done | bytes 196640 | tf_op jit(solution)/shard_map/ppermute | solution.py:34
  94.0 1.2 broadcast_select_fusion.1.refs_14_.refs_5_
  95.2 1.2 broadcast_select_fusion.2.refs_13_.refs_4_
  96.5 3.0 %hidden_grads.1 = (bf16[384,384]{1,0:T(8,128)(2,1)S(1)}, bf16[384,384]{1,0:T(8,128)(2,1)S(1)}, f32[32,8,128]{2,1,0:T(8,128)S(1)}) custom-call(s32[4]{0:T(128)S(1)} %pad_add_fusion.refs_0_, bf16[1,1,768,2048]{3,2,1,0:T(8,128)(2,1)S(1)} %copy-done.3, f32[384,768]{1,0:T(8,128)S(1)} %get-tuple-element.41.refs_2_, f32[384,384]{1,0:T(8,128)S(1)} %get-tuple-element.42.refs_3_, ...), custom_call_target="tpu_custom_call" | custom-call | tf_op jit(solution)/shard_map/hidden_grads/pallas_call | solution.py:267
  99.6 1.5 collective-permute-start.21
  101.0 1.5 collective-permute-start.22
  102.5 0.6 collective-permute-start.23
  103.1 15.5 %all_to_all.10.refs_1_ = f32[32,8,128]{2,1,0:T(8,128)S(1)} all-to-all(f32[32,8,128]{2,1,0:T(8,128)S(1)} %get-tuple-element.48), channel_id=1, replica_groups=mesh['island'=4,'expert'=4,'tensor'=2] {'island','expert','tensor'}, dimensions={0} | all-to-all | bytes 262144 | tf_op jit(solution)/shard_map/all_to_all | solution.py:287
  118.7 3.9 %average_block.1 = (f32[1024,384]{1,0:T(8,128)S(1)}, f32[32,8,128]{2,1,0:T(8,128)}) custom-call(s32[4]{0:T(128)S(1)} %pad_add_fusion.refs_0_, f32[32,8,128]{2,1,0:T(8,128)S(1)} %all_to_all.10.refs_1_, f32[1024,384]{1,0:T(8,128)S(1)} %copy-done.6, bf16[1024,384]{1,0:T(8,128)(2,1)S(1)} %broadcast_select_fusion.3.refs_12_.refs_3_, ...), custom_call_target="tpu_custom_call" | custom-call | tf_op jit(solution)/shard_map/average_block/pallas_call | solution.py:289
  122.8 1.0 collective-permute-start.26
  123.8 1.3 collective-permute-start.24
  125.3 1.2 collective-permute-start.29
  127.1 7.7 %collective-permute-done.26 = f16[512,384]{1,0:T(8,128)(2,1)S(1)} collective-permute-done((f16[512,384]{1,0:T(8,128)(2,1)S(1)}, f16[512,384]{1,0:T(8,128)(2,1)S(1)}, u32[]{:S(2)}, u32[]{:S(2)}) %collective-permute-start.26) | collective-permute-done | bytes 393248 | tf_op jit(solution)/shard_map/ppermute | solution.py:34
  134.8 1.5 collective-permute-start.27
  136.3 0.8 collective-permute-start.25
  137.2 6.6 %all-to-all-start.1 = ((f32[32,8,128]{2,1,0:T(8,128)}), f32[32,8,128]{2,1,0:T(8,128)S(1)}, u32[]{:S(2)}, u32[]{:S(2)}) async-start(f32[32,8,128]{2,1,0:T(8,128)} %get-tuple-element.52), calls=%async_computation.1 | async-start | bytes 262144 | tf_op jit(solution)/shard_map/all_to_all | solution.py:301
  144.1 9.0 %all-to-all-done.1.refs_1_ = f32[32,8,128]{2,1,0:T(8,128)S(1)} async-done(((f32[32,8,128]{2,1,0:T(8,128)}), f32[32,8,128]{2,1,0:T(8,128)S(1)}, u32[]{:S(2)}, u32[]{:S(2)}) %all-to-all-start.1) | async-done | bytes 131104 | tf_op jit(solution)/shard_map/all_to_all | solution.py:301
  153.0 2.8 %copy-done = f32[1,2048,768]{2,1,0:T(8,128)S(1)} copy-done((f32[1,2048,768]{2,1,0:T(8,128)S(1)}, f32[1,2048,768]{2,1,0:T(8,128)}, u32[]{:S(2)}) %copy-start) | copy-done | bytes 6291480
  155.8 1.9 %update_block.8 = (f32[1,2048,768]{2,1,0:T(8,128)}, bf16[1,2048,768]{2,1,0:T(8,128)(2,1)}) custom-call(s32[3]{0:T(128)S(1)} %get-tuple-element.77.refs_0_, f32[32,8,128]{2,1,0:T(8,128)S(1)} %all-to-all-done.1.refs_1_, f32[512,384]{1,0:T(8,128)S(1)} %convert_element_type.33.refs_2_, f32[1,2048,768]{2,1,0:T(8,128)S(1)} %copy-done), custom_call_target="tpu_custom_call" | custom-call | tf_op jit(solution)/shard_map/update_block/pallas_call | solution.py:150
  157.7 2.8 %copy-done.1 = f32[1,2048,768]{2,1,0:T(8,128)S(1)} copy-done((f32[1,2048,768]{2,1,0:T(8,128)S(1)}, f32[1,2048,768]{2,1,0:T(8,128)}, u32[]{:S(2)}) %copy-start.1) | copy-done | bytes 6291480
  160.5 1.9 %update_block.9 = (f32[1,2048,768]{2,1,0:T(8,128)}, bf16[1,2048,768]{2,1,0:T(8,128)(2,1)}) custom-call(s32[3]{0:T(128)S(1)} %get-tuple-element.76.refs_0_, f32[32,8,128]{2,1,0:T(8,128)S(1)} %all-to-all-done.1.refs_1_, f32[512,384]{1,0:T(8,128)S(1)} %convert_element_type.32.refs_2_, ...), custom_call_target="tpu_custom_call", output_to_operand_aliasing={{0}: (4, {}), {1}: (5, {})} | custom-call | tf_op jit(solution)/shard_map/update_block/pallas_call | solution.py:150
  162.5 1.0 convert_element_type.30.refs_2_
  163.6 1.0 convert_element_type.29.refs_2_
  164.6 1.9 %update_block.10 = (f32[1,2048,768]{2,1,0:T(8,128)}, bf16[1,2048,768]{2,1,0:T(8,128)(2,1)}) custom-call(s32[3]{0:T(128)S(1)} %add_add_fusion.5.refs_0_, f32[32,8,128]{2,1,0:T(8,128)S(1)} %all-to-all-done.1.refs_1_, f32[512,384]{1,0:T(8,128)S(1)} %convert_element_type.31.refs_2_, ...), custom_call_target="tpu_custom_call", output_to_operand_aliasing={{0}: (4, {}), {1}: (5, {})} | custom-call | tf_op jit(solution)/shard_map/update_block/pallas_call | solution.py:150
  166.5 1.9 %update_block.11 = (f32[1,2048,768]{2,1,0:T(8,128)}, bf16[1,2048,768]{2,1,0:T(8,128)(2,1)}) custom-call(s32[3]{0:T(128)S(1)} %add_add_fusion.4.refs_0_, f32[32,8,128]{2,1,0:T(8,128)S(1)} %all-to-all-done.1.refs_1_, f32[512,384]{1,0:T(8,128)S(1)} %convert_element_type.30.refs_2_, ...), custom_call_target="tpu_custom_call", output_to_operand_aliasing={{0}: (4, {}), {1}: (5, {})} | custom-call | tf_op jit(solution)/shard_map/update_block/pallas_call | solution.py:150
  168.3 1.9 %update_block.12 = (f32[1,2048,768]{2,1,0:T(8,128)}, bf16[1,2048,768]{2,1,0:T(8,128)(2,1)}) custom-call(s32[3]{0:T(128)S(1)} %add_add_fusion.3.refs_0_, f32[32,8,128]{2,1,0:T(8,128)S(1)} %all-to-all-done.1.refs_1_, f32[512,384]{1,0:T(8,128)S(1)} %convert_element_type.29.refs_2_, ...), custom_call_target="tpu_custom_call", output_to_operand_aliasing={{0}: (4, {}), {1}: (5, {})} | custom-call | tf_op jit(solution)/shard_map/update_block/pallas_call | solution.py:150
  170.2 1.9 %update_block.13 = (f32[1,2048,768]{2,1,0:T(8,128)}, bf16[1,2048,768]{2,1,0:T(8,128)(2,1)}) custom-call(s32[3]{0:T(128)S(1)} %add_add_fusion.2.refs_0_, f32[32,8,128]{2,1,0:T(8,128)S(1)} %all-to-all-done.1.refs_1_, f32[512,384]{1,0:T(8,128)S(1)} %convert_element_type.28.refs_2_, ...), custom_call_target="tpu_custom_call", output_to_operand_aliasing={{0}: (4, {}), {1}: (5, {})} | custom-call | tf_op jit(solution)/shard_map/update_block/pallas_call | solution.py:150
  172.1 1.0 convert_element_type.27.refs_2_
  173.2 1.0 convert_element_type.26.refs_2_
  174.2 1.9 %update_block.14 = (f32[1,2048,768]{2,1,0:T(8,128)}, bf16[1,2048,768]{2,1,0:T(8,128)(2,1)}) custom-call(s32[3]{0:T(128)S(1)} %add_add_fusion.1.refs_0_, f32[32,8,128]{2,1,0:T(8,128)S(1)} %all-to-all-done.1.refs_1_, f32[512,384]{1,0:T(8,128)S(1)} %convert_element_type.27.refs_2_, ...), custom_call_target="tpu_custom_call", output_to_operand_aliasing={{0}: (4, {}), {1}: (5, {})} | custom-call | tf_op jit(solution)/shard_map/update_block/pallas_call | solution.py:150
  176.1 1.9 %update_block.15 = (f32[1,2048,768]{2,1,0:T(8,128)}, bf16[1,2048,768]{2,1,0:T(8,128)(2,1)}) custom-call(s32[3]{0:T(128)S(1)} %add_add_fusion.refs_0_, f32[32,8,128]{2,1,0:T(8,128)S(1)} %all-to-all-done.1.refs_1_, f32[512,384]{1,0:T(8,128)S(1)} %convert_element_type.26.refs_2_, ...), custom_call_target="tpu_custom_call", output_to_operand_aliasing={{0}: (4, {}), {1}: (5, {})} | custom-call | tf_op jit(solution)/shard_map/update_block/pallas_call | solution.py:150
  (65 shorter events, 2.7 us)
Async XLA Ops:
  0.8 8.2 %copy-start.9 = (s32[1,1,4,96]{3,2,1,0:T(4,128)S(1)}, s32[1,1,4,96]{3,2,1,0:T(4,128)}, u32[]{:S(2)}) copy-start(s32[1,1,4,96]{3,2,1,0:T(4,128)} %refs_1_.3) | copy-start | bytes 4612
  0.8 8.2 %copy-start.10 = (f32[1,1,4,96]{3,2,1,0:T(4,128)S(1)}, f32[1,1,4,96]{3,2,1,0:T(4,128)}, u32[]{:S(2)}) copy-start(f32[1,1,4,96]{3,2,1,0:T(4,128)} %refs_3_.9) | copy-start | bytes 4612
  0.8 8.2 %copy-start.11 = (s32[1,1,4]{2,1,0:T(1,128)S(1)}, s32[1,1,4]{2,1,0:T(1,128)}, u32[]{:S(2)}) copy-start(s32[1,1,4]{2,1,0:T(1,128)} %refs_2_.1) | copy-start | bytes 52
  4.4 72.2 %copy-start.2 = (bf16[1,1,2048,768]{3,2,1,0:T(8,128)(2,1)S(1)}, bf16[1,1,2048,768]{3,2,1,0:T(8,128)(2,1)}, u32[]{:S(2)}) copy-start(bf16[1,1,2048,768]{3,2,1,0:T(8,128)(2,1)} %refs_1_.4) | copy-start | bytes 9437188
  4.4 26.9 %collective-permute-start.3 = (bf16[1024,384]{1,0:T(8,128)(2,1)}, bf16[1024,384]{1,0:T(8,128)(2,1)}, u32[]{:S(2)}, u32[]{:S(2)}) collective-permute-start(bf16[1024,384]{1,0:T(8,128)(2,1)} %get-tuple-element.71), channel_id=1, source_target_pairs={{0,8},{8,0},{16,24},{24,16},{1,9},{9,1},{17,25},{25,17},{2,10},{10... | collective-permute-start | bytes 2359304 | tf_op jit(solution)/shard_map/ppermute | solution.py:34
  7.4 36.2 %collective-permute-start.4 = (bf16[1024,384]{1,0:T(8,128)(2,1)}, bf16[1024,384]{1,0:T(8,128)(2,1)}, u32[]{:S(2)}, u32[]{:S(2)}) collective-permute-start(bf16[1024,384]{1,0:T(8,128)(2,1)} %get-tuple-element.73), channel_id=1, source_target_pairs={{0,16},{8,24},{16,0},{24,8},{1,17},{9,25},{17,1},{25,9},{2,18},{10... | collective-permute-start | bytes 2359304 | tf_op jit(solution)/shard_map/ppermute | solution.py:34
  8.9 34.7 %collective-permute-start.5 = (bf16[1024,384]{1,0:T(8,128)(2,1)}, bf16[1024,384]{1,0:T(8,128)(2,1)}, u32[]{:S(2)}, u32[]{:S(2)}) collective-permute-start(bf16[1024,384]{1,0:T(8,128)(2,1)} %get-tuple-element.70), channel_id=1, source_target_pairs={{0,24},{8,16},{16,8},{24,0},{1,25},{9,17},{17,9},{25,1},{2,26},{10... | collective-permute-start | bytes 2359304 | tf_op jit(solution)/shard_map/ppermute | solution.py:34
  9.0 1.0 copy-start.7
  10.0 1.0 copy-start.8
  12.5 0.7 copy-start.12
  13.1 0.7 copy-start.14
  13.8 9.9 %collective-permute-start = (bf16[96,1024]{1,0:T(8,128)(2,1)S(1)}, bf16[96,1024]{1,0:T(8,128)(2,1)S(1)}, u32[]{:S(2)}, u32[]{:S(2)}) collective-permute-start(bf16[96,1024]{1,0:T(8,128)(2,1)S(1)} %get-tuple-element.37), channel_id=1, source_target_pairs={{0,2},{2,0},{4,6},{6,4},{1,3},{3,1},{5,7},{7,5},{8,10},{10,8},{12,... | collective-permute-start | bytes 589832 | tf_op jit(solution)/shard_map/ppermute | solution.py:34
  15.9 13.1 %collective-permute-start.1 = (bf16[96,1024]{1,0:T(8,128)(2,1)S(1)}, bf16[96,1024]{1,0:T(8,128)(2,1)S(1)}, u32[]{:S(2)}, u32[]{:S(2)}) collective-permute-start(bf16[96,1024]{1,0:T(8,128)(2,1)S(1)} %get-tuple-element.38), channel_id=1, source_target_pairs={{0,4},{2,6},{4,0},{6,2},{1,5},{3,7},{5,1},{7,3},{8,12},{10,14},{12... | collective-permute-start | bytes 589832 | tf_op jit(solution)/shard_map/ppermute | solution.py:34
  23.7 7.6 %collective-permute-start.2 = (bf16[96,1024]{1,0:T(8,128)(2,1)S(1)}, bf16[96,1024]{1,0:T(8,128)(2,1)S(1)}, u32[]{:S(2)}, u32[]{:S(2)}) collective-permute-start(bf16[96,1024]{1,0:T(8,128)(2,1)S(1)} %get-tuple-element.39), channel_id=1, source_target_pairs={{0,6},{2,4},{4,2},{6,0},{1,7},{3,5},{5,3},{7,1},{8,14},{10,12},{12... | collective-permute-start | bytes 589832 | tf_op jit(solution)/shard_map/ppermute | solution.py:34
  43.5 1.1 copy-start.4
  48.2 1.1 copy-start.5
  49.3 17.8 %collective-permute-start.19 = (bf16[1024,384]{1,0:T(8,128)(2,1)}, bf16[1024,384]{1,0:T(8,128)(2,1)}, u32[]{:S(2)}, u32[]{:S(2)}) collective-permute-start(bf16[1024,384]{1,0:T(8,128)(2,1)} %get-tuple-element.47), channel_id=1, source_target_pairs={{1,25},{9,17},{16,8},{24,0},{3,27},{11,19},{18,10},{26,2},{5,29},{... | collective-permute-start | bytes 2359304 | tf_op jit(solution)/shard_map/ppermute | solution.py:236
  50.6 22.2 %collective-permute-start.17 = (bf16[1024,384]{1,0:T(8,128)(2,1)}, bf16[1024,384]{1,0:T(8,128)(2,1)}, u32[]{:S(2)}, u32[]{:S(2)}) collective-permute-start(bf16[1024,384]{1,0:T(8,128)(2,1)} %get-tuple-element.47), channel_id=1, source_target_pairs={{1,17},{9,25},{16,0},{24,8},{3,19},{11,27},{18,2},{26,10},{5,21},{... | collective-permute-start | bytes 2359304 | tf_op jit(solution)/shard_map/ppermute | solution.py:236
  51.9 23.1 %collective-permute-start.6 = (bf16[384,1024]{1,0:T(8,128)(2,1)}, bf16[384,1024]{1,0:T(8,128)(2,1)}, u32[]{:S(2)}, u32[]{:S(2)}) collective-permute-start(bf16[384,1024]{1,0:T(8,128)(2,1)} %get-tuple-element.40.refs_2_), channel_id=1, source_target_pairs={{0,1},{1,0},{2,3},{3,2},{4,5},{5,4},{6,7},{7,6},{8,9},{9,8},{10,11... | collective-permute-start | bytes 2359304 | tf_op jit(solution)/shard_map/ppermute | solution.py:34
  54.2 26.0 %collective-permute-start.15 = (bf16[1024,384]{1,0:T(8,128)(2,1)}, bf16[1024,384]{1,0:T(8,128)(2,1)}, u32[]{:S(2)}, u32[]{:S(2)}) collective-permute-start(bf16[1024,384]{1,0:T(8,128)(2,1)} %get-tuple-element.47), channel_id=1, source_target_pairs={{0,8},{8,0},{17,25},{25,17},{2,10},{10,2},{19,27},{27,19},{4,12},{... | collective-permute-start | bytes 2359304 | tf_op jit(solution)/shard_map/ppermute | solution.py:236
  56.7 26.2 %collective-permute-start.14 = (bf16[1024,384]{1,0:T(8,128)(2,1)}, bf16[1024,384]{1,0:T(8,128)(2,1)}, u32[]{:S(2)}, u32[]{:S(2)}) collective-permute-start(bf16[1024,384]{1,0:T(8,128)(2,1)} %get-tuple-element.47), channel_id=1, source_target_pairs={{0,1},{8,9},{17,16},{25,24},{2,3},{10,11},{19,18},{27,26},{4,5},{1... | collective-permute-start | bytes 2359304 | tf_op jit(solution)/shard_map/ppermute | solution.py:246
  67.1 18.4 %collective-permute-start.20 = (bf16[1024,384]{1,0:T(8,128)(2,1)}, bf16[1024,384]{1,0:T(8,128)(2,1)}, u32[]{:S(2)}, u32[]{:S(2)}) collective-permute-start(bf16[1024,384]{1,0:T(8,128)(2,1)} %collective-permute-done.19), channel_id=1, source_target_pairs={{0,1},{8,9},{17,16},{25,24},{2,3},{10,11},{19,18},{27,26},{4,5},{1... | collective-permute-start | bytes 2359304 | tf_op jit(solution)/shard_map/ppermute | solution.py:246
  72.9 21.1 %collective-permute-start.18 = (bf16[1024,384]{1,0:T(8,128)(2,1)}, bf16[1024,384]{1,0:T(8,128)(2,1)}, u32[]{:S(2)}, u32[]{:S(2)}) collective-permute-start(bf16[1024,384]{1,0:T(8,128)(2,1)} %collective-permute-done.17), channel_id=1, source_target_pairs={{0,1},{8,9},{17,16},{25,24},{2,3},{10,11},{19,18},{27,26},{4,5},{1... | collective-permute-start | bytes 2359304 | tf_op jit(solution)/shard_map/ppermute | solution.py:246
  75.0 5.2 %copy-start.13 = (bf16[96,1024]{1,0:T(8,128)(2,1)S(1)}, bf16[96,1024]{1,0:T(8,128)(2,1)}, u32[]{:S(2)}) copy-start(bf16[96,1024]{1,0:T(8,128)(2,1)} %copy-done.12) | copy-start | bytes 589828
  75.0 12.2 %collective-permute-start.7 = (bf16[96,1024]{1,0:T(8,128)(2,1)}, bf16[96,1024]{1,0:T(8,128)(2,1)S(1)}, u32[]{:S(2)}, u32[]{:S(2)}) collective-permute-start(bf16[96,1024]{1,0:T(8,128)(2,1)} %copy-done.14), channel_id=1, source_target_pairs={{0,2},{2,0},{4,6},{6,4},{1,3},{3,1},{5,7},{7,5},{8,10},{10,8},{12,... | collective-permute-start | bytes 589832 | tf_op jit(solution)/shard_map/ppermute | solution.py:34
  80.3 13.2 %collective-permute-start.8 = (bf16[96,1024]{1,0:T(8,128)(2,1)S(1)}, bf16[96,1024]{1,0:T(8,128)(2,1)S(1)}, u32[]{:S(2)}, u32[]{:S(2)}) collective-permute-start(bf16[96,1024]{1,0:T(8,128)(2,1)S(1)} %copy-done.13), channel_id=1, source_target_pairs={{0,4},{2,6},{4,0},{6,2},{1,5},{3,7},{5,1},{7,3},{8,12},{10,14},{12... | collective-permute-start | bytes 589832 | tf_op jit(solution)/shard_map/ppermute | solution.py:34
  82.9 12.3 %collective-permute-start.16 = (bf16[1024,384]{1,0:T(8,128)(2,1)}, bf16[1024,384]{1,0:T(8,128)(2,1)S(1)}, u32[]{:S(2)}, u32[]{:S(2)}) collective-permute-start(bf16[1024,384]{1,0:T(8,128)(2,1)} %collective-permute-done.15), channel_id=1, source_target_pairs={{0,1},{8,9},{17,16},{25,24},{2,3},{10,11},{19,18},{27,26},{4,5},{1... | collective-permute-start | bytes 2359304 | tf_op jit(solution)/shard_map/ppermute | solution.py:246
  85.5 11.0 %copy-start.3 = (bf16[1,1,768,2048]{3,2,1,0:T(8,128)(2,1)S(1)}, bf16[1,1,768,2048]{3,2,1,0:T(8,128)(2,1)}, u32[]{:S(2)}) copy-start(bf16[1,1,768,2048]{3,2,1,0:T(8,128)(2,1)} %refs_1_.5) | copy-start | bytes 9437188
  85.5 7.9 %collective-permute-start.9 = (bf16[96,1024]{1,0:T(8,128)(2,1)S(1)}, bf16[96,1024]{1,0:T(8,128)(2,1)S(1)}, u32[]{:S(2)}, u32[]{:S(2)}) collective-permute-start(bf16[96,1024]{1,0:T(8,128)(2,1)S(1)} %get-tuple-element.46), channel_id=1, source_target_pairs={{0,6},{2,4},{4,2},{6,0},{1,7},{3,5},{5,3},{7,1},{8,14},{10,12},{12... | collective-permute-start | bytes 589832 | tf_op jit(solution)/shard_map/ppermute | solution.py:34
  87.2 9.3 %collective-permute-start.10 = (bf16[96,1024]{1,0:T(8,128)(2,1)S(1)}, bf16[96,1024]{1,0:T(8,128)(2,1)S(1)}, u32[]{:S(2)}, u32[]{:S(2)}) collective-permute-start(bf16[96,1024]{1,0:T(8,128)(2,1)S(1)} %get-tuple-element.43.refs_4_), channel_id=1, source_target_pairs={{0,1},{1,0},{2,3},{3,2},{4,5},{5,4},{6,7},{7,6},{8,9},{9,8},{10,11... | collective-permute-start | bytes 589832 | tf_op jit(solution)/shard_map/ppermute | solution.py:34
  93.4 3.1 %collective-permute-start.11 = (bf16[96,1024]{1,0:T(8,128)(2,1)S(1)}, bf16[96,1024]{1,0:T(8,128)(2,1)S(1)}, u32[]{:S(2)}, u32[]{:S(2)}) collective-permute-start(bf16[96,1024]{1,0:T(8,128)(2,1)S(1)} %collective-permute-done.7.refs_5_), channel_id=1, source_target_pairs={{0,1},{1,0},{2,3},{3,2},{4,5},{5,4},{6,7},{7,6},{8,9},{9,8},{10,11... | collective-permute-start | bytes 589832 | tf_op jit(solution)/shard_map/ppermute | solution.py:34
  93.4 3.1 %collective-permute-start.12 = (bf16[96,1024]{1,0:T(8,128)(2,1)S(1)}, bf16[96,1024]{1,0:T(8,128)(2,1)S(1)}, u32[]{:S(2)}, u32[]{:S(2)}) collective-permute-start(bf16[96,1024]{1,0:T(8,128)(2,1)S(1)} %collective-permute-done.8.refs_6_), channel_id=1, source_target_pairs={{0,1},{1,0},{2,3},{3,2},{4,5},{5,4},{6,7},{7,6},{8,9},{9,8},{10,11... | collective-permute-start | bytes 589832 | tf_op jit(solution)/shard_map/ppermute | solution.py:34
  93.9 2.6 %collective-permute-start.13 = (bf16[96,1024]{1,0:T(8,128)(2,1)S(1)}, bf16[96,1024]{1,0:T(8,128)(2,1)S(1)}, u32[]{:S(2)}, u32[]{:S(2)}) collective-permute-start(bf16[96,1024]{1,0:T(8,128)(2,1)S(1)} %collective-permute-done.9.refs_7_), channel_id=1, source_target_pairs={{0,1},{1,0},{2,3},{3,2},{4,5},{5,4},{6,7},{7,6},{8,9},{9,8},{10,11... | collective-permute-start | bytes 589832 | tf_op jit(solution)/shard_map/ppermute | solution.py:34
  96.5 22.1 %copy-start.6 = (f32[1024,384]{1,0:T(8,128)S(1)}, f32[1024,384]{1,0:T(8,128)}, u32[]{:S(2)}) copy-start(f32[1024,384]{1,0:T(8,128)} %copy-done.5) | copy-start | bytes 4718596
  99.6 19.1 %collective-permute-start.21 = (bf16[384,384]{1,0:T(8,128)(2,1)S(1)}, bf16[384,384]{1,0:T(8,128)(2,1)S(1)}, u32[]{:S(2)}, u32[]{:S(2)}) collective-permute-start(bf16[384,384]{1,0:T(8,128)(2,1)S(1)} %get-tuple-element.51), channel_id=1, source_target_pairs={{0,8},{8,0},{16,24},{24,16},{1,9},{9,1},{17,25},{25,17},{2,10},{10... | collective-permute-start | bytes 884744 | tf_op jit(solution)/shard_map/ppermute | solution.py:34
  101.0 17.6 %collective-permute-start.22 = (bf16[384,384]{1,0:T(8,128)(2,1)S(1)}, bf16[384,384]{1,0:T(8,128)(2,1)S(1)}, u32[]{:S(2)}, u32[]{:S(2)}) collective-permute-start(bf16[384,384]{1,0:T(8,128)(2,1)S(1)} %get-tuple-element.50.refs_7_), channel_id=1, source_target_pairs={{0,16},{8,24},{16,0},{24,8},{1,17},{9,25},{17,1},{25,9},{2,18},{10... | collective-permute-start | bytes 884744 | tf_op jit(solution)/shard_map/ppermute | solution.py:34
  102.5 16.1 %collective-permute-start.23 = (bf16[384,384]{1,0:T(8,128)(2,1)S(1)}, bf16[384,384]{1,0:T(8,128)(2,1)S(1)}, u32[]{:S(2)}, u32[]{:S(2)}) collective-permute-start(bf16[384,384]{1,0:T(8,128)(2,1)S(1)} %get-tuple-element.51), channel_id=1, source_target_pairs={{0,24},{8,16},{16,8},{24,0},{1,25},{9,17},{17,9},{25,1},{2,26},{10... | collective-permute-start | bytes 884744 | tf_op jit(solution)/shard_map/ppermute | solution.py:34
  122.8 12.0 %collective-permute-start.26 = (f16[512,384]{1,0:T(8,128)(2,1)S(1)}, f16[512,384]{1,0:T(8,128)(2,1)S(1)}, u32[]{:S(2)}, u32[]{:S(2)}) collective-permute-start(f16[512,384]{1,0:T(8,128)(2,1)S(1)} %get-tuple-element.55), channel_id=1, source_target_pairs={{0,8},{8,0},{16,24},{24,16},{1,9},{9,1},{17,25},{25,17},{2,10},{10... | collective-permute-start | bytes 1179656 | tf_op jit(solution)/shard_map/ppermute | solution.py:34
  123.8 12.5 %collective-permute-start.24 = (f16[512,384]{1,0:T(8,128)(2,1)S(1)}, f16[512,384]{1,0:T(8,128)(2,1)S(1)}, u32[]{:S(2)}, u32[]{:S(2)}) collective-permute-start(f16[512,384]{1,0:T(8,128)(2,1)S(1)} %get-tuple-element.54), channel_id=1, source_target_pairs={{0,16},{8,24},{16,0},{24,8},{1,17},{9,25},{17,1},{25,9},{2,18},{10... | collective-permute-start | bytes 1179656 | tf_op jit(solution)/shard_map/ppermute | solution.py:34
  125.3 37.1 %collective-permute-start.29 = (f16[512,384]{1,0:T(8,128)(2,1)S(1)}, f16[512,384]{1,0:T(8,128)(2,1)}, u32[]{:S(2)}, u32[]{:S(2)}) collective-permute-start(f16[512,384]{1,0:T(8,128)(2,1)S(1)} %get-tuple-element.54), channel_id=1, source_target_pairs={{0,8},{8,0},{16,24},{24,16},{1,9},{9,1},{17,25},{25,17},{2,10},{10... | collective-permute-start | bytes 1179656 | tf_op jit(solution)/shard_map/ppermute | solution.py:34
  126.6 37.0 %collective-permute-start.28 = (f16[512,384]{1,0:T(8,128)(2,1)S(1)}, f16[512,384]{1,0:T(8,128)(2,1)}, u32[]{:S(2)}, u32[]{:S(2)}) collective-permute-start(f16[512,384]{1,0:T(8,128)(2,1)S(1)} %get-tuple-element.55), channel_id=1, source_target_pairs={{0,16},{8,24},{16,0},{24,8},{1,17},{9,25},{17,1},{25,9},{2,18},{10... | collective-permute-start | bytes 1179656 | tf_op jit(solution)/shard_map/ppermute | solution.py:34
  134.8 37.3 %collective-permute-start.27 = (f16[512,384]{1,0:T(8,128)(2,1)S(1)}, f16[512,384]{1,0:T(8,128)(2,1)}, u32[]{:S(2)}, u32[]{:S(2)}) collective-permute-start(f16[512,384]{1,0:T(8,128)(2,1)S(1)} %collective-permute-done.26), channel_id=1, source_target_pairs={{0,16},{8,24},{16,0},{24,8},{1,17},{9,25},{17,1},{25,9},{2,18},{10... | collective-permute-start | bytes 1179656 | tf_op jit(solution)/shard_map/ppermute | solution.py:34
  136.3 36.8 %collective-permute-start.25 = (f16[512,384]{1,0:T(8,128)(2,1)S(1)}, f16[512,384]{1,0:T(8,128)(2,1)}, u32[]{:S(2)}, u32[]{:S(2)}) collective-permute-start(f16[512,384]{1,0:T(8,128)(2,1)S(1)} %collective-permute-done.24), channel_id=1, source_target_pairs={{0,8},{8,0},{16,24},{24,16},{1,9},{9,1},{17,25},{25,17},{2,10},{10... | collective-permute-start | bytes 1179656 | tf_op jit(solution)/shard_map/ppermute | solution.py:34
  137.2 15.9 %all-to-all-start.1 = ((f32[32,8,128]{2,1,0:T(8,128)}), f32[32,8,128]{2,1,0:T(8,128)S(1)}, u32[]{:S(2)}, u32[]{:S(2)}) async-start(f32[32,8,128]{2,1,0:T(8,128)} %get-tuple-element.52), calls=%async_computation.1 | async-start | bytes 262144 | tf_op jit(solution)/shard_map/all_to_all | solution.py:301
  153.0 2.8 %copy-start = (f32[1,2048,768]{2,1,0:T(8,128)S(1)}, f32[1,2048,768]{2,1,0:T(8,128)}, u32[]{:S(2)}) copy-start(f32[1,2048,768]{2,1,0:T(8,128)} %refs_3_.17) | copy-start | bytes 18874372
  157.7 2.8 %copy-start.1 = (f32[1,2048,768]{2,1,0:T(8,128)S(1)}, f32[1,2048,768]{2,1,0:T(8,128)}, u32[]{:S(2)}) copy-start(f32[1,2048,768]{2,1,0:T(8,128)} %refs_3_.17) | copy-start | bytes 18874372

commit v3 on v2

v3 whole, which is shorter than its diff:
```python
import math

import jax
import jax.numpy as jnp
from jax import lax
from jax.experimental import pallas as pl
from jax.experimental.pallas import tpu as pltpu
from jax.sharding import PartitionSpec as P

F32 = jnp.float32
BF16 = jnp.bfloat16
WIRE = jnp.float16
AXES = ("island", "expert", "tensor")

VMEM = pl.BlockSpec(memory_space=pltpu.VMEM)
SMEM = pl.BlockSpec(memory_space=pltpu.SMEM)
ANY = pl.BlockSpec(memory_space=pl.ANY)


def params(mib):
    return pltpu.CompilerParams(vmem_limit_bytes=mib << 20)


def partner(at, step, size):
    return at ^ step if size & (size - 1) == 0 else (at + step) % size


def origin(at, step, size):
    return at ^ step if size & (size - 1) == 0 else (at - step) % size


def swap(value, axis, step):
    size = lax.axis_size(axis)
    return lax.ppermute(value, axis, [(at, partner(at, step, size)) for at in range(size)])


def dot(a, b, contract):
    return lax.dot_general(a, b, (contract, ((), ())), preferred_element_type=F32)


def pick_kernel(experts, islands, spot, table, count, weight, tokens, grads, drift, *refs):
    outs, blocks, sems = refs[:experts], refs[experts : experts + islands], refs[-1]
    across = spot[4]
    block_rows, block_columns = blocks[0].shape
    copies = []
    for d in range(islands):
        at = partner(spot[3], d, islands)
        top = pl.multiple_of(lax.div(at, across) * block_rows, block_rows)
        left = pl.multiple_of(lax.rem(at, across) * block_columns, block_columns)
        source = drift.at[0, 0, pl.ds(top, block_rows), pl.ds(left, block_columns)]
        copies.append(pltpu.make_async_copy(source, blocks[d], sems.at[d]))
        copies[-1].start()

    slots = table.shape[-1]
    rows = lax.broadcasted_iota(jnp.int32, (slots, slots), 0)
    lanes = lax.broadcasted_iota(jnp.int32, (slots, slots), 1)

    def column(row):
        return jnp.sum(jnp.where(rows == lanes, row, 0), axis=1, keepdims=True)

    for d in range(experts):
        to = partner(spot[0], d, experts)
        live = lax.broadcasted_iota(jnp.int32, (slots, 1), 0) < count[0, 0, to]
        token = column(table[0, 0, pl.ds(to, 1), :].astype(F32)).astype(jnp.int32)
        chance = column(weight[0, 0, pl.ds(to, 1), :])
        ids = lax.broadcasted_iota(jnp.int32, (slots, tokens.shape[1]), 1)
        picks = jnp.where((ids == token) & live, 1.0, 0.0).astype(BF16)
        outs[d][:slots, :] = dot(picks, tokens[0], ((1,), (0,))).astype(BF16)
        picked = dot(picks, grads[0], ((1,), (0,)))
        outs[d][slots:, :] = (chance * picked).astype(BF16)
    for copy in copies:
        copy.wait()


def join_kernel(pieces, blocks, *refs):
    arrived, drifts = refs[:pieces], refs[pieces : pieces + blocks]
    joined, turned, drift_sum = refs[pieces + blocks :]
    slots = arrived[0].shape[0] // 2
    for n, piece in enumerate(arrived):
        joined[n * slots : (n + 1) * slots, :] = piece[:slots, :]
        joined[(pieces + n) * slots : (pieces + n + 1) * slots, :] = piece[slots:, :]
    turned[...] = joined[: pieces * slots, :].T
    added = drifts[0][...].astype(F32)
    for other in drifts[1:]:
        added = added + other[...].astype(F32)
    drift_sum[...] = added


def hidden_kernel(parts, across, spot, gate, down, *refs):
    joined = refs[:parts]
    outs, norms = refs[parts:-1], refs[-1]
    rows, half = joined[0].shape[0] // 2, joined[0].shape[1]
    columns = outs[0].shape[1]
    starts = [pl.multiple_of(origin(spot[1], t, parts) * half, half) for t in range(parts)]
    hidden_gram = 0.0
    for r in range(across):
        first = pl.multiple_of(partner(spot[2], r, across) * columns, columns)
        value = 0.0
        back = 0.0
        for t in range(parts):
            block = gate[0, 0, pl.ds(starts[t], half), pl.ds(first, columns)]
            value = value + dot(joined[t][:rows, :], block, ((1,), (0,)))
            block = down[0, 0, pl.ds(first, columns), pl.ds(starts[t], half)]
            back = back + dot(joined[t][rows:, :], block, ((1,), (1,)))
        rounded = (back * (value / (1.0 + jnp.exp(-value)))).astype(BF16)
        outs[r][...] = rounded
        hidden_gram = hidden_gram + dot(rounded, rounded, ((1,), (1,)))
    input_gram = 0.0
    for t in range(parts):
        inputs = joined[t][:rows, :]
        input_gram = input_gram + dot(inputs, inputs, ((1,), (1,)))
    norms[...] = jnp.full(norms.shape, jnp.sum(hidden_gram * input_gram), F32)


def average_kernel(islands, entries, spot, norms, drift_sum, *refs):
    hiddens = refs[4 : 4 + islands]
    scaled, notes, inputs, total, sems = refs[-5:]

    def fetch(own, rest):
        pltpu.make_async_copy(own, inputs.at[0], sems.at[0]).start()
        for d in range(1, islands):
            pltpu.make_async_copy(rest.at[d - 1], inputs.at[d], sems.at[d]).start()

    pl.when(spot[5] == 1)(lambda: fetch(refs[0], refs[2]))
    pl.when(spot[5] != 1)(lambda: fetch(refs[1], refs[3]))

    group = norms.shape[0] // islands
    average = drift_sum[...]
    for d in range(islands):
        at = origin(spot[3], d, islands)
        square = jnp.sum(norms[pl.ds(at * group, group)], axis=0)[:1, :1]
        scale = jnp.minimum(1.0, math.sqrt(entries) / jnp.sqrt(square + 1e-06))
        pltpu.make_async_copy(refs[0], inputs.at[d], sems.at[d]).wait()
        average = average + scale * dot(inputs[d], hiddens[d][...], ((1,), (0,)))
    average = average / islands
    total[...] = average
    unit = jnp.maximum(jnp.max(jnp.abs(average)), 1e-30) / 32768
    scaled[...] = total[...] * (1 / unit)
    sublane = lax.broadcasted_iota(jnp.int32, notes.shape, 1)
    notes[...] = jnp.where(sublane == 0, jnp.sum(average * average), unit)


def copy_all(sems, pairs):
    copies = [pltpu.make_async_copy(*pair, sems.at[n]) for n, pair in enumerate(pairs)]
    for copy in copies:
        copy.start()
    for copy in copies:
        copy.wait()


def hand_kernel(count, norms, *refs):
    passed, joined, sems = refs[count:]
    pairs = [(refs[n], joined.at[n]) for n in range(count)] + [(norms, passed)]
    copy_all(sems, pairs)


def pass_kernel(count, notes, *refs):
    copy_all(refs[-1], [(refs[n], refs[count + n]) for n in range(count)])


def update_kernel(entries, place, notes, block, momentum, *rest):
    new_momentum, outer_step = rest[-2:]
    square = jnp.sum(notes[...], axis=0)[:1, :1]
    clip = jnp.minimum(1.0, 0.25 * math.sqrt(entries) / jnp.sqrt(square + 1e-06))
    unit = notes[pl.ds(place[2], 1)][0, 1:2, :1]
    clipped = (clip * unit) * block[...]
    moved = 0.9 * momentum[0] + clipped
    new_momentum[0] = moved
    outer_step[0] = (0.7 * (clipped + 0.9 * moved)).astype(BF16)


def update_block(entries, place, notes, block, momentum, outs):
    rows, columns = block.shape
    steps = 2
    tile = rows // steps
    here = pl.BlockSpec((tile, columns), lambda r, place: (r, 0))
    there = pl.BlockSpec(
        (1, tile, columns), lambda r, place: (0, place[0] * steps + r, place[1])
    )
    whole = pl.BlockSpec(notes.shape, lambda r, place: (0, 0, 0))
    return pl.pallas_call(
        lambda *refs: update_kernel(entries, *refs),
        grid_spec=pltpu.PrefetchScalarGridSpec(
            num_scalar_prefetch=1,
            grid=(steps,),
            in_specs=[whole, here, there] + [ANY] * len(outs),
            out_specs=[there, there],
        ),
        out_shape=[
            jax.ShapeDtypeStruct(momentum.shape, F32),
            jax.ShapeDtypeStruct(momentum.shape, BF16),
        ],
        input_output_aliases={4 + n: n for n in range(len(outs))},
        compiler_params=params(32),
        name="update_block",
    )(place, notes, block, momentum, *outs)


def body(
    tokens,
    token_grads,
    slot_token,
    slot_count,
    slot_prob,
    gate_weight,
    down_weight,
    drift,
    momentum,
):
    islands, experts, parts = (lax.axis_size(a) for a in AXES)
    island, expert, part = (lax.axis_index(a) for a in AXES)
    devices = islands * experts * parts
    features, hidden = gate_weight.shape[2:]
    half = features // parts
    across = islands // parts
    columns = hidden // across
    entries = features * hidden * experts * parts
    slots = slot_token.shape[3]
    routed_rows = experts * slots
    holder = island // across
    spot = jnp.stack(
        [expert, part, island % across, island, jnp.int32(across), (part == holder).astype(jnp.int32)]
    ).astype(jnp.int32)
    drift_block = jax.ShapeDtypeStruct((half, columns), BF16)

    picked = pl.pallas_call(
        lambda *refs: pick_kernel(experts, islands, *refs),
        in_specs=[SMEM, VMEM, SMEM, VMEM, VMEM, VMEM, ANY],
        out_specs=[VMEM] * experts + [ANY] * islands,
        out_shape=[jax.ShapeDtypeStruct((2 * slots, half), BF16)] * experts
        + [drift_block] * islands,
        scratch_shapes=[pltpu.SemaphoreType.DMA((islands,))],
        compiler_params=params(32),
        name="pick_slots",
    )(spot, slot_token, slot_count, slot_prob, tokens, token_grads, drift)
    arrived = [picked[0]] + [swap(picked[d], "expert", d) for d in range(experts - 1, 0, -1)]
    blocks = picked[experts:]
    drift_in = [blocks[0]] + [swap(blocks[d], "island", d) for d in range(1, islands)]
    joined, turned, drift_sum = pl.pallas_call(
        lambda *refs: join_kernel(experts, islands, *refs),
        in_specs=[VMEM] * (experts + islands),
        out_specs=[VMEM] * 3,
        out_shape=[
            jax.ShapeDtypeStruct((2 * routed_rows, half), BF16),
            jax.ShapeDtypeStruct((half, routed_rows), BF16),
            jax.ShapeDtypeStruct((half, columns), F32),
        ],
        compiler_params=params(40),
        name="join_slots",
    )(*arrived, *drift_in)

    joined_all = [joined] + [swap(joined, "tensor", t) for t in range(1, parts)]

    def send_features(d):
        pairs = []
        for at in range(islands):
            to = partner(at, d, islands)
            pairs.append((at * parts + to // across, to * parts + to // across))
        return lax.ppermute(turned, ("island", "tensor"), pairs)

    def spread(value):
        result = value
        for t in range(1, parts):
            pairs = []
            for at in range(islands):
                keep = at // across
                pairs.append((at * parts + keep, at * parts + partner(keep, t, parts)))
            moved = lax.ppermute(value, ("island", "tensor"), pairs)
            result = moved if t == 1 else result + moved
        return result

    features_in = [send_features(d) for d in range(1, islands)]
    turned_moved = spread(turned)

    hidden_piece = jax.ShapeDtypeStruct((routed_rows, columns), BF16)
    *hidden_out, norms = pl.pallas_call(
        lambda *refs: hidden_kernel(parts, across, *refs),
        in_specs=[SMEM] + [VMEM] * (2 + parts),
        out_specs=[VMEM] * (across + 1),
        out_shape=[hidden_piece] * across + [jax.ShapeDtypeStruct((devices, 8, 128), F32)],
        compiler_params=params(48),
        name="hidden_grads",
    )(spot, gate_weight, down_weight, *joined_all)

    def hidden_for(d):
        at = partner(island, d, islands) % across
        if islands & (islands - 1) == 0:
            return hidden_out[d % across]
        return lax.select_n((at - island) % across, *hidden_out)

    hidden_of = [hidden_out[0]] + [
        swap(hidden_for(d), "island", d) for d in range(1, islands)
    ]
    norms, features_in = pl.pallas_call(
        lambda *refs: hand_kernel(islands - 1, *refs),
        in_specs=[ANY] * islands,
        out_specs=[ANY] * 2,
        out_shape=[
            jax.ShapeDtypeStruct(norms.shape, F32),
            jax.ShapeDtypeStruct((islands - 1, half, routed_rows), BF16),
        ],
        scratch_shapes=[pltpu.SemaphoreType.DMA((islands,))],
        compiler_params=params(16),
        name="hand_features",
    )(norms, *features_in)
    features_moved = spread(features_in)
    norms = lax.all_to_all(norms, AXES, split_axis=0, concat_axis=0, tiled=True)

    scaled, notes = pl.pallas_call(
        lambda *refs: average_kernel(islands, entries, *refs),
        in_specs=[SMEM, VMEM, VMEM] + [ANY] * 4 + [VMEM] * islands,
        out_specs=[VMEM] * 2,
        out_shape=[
            jax.ShapeDtypeStruct((half, columns), F32),
            jax.ShapeDtypeStruct((devices, 8, 128), F32),
        ],
        scratch_shapes=[
            pltpu.VMEM((islands, half, routed_rows), BF16),
            pltpu.VMEM((half, columns), F32),
            pltpu.SemaphoreType.DMA((islands,)),
        ],
        compiler_params=params(48),
        name="average_block",
    )(spot, norms, drift_sum, turned, turned_moved, features_in, features_moved, *hidden_of)
    notes = lax.all_to_all(notes, AXES, split_axis=0, concat_axis=0, tiled=True)

    rounded = lax.reduce_precision(scaled, 5, 10)
    own = [rounded[: half // 2], rounded[half // 2 :]]
    sent = [h.astype(WIRE) for h in own]
    if islands == 4:
        later = pl.pallas_call(
            lambda *refs: pass_kernel(2, *refs),
            in_specs=[ANY] * 3,
            out_specs=[ANY] * 2,
            out_shape=[jax.ShapeDtypeStruct(h.shape, F32) for h in own],
            scratch_shapes=[pltpu.SemaphoreType.DMA((2,))],
            compiler_params=params(16),
            name="pass_halves",
        )(notes, *own)
        later = [h.astype(WIRE) for h in later]
        beside = swap(sent[0], "island", 1)
        below = swap(sent[1], "island", 2)
        halves = [
            [own[0], beside, swap(later[0], "island", 2), swap(beside, "island", 2)],
            [own[1], swap(later[1], "island", 1), below, swap(below, "island", 1)],
        ]
    else:
        halves = [[o] + [swap(h, "island", d) for d in range(1, islands)] for o, h in zip(own, sent)]

    outs = []
    for d in range(islands):
        at = origin(island, d, islands)
        source = (at * experts + expert) * parts + part
        for n in range(2):
            place = jnp.stack([(at // across) * 2 + n, at % across, source]).astype(jnp.int32)
            block = halves[n][d].astype(F32)
            outs = update_block(entries, place, notes, block, momentum, outs)
    return tuple(outs)


def solution(mesh):
    return jax.shard_map(
        body,
        mesh=mesh,
        in_specs=(
            P("island", "expert", "tensor"),
            P("island", "expert", "tensor"),
            P("island", "expert", None, None),
            P("island", "expert", None),
            P("island", "expert", None, None),
            P("island", "expert", None, "tensor"),
            P("island", "expert", "tensor", None),
            P("island", "expert", None, "tensor"),
            P("expert", None, "tensor"),
        ),
        out_specs=(P("expert", None, "tensor"), P("expert", None, "tensor")),
        check_vma=False,
    )
```

time: 180 us -> 164 us (0.911)
  blocking collectives: 15.5 us -> 0 us
  waiting for transfers between devices: 56.6 us -> 51.1 us
  starting transfers between devices: 49 us -> 53 us
  Pallas kernels: 30.4 us -> 32.3 us
    all_to_all x1 -> x0, blocking collectives: 15.5 us -> none  [body(): norms = lax.all_to_all(norms, AXES, split_axis=0, concat_axis=0, tiled=True)]
    ppermute x23 -> x16, waiting for transfers between devices: 35.9 us -> 21.7 us  [swap(): lax.ppermute(value, axis, [(at, partner(at, step, size)) for at in range(...]
    all_to_all x0 -> x1, waiting for transfers between devices: none -> 9.89 us  [body(): norms = lax.all_to_all(norms, AXES, split_axis=0, concat_axis=0, tiled=True)]
    ppermute x23 -> x16, starting transfers between devices: 29.5 us -> 36.6 us  [swap(): lax.ppermute(value, axis, [(at, partner(at, step, size)) for at in range(...]
    select_n x4 -> x0, other arithmetic: 5.09 us -> none  [spread(): result = jnp.where(part == partner(holder, t, parts), moved, result)]
    unnamed x30, local copies, waits for them, and re-layouts: 11.3 us -> 16.4 us
    all_to_all x1, starting transfers between devices: 6.55 us -> 2.84 us  [body(): notes = lax.all_to_all(notes, AXES, split_axis=0, concat_axis=0, tiled=True)]
    dynamic_slice x1 -> x0, local copies, waits for them, and re-layouts: 3.59 us -> none  [block_of(): lax.dynamic_slice(drift[0, 0], (at // across * half, at % across * column...]
  transfers between devices with their start and end apart: 31 -> 23, of which waited for: 9 -> 7; matrix products, arithmetic and copies ran while one was open for 5% -> 4% of each run, Pallas kernels for 9% -> 12%
where the time goes in v3:
time: 164 us; the launch traced here: 163 us
  starting transfers between devices  53 us (32%)
  waiting for transfers between devices  51.1 us (31%)
  Pallas kernels  32.3 us (20%)
  local copies, waits for them, and re-layouts  16.5 us (10%)
  other arithmetic  9.38 us (6%)
    ppermute x16, starting transfers between devices, swap(): lax.ppermute(value, axis, [(at, partner(at, step, size)) for at in range(...  36.6 us
    ppermute x16, waiting for transfers between devices, swap(): lax.ppermute(value, axis, [(at, partner(at, step, size)) for at in range(...  21.7 us
    unnamed x30, local copies, waits for them, and re-layouts  16.4 us
    pallas_call x8, Pallas kernels, update_block(): pl.pallas_call(lambda *refs: update_kernel(entries, *refs), grid_spec=plt...  15 us
    ppermute x3, waiting for transfers between devices, send_features(): return lax.ppermute(turned, ('island', 'tensor'), pairs)  11.7 us
    all_to_all x1, waiting for transfers between devices, body(): norms = lax.all_to_all(norms, AXES, split_axis=0, concat_axis=0, tiled=True)  9.89 us
    pallas_call x1, Pallas kernels, body(): pl.pallas_call(lambda *refs: hidden_kernel(parts, across, *refs), in_spec...  8 us
    all_to_all x1, waiting for transfers between devices, body(): notes = lax.all_to_all(notes, AXES, split_axis=0, concat_axis=0, tiled=True)  7.76 us
  transfers between devices with their start and end apart: 23, of which 7 were waited for; matrix products, arithmetic and copies ran while one was open for 4% of the time, Pallas kernels for 12%

profile of v3, /device:TPU:0, one launch (start us, length us, event | category | flops | bytes accessed | tf_op | source)
XLA Modules:
  0.0 163.1 jit_solution(11093787210442900274)
XLA Ops:
  0.7 0.1 stack.109.refs_0_
  0.7 1.9 %copy-done.4 = bf16[1,1,2048,768]{3,2,1,0:T(8,128)(2,1)S(1)} copy-done((bf16[1,1,2048,768]{3,2,1,0:T(8,128)(2,1)S(1)}, bf16[1,1,2048,768]{3,2,1,0:T(8,128)(2,1)}, u32[]{:S(2)}) %copy-start.4) | copy-done | bytes 3145752
  2.6 1.0 copy-done.8
  3.7 1.0 copy-done.9
  4.7 0.7 copy-done.10
  5.4 0.7 copy-done.11
  6.1 0.7 copy-done.12
  6.7 1.8 %pick_slots.1 = (bf16[192,1024]{1,0:T(8,128)(2,1)S(1)}, bf16[192,1024]{1,0:T(8,128)(2,1)S(1)}, bf16[192,1024]{1,0:T(8,128)(2,1)S(1)}, bf16[192,1024]{1,0:T(8,128...) custom-call(s32[6]{0:T(128)S(1)} %stack.109.refs_0_, ...), custom_call_target="tpu_custom_call" | custom-call | tf_op jit(solution)/shard_map/pick_slots/pallas_call | solution.py:226
  8.6 5.1 %collective-permute-start = (bf16[192,1024]{1,0:T(8,128)(2,1)S(1)}, bf16[192,1024]{1,0:T(8,128)(2,1)S(1)}, u32[]{:S(2)}, u32[]{:S(2)}) collective-permute-start(bf16[192,1024]{1,0:T(8,128)(2,1)S(1)} %get-tuple-element.37), channel_id=1, source_target_pairs={{0,6},{2,4},{4,2},{6,0},{1,7},{3,5},{5,3},{7,1},{8,14},{10,12},{12... | collective-permute-start | bytes 1179656 | tf_op jit(solution)/shard_map/ppermute | solution.py:34
  13.7 1.5 collective-permute-start.3
  15.2 1.5 collective-permute-start.4
  16.7 0.5 collective-permute-start.5
  17.2 6.5 %collective-permute-done.refs_1_ = bf16[192,1024]{1,0:T(8,128)(2,1)S(1)} collective-permute-done((bf16[192,1024]{1,0:T(8,128)(2,1)S(1)}, bf16[192,1024]{1,0:T(8,128)(2,1)S(1)}, u32[]{:S(2)}, u32[]{:S(2)}) %collective-permute-start) | collective-permute-done | bytes 393248 | tf_op jit(solution)/shard_map/ppermute | solution.py:34
  23.7 16.6 %collective-permute-start.2 = (bf16[192,1024]{1,0:T(8,128)(2,1)S(1)}, bf16[192,1024]{1,0:T(8,128)(2,1)S(1)}, u32[]{:S(2)}, u32[]{:S(2)}) collective-permute-start(bf16[192,1024]{1,0:T(8,128)(2,1)S(1)} %get-tuple-element.39), channel_id=1, source_target_pairs={{0,2},{2,0},{4,6},{6,4},{1,3},{3,1},{5,7},{7,5},{8,10},{10,8},{12,... | collective-permute-start | bytes 1179656 | tf_op jit(solution)/shard_map/ppermute | solution.py:34
  40.3 7.0 %collective-permute-done.1.refs_2_ = bf16[192,1024]{1,0:T(8,128)(2,1)S(1)} collective-permute-done((bf16[192,1024]{1,0:T(8,128)(2,1)S(1)}, bf16[192,1024]{1,0:T(8,128)(2,1)S(1)}, u32[]{:S(2)}, u32[]{:S(2)}) %collective-permute-start.1) | collective-permute-done | bytes 393248 | tf_op jit(solution)/shard_map/ppermute | solution.py:34
  47.3 8.1 %collective-permute-done.2.refs_3_ = bf16[192,1024]{1,0:T(8,128)(2,1)S(1)} collective-permute-done((bf16[192,1024]{1,0:T(8,128)(2,1)S(1)}, bf16[192,1024]{1,0:T(8,128)(2,1)S(1)}, u32[]{:S(2)}, u32[]{:S(2)}) %collective-permute-start.2) | collective-permute-done | bytes 393248 | tf_op jit(solution)/shard_map/ppermute | solution.py:34
  55.5 0.9 join_slots.1
  56.4 1.1 copy-done.6
  57.5 3.4 %collective-permute-start.7 = (bf16[1024,384]{1,0:T(8,128)(2,1)S(1)}, bf16[1024,384]{1,0:T(8,128)(2,1)S(1)}, u32[]{:S(2)}, u32[]{:S(2)}) collective-permute-start(bf16[1024,384]{1,0:T(8,128)(2,1)S(1)} %get-tuple-element.46.refs_3_), channel_id=1, source_target_pairs={{0,8},{8,0},{17,25},{25,17},{2,10},{10,2},{19,27},{27,19},{4,12},{... | collective-permute-start | bytes 2359304 | tf_op jit(solution)/shard_map/ppermute | solution.py:259
  60.9 1.3 collective-permute-start.8
  62.2 1.3 collective-permute-start.9
  63.5 8.0 %hidden_grads.1 = (bf16[384,384]{1,0:T(8,128)(2,1)}, bf16[384,384]{1,0:T(8,128)(2,1)}, f32[32,8,128]{2,1,0:T(8,128)S(1)}) custom-call(s32[6]{0:T(128)S(1)} %stack.109.refs_0_, bf16[1,1,2048,768]{3,2,1,0:T(8,128)(2,1)} %refs_1_.3, bf16[1,1,768,2048]{3,2,1,0:T(8,128)(2,1)} %refs_2_.3, bf16[768,1024]{1,0:T(8,128)(2,1)S(1)} %get-tuple-element.44.refs_3_, ...), custom_call_target="tpu_custom_call" | custom-call | tf_op jit(solution)/shard_map/hidden_grads/pallas_call | solution.py:276
  71.5 3.3 %collective-permute-done.7.refs_1_ = bf16[1024,384]{1,0:T(8,128)(2,1)S(1)} collective-permute-done((bf16[1024,384]{1,0:T(8,128)(2,1)S(1)}, bf16[1024,384]{1,0:T(8,128)(2,1)S(1)}, u32[]{:S(2)}, u32[]{:S(2)}) %collective-permute-start.7) | collective-permute-done | bytes 786464 | tf_op jit(solution)/shard_map/ppermute | solution.py:259
  74.8 8.4 %collective-permute-done.8.refs_2_ = bf16[1024,384]{1,0:T(8,128)(2,1)S(1)} collective-permute-done((bf16[1024,384]{1,0:T(8,128)(2,1)S(1)}, bf16[1024,384]{1,0:T(8,128)(2,1)S(1)}, u32[]{:S(2)}, u32[]{:S(2)}) %collective-permute-start.8) | collective-permute-done | bytes 786464 | tf_op jit(solution)/shard_map/ppermute | solution.py:259
  83.2 0.9 hand_features.1
  84.1 2.7 %collective-permute-start.11 = (bf16[3,1024,384]{2,1,0:T(8,128)(2,1)S(1)}, bf16[3,1024,384]{2,1,0:T(8,128)(2,1)}, u32[]{:S(2)}, u32[]{:S(2)}) collective-permute-start(bf16[3,1024,384]{2,1,0:T(8,128)(2,1)S(1)} %get-tuple-element.49.refs_5_), channel_id=1, source_target_pairs={{0,1},{8,9},{17,16},{25,24},{2,3},{10,11},{19,18},{27,26},{4,5},{1... | collective-permute-start | bytes 7077896 | tf_op jit(solution)/shard_map/ppermute | solution.py:268
  86.8 2.2 %collective-permute-start.10 = (bf16[1024,384]{1,0:T(8,128)(2,1)S(1)}, bf16[1024,384]{1,0:T(8,128)(2,1)}, u32[]{:S(2)}, u32[]{:S(2)}) collective-permute-start(bf16[1024,384]{1,0:T(8,128)(2,1)S(1)} %get-tuple-element.46.refs_3_), channel_id=1, source_target_pairs={{0,1},{8,9},{17,16},{25,24},{2,3},{10,11},{19,18},{27,26},{4,5},{1... | collective-permute-start | bytes 2359304 | tf_op jit(solution)/shard_map/ppermute | solution.py:268
  88.9 0.5 collective-permute-start.12
  89.5 2.9 %collective-permute-start.14 = (bf16[384,384]{1,0:T(8,128)(2,1)}, bf16[384,384]{1,0:T(8,128)(2,1)}, u32[]{:S(2)}, u32[]{:S(2)}) collective-permute-start(bf16[384,384]{1,0:T(8,128)(2,1)} %get-tuple-element.51), channel_id=1, source_target_pairs={{0,24},{8,16},{16,8},{24,0},{1,25},{9,17},{17,9},{25,1},{2,26},{10... | collective-permute-start | bytes 884744 | tf_op jit(solution)/shard_map/ppermute | solution.py:34
  92.4 2.7 %all-to-all-start = ((f32[32,8,128]{2,1,0:T(8,128)}), f32[32,8,128]{2,1,0:T(8,128)S(1)}, u32[]{:S(2)}, u32[]{:S(2)}) async-start(f32[32,8,128]{2,1,0:T(8,128)} %get-tuple-element.47), calls=%async_computation | async-start | bytes 262144 | tf_op jit(solution)/shard_map/all_to_all | solution.py:307
  95.1 9.9 %all-to-all-done.refs_1_ = f32[32,8,128]{2,1,0:T(8,128)S(1)} async-done(((f32[32,8,128]{2,1,0:T(8,128)}), f32[32,8,128]{2,1,0:T(8,128)S(1)}, u32[]{:S(2)}, u32[]{:S(2)}) %all-to-all-start) | async-done | bytes 131104 | tf_op jit(solution)/shard_map/all_to_all | solution.py:307
  105.0 1.4 copy-done.7
  106.4 5.6 %average_block.1 = (f32[1024,384]{1,0:T(8,128)S(1)}, f32[32,8,128]{2,1,0:T(8,128)}) custom-call(s32[6]{0:T(128)S(1)} %stack.109.refs_0_, f32[32,8,128]{2,1,0:T(8,128)S(1)} %all-to-all-done.refs_1_, f32[1024,384]{1,0:T(8,128)S(1)} %copy-done.7, bf16[1024,384]{1,0:T(8,128)(2,1)S(1)} %get-tuple-element.46.refs_3_, ...), custom_call_target="tpu_custom_call" | custom-call | tf_op jit(solution)/shard_map/average_block/pallas_call | solution.py:309
  112.1 0.7 reduce_precision.3
  112.8 1.2 fusion
  114.0 1.5 collective-permute-start.17
  115.5 2.4 %collective-permute-start.15 = (f16[512,384]{1,0:T(8,128)(2,1)}, f16[512,384]{1,0:T(8,128)(2,1)S(1)}, u32[]{:S(2)}, u32[]{:S(2)}) collective-permute-start(f16[512,384]{1,0:T(8,128)(2,1)} %get-tuple-element.71), channel_id=1, source_target_pairs={{0,16},{8,24},{16,0},{24,8},{1,17},{9,25},{17,1},{25,9},{2,18},{10... | collective-permute-start | bytes 1179656 | tf_op jit(solution)/shard_map/ppermute | solution.py:34
  117.9 2.8 %all-to-all-start.1 = ((f32[32,8,128]{2,1,0:T(8,128)}), f32[32,8,128]{2,1,0:T(8,128)S(1)}, u32[]{:S(2)}, u32[]{:S(2)}) async-start(f32[32,8,128]{2,1,0:T(8,128)} %get-tuple-element.52), calls=%async_computation.1 | async-start | bytes 262144 | tf_op jit(solution)/shard_map/all_to_all | solution.py:325
  120.8 0.1 add_add_fusion.5.refs_0_
  121.0 7.8 %all-to-all-done.1.refs_0_.refs_1_ = f32[32,8,128]{2,1,0:T(8,128)S(1)} async-done(((f32[32,8,128]{2,1,0:T(8,128)}), f32[32,8,128]{2,1,0:T(8,128)S(1)}, u32[]{:S(2)}, u32[]{:S(2)}) %all-to-all-start.1) | async-done | bytes 131104 | tf_op jit(solution)/shard_map/all_to_all | solution.py:325
  128.8 1.1 copy-done.2
  129.9 0.1 pass_halves.1
  130.0 0.8 convert_element_type.38
  130.8 0.8 collective-permute-start.20
  131.7 0.8 convert_element_type.36
  132.5 0.7 collective-permute-start.19
  133.2 1.3 collective-permute-start.18
  134.5 1.2 collective-permute-start.16
  136.0 2.8 %copy-done = f32[1,2048,768]{2,1,0:T(8,128)S(1)} copy-done((f32[1,2048,768]{2,1,0:T(8,128)S(1)}, f32[1,2048,768]{2,1,0:T(8,128)}, u32[]{:S(2)}) %copy-start) | copy-done | bytes 6291480
  138.8 1.1 copy-done.3
  139.9 1.9 %update_block.8 = (f32[1,2048,768]{2,1,0:T(8,128)}, bf16[1,2048,768]{2,1,0:T(8,128)(2,1)}) custom-call(s32[3]{0:T(128)S(1)} %get-tuple-element.75.refs_0_, f32[32,8,128]{2,1,0:T(8,128)S(1)} %all-to-all-done.1.refs_0_.refs_1_, f32[512,384]{1,0:T(8,128)S(1)} %copy-done.3, f32[1,2048,768]{2,1,0:T(8,128)S(1)} %copy-done), custom_call_target="tpu_custom_call" | custom-call | tf_op jit(solution)/shard_map/update_block/pallas_call | solution.py:181
  141.8 2.8 %copy-done.1 = f32[1,2048,768]{2,1,0:T(8,128)S(1)} copy-done((f32[1,2048,768]{2,1,0:T(8,128)S(1)}, f32[1,2048,768]{2,1,0:T(8,128)}, u32[]{:S(2)}) %copy-start.1) | copy-done | bytes 6291480
  144.6 1.9 %update_block.9 = (f32[1,2048,768]{2,1,0:T(8,128)}, bf16[1,2048,768]{2,1,0:T(8,128)(2,1)}) custom-call(s32[3]{0:T(128)S(1)} %get-tuple-element.74.refs_0_, f32[32,8,128]{2,1,0:T(8,128)S(1)} %all-to-all-done.1.refs_0_.refs_1_, f32[512,384]{1,0:T(8,128)S(1)} %get-tuple-element.70.refs_2_, ...), custom_call_target="tpu_custom_call", output_to_operand_aliasing={{0}: (4, {}), {1}: (5, {})} | custom-call | tf_op jit(solution)/shard_map/update_block/pallas_call | solution.py:181
  146.5 1.0 convert_element_type.40.refs_2_
  147.6 1.9 %update_block.10 = (f32[1,2048,768]{2,1,0:T(8,128)}, bf16[1,2048,768]{2,1,0:T(8,128)(2,1)}) custom-call(s32[3]{0:T(128)S(1)} %add_add_fusion.5.refs_0_, f32[32,8,128]{2,1,0:T(8,128)S(1)} %all-to-all-done.1.refs_0_.refs_1_, f32[512,384]{1,0:T(8,128)S(1)} %convert_element_type.40.refs_2_, ...), custom_call_target="tpu_custom_call", output_to_operand_aliasing={{0}: (4, {}), {1}: (5, {})} | custom-call | tf_op jit(solution)/shard_map/update_block/pallas_call | solution.py:181
  149.5 1.0 convert_element_type.39.refs_2_
  150.5 1.0 convert_element_type.37.refs_2_
  151.6 1.9 %update_block.11 = (f32[1,2048,768]{2,1,0:T(8,128)}, bf16[1,2048,768]{2,1,0:T(8,128)(2,1)}) custom-call(s32[3]{0:T(128)S(1)} %add_add_fusion.4.refs_0_, f32[32,8,128]{2,1,0:T(8,128)S(1)} %all-to-all-done.1.refs_0_.refs_1_, f32[512,384]{1,0:T(8,128)S(1)} %convert_element_type.39.refs_2_, ...), custom_call_target="tpu_custom_call", output_to_operand_aliasing={{0}: (4, {}), {1}: (5, {})} | custom-call | tf_op jit(solution)/shard_map/update_block/pallas_call | solution.py:181
  153.5 1.9 %update_block.12 = (f32[1,2048,768]{2,1,0:T(8,128)}, bf16[1,2048,768]{2,1,0:T(8,128)(2,1)}) custom-call(s32[3]{0:T(128)S(1)} %add_add_fusion.3.refs_0_, f32[32,8,128]{2,1,0:T(8,128)S(1)} %all-to-all-done.1.refs_0_.refs_1_, f32[512,384]{1,0:T(8,128)S(1)} %convert_element_type.37.refs_2_, ...), custom_call_target="tpu_custom_call", output_to_operand_aliasing={{0}: (4, {}), {1}: (5, {})} | custom-call | tf_op jit(solution)/shard_map/update_block/pallas_call | solution.py:181
  155.3 1.9 %update_block.13 = (f32[1,2048,768]{2,1,0:T(8,128)}, bf16[1,2048,768]{2,1,0:T(8,128)(2,1)}) custom-call(s32[3]{0:T(128)S(1)} %add_add_fusion.2.refs_0_, f32[32,8,128]{2,1,0:T(8,128)S(1)} %all-to-all-done.1.refs_0_.refs_1_, f32[512,384]{1,0:T(8,128)S(1)} %convert_element_type.35.refs_2_, ...), custom_call_target="tpu_custom_call", output_to_operand_aliasing={{0}: (4, {}), {1}: (5, {})} | custom-call | tf_op jit(solution)/shard_map/update_block/pallas_call | solution.py:181
  157.2 1.0 convert_element_type.34.refs_2_
  158.3 1.0 convert_element_type.32.refs_2_
  159.3 1.9 %update_block.14 = (f32[1,2048,768]{2,1,0:T(8,128)}, bf16[1,2048,768]{2,1,0:T(8,128)(2,1)}) custom-call(s32[3]{0:T(128)S(1)} %add_add_fusion.1.refs_0_, f32[32,8,128]{2,1,0:T(8,128)S(1)} %all-to-all-done.1.refs_0_.refs_1_, f32[512,384]{1,0:T(8,128)S(1)} %convert_element_type.34.refs_2_, ...), custom_call_target="tpu_custom_call", output_to_operand_aliasing={{0}: (4, {}), {1}: (5, {})} | custom-call | tf_op jit(solution)/shard_map/update_block/pallas_call | solution.py:181
  161.2 1.9 %update_block.15 = (f32[1,2048,768]{2,1,0:T(8,128)}, bf16[1,2048,768]{2,1,0:T(8,128)(2,1)}) custom-call(s32[3]{0:T(128)S(1)} %add_add_fusion.refs_0_, f32[32,8,128]{2,1,0:T(8,128)S(1)} %all-to-all-done.1.refs_0_.refs_1_, f32[512,384]{1,0:T(8,128)S(1)} %convert_element_type.32.refs_2_, ...), custom_call_target="tpu_custom_call", output_to_operand_aliasing={{0}: (4, {}), {1}: (5, {})} | custom-call | tf_op jit(solution)/shard_map/update_block/pallas_call | solution.py:181
  (45 shorter events, 0.6 us)
Async XLA Ops:
  0.7 1.9 %copy-start.4 = (bf16[1,1,2048,768]{3,2,1,0:T(8,128)(2,1)S(1)}, bf16[1,1,2048,768]{3,2,1,0:T(8,128)(2,1)}, u32[]{:S(2)}) copy-start(bf16[1,1,2048,768]{3,2,1,0:T(8,128)(2,1)} %refs_6_.1) | copy-start | bytes 9437188
  2.6 1.0 copy-start.8
  3.7 1.0 copy-start.9
  4.7 0.7 copy-start.10
  5.4 0.7 copy-start.11
  6.1 0.7 copy-start.12
  8.6 15.2 %collective-permute-start = (bf16[192,1024]{1,0:T(8,128)(2,1)S(1)}, bf16[192,1024]{1,0:T(8,128)(2,1)S(1)}, u32[]{:S(2)}, u32[]{:S(2)}) collective-permute-start(bf16[192,1024]{1,0:T(8,128)(2,1)S(1)} %get-tuple-element.37), channel_id=1, source_target_pairs={{0,6},{2,4},{4,2},{6,0},{1,7},{3,5},{5,3},{7,1},{8,14},{10,12},{12... | collective-permute-start | bytes 1179656 | tf_op jit(solution)/shard_map/ppermute | solution.py:34
  13.7 41.8 %collective-permute-start.3 = (bf16[1024,384]{1,0:T(8,128)(2,1)S(1)}, bf16[1024,384]{1,0:T(8,128)(2,1)S(1)}, u32[]{:S(2)}, u32[]{:S(2)}) collective-permute-start(bf16[1024,384]{1,0:T(8,128)(2,1)S(1)} %get-tuple-element.41), channel_id=1, source_target_pairs={{0,8},{8,0},{16,24},{24,16},{1,9},{9,1},{17,25},{25,17},{2,10},{10... | collective-permute-start | bytes 2359304 | tf_op jit(solution)/shard_map/ppermute | solution.py:34
  15.2 40.3 %collective-permute-start.4 = (bf16[1024,384]{1,0:T(8,128)(2,1)S(1)}, bf16[1024,384]{1,0:T(8,128)(2,1)S(1)}, u32[]{:S(2)}, u32[]{:S(2)}) collective-permute-start(bf16[1024,384]{1,0:T(8,128)(2,1)S(1)} %get-tuple-element.42), channel_id=1, source_target_pairs={{0,16},{8,24},{16,0},{24,8},{1,17},{9,25},{17,1},{25,9},{2,18},{10... | collective-permute-start | bytes 2359304 | tf_op jit(solution)/shard_map/ppermute | solution.py:34
  16.7 38.8 %collective-permute-start.5 = (bf16[1024,384]{1,0:T(8,128)(2,1)S(1)}, bf16[1024,384]{1,0:T(8,128)(2,1)S(1)}, u32[]{:S(2)}, u32[]{:S(2)}) collective-permute-start(bf16[1024,384]{1,0:T(8,128)(2,1)S(1)} %get-tuple-element.43), channel_id=1, source_target_pairs={{0,24},{8,16},{16,8},{24,0},{1,25},{9,17},{17,9},{25,1},{2,26},{10... | collective-permute-start | bytes 2359304 | tf_op jit(solution)/shard_map/ppermute | solution.py:34
  17.2 30.2 %collective-permute-start.1 = (bf16[192,1024]{1,0:T(8,128)(2,1)S(1)}, bf16[192,1024]{1,0:T(8,128)(2,1)S(1)}, u32[]{:S(2)}, u32[]{:S(2)}) collective-permute-start(bf16[192,1024]{1,0:T(8,128)(2,1)S(1)} %get-tuple-element.38), channel_id=1, source_target_pairs={{0,4},{2,6},{4,0},{6,2},{1,5},{3,7},{5,1},{7,3},{8,12},{10,14},{12... | collective-permute-start | bytes 1179656 | tf_op jit(solution)/shard_map/ppermute | solution.py:34
  23.7 31.7 %collective-permute-start.2 = (bf16[192,1024]{1,0:T(8,128)(2,1)S(1)}, bf16[192,1024]{1,0:T(8,128)(2,1)S(1)}, u32[]{:S(2)}, u32[]{:S(2)}) collective-permute-start(bf16[192,1024]{1,0:T(8,128)(2,1)S(1)} %get-tuple-element.39), channel_id=1, source_target_pairs={{0,2},{2,0},{4,6},{6,4},{1,3},{3,1},{5,7},{7,5},{8,10},{10,8},{12,... | collective-permute-start | bytes 1179656 | tf_op jit(solution)/shard_map/ppermute | solution.py:34
  56.4 1.1 copy-start.6
  57.5 6.0 %collective-permute-start.6 = (bf16[768,1024]{1,0:T(8,128)(2,1)S(1)}, bf16[768,1024]{1,0:T(8,128)(2,1)S(1)}, u32[]{:S(2)}, u32[]{:S(2)}) collective-permute-start(bf16[768,1024]{1,0:T(8,128)(2,1)S(1)} %get-tuple-element.44.refs_3_), channel_id=1, source_target_pairs={{0,1},{1,0},{2,3},{3,2},{4,5},{5,4},{6,7},{7,6},{8,9},{9,8},{10,11... | collective-permute-start | bytes 4718600 | tf_op jit(solution)/shard_map/ppermute | solution.py:34
  57.5 17.3 %collective-permute-start.7 = (bf16[1024,384]{1,0:T(8,128)(2,1)S(1)}, bf16[1024,384]{1,0:T(8,128)(2,1)S(1)}, u32[]{:S(2)}, u32[]{:S(2)}) collective-permute-start(bf16[1024,384]{1,0:T(8,128)(2,1)S(1)} %get-tuple-element.46.refs_3_), channel_id=1, source_target_pairs={{0,8},{8,0},{17,25},{25,17},{2,10},{10,2},{19,27},{27,19},{4,12},{... | collective-permute-start | bytes 2359304 | tf_op jit(solution)/shard_map/ppermute | solution.py:259
  60.9 22.3 %collective-permute-start.8 = (bf16[1024,384]{1,0:T(8,128)(2,1)S(1)}, bf16[1024,384]{1,0:T(8,128)(2,1)S(1)}, u32[]{:S(2)}, u32[]{:S(2)}) collective-permute-start(bf16[1024,384]{1,0:T(8,128)(2,1)S(1)} %get-tuple-element.46.refs_3_), channel_id=1, source_target_pairs={{1,17},{9,25},{16,0},{24,8},{3,19},{11,27},{18,2},{26,10},{5,21},{... | collective-permute-start | bytes 2359304 | tf_op jit(solution)/shard_map/ppermute | solution.py:259
  62.2 21.0 %collective-permute-start.9 = (bf16[1024,384]{1,0:T(8,128)(2,1)S(1)}, bf16[1024,384]{1,0:T(8,128)(2,1)S(1)}, u32[]{:S(2)}, u32[]{:S(2)}) collective-permute-start(bf16[1024,384]{1,0:T(8,128)(2,1)S(1)} %get-tuple-element.46.refs_3_), channel_id=1, source_target_pairs={{1,25},{9,17},{16,8},{24,0},{3,27},{11,19},{18,10},{26,2},{5,29},{... | collective-permute-start | bytes 2359304 | tf_op jit(solution)/shard_map/ppermute | solution.py:259
  84.1 20.9 %copy-start.5 = (bf16[3,1024,384]{2,1,0:T(8,128)(2,1)}, bf16[3,1024,384]{2,1,0:T(8,128)(2,1)S(1)}, u32[]{:S(2)}) copy-start(bf16[3,1024,384]{2,1,0:T(8,128)(2,1)S(1)} %get-tuple-element.49.refs_5_) | copy-start | bytes 7077892
  84.1 20.9 %collective-permute-start.11 = (bf16[3,1024,384]{2,1,0:T(8,128)(2,1)S(1)}, bf16[3,1024,384]{2,1,0:T(8,128)(2,1)}, u32[]{:S(2)}, u32[]{:S(2)}) collective-permute-start(bf16[3,1024,384]{2,1,0:T(8,128)(2,1)S(1)} %get-tuple-element.49.refs_5_), channel_id=1, source_target_pairs={{0,1},{8,9},{17,16},{25,24},{2,3},{10,11},{19,18},{27,26},{4,5},{1... | collective-permute-start | bytes 7077896 | tf_op jit(solution)/shard_map/ppermute | solution.py:268
  86.8 8.3 %collective-permute-start.10 = (bf16[1024,384]{1,0:T(8,128)(2,1)S(1)}, bf16[1024,384]{1,0:T(8,128)(2,1)}, u32[]{:S(2)}, u32[]{:S(2)}) collective-permute-start(bf16[1024,384]{1,0:T(8,128)(2,1)S(1)} %get-tuple-element.46.refs_3_), channel_id=1, source_target_pairs={{0,1},{8,9},{17,16},{25,24},{2,3},{10,11},{19,18},{27,26},{4,5},{1... | collective-permute-start | bytes 2359304 | tf_op jit(solution)/shard_map/ppermute | solution.py:268
  88.9 16.1 %collective-permute-start.12 = (bf16[384,384]{1,0:T(8,128)(2,1)}, bf16[384,384]{1,0:T(8,128)(2,1)}, u32[]{:S(2)}, u32[]{:S(2)}) collective-permute-start(bf16[384,384]{1,0:T(8,128)(2,1)} %get-tuple-element.51), channel_id=1, source_target_pairs={{0,8},{8,0},{16,24},{24,16},{1,9},{9,1},{17,25},{25,17},{2,10},{10... | collective-permute-start | bytes 884744 | tf_op jit(solution)/shard_map/ppermute | solution.py:34
  89.5 15.5 %collective-permute-start.13 = (bf16[384,384]{1,0:T(8,128)(2,1)}, bf16[384,384]{1,0:T(8,128)(2,1)}, u32[]{:S(2)}, u32[]{:S(2)}) collective-permute-start(bf16[384,384]{1,0:T(8,128)(2,1)} %get-tuple-element.50.refs_7_), channel_id=1, source_target_pairs={{0,16},{8,24},{16,0},{24,8},{1,17},{9,25},{17,1},{25,9},{2,18},{10... | collective-permute-start | bytes 884744 | tf_op jit(solution)/shard_map/ppermute | solution.py:34
  89.5 15.5 %collective-permute-start.14 = (bf16[384,384]{1,0:T(8,128)(2,1)}, bf16[384,384]{1,0:T(8,128)(2,1)}, u32[]{:S(2)}, u32[]{:S(2)}) collective-permute-start(bf16[384,384]{1,0:T(8,128)(2,1)} %get-tuple-element.51), channel_id=1, source_target_pairs={{0,24},{8,16},{16,8},{24,0},{1,25},{9,17},{17,9},{25,1},{2,26},{10... | collective-permute-start | bytes 884744 | tf_op jit(solution)/shard_map/ppermute | solution.py:34
  92.4 12.6 %all-to-all-start = ((f32[32,8,128]{2,1,0:T(8,128)}), f32[32,8,128]{2,1,0:T(8,128)S(1)}, u32[]{:S(2)}, u32[]{:S(2)}) async-start(f32[32,8,128]{2,1,0:T(8,128)} %get-tuple-element.47), calls=%async_computation | async-start | bytes 262144 | tf_op jit(solution)/shard_map/all_to_all | solution.py:307
  105.0 1.4 copy-start.7
  114.0 19.2 %collective-permute-start.17 = (f16[512,384]{1,0:T(8,128)(2,1)}, f16[512,384]{1,0:T(8,128)(2,1)}, u32[]{:S(2)}, u32[]{:S(2)}) collective-permute-start(f16[512,384]{1,0:T(8,128)(2,1)} %get-tuple-element.72), channel_id=1, source_target_pairs={{0,8},{8,0},{16,24},{24,16},{1,9},{9,1},{17,25},{25,17},{2,10},{10... | collective-permute-start | bytes 1179656 | tf_op jit(solution)/shard_map/ppermute | solution.py:34
  115.5 19.0 %collective-permute-start.15 = (f16[512,384]{1,0:T(8,128)(2,1)}, f16[512,384]{1,0:T(8,128)(2,1)S(1)}, u32[]{:S(2)}, u32[]{:S(2)}) collective-permute-start(f16[512,384]{1,0:T(8,128)(2,1)} %get-tuple-element.71), channel_id=1, source_target_pairs={{0,16},{8,24},{16,0},{24,8},{1,17},{9,25},{17,1},{25,9},{2,18},{10... | collective-permute-start | bytes 1179656 | tf_op jit(solution)/shard_map/ppermute | solution.py:34
  117.9 10.8 %all-to-all-start.1 = ((f32[32,8,128]{2,1,0:T(8,128)}), f32[32,8,128]{2,1,0:T(8,128)S(1)}, u32[]{:S(2)}, u32[]{:S(2)}) async-start(f32[32,8,128]{2,1,0:T(8,128)} %get-tuple-element.52), calls=%async_computation.1 | async-start | bytes 262144 | tf_op jit(solution)/shard_map/all_to_all | solution.py:325
  128.8 1.1 copy-start.2
  129.9 17.7 %slice-start = ((s8[6291456]{0:T(1024)(128)(4,1)}), s8[2097152]{0:T(1024)(128)(4,1)S(1)}, s32[]{:S(2)}) async-start(s8[6291456]{0:T(1024)(128)(4,1)} %bitcast.20), calls=%async_computation.2 | async-start | bytes 4194304
  130.8 18.6 %collective-permute-start.20 = (f16[512,384]{1,0:T(8,128)(2,1)}, f16[512,384]{1,0:T(8,128)(2,1)}, u32[]{:S(2)}, u32[]{:S(2)}) collective-permute-start(f16[512,384]{1,0:T(8,128)(2,1)} %convert_element_type.38), channel_id=1, source_target_pairs={{0,8},{8,0},{16,24},{24,16},{1,9},{9,1},{17,25},{25,17},{2,10},{10... | collective-permute-start | bytes 1179656 | tf_op jit(solution)/shard_map/ppermute | solution.py:34
  132.5 18.1 %collective-permute-start.19 = (f16[512,384]{1,0:T(8,128)(2,1)}, f16[512,384]{1,0:T(8,128)(2,1)}, u32[]{:S(2)}, u32[]{:S(2)}) collective-permute-start(f16[512,384]{1,0:T(8,128)(2,1)} %convert_element_type.36), channel_id=1, source_target_pairs={{0,16},{8,24},{16,0},{24,8},{1,17},{9,25},{17,1},{25,9},{2,18},{10... | collective-permute-start | bytes 1179656 | tf_op jit(solution)/shard_map/ppermute | solution.py:34
  133.2 24.0 %collective-permute-start.18 = (f16[512,384]{1,0:T(8,128)(2,1)}, f16[512,384]{1,0:T(8,128)(2,1)}, u32[]{:S(2)}, u32[]{:S(2)}) collective-permute-start(f16[512,384]{1,0:T(8,128)(2,1)} %collective-permute-done.17), channel_id=1, source_target_pairs={{0,16},{8,24},{16,0},{24,8},{1,17},{9,25},{17,1},{25,9},{2,18},{10... | collective-permute-start | bytes 1179656 | tf_op jit(solution)/shard_map/ppermute | solution.py:34
  134.5 23.8 %collective-permute-start.16 = (f16[512,384]{1,0:T(8,128)(2,1)S(1)}, f16[512,384]{1,0:T(8,128)(2,1)}, u32[]{:S(2)}, u32[]{:S(2)}) collective-permute-start(f16[512,384]{1,0:T(8,128)(2,1)S(1)} %collective-permute-done.15), channel_id=1, source_target_pairs={{0,8},{8,0},{16,24},{24,16},{1,9},{9,1},{17,25},{25,17},{2,10},{10... | collective-permute-start | bytes 1179656 | tf_op jit(solution)/shard_map/ppermute | solution.py:34
  136.0 2.8 %copy-start = (f32[1,2048,768]{2,1,0:T(8,128)S(1)}, f32[1,2048,768]{2,1,0:T(8,128)}, u32[]{:S(2)}) copy-start(f32[1,2048,768]{2,1,0:T(8,128)} %refs_3_.17) | copy-start | bytes 18874372
  138.8 1.1 copy-start.3
  141.8 2.8 %copy-start.1 = (f32[1,2048,768]{2,1,0:T(8,128)S(1)}, f32[1,2048,768]{2,1,0:T(8,128)}, u32[]{:S(2)}) copy-start(f32[1,2048,768]{2,1,0:T(8,128)} %refs_3_.17) | copy-start | bytes 18874372
  144.6 3.0 %slice-start.1 = ((s8[6291456]{0:T(1024)(128)(4,1)}), s8[4194304]{0:T(1024)(128)(4,1)S(1)}, s32[]{:S(2)}) async-start(s8[6291456]{0:T(1024)(128)(4,1)} %bitcast.20), calls=%async_computation.3 | async-start | bytes 8388608

commit v4 on v3

v4 whole, which is shorter than its diff:
```python
import math

import jax
import jax.numpy as jnp
from jax import lax
from jax.experimental import pallas as pl
from jax.experimental.pallas import tpu as pltpu
from jax.sharding import PartitionSpec as P

F32 = jnp.float32
BF16 = jnp.bfloat16
WIRE = jnp.float16
AXES = ("island", "expert", "tensor")

VMEM = pl.BlockSpec(memory_space=pltpu.VMEM)
SMEM = pl.BlockSpec(memory_space=pltpu.SMEM)
ANY = pl.BlockSpec(memory_space=pl.ANY)


def params(mib):
    return pltpu.CompilerParams(vmem_limit_bytes=mib << 20)


def partner(at, step, size):
    return at ^ step if size & (size - 1) == 0 else (at + step) % size


def origin(at, step, size):
    return at ^ step if size & (size - 1) == 0 else (at - step) % size


def swap(value, axis, step):
    size = lax.axis_size(axis)
    return lax.ppermute(value, axis, [(at, partner(at, step, size)) for at in range(size)])


def dot(a, b, contract):
    return lax.dot_general(a, b, (contract, ((), ())), preferred_element_type=F32)


def copy_all(sems, pairs):
    copies = [pltpu.make_async_copy(*pair, sems.at[n]) for n, pair in enumerate(pairs)]
    for copy in copies:
        copy.start()
    return copies


def pick_kernel(experts, islands, pieces, spot, *refs):
    sources, drift = refs[:5], refs[5]
    outs, blocks = refs[6 : 6 + experts], refs[6 + experts : -6]
    table, count, weight, tokens, grads, sems = refs[-6:]
    loads = copy_all(sems, list(zip(sources, refs[-6:-1])))
    rows, columns = blocks[0].shape
    pairs = []
    for d, first, count_rows, target, at_row in pieces:
        at = partner(spot[3], d, islands)
        top = pl.multiple_of(lax.div(at, spot[4]) * rows, rows) + first
        left = pl.multiple_of(lax.rem(at, spot[4]) * columns, columns)
        pairs.append(
            (
                drift.at[0, 0, pl.ds(top, count_rows), pl.ds(left, columns)],
                blocks[target].at[pl.ds(at_row, count_rows)],
            )
        )
    copies = copy_all(sems.at[pl.ds(5, len(pairs))], pairs)
    for copy in loads:
        copy.wait()

    slots = table.shape[-1]
    rows = lax.broadcasted_iota(jnp.int32, (slots, slots), 0)
    lanes = lax.broadcasted_iota(jnp.int32, (slots, slots), 1)

    def column(row):
        return jnp.sum(jnp.where(rows == lanes, row, 0), axis=1, keepdims=True)

    for d in range(experts):
        to = partner(spot[0], d, experts)
        live = lax.broadcasted_iota(jnp.int32, (slots, 1), 0) < count[0, 0, to]
        token = column(table[0, 0, pl.ds(to, 1), :].astype(F32)).astype(jnp.int32)
        chance = column(weight[0, 0, pl.ds(to, 1), :])
        ids = lax.broadcasted_iota(jnp.int32, (slots, tokens.shape[1]), 1)
        picks = jnp.where((ids == token) & live, 1.0, 0.0).astype(BF16)
        outs[d][:slots, :] = dot(picks, tokens[0], ((1,), (0,))).astype(BF16)
        picked = dot(picks, grads[0], ((1,), (0,)))
        outs[d][slots:, :] = (chance * picked).astype(BF16)
    for copy in copies:
        copy.wait()


def join_kernel(count, blocks, *refs):
    arrived, drifts = refs[:count], refs[count : count + blocks]
    joined, turned, drift_sum = refs[count + blocks : count + blocks + 3]
    slots = arrived[0].shape[0] // 2
    rows = drift_sum.shape[0]
    for n, ref in enumerate(refs[count + blocks + 3 :]):
        ref[...] = drifts[1 + n][rows:, :]
    for n, piece in enumerate(arrived):
        joined[n * slots : (n + 1) * slots, :] = piece[:slots, :]
        joined[(count + n) * slots : (count + n + 1) * slots, :] = piece[slots:, :]
    turned[...] = joined[: count * slots, :].T
    added = drifts[0][...].astype(F32)
    for other in drifts[1:]:
        added = added + other[:rows, :].astype(F32)
    drift_sum[...] = added


def hidden_kernel(parts, across, spot, gate, down, *refs):
    joined, outs = refs[:parts], refs[parts : parts + across]
    norms, gate_part, down_part, inputs, sems = refs[parts + across :]
    rows, half = joined[0].shape[0] // 2, joined[0].shape[1]
    columns = outs[0].shape[1]
    loads = [[pltpu.make_async_copy(joined[t], inputs.at[t], sems.at[t])] for t in range(parts)]
    for r in range(across):
        first = pl.multiple_of(partner(spot[2], r, across) * columns, columns)
        at = parts + 2 * r
        loads.append(
            [
                pltpu.make_async_copy(
                    gate.at[0, 0, :, pl.ds(first, columns)], gate_part.at[r], sems.at[at]
                ),
                pltpu.make_async_copy(
                    down.at[0, 0, pl.ds(first, columns), :], down_part.at[r], sems.at[at + 1]
                ),
            ]
        )
    for group in loads:
        for copy in group:
            copy.start()
    starts = [pl.multiple_of(origin(spot[1], t, parts) * half, half) for t in range(parts)]
    input_gram = 0.0
    for t in range(parts):
        loads[t][0].wait()
        features = inputs[t, :rows, :]
        input_gram = input_gram + dot(features, features, ((1,), (1,)))
    hidden_gram = 0.0
    for r in range(across):
        value = 0.0
        back = 0.0
        loads[parts + r][0].wait()
        for t in range(parts):
            block = gate_part[r, pl.ds(starts[t], half), :]
            value = value + dot(inputs[t, :rows, :], block, ((1,), (0,)))
        loads[parts + r][1].wait()
        for t in range(parts):
            block = down_part[r, :, pl.ds(starts[t], half)]
            back = back + dot(inputs[t, rows:, :], block, ((1,), (1,)))
        rounded = (back * (value / (1.0 + jnp.exp(-value)))).astype(BF16)
        outs[r][...] = rounded
        hidden_gram = hidden_gram + dot(rounded, rounded, ((1,), (1,)))
    norms[...] = jnp.full(norms.shape, jnp.sum(hidden_gram * input_gram), F32)


def average_kernel(islands, entries, tiles, relays, spot, norms, *refs):
    drift_sum, own, moved = refs[:3]
    handed = refs[3 + islands : 3 + islands + relays]
    scaled, notes, inputs, hiddens, total, extra, sems = refs[-7:]
    rows = total.shape[0] // tiles
    across = [pltpu.make_async_copy(refs[3 + d], hiddens.at[d], sems.at[0, d]) for d in range(islands)]
    if handed:
        size = handed[0].shape[0]
        for n, ref in enumerate(handed):
            place = extra.at[pl.ds(n * size, size)]
            across.append(pltpu.make_async_copy(ref, place, sems.at[0, islands + n]))
    for copy in across:
        copy.start()

    def part(m):
        return pl.ds(m * rows, rows)

    def fetch(features):
        for m in range(tiles):
            pltpu.make_async_copy(drift_sum.at[part(m)], total.at[part(m)], sems.at[1 + m, islands]).start()
            for d in range(islands):
                source = features.at[d, part(m)]
                pltpu.make_async_copy(source, inputs.at[d, part(m)], sems.at[1 + m, d]).start()

    pl.when(spot[5] == 1)(lambda: fetch(own))
    pl.when(spot[5] != 1)(lambda: fetch(moved))

    group = norms.shape[0] // islands
    scales = []
    for d in range(islands):
        at = origin(spot[3], d, islands)
        square = jnp.sum(norms[pl.ds(at * group, group)], axis=0)[:1, :1]
        scales.append(jnp.minimum(1.0, math.sqrt(entries) / jnp.sqrt(square + 1e-06)) / islands)
    for copy in across:
        copy.wait()
    square = 0.0
    peak = 0.0
    for m in range(tiles):
        pltpu.make_async_copy(drift_sum.at[part(m)], total.at[part(m)], sems.at[1 + m, islands]).wait()
        average = total[part(m), :]
        if handed:
            average = average + extra[part(m), :].astype(F32)
        average = average * (1.0 / islands)
        for d in range(islands):
            pltpu.make_async_copy(
                own.at[d, part(m)], inputs.at[d, part(m)], sems.at[1 + m, d]
            ).wait()
            average = average + scales[d] * dot(inputs[d, part(m)], hiddens[d], ((1,), (0,)))
        total[part(m), :] = average
        square = square + jnp.sum(average * average, axis=0, keepdims=True)
        peak = jnp.maximum(peak, jnp.max(jnp.abs(average), axis=0, keepdims=True))
    unit = jnp.maximum(jnp.max(peak), 1e-30) / 32768
    scaled[...] = total[...] * (1 / unit)
    sublane = lax.broadcasted_iota(jnp.int32, notes.shape, 1)
    notes[...] = jnp.where(sublane == 0, jnp.sum(square), unit)


def hand_kernel(count, norms, *refs):
    passed, joined, sems = refs[-3:]
    pairs = [(refs[n], joined.at[n]) for n in range(count)] + [(norms, passed)]
    for copy in copy_all(sems, pairs):
        copy.wait()


def pass_kernel(count, notes, *refs):
    for copy in copy_all(refs[-1], [(refs[n], refs[count + n]) for n in range(count)]):
        copy.wait()


def update_kernel(entries, count, place, notes, momentum, *refs):
    pieces = refs[:count]
    new_momentum, outer_step, values, old, step, loads, stores = refs[-7:]
    rows, columns = pieces[0].shape
    spots = []
    for n in range(count):
        top = pl.multiple_of(place[3 * n] * rows, rows)
        left = pl.multiple_of(place[3 * n + 1] * columns, columns)
        spots.append((0, pl.ds(top, rows), pl.ds(left, columns)))
    pairs = []
    for n in range(count):
        pairs += [(pieces[n], values.at[n]), (momentum.at[spots[n]], old.at[n])]
    fetched = copy_all(loads, pairs)
    square = jnp.sum(notes[...], axis=0)[:1, :1]
    clip = jnp.minimum(1.0, 0.25 * math.sqrt(entries) / jnp.sqrt(square + 1e-06))
    stored = []
    for n in range(count):
        unit = notes[pl.ds(place[3 * n + 2], 1)][0, 1:2, :1]
        fetched[2 * n].wait()
        fetched[2 * n + 1].wait()
        clipped = (clip * unit) * values[n]
        moved = 0.9 * old[n] + clipped
        old[n] = moved
        step[n] = (0.7 * (clipped + 0.9 * moved)).astype(BF16)
        pairs = [(old.at[n], new_momentum.at[spots[n]]), (step.at[n], outer_step.at[spots[n]])]
        stored += copy_all(stores.at[n], pairs)
    for copy in stored:
        copy.wait()


def update_pieces(entries, places, notes, momentum, pieces, outs):
    count = len(pieces)
    shape = (count, *pieces[0].shape)
    return pl.pallas_call(
        lambda *refs: update_kernel(entries, count, *refs),
        in_specs=[SMEM, VMEM] + [ANY] * (1 + count + len(outs)),
        out_specs=[ANY, ANY],
        out_shape=[
            jax.ShapeDtypeStruct(momentum.shape, F32),
            jax.ShapeDtypeStruct(momentum.shape, BF16),
        ],
        scratch_shapes=[
            pltpu.VMEM(shape, F32),
            pltpu.VMEM(shape, F32),
            pltpu.VMEM(shape, BF16),
            pltpu.SemaphoreType.DMA((2 * count,)),
            pltpu.SemaphoreType.DMA((count, 2)),
        ],
        input_output_aliases={3 + count + n: n for n in range(len(outs))},
        compiler_params=params(48),
        name="update_pieces",
    )(jnp.concatenate(places), notes, momentum, *pieces, *outs)


def body(
    tokens,
    token_grads,
    slot_token,
    slot_count,
    slot_prob,
    gate_weight,
    down_weight,
    drift,
    momentum,
):
    islands, experts, parts = (lax.axis_size(a) for a in AXES)
    island, expert, part = (lax.axis_index(a) for a in AXES)
    devices = islands * experts * parts
    features, hidden = gate_weight.shape[2:]
    half = features // parts
    across = islands // parts
    columns = hidden // across
    entries = features * hidden * experts * parts
    slots = slot_token.shape[3]
    routed_rows = experts * slots
    holder = island // across
    spot = jnp.stack(
        [expert, part, island % across, island, jnp.int32(across), (part == holder).astype(jnp.int32)]
    ).astype(jnp.int32)

    handed = half // 2 if islands == 4 else 0
    steps = [0, 1, 2] if handed else list(range(islands))
    pieces = [(d, 0, half, n, 0) for n, d in enumerate(steps)]
    if handed:
        pieces += [(3, 0, handed, 1, half), (3, handed, handed, 2, half)]
    block_rows = [half + (handed if d else 0) for d in steps]
    picked = pl.pallas_call(
        lambda *refs: pick_kernel(experts, islands, pieces, *refs),
        in_specs=[SMEM] + [ANY] * 6,
        out_specs=[VMEM] * experts + [ANY] * len(steps),
        out_shape=[jax.ShapeDtypeStruct((2 * slots, half), BF16)] * experts
        + [jax.ShapeDtypeStruct((rows, columns), BF16) for rows in block_rows],
        scratch_shapes=[
            pltpu.VMEM(slot_token.shape, jnp.int32),
            pltpu.SMEM(slot_count.shape, jnp.int32),
            pltpu.VMEM(slot_prob.shape, F32),
            pltpu.VMEM(tokens.shape, BF16),
            pltpu.VMEM(token_grads.shape, BF16),
            pltpu.SemaphoreType.DMA((5 + len(pieces),)),
        ],
        compiler_params=params(56),
        name="pick_slots",
    )(spot, slot_token, slot_count, slot_prob, tokens, token_grads, drift)
    arrived = [picked[0]] + [swap(picked[d], "expert", d) for d in range(1, experts)]
    blocks = picked[experts:]
    drift_in = [blocks[0]] + [swap(blocks[d], "island", d) for d in steps[1:]]
    joined, turned, drift_sum, *relays = pl.pallas_call(
        lambda *refs: join_kernel(experts, len(steps), *refs),
        in_specs=[VMEM] * (experts + len(steps)),
        out_specs=[VMEM] * (5 if handed else 3),
        out_shape=[
            jax.ShapeDtypeStruct((2 * routed_rows, half), BF16),
            jax.ShapeDtypeStruct((half, routed_rows), BF16),
            jax.ShapeDtypeStruct((half, columns), F32),
        ]
        + [jax.ShapeDtypeStruct((handed, columns), BF16)] * (2 if handed else 0),
        compiler_params=params(12 + routed_rows // 48),
        name="join_slots",
    )(*arrived, *drift_in)
    relays = [swap(v, "island", 2 - n) for n, v in enumerate(relays)]

    joined_all = [joined] + [swap(joined, "tensor", t) for t in range(1, parts)]

    def send_features(d):
        pairs = []
        for at in range(islands):
            to = partner(at, d, islands)
            pairs.append((at * parts + to // across, to * parts + to // across))
        return lax.ppermute(turned, ("island", "tensor"), pairs)

    def spread(value):
        result = value
        for t in range(1, parts):
            pairs = []
            for at in range(islands):
                keep = at // across
                pairs.append((at * parts + keep, at * parts + partner(keep, t, parts)))
            moved = lax.ppermute(value, ("island", "tensor"), pairs)
            result = moved if t == 1 else result + moved
        return result

    features_in = [send_features(d) for d in range(1, islands)]

    hidden_piece = jax.ShapeDtypeStruct((routed_rows, columns), BF16)
    *hidden_out, norms = pl.pallas_call(
        lambda *refs: hidden_kernel(parts, across, *refs),
        in_specs=[SMEM] + [ANY] * (2 + parts),
        out_specs=[VMEM] * (across + 1),
        out_shape=[hidden_piece] * across + [jax.ShapeDtypeStruct((devices, 8, 128), F32)],
        scratch_shapes=[
            pltpu.VMEM((across, features, columns), BF16),
            pltpu.VMEM((across, columns, features), BF16),
            pltpu.VMEM((parts, 2 * routed_rows, half), BF16),
            pltpu.SemaphoreType.DMA((parts + 2 * across,)),
        ],
        compiler_params=params(16 + routed_rows // 48),
        name="hidden_grads",
    )(spot, gate_weight, down_weight, *joined_all)

    def hidden_for(d):
        at = partner(island, d, islands) % across
        if islands & (islands - 1) == 0:
            return hidden_out[d % across]
        return lax.select_n((at - island) % across, *hidden_out)

    hidden_of = [hidden_out[0]] + [
        swap(hidden_for(d), "island", d) for d in range(1, islands)
    ]
    norms, features_in = pl.pallas_call(
        lambda *refs: hand_kernel(islands, *refs),
        in_specs=[ANY] * (islands + 1 + len(relays)),
        out_specs=[ANY] * 2,
        out_shape=[
            jax.ShapeDtypeStruct(norms.shape, F32),
            jax.ShapeDtypeStruct((islands, half, routed_rows), BF16),
        ],
        scratch_shapes=[pltpu.SemaphoreType.DMA((islands + 1,))],
        compiler_params=params(2),
        name="hand_features",
    )(norms, turned, *features_in, *relays)
    features_moved = spread(features_in)
    norms = lax.all_to_all(norms, AXES, split_axis=0, concat_axis=0, tiled=True)

    scaled, notes = pl.pallas_call(
        lambda *refs: average_kernel(islands, entries, 4, len(relays), *refs),
        in_specs=[SMEM, VMEM] + [ANY] * (3 + islands + len(relays)),
        out_specs=[VMEM] * 2,
        out_shape=[
            jax.ShapeDtypeStruct((half, columns), F32),
            jax.ShapeDtypeStruct((devices, 8, 128), F32),
        ],
        scratch_shapes=[
            pltpu.VMEM((islands, half, routed_rows), BF16),
            pltpu.VMEM((islands, routed_rows, columns), BF16),
            pltpu.VMEM((half, columns), F32),
            pltpu.VMEM((half, columns), BF16),
            pltpu.SemaphoreType.DMA((5, islands + 2)),
        ],
        compiler_params=params(8 + routed_rows // 48),
        name="average_block",
    )(spot, norms, drift_sum, features_in, features_moved, *hidden_of, *relays)
    notes = lax.all_to_all(notes, AXES, split_axis=0, concat_axis=0, tiled=True)

    first, second = scaled[: half // 2], scaled[half // 2 :]
    sent = [first.astype(WIRE), second.astype(WIRE)]
    own = lax.reduce_precision(scaled, 5, 10)

    def places(at, pieces, n):
        source = (at * experts + expert) * parts + part
        top = (at // across) * pieces + n
        return jnp.stack([top, at % across, source]).astype(jnp.int32)

    def update(outs, pieces):
        spots = [places(origin(island, d, islands), *n) for d, n, _ in pieces]
        values = [v.astype(F32) for _, _, v in pieces]
        return update_pieces(entries, spots, notes, momentum, values, outs)

    outs = update([], [(0, (1, 0), own)])
    if islands == 4:
        later = pl.pallas_call(
            lambda *refs: pass_kernel(2, *refs),
            in_specs=[ANY] * 3,
            out_specs=[ANY] * 2,
            out_shape=[jax.ShapeDtypeStruct(first.shape, F32)] * 2,
            scratch_shapes=[pltpu.SemaphoreType.DMA((2,))],
            compiler_params=params(2),
            name="pass_halves",
        )(notes, first, second)
        later = [h.astype(WIRE) for h in later]
        beside = swap(sent[0], "island", 1)
        below = swap(sent[1], "island", 2)
        far = [swap(beside, "island", 2), swap(below, "island", 1)]
        crossed = [swap(later[0], "island", 2), swap(later[1], "island", 1)]
        outs = update(outs, [(1, (2, 0), beside), (2, (2, 1), below)])
        outs = update(outs, [(2, (2, 0), crossed[0]), (1, (2, 1), crossed[1])])
        outs = update(outs, [(3, (2, 0), far[0]), (3, (2, 1), far[1])])
    else:
        for d in range(1, islands):
            moved = [swap(h, "island", d) for h in sent]
            outs = update(outs, [(d, (2, n), h) for n, h in enumerate(moved)])
    return tuple(outs)


def solution(mesh):
    return jax.shard_map(
        body,
        mesh=mesh,
        in_specs=(
            P("island", "expert", "tensor"),
            P("island", "expert", "tensor"),
            P("island", "expert", None, None),
            P("island", "expert", None),
            P("island", "expert", None, None),
            P("island", "expert", None, "tensor"),
            P("island", "expert", "tensor", None),
            P("island", "expert", None, "tensor"),
            P("expert", None, "tensor"),
        ),
        out_specs=(P("expert", None, "tensor"), P("expert", None, "tensor")),
        check_vma=False,
    )
```

time: 164 us -> 248 us (1.51)
  Pallas kernels: 32.3 us -> 133 us
  blocking collectives: 0 us -> 31.3 us
  starting transfers between devices: 53 us -> 29 us
  local copies, waits for them, and re-layouts: 16.5 us -> 3 us
  waiting for transfers between devices: 51.1 us -> 46.1 us
  other arithmetic: 9.38 us -> 4.92 us
    pallas_call x12 -> x8, Pallas kernels: 24.2 us -> 125 us  [the longest x1 98.5 us: body(): pl.pallas_call(lambda *refs: pick_kernel(experts, islands, pieces, *refs)...]
    all_to_all x0 -> x2, blocking collectives: none -> 31.3 us  [the longest x1 17.3 us: body(): norms = lax.all_to_all(norms, AXES, split_axis=0, concat_axis=0, tiled=True)]
    ppermute x16 -> x17, waiting for transfers between devices: 21.7 us -> 46.1 us  [swap(): lax.ppermute(value, axis, [(at, partner(at, step, size)) for at in range(...]
    all_to_all x2 -> x0, waiting for transfers between devices: 17.6 us -> none  [the longest x1 9.89 us: body(): norms = lax.all_to_all(norms, AXES, split_axis=0, concat_axis=0, tiled=True)]
    unnamed x30 -> x10, local copies, waits for them, and re-layouts: 16.4 us -> 2.14 us
    ppermute x16 -> x17, starting transfers between devices: 36.6 us -> 22.5 us  [swap(): lax.ppermute(value, axis, [(at, partner(at, step, size)) for at in range(...]
    ppermute x3, waiting for transfers between devices: 11.7 us -> 0.01 us  [send_features(): return lax.ppermute(turned, ('island', 'tensor'), pairs)]
    all_to_all x2 -> x0, starting transfers between devices: 5.5 us -> none  [the longest x1 2.84 us: body(): notes = lax.all_to_all(notes, AXES, split_axis=0, concat_axis=0, tiled=True)]
  transfers between devices with their start and end apart: 23 -> 21, of which waited for: 7 -> 6; matrix products, arithmetic and copies ran while one was open for 4% -> 2% of each run, Pallas kernels for 12% -> 7%
where the time goes in v4:
time: 248 us
  Pallas kernels  133 us (54%)
  waiting for transfers between devices  46.1 us (19%)
  blocking collectives  31.3 us (13%)
  starting transfers between devices  29 us (12%)
  other arithmetic  4.92 us (2%)
  local copies, waits for them, and re-layouts  3 us (1%)
    pallas_call x1, Pallas kernels, body(): pl.pallas_call(lambda *refs: pick_kernel(experts, islands, pieces, *refs)...  98.5 us
    ppermute x17, waiting for transfers between devices, swap(): lax.ppermute(value, axis, [(at, partner(at, step, size)) for at in range(...  46.1 us
    ppermute x17, starting transfers between devices, swap(): lax.ppermute(value, axis, [(at, partner(at, step, size)) for at in range(...  22.5 us
    all_to_all x1, blocking collectives, body(): norms = lax.all_to_all(norms, AXES, split_axis=0, concat_axis=0, tiled=True)  17.3 us
    pallas_call x4, Pallas kernels, update_pieces(): pl.pallas_call(lambda *refs: update_kernel(entries, count, *refs), in_spe...  14.1 us
    all_to_all x1, blocking collectives, body(): notes = lax.all_to_all(notes, AXES, split_axis=0, concat_axis=0, tiled=True)  14 us
    pallas_call x1, Pallas kernels, body(): pl.pallas_call(lambda *refs: average_kernel(islands, entries, 4, len(rela...  11.7 us
    pallas_call x1, Pallas kernels, body(): pl.pallas_call(lambda *refs: hidden_kernel(parts, across, *refs), in_spec...  7.07 us
  transfers between devices with their start and end apart: 21, of which 6 were waited for; matrix products, arithmetic and copies ran while one was open for 2% of the time, Pallas kernels for 7%

profile of v4, /device:TPU:0, one launch (start us, length us, event | category | flops | bytes accessed | tf_op | source)
XLA Modules:
  0.0 247.9 jit_solution(9089603171334089660)
XLA Ops:
  0.7 0.6 stack.83.refs_0_
  1.3 98.5 %pick_slots.1 = (bf16[192,1024]{1,0:T(8,128)(2,1)}, bf16[192,1024]{1,0:T(8,128)(2,1)}, bf16[192,1024]{1,0:T(8,128)(2,1)}, bf16[192,1024]{1,0:T(8,128)(2,1)}, bf1...) custom-call(s32[6]{0:T(128)} %stack.83.refs_0_, s32[1,1,4,96]{3,2,1,0:T(4,128)} %refs_1_.2, ...), custom_call_target="tpu_custom_call" | custom-call | tf_op jit(solution)/shard_map/pick_slots/pallas_call | solution.py:308
  99.7 0.0 copy-start
  99.7 3.0 %collective-permute-start.3 = (bf16[1536,384]{1,0:T(8,128)(2,1)}, bf16[1536,384]{1,0:T(8,128)(2,1)S(1)}, u32[]{:S(2)}, u32[]{:S(2)}) collective-permute-start(bf16[1536,384]{1,0:T(8,128)(2,1)} %get-tuple-element.34), channel_id=1, source_target_pairs={{0,8},{8,0},{16,24},{24,16},{1,9},{9,1},{17,25},{25,17},{2,10},{10... | collective-permute-start | bytes 3538952 | tf_op jit(solution)/shard_map/ppermute | solution.py:34
  102.7 1.5 collective-permute-start.4
  104.3 1.6 collective-permute-start
  105.8 2.6 %collective-permute-start.1 = (bf16[192,1024]{1,0:T(8,128)(2,1)}, bf16[192,1024]{1,0:T(8,128)(2,1)S(1)}, u32[]{:S(2)}, u32[]{:S(2)}) collective-permute-start(bf16[192,1024]{1,0:T(8,128)(2,1)} %get-tuple-element.31), channel_id=1, source_target_pairs={{0,4},{2,6},{4,0},{6,2},{1,5},{3,7},{5,1},{7,3},{8,12},{10,14},{12... | collective-permute-start | bytes 1179656 | tf_op jit(solution)/shard_map/ppermute | solution.py:34
  108.4 0.2 collective-permute-start.2
  108.7 13.5 %collective-permute-done.refs_1_ = bf16[192,1024]{1,0:T(8,128)(2,1)S(1)} collective-permute-done((bf16[192,1024]{1,0:T(8,128)(2,1)}, bf16[192,1024]{1,0:T(8,128)(2,1)S(1)}, u32[]{:S(2)}, u32[]{:S(2)}) %collective-permute-start) | collective-permute-done | bytes 393248 | tf_op jit(solution)/shard_map/ppermute | solution.py:34
  122.1 13.7 %collective-permute-done.1.refs_2_ = bf16[192,1024]{1,0:T(8,128)(2,1)S(1)} collective-permute-done((bf16[192,1024]{1,0:T(8,128)(2,1)}, bf16[192,1024]{1,0:T(8,128)(2,1)S(1)}, u32[]{:S(2)}, u32[]{:S(2)}) %collective-permute-start.1) | collective-permute-done | bytes 393248 | tf_op jit(solution)/shard_map/ppermute | solution.py:34
  135.9 0.0 collective-permute-done.2.refs_3_
  135.9 0.0 collective-permute-done.3.refs_5_
  135.9 0.0 collective-permute-done.4.refs_6_
  135.9 1.1 copy-done.2
  137.0 1.0 copy-done.3
  138.0 0.7 join_slots.1
  138.7 0.1 collective-permute-start.5
  138.8 2.4 collective-permute-start.6
  141.3 1.3 collective-permute-start.7
  142.6 1.3 collective-permute-start.8
  143.9 1.6 collective-permute-start.10
  145.4 2.7 %collective-permute-start.9 = (bf16[512,384]{1,0:T(8,128)(2,1)S(1)}, bf16[512,384]{1,0:T(8,128)(2,1)S(1)}, u32[]{:S(2)}, u32[]{:S(2)}) collective-permute-start(bf16[512,384]{1,0:T(8,128)(2,1)S(1)} %get-tuple-element.39), channel_id=1, source_target_pairs={{0,16},{8,24},{16,0},{24,8},{1,17},{9,25},{17,1},{25,9},{2,18},{10... | collective-permute-start | bytes 1179656 | tf_op jit(solution)/shard_map/ppermute | solution.py:34
  148.2 7.1 %hidden_grads.1 = (bf16[384,384]{1,0:T(8,128)(2,1)S(1)}, bf16[384,384]{1,0:T(8,128)(2,1)S(1)}, f32[32,8,128]{2,1,0:T(8,128)S(1)}) custom-call(s32[6]{0:T(128)S(1)} %copy-done.4, bf16[1,1,2048,768]{3,2,1,0:T(8,128)(2,1)S(1)} %copy-done, bf16[1,1,768,2048]{3,2,1,0:T(8,128)(2,1)S(1)} %copy-done.1, bf16[768,1024]{1,0:T(8,128)(2,1)S(1)} %get-tuple-element.36.refs_3_, ...), custom_call_target="tpu_custom_call" | custom-call | tf_op jit(solution)/shard_map/hidden_grads/pallas_call | solution.py:366
  155.3 11.2 %collective-permute-done.10.refs_6_.refs_10_ = bf16[512,384]{1,0:T(8,128)(2,1)S(1)} collective-permute-done((bf16[512,384]{1,0:T(8,128)(2,1)S(1)}, bf16[512,384]{1,0:T(8,128)(2,1)S(1)}, u32[]{:S(2)}, u32[]{:S(2)}) %collective-permute-start.10) | collective-permute-done | bytes 393248 | tf_op jit(solution)/shard_map/ppermute | solution.py:34
  166.5 5.5 %collective-permute-done.9.refs_5_.refs_9_ = bf16[512,384]{1,0:T(8,128)(2,1)S(1)} collective-permute-done((bf16[512,384]{1,0:T(8,128)(2,1)S(1)}, bf16[512,384]{1,0:T(8,128)(2,1)S(1)}, u32[]{:S(2)}, u32[]{:S(2)}) %collective-permute-start.9) | collective-permute-done | bytes 393248 | tf_op jit(solution)/shard_map/ppermute | solution.py:34
  172.0 0.0 collective-permute-done.6.refs_2_
  172.0 0.0 collective-permute-done.7.refs_3_
  172.0 0.0 collective-permute-done.8.refs_4_
  172.0 0.4 hand_features.1
  172.5 1.5 collective-permute-start.11
  174.0 1.6 collective-permute-start.12
  175.5 0.0 collective-permute-start.13
  175.5 2.0 collective-permute-start.14
  177.5 17.3 %all_to_all.10.refs_1_ = f32[32,8,128]{2,1,0:T(8,128)S(1)} all-to-all(f32[32,8,128]{2,1,0:T(8,128)S(1)} %get-tuple-element.41), channel_id=1, replica_groups=mesh['island'=4,'expert'=4,'tensor'=2] {'island','expert','tensor'}, dimensions={0} | all-to-all | bytes 262144 | tf_op jit(solution)/shard_map/all_to_all | solution.py:403
  194.8 0.0 collective-permute-done.11.refs_4_
  194.8 11.7 %average_block.1 = (f32[1024,384]{1,0:T(8,128)S(1)}, f32[32,8,128]{2,1,0:T(8,128)S(1)}) custom-call(s32[6]{0:T(128)S(1)} %copy-done.4, f32[32,8,128]{2,1,0:T(8,128)S(1)} %all_to_all.10.refs_1_, f32[1024,384]{1,0:T(8,128)S(1)} %get-tuple-element.42.refs_2_, bf16[4,1024,384]{2,1,0:T(8,128)(2,1)S(1)} %get-tuple-element.43.refs_3_, ...), custom_call_target="tpu_custom_call" | custom-call | tf_op jit(solution)/shard_map/average_block/pallas_call | solution.py:405
  206.5 0.2 fusion
  206.7 0.9 collective-permute-start.15
  207.6 0.7 collective-permute-start.17
  208.3 14.0 %all_to_all.11.refs_0_.refs_1_ = f32[32,8,128]{2,1,0:T(8,128)S(1)} all-to-all(f32[32,8,128]{2,1,0:T(8,128)S(1)} %get-tuple-element.46), channel_id=1, replica_groups=mesh['island'=4,'expert'=4,'tensor'=2] {'island','expert','tensor'}, dimensions={0} | all-to-all | bytes 262144 | tf_op jit(solution)/shard_map/all_to_all | solution.py:423
  222.3 0.1 pass_halves.1
  222.5 0.8 convert_element_type.35
  223.3 0.8 collective-permute-start.19
  224.1 0.8 convert_element_type.37
  224.9 0.7 collective-permute-start.20
  225.6 1.3 collective-permute-start.16
  227.0 1.2 collective-permute-start.18
  228.2 0.1 concatenate.11.refs_0_
  228.2 0.1 concatenate.10.refs_0_
  228.3 0.1 concatenate.9.refs_0_
  228.4 0.1 pad_add_fusion.refs_0_
  228.5 0.7 reduce_precision.3.refs_3_
  229.2 3.9 %update_pieces.4 = (f32[1,2048,768]{2,1,0:T(8,128)}, bf16[1,2048,768]{2,1,0:T(8,128)(2,1)}) custom-call(s32[3]{0:T(128)S(1)} %pad_add_fusion.refs_0_, f32[32,8,128]{2,1,0:T(8,128)S(1)} %all_to_all.11.refs_0_.refs_1_, f32[1,2048,768]{2,1,0:T(8,128)} %refs_2_.11, f32[1024,384]{1,0:T(8,128)S(1)} %reduce_precision.3.refs_3_), custom_call_target="tpu_custom_call" | custom-call | tf_op jit(solution)/shard_map/update_pieces/pallas_call | solution.py:255
  233.1 0.1 convert_element_type.39.refs_3_
  233.1 0.1 convert_element_type.40.refs_4_
  233.2 3.4 %update_pieces.5 = (f32[1,2048,768]{2,1,0:T(8,128)}, bf16[1,2048,768]{2,1,0:T(8,128)(2,1)}) custom-call(s32[6]{0:T(128)S(1)} %concatenate.11.refs_0_, f32[32,8,128]{2,1,0:T(8,128)S(1)} %all_to_all.11.refs_0_.refs_1_, f32[1,2048,768]{2,1,0:T(8,128)} %refs_2_.11, ...), custom_call_target="tpu_custom_call", output_to_operand_aliasing={{0}: (5, {}), {1}: (6, {})} | custom-call | tf_op jit(solution)/shard_map/update_pieces/pallas_call | solution.py:255
  236.6 1.0 convert_element_type.36.refs_3_
  237.7 1.0 convert_element_type.38.refs_4_
  238.7 3.4 %update_pieces.6 = (f32[1,2048,768]{2,1,0:T(8,128)}, bf16[1,2048,768]{2,1,0:T(8,128)(2,1)}) custom-call(s32[6]{0:T(128)S(1)} %concatenate.10.refs_0_, f32[32,8,128]{2,1,0:T(8,128)S(1)} %all_to_all.11.refs_0_.refs_1_, f32[1,2048,768]{2,1,0:T(8,128)} %refs_2_.11, ...), custom_call_target="tpu_custom_call", output_to_operand_aliasing={{0}: (5, {}), {1}: (6, {})} | custom-call | tf_op jit(solution)/shard_map/update_pieces/pallas_call | solution.py:255
  242.1 1.1 collective-permute-done.16
  243.3 0.1 convert_element_type.32.refs_3_
  243.3 1.0 collective-permute-done.18
  244.3 0.1 convert_element_type.34.refs_4_
  244.4 3.4 %update_pieces.7 = (f32[1,2048,768]{2,1,0:T(8,128)}, bf16[1,2048,768]{2,1,0:T(8,128)(2,1)}) custom-call(s32[6]{0:T(128)S(1)} %concatenate.9.refs_0_, f32[32,8,128]{2,1,0:T(8,128)S(1)} %all_to_all.11.refs_0_.refs_1_, f32[1,2048,768]{2,1,0:T(8,128)} %refs_2_.11, ...), custom_call_target="tpu_custom_call", output_to_operand_aliasing={{0}: (5, {}), {1}: (6, {})} | custom-call | tf_op jit(solution)/shard_map/update_pieces/pallas_call | solution.py:255
  (15 shorter events, 0.0 us)
Async XLA Ops:
  1.3 146.9 %copy-start.1 = (bf16[1,1,768,2048]{3,2,1,0:T(8,128)(2,1)S(1)}, bf16[1,1,768,2048]{3,2,1,0:T(8,128)(2,1)}, u32[]{:S(2)}) copy-start(bf16[1,1,768,2048]{3,2,1,0:T(8,128)(2,1)} %refs_2_.7) | copy-start | bytes 9437188
  1.3 146.9 %copy-start.4 = (s32[6]{0:T(128)S(1)}, s32[6]{0:T(128)}, u32[]{:S(2)}) copy-start(s32[6]{0:T(128)} %stack.83.refs_0_) | copy-start | bytes 76
  99.7 48.4 %copy-start = (bf16[1,1,2048,768]{3,2,1,0:T(8,128)(2,1)S(1)}, bf16[1,1,2048,768]{3,2,1,0:T(8,128)(2,1)}, u32[]{:S(2)}) copy-start(bf16[1,1,2048,768]{3,2,1,0:T(8,128)(2,1)} %refs_1_.3) | copy-start | bytes 9437188
  99.7 36.1 %collective-permute-start.3 = (bf16[1536,384]{1,0:T(8,128)(2,1)}, bf16[1536,384]{1,0:T(8,128)(2,1)S(1)}, u32[]{:S(2)}, u32[]{:S(2)}) collective-permute-start(bf16[1536,384]{1,0:T(8,128)(2,1)} %get-tuple-element.34), channel_id=1, source_target_pairs={{0,8},{8,0},{16,24},{24,16},{1,9},{9,1},{17,25},{25,17},{2,10},{10... | collective-permute-start | bytes 3538952 | tf_op jit(solution)/shard_map/ppermute | solution.py:34
  102.7 33.1 %collective-permute-start.4 = (bf16[1536,384]{1,0:T(8,128)(2,1)}, bf16[1536,384]{1,0:T(8,128)(2,1)S(1)}, u32[]{:S(2)}, u32[]{:S(2)}) collective-permute-start(bf16[1536,384]{1,0:T(8,128)(2,1)} %get-tuple-element.35), channel_id=1, source_target_pairs={{0,16},{8,24},{16,0},{24,8},{1,17},{9,25},{17,1},{25,9},{2,18},{10... | collective-permute-start | bytes 3538952 | tf_op jit(solution)/shard_map/ppermute | solution.py:34
  104.3 17.9 %collective-permute-start = (bf16[192,1024]{1,0:T(8,128)(2,1)}, bf16[192,1024]{1,0:T(8,128)(2,1)S(1)}, u32[]{:S(2)}, u32[]{:S(2)}) collective-permute-start(bf16[192,1024]{1,0:T(8,128)(2,1)} %get-tuple-element.30), channel_id=1, source_target_pairs={{0,2},{2,0},{4,6},{6,4},{1,3},{3,1},{5,7},{7,5},{8,10},{10,8},{12,... | collective-permute-start | bytes 1179656 | tf_op jit(solution)/shard_map/ppermute | solution.py:34
  105.8 30.0 %collective-permute-start.1 = (bf16[192,1024]{1,0:T(8,128)(2,1)}, bf16[192,1024]{1,0:T(8,128)(2,1)S(1)}, u32[]{:S(2)}, u32[]{:S(2)}) collective-permute-start(bf16[192,1024]{1,0:T(8,128)(2,1)} %get-tuple-element.31), channel_id=1, source_target_pairs={{0,4},{2,6},{4,0},{6,2},{1,5},{3,7},{5,1},{7,3},{8,12},{10,14},{12... | collective-permute-start | bytes 1179656 | tf_op jit(solution)/shard_map/ppermute | solution.py:34
  108.4 27.4 %collective-permute-start.2 = (bf16[192,1024]{1,0:T(8,128)(2,1)}, bf16[192,1024]{1,0:T(8,128)(2,1)S(1)}, u32[]{:S(2)}, u32[]{:S(2)}) collective-permute-start(bf16[192,1024]{1,0:T(8,128)(2,1)} %get-tuple-element.32), channel_id=1, source_target_pairs={{0,6},{2,4},{4,2},{6,0},{1,7},{3,5},{5,3},{7,1},{8,14},{10,12},{12... | collective-permute-start | bytes 1179656 | tf_op jit(solution)/shard_map/ppermute | solution.py:34
  135.9 1.1 copy-start.2
  137.0 1.0 copy-start.3
  138.7 6.7 %collective-permute-start.5 = (bf16[768,1024]{1,0:T(8,128)(2,1)S(1)}, bf16[768,1024]{1,0:T(8,128)(2,1)S(1)}, u32[]{:S(2)}, u32[]{:S(2)}) collective-permute-start(bf16[768,1024]{1,0:T(8,128)(2,1)S(1)} %get-tuple-element.36.refs_3_), channel_id=1, source_target_pairs={{0,1},{1,0},{2,3},{3,2},{4,5},{5,4},{6,7},{7,6},{8,9},{9,8},{10,11... | collective-permute-start | bytes 4718600 | tf_op jit(solution)/shard_map/ppermute | solution.py:34
  138.8 33.2 %collective-permute-start.6 = (bf16[1024,384]{1,0:T(8,128)(2,1)S(1)}, bf16[1024,384]{1,0:T(8,128)(2,1)S(1)}, u32[]{:S(2)}, u32[]{:S(2)}) collective-permute-start(bf16[1024,384]{1,0:T(8,128)(2,1)S(1)} %get-tuple-element.38.refs_1_), channel_id=1, source_target_pairs={{0,8},{8,0},{17,25},{25,17},{2,10},{10,2},{19,27},{27,19},{4,12},{... | collective-permute-start | bytes 2359304 | tf_op jit(solution)/shard_map/ppermute | solution.py:350
  141.3 30.7 %collective-permute-start.7 = (bf16[1024,384]{1,0:T(8,128)(2,1)S(1)}, bf16[1024,384]{1,0:T(8,128)(2,1)S(1)}, u32[]{:S(2)}, u32[]{:S(2)}) collective-permute-start(bf16[1024,384]{1,0:T(8,128)(2,1)S(1)} %get-tuple-element.38.refs_1_), channel_id=1, source_target_pairs={{1,17},{9,25},{16,0},{24,8},{3,19},{11,27},{18,2},{26,10},{5,21},{... | collective-permute-start | bytes 2359304 | tf_op jit(solution)/shard_map/ppermute | solution.py:350
  142.6 29.4 %collective-permute-start.8 = (bf16[1024,384]{1,0:T(8,128)(2,1)S(1)}, bf16[1024,384]{1,0:T(8,128)(2,1)S(1)}, u32[]{:S(2)}, u32[]{:S(2)}) collective-permute-start(bf16[1024,384]{1,0:T(8,128)(2,1)S(1)} %get-tuple-element.38.refs_1_), channel_id=1, source_target_pairs={{1,25},{9,17},{16,8},{24,0},{3,27},{11,19},{18,10},{26,2},{5,29},{... | collective-permute-start | bytes 2359304 | tf_op jit(solution)/shard_map/ppermute | solution.py:350
  143.9 22.6 %collective-permute-start.10 = (bf16[512,384]{1,0:T(8,128)(2,1)S(1)}, bf16[512,384]{1,0:T(8,128)(2,1)S(1)}, u32[]{:S(2)}, u32[]{:S(2)}) collective-permute-start(bf16[512,384]{1,0:T(8,128)(2,1)S(1)} %get-tuple-element.40), channel_id=1, source_target_pairs={{0,8},{8,0},{16,24},{24,16},{1,9},{9,1},{17,25},{25,17},{2,10},{10... | collective-permute-start | bytes 1179656 | tf_op jit(solution)/shard_map/ppermute | solution.py:34
  145.4 26.6 %collective-permute-start.9 = (bf16[512,384]{1,0:T(8,128)(2,1)S(1)}, bf16[512,384]{1,0:T(8,128)(2,1)S(1)}, u32[]{:S(2)}, u32[]{:S(2)}) collective-permute-start(bf16[512,384]{1,0:T(8,128)(2,1)S(1)} %get-tuple-element.39), channel_id=1, source_target_pairs={{0,16},{8,24},{16,0},{24,8},{1,17},{9,25},{17,1},{25,9},{2,18},{10... | collective-permute-start | bytes 1179656 | tf_op jit(solution)/shard_map/ppermute | solution.py:34
  172.5 22.3 %collective-permute-start.11 = (bf16[4,1024,384]{2,1,0:T(8,128)(2,1)S(1)}, bf16[4,1024,384]{2,1,0:T(8,128)(2,1)S(1)}, u32[]{:S(2)}, u32[]{:S(2)}) collective-permute-start(bf16[4,1024,384]{2,1,0:T(8,128)(2,1)S(1)} %get-tuple-element.43.refs_3_), channel_id=1, source_target_pairs={{0,1},{8,9},{17,16},{25,24},{2,3},{10,11},{19,18},{27,26},{4,5},{1... | collective-permute-start | bytes 9437192 | tf_op jit(solution)/shard_map/ppermute | solution.py:359
  174.0 20.8 %collective-permute-start.12 = (bf16[384,384]{1,0:T(8,128)(2,1)S(1)}, bf16[384,384]{1,0:T(8,128)(2,1)S(1)}, u32[]{:S(2)}, u32[]{:S(2)}) collective-permute-start(bf16[384,384]{1,0:T(8,128)(2,1)S(1)} %get-tuple-element.45), channel_id=1, source_target_pairs={{0,8},{8,0},{16,24},{24,16},{1,9},{9,1},{17,25},{25,17},{2,10},{10... | collective-permute-start | bytes 884744 | tf_op jit(solution)/shard_map/ppermute | solution.py:34
  175.5 19.3 %collective-permute-start.13 = (bf16[384,384]{1,0:T(8,128)(2,1)S(1)}, bf16[384,384]{1,0:T(8,128)(2,1)S(1)}, u32[]{:S(2)}, u32[]{:S(2)}) collective-permute-start(bf16[384,384]{1,0:T(8,128)(2,1)S(1)} %get-tuple-element.44.refs_5_), channel_id=1, source_target_pairs={{0,16},{8,24},{16,0},{24,8},{1,17},{9,25},{17,1},{25,9},{2,18},{10... | collective-permute-start | bytes 884744 | tf_op jit(solution)/shard_map/ppermute | solution.py:34
  175.5 19.3 %collective-permute-start.14 = (bf16[384,384]{1,0:T(8,128)(2,1)S(1)}, bf16[384,384]{1,0:T(8,128)(2,1)S(1)}, u32[]{:S(2)}, u32[]{:S(2)}) collective-permute-start(bf16[384,384]{1,0:T(8,128)(2,1)S(1)} %get-tuple-element.45), channel_id=1, source_target_pairs={{0,24},{8,16},{16,8},{24,0},{1,25},{9,17},{17,9},{25,1},{2,26},{10... | collective-permute-start | bytes 884744 | tf_op jit(solution)/shard_map/ppermute | solution.py:34
  206.7 18.9 %collective-permute-start.15 = (f16[512,384]{1,0:T(8,128)(2,1)S(1)}, f16[512,384]{1,0:T(8,128)(2,1)S(1)}, u32[]{:S(2)}, u32[]{:S(2)}) collective-permute-start(f16[512,384]{1,0:T(8,128)(2,1)S(1)} %get-tuple-element.57), channel_id=1, source_target_pairs={{0,8},{8,0},{16,24},{24,16},{1,9},{9,1},{17,25},{25,17},{2,10},{10... | collective-permute-start | bytes 1179656 | tf_op jit(solution)/shard_map/ppermute | solution.py:34
  207.6 19.4 %collective-permute-start.17 = (f16[512,384]{1,0:T(8,128)(2,1)S(1)}, f16[512,384]{1,0:T(8,128)(2,1)S(1)}, u32[]{:S(2)}, u32[]{:S(2)}) collective-permute-start(f16[512,384]{1,0:T(8,128)(2,1)S(1)} %get-tuple-element.58), channel_id=1, source_target_pairs={{0,16},{8,24},{16,0},{24,8},{1,17},{9,25},{17,1},{25,9},{2,18},{10... | collective-permute-start | bytes 1179656 | tf_op jit(solution)/shard_map/ppermute | solution.py:34
  223.3 13.3 %collective-permute-start.19 = (f16[512,384]{1,0:T(8,128)(2,1)}, f16[512,384]{1,0:T(8,128)(2,1)}, u32[]{:S(2)}, u32[]{:S(2)}) collective-permute-start(f16[512,384]{1,0:T(8,128)(2,1)} %convert_element_type.35), channel_id=1, source_target_pairs={{0,16},{8,24},{16,0},{24,8},{1,17},{9,25},{17,1},{25,9},{2,18},{10... | collective-permute-start | bytes 1179656 | tf_op jit(solution)/shard_map/ppermute | solution.py:34
  224.9 12.7 %collective-permute-start.20 = (f16[512,384]{1,0:T(8,128)(2,1)}, f16[512,384]{1,0:T(8,128)(2,1)}, u32[]{:S(2)}, u32[]{:S(2)}) collective-permute-start(f16[512,384]{1,0:T(8,128)(2,1)} %convert_element_type.37), channel_id=1, source_target_pairs={{0,8},{8,0},{16,24},{24,16},{1,9},{9,1},{17,25},{25,17},{2,10},{10... | collective-permute-start | bytes 1179656 | tf_op jit(solution)/shard_map/ppermute | solution.py:34
  225.6 17.6 %collective-permute-start.16 = (f16[512,384]{1,0:T(8,128)(2,1)S(1)}, f16[512,384]{1,0:T(8,128)(2,1)S(1)}, u32[]{:S(2)}, u32[]{:S(2)}) collective-permute-start(f16[512,384]{1,0:T(8,128)(2,1)S(1)} %collective-permute-done.15), channel_id=1, source_target_pairs={{0,16},{8,24},{16,0},{24,8},{1,17},{9,25},{17,1},{25,9},{2,18},{10... | collective-permute-start | bytes 1179656 | tf_op jit(solution)/shard_map/ppermute | solution.py:34
  227.0 17.4 %collective-permute-start.18 = (f16[512,384]{1,0:T(8,128)(2,1)S(1)}, f16[512,384]{1,0:T(8,128)(2,1)S(1)}, u32[]{:S(2)}, u32[]{:S(2)}) collective-permute-start(f16[512,384]{1,0:T(8,128)(2,1)S(1)} %collective-permute-done.17), channel_id=1, source_target_pairs={{0,8},{8,0},{16,24},{24,16},{1,9},{9,1},{17,25},{25,17},{2,10},{10... | collective-permute-start | bytes 1179656 | tf_op jit(solution)/shard_map/ppermute | solution.py:34

commit v5 on v4

v5 whole, which is shorter than its diff:
```python
import math

import jax
import jax.numpy as jnp
from jax import lax
from jax.experimental import pallas as pl
from jax.experimental.pallas import tpu as pltpu
from jax.sharding import PartitionSpec as P

F32 = jnp.float32
BF16 = jnp.bfloat16
WIRE = jnp.float16
AXES = ("island", "expert", "tensor")

VMEM = pl.BlockSpec(memory_space=pltpu.VMEM)
SMEM = pl.BlockSpec(memory_space=pltpu.SMEM)
ANY = pl.BlockSpec(memory_space=pl.ANY)


def params(mib):
    return pltpu.CompilerParams(vmem_limit_bytes=mib << 20)


def partner(at, step, size):
    return at ^ step if size & (size - 1) == 0 else (at + step) % size


def origin(at, step, size):
    return at ^ step if size & (size - 1) == 0 else (at - step) % size


def swap(value, axis, step):
    size = lax.axis_size(axis)
    return lax.ppermute(value, axis, [(at, partner(at, step, size)) for at in range(size)])


def dot(a, b, contract):
    return lax.dot_general(a, b, (contract, ((), ())), preferred_element_type=F32)


def copy_all(sems, pairs):
    copies = [pltpu.make_async_copy(*pair, sems.at[n]) for n, pair in enumerate(pairs)]
    for copy in copies:
        copy.start()
    return copies


def pick_kernel(experts, islands, pieces, spot, *refs):
    sources, drift = refs[:5], refs[5]
    outs, blocks = refs[6 : 6 + experts], refs[6 + experts : -6]
    table, count, weight, tokens, grads, sems = refs[-6:]
    loads = copy_all(sems, list(zip(sources, refs[-6:-1])))
    rows, columns = blocks[0].shape
    pairs = []
    for d, first, count_rows, target, at_row in pieces:
        at = partner(spot[3], d, islands)
        top = pl.multiple_of(lax.div(at, spot[4]) * rows, rows) + first
        left = pl.multiple_of(lax.rem(at, spot[4]) * columns, columns)
        pairs.append(
            (
                drift.at[0, 0, pl.ds(top, count_rows), pl.ds(left, columns)],
                blocks[target].at[pl.ds(at_row, count_rows)],
            )
        )
    copies = copy_all(sems.at[pl.ds(5, len(pairs))], pairs)
    for copy in loads:
        copy.wait()

    slots = table.shape[-1]
    rows = lax.broadcasted_iota(jnp.int32, (slots, slots), 0)
    lanes = lax.broadcasted_iota(jnp.int32, (slots, slots), 1)

    def column(row):
        return jnp.sum(jnp.where(rows == lanes, row, 0), axis=1, keepdims=True)

    for d in range(experts):
        to = partner(spot[0], d, experts)
        live = lax.broadcasted_iota(jnp.int32, (slots, 1), 0) < count[0, 0, to]
        token = column(table[0, 0, pl.ds(to, 1), :].astype(F32)).astype(jnp.int32)
        chance = column(weight[0, 0, pl.ds(to, 1), :])
        ids = lax.broadcasted_iota(jnp.int32, (slots, tokens.shape[1]), 1)
        picks = jnp.where((ids == token) & live, 1.0, 0.0).astype(BF16)
        outs[d][:slots, :] = dot(picks, tokens[0], ((1,), (0,))).astype(BF16)
        picked = dot(picks, grads[0], ((1,), (0,)))
        outs[d][slots:, :] = (chance * picked).astype(BF16)
    for copy in copies:
        copy.wait()


def join_kernel(count, blocks, *refs):
    arrived, drifts = refs[:count], refs[count : count + blocks]
    joined, turned, drift_sum = refs[count + blocks : count + blocks + 3]
    slots = arrived[0].shape[0] // 2
    rows = drift_sum.shape[0]
    for n, ref in enumerate(refs[count + blocks + 3 :]):
        ref[...] = drifts[1 + n][rows:, :]
    for n, piece in enumerate(arrived):
        joined[n * slots : (n + 1) * slots, :] = piece[:slots, :]
        joined[(count + n) * slots : (count + n + 1) * slots, :] = piece[slots:, :]
    turned[...] = joined[: count * slots, :].T
    added = drifts[0][...].astype(F32)
    for other in drifts[1:]:
        added = added + other[:rows, :].astype(F32)
    drift_sum[...] = added


def hidden_kernel(parts, across, spot, gate, down, *refs):
    joined, outs, norms = refs[:parts], refs[parts : parts + across], refs[-1]
    rows, half = joined[0].shape[0] // 2, joined[0].shape[1]
    columns = outs[0].shape[1]
    starts = [pl.multiple_of(origin(spot[1], t, parts) * half, half) for t in range(parts)]
    hidden_gram = 0.0
    for r in range(across):
        first = pl.multiple_of(partner(spot[2], r, across) * columns, columns)
        value = 0.0
        back = 0.0
        for t in range(parts):
            block = gate[0, 0, pl.ds(starts[t], half), pl.ds(first, columns)]
            value = value + dot(joined[t][:rows, :], block, ((1,), (0,)))
            block = down[0, 0, pl.ds(first, columns), pl.ds(starts[t], half)]
            back = back + dot(joined[t][rows:, :], block, ((1,), (1,)))
        rounded = (back * (value / (1.0 + jnp.exp(-value)))).astype(BF16)
        outs[r][...] = rounded
        hidden_gram = hidden_gram + dot(rounded, rounded, ((1,), (1,)))
    input_gram = 0.0
    for t in range(parts):
        features = joined[t][:rows, :]
        input_gram = input_gram + dot(features, features, ((1,), (1,)))
    norms[...] = jnp.full(norms.shape, jnp.sum(hidden_gram * input_gram), F32)


def average_kernel(islands, entries, tiles, spot, norms, drift_sum, own, moved, *refs):
    hiddens, handed = refs[:islands], refs[islands:-4]
    scaled, notes, total, square = refs[-4:]
    rows = total.shape[0] // tiles
    group = norms.shape[0] // islands
    scales = []
    for d in range(islands):
        at = origin(spot[3], d, islands)
        norm = jnp.sum(norms[pl.ds(at * group, group)], axis=0)[:1, :1]
        scales.append(jnp.minimum(1.0, math.sqrt(entries) / jnp.sqrt(norm + 1e-06)) / islands)

    def compute(features):
        squares = 0.0
        for m in range(tiles):
            part = slice(m * rows, (m + 1) * rows)
            average = drift_sum[part, :]
            if handed:
                size = handed[0].shape[0]
                n, first = divmod(m * rows, size)
                average = average + handed[n][first : first + rows, :].astype(F32)
            average = average * (1.0 / islands)
            for d in range(islands):
                average = average + scales[d] * dot(features[d, part, :], hiddens[d][...], ((1,), (0,)))
            total[part, :] = average
            squares = squares + jnp.sum(average * average, axis=0, keepdims=True)
        square[...] = squares

    pl.when(spot[5] == 1)(lambda: compute(own))
    pl.when(spot[5] != 1)(lambda: compute(moved))
    peak = jnp.max(jnp.abs(total[...]))
    unit = jnp.maximum(peak, 1e-30) / 32768
    scaled[...] = total[...] * (1 / unit)
    sublane = lax.broadcasted_iota(jnp.int32, notes.shape, 1)
    notes[...] = jnp.where(sublane == 0, jnp.sum(square[...]), unit)


def hand_kernel(count, norms, *refs):
    passed, joined = refs[-2:]
    for n in range(count):
        joined[n] = refs[n][...]
    passed[...] = norms[...]


def own_kernel(slots, block, slots_out, block_out):
    slots_out[...] = slots[...]
    block_out[...] = block[...]


def update_kernel(entries, pieces, place, notes, momentum, *refs):
    values = refs[: len(pieces)]
    new_momentum, outer_step, moved, step, sems = refs[-5:]
    square = jnp.sum(notes[...], axis=0)[:1, :1]
    clip = jnp.minimum(1.0, 0.25 * math.sqrt(entries) / jnp.sqrt(square + 1e-06))
    columns = values[0].shape[1]
    stored = []
    for n, (d, first) in enumerate(pieces):
        rows = values[n].shape[0]
        top = pl.multiple_of(place[3 * d], 32) + first
        left = pl.multiple_of(place[3 * d + 1], columns)
        unit = notes[pl.ds(place[3 * d + 2], 1)][0, 1:2, :1]
        for m in range(2):
            size = rows // 2
            here = pl.ds(m * size, size)
            there = (0, pl.ds(pl.multiple_of(top + m * size, 32), size), pl.ds(left, columns))
            clipped = (clip * unit) * values[n][here, :]
            fresh = 0.9 * momentum[there] + clipped
            moved[d, pl.ds(first + m * size, size), :] = fresh
            step[d, pl.ds(first + m * size, size), :] = (0.7 * (clipped + 0.9 * fresh)).astype(BF16)
            source = (d, pl.ds(first + m * size, size))
            for k, (here_ref, there_ref) in enumerate(((moved, new_momentum), (step, outer_step))):
                copy = pltpu.make_async_copy(here_ref.at[source], there_ref.at[there], sems.at[n, m, k])
                copy.start()
                stored.append(copy)
    for copy in stored:
        copy.wait()


def body(
    tokens,
    token_grads,
    slot_token,
    slot_count,
    slot_prob,
    gate_weight,
    down_weight,
    drift,
    momentum,
):
    islands, experts, parts = (lax.axis_size(a) for a in AXES)
    island, expert, part = (lax.axis_index(a) for a in AXES)
    devices = islands * experts * parts
    features, hidden = gate_weight.shape[2:]
    half = features // parts
    across = islands // parts
    columns = hidden // across
    entries = features * hidden * experts * parts
    slots = slot_token.shape[3]
    routed_rows = experts * slots
    holder = island // across
    spot = jnp.stack(
        [expert, part, island % across, island, jnp.int32(across), (part == holder).astype(jnp.int32)]
    ).astype(jnp.int32)

    handed = half // 2 if islands == 4 else 0
    steps = [0, 1, 2] if handed else list(range(islands))
    pieces = [(d, 0, half, n, 0) for n, d in enumerate(steps)]
    if handed:
        pieces += [(3, 0, handed, 1, half), (3, handed, handed, 2, half)]
    block_rows = [half + (handed if d else 0) for d in steps]
    picked = pl.pallas_call(
        lambda *refs: pick_kernel(experts, islands, pieces, *refs),
        in_specs=[SMEM] + [ANY] * 6,
        out_specs=[VMEM] * (experts + len(steps)),
        out_shape=[jax.ShapeDtypeStruct((2 * slots, half), BF16)] * experts
        + [jax.ShapeDtypeStruct((rows, columns), BF16) for rows in block_rows],
        scratch_shapes=[
            pltpu.VMEM(slot_token.shape, jnp.int32),
            pltpu.SMEM(slot_count.shape, jnp.int32),
            pltpu.VMEM(slot_prob.shape, F32),
            pltpu.VMEM(tokens.shape, BF16),
            pltpu.VMEM(token_grads.shape, BF16),
            pltpu.SemaphoreType.DMA((5 + len(pieces),)),
        ],
        compiler_params=params(56),
        name="pick_slots",
    )(spot, slot_token, slot_count, slot_prob, tokens, token_grads, drift)
    arrived = [picked[0]] + [swap(picked[d], "expert", d) for d in range(1, experts)]
    blocks = list(picked[experts:])
    arrived[0], blocks[0] = pl.pallas_call(
        own_kernel,
        in_specs=[VMEM] * 2,
        out_specs=[VMEM] * 2,
        out_shape=[
            jax.ShapeDtypeStruct((2 * slots, half), BF16),
            jax.ShapeDtypeStruct((half, columns), BF16),
        ],
        compiler_params=params(6),
        name="own_parts",
    )(arrived[0], blocks[0])
    drift_in = [blocks[0]] + [swap(blocks[d], "island", d) for d in steps[1:]]
    joined, turned, drift_sum, *relays = pl.pallas_call(
        lambda *refs: join_kernel(experts, len(steps), *refs),
        in_specs=[VMEM] * (experts + len(steps)),
        out_specs=[VMEM] * (5 if handed else 3),
        out_shape=[
            jax.ShapeDtypeStruct((2 * routed_rows, half), BF16),
            jax.ShapeDtypeStruct((half, routed_rows), BF16),
            jax.ShapeDtypeStruct((half, columns), F32),
        ]
        + [jax.ShapeDtypeStruct((handed, columns), BF16)] * (2 if handed else 0),
        compiler_params=params(12 + routed_rows // 48),
        name="join_slots",
    )(*arrived, *drift_in)
    relays = [swap(v, "island", 2 - n) for n, v in enumerate(relays)]

    joined_all = [joined] + [swap(joined, "tensor", t) for t in range(1, parts)]

    def send_features(d):
        pairs = []
        for at in range(islands):
            to = partner(at, d, islands)
            pairs.append((at * parts + to // across, to * parts + to // across))
        return lax.ppermute(turned, ("island", "tensor"), pairs)

    def spread(value):
        result = value
        for t in range(1, parts):
            pairs = []
            for at in range(islands):
                keep = at // across
                pairs.append((at * parts + keep, at * parts + partner(keep, t, parts)))
            moved = lax.ppermute(value, ("island", "tensor"), pairs)
            result = moved if t == 1 else result + moved
        return result

    features_in = [send_features(d) for d in range(1, islands)]

    hidden_piece = jax.ShapeDtypeStruct((routed_rows, columns), BF16)
    *hidden_out, norms = pl.pallas_call(
        lambda *refs: hidden_kernel(parts, across, *refs),
        in_specs=[SMEM] + [VMEM] * (2 + parts),
        out_specs=[VMEM] * (across + 1),
        out_shape=[hidden_piece] * across + [jax.ShapeDtypeStruct((devices, 8, 128), F32)],
        compiler_params=params(16 + routed_rows // 48),
        name="hidden_grads",
    )(spot, gate_weight, down_weight, *joined_all)

    def hidden_for(d):
        at = partner(island, d, islands) % across
        if islands & (islands - 1) == 0:
            return hidden_out[d % across]
        return lax.select_n((at - island) % across, *hidden_out)

    hidden_of = [hidden_out[0]] + [
        swap(hidden_for(d), "island", d) for d in range(1, islands)
    ]
    norms, features_in = pl.pallas_call(
        lambda *refs: hand_kernel(islands, *refs),
        in_specs=[VMEM] * (islands + 1) + [ANY] * len(relays),
        out_specs=[VMEM] * 2,
        out_shape=[
            jax.ShapeDtypeStruct(norms.shape, F32),
            jax.ShapeDtypeStruct((islands, half, routed_rows), BF16),
        ],
        compiler_params=params(4 + routed_rows // 48),
        name="hand_features",
    )(norms, turned, *features_in, *relays)
    features_moved = spread(features_in)
    norms = lax.all_to_all(norms, AXES, split_axis=0, concat_axis=0, tiled=True)

    scaled, notes = pl.pallas_call(
        lambda *refs: average_kernel(islands, entries, 4, *refs),
        in_specs=[SMEM] + [VMEM] * (4 + islands + len(relays)),
        out_specs=[VMEM] * 2,
        out_shape=[
            jax.ShapeDtypeStruct((half, columns), F32),
            jax.ShapeDtypeStruct((devices, 8, 128), F32),
        ],
        scratch_shapes=[pltpu.VMEM((half, columns), F32), pltpu.VMEM((1, columns), F32)],
        compiler_params=params(8 + routed_rows // 48),
        name="average_block",
    )(spot, norms, drift_sum, features_in, features_moved, *hidden_of, *relays)
    notes = lax.all_to_all(notes, AXES, split_axis=0, concat_axis=0, tiled=True)

    parted = half // 2 if islands == 4 else half
    sent = [scaled[first : first + parted].astype(WIRE) for first in range(0, half, parted)]
    values = {(0, 0): lax.reduce_precision(scaled, 5, 10)}
    if islands == 4:
        beside, below = swap(sent[0], "island", 1), swap(sent[1], "island", 2)
        values[1, 0], values[2, parted] = beside, below
        values[2, 0], values[1, parted] = swap(sent[0], "island", 2), swap(sent[1], "island", 1)
        values[3, 0], values[3, parted] = swap(beside, "island", 2), swap(below, "island", 1)
    else:
        for d in range(1, islands):
            values[d, 0] = swap(sent[0], "island", d)
    place = []
    for d in range(islands):
        at = origin(island, d, islands)
        source = (at * experts + expert) * parts + part
        place += [(at // across) * half, (at % across) * columns, source]
    block = (islands, half, columns)
    return tuple(
        pl.pallas_call(
            lambda *refs: update_kernel(entries, list(values), *refs),
            in_specs=[SMEM] + [VMEM] * (2 + len(values)),
            out_specs=[ANY, ANY],
            out_shape=[
                jax.ShapeDtypeStruct(momentum.shape, F32),
                jax.ShapeDtypeStruct(momentum.shape, BF16),
            ],
            scratch_shapes=[
                pltpu.VMEM(block, F32),
                pltpu.VMEM(block, BF16),
                pltpu.SemaphoreType.DMA((len(values), 2, 2)),
            ],
            compiler_params=params(14),
            name="update_outputs",
        )(
            jnp.stack(place).astype(jnp.int32),
            notes,
            momentum,
            *[v.astype(F32) for v in values.values()],
        )
    )


def solution(mesh):
    return jax.shard_map(
        body,
        mesh=mesh,
        in_specs=(
            P("island", "expert", "tensor"),
            P("island", "expert", "tensor"),
            P("island", "expert", None, None),
            P("island", "expert", None),
            P("island", "expert", None, None),
            P("island", "expert", None, "tensor"),
            P("island", "expert", "tensor", None),
            P("island", "expert", None, "tensor"),
            P("expert", None, "tensor"),
        ),
        out_specs=(P("expert", None, "tensor"), P("expert", None, "tensor")),
        check_vma=False,
    )
```

time: 248 us -> 152 us (0.61); the launches traced: 248 us -> 149 us
  Pallas kernels: 133 us -> 20.6 us
  blocking collectives: 31.3 us -> 16.5 us
  local copies, waits for them, and re-layouts: 3 us -> 11.2 us
  waiting for transfers between devices: 46.1 us -> 54 us
  starting transfers between devices: 29 us -> 35.1 us
  other arithmetic: 4.92 us -> 10.6 us
    pallas_call x1, Pallas kernels: 98.5 us -> 5.38 us  [body(): pl.pallas_call(lambda *refs: pick_kernel(experts, islands, pieces, *refs)...]
    pallas_call x7 -> x4, Pallas kernels: 26.3 us -> 9.03 us  [the longest x1 4.63 us: body(): pl.pallas_call(lambda *refs: update_kernel(entries, list(values), *refs),...]
    all_to_all x1 -> x0, blocking collectives: 14 us -> none  [body(): notes = lax.all_to_all(notes, AXES, split_axis=0, concat_axis=0, tiled=True)]
    ppermute x17, waiting for transfers between devices: 46.1 us -> 54 us  [swap(): lax.ppermute(value, axis, [(at, partner(at, step, size)) for at in range(...]
    unnamed x10 -> x20, local copies, waits for them, and re-layouts: 2.14 us -> 9.46 us
    all_to_all x0 -> x1, starting transfers between devices: none -> 7.31 us  [body(): notes = lax.all_to_all(notes, AXES, split_axis=0, concat_axis=0, tiled=True)]
    convert_element_type x8 -> x6, other arithmetic: 3.93 us -> 9.84 us  [body(): v.astype(F32)]
  transfers between devices with their start and end apart: 21 -> 22, of which waited for: 6 -> 5; matrix products, arithmetic and copies ran while one was open for 2% -> 7% of each run, Pallas kernels for 7% -> 4%
where the time goes in v5:
time: 152 us; the launch traced here: 149 us
  waiting for transfers between devices  54 us (36%)
  starting transfers between devices  35.1 us (23%)
  Pallas kernels  20.6 us (14%)
  blocking collectives  16.5 us (11%)
  local copies, waits for them, and re-layouts  11.2 us (7%)
  other arithmetic  10.6 us (7%)
    ppermute x17, waiting for transfers between devices, swap(): lax.ppermute(value, axis, [(at, partner(at, step, size)) for at in range(...  54 us
    ppermute x17, starting transfers between devices, swap(): lax.ppermute(value, axis, [(at, partner(at, step, size)) for at in range(...  21.2 us
    all_to_all x1, blocking collectives, body(): norms = lax.all_to_all(norms, AXES, split_axis=0, concat_axis=0, tiled=True)  16.5 us
    convert_element_type x6, other arithmetic, body(): v.astype(F32)  9.84 us
    unnamed x20, local copies, waits for them, and re-layouts  9.46 us
    all_to_all x1, starting transfers between devices, body(): notes = lax.all_to_all(notes, AXES, split_axis=0, concat_axis=0, tiled=True)  7.31 us
    pallas_call x1, Pallas kernels, body(): pl.pallas_call(lambda *refs: hidden_kernel(parts, across, *refs), in_spec...  5.45 us
    pallas_call x1, Pallas kernels, body(): pl.pallas_call(lambda *refs: pick_kernel(experts, islands, pieces, *refs)...  5.38 us
  transfers between devices with their start and end apart: 22, of which 5 were waited for; matrix products, arithmetic and copies ran while one was open for 7% of the time, Pallas kernels for 4%

profile of v5, /device:TPU:0, one launch (start us, length us, event | category | flops | bytes accessed | tf_op | source)
XLA Modules:
  0.0 149.1 jit_solution(12821311194150184598)
XLA Ops:
  0.7 0.6 stack.79.refs_0_
  1.3 5.4 %pick_slots.1 = (bf16[192,1024]{1,0:T(8,128)(2,1)}, bf16[192,1024]{1,0:T(8,128)(2,1)}, bf16[192,1024]{1,0:T(8,128)(2,1)}, bf16[192,1024]{1,0:T(8,128)(2,1)}, bf1...) custom-call(s32[6]{0:T(128)} %stack.79.refs_0_, s32[1,1,4,96]{3,2,1,0:T(4,128)} %refs_1_.2, ...), custom_call_target="tpu_custom_call" | custom-call | tf_op jit(solution)/shard_map/pick_slots/pallas_call | solution.py:241
  6.7 3.0 %collective-permute-start.3 = (bf16[1536,384]{1,0:T(8,128)(2,1)}, bf16[1536,384]{1,0:T(8,128)(2,1)S(1)}, u32[]{:S(2)}, u32[]{:S(2)}) collective-permute-start(bf16[1536,384]{1,0:T(8,128)(2,1)} %get-tuple-element.30), channel_id=1, source_target_pairs={{0,8},{8,0},{16,24},{24,16},{1,9},{9,1},{17,25},{25,17},{2,10},{10... | collective-permute-start | bytes 3538952 | tf_op jit(solution)/shard_map/ppermute | solution.py:34
  9.7 1.5 %collective-permute-start.4 = (bf16[1536,384]{1,0:T(8,128)(2,1)}, bf16[1536,384]{1,0:T(8,128)(2,1)S(1)}, u32[]{:S(2)}, u32[]{:S(2)}) collective-permute-start(bf16[1536,384]{1,0:T(8,128)(2,1)} %get-tuple-element.31), channel_id=1, source_target_pairs={{0,16},{8,24},{16,0},{24,8},{1,17},{9,25},{17,1},{25,9},{2,18},{10... | collective-permute-start | bytes 3538952 | tf_op jit(solution)/shard_map/ppermute | solution.py:34
  11.2 1.6 %collective-permute-start = (bf16[192,1024]{1,0:T(8,128)(2,1)}, bf16[192,1024]{1,0:T(8,128)(2,1)S(1)}, u32[]{:S(2)}, u32[]{:S(2)}) collective-permute-start(bf16[192,1024]{1,0:T(8,128)(2,1)} %get-tuple-element.26), channel_id=1, source_target_pairs={{0,2},{2,0},{4,6},{6,4},{1,3},{3,1},{5,7},{7,5},{8,10},{10,8},{12,... | collective-permute-start | bytes 1179656 | tf_op jit(solution)/shard_map/ppermute | solution.py:34
  12.8 2.6 %collective-permute-start.1 = (bf16[192,1024]{1,0:T(8,128)(2,1)}, bf16[192,1024]{1,0:T(8,128)(2,1)S(1)}, u32[]{:S(2)}, u32[]{:S(2)}) collective-permute-start(bf16[192,1024]{1,0:T(8,128)(2,1)} %get-tuple-element.27), channel_id=1, source_target_pairs={{0,4},{2,6},{4,0},{6,2},{1,5},{3,7},{5,1},{7,3},{8,12},{10,14},{12... | collective-permute-start | bytes 1179656 | tf_op jit(solution)/shard_map/ppermute | solution.py:34
  15.3 0.2 collective-permute-start.2
  15.6 1.1 copy-done.7
  16.7 1.0 copy-done.8
  17.7 0.1 own_parts.1
  17.8 11.3 %collective-permute-done.refs_1_ = bf16[192,1024]{1,0:T(8,128)(2,1)S(1)} collective-permute-done((bf16[192,1024]{1,0:T(8,128)(2,1)}, bf16[192,1024]{1,0:T(8,128)(2,1)S(1)}, u32[]{:S(2)}, u32[]{:S(2)}) %collective-permute-start) | collective-permute-done | bytes 393248 | tf_op jit(solution)/shard_map/ppermute | solution.py:34
  29.1 13.7 %collective-permute-done.1.refs_2_ = bf16[192,1024]{1,0:T(8,128)(2,1)S(1)} collective-permute-done((bf16[192,1024]{1,0:T(8,128)(2,1)}, bf16[192,1024]{1,0:T(8,128)(2,1)S(1)}, u32[]{:S(2)}, u32[]{:S(2)}) %collective-permute-start.1) | collective-permute-done | bytes 393248 | tf_op jit(solution)/shard_map/ppermute | solution.py:34
  42.8 0.0 collective-permute-done.2.refs_3_
  42.8 0.0 collective-permute-done.3.refs_5_
  42.8 0.0 copy-start.5
  42.8 0.7 join_slots.1
  43.6 0.1 collective-permute-start.5
  43.6 1.4 collective-permute-start.8
  45.1 1.3 collective-permute-start.7
  46.4 2.4 %collective-permute-start.6 = (bf16[1024,384]{1,0:T(8,128)(2,1)S(1)}, bf16[1024,384]{1,0:T(8,128)(2,1)S(1)}, u32[]{:S(2)}, u32[]{:S(2)}) collective-permute-start(bf16[1024,384]{1,0:T(8,128)(2,1)S(1)} %get-tuple-element.34.refs_1_), channel_id=1, source_target_pairs={{0,8},{8,0},{17,25},{25,17},{2,10},{10,2},{19,27},{27,19},{4,12},{... | collective-permute-start | bytes 2359304 | tf_op jit(solution)/shard_map/ppermute | solution.py:294
  48.8 1.0 collective-permute-start.9
  49.9 0.0 collective-permute-done.5.refs_4_
  49.9 1.5 %collective-permute-start.10 = (bf16[512,384]{1,0:T(8,128)(2,1)S(1)}, bf16[512,384]{1,0:T(8,128)(2,1)S(1)}, u32[]{:S(2)}, u32[]{:S(2)}) collective-permute-start(bf16[512,384]{1,0:T(8,128)(2,1)S(1)} %get-tuple-element.36), channel_id=1, source_target_pairs={{0,8},{8,0},{16,24},{24,16},{1,9},{9,1},{17,25},{25,17},{2,10},{10... | collective-permute-start | bytes 1179656 | tf_op jit(solution)/shard_map/ppermute | solution.py:34
  51.4 5.4 %hidden_grads.1 = (bf16[384,384]{1,0:T(8,128)(2,1)S(1)}, bf16[384,384]{1,0:T(8,128)(2,1)S(1)}, f32[32,8,128]{2,1,0:T(8,128)S(1)}) custom-call(s32[6]{0:T(128)S(1)} %copy-done.9, bf16[1,1,2048,768]{3,2,1,0:T(8,128)(2,1)S(1)} %copy-done.5, bf16[1,1,768,2048]{3,2,1,0:T(8,128)(2,1)S(1)} %copy-done.6, bf16[768,1024]{1,0:T(8,128)(2,1)S(1)} %get-tuple-element.32.refs_3_, ...), custom_call_target="tpu_custom_call" | custom-call | tf_op jit(solution)/shard_map/hidden_grads/pallas_call | solution.py:310
  56.8 18.6 %collective-permute-done.9.refs_5_.refs_9_ = bf16[512,384]{1,0:T(8,128)(2,1)S(1)} collective-permute-done((bf16[512,384]{1,0:T(8,128)(2,1)S(1)}, bf16[512,384]{1,0:T(8,128)(2,1)S(1)}, u32[]{:S(2)}, u32[]{:S(2)}) %collective-permute-start.9) | collective-permute-done | bytes 393248 | tf_op jit(solution)/shard_map/ppermute | solution.py:34
  75.4 0.0 collective-permute-done.6.refs_2_
  75.4 0.3 hand_features.1
  75.7 1.5 %collective-permute-start.11 = (bf16[4,1024,384]{2,1,0:T(8,128)(2,1)S(1)}, bf16[4,1024,384]{2,1,0:T(8,128)(2,1)S(1)}, u32[]{:S(2)}, u32[]{:S(2)}) collective-permute-start(bf16[4,1024,384]{2,1,0:T(8,128)(2,1)S(1)} %get-tuple-element.39.refs_3_), channel_id=1, source_target_pairs={{0,1},{8,9},{17,16},{25,24},{2,3},{10,11},{19,18},{27,26},{4,5},{1... | collective-permute-start | bytes 9437192 | tf_op jit(solution)/shard_map/ppermute | solution.py:303
  77.2 0.1 collective-permute-start.13
  77.3 2.2 %collective-permute-start.14 = (bf16[384,384]{1,0:T(8,128)(2,1)S(1)}, bf16[384,384]{1,0:T(8,128)(2,1)S(1)}, u32[]{:S(2)}, u32[]{:S(2)}) collective-permute-start(bf16[384,384]{1,0:T(8,128)(2,1)S(1)} %get-tuple-element.41), channel_id=1, source_target_pairs={{0,24},{8,16},{16,8},{24,0},{1,25},{9,17},{17,9},{25,1},{2,26},{10... | collective-permute-start | bytes 884744 | tf_op jit(solution)/shard_map/ppermute | solution.py:34
  79.5 1.3 collective-permute-start.12
  80.8 16.5 %all_to_all.10.refs_1_ = f32[32,8,128]{2,1,0:T(8,128)S(1)} all-to-all(f32[32,8,128]{2,1,0:T(8,128)S(1)} %get-tuple-element.37), channel_id=1, replica_groups=mesh['island'=4,'expert'=4,'tensor'=2] {'island','expert','tensor'}, dimensions={0} | all-to-all | bytes 262144 | tf_op jit(solution)/shard_map/all_to_all | solution.py:340
  97.2 0.0 collective-permute-done.13.refs_7_
  97.2 0.0 collective-permute-done.14.refs_8_
  97.3 0.0 collective-permute-done.12.refs_6_
  97.3 0.0 collective-permute-done.11.refs_4_
  97.3 4.0 %average_block.1 = (f32[1024,384]{1,0:T(8,128)S(1)}, f32[32,8,128]{2,1,0:T(8,128)}) custom-call(s32[6]{0:T(128)S(1)} %copy-done.9, f32[32,8,128]{2,1,0:T(8,128)S(1)} %all_to_all.10.refs_1_, f32[1024,384]{1,0:T(8,128)S(1)} %get-tuple-element.38.refs_2_, bf16[4,1024,384]{2,1,0:T(8,128)(2,1)S(1)} %get-tuple-element.39.refs_3_, ...), custom_call_target="tpu_custom_call" | custom-call | tf_op jit(solution)/shard_map/average_block/pallas_call | solution.py:342
  101.3 0.8 fusion
  102.1 1.1 fusion.1
  103.2 0.8 collective-permute-start.16
  104.0 0.7 collective-permute-start.15
  104.7 1.3 collective-permute-start.18
  106.0 1.2 collective-permute-start.17
  107.2 8.2 %collective-permute-done.16 = f16[512,384]{1,0:T(8,128)(2,1)} collective-permute-done((f16[512,384]{1,0:T(8,128)(2,1)}, f16[512,384]{1,0:T(8,128)(2,1)}, u32[]{:S(2)}, u32[]{:S(2)}) %collective-permute-start.16) | collective-permute-done | bytes 393248 | tf_op jit(solution)/shard_map/ppermute | solution.py:34
  115.4 0.9 collective-permute-start.20
  116.4 0.0 collective-permute-done.15
  116.4 1.1 collective-permute-start.19
  117.5 7.3 %all-to-all-start.1 = ((f32[32,8,128]{2,1,0:T(8,128)}), f32[32,8,128]{2,1,0:T(8,128)S(1)}, u32[]{:S(2)}, u32[]{:S(2)}) async-start(f32[32,8,128]{2,1,0:T(8,128)} %get-tuple-element.42), calls=%async_computation.1 | async-start | bytes 262144 | tf_op jit(solution)/shard_map/all_to_all | solution.py:354
  124.9 0.1 stack.72.refs_0_
  125.0 1.1 convert_element_type.21.refs_4_
  126.0 1.0 convert_element_type.22.refs_5_
  127.1 1.9 %convert_element_type.24.refs_7_ = f32[512,384]{1,0:T(8,128)} convert(f16[512,384]{1,0:T(8,128)(2,1)} %collective-permute-done.18) | non-fusion elementwise | flops 196608 | bytes 1179648 | tf_op jit(solution)/shard_map/convert_element_type | solution.py:393
  129.0 0.0 collective-permute-done.17
  129.0 1.9 %convert_element_type.23.refs_6_ = f32[512,384]{1,0:T(8,128)} convert(f16[512,384]{1,0:T(8,128)(2,1)} %collective-permute-done.17) | non-fusion elementwise | flops 196608 | bytes 1179648 | tf_op jit(solution)/shard_map/convert_element_type | solution.py:393
  131.0 2.2 %collective-permute-done.20 = f16[512,384]{1,0:T(8,128)(2,1)} collective-permute-done((f16[512,384]{1,0:T(8,128)(2,1)}, f16[512,384]{1,0:T(8,128)(2,1)}, u32[]{:S(2)}, u32[]{:S(2)}) %collective-permute-start.20) | collective-permute-done | bytes 393248 | tf_op jit(solution)/shard_map/ppermute | solution.py:34
  133.1 1.9 %convert_element_type.26.refs_9_ = f32[512,384]{1,0:T(8,128)} convert(f16[512,384]{1,0:T(8,128)(2,1)} %collective-permute-done.20) | non-fusion elementwise | flops 196608 | bytes 1179648 | tf_op jit(solution)/shard_map/convert_element_type | solution.py:393
  135.1 0.0 collective-permute-done.19
  135.1 1.9 %convert_element_type.25.refs_8_ = f32[512,384]{1,0:T(8,128)} convert(f16[512,384]{1,0:T(8,128)(2,1)} %collective-permute-done.19) | non-fusion elementwise | flops 196608 | bytes 1179648 | tf_op jit(solution)/shard_map/convert_element_type | solution.py:393
  137.0 2.8 %copy-done = f32[1,2048,768]{2,1,0:T(8,128)S(1)} copy-done((f32[1,2048,768]{2,1,0:T(8,128)S(1)}, f32[1,2048,768]{2,1,0:T(8,128)}, u32[]{:S(2)}) %copy-start) | copy-done | bytes 6291480
  139.8 1.1 copy-done.1
  141.0 1.1 copy-done.2
  142.1 1.1 copy-done.3
  143.2 1.1 copy-done.4
  144.4 4.6 %update_outputs.1 = (f32[1,2048,768]{2,1,0:T(8,128)}, bf16[1,2048,768]{2,1,0:T(8,128)(2,1)}) custom-call(s32[12]{0:T(128)S(1)} %stack.72.refs_0_, f32[32,8,128]{2,1,0:T(8,128)S(1)} %all-to-all-done.1.refs_1_, f32[1,2048,768]{2,1,0:T(8,128)S(1)} %copy-done, f32[1024,384]{1,0:T(8,128)S(1)} %get-tuple-element.45.refs_3_, ...), custom_call_target="tpu_custom_call" | custom-call | tf_op jit(solution)/shard_map/update_outputs/pallas_call | solution.py:374
  (18 shorter events, 0.0 us)
Async XLA Ops:
  1.3 50.1 %copy-start.6 = (bf16[1,1,768,2048]{3,2,1,0:T(8,128)(2,1)S(1)}, bf16[1,1,768,2048]{3,2,1,0:T(8,128)(2,1)}, u32[]{:S(2)}) copy-start(bf16[1,1,768,2048]{3,2,1,0:T(8,128)(2,1)} %refs_2_.4) | copy-start | bytes 9437188
  6.7 36.1 %collective-permute-start.3 = (bf16[1536,384]{1,0:T(8,128)(2,1)}, bf16[1536,384]{1,0:T(8,128)(2,1)S(1)}, u32[]{:S(2)}, u32[]{:S(2)}) collective-permute-start(bf16[1536,384]{1,0:T(8,128)(2,1)} %get-tuple-element.30), channel_id=1, source_target_pairs={{0,8},{8,0},{16,24},{24,16},{1,9},{9,1},{17,25},{25,17},{2,10},{10... | collective-permute-start | bytes 3538952 | tf_op jit(solution)/shard_map/ppermute | solution.py:34
  9.7 33.1 %collective-permute-start.4 = (bf16[1536,384]{1,0:T(8,128)(2,1)}, bf16[1536,384]{1,0:T(8,128)(2,1)S(1)}, u32[]{:S(2)}, u32[]{:S(2)}) collective-permute-start(bf16[1536,384]{1,0:T(8,128)(2,1)} %get-tuple-element.31), channel_id=1, source_target_pairs={{0,16},{8,24},{16,0},{24,8},{1,17},{9,25},{17,1},{25,9},{2,18},{10... | collective-permute-start | bytes 3538952 | tf_op jit(solution)/shard_map/ppermute | solution.py:34
  11.2 17.9 %collective-permute-start = (bf16[192,1024]{1,0:T(8,128)(2,1)}, bf16[192,1024]{1,0:T(8,128)(2,1)S(1)}, u32[]{:S(2)}, u32[]{:S(2)}) collective-permute-start(bf16[192,1024]{1,0:T(8,128)(2,1)} %get-tuple-element.26), channel_id=1, source_target_pairs={{0,2},{2,0},{4,6},{6,4},{1,3},{3,1},{5,7},{7,5},{8,10},{10,8},{12,... | collective-permute-start | bytes 1179656 | tf_op jit(solution)/shard_map/ppermute | solution.py:34
  12.8 30.0 %collective-permute-start.1 = (bf16[192,1024]{1,0:T(8,128)(2,1)}, bf16[192,1024]{1,0:T(8,128)(2,1)S(1)}, u32[]{:S(2)}, u32[]{:S(2)}) collective-permute-start(bf16[192,1024]{1,0:T(8,128)(2,1)} %get-tuple-element.27), channel_id=1, source_target_pairs={{0,4},{2,6},{4,0},{6,2},{1,5},{3,7},{5,1},{7,3},{8,12},{10,14},{12... | collective-permute-start | bytes 1179656 | tf_op jit(solution)/shard_map/ppermute | solution.py:34
  15.3 27.4 %collective-permute-start.2 = (bf16[192,1024]{1,0:T(8,128)(2,1)}, bf16[192,1024]{1,0:T(8,128)(2,1)S(1)}, u32[]{:S(2)}, u32[]{:S(2)}) collective-permute-start(bf16[192,1024]{1,0:T(8,128)(2,1)} %get-tuple-element.28), channel_id=1, source_target_pairs={{0,6},{2,4},{4,2},{6,0},{1,7},{3,5},{5,3},{7,1},{8,14},{10,12},{12... | collective-permute-start | bytes 1179656 | tf_op jit(solution)/shard_map/ppermute | solution.py:34
  15.6 1.1 copy-start.7
  16.7 1.0 copy-start.8
  42.8 8.6 %copy-start.5 = (bf16[1,1,2048,768]{3,2,1,0:T(8,128)(2,1)S(1)}, bf16[1,1,2048,768]{3,2,1,0:T(8,128)(2,1)}, u32[]{:S(2)}) copy-start(bf16[1,1,2048,768]{3,2,1,0:T(8,128)(2,1)} %refs_1_.3) | copy-start | bytes 9437188
  42.8 8.6 %copy-start.9 = (s32[6]{0:T(128)S(1)}, s32[6]{0:T(128)}, u32[]{:S(2)}) copy-start(s32[6]{0:T(128)} %stack.79.refs_0_) | copy-start | bytes 76
  43.6 6.3 %collective-permute-start.5 = (bf16[768,1024]{1,0:T(8,128)(2,1)S(1)}, bf16[768,1024]{1,0:T(8,128)(2,1)S(1)}, u32[]{:S(2)}, u32[]{:S(2)}) collective-permute-start(bf16[768,1024]{1,0:T(8,128)(2,1)S(1)} %get-tuple-element.32.refs_3_), channel_id=1, source_target_pairs={{0,1},{1,0},{2,3},{3,2},{4,5},{5,4},{6,7},{7,6},{8,9},{9,8},{10,11... | collective-permute-start | bytes 4718600 | tf_op jit(solution)/shard_map/ppermute | solution.py:34
  43.6 31.8 %collective-permute-start.8 = (bf16[1024,384]{1,0:T(8,128)(2,1)S(1)}, bf16[1024,384]{1,0:T(8,128)(2,1)S(1)}, u32[]{:S(2)}, u32[]{:S(2)}) collective-permute-start(bf16[1024,384]{1,0:T(8,128)(2,1)S(1)} %get-tuple-element.34.refs_1_), channel_id=1, source_target_pairs={{1,25},{9,17},{16,8},{24,0},{3,27},{11,19},{18,10},{26,2},{5,29},{... | collective-permute-start | bytes 2359304 | tf_op jit(solution)/shard_map/ppermute | solution.py:294
  45.1 30.3 %collective-permute-start.7 = (bf16[1024,384]{1,0:T(8,128)(2,1)S(1)}, bf16[1024,384]{1,0:T(8,128)(2,1)S(1)}, u32[]{:S(2)}, u32[]{:S(2)}) collective-permute-start(bf16[1024,384]{1,0:T(8,128)(2,1)S(1)} %get-tuple-element.34.refs_1_), channel_id=1, source_target_pairs={{1,17},{9,25},{16,0},{24,8},{3,19},{11,27},{18,2},{26,10},{5,21},{... | collective-permute-start | bytes 2359304 | tf_op jit(solution)/shard_map/ppermute | solution.py:294
  46.4 29.1 %collective-permute-start.6 = (bf16[1024,384]{1,0:T(8,128)(2,1)S(1)}, bf16[1024,384]{1,0:T(8,128)(2,1)S(1)}, u32[]{:S(2)}, u32[]{:S(2)}) collective-permute-start(bf16[1024,384]{1,0:T(8,128)(2,1)S(1)} %get-tuple-element.34.refs_1_), channel_id=1, source_target_pairs={{0,8},{8,0},{17,25},{25,17},{2,10},{10,2},{19,27},{27,19},{4,12},{... | collective-permute-start | bytes 2359304 | tf_op jit(solution)/shard_map/ppermute | solution.py:294
  48.8 26.6 %collective-permute-start.9 = (bf16[512,384]{1,0:T(8,128)(2,1)S(1)}, bf16[512,384]{1,0:T(8,128)(2,1)S(1)}, u32[]{:S(2)}, u32[]{:S(2)}) collective-permute-start(bf16[512,384]{1,0:T(8,128)(2,1)S(1)} %get-tuple-element.35), channel_id=1, source_target_pairs={{0,16},{8,24},{16,0},{24,8},{1,17},{9,25},{17,1},{25,9},{2,18},{10... | collective-permute-start | bytes 1179656 | tf_op jit(solution)/shard_map/ppermute | solution.py:34
  49.9 25.5 %collective-permute-start.10 = (bf16[512,384]{1,0:T(8,128)(2,1)S(1)}, bf16[512,384]{1,0:T(8,128)(2,1)S(1)}, u32[]{:S(2)}, u32[]{:S(2)}) collective-permute-start(bf16[512,384]{1,0:T(8,128)(2,1)S(1)} %get-tuple-element.36), channel_id=1, source_target_pairs={{0,8},{8,0},{16,24},{24,16},{1,9},{9,1},{17,25},{25,17},{2,10},{10... | collective-permute-start | bytes 1179656 | tf_op jit(solution)/shard_map/ppermute | solution.py:34
  75.7 21.5 %collective-permute-start.11 = (bf16[4,1024,384]{2,1,0:T(8,128)(2,1)S(1)}, bf16[4,1024,384]{2,1,0:T(8,128)(2,1)S(1)}, u32[]{:S(2)}, u32[]{:S(2)}) collective-permute-start(bf16[4,1024,384]{2,1,0:T(8,128)(2,1)S(1)} %get-tuple-element.39.refs_3_), channel_id=1, source_target_pairs={{0,1},{8,9},{17,16},{25,24},{2,3},{10,11},{19,18},{27,26},{4,5},{1... | collective-permute-start | bytes 9437192 | tf_op jit(solution)/shard_map/ppermute | solution.py:303
  77.2 20.0 %collective-permute-start.13 = (bf16[384,384]{1,0:T(8,128)(2,1)S(1)}, bf16[384,384]{1,0:T(8,128)(2,1)S(1)}, u32[]{:S(2)}, u32[]{:S(2)}) collective-permute-start(bf16[384,384]{1,0:T(8,128)(2,1)S(1)} %get-tuple-element.40.refs_5_), channel_id=1, source_target_pairs={{0,16},{8,24},{16,0},{24,8},{1,17},{9,25},{17,1},{25,9},{2,18},{10... | collective-permute-start | bytes 884744 | tf_op jit(solution)/shard_map/ppermute | solution.py:34
  77.3 20.0 %collective-permute-start.14 = (bf16[384,384]{1,0:T(8,128)(2,1)S(1)}, bf16[384,384]{1,0:T(8,128)(2,1)S(1)}, u32[]{:S(2)}, u32[]{:S(2)}) collective-permute-start(bf16[384,384]{1,0:T(8,128)(2,1)S(1)} %get-tuple-element.41), channel_id=1, source_target_pairs={{0,24},{8,16},{16,8},{24,0},{1,25},{9,17},{17,9},{25,1},{2,26},{10... | collective-permute-start | bytes 884744 | tf_op jit(solution)/shard_map/ppermute | solution.py:34
  79.5 17.8 %collective-permute-start.12 = (bf16[384,384]{1,0:T(8,128)(2,1)S(1)}, bf16[384,384]{1,0:T(8,128)(2,1)S(1)}, u32[]{:S(2)}, u32[]{:S(2)}) collective-permute-start(bf16[384,384]{1,0:T(8,128)(2,1)S(1)} %get-tuple-element.41), channel_id=1, source_target_pairs={{0,8},{8,0},{16,24},{24,16},{1,9},{9,1},{17,25},{25,17},{2,10},{10... | collective-permute-start | bytes 884744 | tf_op jit(solution)/shard_map/ppermute | solution.py:34
  103.2 12.3 %collective-permute-start.16 = (f16[512,384]{1,0:T(8,128)(2,1)}, f16[512,384]{1,0:T(8,128)(2,1)}, u32[]{:S(2)}, u32[]{:S(2)}) collective-permute-start(f16[512,384]{1,0:T(8,128)(2,1)} %get-tuple-element.46), channel_id=1, source_target_pairs={{0,16},{8,24},{16,0},{24,8},{1,17},{9,25},{17,1},{25,9},{2,18},{10... | collective-permute-start | bytes 1179656 | tf_op jit(solution)/shard_map/ppermute | solution.py:34
  104.0 12.4 %collective-permute-start.15 = (f16[512,384]{1,0:T(8,128)(2,1)}, f16[512,384]{1,0:T(8,128)(2,1)}, u32[]{:S(2)}, u32[]{:S(2)}) collective-permute-start(f16[512,384]{1,0:T(8,128)(2,1)} %get-tuple-element.47), channel_id=1, source_target_pairs={{0,8},{8,0},{16,24},{24,16},{1,9},{9,1},{17,25},{25,17},{2,10},{10... | collective-permute-start | bytes 1179656 | tf_op jit(solution)/shard_map/ppermute | solution.py:34
  104.7 22.4 %collective-permute-start.18 = (f16[512,384]{1,0:T(8,128)(2,1)}, f16[512,384]{1,0:T(8,128)(2,1)}, u32[]{:S(2)}, u32[]{:S(2)}) collective-permute-start(f16[512,384]{1,0:T(8,128)(2,1)} %get-tuple-element.46), channel_id=1, source_target_pairs={{0,8},{8,0},{16,24},{24,16},{1,9},{9,1},{17,25},{25,17},{2,10},{10... | collective-permute-start | bytes 1179656 | tf_op jit(solution)/shard_map/ppermute | solution.py:34
  106.0 23.0 %collective-permute-start.17 = (f16[512,384]{1,0:T(8,128)(2,1)}, f16[512,384]{1,0:T(8,128)(2,1)}, u32[]{:S(2)}, u32[]{:S(2)}) collective-permute-start(f16[512,384]{1,0:T(8,128)(2,1)} %get-tuple-element.47), channel_id=1, source_target_pairs={{0,16},{8,24},{16,0},{24,8},{1,17},{9,25},{17,1},{25,9},{2,18},{10... | collective-permute-start | bytes 1179656 | tf_op jit(solution)/shard_map/ppermute | solution.py:34
  115.4 17.7 %collective-permute-start.20 = (f16[512,384]{1,0:T(8,128)(2,1)}, f16[512,384]{1,0:T(8,128)(2,1)}, u32[]{:S(2)}, u32[]{:S(2)}) collective-permute-start(f16[512,384]{1,0:T(8,128)(2,1)} %collective-permute-done.16), channel_id=1, source_target_pairs={{0,8},{8,0},{16,24},{24,16},{1,9},{9,1},{17,25},{25,17},{2,10},{10... | collective-permute-start | bytes 1179656 | tf_op jit(solution)/shard_map/ppermute | solution.py:34
  116.4 18.7 %collective-permute-start.19 = (f16[512,384]{1,0:T(8,128)(2,1)}, f16[512,384]{1,0:T(8,128)(2,1)}, u32[]{:S(2)}, u32[]{:S(2)}) collective-permute-start(f16[512,384]{1,0:T(8,128)(2,1)} %collective-permute-done.15), channel_id=1, source_target_pairs={{0,16},{8,24},{16,0},{24,8},{1,17},{9,25},{17,1},{25,9},{2,18},{10... | collective-permute-start | bytes 1179656 | tf_op jit(solution)/shard_map/ppermute | solution.py:34
  117.5 19.6 %all-to-all-start.1 = ((f32[32,8,128]{2,1,0:T(8,128)}), f32[32,8,128]{2,1,0:T(8,128)S(1)}, u32[]{:S(2)}, u32[]{:S(2)}) async-start(f32[32,8,128]{2,1,0:T(8,128)} %get-tuple-element.42), calls=%async_computation.1 | async-start | bytes 262144 | tf_op jit(solution)/shard_map/all_to_all | solution.py:354
  137.0 2.8 %copy-start = (f32[1,2048,768]{2,1,0:T(8,128)S(1)}, f32[1,2048,768]{2,1,0:T(8,128)}, u32[]{:S(2)}) copy-start(f32[1,2048,768]{2,1,0:T(8,128)} %refs_2_.5) | copy-start | bytes 18874372
  139.8 1.1 copy-start.1
  140.9 1.1 copy-start.2
  142.1 1.1 copy-start.3
  143.2 1.1 copy-start.4

commit v6 on v5

--- a/solution.py
+++ b/solution.py
@@ -47,22 +47,19 @@
 
 def pick_kernel(experts, islands, pieces, spot, *refs):
     sources, drift = refs[:5], refs[5]
-    outs, blocks = refs[6 : 6 + experts], refs[6 + experts : -6]
-    table, count, weight, tokens, grads, sems = refs[-6:]
-    loads = copy_all(sems, list(zip(sources, refs[-6:-1])))
+    outs, blocks = refs[6 : 6 + experts], refs[6 + experts : -10]
+    table, count, weight, tokens, grads, picked, cut, sems, in_sems, out_sems = refs[-10:]
+    loads = copy_all(sems, list(zip(sources, refs[-10:-5])))
     rows, columns = blocks[0].shape
-    pairs = []
+    pairs, stores = [], []
     for d, first, count_rows, target, at_row in pieces:
         at = partner(spot[3], d, islands)
         top = pl.multiple_of(lax.div(at, spot[4]) * rows, rows) + first
         left = pl.multiple_of(lax.rem(at, spot[4]) * columns, columns)
-        pairs.append(
-            (
-                drift.at[0, 0, pl.ds(top, count_rows), pl.ds(left, columns)],
-                blocks[target].at[pl.ds(at_row, count_rows)],
-            )
-        )
-    copies = copy_all(sems.at[pl.ds(5, len(pairs))], pairs)
+        place = pl.ds(sum(p[2] for p in pieces[: len(pairs)]), count_rows)
+        pairs.append((drift.at[0, 0, pl.ds(top, count_rows), pl.ds(left, columns)], cut.at[place]))
+        stores.append((cut.at[place], blocks[target].at[pl.ds(at_row, count_rows)]))
+    copies = copy_all(in_sems, pairs)
     for copy in loads:
         copy.wait()
 
@@ -73,17 +70,24 @@
     def column(row):
         return jnp.sum(jnp.where(rows == lanes, row, 0), axis=1, keepdims=True)
 
-    for d in range(experts):
+    done = []
+    for d in [*range(1, experts), 0]:
         to = partner(spot[0], d, experts)
         live = lax.broadcasted_iota(jnp.int32, (slots, 1), 0) < count[0, 0, to]
         token = column(table[0, 0, pl.ds(to, 1), :].astype(F32)).astype(jnp.int32)
         chance = column(weight[0, 0, pl.ds(to, 1), :])
         ids = lax.broadcasted_iota(jnp.int32, (slots, tokens.shape[1]), 1)
         picks = jnp.where((ids == token) & live, 1.0, 0.0).astype(BF16)
-        outs[d][:slots, :] = dot(picks, tokens[0], ((1,), (0,))).astype(BF16)
-        picked = dot(picks, grads[0], ((1,), (0,)))
-        outs[d][slots:, :] = (chance * picked).astype(BF16)
-    for copy in copies:
+        picked[d, :slots, :] = dot(picks, tokens[0], ((1,), (0,))).astype(BF16)
+        chosen = dot(picks, grads[0], ((1,), (0,)))
+        picked[d, slots:, :] = (chance * chosen).astype(BF16)
+        done.append(pltpu.make_async_copy(picked.at[d], outs[d], out_sems.at[len(pairs) + d]))
+        done[-1].start()
+    for n, copy in enumerate(copies):
+        copy.wait()
+        done.append(pltpu.make_async_copy(*stores[n], out_sems.at[n]))
+        done[-1].start()
+    for copy in done:
         copy.wait()
 
 
@@ -130,8 +134,8 @@
 
 
 def average_kernel(islands, entries, tiles, spot, norms, drift_sum, own, moved, *refs):
-    hiddens, handed = refs[:islands], refs[islands:-4]
-    scaled, notes, total, square = refs[-4:]
+    hiddens, handed = refs[:islands], refs[islands:-5]
+    *halves, notes, total, square = refs[-5:]
     rows = total.shape[0] // tiles
     group = norms.shape[0] // islands
     scales = []
@@ -160,16 +164,19 @@
     pl.when(spot[5] != 1)(lambda: compute(moved))
     peak = jnp.max(jnp.abs(total[...]))
     unit = jnp.maximum(peak, 1e-30) / 32768
-    scaled[...] = total[...] * (1 / unit)
+    for n, half in enumerate(halves):
+        size = half.shape[0]
+        value = total[n * size : (n + 1) * size, :] * (1 / unit)
+        spread_out = value * 8193.0
+        value = spread_out - (spread_out - value)
+        half[...] = jnp.where(jnp.abs(value) < 2.0**-13, 0.0, value)
     sublane = lax.broadcasted_iota(jnp.int32, notes.shape, 1)
     notes[...] = jnp.where(sublane == 0, jnp.sum(square[...]), unit)
 
 
-def hand_kernel(count, norms, *refs):
-    passed, joined = refs[-2:]
+def hand_kernel(count, *refs):
     for n in range(count):
-        joined[n] = refs[n][...]
-    passed[...] = norms[...]
+        refs[-1][n] = refs[n][...]
 
 
 def own_kernel(slots, block, slots_out, block_out):
@@ -179,31 +186,54 @@
 
 def update_kernel(entries, pieces, place, notes, momentum, *refs):
     values = refs[: len(pieces)]
-    new_momentum, outer_step, moved, step, sems = refs[-5:]
+    new_momentum, outer_step, moved, step, in_sems, out_sems = refs[-6:]
+    rows, columns = values[0].shape
+    spots, loads = [], []
+    for n, (d, first) in enumerate(pieces):
+        top = pl.multiple_of(pl.multiple_of(place[3 * d], 32) + first, 32)
+        left = pl.multiple_of(place[3 * d + 1], columns)
+        spots.append((0, pl.ds(top, rows), pl.ds(left, columns)))
+        loads.append(pltpu.make_async_copy(momentum.at[spots[n]], moved.at[n], in_sems.at[n]))
+        loads[-1].start()
     square = jnp.sum(notes[...], axis=0)[:1, :1]
     clip = jnp.minimum(1.0, 0.25 * math.sqrt(entries) / jnp.sqrt(square + 1e-06))
-    columns = values[0].shape[1]
     stored = []
-    for n, (d, first) in enumerate(pieces):
-        rows = values[n].shape[0]
-        top = pl.multiple_of(place[3 * d], 32) + first
-        left = pl.multiple_of(place[3 * d + 1], columns)
+    for n, (d, _) in enumerate(pieces):
         unit = notes[pl.ds(place[3 * d + 2], 1)][0, 1:2, :1]
-        for m in range(2):
-            size = rows // 2
-            here = pl.ds(m * size, size)
-            there = (0, pl.ds(pl.multiple_of(top + m * size, 32), size), pl.ds(left, columns))
-            clipped = (clip * unit) * values[n][here, :]
-            fresh = 0.9 * momentum[there] + clipped
-            moved[d, pl.ds(first + m * size, size), :] = fresh
-            step[d, pl.ds(first + m * size, size), :] = (0.7 * (clipped + 0.9 * fresh)).astype(BF16)
-            source = (d, pl.ds(first + m * size, size))
-            for k, (here_ref, there_ref) in enumerate(((moved, new_momentum), (step, outer_step))):
-                copy = pltpu.make_async_copy(here_ref.at[source], there_ref.at[there], sems.at[n, m, k])
-                copy.start()
-                stored.append(copy)
+        loads[n].wait()
+        clipped = (clip * unit) * values[n][...]
+        fresh = 0.9 * moved[n] + clipped
+        moved[n] = fresh
+        step[n] = (0.7 * (clipped + 0.9 * fresh)).astype(BF16)
+        for k, (here, there) in enumerate(((moved, new_momentum), (step, outer_step))):
+            stored.append(pltpu.make_async_copy(here.at[n], there.at[spots[n]], out_sems.at[n, k]))
+            stored[-1].start()
     for copy in stored:
         copy.wait()
+
+
+def update_pieces(entries, place, notes, momentum, values, outs, cost):
+    pieces, arrays = list(values), [v.astype(F32) for v in values.values()]
+    shape = (len(pieces), *arrays[0].shape)
+    return pl.pallas_call(
+        lambda *refs: update_kernel(entries, pieces, *refs),
+        in_specs=[SMEM, VMEM, ANY] + [VMEM] * len(pieces) + [ANY] * len(outs),
+        out_specs=[ANY, ANY],
+        out_shape=[
+            jax.ShapeDtypeStruct(momentum.shape, F32),
+            jax.ShapeDtypeStruct(momentum.shape, BF16),
+        ],
+        scratch_shapes=[
+            pltpu.VMEM(shape, F32),
+            pltpu.VMEM(shape, BF16),
+            pltpu.SemaphoreType.DMA((len(pieces),)),
+            pltpu.SemaphoreType.DMA((len(pieces), 2)),
+        ],
+        input_output_aliases={3 + len(pieces) + n: n for n in range(len(outs))},
+        cost_estimate=pl.CostEstimate(flops=0, bytes_accessed=cost, transcendentals=0),
+        compiler_params=params(50),
+        name="update_pieces",
+    )(place, notes, momentum, *arrays, *outs)
 
 
 def body(
@@ -241,7 +271,7 @@
     picked = pl.pallas_call(
         lambda *refs: pick_kernel(experts, islands, pieces, *refs),
         in_specs=[SMEM] + [ANY] * 6,
-        out_specs=[VMEM] * (experts + len(steps)),
+        out_specs=[ANY] * (experts + len(steps)),
         out_shape=[jax.ShapeDtypeStruct((2 * slots, half), BF16)] * experts
         + [jax.ShapeDtypeStruct((rows, columns), BF16) for rows in block_rows],
         scratch_shapes=[
@@ -250,7 +280,11 @@
             pltpu.VMEM(slot_prob.shape, F32),
             pltpu.VMEM(tokens.shape, BF16),
             pltpu.VMEM(token_grads.shape, BF16),
-            pltpu.SemaphoreType.DMA((5 + len(pieces),)),
+            pltpu.VMEM((experts, 2 * slots, half), BF16),
+            pltpu.VMEM((sum(p[2] for p in pieces), columns), BF16),
+            pltpu.SemaphoreType.DMA((5,)),
+            pltpu.SemaphoreType.DMA((len(pieces),)),
+            pltpu.SemaphoreType.DMA((len(pieces) + experts,)),
         ],
         compiler_params=params(56),
         name="pick_slots",
@@ -325,74 +359,57 @@
     hidden_of = [hidden_out[0]] + [
         swap(hidden_for(d), "island", d) for d in range(1, islands)
     ]
-    norms, features_in = pl.pallas_call(
+    norms = lax.all_to_all(norms, AXES, split_axis=0, concat_axis=0, tiled=True)
+    features_in = pl.pallas_call(
         lambda *refs: hand_kernel(islands, *refs),
-        in_specs=[VMEM] * (islands + 1) + [ANY] * len(relays),
-        out_specs=[VMEM] * 2,
-        out_shape=[
-            jax.ShapeDtypeStruct(norms.shape, F32),
-            jax.ShapeDtypeStruct((islands, half, routed_rows), BF16),
-        ],
+        in_specs=[VMEM] * islands + [ANY] * (1 + len(relays)),
+        out_specs=VMEM,
+        out_shape=jax.ShapeDtypeStruct((islands, half, routed_rows), BF16),
         compiler_params=params(4 + routed_rows // 48),
         name="hand_features",
-    )(norms, turned, *features_in, *relays)
+    )(turned, *features_in, norms, *relays)
     features_moved = spread(features_in)
-    norms = lax.all_to_all(norms, AXES, split_axis=0, concat_axis=0, tiled=True)
-
-    scaled, notes = pl.pallas_call(
+
+    *halves, notes = pl.pallas_call(
         lambda *refs: average_kernel(islands, entries, 4, *refs),
         in_specs=[SMEM] + [VMEM] * (4 + islands + len(relays)),
-        out_specs=[VMEM] * 2,
-        out_shape=[
-            jax.ShapeDtypeStruct((half, columns), F32),
-            jax.ShapeDtypeStruct((devices, 8, 128), F32),
-        ],
+        out_specs=[VMEM] * 3,
+        out_shape=[jax.ShapeDtypeStruct((half // 2, columns), F32)] * 2
+        + [jax.ShapeDtypeStruct((devices, 8, 128), F32)],
         scratch_shapes=[pltpu.VMEM((half, columns), F32), pltpu.VMEM((1, columns), F32)],
         compiler_params=params(8 + routed_rows // 48),
         name="average_block",
     )(spot, norms, drift_sum, features_in, features_moved, *hidden_of, *relays)
     notes = lax.all_to_all(notes, AXES, split_axis=0, concat_axis=0, tiled=True)
 
-    parted = half // 2 if islands == 4 else half
-    sent = [scaled[first : first + parted].astype(WIRE) for first in range(0, half, parted)]
-    values = {(0, 0): lax.reduce_precision(scaled, 5, 10)}
+    parted = half // 2
+    sent = [v.astype(WIRE) for v in halves]
+    values = {(0, 0): halves[0], (0, parted): halves[1]}
+    last = {}
     if islands == 4:
+        nothing = jnp.minimum(notes[0, 1:2, :1], 0.0).astype(WIRE)
+
+        def after_notes(value):
+            return lax.dynamic_update_slice(value, value[:1, :128] + nothing, (0, 0))
+
+        values[2, 0], values[1, parted] = swap(sent[0], "island", 2), swap(sent[1], "island", 1)
         beside, below = swap(sent[0], "island", 1), swap(sent[1], "island", 2)
+        beside, below = after_notes(beside), after_notes(below)
         values[1, 0], values[2, parted] = beside, below
-        values[2, 0], values[1, parted] = swap(sent[0], "island", 2), swap(sent[1], "island", 1)
-        values[3, 0], values[3, parted] = swap(beside, "island", 2), swap(below, "island", 1)
+        last[3, 0], last[3, parted] = swap(beside, "island", 2), swap(below, "island", 1)
     else:
         for d in range(1, islands):
-            values[d, 0] = swap(sent[0], "island", d)
+            for n in range(2):
+                last[d, n * parted] = swap(sent[n], "island", d)
     place = []
     for d in range(islands):
         at = origin(island, d, islands)
         source = (at * experts + expert) * parts + part
         place += [(at // across) * half, (at % across) * columns, source]
-    block = (islands, half, columns)
-    return tuple(
-        pl.pallas_call(
-            lambda *refs: update_kernel(entries, list(values), *refs),
-            in_specs=[SMEM] + [VMEM] * (2 + len(values)),
-            out_specs=[ANY, ANY],
-            out_shape=[
-                jax.ShapeDtypeStruct(momentum.shape, F32),
-                jax.ShapeDtypeStruct(momentum.shape, BF16),
-            ],
-            scratch_shapes=[
-                pltpu.VMEM(block, F32),
-                pltpu.VMEM(block, BF16),
-                pltpu.SemaphoreType.DMA((len(values), 2, 2)),
-            ],
-            compiler_params=params(14),
-            name="update_outputs",
-        )(
-            jnp.stack(place).astype(jnp.int32),
-            notes,
-            momentum,
-            *[v.astype(F32) for v in values.values()],
-        )
-    )
+    place = jnp.stack(place).astype(jnp.int32)
+    outs = update_pieces(entries, place, notes, momentum, values, [], 12 * momentum.size)
+    outs = update_pieces(entries, place, notes, momentum, last, outs, 3 * momentum.size)
+    return tuple(outs)
 
 
 def solution(mesh):

time: 152 us -> 150 us (0.987); the launches traced: 149 us -> 149 us
  blocking collectives: 16.5 us -> 0 us
  starting transfers between devices: 35.1 us -> 47.8 us
  Pallas kernels: 20.6 us -> 28.4 us
  other arithmetic: 10.6 us -> 6.67 us
  local copies, waits for them, and re-layouts: 11.2 us -> 8.89 us
    all_to_all x1 -> x0, blocking collectives: 16.5 us -> none  [body(): norms = lax.all_to_all(norms, AXES, split_axis=0, concat_axis=0, tiled=True)]
    all_to_all x0 -> x1, starting transfers between devices: none -> 8.36 us  [body(): norms = lax.all_to_all(norms, AXES, split_axis=0, concat_axis=0, tiled=True)]
    convert_element_type x6 -> x8, other arithmetic: 9.84 us -> 5.3 us  [the longest x6 5.2 us: update_pieces(): pieces, arrays = (list(values), [v.astype(F32) for v in values.values()])]
    unnamed x20 -> x22, local copies, waits for them, and re-layouts: 9.46 us -> 4.99 us
    all_to_all x1, waiting for transfers between devices: 0.01 us -> 4.26 us  [body(): notes = lax.all_to_all(notes, AXES, split_axis=0, concat_axis=0, tiled=True)]
    pallas_call x1 -> x2, Pallas kernels: 4.63 us -> 8.86 us  [update_pieces(): pl.pallas_call(lambda *refs: update_kernel(entries, pieces, *refs), in_sp...]
    ppermute x17, waiting for transfers between devices: 54 us -> 50.9 us  [swap(): lax.ppermute(value, axis, [(at, partner(at, step, size)) for at in range(...]
    ppermute x17, starting transfers between devices: 21.2 us -> 23.8 us  [swap(): lax.ppermute(value, axis, [(at, partner(at, step, size)) for at in range(...]
  transfers between devices with their start and end apart: 22 -> 23, of which waited for: 5 -> 10; matrix products, arithmetic and copies ran while one was open for 7% -> 6% of each run, Pallas kernels for 4% -> 8%
where the time goes in v6:
time: 150 us; the launch traced here: 149 us
  waiting for transfers between devices  55.3 us (37%)
  starting transfers between devices  47.8 us (32%)
  Pallas kernels  28.4 us (19%)
  local copies, waits for them, and re-layouts  8.89 us (6%)
  other arithmetic  6.67 us (4%)
  between operations  1.68 us (1%)
    ppermute x17, waiting for transfers between devices, swap(): lax.ppermute(value, axis, [(at, partner(at, step, size)) for at in range(...  50.9 us
    ppermute x17, starting transfers between devices, swap(): lax.ppermute(value, axis, [(at, partner(at, step, size)) for at in range(...  23.8 us
    pallas_call x2, Pallas kernels, update_pieces(): pl.pallas_call(lambda *refs: update_kernel(entries, pieces, *refs), in_sp...  8.86 us
    all_to_all x1, starting transfers between devices, body(): notes = lax.all_to_all(notes, AXES, split_axis=0, concat_axis=0, tiled=True)  8.37 us
    all_to_all x1, starting transfers between devices, body(): norms = lax.all_to_all(norms, AXES, split_axis=0, concat_axis=0, tiled=True)  8.36 us
    pallas_call x1, Pallas kernels, body(): pl.pallas_call(lambda *refs: hidden_kernel(parts, across, *refs), in_spec...  6.09 us
    pallas_call x1, Pallas kernels, body(): pl.pallas_call(lambda *refs: pick_kernel(experts, islands, pieces, *refs)...  5.82 us
    convert_element_type x6, other arithmetic, update_pieces(): pieces, arrays = (list(values), [v.astype(F32) for v in values.values()])  5.2 us
  transfers between devices with their start and end apart: 23, of which 10 were waited for; matrix products, arithmetic and copies ran while one was open for 6% of the time, Pallas kernels for 8%

profile of v6, /device:TPU:0, one launch (start us, length us, event | category | flops | bytes accessed | tf_op | source)
XLA Modules:
  0.0 148.8 jit_solution(13434873365413934990)
XLA Ops:
  0.7 0.7 stack.79.refs_0_
  1.3 5.8 %pick_slots.1 = (bf16[192,1024]{1,0:T(8,128)(2,1)}, bf16[192,1024]{1,0:T(8,128)(2,1)}, bf16[192,1024]{1,0:T(8,128)(2,1)}, bf16[192,1024]{1,0:T(8,128)(2,1)}, bf1...) custom-call(s32[6]{0:T(128)} %stack.79.refs_0_, s32[1,1,4,96]{3,2,1,0:T(4,128)} %refs_1_.2, ...), custom_call_target="tpu_custom_call" | custom-call | tf_op jit(solution)/shard_map/pick_slots/pallas_call | solution.py:271
  7.2 0.0 copy-start
  7.2 3.0 %collective-permute-start.3 = (bf16[1536,384]{1,0:T(8,128)(2,1)}, bf16[1536,384]{1,0:T(8,128)(2,1)S(1)}, u32[]{:S(2)}, u32[]{:S(2)}) collective-permute-start(bf16[1536,384]{1,0:T(8,128)(2,1)} %get-tuple-element.31), channel_id=1, source_target_pairs={{0,8},{8,0},{16,24},{24,16},{1,9},{9,1},{17,25},{25,17},{2,10},{10... | collective-permute-start | bytes 3538952 | tf_op jit(solution)/shard_map/ppermute | solution.py:34
  10.2 1.5 %collective-permute-start.4 = (bf16[1536,384]{1,0:T(8,128)(2,1)}, bf16[1536,384]{1,0:T(8,128)(2,1)S(1)}, u32[]{:S(2)}, u32[]{:S(2)}) collective-permute-start(bf16[1536,384]{1,0:T(8,128)(2,1)} %get-tuple-element.32), channel_id=1, source_target_pairs={{0,16},{8,24},{16,0},{24,8},{1,17},{9,25},{17,1},{25,9},{2,18},{10... | collective-permute-start | bytes 3538952 | tf_op jit(solution)/shard_map/ppermute | solution.py:34
  11.7 1.6 %collective-permute-start = (bf16[192,1024]{1,0:T(8,128)(2,1)}, bf16[192,1024]{1,0:T(8,128)(2,1)S(1)}, u32[]{:S(2)}, u32[]{:S(2)}) collective-permute-start(bf16[192,1024]{1,0:T(8,128)(2,1)} %get-tuple-element.27), channel_id=1, source_target_pairs={{0,2},{2,0},{4,6},{6,4},{1,3},{3,1},{5,7},{7,5},{8,10},{10,8},{12,... | collective-permute-start | bytes 1179656 | tf_op jit(solution)/shard_map/ppermute | solution.py:34
  13.3 2.6 %collective-permute-start.1 = (bf16[192,1024]{1,0:T(8,128)(2,1)}, bf16[192,1024]{1,0:T(8,128)(2,1)S(1)}, u32[]{:S(2)}, u32[]{:S(2)}) collective-permute-start(bf16[192,1024]{1,0:T(8,128)(2,1)} %get-tuple-element.28), channel_id=1, source_target_pairs={{0,4},{2,6},{4,0},{6,2},{1,5},{3,7},{5,1},{7,3},{8,12},{10,14},{12... | collective-permute-start | bytes 1179656 | tf_op jit(solution)/shard_map/ppermute | solution.py:34
  15.9 0.2 collective-permute-start.2
  16.1 1.1 copy-done.4
  17.2 1.0 copy-done.5
  18.2 0.1 own_parts.1
  18.3 11.3 %collective-permute-done.refs_1_ = bf16[192,1024]{1,0:T(8,128)(2,1)S(1)} collective-permute-done((bf16[192,1024]{1,0:T(8,128)(2,1)}, bf16[192,1024]{1,0:T(8,128)(2,1)S(1)}, u32[]{:S(2)}, u32[]{:S(2)}) %collective-permute-start) | collective-permute-done | bytes 393248 | tf_op jit(solution)/shard_map/ppermute | solution.py:34
  29.6 13.7 %collective-permute-done.1.refs_2_ = bf16[192,1024]{1,0:T(8,128)(2,1)S(1)} collective-permute-done((bf16[192,1024]{1,0:T(8,128)(2,1)}, bf16[192,1024]{1,0:T(8,128)(2,1)S(1)}, u32[]{:S(2)}, u32[]{:S(2)}) %collective-permute-start.1) | collective-permute-done | bytes 393248 | tf_op jit(solution)/shard_map/ppermute | solution.py:34
  43.3 0.0 collective-permute-done.2.refs_3_
  43.3 0.0 collective-permute-done.3.refs_5_
  43.3 1.4 join_slots.1
  44.7 0.0 collective-permute-start.5
  44.7 1.3 collective-permute-start.8
  46.0 1.3 collective-permute-start.7
  47.3 2.4 %collective-permute-start.6 = (bf16[1024,384]{1,0:T(8,128)(2,1)S(1)}, bf16[1024,384]{1,0:T(8,128)(2,1)}, u32[]{:S(2)}, u32[]{:S(2)}) collective-permute-start(bf16[1024,384]{1,0:T(8,128)(2,1)S(1)} %get-tuple-element.36.refs_0_), channel_id=1, source_target_pairs={{0,8},{8,0},{17,25},{25,17},{2,10},{10,2},{19,27},{27,19},{4,12},{... | collective-permute-start | bytes 2359304 | tf_op jit(solution)/shard_map/ppermute | solution.py:328
  49.7 1.8 %collective-permute-start.9 = (bf16[512,384]{1,0:T(8,128)(2,1)}, bf16[512,384]{1,0:T(8,128)(2,1)S(1)}, u32[]{:S(2)}, u32[]{:S(2)}) collective-permute-start(bf16[512,384]{1,0:T(8,128)(2,1)} %get-tuple-element.37), channel_id=1, source_target_pairs={{0,16},{8,24},{16,0},{24,8},{1,17},{9,25},{17,1},{25,9},{2,18},{10... | collective-permute-start | bytes 1179656 | tf_op jit(solution)/shard_map/ppermute | solution.py:34
  51.5 1.5 %collective-permute-start.10 = (bf16[512,384]{1,0:T(8,128)(2,1)}, bf16[512,384]{1,0:T(8,128)(2,1)S(1)}, u32[]{:S(2)}, u32[]{:S(2)}) collective-permute-start(bf16[512,384]{1,0:T(8,128)(2,1)} %get-tuple-element.38), channel_id=1, source_target_pairs={{0,8},{8,0},{16,24},{24,16},{1,9},{9,1},{17,25},{25,17},{2,10},{10... | collective-permute-start | bytes 1179656 | tf_op jit(solution)/shard_map/ppermute | solution.py:34
  53.0 6.1 %hidden_grads.1 = (bf16[384,384]{1,0:T(8,128)(2,1)S(1)}, bf16[384,384]{1,0:T(8,128)(2,1)S(1)}, f32[32,8,128]{2,1,0:T(8,128)}) custom-call(s32[6]{0:T(128)S(1)} %copy-done.8, bf16[1,1,2048,768]{3,2,1,0:T(8,128)(2,1)S(1)} %copy-done, bf16[1,1,768,2048]{3,2,1,0:T(8,128)(2,1)S(1)} %copy-done.1, bf16[768,1024]{1,0:T(8,128)(2,1)S(1)} %get-tuple-element.33.refs_3_, ...), custom_call_target="tpu_custom_call" | custom-call | tf_op jit(solution)/shard_map/hidden_grads/pallas_call | solution.py:344
  59.1 0.7 copy-done.6
  59.9 0.7 copy-done.9
  60.6 8.4 %all-to-all-start = ((f32[32,8,128]{2,1,0:T(8,128)}), f32[32,8,128]{2,1,0:T(8,128)S(1)}, u32[]{:S(2)}, u32[]{:S(2)}) async-start(f32[32,8,128]{2,1,0:T(8,128)} %get-tuple-element.34), calls=%async_computation | async-start | bytes 262144 | tf_op jit(solution)/shard_map/all_to_all | solution.py:362
  68.9 8.5 %collective-permute-done.9.refs_5_.refs_9_ = bf16[512,384]{1,0:T(8,128)(2,1)S(1)} collective-permute-done((bf16[512,384]{1,0:T(8,128)(2,1)}, bf16[512,384]{1,0:T(8,128)(2,1)S(1)}, u32[]{:S(2)}, u32[]{:S(2)}) %collective-permute-start.9) | collective-permute-done | bytes 393248 | tf_op jit(solution)/shard_map/ppermute | solution.py:34
  77.5 0.2 all-to-all-done.refs_4_.refs_1_
  77.7 1.5 hand_features.1.refs_3_
  79.1 2.2 %collective-permute-start.11 = (bf16[4,1024,384]{2,1,0:T(8,128)(2,1)S(1)}, bf16[4,1024,384]{2,1,0:T(8,128)(2,1)S(1)}, u32[]{:S(2)}, u32[]{:S(2)}) collective-permute-start(bf16[4,1024,384]{2,1,0:T(8,128)(2,1)S(1)} %hand_features.1.refs_3_), channel_id=1, source_target_pairs={{0,1},{8,9},{17,16},{25,24},{2,3},{10,11},{19,18},{27,26},{4,5},{1... | collective-permute-start | bytes 9437192 | tf_op jit(solution)/shard_map/ppermute | solution.py:337
  81.3 0.1 collective-permute-start.13
  81.4 2.1 %collective-permute-start.14 = (bf16[384,384]{1,0:T(8,128)(2,1)S(1)}, bf16[384,384]{1,0:T(8,128)(2,1)S(1)}, u32[]{:S(2)}, u32[]{:S(2)}) collective-permute-start(bf16[384,384]{1,0:T(8,128)(2,1)S(1)} %copy-done.10), channel_id=1, source_target_pairs={{0,24},{8,16},{16,8},{24,0},{1,25},{9,17},{17,9},{25,1},{2,26},{10... | collective-permute-start | bytes 884744 | tf_op jit(solution)/shard_map/ppermute | solution.py:34
  83.5 1.4 collective-permute-start.12
  84.9 11.0 %collective-permute-done.13.refs_7_ = bf16[384,384]{1,0:T(8,128)(2,1)S(1)} collective-permute-done((bf16[384,384]{1,0:T(8,128)(2,1)S(1)}, bf16[384,384]{1,0:T(8,128)(2,1)S(1)}, u32[]{:S(2)}, u32[]{:S(2)}) %collective-permute-start.13) | collective-permute-done | bytes 294944 | tf_op jit(solution)/shard_map/ppermute | solution.py:34
  95.9 1.3 collective-permute-done.12.refs_6_
  97.2 1.4 copy-done.3
  98.6 4.7 %average_block.1 = (f32[512,384]{1,0:T(8,128)S(1)}, f32[512,384]{1,0:T(8,128)S(1)}, f32[32,8,128]{2,1,0:T(8,128)}) custom-call(s32[6]{0:T(128)S(1)} %copy-done.8, f32[32,8,128]{2,1,0:T(8,128)S(1)} %all-to-all-done.refs_4_.refs_1_, f32[1024,384]{1,0:T(8,128)S(1)} %copy-done.3, bf16[4,1024,384]{2,1,0:T(8,128)(2,1)S(1)} %hand_features.1.refs_3_, ...), custom_call_target="tpu_custom_call" | custom-call | tf_op jit(solution)/shard_map/average_block/pallas_call | solution.py:373
  103.3 0.1 convert_element_type.32
  103.4 1.7 %collective-permute-start.17 = (f16[512,384]{1,0:T(8,128)(2,1)S(1)}, f16[512,384]{1,0:T(8,128)(2,1)}, u32[]{:S(2)}, u32[]{:S(2)}) collective-permute-start(f16[512,384]{1,0:T(8,128)(2,1)S(1)} %convert_element_type.32), channel_id=1, source_target_pairs={{0,16},{8,24},{16,0},{24,8},{1,17},{9,25},{17,1},{25,9},{2,18},{10... | collective-permute-start | bytes 1179656 | tf_op jit(solution)/shard_map/ppermute | solution.py:34
  105.1 8.4 %all-to-all-start.1 = ((f32[32,8,128]{2,1,0:T(8,128)}), f32[32,8,128]{2,1,0:T(8,128)S(1)}, u32[]{:S(2)}, u32[]{:S(2)}) async-start(f32[32,8,128]{2,1,0:T(8,128)} %get-tuple-element.41), calls=%async_computation.1 | async-start | bytes 262144 | tf_op jit(solution)/shard_map/all_to_all | solution.py:383
  113.5 0.1 convert_element_type.29
  113.6 1.8 %collective-permute-start.15 = (f16[512,384]{1,0:T(8,128)(2,1)S(1)}, f16[512,384]{1,0:T(8,128)(2,1)}, u32[]{:S(2)}, u32[]{:S(2)}) collective-permute-start(f16[512,384]{1,0:T(8,128)(2,1)S(1)} %convert_element_type.29), channel_id=1, source_target_pairs={{0,8},{8,0},{16,24},{24,16},{1,9},{9,1},{17,25},{25,17},{2,10},{10... | collective-permute-start | bytes 1179656 | tf_op jit(solution)/shard_map/ppermute | solution.py:34
  115.4 0.3 collective-permute-start.20
  115.6 1.8 %collective-permute-start.19 = (f16[512,384]{1,0:T(8,128)(2,1)S(1)}, f16[512,384]{1,0:T(8,128)(2,1)S(1)}, u32[]{:S(2)}, u32[]{:S(2)}) collective-permute-start(f16[512,384]{1,0:T(8,128)(2,1)S(1)} %convert_element_type.29), channel_id=1, source_target_pairs={{0,16},{8,24},{16,0},{24,8},{1,17},{9,25},{17,1},{25,9},{2,18},{10... | collective-permute-start | bytes 1179656 | tf_op jit(solution)/shard_map/ppermute | solution.py:34
  117.4 4.3 %all-to-all-done.1.refs_1_ = f32[32,8,128]{2,1,0:T(8,128)S(1)} async-done(((f32[32,8,128]{2,1,0:T(8,128)}), f32[32,8,128]{2,1,0:T(8,128)S(1)}, u32[]{:S(2)}, u32[]{:S(2)}) %all-to-all-start.1) | async-done | bytes 131104 | tf_op jit(solution)/shard_map/all_to_all | solution.py:383
  121.7 0.5 slice.13
  122.9 0.7 slice_add_fusion
  123.5 1.3 dynamic_update_slice.7
  124.9 0.8 collective-permute-start.18
  125.7 1.1 collective-permute-done.15
  126.7 0.7 slice_add_fusion.1
  127.4 1.3 dynamic_update_slice.6
  128.7 1.7 %collective-permute-start.16 = (f16[512,384]{1,0:T(8,128)(2,1)}, f16[512,384]{1,0:T(8,128)(2,1)}, u32[]{:S(2)}, u32[]{:S(2)}) collective-permute-start(f16[512,384]{1,0:T(8,128)(2,1)} %dynamic_update_slice.6), channel_id=1, source_target_pairs={{0,16},{8,24},{16,0},{24,8},{1,17},{9,25},{17,1},{25,9},{2,18},{10... | collective-permute-start | bytes 1179656 | tf_op jit(solution)/shard_map/ppermute | solution.py:34
  130.4 0.1 stack.72.refs_0_
  130.5 1.1 convert_element_type.36.refs_7_
  131.6 1.9 %convert_element_type.37.refs_8_ = f32[512,384]{1,0:T(8,128)} convert(f16[512,384]{1,0:T(8,128)(2,1)} %dynamic_update_slice.7) | non-fusion elementwise | flops 196608 | bytes 1179648 | tf_op jit(solution)/shard_map/convert_element_type | solution.py:216
  133.5 1.6 %collective-permute-done.20 = f16[512,384]{1,0:T(8,128)(2,1)S(1)} collective-permute-done((f16[512,384]{1,0:T(8,128)(2,1)S(1)}, f16[512,384]{1,0:T(8,128)(2,1)S(1)}, u32[]{:S(2)}, u32[]{:S(2)}) %collective-permute-start.20) | collective-permute-done | bytes 393248 | tf_op jit(solution)/shard_map/ppermute | solution.py:34
  135.1 0.1 convert_element_type.35.refs_6_
  135.1 0.1 convert_element_type.34.refs_5_
  135.2 5.5 %update_pieces.2 = (f32[1,2048,768]{2,1,0:T(8,128)}, bf16[1,2048,768]{2,1,0:T(8,128)(2,1)}) custom-call(s32[12]{0:T(128)S(1)} %stack.72.refs_0_, f32[32,8,128]{2,1,0:T(8,128)S(1)} %all-to-all-done.1.refs_1_, f32[1,2048,768]{2,1,0:T(8,128)} %refs_2_.7, f32[512,384]{1,0:T(8,128)S(1)} %get-tuple-element.42.refs_3_, f32[512,384]{1,0:T(8,128)S(1)} %get-tuple-element.43.refs_4_, ...), custom_call_target="tpu_custom_call" | custom-call | bytes 18874368 | tf_op jit(solution)/shard_map/update_pieces/pallas_call | solution.py:218
  140.7 2.4 %collective-permute-done.18 = f16[512,384]{1,0:T(8,128)(2,1)} collective-permute-done((f16[512,384]{1,0:T(8,128)(2,1)}, f16[512,384]{1,0:T(8,128)(2,1)}, u32[]{:S(2)}, u32[]{:S(2)}) %collective-permute-start.18) | collective-permute-done | bytes 393248 | tf_op jit(solution)/shard_map/ppermute | solution.py:34
  143.1 1.0 convert_element_type.33.refs_4_
  144.2 1.0 convert_element_type.31.refs_3_
  145.3 3.3 %update_pieces.3 = (f32[1,2048,768]{2,1,0:T(8,128)}, bf16[1,2048,768]{2,1,0:T(8,128)(2,1)}) custom-call(s32[12]{0:T(128)S(1)} %stack.72.refs_0_, f32[32,8,128]{2,1,0:T(8,128)S(1)} %all-to-all-done.1.refs_1_, f32[1,2048,768]{2,1,0:T(8,128)} %refs_2_.7, f32[512,384]{1,0:T(8,128)S(1)} %convert_element_type.31.refs_3_, ...), custom_call_target="tpu_custom_call", output_to_operand_aliasing={{0}: (5, {}), {1}: (6, {})} | custom-call | bytes 4718592 | tf_op jit(solution)/shard_map/update_pieces/pallas_call | solution.py:218
  (27 shorter events, 0.1 us)
Async XLA Ops:
  1.3 51.7 %copy-start.1 = (bf16[1,1,768,2048]{3,2,1,0:T(8,128)(2,1)S(1)}, bf16[1,1,768,2048]{3,2,1,0:T(8,128)(2,1)}, u32[]{:S(2)}) copy-start(bf16[1,1,768,2048]{3,2,1,0:T(8,128)(2,1)} %refs_2_.5) | copy-start | bytes 9437188
  1.3 51.7 %copy-start.8 = (s32[6]{0:T(128)S(1)}, s32[6]{0:T(128)}, u32[]{:S(2)}) copy-start(s32[6]{0:T(128)} %stack.79.refs_0_) | copy-start | bytes 76
  7.2 45.9 %copy-start = (bf16[1,1,2048,768]{3,2,1,0:T(8,128)(2,1)S(1)}, bf16[1,1,2048,768]{3,2,1,0:T(8,128)(2,1)}, u32[]{:S(2)}) copy-start(bf16[1,1,2048,768]{3,2,1,0:T(8,128)(2,1)} %refs_1_.3) | copy-start | bytes 9437188
  7.2 36.1 %collective-permute-start.3 = (bf16[1536,384]{1,0:T(8,128)(2,1)}, bf16[1536,384]{1,0:T(8,128)(2,1)S(1)}, u32[]{:S(2)}, u32[]{:S(2)}) collective-permute-start(bf16[1536,384]{1,0:T(8,128)(2,1)} %get-tuple-element.31), channel_id=1, source_target_pairs={{0,8},{8,0},{16,24},{24,16},{1,9},{9,1},{17,25},{25,17},{2,10},{10... | collective-permute-start | bytes 3538952 | tf_op jit(solution)/shard_map/ppermute | solution.py:34
  10.2 33.1 %collective-permute-start.4 = (bf16[1536,384]{1,0:T(8,128)(2,1)}, bf16[1536,384]{1,0:T(8,128)(2,1)S(1)}, u32[]{:S(2)}, u32[]{:S(2)}) collective-permute-start(bf16[1536,384]{1,0:T(8,128)(2,1)} %get-tuple-element.32), channel_id=1, source_target_pairs={{0,16},{8,24},{16,0},{24,8},{1,17},{9,25},{17,1},{25,9},{2,18},{10... | collective-permute-start | bytes 3538952 | tf_op jit(solution)/shard_map/ppermute | solution.py:34
  11.7 17.9 %collective-permute-start = (bf16[192,1024]{1,0:T(8,128)(2,1)}, bf16[192,1024]{1,0:T(8,128)(2,1)S(1)}, u32[]{:S(2)}, u32[]{:S(2)}) collective-permute-start(bf16[192,1024]{1,0:T(8,128)(2,1)} %get-tuple-element.27), channel_id=1, source_target_pairs={{0,2},{2,0},{4,6},{6,4},{1,3},{3,1},{5,7},{7,5},{8,10},{10,8},{12,... | collective-permute-start | bytes 1179656 | tf_op jit(solution)/shard_map/ppermute | solution.py:34
  13.3 30.0 %collective-permute-start.1 = (bf16[192,1024]{1,0:T(8,128)(2,1)}, bf16[192,1024]{1,0:T(8,128)(2,1)S(1)}, u32[]{:S(2)}, u32[]{:S(2)}) collective-permute-start(bf16[192,1024]{1,0:T(8,128)(2,1)} %get-tuple-element.28), channel_id=1, source_target_pairs={{0,4},{2,6},{4,0},{6,2},{1,5},{3,7},{5,1},{7,3},{8,12},{10,14},{12... | collective-permute-start | bytes 1179656 | tf_op jit(solution)/shard_map/ppermute | solution.py:34
  15.9 27.4 %collective-permute-start.2 = (bf16[192,1024]{1,0:T(8,128)(2,1)}, bf16[192,1024]{1,0:T(8,128)(2,1)S(1)}, u32[]{:S(2)}, u32[]{:S(2)}) collective-permute-start(bf16[192,1024]{1,0:T(8,128)(2,1)} %get-tuple-element.29), channel_id=1, source_target_pairs={{0,6},{2,4},{4,2},{6,0},{1,7},{3,5},{5,3},{7,1},{8,14},{10,12},{12... | collective-permute-start | bytes 1179656 | tf_op jit(solution)/shard_map/ppermute | solution.py:34
  16.1 1.1 copy-start.4
  17.2 1.0 copy-start.5
  44.7 14.5 %copy-start.2 = (f32[1024,384]{1,0:T(8,128)}, f32[1024,384]{1,0:T(8,128)S(1)}, u32[]{:S(2)}) copy-start(f32[1024,384]{1,0:T(8,128)S(1)} %get-tuple-element.35.refs_2_) | copy-start | bytes 4718596
  44.7 6.9 %collective-permute-start.5 = (bf16[768,1024]{1,0:T(8,128)(2,1)S(1)}, bf16[768,1024]{1,0:T(8,128)(2,1)S(1)}, u32[]{:S(2)}, u32[]{:S(2)}) collective-permute-start(bf16[768,1024]{1,0:T(8,128)(2,1)S(1)} %get-tuple-element.33.refs_3_), channel_id=1, source_target_pairs={{0,1},{1,0},{2,3},{3,2},{4,5},{5,4},{6,7},{7,6},{8,9},{9,8},{10,11... | collective-permute-start | bytes 4718600 | tf_op jit(solution)/shard_map/ppermute | solution.py:34
  44.7 32.8 %collective-permute-start.8 = (bf16[1024,384]{1,0:T(8,128)(2,1)S(1)}, bf16[1024,384]{1,0:T(8,128)(2,1)S(1)}, u32[]{:S(2)}, u32[]{:S(2)}) collective-permute-start(bf16[1024,384]{1,0:T(8,128)(2,1)S(1)} %get-tuple-element.36.refs_0_), channel_id=1, source_target_pairs={{1,25},{9,17},{16,8},{24,0},{3,27},{11,19},{18,10},{26,2},{5,29},{... | collective-permute-start | bytes 2359304 | tf_op jit(solution)/shard_map/ppermute | solution.py:328
  46.0 31.5 %collective-permute-start.7 = (bf16[1024,384]{1,0:T(8,128)(2,1)S(1)}, bf16[1024,384]{1,0:T(8,128)(2,1)S(1)}, u32[]{:S(2)}, u32[]{:S(2)}) collective-permute-start(bf16[1024,384]{1,0:T(8,128)(2,1)S(1)} %get-tuple-element.36.refs_0_), channel_id=1, source_target_pairs={{1,17},{9,25},{16,0},{24,8},{3,19},{11,27},{18,2},{26,10},{5,21},{... | collective-permute-start | bytes 2359304 | tf_op jit(solution)/shard_map/ppermute | solution.py:328
  47.3 30.2 %collective-permute-start.6 = (bf16[1024,384]{1,0:T(8,128)(2,1)S(1)}, bf16[1024,384]{1,0:T(8,128)(2,1)}, u32[]{:S(2)}, u32[]{:S(2)}) collective-permute-start(bf16[1024,384]{1,0:T(8,128)(2,1)S(1)} %get-tuple-element.36.refs_0_), channel_id=1, source_target_pairs={{0,8},{8,0},{17,25},{25,17},{2,10},{10,2},{19,27},{27,19},{4,12},{... | collective-permute-start | bytes 2359304 | tf_op jit(solution)/shard_map/ppermute | solution.py:328
  49.7 27.8 %collective-permute-start.9 = (bf16[512,384]{1,0:T(8,128)(2,1)}, bf16[512,384]{1,0:T(8,128)(2,1)S(1)}, u32[]{:S(2)}, u32[]{:S(2)}) collective-permute-start(bf16[512,384]{1,0:T(8,128)(2,1)} %get-tuple-element.37), channel_id=1, source_target_pairs={{0,16},{8,24},{16,0},{24,8},{1,17},{9,25},{17,1},{25,9},{2,18},{10... | collective-permute-start | bytes 1179656 | tf_op jit(solution)/shard_map/ppermute | solution.py:34
  51.5 26.0 %collective-permute-start.10 = (bf16[512,384]{1,0:T(8,128)(2,1)}, bf16[512,384]{1,0:T(8,128)(2,1)S(1)}, u32[]{:S(2)}, u32[]{:S(2)}) collective-permute-start(bf16[512,384]{1,0:T(8,128)(2,1)} %get-tuple-element.38), channel_id=1, source_target_pairs={{0,8},{8,0},{16,24},{24,16},{1,9},{9,1},{17,25},{25,17},{2,10},{10... | collective-permute-start | bytes 1179656 | tf_op jit(solution)/shard_map/ppermute | solution.py:34
  59.1 0.7 copy-start.6
  59.9 0.7 copy-start.9
  60.6 17.1 %all-to-all-start = ((f32[32,8,128]{2,1,0:T(8,128)}), f32[32,8,128]{2,1,0:T(8,128)S(1)}, u32[]{:S(2)}, u32[]{:S(2)}) async-start(f32[32,8,128]{2,1,0:T(8,128)} %get-tuple-element.34), calls=%async_computation | async-start | bytes 262144 | tf_op jit(solution)/shard_map/all_to_all | solution.py:362
  77.7 3.7 %copy-start.7 = (bf16[384,384]{1,0:T(8,128)(2,1)S(1)}, bf16[384,384]{1,0:T(8,128)(2,1)}, u32[]{:S(2)}) copy-start(bf16[384,384]{1,0:T(8,128)(2,1)} %copy-done.6) | copy-start | bytes 884740
  77.7 3.7 %copy-start.10 = (bf16[384,384]{1,0:T(8,128)(2,1)S(1)}, bf16[384,384]{1,0:T(8,128)(2,1)}, u32[]{:S(2)}) copy-start(bf16[384,384]{1,0:T(8,128)(2,1)} %copy-done.9) | copy-start | bytes 884740
  79.1 18.1 %collective-permute-start.11 = (bf16[4,1024,384]{2,1,0:T(8,128)(2,1)S(1)}, bf16[4,1024,384]{2,1,0:T(8,128)(2,1)S(1)}, u32[]{:S(2)}, u32[]{:S(2)}) collective-permute-start(bf16[4,1024,384]{2,1,0:T(8,128)(2,1)S(1)} %hand_features.1.refs_3_), channel_id=1, source_target_pairs={{0,1},{8,9},{17,16},{25,24},{2,3},{10,11},{19,18},{27,26},{4,5},{1... | collective-permute-start | bytes 9437192 | tf_op jit(solution)/shard_map/ppermute | solution.py:337
  81.3 14.6 %collective-permute-start.13 = (bf16[384,384]{1,0:T(8,128)(2,1)S(1)}, bf16[384,384]{1,0:T(8,128)(2,1)S(1)}, u32[]{:S(2)}, u32[]{:S(2)}) collective-permute-start(bf16[384,384]{1,0:T(8,128)(2,1)S(1)} %copy-done.7), channel_id=1, source_target_pairs={{0,16},{8,24},{16,0},{24,8},{1,17},{9,25},{17,1},{25,9},{2,18},{10... | collective-permute-start | bytes 884744 | tf_op jit(solution)/shard_map/ppermute | solution.py:34
  81.4 14.5 %collective-permute-start.14 = (bf16[384,384]{1,0:T(8,128)(2,1)S(1)}, bf16[384,384]{1,0:T(8,128)(2,1)S(1)}, u32[]{:S(2)}, u32[]{:S(2)}) collective-permute-start(bf16[384,384]{1,0:T(8,128)(2,1)S(1)} %copy-done.10), channel_id=1, source_target_pairs={{0,24},{8,16},{16,8},{24,0},{1,25},{9,17},{17,9},{25,1},{2,26},{10... | collective-permute-start | bytes 884744 | tf_op jit(solution)/shard_map/ppermute | solution.py:34
  83.5 13.7 %collective-permute-start.12 = (bf16[384,384]{1,0:T(8,128)(2,1)S(1)}, bf16[384,384]{1,0:T(8,128)(2,1)S(1)}, u32[]{:S(2)}, u32[]{:S(2)}) collective-permute-start(bf16[384,384]{1,0:T(8,128)(2,1)S(1)} %copy-done.10), channel_id=1, source_target_pairs={{0,8},{8,0},{16,24},{24,16},{1,9},{9,1},{17,25},{25,17},{2,10},{10... | collective-permute-start | bytes 884744 | tf_op jit(solution)/shard_map/ppermute | solution.py:34
  97.2 1.4 copy-start.3
  103.4 19.4 %collective-permute-start.17 = (f16[512,384]{1,0:T(8,128)(2,1)S(1)}, f16[512,384]{1,0:T(8,128)(2,1)}, u32[]{:S(2)}, u32[]{:S(2)}) collective-permute-start(f16[512,384]{1,0:T(8,128)(2,1)S(1)} %convert_element_type.32), channel_id=1, source_target_pairs={{0,16},{8,24},{16,0},{24,8},{1,17},{9,25},{17,1},{25,9},{2,18},{10... | collective-permute-start | bytes 1179656 | tf_op jit(solution)/shard_map/ppermute | solution.py:34
  105.1 16.6 %all-to-all-start.1 = ((f32[32,8,128]{2,1,0:T(8,128)}), f32[32,8,128]{2,1,0:T(8,128)S(1)}, u32[]{:S(2)}, u32[]{:S(2)}) async-start(f32[32,8,128]{2,1,0:T(8,128)} %get-tuple-element.41), calls=%async_computation.1 | async-start | bytes 262144 | tf_op jit(solution)/shard_map/all_to_all | solution.py:383
  113.6 13.2 %collective-permute-start.15 = (f16[512,384]{1,0:T(8,128)(2,1)S(1)}, f16[512,384]{1,0:T(8,128)(2,1)}, u32[]{:S(2)}, u32[]{:S(2)}) collective-permute-start(f16[512,384]{1,0:T(8,128)(2,1)S(1)} %convert_element_type.29), channel_id=1, source_target_pairs={{0,8},{8,0},{16,24},{24,16},{1,9},{9,1},{17,25},{25,17},{2,10},{10... | collective-permute-start | bytes 1179656 | tf_op jit(solution)/shard_map/ppermute | solution.py:34
  115.4 19.7 %collective-permute-start.20 = (f16[512,384]{1,0:T(8,128)(2,1)S(1)}, f16[512,384]{1,0:T(8,128)(2,1)S(1)}, u32[]{:S(2)}, u32[]{:S(2)}) collective-permute-start(f16[512,384]{1,0:T(8,128)(2,1)S(1)} %convert_element_type.32), channel_id=1, source_target_pairs={{0,8},{8,0},{16,24},{24,16},{1,9},{9,1},{17,25},{25,17},{2,10},{10... | collective-permute-start | bytes 1179656 | tf_op jit(solution)/shard_map/ppermute | solution.py:34
  115.6 19.5 %collective-permute-start.19 = (f16[512,384]{1,0:T(8,128)(2,1)S(1)}, f16[512,384]{1,0:T(8,128)(2,1)S(1)}, u32[]{:S(2)}, u32[]{:S(2)}) collective-permute-start(f16[512,384]{1,0:T(8,128)(2,1)S(1)} %convert_element_type.29), channel_id=1, source_target_pairs={{0,16},{8,24},{16,0},{24,8},{1,17},{9,25},{17,1},{25,9},{2,18},{10... | collective-permute-start | bytes 1179656 | tf_op jit(solution)/shard_map/ppermute | solution.py:34
  124.9 18.3 %collective-permute-start.18 = (f16[512,384]{1,0:T(8,128)(2,1)}, f16[512,384]{1,0:T(8,128)(2,1)}, u32[]{:S(2)}, u32[]{:S(2)}) collective-permute-start(f16[512,384]{1,0:T(8,128)(2,1)} %dynamic_update_slice.7), channel_id=1, source_target_pairs={{0,8},{8,0},{16,24},{24,16},{1,9},{9,1},{17,25},{25,17},{2,10},{10... | collective-permute-start | bytes 1179656 | tf_op jit(solution)/shard_map/ppermute | solution.py:34
  128.7 15.5 %collective-permute-start.16 = (f16[512,384]{1,0:T(8,128)(2,1)}, f16[512,384]{1,0:T(8,128)(2,1)}, u32[]{:S(2)}, u32[]{:S(2)}) collective-permute-start(f16[512,384]{1,0:T(8,128)(2,1)} %dynamic_update_slice.6), channel_id=1, source_target_pairs={{0,16},{8,24},{16,0},{24,8},{1,17},{9,25},{17,1},{25,9},{2,18},{10... | collective-permute-start | bytes 1179656 | tf_op jit(solution)/shard_map/ppermute | solution.py:34

commit v7 on v6

--- a/solution.py
+++ b/solution.py
@@ -11,6 +11,7 @@
 BF16 = jnp.bfloat16
 WIRE = jnp.float16
 AXES = ("island", "expert", "tensor")
+NOTE_ROWS = 16
 
 VMEM = pl.BlockSpec(memory_space=pltpu.VMEM)
 SMEM = pl.BlockSpec(memory_space=pltpu.SMEM)
@@ -109,22 +110,22 @@
 
 
 def hidden_kernel(parts, across, spot, gate, down, *refs):
-    joined, outs, norms = refs[:parts], refs[parts : parts + across], refs[-1]
+    joined, out, norms = refs[:parts], refs[parts], refs[-1]
     rows, half = joined[0].shape[0] // 2, joined[0].shape[1]
-    columns = outs[0].shape[1]
+    columns = out.shape[2]
     starts = [pl.multiple_of(origin(spot[1], t, parts) * half, half) for t in range(parts)]
     hidden_gram = 0.0
     for r in range(across):
-        first = pl.multiple_of(partner(spot[2], r, across) * columns, columns)
+        first = r * columns
         value = 0.0
         back = 0.0
         for t in range(parts):
-            block = gate[0, 0, pl.ds(starts[t], half), pl.ds(first, columns)]
+            block = gate[0, 0, pl.ds(starts[t], half), first : first + columns]
             value = value + dot(joined[t][:rows, :], block, ((1,), (0,)))
-            block = down[0, 0, pl.ds(first, columns), pl.ds(starts[t], half)]
+            block = down[0, 0, first : first + columns, pl.ds(starts[t], half)]
             back = back + dot(joined[t][rows:, :], block, ((1,), (1,)))
         rounded = (back * (value / (1.0 + jnp.exp(-value)))).astype(BF16)
-        outs[r][...] = rounded
+        out[r] = rounded
         hidden_gram = hidden_gram + dot(rounded, rounded, ((1,), (1,)))
     input_gram = 0.0
     for t in range(parts):
@@ -133,16 +134,16 @@
     norms[...] = jnp.full(norms.shape, jnp.sum(hidden_gram * input_gram), F32)
 
 
-def average_kernel(islands, entries, tiles, spot, norms, drift_sum, own, moved, *refs):
-    hiddens, handed = refs[:islands], refs[islands:-5]
-    *halves, notes, total, square = refs[-5:]
+def average_kernel(islands, entries, tiles, spot, drift_sum, own, moved, *refs):
+    messages = refs[:islands]
+    *halves, notes, total, square = refs[islands:]
     rows = total.shape[0] // tiles
-    group = norms.shape[0] // islands
+    slots = own.shape[2]
     scales = []
-    for d in range(islands):
-        at = origin(spot[3], d, islands)
-        norm = jnp.sum(norms[pl.ds(at * group, group)], axis=0)[:1, :1]
+    for message in messages:
+        norm = sum(message[n : n + 1, :1].astype(F32) for n in range(3))
         scales.append(jnp.minimum(1.0, math.sqrt(entries) / jnp.sqrt(norm + 1e-06)) / islands)
+    handed = [m for m in messages[:0:-1] if m.shape[0] > NOTE_ROWS + slots]
 
     def compute(features):
         squares = 0.0
@@ -150,12 +151,14 @@
             part = slice(m * rows, (m + 1) * rows)
             average = drift_sum[part, :]
             if handed:
-                size = handed[0].shape[0]
+                size = handed[0].shape[0] - NOTE_ROWS - slots
                 n, first = divmod(m * rows, size)
+                first += NOTE_ROWS + slots
                 average = average + handed[n][first : first + rows, :].astype(F32)
             average = average * (1.0 / islands)
             for d in range(islands):
-                average = average + scales[d] * dot(features[d, part, :], hiddens[d][...], ((1,), (0,)))
+                factor = messages[d][NOTE_ROWS : NOTE_ROWS + slots, :]
+                average = average + scales[d] * dot(features[d, part, :], factor, ((1,), (0,)))
             total[part, :] = average
             squares = squares + jnp.sum(average * average, axis=0, keepdims=True)
         square[...] = squares
@@ -174,9 +177,25 @@
     notes[...] = jnp.where(sublane == 0, jnp.sum(square[...]), unit)
 
 
-def hand_kernel(count, *refs):
-    for n in range(count):
-        refs[-1][n] = refs[n][...]
+def hand_kernel(islands, tails, spot, norms, hidden, *refs):
+    features, relays = refs[:islands], refs[islands : islands + len(tails)]
+    joined, *messages = refs[islands + len(tails) :]
+    across, slots, columns = hidden.shape
+    for n in range(islands):
+        joined[n] = features[n][...]
+    left = jnp.sum(norms[...], axis=0)[:1, :1]
+    rows = lax.broadcasted_iota(jnp.int32, (NOTE_ROWS, columns), 0)
+    note = jnp.zeros((NOTE_ROWS, columns), F32)
+    for n in range(3):
+        summand = left.astype(BF16).astype(F32)
+        note = jnp.where(rows == n, summand, note)
+        left = left - summand
+    for d, message in enumerate(messages):
+        message[:NOTE_ROWS, :] = note.astype(BF16)
+        block = lax.rem(partner(spot[3], d, islands), across)
+        message[NOTE_ROWS : NOTE_ROWS + slots, :] = hidden[pl.ds(block, 1)][0]
+        if d in tails:
+            message[NOTE_ROWS + slots :, :] = relays[tails.index(d)][...]
 
 
 def own_kernel(slots, block, slots_out, block_out):
@@ -186,7 +205,7 @@
 
 def update_kernel(entries, pieces, place, notes, momentum, *refs):
     values = refs[: len(pieces)]
-    new_momentum, outer_step, moved, step, in_sems, out_sems = refs[-6:]
+    new_momentum, outer_step, moved, step, in_sems, sems = refs[-6:]
     rows, columns = values[0].shape
     spots, loads = [], []
     for n, (d, first) in enumerate(pieces):
@@ -198,42 +217,18 @@
     square = jnp.sum(notes[...], axis=0)[:1, :1]
     clip = jnp.minimum(1.0, 0.25 * math.sqrt(entries) / jnp.sqrt(square + 1e-06))
     stored = []
-    for n, (d, _) in enumerate(pieces):
+    for n, (d, first) in enumerate(pieces):
         unit = notes[pl.ds(place[3 * d + 2], 1)][0, 1:2, :1]
+        clipped = (clip * unit) * values[n][...]
         loads[n].wait()
-        clipped = (clip * unit) * values[n][...]
         fresh = 0.9 * moved[n] + clipped
         moved[n] = fresh
         step[n] = (0.7 * (clipped + 0.9 * fresh)).astype(BF16)
-        for k, (here, there) in enumerate(((moved, new_momentum), (step, outer_step))):
-            stored.append(pltpu.make_async_copy(here.at[n], there.at[spots[n]], out_sems.at[n, k]))
+        for k, (here, out) in enumerate(((moved, new_momentum), (step, outer_step))):
+            stored.append(pltpu.make_async_copy(here.at[n], out.at[spots[n]], sems.at[n, k]))
             stored[-1].start()
     for copy in stored:
         copy.wait()
-
-
-def update_pieces(entries, place, notes, momentum, values, outs, cost):
-    pieces, arrays = list(values), [v.astype(F32) for v in values.values()]
-    shape = (len(pieces), *arrays[0].shape)
-    return pl.pallas_call(
-        lambda *refs: update_kernel(entries, pieces, *refs),
-        in_specs=[SMEM, VMEM, ANY] + [VMEM] * len(pieces) + [ANY] * len(outs),
-        out_specs=[ANY, ANY],
-        out_shape=[
-            jax.ShapeDtypeStruct(momentum.shape, F32),
-            jax.ShapeDtypeStruct(momentum.shape, BF16),
-        ],
-        scratch_shapes=[
-            pltpu.VMEM(shape, F32),
-            pltpu.VMEM(shape, BF16),
-            pltpu.SemaphoreType.DMA((len(pieces),)),
-            pltpu.SemaphoreType.DMA((len(pieces), 2)),
-        ],
-        input_output_aliases={3 + len(pieces) + n: n for n in range(len(outs))},
-        cost_estimate=pl.CostEstimate(flops=0, bytes_accessed=cost, transcendentals=0),
-        compiler_params=params(50),
-        name="update_pieces",
-    )(place, notes, momentum, *arrays, *outs)
 
 
 def body(
@@ -316,7 +311,6 @@
         compiler_params=params(12 + routed_rows // 48),
         name="join_slots",
     )(*arrived, *drift_in)
-    relays = [swap(v, "island", 2 - n) for n, v in enumerate(relays)]
 
     joined_all = [joined] + [swap(joined, "tensor", t) for t in range(1, parts)]
 
@@ -340,46 +334,45 @@
 
     features_in = [send_features(d) for d in range(1, islands)]
 
-    hidden_piece = jax.ShapeDtypeStruct((routed_rows, columns), BF16)
-    *hidden_out, norms = pl.pallas_call(
+    hidden_out, norms = pl.pallas_call(
         lambda *refs: hidden_kernel(parts, across, *refs),
         in_specs=[SMEM] + [VMEM] * (2 + parts),
-        out_specs=[VMEM] * (across + 1),
-        out_shape=[hidden_piece] * across + [jax.ShapeDtypeStruct((devices, 8, 128), F32)],
+        out_specs=[VMEM] * 2,
+        out_shape=[
+            jax.ShapeDtypeStruct((across, routed_rows, columns), BF16),
+            jax.ShapeDtypeStruct((experts * parts, 8, 128), F32),
+        ],
         compiler_params=params(16 + routed_rows // 48),
         name="hidden_grads",
     )(spot, gate_weight, down_weight, *joined_all)
-
-    def hidden_for(d):
-        at = partner(island, d, islands) % across
-        if islands & (islands - 1) == 0:
-            return hidden_out[d % across]
-        return lax.select_n((at - island) % across, *hidden_out)
-
-    hidden_of = [hidden_out[0]] + [
-        swap(hidden_for(d), "island", d) for d in range(1, islands)
+    norms = lax.all_to_all(norms, AXES[1:], split_axis=0, concat_axis=0, tiled=True)
+
+    tails = [2, 1] if handed else []
+    message_rows = [
+        NOTE_ROWS + routed_rows + (half - handed if d in tails else 0) for d in range(islands)
     ]
-    norms = lax.all_to_all(norms, AXES, split_axis=0, concat_axis=0, tiled=True)
-    features_in = pl.pallas_call(
-        lambda *refs: hand_kernel(islands, *refs),
-        in_specs=[VMEM] * islands + [ANY] * (1 + len(relays)),
-        out_specs=VMEM,
-        out_shape=jax.ShapeDtypeStruct((islands, half, routed_rows), BF16),
-        compiler_params=params(4 + routed_rows // 48),
-        name="hand_features",
-    )(turned, *features_in, norms, *relays)
+    features_in, *messages = pl.pallas_call(
+        lambda *refs: hand_kernel(islands, tails, *refs),
+        in_specs=[SMEM] + [VMEM] * (2 + islands + len(relays)),
+        out_specs=[VMEM] * (1 + islands),
+        out_shape=[jax.ShapeDtypeStruct((islands, half, routed_rows), BF16)]
+        + [jax.ShapeDtypeStruct((rows, columns), BF16) for rows in message_rows],
+        compiler_params=params(6 + routed_rows // 48),
+        name="hand_on",
+    )(spot, norms, hidden_out, turned, *features_in, *relays)
     features_moved = spread(features_in)
+    messages_in = [messages[0]] + [swap(messages[d], "island", d) for d in range(1, islands)]
 
     *halves, notes = pl.pallas_call(
         lambda *refs: average_kernel(islands, entries, 4, *refs),
-        in_specs=[SMEM] + [VMEM] * (4 + islands + len(relays)),
+        in_specs=[SMEM] + [VMEM] * (3 + islands),
         out_specs=[VMEM] * 3,
         out_shape=[jax.ShapeDtypeStruct((half // 2, columns), F32)] * 2
         + [jax.ShapeDtypeStruct((devices, 8, 128), F32)],
         scratch_shapes=[pltpu.VMEM((half, columns), F32), pltpu.VMEM((1, columns), F32)],
         compiler_params=params(8 + routed_rows // 48),
         name="average_block",
-    )(spot, norms, drift_sum, features_in, features_moved, *hidden_of, *relays)
+    )(spot, drift_sum, features_in, features_moved, *messages_in)
     notes = lax.all_to_all(notes, AXES, split_axis=0, concat_axis=0, tiled=True)
 
     parted = half // 2
@@ -387,14 +380,8 @@
     values = {(0, 0): halves[0], (0, parted): halves[1]}
     last = {}
     if islands == 4:
-        nothing = jnp.minimum(notes[0, 1:2, :1], 0.0).astype(WIRE)
-
-        def after_notes(value):
-            return lax.dynamic_update_slice(value, value[:1, :128] + nothing, (0, 0))
-
         values[2, 0], values[1, parted] = swap(sent[0], "island", 2), swap(sent[1], "island", 1)
         beside, below = swap(sent[0], "island", 1), swap(sent[1], "island", 2)
-        beside, below = after_notes(beside), after_notes(below)
         values[1, 0], values[2, parted] = beside, below
         last[3, 0], last[3, parted] = swap(beside, "island", 2), swap(below, "island", 1)
     else:
@@ -407,9 +394,26 @@
         source = (at * experts + expert) * parts + part
         place += [(at // across) * half, (at % across) * columns, source]
     place = jnp.stack(place).astype(jnp.int32)
-    outs = update_pieces(entries, place, notes, momentum, values, [], 12 * momentum.size)
-    outs = update_pieces(entries, place, notes, momentum, last, outs, 3 * momentum.size)
-    return tuple(outs)
+    values |= last
+    return tuple(
+        pl.pallas_call(
+            lambda *refs: update_kernel(entries, list(values), *refs),
+            in_specs=[SMEM, VMEM, ANY] + [VMEM] * len(values),
+            out_specs=[ANY, ANY],
+            out_shape=[
+                jax.ShapeDtypeStruct(momentum.shape, F32),
+                jax.ShapeDtypeStruct(momentum.shape, BF16),
+            ],
+            scratch_shapes=[
+                pltpu.VMEM((len(values), parted, columns), F32),
+                pltpu.VMEM((len(values), parted, columns), BF16),
+                pltpu.SemaphoreType.DMA((len(values),)),
+                pltpu.SemaphoreType.DMA((len(values), 2)),
+            ],
+            compiler_params=params(50),
+            name="update_outputs",
+        )(place, notes, momentum, *[v.astype(F32) for v in values.values()])
+    )
 
 
 def solution(mesh):

time: 150 us -> 154 us (1.027)
  waiting for transfers between devices: 55.3 us -> 70.2 us
  starting transfers between devices: 47.8 us -> 37.5 us
  other arithmetic: 6.67 us -> 10.7 us
  Pallas kernels: 28.4 us -> 25.9 us
    ppermute x17 -> x15, waiting for transfers between devices: 50.9 us -> 64.3 us  [swap(): lax.ppermute(value, axis, [(at, partner(at, step, size)) for at in range(...]
    ppermute x17 -> x15, starting transfers between devices: 23.8 us -> 17.9 us  [swap(): lax.ppermute(value, axis, [(at, partner(at, step, size)) for at in range(...]
    all_to_all x1, starting transfers between devices: 8.37 us -> 2.6 us  [body(): notes = lax.all_to_all(notes, AXES, split_axis=0, concat_axis=0, tiled=True)]
    convert_element_type x6, other arithmetic: 5.2 us -> 9.83 us  [body(): v.astype(F32)]
    all_to_all x1, waiting for transfers between devices: 0.15 us -> 4.7 us  [body(): lax.all_to_all(norms, AXES[1:], split_axis=0, concat_axis=0, tiled=True)]
    all_to_all x1, waiting for transfers between devices: 4.26 us -> 0.01 us  [body(): notes = lax.all_to_all(notes, AXES, split_axis=0, concat_axis=0, tiled=True)]
    dynamic_update_slice x2 -> x0, local copies, waits for them, and re-layouts: 2.62 us -> none  [after_notes(): return lax.dynamic_update_slice(value, value[:1, :128] + nothing, (0, 0))]
    unnamed x22, local copies, waits for them, and re-layouts: 4.99 us -> 7.49 us
  transfers between devices with their start and end apart: 23 -> 21, of which waited for: 10 -> 10; matrix products, arithmetic and copies ran while one was open for 6% -> 7% of each run, Pallas kernels for 8% -> 4%
where the time goes in v7:
time: 154 us
  waiting for transfers between devices  70.2 us (46%)
  starting transfers between devices  37.5 us (24%)
  Pallas kernels  25.9 us (17%)
  other arithmetic  10.7 us (7%)
  local copies, waits for them, and re-layouts  8.19 us (5%)
    ppermute x15, waiting for transfers between devices, swap(): lax.ppermute(value, axis, [(at, partner(at, step, size)) for at in range(...  64.3 us
    ppermute x15, starting transfers between devices, swap(): lax.ppermute(value, axis, [(at, partner(at, step, size)) for at in range(...  17.9 us
    all_to_all x1, starting transfers between devices, body(): lax.all_to_all(norms, AXES[1:], split_axis=0, concat_axis=0, tiled=True)  10.2 us
    convert_element_type x6, other arithmetic, body(): v.astype(F32)  9.83 us
    unnamed x22, local copies, waits for them, and re-layouts  7.49 us
    pallas_call x1, Pallas kernels, body(): pl.pallas_call(lambda *refs: update_kernel(entries, list(values), *refs),...  7.23 us
    pallas_call x1, Pallas kernels, body(): pl.pallas_call(lambda *refs: pick_kernel(experts, islands, pieces, *refs)...  5.82 us
    pallas_call x1, Pallas kernels, body(): pl.pallas_call(lambda *refs: hidden_kernel(parts, across, *refs), in_spec...  5.43 us
  transfers between devices with their start and end apart: 21, of which 10 were waited for; matrix products, arithmetic and copies ran while one was open for 7% of the time, Pallas kernels for 4%

profile of v7, /device:TPU:0, one launch (start us, length us, event | category | flops | bytes accessed | tf_op | source)
XLA Modules:
  0.0 153.6 jit_solution(4437262352809227441)
XLA Ops:
  0.7 0.6 stack.79.refs_0_
  1.3 5.8 %pick_slots.1 = (bf16[192,1024]{1,0:T(8,128)(2,1)}, bf16[192,1024]{1,0:T(8,128)(2,1)}, bf16[192,1024]{1,0:T(8,128)(2,1)}, bf16[192,1024]{1,0:T(8,128)(2,1)}, bf1...) custom-call(s32[6]{0:T(128)} %stack.79.refs_0_, s32[1,1,4,96]{3,2,1,0:T(4,128)} %refs_1_.2, ...), custom_call_target="tpu_custom_call" | custom-call | tf_op jit(solution)/shard_map/pick_slots/pallas_call | solution.py:266
  7.1 0.0 copy-start.1
  7.1 3.0 %collective-permute-start.3 = (bf16[1536,384]{1,0:T(8,128)(2,1)}, bf16[1536,384]{1,0:T(8,128)(2,1)S(1)}, u32[]{:S(2)}, u32[]{:S(2)}) collective-permute-start(bf16[1536,384]{1,0:T(8,128)(2,1)} %get-tuple-element.33), channel_id=1, source_target_pairs={{0,8},{8,0},{16,24},{24,16},{1,9},{9,1},{17,25},{25,17},{2,10},{10... | collective-permute-start | bytes 3538952 | tf_op jit(solution)/shard_map/ppermute | solution.py:35
  10.1 1.5 collective-permute-start.4
  11.6 1.6 %collective-permute-start = (bf16[192,1024]{1,0:T(8,128)(2,1)}, bf16[192,1024]{1,0:T(8,128)(2,1)S(1)}, u32[]{:S(2)}, u32[]{:S(2)}) collective-permute-start(bf16[192,1024]{1,0:T(8,128)(2,1)} %get-tuple-element.29), channel_id=1, source_target_pairs={{0,2},{2,0},{4,6},{6,4},{1,3},{3,1},{5,7},{7,5},{8,10},{10,8},{12,... | collective-permute-start | bytes 1179656 | tf_op jit(solution)/shard_map/ppermute | solution.py:35
  13.2 2.6 %collective-permute-start.1 = (bf16[192,1024]{1,0:T(8,128)(2,1)}, bf16[192,1024]{1,0:T(8,128)(2,1)S(1)}, u32[]{:S(2)}, u32[]{:S(2)}) collective-permute-start(bf16[192,1024]{1,0:T(8,128)(2,1)} %get-tuple-element.30), channel_id=1, source_target_pairs={{0,4},{2,6},{4,0},{6,2},{1,5},{3,7},{5,1},{7,3},{8,12},{10,14},{12... | collective-permute-start | bytes 1179656 | tf_op jit(solution)/shard_map/ppermute | solution.py:35
  15.8 0.2 collective-permute-start.2
  16.0 1.1 copy-done.3
  17.2 1.0 copy-done.8
  18.2 0.1 own_parts.1
  18.2 11.3 %collective-permute-done.refs_1_ = bf16[192,1024]{1,0:T(8,128)(2,1)S(1)} collective-permute-done((bf16[192,1024]{1,0:T(8,128)(2,1)}, bf16[192,1024]{1,0:T(8,128)(2,1)S(1)}, u32[]{:S(2)}, u32[]{:S(2)}) %collective-permute-start) | collective-permute-done | bytes 393248 | tf_op jit(solution)/shard_map/ppermute | solution.py:35
  29.5 13.7 %collective-permute-done.1.refs_2_ = bf16[192,1024]{1,0:T(8,128)(2,1)S(1)} collective-permute-done((bf16[192,1024]{1,0:T(8,128)(2,1)}, bf16[192,1024]{1,0:T(8,128)(2,1)S(1)}, u32[]{:S(2)}, u32[]{:S(2)}) %collective-permute-start.1) | collective-permute-done | bytes 393248 | tf_op jit(solution)/shard_map/ppermute | solution.py:35
  43.2 0.7 join_slots.1
  44.0 0.0 copy-start.6
  44.0 0.7 copy-done.6
  44.7 1.3 collective-permute-start.8
  46.0 1.3 collective-permute-start.7
  47.3 2.4 %collective-permute-start.6 = (bf16[1024,384]{1,0:T(8,128)(2,1)S(1)}, bf16[1024,384]{1,0:T(8,128)(2,1)}, u32[]{:S(2)}, u32[]{:S(2)}) collective-permute-start(bf16[1024,384]{1,0:T(8,128)(2,1)S(1)} %get-tuple-element.39.refs_3_), channel_id=1, source_target_pairs={{0,8},{8,0},{17,25},{25,17},{2,10},{10,2},{19,27},{27,19},{4,12},{... | collective-permute-start | bytes 2359304 | tf_op jit(solution)/shard_map/ppermute | solution.py:322
  49.8 0.0 collective-permute-done.5.refs_4_
  49.8 5.4 %hidden_grads.1 = (bf16[2,384,384]{2,1,0:T(8,128)(2,1)S(1)}, f32[8,8,128]{2,1,0:T(8,128)S(1)}) custom-call(s32[6]{0:T(128)S(1)} %copy-done.10, bf16[1,1,2048,768]{3,2,1,0:T(8,128)(2,1)S(1)} %copy-done.1, bf16[1,1,768,2048]{3,2,1,0:T(8,128)(2,1)S(1)} %copy-done.2, bf16[768,1024]{1,0:T(8,128)(2,1)S(1)} %get-tuple-element.36.refs_3_, ...), custom_call_target="tpu_custom_call" | custom-call | tf_op jit(solution)/shard_map/hidden_grads/pallas_call | solution.py:337
  55.3 0.0 copy-start.4
  55.3 0.8 copy-done.4
  56.1 0.6 copy-done.9
  56.7 10.2 %all-to-all-start = ((f32[8,8,128]{2,1,0:T(8,128)}), f32[8,8,128]{2,1,0:T(8,128)}, u32[]{:S(2)}, u32[]{:S(2)}) async-start(f32[8,8,128]{2,1,0:T(8,128)} %copy-done.9), calls=%async_computation | async-start | bytes 65536 | tf_op jit(solution)/shard_map/all_to_all | solution.py:348
  66.9 0.0 collective-permute-done.8.refs_6_
  66.9 1.1 collective-permute-done.7.refs_5_
  68.0 0.0 collective-permute-done.6.refs_4_
  68.0 4.7 %all-to-all-done.refs_1_ = f32[8,8,128]{2,1,0:T(8,128)} async-done(((f32[8,8,128]{2,1,0:T(8,128)}), f32[8,8,128]{2,1,0:T(8,128)}, u32[]{:S(2)}, u32[]{:S(2)}) %all-to-all-start) | async-done | bytes 32800 | tf_op jit(solution)/shard_map/all_to_all | solution.py:348
  72.7 1.1 copy-done.5
  73.8 1.0 copy-done.7
  74.8 1.8 %hand_on.1 = (bf16[4,1024,384]{2,1,0:T(8,128)(2,1)S(1)}, bf16[400,384]{1,0:T(8,128)(2,1)S(1)}, bf16[912,384]{1,0:T(8,128)(2,1)S(1)}, bf16[912,384]{1,0:T(8,128)(2,1)S(1)}, bf16[400,384]{1,0:T(8,128)(2,1)S(1)}) custom-call(s32[6]{0:T(128)S(1)} %copy-done.10, f32[8,8,128]{2,1,0:T(8,128)} %all-to-all-done.refs_1_, bf16[2,384,384]{2,1,0:T(8,128)(2,1)S(1)} %copy-done.5, ...), custom_call_target="tpu_custom_call" | custom-call | tf_op jit(solution)/shard_map/hand_on/pallas_call | solution.py:354
  76.7 1.8 %collective-permute-start.9 = (bf16[4,1024,384]{2,1,0:T(8,128)(2,1)S(1)}, bf16[4,1024,384]{2,1,0:T(8,128)(2,1)S(1)}, u32[]{:S(2)}, u32[]{:S(2)}) collective-permute-start(bf16[4,1024,384]{2,1,0:T(8,128)(2,1)S(1)} %get-tuple-element.42.refs_2_), channel_id=1, source_target_pairs={{0,1},{8,9},{17,16},{25,24},{2,3},{10,11},{19,18},{27,26},{4,5},{1... | collective-permute-start | bytes 9437192 | tf_op jit(solution)/shard_map/ppermute | solution.py:331
  78.5 1.6 %collective-permute-start.10 = (bf16[912,384]{1,0:T(8,128)(2,1)S(1)}, bf16[912,384]{1,0:T(8,128)(2,1)S(1)}, u32[]{:S(2)}, u32[]{:S(2)}) collective-permute-start(bf16[912,384]{1,0:T(8,128)(2,1)S(1)} %get-tuple-element.44), channel_id=1, source_target_pairs={{0,8},{8,0},{16,24},{24,16},{1,9},{9,1},{17,25},{25,17},{2,10},{10... | collective-permute-start | bytes 2101256 | tf_op jit(solution)/shard_map/ppermute | solution.py:35
  80.1 1.1 collective-permute-start.11
  81.2 0.9 collective-permute-start.12
  82.1 22.1 %collective-permute-done.12.refs_7_ = bf16[400,384]{1,0:T(8,128)(2,1)S(1)} collective-permute-done((bf16[400,384]{1,0:T(8,128)(2,1)S(1)}, bf16[400,384]{1,0:T(8,128)(2,1)S(1)}, u32[]{:S(2)}, u32[]{:S(2)}) %collective-permute-start.12) | collective-permute-done | bytes 307232 | tf_op jit(solution)/shard_map/ppermute | solution.py:35
  104.1 0.0 collective-permute-done.10.refs_5_
  104.1 0.5 collective-permute-done.11.refs_6_
  104.7 0.0 collective-permute-done.9.refs_3_
  104.7 4.7 %average_block.1 = (f32[512,384]{1,0:T(8,128)S(1)}, f32[512,384]{1,0:T(8,128)S(1)}, f32[32,8,128]{2,1,0:T(8,128)}) custom-call(s32[6]{0:T(128)S(1)} %copy-done.10, f32[1024,384]{1,0:T(8,128)S(1)} %get-tuple-element.35.refs_1_, bf16[4,1024,384]{2,1,0:T(8,128)(2,1)S(1)} %get-tuple-element.42.refs_2_, bf16[4,1024,384]{2,1,0:T(8,128)(2,1)S(1)} %collective-permute-done.9.refs_3_, ...), custom_call_target="tpu_custom_call" | custom-call | tf_op jit(solution)/shard_map/average_block/pallas_call | solution.py:366
  109.4 0.1 convert_element_type.27
  109.5 1.7 %collective-permute-start.16 = (f16[512,384]{1,0:T(8,128)(2,1)S(1)}, f16[512,384]{1,0:T(8,128)(2,1)}, u32[]{:S(2)}, u32[]{:S(2)}) collective-permute-start(f16[512,384]{1,0:T(8,128)(2,1)S(1)} %convert_element_type.27), channel_id=1, source_target_pairs={{0,16},{8,24},{16,0},{24,8},{1,17},{9,25},{17,1},{25,9},{2,18},{10... | collective-permute-start | bytes 1179656 | tf_op jit(solution)/shard_map/ppermute | solution.py:35
  111.1 0.8 convert_element_type.25
  111.9 0.5 collective-permute-start.15
  112.4 1.5 collective-permute-start.14
  113.9 0.4 collective-permute-start.13
  114.4 7.2 %collective-permute-done.16 = f16[512,384]{1,0:T(8,128)(2,1)} collective-permute-done((f16[512,384]{1,0:T(8,128)(2,1)S(1)}, f16[512,384]{1,0:T(8,128)(2,1)}, u32[]{:S(2)}, u32[]{:S(2)}) %collective-permute-start.16) | collective-permute-done | bytes 393248 | tf_op jit(solution)/shard_map/ppermute | solution.py:35
  121.6 0.8 collective-permute-start.18
  122.5 1.8 %collective-permute-done.15 = f16[512,384]{1,0:T(8,128)(2,1)} collective-permute-done((f16[512,384]{1,0:T(8,128)(2,1)}, f16[512,384]{1,0:T(8,128)(2,1)}, u32[]{:S(2)}, u32[]{:S(2)}) %collective-permute-start.15) | collective-permute-done | bytes 393248 | tf_op jit(solution)/shard_map/ppermute | solution.py:35
  124.2 0.5 collective-permute-start.17
  124.7 2.6 %all-to-all-start.1 = ((f32[32,8,128]{2,1,0:T(8,128)}), f32[32,8,128]{2,1,0:T(8,128)S(1)}, u32[]{:S(2)}, u32[]{:S(2)}) async-start(f32[32,8,128]{2,1,0:T(8,128)} %get-tuple-element.47), calls=%async_computation.1 | async-start | bytes 262144 | tf_op jit(solution)/shard_map/all_to_all | solution.py:376
  127.4 0.1 stack.72.refs_0_
  127.5 1.1 convert_element_type.29.refs_7_
  128.6 1.9 %convert_element_type.30.refs_8_ = f32[512,384]{1,0:T(8,128)} convert(f16[512,384]{1,0:T(8,128)(2,1)} %collective-permute-done.16) | non-fusion elementwise | flops 196608 | bytes 1179648 | tf_op jit(solution)/shard_map/convert_element_type | solution.py:415
  130.5 2.8 %collective-permute-done.14 = f16[512,384]{1,0:T(8,128)(2,1)} collective-permute-done((f16[512,384]{1,0:T(8,128)(2,1)S(1)}, f16[512,384]{1,0:T(8,128)(2,1)}, u32[]{:S(2)}, u32[]{:S(2)}) %collective-permute-start.14) | collective-permute-done | bytes 393248 | tf_op jit(solution)/shard_map/ppermute | solution.py:35
  133.3 1.0 convert_element_type.28.refs_6_
  134.4 0.0 collective-permute-done.13
  134.4 1.9 %convert_element_type.26.refs_5_ = f32[512,384]{1,0:T(8,128)} convert(f16[512,384]{1,0:T(8,128)(2,1)} %collective-permute-done.13) | non-fusion elementwise | flops 196608 | bytes 1179648 | tf_op jit(solution)/shard_map/convert_element_type | solution.py:415
  136.3 4.9 %collective-permute-done.18 = f16[512,384]{1,0:T(8,128)(2,1)} collective-permute-done((f16[512,384]{1,0:T(8,128)(2,1)}, f16[512,384]{1,0:T(8,128)(2,1)}, u32[]{:S(2)}, u32[]{:S(2)}) %collective-permute-start.18) | collective-permute-done | bytes 393248 | tf_op jit(solution)/shard_map/ppermute | solution.py:35
  141.2 1.9 %convert_element_type.32.refs_10_ = f32[512,384]{1,0:T(8,128)} convert(f16[512,384]{1,0:T(8,128)(2,1)} %collective-permute-done.18) | non-fusion elementwise | flops 196608 | bytes 1179648 | tf_op jit(solution)/shard_map/convert_element_type | solution.py:415
  143.1 1.9 %convert_element_type.31.refs_9_ = f32[512,384]{1,0:T(8,128)} convert(f16[512,384]{1,0:T(8,128)(2,1)} %collective-permute-done.17) | non-fusion elementwise | flops 196608 | bytes 1179648 | tf_op jit(solution)/shard_map/convert_element_type | solution.py:415
  145.0 1.1 copy-done
  146.2 7.2 %update_outputs.1 = (f32[1,2048,768]{2,1,0:T(8,128)}, bf16[1,2048,768]{2,1,0:T(8,128)(2,1)}) custom-call(s32[12]{0:T(128)S(1)} %stack.72.refs_0_, f32[32,8,128]{2,1,0:T(8,128)S(1)} %all-to-all-done.1.refs_1_, f32[1,2048,768]{2,1,0:T(8,128)} %refs_2_.5, f32[512,384]{1,0:T(8,128)S(1)} %get-tuple-element.48.refs_3_, f32[512,384]{1,0:T(8,128)S(1)} %get-tuple-element.49.refs_4_, ...), custom_call_target="tpu_custom_call" | custom-call | tf_op jit(solution)/shard_map/update_outputs/pallas_call | solution.py:399
  (17 shorter events, 0.0 us)
Async XLA Ops:
  1.3 48.5 %copy-start.2 = (bf16[1,1,768,2048]{3,2,1,0:T(8,128)(2,1)S(1)}, bf16[1,1,768,2048]{3,2,1,0:T(8,128)(2,1)}, u32[]{:S(2)}) copy-start(bf16[1,1,768,2048]{3,2,1,0:T(8,128)(2,1)} %refs_2_.4) | copy-start | bytes 9437188
  1.3 48.5 %copy-start.10 = (s32[6]{0:T(128)S(1)}, s32[6]{0:T(128)}, u32[]{:S(2)}) copy-start(s32[6]{0:T(128)} %stack.79.refs_0_) | copy-start | bytes 76
  7.1 42.7 %copy-start.1 = (bf16[1,1,2048,768]{3,2,1,0:T(8,128)(2,1)S(1)}, bf16[1,1,2048,768]{3,2,1,0:T(8,128)(2,1)}, u32[]{:S(2)}) copy-start(bf16[1,1,2048,768]{3,2,1,0:T(8,128)(2,1)} %refs_1_.3) | copy-start | bytes 9437188
  7.1 36.1 %collective-permute-start.3 = (bf16[1536,384]{1,0:T(8,128)(2,1)}, bf16[1536,384]{1,0:T(8,128)(2,1)S(1)}, u32[]{:S(2)}, u32[]{:S(2)}) collective-permute-start(bf16[1536,384]{1,0:T(8,128)(2,1)} %get-tuple-element.33), channel_id=1, source_target_pairs={{0,8},{8,0},{16,24},{24,16},{1,9},{9,1},{17,25},{25,17},{2,10},{10... | collective-permute-start | bytes 3538952 | tf_op jit(solution)/shard_map/ppermute | solution.py:35
  10.1 33.1 %collective-permute-start.4 = (bf16[1536,384]{1,0:T(8,128)(2,1)}, bf16[1536,384]{1,0:T(8,128)(2,1)S(1)}, u32[]{:S(2)}, u32[]{:S(2)}) collective-permute-start(bf16[1536,384]{1,0:T(8,128)(2,1)} %get-tuple-element.34), channel_id=1, source_target_pairs={{0,16},{8,24},{16,0},{24,8},{1,17},{9,25},{17,1},{25,9},{2,18},{10... | collective-permute-start | bytes 3538952 | tf_op jit(solution)/shard_map/ppermute | solution.py:35
  11.6 17.9 %collective-permute-start = (bf16[192,1024]{1,0:T(8,128)(2,1)}, bf16[192,1024]{1,0:T(8,128)(2,1)S(1)}, u32[]{:S(2)}, u32[]{:S(2)}) collective-permute-start(bf16[192,1024]{1,0:T(8,128)(2,1)} %get-tuple-element.29), channel_id=1, source_target_pairs={{0,2},{2,0},{4,6},{6,4},{1,3},{3,1},{5,7},{7,5},{8,10},{10,8},{12,... | collective-permute-start | bytes 1179656 | tf_op jit(solution)/shard_map/ppermute | solution.py:35
  13.2 30.0 %collective-permute-start.1 = (bf16[192,1024]{1,0:T(8,128)(2,1)}, bf16[192,1024]{1,0:T(8,128)(2,1)S(1)}, u32[]{:S(2)}, u32[]{:S(2)}) collective-permute-start(bf16[192,1024]{1,0:T(8,128)(2,1)} %get-tuple-element.30), channel_id=1, source_target_pairs={{0,4},{2,6},{4,0},{6,2},{1,5},{3,7},{5,1},{7,3},{8,12},{10,14},{12... | collective-permute-start | bytes 1179656 | tf_op jit(solution)/shard_map/ppermute | solution.py:35
  15.8 27.4 %collective-permute-start.2 = (bf16[192,1024]{1,0:T(8,128)(2,1)}, bf16[192,1024]{1,0:T(8,128)(2,1)S(1)}, u32[]{:S(2)}, u32[]{:S(2)}) collective-permute-start(bf16[192,1024]{1,0:T(8,128)(2,1)} %get-tuple-element.31), channel_id=1, source_target_pairs={{0,6},{2,4},{4,2},{6,0},{1,7},{3,5},{5,3},{7,1},{8,14},{10,12},{12... | collective-permute-start | bytes 1179656 | tf_op jit(solution)/shard_map/ppermute | solution.py:35
  16.0 1.1 copy-start.3
  17.2 1.0 copy-start.8
  44.0 0.7 copy-start.6
  44.7 5.0 %collective-permute-start.5 = (bf16[768,1024]{1,0:T(8,128)(2,1)S(1)}, bf16[768,1024]{1,0:T(8,128)(2,1)S(1)}, u32[]{:S(2)}, u32[]{:S(2)}) collective-permute-start(bf16[768,1024]{1,0:T(8,128)(2,1)S(1)} %get-tuple-element.36.refs_3_), channel_id=1, source_target_pairs={{0,1},{1,0},{2,3},{3,2},{4,5},{5,4},{6,7},{7,6},{8,9},{9,8},{10,11... | collective-permute-start | bytes 4718600 | tf_op jit(solution)/shard_map/ppermute | solution.py:35
  44.7 22.2 %collective-permute-start.8 = (bf16[1024,384]{1,0:T(8,128)(2,1)S(1)}, bf16[1024,384]{1,0:T(8,128)(2,1)S(1)}, u32[]{:S(2)}, u32[]{:S(2)}) collective-permute-start(bf16[1024,384]{1,0:T(8,128)(2,1)S(1)} %get-tuple-element.39.refs_3_), channel_id=1, source_target_pairs={{1,25},{9,17},{16,8},{24,0},{3,27},{11,19},{18,10},{26,2},{5,29},{... | collective-permute-start | bytes 2359304 | tf_op jit(solution)/shard_map/ppermute | solution.py:322
  46.0 22.0 %collective-permute-start.7 = (bf16[1024,384]{1,0:T(8,128)(2,1)S(1)}, bf16[1024,384]{1,0:T(8,128)(2,1)}, u32[]{:S(2)}, u32[]{:S(2)}) collective-permute-start(bf16[1024,384]{1,0:T(8,128)(2,1)S(1)} %get-tuple-element.39.refs_3_), channel_id=1, source_target_pairs={{1,17},{9,25},{16,0},{24,8},{3,19},{11,27},{18,2},{26,10},{5,21},{... | collective-permute-start | bytes 2359304 | tf_op jit(solution)/shard_map/ppermute | solution.py:322
  47.3 20.7 %collective-permute-start.6 = (bf16[1024,384]{1,0:T(8,128)(2,1)S(1)}, bf16[1024,384]{1,0:T(8,128)(2,1)}, u32[]{:S(2)}, u32[]{:S(2)}) collective-permute-start(bf16[1024,384]{1,0:T(8,128)(2,1)S(1)} %get-tuple-element.39.refs_3_), channel_id=1, source_target_pairs={{0,8},{8,0},{17,25},{25,17},{2,10},{10,2},{19,27},{27,19},{4,12},{... | collective-permute-start | bytes 2359304 | tf_op jit(solution)/shard_map/ppermute | solution.py:322
  55.3 0.8 copy-start.4
  56.1 0.6 copy-start.9
  56.7 16.1 %all-to-all-start = ((f32[8,8,128]{2,1,0:T(8,128)}), f32[8,8,128]{2,1,0:T(8,128)}, u32[]{:S(2)}, u32[]{:S(2)}) async-start(f32[8,8,128]{2,1,0:T(8,128)} %copy-done.9), calls=%async_computation | async-start | bytes 65536 | tf_op jit(solution)/shard_map/all_to_all | solution.py:348
  72.7 1.1 copy-start.5
  73.8 1.0 copy-start.7
  76.7 28.0 %collective-permute-start.9 = (bf16[4,1024,384]{2,1,0:T(8,128)(2,1)S(1)}, bf16[4,1024,384]{2,1,0:T(8,128)(2,1)S(1)}, u32[]{:S(2)}, u32[]{:S(2)}) collective-permute-start(bf16[4,1024,384]{2,1,0:T(8,128)(2,1)S(1)} %get-tuple-element.42.refs_2_), channel_id=1, source_target_pairs={{0,1},{8,9},{17,16},{25,24},{2,3},{10,11},{19,18},{27,26},{4,5},{1... | collective-permute-start | bytes 9437192 | tf_op jit(solution)/shard_map/ppermute | solution.py:331
  78.5 25.6 %collective-permute-start.10 = (bf16[912,384]{1,0:T(8,128)(2,1)S(1)}, bf16[912,384]{1,0:T(8,128)(2,1)S(1)}, u32[]{:S(2)}, u32[]{:S(2)}) collective-permute-start(bf16[912,384]{1,0:T(8,128)(2,1)S(1)} %get-tuple-element.44), channel_id=1, source_target_pairs={{0,8},{8,0},{16,24},{24,16},{1,9},{9,1},{17,25},{25,17},{2,10},{10... | collective-permute-start | bytes 2101256 | tf_op jit(solution)/shard_map/ppermute | solution.py:35
  80.1 24.6 %collective-permute-start.11 = (bf16[912,384]{1,0:T(8,128)(2,1)S(1)}, bf16[912,384]{1,0:T(8,128)(2,1)S(1)}, u32[]{:S(2)}, u32[]{:S(2)}) collective-permute-start(bf16[912,384]{1,0:T(8,128)(2,1)S(1)} %get-tuple-element.45), channel_id=1, source_target_pairs={{0,16},{8,24},{16,0},{24,8},{1,17},{9,25},{17,1},{25,9},{2,18},{10... | collective-permute-start | bytes 2101256 | tf_op jit(solution)/shard_map/ppermute | solution.py:35
  81.2 22.9 %collective-permute-start.12 = (bf16[400,384]{1,0:T(8,128)(2,1)S(1)}, bf16[400,384]{1,0:T(8,128)(2,1)S(1)}, u32[]{:S(2)}, u32[]{:S(2)}) collective-permute-start(bf16[400,384]{1,0:T(8,128)(2,1)S(1)} %get-tuple-element.46), channel_id=1, source_target_pairs={{0,24},{8,16},{16,8},{24,0},{1,25},{9,17},{17,9},{25,1},{2,26},{10... | collective-permute-start | bytes 921608 | tf_op jit(solution)/shard_map/ppermute | solution.py:35
  109.5 12.2 %collective-permute-start.16 = (f16[512,384]{1,0:T(8,128)(2,1)S(1)}, f16[512,384]{1,0:T(8,128)(2,1)}, u32[]{:S(2)}, u32[]{:S(2)}) collective-permute-start(f16[512,384]{1,0:T(8,128)(2,1)S(1)} %convert_element_type.27), channel_id=1, source_target_pairs={{0,16},{8,24},{16,0},{24,8},{1,17},{9,25},{17,1},{25,9},{2,18},{10... | collective-permute-start | bytes 1179656 | tf_op jit(solution)/shard_map/ppermute | solution.py:35
  111.9 12.3 %collective-permute-start.15 = (f16[512,384]{1,0:T(8,128)(2,1)}, f16[512,384]{1,0:T(8,128)(2,1)}, u32[]{:S(2)}, u32[]{:S(2)}) collective-permute-start(f16[512,384]{1,0:T(8,128)(2,1)} %convert_element_type.25), channel_id=1, source_target_pairs={{0,8},{8,0},{16,24},{24,16},{1,9},{9,1},{17,25},{25,17},{2,10},{10... | collective-permute-start | bytes 1179656 | tf_op jit(solution)/shard_map/ppermute | solution.py:35
  112.4 20.9 %collective-permute-start.14 = (f16[512,384]{1,0:T(8,128)(2,1)S(1)}, f16[512,384]{1,0:T(8,128)(2,1)}, u32[]{:S(2)}, u32[]{:S(2)}) collective-permute-start(f16[512,384]{1,0:T(8,128)(2,1)S(1)} %convert_element_type.27), channel_id=1, source_target_pairs={{0,8},{8,0},{16,24},{24,16},{1,9},{9,1},{17,25},{25,17},{2,10},{10... | collective-permute-start | bytes 1179656 | tf_op jit(solution)/shard_map/ppermute | solution.py:35
  113.9 20.4 %collective-permute-start.13 = (f16[512,384]{1,0:T(8,128)(2,1)}, f16[512,384]{1,0:T(8,128)(2,1)}, u32[]{:S(2)}, u32[]{:S(2)}) collective-permute-start(f16[512,384]{1,0:T(8,128)(2,1)} %convert_element_type.25), channel_id=1, source_target_pairs={{0,16},{8,24},{16,0},{24,8},{1,17},{9,25},{17,1},{25,9},{2,18},{10... | collective-permute-start | bytes 1179656 | tf_op jit(solution)/shard_map/ppermute | solution.py:35
  121.6 19.5 %collective-permute-start.18 = (f16[512,384]{1,0:T(8,128)(2,1)}, f16[512,384]{1,0:T(8,128)(2,1)}, u32[]{:S(2)}, u32[]{:S(2)}) collective-permute-start(f16[512,384]{1,0:T(8,128)(2,1)} %collective-permute-done.16), channel_id=1, source_target_pairs={{0,8},{8,0},{16,24},{24,16},{1,9},{9,1},{17,25},{25,17},{2,10},{10... | collective-permute-start | bytes 1179656 | tf_op jit(solution)/shard_map/ppermute | solution.py:35
  124.2 18.9 %collective-permute-start.17 = (f16[512,384]{1,0:T(8,128)(2,1)}, f16[512,384]{1,0:T(8,128)(2,1)}, u32[]{:S(2)}, u32[]{:S(2)}) collective-permute-start(f16[512,384]{1,0:T(8,128)(2,1)} %collective-permute-done.15), channel_id=1, source_target_pairs={{0,16},{8,24},{16,0},{24,8},{1,17},{9,25},{17,1},{25,9},{2,18},{10... | collective-permute-start | bytes 1179656 | tf_op jit(solution)/shard_map/ppermute | solution.py:35
  124.7 20.4 %all-to-all-start.1 = ((f32[32,8,128]{2,1,0:T(8,128)}), f32[32,8,128]{2,1,0:T(8,128)S(1)}, u32[]{:S(2)}, u32[]{:S(2)}) async-start(f32[32,8,128]{2,1,0:T(8,128)} %get-tuple-element.47), calls=%async_computation.1 | async-start | bytes 262144 | tf_op jit(solution)/shard_map/all_to_all | solution.py:376
  145.0 1.1 copy-start

commit v8 on v7

--- a/solution.py
+++ b/solution.py
@@ -1,3 +1,4 @@
+import functools
 import math
 
 import jax
@@ -11,7 +12,6 @@
 BF16 = jnp.bfloat16
 WIRE = jnp.float16
 AXES = ("island", "expert", "tensor")
-NOTE_ROWS = 16
 
 VMEM = pl.BlockSpec(memory_space=pltpu.VMEM)
 SMEM = pl.BlockSpec(memory_space=pltpu.SMEM)
@@ -46,24 +46,12 @@
     return copies
 
 
-def pick_kernel(experts, islands, pieces, spot, *refs):
-    sources, drift = refs[:5], refs[5]
-    outs, blocks = refs[6 : 6 + experts], refs[6 + experts : -10]
-    table, count, weight, tokens, grads, picked, cut, sems, in_sems, out_sems = refs[-10:]
-    loads = copy_all(sems, list(zip(sources, refs[-10:-5])))
-    rows, columns = blocks[0].shape
-    pairs, stores = [], []
-    for d, first, count_rows, target, at_row in pieces:
-        at = partner(spot[3], d, islands)
-        top = pl.multiple_of(lax.div(at, spot[4]) * rows, rows) + first
-        left = pl.multiple_of(lax.rem(at, spot[4]) * columns, columns)
-        place = pl.ds(sum(p[2] for p in pieces[: len(pairs)]), count_rows)
-        pairs.append((drift.at[0, 0, pl.ds(top, count_rows), pl.ds(left, columns)], cut.at[place]))
-        stores.append((cut.at[place], blocks[target].at[pl.ds(at_row, count_rows)]))
-    copies = copy_all(in_sems, pairs)
+def pick_kernel(experts, spot, *refs):
+    sources, outs = refs[:5], refs[5 : 5 + experts]
+    table, count, weight, tokens, grads, sems = refs[5 + experts :]
+    loads = copy_all(sems, list(zip(sources, refs[5 + experts : -1])))
     for copy in loads:
         copy.wait()
-
     slots = table.shape[-1]
     rows = lax.broadcasted_iota(jnp.int32, (slots, slots), 0)
     lanes = lax.broadcasted_iota(jnp.int32, (slots, slots), 1)
@@ -71,38 +59,46 @@
     def column(row):
         return jnp.sum(jnp.where(rows == lanes, row, 0), axis=1, keepdims=True)
 
-    done = []
-    for d in [*range(1, experts), 0]:
+    for d in range(experts):
         to = partner(spot[0], d, experts)
         live = lax.broadcasted_iota(jnp.int32, (slots, 1), 0) < count[0, 0, to]
         token = column(table[0, 0, pl.ds(to, 1), :].astype(F32)).astype(jnp.int32)
         chance = column(weight[0, 0, pl.ds(to, 1), :])
         ids = lax.broadcasted_iota(jnp.int32, (slots, tokens.shape[1]), 1)
         picks = jnp.where((ids == token) & live, 1.0, 0.0).astype(BF16)
-        picked[d, :slots, :] = dot(picks, tokens[0], ((1,), (0,))).astype(BF16)
+        outs[d][:slots, :] = dot(picks, tokens[0], ((1,), (0,))).astype(BF16)
         chosen = dot(picks, grads[0], ((1,), (0,)))
-        picked[d, slots:, :] = (chance * chosen).astype(BF16)
-        done.append(pltpu.make_async_copy(picked.at[d], outs[d], out_sems.at[len(pairs) + d]))
-        done[-1].start()
-    for n, copy in enumerate(copies):
+        outs[d][slots:, :] = (chance * chosen).astype(BF16)
+
+
+def cut_kernel(islands, pieces, spot, drift, *refs):
+    *blocks, sems = refs
+    rows, columns = blocks[0].shape
+    pairs = []
+    for d, first, count_rows, target, at_row in pieces:
+        at = partner(spot[3], d, islands)
+        top = pl.multiple_of(lax.div(at, spot[4]) * rows, rows) + first
+        left = pl.multiple_of(lax.rem(at, spot[4]) * columns, columns)
+        source = drift.at[0, 0, pl.ds(top, count_rows), pl.ds(left, columns)]
+        pairs.append((source, blocks[target].at[pl.ds(at_row, count_rows)]))
+    for copy in copy_all(sems, pairs):
         copy.wait()
-        done.append(pltpu.make_async_copy(*stores[n], out_sems.at[n]))
-        done[-1].start()
-    for copy in done:
-        copy.wait()
-
-
-def join_kernel(count, blocks, *refs):
-    arrived, drifts = refs[:count], refs[count : count + blocks]
-    joined, turned, drift_sum = refs[count + blocks : count + blocks + 3]
+
+
+def gather_kernel(count, *refs):
+    arrived, joined = refs[:count], refs[count]
     slots = arrived[0].shape[0] // 2
-    rows = drift_sum.shape[0]
-    for n, ref in enumerate(refs[count + blocks + 3 :]):
-        ref[...] = drifts[1 + n][rows:, :]
     for n, piece in enumerate(arrived):
         joined[n * slots : (n + 1) * slots, :] = piece[:slots, :]
         joined[(count + n) * slots : (count + n + 1) * slots, :] = piece[slots:, :]
-    turned[...] = joined[: count * slots, :].T
+
+
+def join_kernel(blocks, joined, *refs):
+    drifts, (turned, drift_sum) = refs[:blocks], refs[blocks : blocks + 2]
+    rows = drift_sum.shape[0]
+    for n, ref in enumerate(refs[blocks + 2 :]):
+        ref[...] = drifts[1 + n][rows:, :]
+    turned[...] = joined[: joined.shape[0] // 2, :].T
     added = drifts[0][...].astype(F32)
     for other in drifts[1:]:
         added = added + other[:rows, :].astype(F32)
@@ -134,16 +130,18 @@
     norms[...] = jnp.full(norms.shape, jnp.sum(hidden_gram * input_gram), F32)
 
 
-def average_kernel(islands, entries, tiles, spot, drift_sum, own, moved, *refs):
+def average_kernel(islands, entries, tiles, spot, norms, drift_sum, own, moved, *refs):
     messages = refs[:islands]
     *halves, notes, total, square = refs[islands:]
     rows = total.shape[0] // tiles
     slots = own.shape[2]
+    group = norms.shape[0] // islands
     scales = []
-    for message in messages:
-        norm = sum(message[n : n + 1, :1].astype(F32) for n in range(3))
+    for d in range(islands):
+        at = origin(spot[3], d, islands)
+        norm = jnp.sum(norms[pl.ds(at * group, group)], axis=0)[:1, :1]
         scales.append(jnp.minimum(1.0, math.sqrt(entries) / jnp.sqrt(norm + 1e-06)) / islands)
-    handed = [m for m in messages[:0:-1] if m.shape[0] > NOTE_ROWS + slots]
+    handed = [m for m in messages[:0:-1] if m.shape[0] > slots]
 
     def compute(features):
         squares = 0.0
@@ -151,13 +149,13 @@
             part = slice(m * rows, (m + 1) * rows)
             average = drift_sum[part, :]
             if handed:
-                size = handed[0].shape[0] - NOTE_ROWS - slots
+                size = handed[0].shape[0] - slots
                 n, first = divmod(m * rows, size)
-                first += NOTE_ROWS + slots
+                first += slots
                 average = average + handed[n][first : first + rows, :].astype(F32)
             average = average * (1.0 / islands)
             for d in range(islands):
-                factor = messages[d][NOTE_ROWS : NOTE_ROWS + slots, :]
+                factor = messages[d][:slots, :]
                 average = average + scales[d] * dot(features[d, part, :], factor, ((1,), (0,)))
             total[part, :] = average
             squares = squares + jnp.sum(average * average, axis=0, keepdims=True)
@@ -179,23 +177,16 @@
 
 def hand_kernel(islands, tails, spot, norms, hidden, *refs):
     features, relays = refs[:islands], refs[islands : islands + len(tails)]
-    joined, *messages = refs[islands + len(tails) :]
-    across, slots, columns = hidden.shape
+    joined, passed, *messages = refs[islands + len(tails) :]
+    across, slots, _ = hidden.shape
     for n in range(islands):
         joined[n] = features[n][...]
-    left = jnp.sum(norms[...], axis=0)[:1, :1]
-    rows = lax.broadcasted_iota(jnp.int32, (NOTE_ROWS, columns), 0)
-    note = jnp.zeros((NOTE_ROWS, columns), F32)
-    for n in range(3):
-        summand = left.astype(BF16).astype(F32)
-        note = jnp.where(rows == n, summand, note)
-        left = left - summand
+    passed[...] = norms[...]
     for d, message in enumerate(messages):
-        message[:NOTE_ROWS, :] = note.astype(BF16)
         block = lax.rem(partner(spot[3], d, islands), across)
-        message[NOTE_ROWS : NOTE_ROWS + slots, :] = hidden[pl.ds(block, 1)][0]
+        message[:slots, :] = hidden[pl.ds(block, 1)][0]
         if d in tails:
-            message[NOTE_ROWS + slots :, :] = relays[tails.index(d)][...]
+            message[slots:, :] = relays[tails.index(d)][...]
 
 
 def own_kernel(slots, block, slots_out, block_out):
@@ -264,29 +255,33 @@
         pieces += [(3, 0, handed, 1, half), (3, handed, handed, 2, half)]
     block_rows = [half + (handed if d else 0) for d in steps]
     picked = pl.pallas_call(
-        lambda *refs: pick_kernel(experts, islands, pieces, *refs),
-        in_specs=[SMEM] + [ANY] * 6,
-        out_specs=[ANY] * (experts + len(steps)),
-        out_shape=[jax.ShapeDtypeStruct((2 * slots, half), BF16)] * experts
-        + [jax.ShapeDtypeStruct((rows, columns), BF16) for rows in block_rows],
+        lambda *refs: pick_kernel(experts, *refs),
+        in_specs=[SMEM] + [ANY] * 5,
+        out_specs=[VMEM] * experts,
+        out_shape=[jax.ShapeDtypeStruct((2 * slots, half), BF16)] * experts,
         scratch_shapes=[
             pltpu.VMEM(slot_token.shape, jnp.int32),
             pltpu.SMEM(slot_count.shape, jnp.int32),
             pltpu.VMEM(slot_prob.shape, F32),
             pltpu.VMEM(tokens.shape, BF16),
             pltpu.VMEM(token_grads.shape, BF16),
-            pltpu.VMEM((experts, 2 * slots, half), BF16),
-            pltpu.VMEM((sum(p[2] for p in pieces), columns), BF16),
             pltpu.SemaphoreType.DMA((5,)),
-            pltpu.SemaphoreType.DMA((len(pieces),)),
-            pltpu.SemaphoreType.DMA((len(pieces) + experts,)),
         ],
         compiler_params=params(56),
         name="pick_slots",
-    )(spot, slot_token, slot_count, slot_prob, tokens, token_grads, drift)
+    )(spot, slot_token, slot_count, slot_prob, tokens, token_grads)
+    blocks = pl.pallas_call(
+        lambda *refs: cut_kernel(islands, pieces, *refs),
+        in_specs=[SMEM, ANY],
+        out_specs=[VMEM] * len(steps),
+        out_shape=[jax.ShapeDtypeStruct((rows, columns), BF16) for rows in block_rows],
+        scratch_shapes=[pltpu.SemaphoreType.DMA((len(pieces),))],
+        compiler_params=params(56),
+        name="cut_drift",
+    )(spot, drift)
     arrived = [picked[0]] + [swap(picked[d], "expert", d) for d in range(1, experts)]
-    blocks = list(picked[experts:])
-    arrived[0], blocks[0] = pl.pallas_call(
+    drift_in = [blocks[0]] + [swap(blocks[d], "island", d) for d in steps[1:]]
+    arrived[0], drift_in[0] = pl.pallas_call(
         own_kernel,
         in_specs=[VMEM] * 2,
         out_specs=[VMEM] * 2,
@@ -296,21 +291,27 @@
         ],
         compiler_params=params(6),
         name="own_parts",
-    )(arrived[0], blocks[0])
-    drift_in = [blocks[0]] + [swap(blocks[d], "island", d) for d in steps[1:]]
-    joined, turned, drift_sum, *relays = pl.pallas_call(
-        lambda *refs: join_kernel(experts, len(steps), *refs),
-        in_specs=[VMEM] * (experts + len(steps)),
-        out_specs=[VMEM] * (5 if handed else 3),
+    )(arrived[0], drift_in[0])
+    joined = pl.pallas_call(
+        lambda *refs: gather_kernel(experts, *refs),
+        in_specs=[VMEM] * experts,
+        out_specs=VMEM,
+        out_shape=jax.ShapeDtypeStruct((2 * routed_rows, half), BF16),
+        compiler_params=params(6 + routed_rows // 48),
+        name="gather_slots",
+    )(*arrived)
+    turned, drift_sum, *relays = pl.pallas_call(
+        lambda *refs: join_kernel(len(steps), *refs),
+        in_specs=[VMEM] * (1 + len(steps)),
+        out_specs=[VMEM] * (4 if handed else 2),
         out_shape=[
-            jax.ShapeDtypeStruct((2 * routed_rows, half), BF16),
             jax.ShapeDtypeStruct((half, routed_rows), BF16),
             jax.ShapeDtypeStruct((half, columns), F32),
         ]
         + [jax.ShapeDtypeStruct((handed, columns), BF16)] * (2 if handed else 0),
         compiler_params=params(12 + routed_rows // 48),
-        name="join_slots",
-    )(*arrived, *drift_in)
+        name="join_blocks",
+    )(joined, *drift_in)
 
     joined_all = [joined] + [swap(joined, "tensor", t) for t in range(1, parts)]
 
@@ -340,39 +341,41 @@
         out_specs=[VMEM] * 2,
         out_shape=[
             jax.ShapeDtypeStruct((across, routed_rows, columns), BF16),
-            jax.ShapeDtypeStruct((experts * parts, 8, 128), F32),
+            jax.ShapeDtypeStruct((devices, 8, 128), F32),
         ],
         compiler_params=params(16 + routed_rows // 48),
         name="hidden_grads",
     )(spot, gate_weight, down_weight, *joined_all)
-    norms = lax.all_to_all(norms, AXES[1:], split_axis=0, concat_axis=0, tiled=True)
-
     tails = [2, 1] if handed else []
     message_rows = [
-        NOTE_ROWS + routed_rows + (half - handed if d in tails else 0) for d in range(islands)
+        routed_rows + (half - handed if d in tails else 0) for d in range(islands)
     ]
-    features_in, *messages = pl.pallas_call(
+    features_in, norms, *messages = pl.pallas_call(
         lambda *refs: hand_kernel(islands, tails, *refs),
         in_specs=[SMEM] + [VMEM] * (2 + islands + len(relays)),
-        out_specs=[VMEM] * (1 + islands),
-        out_shape=[jax.ShapeDtypeStruct((islands, half, routed_rows), BF16)]
+        out_specs=[VMEM] * (2 + islands),
+        out_shape=[
+            jax.ShapeDtypeStruct((islands, half, routed_rows), BF16),
+            jax.ShapeDtypeStruct(norms.shape, F32),
+        ]
         + [jax.ShapeDtypeStruct((rows, columns), BF16) for rows in message_rows],
         compiler_params=params(6 + routed_rows // 48),
         name="hand_on",
     )(spot, norms, hidden_out, turned, *features_in, *relays)
     features_moved = spread(features_in)
+    norms = lax.all_to_all(norms, AXES, split_axis=0, concat_axis=0, tiled=True)
     messages_in = [messages[0]] + [swap(messages[d], "island", d) for d in range(1, islands)]
 
     *halves, notes = pl.pallas_call(
-        lambda *refs: average_kernel(islands, entries, 4, *refs),
-        in_specs=[SMEM] + [VMEM] * (3 + islands),
+        lambda *refs: average_kernel(islands, entries, 2, *refs),
+        in_specs=[SMEM] + [VMEM] * (4 + islands),
         out_specs=[VMEM] * 3,
         out_shape=[jax.ShapeDtypeStruct((half // 2, columns), F32)] * 2
         + [jax.ShapeDtypeStruct((devices, 8, 128), F32)],
         scratch_shapes=[pltpu.VMEM((half, columns), F32), pltpu.VMEM((1, columns), F32)],
         compiler_params=params(8 + routed_rows // 48),
         name="average_block",
-    )(spot, drift_sum, features_in, features_moved, *messages_in)
+    )(spot, norms, drift_sum, features_in, features_moved, *messages_in)
     notes = lax.all_to_all(notes, AXES, split_axis=0, concat_axis=0, tiled=True)
 
     parted = half // 2
@@ -394,11 +397,11 @@
         source = (at * experts + expert) * parts + part
         place += [(at // across) * half, (at % across) * columns, source]
     place = jnp.stack(place).astype(jnp.int32)
-    values |= last
-    return tuple(
-        pl.pallas_call(
-            lambda *refs: update_kernel(entries, list(values), *refs),
-            in_specs=[SMEM, VMEM, ANY] + [VMEM] * len(values),
+    outs = []
+    for values, cost in ((values, 12), (last, 3)):
+        outs = pl.pallas_call(
+            functools.partial(update_kernel, entries, list(values)),
+            in_specs=[SMEM, VMEM, ANY] + [VMEM] * len(values) + [ANY] * len(outs),
             out_specs=[ANY, ANY],
             out_shape=[
                 jax.ShapeDtypeStruct(momentum.shape, F32),
@@ -410,10 +413,14 @@
                 pltpu.SemaphoreType.DMA((len(values),)),
                 pltpu.SemaphoreType.DMA((len(values), 2)),
             ],
+            input_output_aliases={3 + len(values) + n: n for n in range(len(outs))},
+            cost_estimate=pl.CostEstimate(
+                flops=0, bytes_accessed=cost * momentum.size, transcendentals=0
+            ),
             compiler_params=params(50),
-            name="update_outputs",
-        )(place, notes, momentum, *[v.astype(F32) for v in values.values()])
-    )
+            name="update_pieces",
+        )(place, notes, momentum, *[v.astype(F32) for v in values.values()], *outs)
+    return tuple(outs)
 
 
 def solution(mesh):

time: 154 us -> 144 us (0.935)
  blocking collectives: 0 us -> 21.3 us
  waiting for transfers between devices: 70.2 us -> 50.4 us
  starting transfers between devices: 37.5 us -> 30.2 us
  local copies, waits for them, and re-layouts: 8.19 us -> 3 us
  Pallas kernels: 25.9 us -> 28.5 us
  other arithmetic: 10.7 us -> 8.93 us
    ppermute x15, waiting for transfers between devices: 64.3 us -> 32.8 us  [swap(): lax.ppermute(value, axis, [(at, partner(at, step, size)) for at in range(...]
    all_to_all x0 -> x1, blocking collectives: none -> 21.3 us  [body(): norms = lax.all_to_all(norms, AXES, split_axis=0, concat_axis=0, tiled=True)]
    ppermute x3, waiting for transfers between devices: 1.15 us -> 12.9 us  [send_features(): return lax.ppermute(turned, ('island', 'tensor'), pairs)]
    all_to_all x1 -> x0, starting transfers between devices: 10.2 us -> none  [body(): lax.all_to_all(norms, AXES[1:], split_axis=0, concat_axis=0, tiled=True)]
    unnamed x22 -> x12, local copies, waits for them, and re-layouts: 7.49 us -> 2.28 us
    all_to_all x1, waiting for transfers between devices: 0.01 us -> 4.78 us  [body(): notes = lax.all_to_all(notes, AXES, split_axis=0, concat_axis=0, tiled=True)]
    all_to_all x1 -> x0, waiting for transfers between devices: 4.7 us -> none  [body(): lax.all_to_all(norms, AXES[1:], split_axis=0, concat_axis=0, tiled=True)]
    pallas_call x4 -> x7, Pallas kernels: 18.5 us -> 22 us  [the longest x2 8.69 us: body(): pl.pallas_call(functools.partial(update_kernel, entries, list(values)), i...]
  transfers between devices with their start and end apart: 21 -> 20, of which waited for: 10 -> 9; matrix products, arithmetic and copies ran while one was open for 7% -> 6% of each run, Pallas kernels for 4% -> 11%
where the time goes in v8:
time: 144 us; the launch traced here: 143 us
  waiting for transfers between devices  50.4 us (35%)
  starting transfers between devices  30.2 us (21%)
  Pallas kernels  28.5 us (20%)
  blocking collectives  21.3 us (15%)
  other arithmetic  8.93 us (6%)
  local copies, waits for them, and re-layouts  3 us (2%)
    ppermute x15, waiting for transfers between devices, swap(): lax.ppermute(value, axis, [(at, partner(at, step, size)) for at in range(...  32.8 us
    all_to_all x1, blocking collectives, body(): norms = lax.all_to_all(norms, AXES, split_axis=0, concat_axis=0, tiled=True)  21.3 us
    ppermute x15, starting transfers between devices, swap(): lax.ppermute(value, axis, [(at, partner(at, step, size)) for at in range(...  18.1 us
    ppermute x3, waiting for transfers between devices, send_features(): return lax.ppermute(turned, ('island', 'tensor'), pairs)  12.9 us
    pallas_call x2, Pallas kernels, body(): pl.pallas_call(functools.partial(update_kernel, entries, list(values)), i...  8.69 us
    convert_element_type x6, other arithmetic, body(): v.astype(F32)  8.08 us
    all_to_all x1, starting transfers between devices, body(): notes = lax.all_to_all(notes, AXES, split_axis=0, concat_axis=0, tiled=True)  5.55 us
    pallas_call x1, Pallas kernels, body(): pl.pallas_call(lambda *refs: hidden_kernel(parts, across, *refs), in_spec...  5.42 us
  transfers between devices with their start and end apart: 20, of which 9 were waited for; matrix products, arithmetic and copies ran while one was open for 6% of the time, Pallas kernels for 11%

profile of v8, /device:TPU:0, one launch (start us, length us, event | category | flops | bytes accessed | tf_op | source)
XLA Modules:
  0.0 143.4 jit_solution(4543027990564539974)
XLA Ops:
  0.7 0.6 stack.79.refs_0_
  1.3 3.6 %pick_slots.1 = (bf16[192,1024]{1,0:T(8,128)(2,1)}, bf16[192,1024]{1,0:T(8,128)(2,1)}, bf16[192,1024]{1,0:T(8,128)(2,1)}, bf16[192,1024]{1,0:T(8,128)(2,1)}) custom-call(s32[6]{0:T(128)} %stack.79.refs_0_, s32[1,1,4,96]{3,2,1,0:T(4,128)} %refs_1_.3, s32[1,1,4]{2,1,0:T(1,128)} %refs_2_.2, f32[1,1,4,96]{3,2,1,0:T(4,128)} %refs_3_.1, ...), custom_call_target="tpu_custom_call" | custom-call | tf_op jit(solution)/shard_map/pick_slots/pallas_call | solution.py:257
  4.9 3.1 %collective-permute-start = (bf16[192,1024]{1,0:T(8,128)(2,1)}, bf16[192,1024]{1,0:T(8,128)(2,1)S(1)}, u32[]{:S(2)}, u32[]{:S(2)}) collective-permute-start(bf16[192,1024]{1,0:T(8,128)(2,1)} %get-tuple-element.31), channel_id=1, source_target_pairs={{0,2},{2,0},{4,6},{6,4},{1,3},{3,1},{5,7},{7,5},{8,10},{10,8},{12,... | collective-permute-start | bytes 1179656 | tf_op jit(solution)/shard_map/ppermute | solution.py:35
  7.9 2.6 %collective-permute-start.1 = (bf16[192,1024]{1,0:T(8,128)(2,1)}, bf16[192,1024]{1,0:T(8,128)(2,1)S(1)}, u32[]{:S(2)}, u32[]{:S(2)}) collective-permute-start(bf16[192,1024]{1,0:T(8,128)(2,1)} %get-tuple-element.32), channel_id=1, source_target_pairs={{0,4},{2,6},{4,0},{6,2},{1,5},{3,7},{5,1},{7,3},{8,12},{10,14},{12... | collective-permute-start | bytes 1179656 | tf_op jit(solution)/shard_map/ppermute | solution.py:35
  10.5 0.0 collective-permute-start.2
  10.5 4.2 %cut_drift.1 = (bf16[1024,384]{1,0:T(8,128)(2,1)}, bf16[1536,384]{1,0:T(8,128)(2,1)}, bf16[1536,384]{1,0:T(8,128)(2,1)}) custom-call(s32[6]{0:T(128)} %stack.79.refs_0_, bf16[1,1,2048,768]{3,2,1,0:T(8,128)(2,1)} %refs_1_.4), custom_call_target="tpu_custom_call" | custom-call | tf_op jit(solution)/shard_map/cut_drift/pallas_call | solution.py:273
  14.7 1.8 %collective-permute-start.4 = (bf16[1536,384]{1,0:T(8,128)(2,1)}, bf16[1536,384]{1,0:T(8,128)(2,1)S(1)}, u32[]{:S(2)}, u32[]{:S(2)}) collective-permute-start(bf16[1536,384]{1,0:T(8,128)(2,1)} %get-tuple-element.37), channel_id=1, source_target_pairs={{0,8},{8,0},{16,24},{24,16},{1,9},{9,1},{17,25},{25,17},{2,10},{10... | collective-permute-start | bytes 3538952 | tf_op jit(solution)/shard_map/ppermute | solution.py:35
  16.5 1.5 %collective-permute-start.5 = (bf16[1536,384]{1,0:T(8,128)(2,1)}, bf16[1536,384]{1,0:T(8,128)(2,1)S(1)}, u32[]{:S(2)}, u32[]{:S(2)}) collective-permute-start(bf16[1536,384]{1,0:T(8,128)(2,1)} %get-tuple-element.38), channel_id=1, source_target_pairs={{0,16},{8,24},{16,0},{24,8},{1,17},{9,25},{17,1},{25,9},{2,18},{10... | collective-permute-start | bytes 3538952 | tf_op jit(solution)/shard_map/ppermute | solution.py:35
  18.0 1.1 copy-done.3
  19.2 0.1 own_parts.1
  19.3 5.7 %collective-permute-done.refs_1_ = bf16[192,1024]{1,0:T(8,128)(2,1)S(1)} collective-permute-done((bf16[192,1024]{1,0:T(8,128)(2,1)}, bf16[192,1024]{1,0:T(8,128)(2,1)S(1)}, u32[]{:S(2)}, u32[]{:S(2)}) %collective-permute-start) | collective-permute-done | bytes 393248 | tf_op jit(solution)/shard_map/ppermute | solution.py:35
  24.9 13.0 %collective-permute-done.1.refs_2_ = bf16[192,1024]{1,0:T(8,128)(2,1)S(1)} collective-permute-done((bf16[192,1024]{1,0:T(8,128)(2,1)}, bf16[192,1024]{1,0:T(8,128)(2,1)S(1)}, u32[]{:S(2)}, u32[]{:S(2)}) %collective-permute-start.1) | collective-permute-done | bytes 393248 | tf_op jit(solution)/shard_map/ppermute | solution.py:35
  37.9 0.0 collective-permute-done.2.refs_3_
  38.0 0.1 gather_slots.1.refs_3_.refs_0_
  38.1 0.0 copy-start.1
  38.1 0.1 collective-permute-start.3
  38.2 4.0 %collective-permute-done.4.refs_2_ = bf16[1536,384]{1,0:T(8,128)(2,1)S(1)} collective-permute-done((bf16[1536,384]{1,0:T(8,128)(2,1)}, bf16[1536,384]{1,0:T(8,128)(2,1)S(1)}, u32[]{:S(2)}, u32[]{:S(2)}) %collective-permute-start.4) | collective-permute-done | bytes 1179680 | tf_op jit(solution)/shard_map/ppermute | solution.py:35
  42.2 1.2 collective-permute-done.5.refs_3_
  43.4 0.7 join_blocks.1
  44.1 1.3 collective-permute-start.8
  45.4 1.3 collective-permute-start.7
  46.7 2.4 %collective-permute-start.6 = (bf16[1024,384]{1,0:T(8,128)(2,1)S(1)}, bf16[1024,384]{1,0:T(8,128)(2,1)S(1)}, u32[]{:S(2)}, u32[]{:S(2)}) collective-permute-start(bf16[1024,384]{1,0:T(8,128)(2,1)S(1)} %get-tuple-element.39.refs_3_), channel_id=1, source_target_pairs={{0,8},{8,0},{17,25},{25,17},{2,10},{10,2},{19,27},{27,19},{4,12},{... | collective-permute-start | bytes 2359304 | tf_op jit(solution)/shard_map/ppermute | solution.py:323
  49.1 0.0 collective-permute-done.3.refs_4_
  49.2 5.4 %hidden_grads.1 = (bf16[2,384,384]{2,1,0:T(8,128)(2,1)S(1)}, f32[32,8,128]{2,1,0:T(8,128)S(1)}) custom-call(s32[6]{0:T(128)S(1)} %copy-done.5, bf16[1,1,2048,768]{3,2,1,0:T(8,128)(2,1)S(1)} %copy-done.1, bf16[1,1,768,2048]{3,2,1,0:T(8,128)(2,1)S(1)} %copy-done.2, bf16[768,1024]{1,0:T(8,128)(2,1)S(1)} %gather_slots.1.refs_3_.refs_0_, ...), custom_call_target="tpu_custom_call" | custom-call | tf_op jit(solution)/shard_map/hidden_grads/pallas_call | solution.py:338
  54.6 12.3 %collective-permute-done.8.refs_6_ = bf16[1024,384]{1,0:T(8,128)(2,1)S(1)} collective-permute-done((bf16[1024,384]{1,0:T(8,128)(2,1)S(1)}, bf16[1024,384]{1,0:T(8,128)(2,1)S(1)}, u32[]{:S(2)}, u32[]{:S(2)}) %collective-permute-start.8) | collective-permute-done | bytes 786464 | tf_op jit(solution)/shard_map/ppermute | solution.py:323
  66.9 0.5 collective-permute-done.7.refs_5_
  67.4 0.0 collective-permute-done.6.refs_4_
  67.5 1.0 hand_on.1
  68.4 1.5 %collective-permute-start.9 = (bf16[4,1024,384]{2,1,0:T(8,128)(2,1)S(1)}, bf16[4,1024,384]{2,1,0:T(8,128)(2,1)S(1)}, u32[]{:S(2)}, u32[]{:S(2)}) collective-permute-start(bf16[4,1024,384]{2,1,0:T(8,128)(2,1)S(1)} %get-tuple-element.44.refs_3_), channel_id=1, source_target_pairs={{0,1},{8,9},{17,16},{25,24},{2,3},{10,11},{19,18},{27,26},{4,5},{1... | collective-permute-start | bytes 9437192 | tf_op jit(solution)/shard_map/ppermute | solution.py:332
  69.9 1.1 collective-permute-start.10
  71.0 0.0 collective-permute-start.11
  71.0 2.5 %collective-permute-start.12 = (bf16[384,384]{1,0:T(8,128)(2,1)S(1)}, bf16[384,384]{1,0:T(8,128)(2,1)S(1)}, u32[]{:S(2)}, u32[]{:S(2)}) collective-permute-start(bf16[384,384]{1,0:T(8,128)(2,1)S(1)} %get-tuple-element.48), channel_id=1, source_target_pairs={{0,24},{8,16},{16,8},{24,0},{1,25},{9,17},{17,9},{25,1},{2,26},{10... | collective-permute-start | bytes 884744 | tf_op jit(solution)/shard_map/ppermute | solution.py:35
  73.5 21.3 %all_to_all.10.refs_1_ = f32[32,8,128]{2,1,0:T(8,128)S(1)} all-to-all(f32[32,8,128]{2,1,0:T(8,128)S(1)} %get-tuple-element.42), channel_id=1, replica_groups=mesh['island'=4,'expert'=4,'tensor'=2] {'island','expert','tensor'}, dimensions={0} | all-to-all | bytes 262144 | tf_op jit(solution)/shard_map/all_to_all | solution.py:366
  94.8 0.0 collective-permute-done.12.refs_8_
  94.8 0.0 collective-permute-done.10.refs_6_
  94.8 0.0 collective-permute-done.11.refs_7_
  94.8 0.0 collective-permute-done.9.refs_4_
  94.8 4.7 %average_block.1 = (f32[512,384]{1,0:T(8,128)S(1)}, f32[512,384]{1,0:T(8,128)S(1)}, f32[32,8,128]{2,1,0:T(8,128)}) custom-call(s32[6]{0:T(128)S(1)} %copy-done.5, f32[32,8,128]{2,1,0:T(8,128)S(1)} %all_to_all.10.refs_1_, f32[1024,384]{1,0:T(8,128)S(1)} %get-tuple-element.43.refs_2_, bf16[4,1024,384]{2,1,0:T(8,128)(2,1)S(1)} %get-tuple-element.44.refs_3_, ...), custom_call_target="tpu_custom_call" | custom-call | tf_op jit(solution)/shard_map/average_block/pallas_call | solution.py:369
  99.5 0.1 convert_element_type.27
  99.6 1.8 %collective-permute-start.15 = (f16[512,384]{1,0:T(8,128)(2,1)S(1)}, f16[512,384]{1,0:T(8,128)(2,1)}, u32[]{:S(2)}, u32[]{:S(2)}) collective-permute-start(f16[512,384]{1,0:T(8,128)(2,1)S(1)} %convert_element_type.27), channel_id=1, source_target_pairs={{0,16},{8,24},{16,0},{24,8},{1,17},{9,25},{17,1},{25,9},{2,18},{10... | collective-permute-start | bytes 1179656 | tf_op jit(solution)/shard_map/ppermute | solution.py:35
  101.4 0.8 convert_element_type.25
  102.2 1.1 collective-permute-start.13
  103.2 1.0 collective-permute-start.18
  104.2 0.3 collective-permute-start.17
  104.5 7.2 %collective-permute-done.15 = f16[512,384]{1,0:T(8,128)(2,1)} collective-permute-done((f16[512,384]{1,0:T(8,128)(2,1)S(1)}, f16[512,384]{1,0:T(8,128)(2,1)}, u32[]{:S(2)}, u32[]{:S(2)}) %collective-permute-start.15) | collective-permute-done | bytes 393248 | tf_op jit(solution)/shard_map/ppermute | solution.py:35
  111.7 1.1 collective-permute-start.16
  112.8 1.7 %collective-permute-done.13 = f16[512,384]{1,0:T(8,128)(2,1)} collective-permute-done((f16[512,384]{1,0:T(8,128)(2,1)}, f16[512,384]{1,0:T(8,128)(2,1)}, u32[]{:S(2)}, u32[]{:S(2)}) %collective-permute-start.13) | collective-permute-done | bytes 393248 | tf_op jit(solution)/shard_map/ppermute | solution.py:35
  114.5 0.3 collective-permute-start.14
  114.8 5.5 %all-to-all-start.1 = ((f32[32,8,128]{2,1,0:T(8,128)}), f32[32,8,128]{2,1,0:T(8,128)S(1)}, u32[]{:S(2)}, u32[]{:S(2)}) async-start(f32[32,8,128]{2,1,0:T(8,128)} %get-tuple-element.49), calls=%async_computation.1 | async-start | bytes 262144 | tf_op jit(solution)/shard_map/all_to_all | solution.py:379
  120.5 0.1 stack.72.place
  120.5 1.1 convert_element_type.31.refs_4_
  121.6 2.0 %convert_element_type.32.refs_5_ = f32[512,384]{1,0:T(8,128)} convert(f16[512,384]{1,0:T(8,128)(2,1)} %collective-permute-done.15) | non-fusion elementwise | flops 196608 | bytes 1179648 | tf_op jit(solution)/shard_map/convert_element_type | solution.py:422
  123.6 0.0 collective-permute-done.18
  123.6 1.0 convert_element_type.30.refs_3_
  124.6 0.0 collective-permute-done.17
  124.6 1.9 %convert_element_type.29.refs_2_ = f32[512,384]{1,0:T(8,128)} convert(f16[512,384]{1,0:T(8,128)(2,1)} %collective-permute-done.17) | non-fusion elementwise | flops 196608 | bytes 1179648 | tf_op jit(solution)/shard_map/convert_element_type | solution.py:422
  126.5 4.8 %all-to-all-done.1.notes = f32[32,8,128]{2,1,0:T(8,128)S(1)} async-done(((f32[32,8,128]{2,1,0:T(8,128)}), f32[32,8,128]{2,1,0:T(8,128)S(1)}, u32[]{:S(2)}, u32[]{:S(2)}) %all-to-all-start.1) | async-done | bytes 131104 | tf_op jit(solution)/shard_map/all_to_all | solution.py:379
  131.3 1.1 copy-done
  132.5 5.4 %update_pieces.2 = (f32[1,2048,768]{2,1,0:T(8,128)}, bf16[1,2048,768]{2,1,0:T(8,128)(2,1)}) custom-call(s32[12]{0:T(128)S(1)} %stack.72.place, f32[32,8,128]{2,1,0:T(8,128)S(1)} %all-to-all-done.1.notes, f32[1,2048,768]{2,1,0:T(8,128)} %momentum.3, f32[512,384]{1,0:T(8,128)S(1)} %get-tuple-element.50.refs_0_, f32[512,384]{1,0:T(8,128)S(1)} %get-tuple-element.51.refs_1_, ...), custom_call_target="tpu_custom_call" | custom-call | bytes 18874368 | tf_op jit(solution)/shard_map/update_pieces/pallas_call | solution.py:402
  137.9 0.0 collective-permute-done.16
  137.9 1.0 convert_element_type.28.refs_1_
  139.0 0.0 collective-permute-done.14
  139.0 1.0 convert_element_type.26.refs_0_
  140.0 3.2 %update_pieces.3 = (f32[1,2048,768]{2,1,0:T(8,128)}, bf16[1,2048,768]{2,1,0:T(8,128)(2,1)}) custom-call(s32[12]{0:T(128)S(1)} %stack.72.place, f32[32,8,128]{2,1,0:T(8,128)S(1)} %all-to-all-done.1.notes, f32[1,2048,768]{2,1,0:T(8,128)} %momentum.3, f32[512,384]{1,0:T(8,128)S(1)} %convert_element_type.26.refs_0_, ...), custom_call_target="tpu_custom_call", output_to_operand_aliasing={{0}: (5, {}), {1}: (6, {})} | custom-call | bytes 4718592 | tf_op jit(solution)/shard_map/update_pieces/pallas_call | solution.py:402
  (9 shorter events, 0.0 us)
Async XLA Ops:
  4.8 13.2 %copy-start.4 = (bf16[192,1024]{1,0:T(8,128)(2,1)S(1)}, bf16[192,1024]{1,0:T(8,128)(2,1)}, u32[]{:S(2)}) copy-start(bf16[192,1024]{1,0:T(8,128)(2,1)} %get-tuple-element.28.slots) | copy-start | bytes 1179652
  4.9 20.1 %collective-permute-start = (bf16[192,1024]{1,0:T(8,128)(2,1)}, bf16[192,1024]{1,0:T(8,128)(2,1)S(1)}, u32[]{:S(2)}, u32[]{:S(2)}) collective-permute-start(bf16[192,1024]{1,0:T(8,128)(2,1)} %get-tuple-element.31), channel_id=1, source_target_pairs={{0,2},{2,0},{4,6},{6,4},{1,3},{3,1},{5,7},{7,5},{8,10},{10,8},{12,... | collective-permute-start | bytes 1179656 | tf_op jit(solution)/shard_map/ppermute | solution.py:35
  7.9 30.0 %collective-permute-start.1 = (bf16[192,1024]{1,0:T(8,128)(2,1)}, bf16[192,1024]{1,0:T(8,128)(2,1)S(1)}, u32[]{:S(2)}, u32[]{:S(2)}) collective-permute-start(bf16[192,1024]{1,0:T(8,128)(2,1)} %get-tuple-element.32), channel_id=1, source_target_pairs={{0,4},{2,6},{4,0},{6,2},{1,5},{3,7},{5,1},{7,3},{8,12},{10,14},{12... | collective-permute-start | bytes 1179656 | tf_op jit(solution)/shard_map/ppermute | solution.py:35
  10.5 27.4 %collective-permute-start.2 = (bf16[192,1024]{1,0:T(8,128)(2,1)}, bf16[192,1024]{1,0:T(8,128)(2,1)S(1)}, u32[]{:S(2)}, u32[]{:S(2)}) collective-permute-start(bf16[192,1024]{1,0:T(8,128)(2,1)} %get-tuple-element.33), channel_id=1, source_target_pairs={{0,6},{2,4},{4,2},{6,0},{1,7},{3,5},{5,3},{7,1},{8,14},{10,12},{12... | collective-permute-start | bytes 1179656 | tf_op jit(solution)/shard_map/ppermute | solution.py:35
  14.7 27.4 %collective-permute-start.4 = (bf16[1536,384]{1,0:T(8,128)(2,1)}, bf16[1536,384]{1,0:T(8,128)(2,1)S(1)}, u32[]{:S(2)}, u32[]{:S(2)}) collective-permute-start(bf16[1536,384]{1,0:T(8,128)(2,1)} %get-tuple-element.37), channel_id=1, source_target_pairs={{0,8},{8,0},{16,24},{24,16},{1,9},{9,1},{17,25},{25,17},{2,10},{10... | collective-permute-start | bytes 3538952 | tf_op jit(solution)/shard_map/ppermute | solution.py:35
  16.5 26.9 %collective-permute-start.5 = (bf16[1536,384]{1,0:T(8,128)(2,1)}, bf16[1536,384]{1,0:T(8,128)(2,1)S(1)}, u32[]{:S(2)}, u32[]{:S(2)}) collective-permute-start(bf16[1536,384]{1,0:T(8,128)(2,1)} %get-tuple-element.38), channel_id=1, source_target_pairs={{0,16},{8,24},{16,0},{24,8},{1,17},{9,25},{17,1},{25,9},{2,18},{10... | collective-permute-start | bytes 3538952 | tf_op jit(solution)/shard_map/ppermute | solution.py:35
  18.0 1.1 copy-start.3
  37.9 11.2 %copy-start.2 = (bf16[1,1,768,2048]{3,2,1,0:T(8,128)(2,1)S(1)}, bf16[1,1,768,2048]{3,2,1,0:T(8,128)(2,1)}, u32[]{:S(2)}) copy-start(bf16[1,1,768,2048]{3,2,1,0:T(8,128)(2,1)} %refs_2_.3) | copy-start | bytes 9437188
  38.1 11.1 %copy-start.1 = (bf16[1,1,2048,768]{3,2,1,0:T(8,128)(2,1)S(1)}, bf16[1,1,2048,768]{3,2,1,0:T(8,128)(2,1)}, u32[]{:S(2)}) copy-start(bf16[1,1,2048,768]{3,2,1,0:T(8,128)(2,1)} %refs_1_.5) | copy-start | bytes 9437188
  38.1 11.1 %copy-start.5 = (s32[6]{0:T(128)S(1)}, s32[6]{0:T(128)}, u32[]{:S(2)}) copy-start(s32[6]{0:T(128)} %stack.79.refs_0_) | copy-start | bytes 76
  38.1 11.0 %collective-permute-start.3 = (bf16[768,1024]{1,0:T(8,128)(2,1)S(1)}, bf16[768,1024]{1,0:T(8,128)(2,1)S(1)}, u32[]{:S(2)}, u32[]{:S(2)}) collective-permute-start(bf16[768,1024]{1,0:T(8,128)(2,1)S(1)} %gather_slots.1.refs_3_.refs_0_), channel_id=1, source_target_pairs={{0,1},{1,0},{2,3},{3,2},{4,5},{5,4},{6,7},{7,6},{8,9},{9,8},{10,11... | collective-permute-start | bytes 4718600 | tf_op jit(solution)/shard_map/ppermute | solution.py:35
  44.1 22.9 %collective-permute-start.8 = (bf16[1024,384]{1,0:T(8,128)(2,1)S(1)}, bf16[1024,384]{1,0:T(8,128)(2,1)S(1)}, u32[]{:S(2)}, u32[]{:S(2)}) collective-permute-start(bf16[1024,384]{1,0:T(8,128)(2,1)S(1)} %get-tuple-element.39.refs_3_), channel_id=1, source_target_pairs={{1,25},{9,17},{16,8},{24,0},{3,27},{11,19},{18,10},{26,2},{5,29},{... | collective-permute-start | bytes 2359304 | tf_op jit(solution)/shard_map/ppermute | solution.py:323
  45.4 22.1 %collective-permute-start.7 = (bf16[1024,384]{1,0:T(8,128)(2,1)S(1)}, bf16[1024,384]{1,0:T(8,128)(2,1)S(1)}, u32[]{:S(2)}, u32[]{:S(2)}) collective-permute-start(bf16[1024,384]{1,0:T(8,128)(2,1)S(1)} %get-tuple-element.39.refs_3_), channel_id=1, source_target_pairs={{1,17},{9,25},{16,0},{24,8},{3,19},{11,27},{18,2},{26,10},{5,21},{... | collective-permute-start | bytes 2359304 | tf_op jit(solution)/shard_map/ppermute | solution.py:323
  46.7 20.8 %collective-permute-start.6 = (bf16[1024,384]{1,0:T(8,128)(2,1)S(1)}, bf16[1024,384]{1,0:T(8,128)(2,1)S(1)}, u32[]{:S(2)}, u32[]{:S(2)}) collective-permute-start(bf16[1024,384]{1,0:T(8,128)(2,1)S(1)} %get-tuple-element.39.refs_3_), channel_id=1, source_target_pairs={{0,8},{8,0},{17,25},{25,17},{2,10},{10,2},{19,27},{27,19},{4,12},{... | collective-permute-start | bytes 2359304 | tf_op jit(solution)/shard_map/ppermute | solution.py:323
  68.4 26.3 %collective-permute-start.9 = (bf16[4,1024,384]{2,1,0:T(8,128)(2,1)S(1)}, bf16[4,1024,384]{2,1,0:T(8,128)(2,1)S(1)}, u32[]{:S(2)}, u32[]{:S(2)}) collective-permute-start(bf16[4,1024,384]{2,1,0:T(8,128)(2,1)S(1)} %get-tuple-element.44.refs_3_), channel_id=1, source_target_pairs={{0,1},{8,9},{17,16},{25,24},{2,3},{10,11},{19,18},{27,26},{4,5},{1... | collective-permute-start | bytes 9437192 | tf_op jit(solution)/shard_map/ppermute | solution.py:332
  69.9 24.8 %collective-permute-start.10 = (bf16[896,384]{1,0:T(8,128)(2,1)S(1)}, bf16[896,384]{1,0:T(8,128)(2,1)S(1)}, u32[]{:S(2)}, u32[]{:S(2)}) collective-permute-start(bf16[896,384]{1,0:T(8,128)(2,1)S(1)} %get-tuple-element.46), channel_id=1, source_target_pairs={{0,8},{8,0},{16,24},{24,16},{1,9},{9,1},{17,25},{25,17},{2,10},{10... | collective-permute-start | bytes 2064392 | tf_op jit(solution)/shard_map/ppermute | solution.py:35
  71.0 23.8 %collective-permute-start.11 = (bf16[896,384]{1,0:T(8,128)(2,1)S(1)}, bf16[896,384]{1,0:T(8,128)(2,1)S(1)}, u32[]{:S(2)}, u32[]{:S(2)}) collective-permute-start(bf16[896,384]{1,0:T(8,128)(2,1)S(1)} %get-tuple-element.47), channel_id=1, source_target_pairs={{0,16},{8,24},{16,0},{24,8},{1,17},{9,25},{17,1},{25,9},{2,18},{10... | collective-permute-start | bytes 2064392 | tf_op jit(solution)/shard_map/ppermute | solution.py:35
  71.0 23.8 %collective-permute-start.12 = (bf16[384,384]{1,0:T(8,128)(2,1)S(1)}, bf16[384,384]{1,0:T(8,128)(2,1)S(1)}, u32[]{:S(2)}, u32[]{:S(2)}) collective-permute-start(bf16[384,384]{1,0:T(8,128)(2,1)S(1)} %get-tuple-element.48), channel_id=1, source_target_pairs={{0,24},{8,16},{16,8},{24,0},{1,25},{9,17},{17,9},{25,1},{2,26},{10... | collective-permute-start | bytes 884744 | tf_op jit(solution)/shard_map/ppermute | solution.py:35
  99.6 12.1 %collective-permute-start.15 = (f16[512,384]{1,0:T(8,128)(2,1)S(1)}, f16[512,384]{1,0:T(8,128)(2,1)}, u32[]{:S(2)}, u32[]{:S(2)}) collective-permute-start(f16[512,384]{1,0:T(8,128)(2,1)S(1)} %convert_element_type.27), channel_id=1, source_target_pairs={{0,16},{8,24},{16,0},{24,8},{1,17},{9,25},{17,1},{25,9},{2,18},{10... | collective-permute-start | bytes 1179656 | tf_op jit(solution)/shard_map/ppermute | solution.py:35
  102.2 12.3 %collective-permute-start.13 = (f16[512,384]{1,0:T(8,128)(2,1)}, f16[512,384]{1,0:T(8,128)(2,1)}, u32[]{:S(2)}, u32[]{:S(2)}) collective-permute-start(f16[512,384]{1,0:T(8,128)(2,1)} %convert_element_type.25), channel_id=1, source_target_pairs={{0,8},{8,0},{16,24},{24,16},{1,9},{9,1},{17,25},{25,17},{2,10},{10... | collective-permute-start | bytes 1179656 | tf_op jit(solution)/shard_map/ppermute | solution.py:35
  103.2 20.4 %collective-permute-start.18 = (f16[512,384]{1,0:T(8,128)(2,1)S(1)}, f16[512,384]{1,0:T(8,128)(2,1)}, u32[]{:S(2)}, u32[]{:S(2)}) collective-permute-start(f16[512,384]{1,0:T(8,128)(2,1)S(1)} %convert_element_type.27), channel_id=1, source_target_pairs={{0,8},{8,0},{16,24},{24,16},{1,9},{9,1},{17,25},{25,17},{2,10},{10... | collective-permute-start | bytes 1179656 | tf_op jit(solution)/shard_map/ppermute | solution.py:35
  104.2 20.4 %collective-permute-start.17 = (f16[512,384]{1,0:T(8,128)(2,1)}, f16[512,384]{1,0:T(8,128)(2,1)}, u32[]{:S(2)}, u32[]{:S(2)}) collective-permute-start(f16[512,384]{1,0:T(8,128)(2,1)} %convert_element_type.25), channel_id=1, source_target_pairs={{0,16},{8,24},{16,0},{24,8},{1,17},{9,25},{17,1},{25,9},{2,18},{10... | collective-permute-start | bytes 1179656 | tf_op jit(solution)/shard_map/ppermute | solution.py:35
  111.7 26.2 %collective-permute-start.16 = (f16[512,384]{1,0:T(8,128)(2,1)}, f16[512,384]{1,0:T(8,128)(2,1)}, u32[]{:S(2)}, u32[]{:S(2)}) collective-permute-start(f16[512,384]{1,0:T(8,128)(2,1)} %collective-permute-done.15), channel_id=1, source_target_pairs={{0,8},{8,0},{16,24},{24,16},{1,9},{9,1},{17,25},{25,17},{2,10},{10... | collective-permute-start | bytes 1179656 | tf_op jit(solution)/shard_map/ppermute | solution.py:35
  114.5 24.5 %collective-permute-start.14 = (f16[512,384]{1,0:T(8,128)(2,1)}, f16[512,384]{1,0:T(8,128)(2,1)}, u32[]{:S(2)}, u32[]{:S(2)}) collective-permute-start(f16[512,384]{1,0:T(8,128)(2,1)} %collective-permute-done.13), channel_id=1, source_target_pairs={{0,16},{8,24},{16,0},{24,8},{1,17},{9,25},{17,1},{25,9},{2,18},{10... | collective-permute-start | bytes 1179656 | tf_op jit(solution)/shard_map/ppermute | solution.py:35
  114.8 16.5 %all-to-all-start.1 = ((f32[32,8,128]{2,1,0:T(8,128)}), f32[32,8,128]{2,1,0:T(8,128)S(1)}, u32[]{:S(2)}, u32[]{:S(2)}) async-start(f32[32,8,128]{2,1,0:T(8,128)} %get-tuple-element.49), calls=%async_computation.1 | async-start | bytes 262144 | tf_op jit(solution)/shard_map/all_to_all | solution.py:379
  131.3 1.1 copy-start

commit v9 on v8

--- a/solution.py
+++ b/solution.py
@@ -235,7 +235,6 @@
 ):
     islands, experts, parts = (lax.axis_size(a) for a in AXES)
     island, expert, part = (lax.axis_index(a) for a in AXES)
-    devices = islands * experts * parts
     features, hidden = gate_weight.shape[2:]
     half = features // parts
     across = islands // parts
@@ -341,7 +340,7 @@
         out_specs=[VMEM] * 2,
         out_shape=[
             jax.ShapeDtypeStruct((across, routed_rows, columns), BF16),
-            jax.ShapeDtypeStruct((devices, 8, 128), F32),
+            jax.ShapeDtypeStruct((1, 8, 128), F32),
         ],
         compiler_params=params(16 + routed_rows // 48),
         name="hidden_grads",
@@ -363,7 +362,7 @@
         name="hand_on",
     )(spot, norms, hidden_out, turned, *features_in, *relays)
     features_moved = spread(features_in)
-    norms = lax.all_to_all(norms, AXES, split_axis=0, concat_axis=0, tiled=True)
+    norms = lax.all_gather(norms, AXES, axis=0, tiled=True)
     messages_in = [messages[0]] + [swap(messages[d], "island", d) for d in range(1, islands)]
 
     *halves, notes = pl.pallas_call(
@@ -371,12 +370,12 @@
         in_specs=[SMEM] + [VMEM] * (4 + islands),
         out_specs=[VMEM] * 3,
         out_shape=[jax.ShapeDtypeStruct((half // 2, columns), F32)] * 2
-        + [jax.ShapeDtypeStruct((devices, 8, 128), F32)],
+        + [jax.ShapeDtypeStruct((1, 8, 128), F32)],
         scratch_shapes=[pltpu.VMEM((half, columns), F32), pltpu.VMEM((1, columns), F32)],
         compiler_params=params(8 + routed_rows // 48),
         name="average_block",
     )(spot, norms, drift_sum, features_in, features_moved, *messages_in)
-    notes = lax.all_to_all(notes, AXES, split_axis=0, concat_axis=0, tiled=True)
+    notes = lax.all_gather(notes, AXES, axis=0, tiled=True)
 
     parted = half // 2
     sent = [v.astype(WIRE) for v in halves]

time: 144 us -> 183 us (1.27)
  blocking collectives: 21.3 us -> 77.6 us
  starting transfers between devices: 30.2 us -> 23.3 us
  other arithmetic: 8.93 us -> 4.06 us
  waiting for transfers between devices: 50.4 us -> 46.7 us
    all_gather x0 -> x2, blocking collectives: none -> 77.6 us  [the longest x1 40.6 us: body(): norms = lax.all_gather(norms, AXES, axis=0, tiled=True)]
    all_to_all x1 -> x0, blocking collectives: 21.3 us -> none  [body(): norms = lax.all_to_all(norms, AXES, split_axis=0, concat_axis=0, tiled=True)]
    all_to_all x1 -> x0, starting transfers between devices: 5.55 us -> none  [body(): notes = lax.all_to_all(notes, AXES, split_axis=0, concat_axis=0, tiled=True)]
    convert_element_type x6, other arithmetic: 8.08 us -> 3.21 us  [body(): v.astype(F32)]
    all_to_all x1 -> x0, waiting for transfers between devices: 4.78 us -> none  [body(): notes = lax.all_to_all(notes, AXES, split_axis=0, concat_axis=0, tiled=True)]
  transfers between devices with their start and end apart: 20 -> 19, of which waited for: 9 -> 8; matrix products, arithmetic and copies ran while one was open for 6% -> 2% of each run, Pallas kernels for 11% -> 9%
where the time goes in v9:
time: 183 us; the launch traced here: 182 us
  blocking collectives  77.6 us (42%)
  waiting for transfers between devices  46.7 us (26%)
  Pallas kernels  27.9 us (15%)
  starting transfers between devices  23.3 us (13%)
  other arithmetic  4.06 us (2%)
  local copies, waits for them, and re-layouts  1.83 us (1%)
    all_gather x1, blocking collectives, body(): norms = lax.all_gather(norms, AXES, axis=0, tiled=True)  40.6 us
    all_gather x1, blocking collectives, body(): notes = lax.all_gather(notes, AXES, axis=0, tiled=True)  37 us
    ppermute x15, waiting for transfers between devices, swap(): lax.ppermute(value, axis, [(at, partner(at, step, size)) for at in range(...  33.9 us
    ppermute x15, starting transfers between devices, swap(): lax.ppermute(value, axis, [(at, partner(at, step, size)) for at in range(...  16.8 us
    ppermute x3, waiting for transfers between devices, send_features(): return lax.ppermute(turned, ('island', 'tensor'), pairs)  12.8 us
    pallas_call x2, Pallas kernels, body(): pl.pallas_call(functools.partial(update_kernel, entries, list(values)), i...  8.7 us
    pallas_call x1, Pallas kernels, body(): pl.pallas_call(lambda *refs: hidden_kernel(parts, across, *refs), in_spec...  5.44 us
    ppermute x3, starting transfers between devices, send_features(): return lax.ppermute(turned, ('island', 'tensor'), pairs)  5.03 us
  transfers between devices with their start and end apart: 19, of which 8 were waited for; matrix products, arithmetic and copies ran while one was open for 2% of the time, Pallas kernels for 9%

profile of v9, /device:TPU:0, one launch (start us, length us, event | category | flops | bytes accessed | tf_op | source)
XLA Modules:
  0.0 182.4 jit_solution(12623451108206562658)
XLA Ops:
  0.7 0.6 stack.79.refs_0_
  1.3 3.6 %pick_slots.1 = (bf16[192,1024]{1,0:T(8,128)(2,1)}, bf16[192,1024]{1,0:T(8,128)(2,1)}, bf16[192,1024]{1,0:T(8,128)(2,1)}, bf16[192,1024]{1,0:T(8,128)(2,1)}) custom-call(s32[6]{0:T(128)} %stack.79.refs_0_, s32[1,1,4,96]{3,2,1,0:T(4,128)} %refs_1_.3, s32[1,1,4]{2,1,0:T(1,128)} %refs_2_.2, f32[1,1,4,96]{3,2,1,0:T(4,128)} %refs_3_.1, ...), custom_call_target="tpu_custom_call" | custom-call | tf_op jit(solution)/shard_map/pick_slots/pallas_call | solution.py:256
  4.8 0.0 copy-start.3
  4.8 3.1 %collective-permute-start = (bf16[192,1024]{1,0:T(8,128)(2,1)}, bf16[192,1024]{1,0:T(8,128)(2,1)S(1)}, u32[]{:S(2)}, u32[]{:S(2)}) collective-permute-start(bf16[192,1024]{1,0:T(8,128)(2,1)} %get-tuple-element.31), channel_id=1, source_target_pairs={{0,2},{2,0},{4,6},{6,4},{1,3},{3,1},{5,7},{7,5},{8,10},{10,8},{12,... | collective-permute-start | bytes 1179656 | tf_op jit(solution)/shard_map/ppermute | solution.py:35
  7.9 2.6 %collective-permute-start.1 = (bf16[192,1024]{1,0:T(8,128)(2,1)}, bf16[192,1024]{1,0:T(8,128)(2,1)S(1)}, u32[]{:S(2)}, u32[]{:S(2)}) collective-permute-start(bf16[192,1024]{1,0:T(8,128)(2,1)} %get-tuple-element.32), channel_id=1, source_target_pairs={{0,4},{2,6},{4,0},{6,2},{1,5},{3,7},{5,1},{7,3},{8,12},{10,14},{12... | collective-permute-start | bytes 1179656 | tf_op jit(solution)/shard_map/ppermute | solution.py:35
  10.5 0.0 collective-permute-start.2
  10.5 4.2 %cut_drift.1 = (bf16[1024,384]{1,0:T(8,128)(2,1)}, bf16[1536,384]{1,0:T(8,128)(2,1)}, bf16[1536,384]{1,0:T(8,128)(2,1)}) custom-call(s32[6]{0:T(128)} %stack.79.refs_0_, bf16[1,1,2048,768]{3,2,1,0:T(8,128)(2,1)} %refs_1_.4), custom_call_target="tpu_custom_call" | custom-call | tf_op jit(solution)/shard_map/cut_drift/pallas_call | solution.py:272
  14.7 1.8 collective-permute-start.4
  16.5 1.5 collective-permute-start.5
  18.0 1.1 copy-done.2
  19.2 0.1 own_parts.1
  19.3 5.7 %collective-permute-done.refs_1_ = bf16[192,1024]{1,0:T(8,128)(2,1)S(1)} collective-permute-done((bf16[192,1024]{1,0:T(8,128)(2,1)}, bf16[192,1024]{1,0:T(8,128)(2,1)S(1)}, u32[]{:S(2)}, u32[]{:S(2)}) %collective-permute-start) | collective-permute-done | bytes 393248 | tf_op jit(solution)/shard_map/ppermute | solution.py:35
  24.9 13.0 %collective-permute-done.1.refs_2_ = bf16[192,1024]{1,0:T(8,128)(2,1)S(1)} collective-permute-done((bf16[192,1024]{1,0:T(8,128)(2,1)}, bf16[192,1024]{1,0:T(8,128)(2,1)S(1)}, u32[]{:S(2)}, u32[]{:S(2)}) %collective-permute-start.1) | collective-permute-done | bytes 393248 | tf_op jit(solution)/shard_map/ppermute | solution.py:35
  37.9 0.0 collective-permute-done.2.refs_3_
  37.9 0.1 gather_slots.1.refs_3_.refs_0_
  38.0 0.0 copy-start
  38.1 0.0 copy-start.4
  38.1 0.1 collective-permute-start.3
  38.1 4.0 %collective-permute-done.4.refs_2_ = bf16[1536,384]{1,0:T(8,128)(2,1)S(1)} collective-permute-done((bf16[1536,384]{1,0:T(8,128)(2,1)}, bf16[1536,384]{1,0:T(8,128)(2,1)S(1)}, u32[]{:S(2)}, u32[]{:S(2)}) %collective-permute-start.4) | collective-permute-done | bytes 1179680 | tf_op jit(solution)/shard_map/ppermute | solution.py:35
  42.2 1.2 collective-permute-done.5.refs_3_
  43.4 0.7 join_blocks.1
  44.1 1.3 collective-permute-start.8
  45.4 1.3 collective-permute-start.7
  46.7 2.4 %collective-permute-start.6 = (bf16[1024,384]{1,0:T(8,128)(2,1)S(1)}, bf16[1024,384]{1,0:T(8,128)(2,1)S(1)}, u32[]{:S(2)}, u32[]{:S(2)}) collective-permute-start(bf16[1024,384]{1,0:T(8,128)(2,1)S(1)} %get-tuple-element.39.refs_3_), channel_id=1, source_target_pairs={{0,8},{8,0},{17,25},{25,17},{2,10},{10,2},{19,27},{27,19},{4,12},{... | collective-permute-start | bytes 2359304 | tf_op jit(solution)/shard_map/ppermute | solution.py:322
  49.1 0.0 collective-permute-done.3.refs_4_
  49.1 5.4 %hidden_grads.1 = (bf16[2,384,384]{2,1,0:T(8,128)(2,1)S(1)}, f32[1,8,128]{2,1,0:T(8,128)S(1)}) custom-call(s32[6]{0:T(128)S(1)} %copy-done.4, bf16[1,1,2048,768]{3,2,1,0:T(8,128)(2,1)S(1)} %copy-done, bf16[1,1,768,2048]{3,2,1,0:T(8,128)(2,1)S(1)} %copy-done.1, bf16[768,1024]{1,0:T(8,128)(2,1)S(1)} %gather_slots.1.refs_3_.refs_0_, ...), custom_call_target="tpu_custom_call" | custom-call | tf_op jit(solution)/shard_map/hidden_grads/pallas_call | solution.py:337
  54.6 12.3 %collective-permute-done.8.refs_6_ = bf16[1024,384]{1,0:T(8,128)(2,1)S(1)} collective-permute-done((bf16[1024,384]{1,0:T(8,128)(2,1)S(1)}, bf16[1024,384]{1,0:T(8,128)(2,1)S(1)}, u32[]{:S(2)}, u32[]{:S(2)}) %collective-permute-start.8) | collective-permute-done | bytes 786464 | tf_op jit(solution)/shard_map/ppermute | solution.py:322
  66.9 0.5 collective-permute-done.7.refs_5_
  67.4 0.0 collective-permute-done.6.refs_4_
  67.4 1.0 hand_on.1
  68.4 1.5 collective-permute-start.9
  69.9 1.1 collective-permute-start.10
  71.0 0.0 collective-permute-start.11
  71.0 2.5 %collective-permute-start.12 = (bf16[384,384]{1,0:T(8,128)(2,1)S(1)}, bf16[384,384]{1,0:T(8,128)(2,1)S(1)}, u32[]{:S(2)}, u32[]{:S(2)}) collective-permute-start(bf16[384,384]{1,0:T(8,128)(2,1)S(1)} %get-tuple-element.48), channel_id=1, source_target_pairs={{0,24},{8,16},{16,8},{24,0},{1,25},{9,17},{17,9},{25,1},{2,26},{10... | collective-permute-start | bytes 884744 | tf_op jit(solution)/shard_map/ppermute | solution.py:35
  73.5 40.6 %all_gather.6.refs_1_ = f32[32,8,128]{2,1,0:T(8,128)S(1)} all-gather(f32[1,8,128]{2,1,0:T(8,128)S(1)} %get-tuple-element.42), channel_id=1, replica_groups=mesh['island'=4,'expert'=4,'tensor'=2] {'island','expert','tensor'}, dimensions={0}, use_global_device_ids=true | all-gather | bytes 135168 | tf_op jit(solution)/shard_map/all_gather | solution.py:365
  114.1 0.0 collective-permute-done.12.refs_8_
  114.1 0.0 collective-permute-done.10.refs_6_
  114.1 0.0 collective-permute-done.11.refs_7_
  114.1 0.0 collective-permute-done.9.refs_4_
  114.1 4.1 %average_block.1 = (f32[512,384]{1,0:T(8,128)S(1)}, f32[512,384]{1,0:T(8,128)S(1)}, f32[1,8,128]{2,1,0:T(8,128)S(1)}) custom-call(s32[6]{0:T(128)S(1)} %copy-done.4, f32[32,8,128]{2,1,0:T(8,128)S(1)} %all_gather.6.refs_1_, f32[1024,384]{1,0:T(8,128)S(1)} %get-tuple-element.43.refs_2_, bf16[4,1024,384]{2,1,0:T(8,128)(2,1)S(1)} %get-tuple-element.44.refs_3_, ...), custom_call_target="tpu_custom_call" | custom-call | tf_op jit(solution)/shard_map/average_block/pallas_call | solution.py:368
  118.2 0.8 convert_element_type.27
  119.0 2.1 %collective-permute-start.15 = (f16[512,384]{1,0:T(8,128)(2,1)}, f16[512,384]{1,0:T(8,128)(2,1)S(1)}, u32[]{:S(2)}, u32[]{:S(2)}) collective-permute-start(f16[512,384]{1,0:T(8,128)(2,1)} %convert_element_type.27), channel_id=1, source_target_pairs={{0,16},{8,24},{16,0},{24,8},{1,17},{9,25},{17,1},{25,9},{2,18},{10... | collective-permute-start | bytes 1179656 | tf_op jit(solution)/shard_map/ppermute | solution.py:35
  121.1 0.1 convert_element_type.25
  121.2 0.1 collective-permute-start.13
  121.2 2.0 %collective-permute-start.18 = (f16[512,384]{1,0:T(8,128)(2,1)}, f16[512,384]{1,0:T(8,128)(2,1)}, u32[]{:S(2)}, u32[]{:S(2)}) collective-permute-start(f16[512,384]{1,0:T(8,128)(2,1)} %convert_element_type.27), channel_id=1, source_target_pairs={{0,8},{8,0},{16,24},{24,16},{1,9},{9,1},{17,25},{25,17},{2,10},{10... | collective-permute-start | bytes 1179656 | tf_op jit(solution)/shard_map/ppermute | solution.py:35
  123.2 0.0 collective-permute-start.17
  123.2 7.9 %collective-permute-done.15 = f16[512,384]{1,0:T(8,128)(2,1)S(1)} collective-permute-done((f16[512,384]{1,0:T(8,128)(2,1)}, f16[512,384]{1,0:T(8,128)(2,1)S(1)}, u32[]{:S(2)}, u32[]{:S(2)}) %collective-permute-start.15) | collective-permute-done | bytes 393248 | tf_op jit(solution)/shard_map/ppermute | solution.py:35
  131.2 0.0 collective-permute-start.16
  131.2 2.0 %collective-permute-done.13 = f16[512,384]{1,0:T(8,128)(2,1)S(1)} collective-permute-done((f16[512,384]{1,0:T(8,128)(2,1)S(1)}, f16[512,384]{1,0:T(8,128)(2,1)S(1)}, u32[]{:S(2)}, u32[]{:S(2)}) %collective-permute-start.13) | collective-permute-done | bytes 393248 | tf_op jit(solution)/shard_map/ppermute | solution.py:35
  133.2 0.1 collective-permute-start.14
  133.3 0.1 stack.72.place
  133.3 37.0 %all_gather.7.notes = f32[32,8,128]{2,1,0:T(8,128)S(1)} all-gather(f32[1,8,128]{2,1,0:T(8,128)S(1)} %get-tuple-element.49), channel_id=1, replica_groups=mesh['island'=4,'expert'=4,'tensor'=2] {'island','expert','tensor'}, dimensions={0}, use_global_device_ids=true | all-gather | bytes 135168 | tf_op jit(solution)/shard_map/all_gather | solution.py:378
  170.3 0.1 convert_element_type.31.refs_4_
  170.4 1.0 convert_element_type.32.refs_5_
  171.3 0.0 collective-permute-done.18
  171.3 1.0 convert_element_type.30.refs_3_
  172.4 0.0 collective-permute-done.17
  172.4 1.0 convert_element_type.29.refs_2_
  173.4 5.5 %update_pieces.2 = (f32[1,2048,768]{2,1,0:T(8,128)}, bf16[1,2048,768]{2,1,0:T(8,128)(2,1)}) custom-call(s32[12]{0:T(128)S(1)} %stack.72.place, f32[32,8,128]{2,1,0:T(8,128)S(1)} %all_gather.7.notes, f32[1,2048,768]{2,1,0:T(8,128)} %momentum.3, f32[512,384]{1,0:T(8,128)S(1)} %get-tuple-element.50.refs_0_, f32[512,384]{1,0:T(8,128)S(1)} %get-tuple-element.51.refs_1_, ...), custom_call_target="tpu_custom_call" | custom-call | bytes 18874368 | tf_op jit(solution)/shard_map/update_pieces/pallas_call | solution.py:401
  178.9 0.0 collective-permute-done.16
  178.9 0.1 convert_element_type.28.refs_1_
  179.0 0.0 collective-permute-done.14
  179.0 0.1 convert_element_type.26.refs_0_
  179.0 3.2 %update_pieces.3 = (f32[1,2048,768]{2,1,0:T(8,128)}, bf16[1,2048,768]{2,1,0:T(8,128)(2,1)}) custom-call(s32[12]{0:T(128)S(1)} %stack.72.place, f32[32,8,128]{2,1,0:T(8,128)S(1)} %all_gather.7.notes, f32[1,2048,768]{2,1,0:T(8,128)} %momentum.3, f32[512,384]{1,0:T(8,128)S(1)} %convert_element_type.26.refs_0_, ...), custom_call_target="tpu_custom_call", output_to_operand_aliasing={{0}: (5, {}), {1}: (6, {})} | custom-call | bytes 4718592 | tf_op jit(solution)/shard_map/update_pieces/pallas_call | solution.py:401
  (6 shorter events, 0.0 us)
Async XLA Ops:
  4.8 13.2 %copy-start.3 = (bf16[192,1024]{1,0:T(8,128)(2,1)S(1)}, bf16[192,1024]{1,0:T(8,128)(2,1)}, u32[]{:S(2)}) copy-start(bf16[192,1024]{1,0:T(8,128)(2,1)} %get-tuple-element.28.slots) | copy-start | bytes 1179652
  4.8 20.1 %collective-permute-start = (bf16[192,1024]{1,0:T(8,128)(2,1)}, bf16[192,1024]{1,0:T(8,128)(2,1)S(1)}, u32[]{:S(2)}, u32[]{:S(2)}) collective-permute-start(bf16[192,1024]{1,0:T(8,128)(2,1)} %get-tuple-element.31), channel_id=1, source_target_pairs={{0,2},{2,0},{4,6},{6,4},{1,3},{3,1},{5,7},{7,5},{8,10},{10,8},{12,... | collective-permute-start | bytes 1179656 | tf_op jit(solution)/shard_map/ppermute | solution.py:35
  7.9 30.0 %collective-permute-start.1 = (bf16[192,1024]{1,0:T(8,128)(2,1)}, bf16[192,1024]{1,0:T(8,128)(2,1)S(1)}, u32[]{:S(2)}, u32[]{:S(2)}) collective-permute-start(bf16[192,1024]{1,0:T(8,128)(2,1)} %get-tuple-element.32), channel_id=1, source_target_pairs={{0,4},{2,6},{4,0},{6,2},{1,5},{3,7},{5,1},{7,3},{8,12},{10,14},{12... | collective-permute-start | bytes 1179656 | tf_op jit(solution)/shard_map/ppermute | solution.py:35
  10.5 27.4 %collective-permute-start.2 = (bf16[192,1024]{1,0:T(8,128)(2,1)}, bf16[192,1024]{1,0:T(8,128)(2,1)S(1)}, u32[]{:S(2)}, u32[]{:S(2)}) collective-permute-start(bf16[192,1024]{1,0:T(8,128)(2,1)} %get-tuple-element.33), channel_id=1, source_target_pairs={{0,6},{2,4},{4,2},{6,0},{1,7},{3,5},{5,3},{7,1},{8,14},{10,12},{12... | collective-permute-start | bytes 1179656 | tf_op jit(solution)/shard_map/ppermute | solution.py:35
  14.7 27.4 %collective-permute-start.4 = (bf16[1536,384]{1,0:T(8,128)(2,1)}, bf16[1536,384]{1,0:T(8,128)(2,1)S(1)}, u32[]{:S(2)}, u32[]{:S(2)}) collective-permute-start(bf16[1536,384]{1,0:T(8,128)(2,1)} %get-tuple-element.37), channel_id=1, source_target_pairs={{0,8},{8,0},{16,24},{24,16},{1,9},{9,1},{17,25},{25,17},{2,10},{10... | collective-permute-start | bytes 3538952 | tf_op jit(solution)/shard_map/ppermute | solution.py:35
  16.5 26.9 %collective-permute-start.5 = (bf16[1536,384]{1,0:T(8,128)(2,1)}, bf16[1536,384]{1,0:T(8,128)(2,1)S(1)}, u32[]{:S(2)}, u32[]{:S(2)}) collective-permute-start(bf16[1536,384]{1,0:T(8,128)(2,1)} %get-tuple-element.38), channel_id=1, source_target_pairs={{0,16},{8,24},{16,0},{24,8},{1,17},{9,25},{17,1},{25,9},{2,18},{10... | collective-permute-start | bytes 3538952 | tf_op jit(solution)/shard_map/ppermute | solution.py:35
  18.0 1.1 copy-start.2
  37.9 11.2 %copy-start.1 = (bf16[1,1,768,2048]{3,2,1,0:T(8,128)(2,1)S(1)}, bf16[1,1,768,2048]{3,2,1,0:T(8,128)(2,1)}, u32[]{:S(2)}) copy-start(bf16[1,1,768,2048]{3,2,1,0:T(8,128)(2,1)} %refs_2_.3) | copy-start | bytes 9437188
  38.0 11.1 %copy-start = (bf16[1,1,2048,768]{3,2,1,0:T(8,128)(2,1)S(1)}, bf16[1,1,2048,768]{3,2,1,0:T(8,128)(2,1)}, u32[]{:S(2)}) copy-start(bf16[1,1,2048,768]{3,2,1,0:T(8,128)(2,1)} %refs_1_.5) | copy-start | bytes 9437188
  38.1 11.1 %copy-start.4 = (s32[6]{0:T(128)S(1)}, s32[6]{0:T(128)}, u32[]{:S(2)}) copy-start(s32[6]{0:T(128)} %stack.79.refs_0_) | copy-start | bytes 76
  38.1 11.0 %collective-permute-start.3 = (bf16[768,1024]{1,0:T(8,128)(2,1)S(1)}, bf16[768,1024]{1,0:T(8,128)(2,1)S(1)}, u32[]{:S(2)}, u32[]{:S(2)}) collective-permute-start(bf16[768,1024]{1,0:T(8,128)(2,1)S(1)} %gather_slots.1.refs_3_.refs_0_), channel_id=1, source_target_pairs={{0,1},{1,0},{2,3},{3,2},{4,5},{5,4},{6,7},{7,6},{8,9},{9,8},{10,11... | collective-permute-start | bytes 4718600 | tf_op jit(solution)/shard_map/ppermute | solution.py:35
  44.1 22.9 %collective-permute-start.8 = (bf16[1024,384]{1,0:T(8,128)(2,1)S(1)}, bf16[1024,384]{1,0:T(8,128)(2,1)S(1)}, u32[]{:S(2)}, u32[]{:S(2)}) collective-permute-start(bf16[1024,384]{1,0:T(8,128)(2,1)S(1)} %get-tuple-element.39.refs_3_), channel_id=1, source_target_pairs={{1,25},{9,17},{16,8},{24,0},{3,27},{11,19},{18,10},{26,2},{5,29},{... | collective-permute-start | bytes 2359304 | tf_op jit(solution)/shard_map/ppermute | solution.py:322
  45.4 22.1 %collective-permute-start.7 = (bf16[1024,384]{1,0:T(8,128)(2,1)S(1)}, bf16[1024,384]{1,0:T(8,128)(2,1)S(1)}, u32[]{:S(2)}, u32[]{:S(2)}) collective-permute-start(bf16[1024,384]{1,0:T(8,128)(2,1)S(1)} %get-tuple-element.39.refs_3_), channel_id=1, source_target_pairs={{1,17},{9,25},{16,0},{24,8},{3,19},{11,27},{18,2},{26,10},{5,21},{... | collective-permute-start | bytes 2359304 | tf_op jit(solution)/shard_map/ppermute | solution.py:322
  46.7 20.8 %collective-permute-start.6 = (bf16[1024,384]{1,0:T(8,128)(2,1)S(1)}, bf16[1024,384]{1,0:T(8,128)(2,1)S(1)}, u32[]{:S(2)}, u32[]{:S(2)}) collective-permute-start(bf16[1024,384]{1,0:T(8,128)(2,1)S(1)} %get-tuple-element.39.refs_3_), channel_id=1, source_target_pairs={{0,8},{8,0},{17,25},{25,17},{2,10},{10,2},{19,27},{27,19},{4,12},{... | collective-permute-start | bytes 2359304 | tf_op jit(solution)/shard_map/ppermute | solution.py:322
  68.4 45.7 %collective-permute-start.9 = (bf16[4,1024,384]{2,1,0:T(8,128)(2,1)S(1)}, bf16[4,1024,384]{2,1,0:T(8,128)(2,1)S(1)}, u32[]{:S(2)}, u32[]{:S(2)}) collective-permute-start(bf16[4,1024,384]{2,1,0:T(8,128)(2,1)S(1)} %get-tuple-element.44.refs_3_), channel_id=1, source_target_pairs={{0,1},{8,9},{17,16},{25,24},{2,3},{10,11},{19,18},{27,26},{4,5},{1... | collective-permute-start | bytes 9437192 | tf_op jit(solution)/shard_map/ppermute | solution.py:331
  69.9 44.2 %collective-permute-start.10 = (bf16[896,384]{1,0:T(8,128)(2,1)S(1)}, bf16[896,384]{1,0:T(8,128)(2,1)S(1)}, u32[]{:S(2)}, u32[]{:S(2)}) collective-permute-start(bf16[896,384]{1,0:T(8,128)(2,1)S(1)} %get-tuple-element.46), channel_id=1, source_target_pairs={{0,8},{8,0},{16,24},{24,16},{1,9},{9,1},{17,25},{25,17},{2,10},{10... | collective-permute-start | bytes 2064392 | tf_op jit(solution)/shard_map/ppermute | solution.py:35
  71.0 43.1 %collective-permute-start.11 = (bf16[896,384]{1,0:T(8,128)(2,1)S(1)}, bf16[896,384]{1,0:T(8,128)(2,1)S(1)}, u32[]{:S(2)}, u32[]{:S(2)}) collective-permute-start(bf16[896,384]{1,0:T(8,128)(2,1)S(1)} %get-tuple-element.47), channel_id=1, source_target_pairs={{0,16},{8,24},{16,0},{24,8},{1,17},{9,25},{17,1},{25,9},{2,18},{10... | collective-permute-start | bytes 2064392 | tf_op jit(solution)/shard_map/ppermute | solution.py:35
  71.0 43.1 %collective-permute-start.12 = (bf16[384,384]{1,0:T(8,128)(2,1)S(1)}, bf16[384,384]{1,0:T(8,128)(2,1)S(1)}, u32[]{:S(2)}, u32[]{:S(2)}) collective-permute-start(bf16[384,384]{1,0:T(8,128)(2,1)S(1)} %get-tuple-element.48), channel_id=1, source_target_pairs={{0,24},{8,16},{16,8},{24,0},{1,25},{9,17},{17,9},{25,1},{2,26},{10... | collective-permute-start | bytes 884744 | tf_op jit(solution)/shard_map/ppermute | solution.py:35
  119.0 12.1 %collective-permute-start.15 = (f16[512,384]{1,0:T(8,128)(2,1)}, f16[512,384]{1,0:T(8,128)(2,1)S(1)}, u32[]{:S(2)}, u32[]{:S(2)}) collective-permute-start(f16[512,384]{1,0:T(8,128)(2,1)} %convert_element_type.27), channel_id=1, source_target_pairs={{0,16},{8,24},{16,0},{24,8},{1,17},{9,25},{17,1},{25,9},{2,18},{10... | collective-permute-start | bytes 1179656 | tf_op jit(solution)/shard_map/ppermute | solution.py:35
  121.2 12.0 %collective-permute-start.13 = (f16[512,384]{1,0:T(8,128)(2,1)S(1)}, f16[512,384]{1,0:T(8,128)(2,1)S(1)}, u32[]{:S(2)}, u32[]{:S(2)}) collective-permute-start(f16[512,384]{1,0:T(8,128)(2,1)S(1)} %convert_element_type.25), channel_id=1, source_target_pairs={{0,8},{8,0},{16,24},{24,16},{1,9},{9,1},{17,25},{25,17},{2,10},{10... | collective-permute-start | bytes 1179656 | tf_op jit(solution)/shard_map/ppermute | solution.py:35
  121.2 50.1 %collective-permute-start.18 = (f16[512,384]{1,0:T(8,128)(2,1)}, f16[512,384]{1,0:T(8,128)(2,1)}, u32[]{:S(2)}, u32[]{:S(2)}) collective-permute-start(f16[512,384]{1,0:T(8,128)(2,1)} %convert_element_type.27), channel_id=1, source_target_pairs={{0,8},{8,0},{16,24},{24,16},{1,9},{9,1},{17,25},{25,17},{2,10},{10... | collective-permute-start | bytes 1179656 | tf_op jit(solution)/shard_map/ppermute | solution.py:35
  123.2 49.1 %collective-permute-start.17 = (f16[512,384]{1,0:T(8,128)(2,1)S(1)}, f16[512,384]{1,0:T(8,128)(2,1)}, u32[]{:S(2)}, u32[]{:S(2)}) collective-permute-start(f16[512,384]{1,0:T(8,128)(2,1)S(1)} %convert_element_type.25), channel_id=1, source_target_pairs={{0,16},{8,24},{16,0},{24,8},{1,17},{9,25},{17,1},{25,9},{2,18},{10... | collective-permute-start | bytes 1179656 | tf_op jit(solution)/shard_map/ppermute | solution.py:35
  131.2 47.7 %collective-permute-start.16 = (f16[512,384]{1,0:T(8,128)(2,1)S(1)}, f16[512,384]{1,0:T(8,128)(2,1)S(1)}, u32[]{:S(2)}, u32[]{:S(2)}) collective-permute-start(f16[512,384]{1,0:T(8,128)(2,1)S(1)} %collective-permute-done.15), channel_id=1, source_target_pairs={{0,8},{8,0},{16,24},{24,16},{1,9},{9,1},{17,25},{25,17},{2,10},{10... | collective-permute-start | bytes 1179656 | tf_op jit(solution)/shard_map/ppermute | solution.py:35
  133.2 45.8 %collective-permute-start.14 = (f16[512,384]{1,0:T(8,128)(2,1)S(1)}, f16[512,384]{1,0:T(8,128)(2,1)S(1)}, u32[]{:S(2)}, u32[]{:S(2)}) collective-permute-start(f16[512,384]{1,0:T(8,128)(2,1)S(1)} %collective-permute-done.13), channel_id=1, source_target_pairs={{0,16},{8,24},{16,0},{24,8},{1,17},{9,25},{17,1},{25,9},{2,18},{10... | collective-permute-start | bytes 1179656 | tf_op jit(solution)/shard_map/ppermute | solution.py:35

commit v10 on v8

--- a/solution.py
+++ b/solution.py
@@ -105,10 +105,11 @@
     drift_sum[...] = added
 
 
-def hidden_kernel(parts, across, spot, gate, down, *refs):
-    joined, out, norms = refs[:parts], refs[parts], refs[-1]
-    rows, half = joined[0].shape[0] // 2, joined[0].shape[1]
-    columns = out.shape[2]
+def hidden_kernel(parts, islands, tails, spot, gate, down, *refs):
+    joined, relays = refs[:parts], refs[parts : parts + len(tails)]
+    *messages, norms, hidden = refs[parts + len(tails) :]
+    across, slots, columns = hidden.shape
+    half = joined[0].shape[1]
     starts = [pl.multiple_of(origin(spot[1], t, parts) * half, half) for t in range(parts)]
     hidden_gram = 0.0
     for r in range(across):
@@ -117,24 +118,29 @@
         back = 0.0
         for t in range(parts):
             block = gate[0, 0, pl.ds(starts[t], half), first : first + columns]
-            value = value + dot(joined[t][:rows, :], block, ((1,), (0,)))
+            value = value + dot(joined[t][:slots, :], block, ((1,), (0,)))
             block = down[0, 0, first : first + columns, pl.ds(starts[t], half)]
-            back = back + dot(joined[t][rows:, :], block, ((1,), (1,)))
+            back = back + dot(joined[t][slots:, :], block, ((1,), (1,)))
         rounded = (back * (value / (1.0 + jnp.exp(-value)))).astype(BF16)
-        out[r] = rounded
+        hidden[r] = rounded
         hidden_gram = hidden_gram + dot(rounded, rounded, ((1,), (1,)))
+    for d, message in enumerate(messages):
+        block = lax.rem(partner(spot[3], d, islands), across)
+        message[:slots, :] = hidden[pl.ds(block, 1)][0]
+        if d in tails:
+            message[slots:, :] = relays[tails.index(d)][...]
     input_gram = 0.0
     for t in range(parts):
-        features = joined[t][:rows, :]
+        features = joined[t][:slots, :]
         input_gram = input_gram + dot(features, features, ((1,), (1,)))
     norms[...] = jnp.full(norms.shape, jnp.sum(hidden_gram * input_gram), F32)
 
 
-def average_kernel(islands, entries, tiles, spot, norms, drift_sum, own, moved, *refs):
-    messages = refs[:islands]
-    *halves, notes, total, square = refs[islands:]
+def average_kernel(islands, entries, tiles, count, spot, norms, drift_sum, *refs):
+    features, messages = refs[:count], refs[count : count + islands]
+    *halves, notes, total, square = refs[count + islands :]
     rows = total.shape[0] // tiles
-    slots = own.shape[2]
+    slots = features[0].shape[1]
     group = norms.shape[0] // islands
     scales = []
     for d in range(islands):
@@ -143,7 +149,7 @@
         scales.append(jnp.minimum(1.0, math.sqrt(entries) / jnp.sqrt(norm + 1e-06)) / islands)
     handed = [m for m in messages[:0:-1] if m.shape[0] > slots]
 
-    def compute(features):
+    def compute(blocks):
         squares = 0.0
         for m in range(tiles):
             part = slice(m * rows, (m + 1) * rows)
@@ -155,14 +161,20 @@
                 average = average + handed[n][first : first + rows, :].astype(F32)
             average = average * (1.0 / islands)
             for d in range(islands):
-                factor = messages[d][:slots, :]
-                average = average + scales[d] * dot(features[d, part, :], factor, ((1,), (0,)))
+                size = total.shape[0] // len(blocks[d])
+                n, first = divmod(m * rows, size)
+                block = blocks[d][n][first : first + rows, :]
+                average = average + scales[d] * dot(block, messages[d][:slots, :], ((1,), (0,)))
             total[part, :] = average
             squares = squares + jnp.sum(average * average, axis=0, keepdims=True)
         square[...] = squares
 
-    pl.when(spot[5] == 1)(lambda: compute(own))
-    pl.when(spot[5] != 1)(lambda: compute(moved))
+    if count == islands:
+        compute([[ref] for ref in features])
+    else:
+        turned, first, second, other, *others = features
+        pl.when(spot[5] == 1)(lambda: compute([[turned], [first], [other], others]))
+        pl.when(spot[5] != 1)(lambda: compute([[other], others, [first], [second]]))
     peak = jnp.max(jnp.abs(total[...]))
     unit = jnp.maximum(peak, 1e-30) / 32768
     for n, half in enumerate(halves):
@@ -175,18 +187,15 @@
     notes[...] = jnp.where(sublane == 0, jnp.sum(square[...]), unit)
 
 
-def hand_kernel(islands, tails, spot, norms, hidden, *refs):
-    features, relays = refs[:islands], refs[islands : islands + len(tails)]
-    joined, passed, *messages = refs[islands + len(tails) :]
-    across, slots, _ = hidden.shape
-    for n in range(islands):
-        joined[n] = features[n][...]
+def choose_kernel(spot, one, other, out):
+    out[...] = jnp.where(spot[5] == 1, one[...], other[...])
+
+
+def choose_halves_kernel(spot, norms, one, other, earlier, top, bottom, passed):
+    size = top.shape[0]
+    top[...] = jnp.where(spot[5] == 1, one[:size, :], other[:size, :])
+    bottom[...] = jnp.where(spot[5] == 1, one[size:, :], other[size:, :])
     passed[...] = norms[...]
-    for d, message in enumerate(messages):
-        block = lax.rem(partner(spot[3], d, islands), across)
-        message[:slots, :] = hidden[pl.ds(block, 1)][0]
-        if d in tails:
-            message[slots:, :] = relays[tails.index(d)][...]
 
 
 def own_kernel(slots, block, slots_out, block_out):
@@ -315,67 +324,67 @@
 
     joined_all = [joined] + [swap(joined, "tensor", t) for t in range(1, parts)]
 
-    def send_features(d):
-        pairs = []
+    tails = [2, 1] if handed else []
+    message_rows = [routed_rows + (half - handed if d in tails else 0) for d in range(islands)]
+    *messages, norms = pl.pallas_call(
+        lambda *refs: hidden_kernel(parts, islands, tails, *refs),
+        in_specs=[SMEM] + [VMEM] * (2 + parts + len(tails)),
+        out_specs=[VMEM] * (islands + 1),
+        out_shape=[jax.ShapeDtypeStruct((rows, columns), BF16) for rows in message_rows]
+        + [jax.ShapeDtypeStruct((devices, 8, 128), F32)],
+        scratch_shapes=[pltpu.VMEM((across, routed_rows, columns), BF16)],
+        compiler_params=params(18 + routed_rows // 48),
+        name="hidden_grads",
+    )(spot, gate_weight, down_weight, *joined_all, *relays)
+    messages_in = [messages[0]] + [swap(messages[d], "island", d) for d in range(1, islands)]
+
+    if handed and parts == 2:
+        pairs, onward = [], []
         for at in range(islands):
-            to = partner(at, d, islands)
-            pairs.append((at * parts + to // across, to * parts + to // across))
-        return lax.ppermute(turned, ("island", "tensor"), pairs)
-
-    def spread(value):
-        result = value
-        for t in range(1, parts):
-            pairs = []
-            for at in range(islands):
-                keep = at // across
-                pairs.append((at * parts + keep, at * parts + partner(keep, t, parts)))
-            moved = lax.ppermute(value, ("island", "tensor"), pairs)
-            result = moved if t == 1 else result + moved
-        return result
-
-    features_in = [send_features(d) for d in range(1, islands)]
-
-    hidden_out, norms = pl.pallas_call(
-        lambda *refs: hidden_kernel(parts, across, *refs),
-        in_specs=[SMEM] + [VMEM] * (2 + parts),
-        out_specs=[VMEM] * 2,
-        out_shape=[
-            jax.ShapeDtypeStruct((across, routed_rows, columns), BF16),
-            jax.ShapeDtypeStruct((devices, 8, 128), F32),
-        ],
-        compiler_params=params(16 + routed_rows // 48),
-        name="hidden_grads",
-    )(spot, gate_weight, down_weight, *joined_all)
-    tails = [2, 1] if handed else []
-    message_rows = [
-        routed_rows + (half - handed if d in tails else 0) for d in range(islands)
-    ]
-    features_in, norms, *messages = pl.pallas_call(
-        lambda *refs: hand_kernel(islands, tails, *refs),
-        in_specs=[SMEM] + [VMEM] * (2 + islands + len(relays)),
-        out_specs=[VMEM] * (2 + islands),
-        out_shape=[
-            jax.ShapeDtypeStruct((islands, half, routed_rows), BF16),
-            jax.ShapeDtypeStruct(norms.shape, F32),
-        ]
-        + [jax.ShapeDtypeStruct((rows, columns), BF16) for rows in message_rows],
-        compiler_params=params(6 + routed_rows // 48),
-        name="hand_on",
-    )(spot, norms, hidden_out, turned, *features_in, *relays)
-    features_moved = spread(features_in)
+            keep = at // across
+            pairs += [
+                (at * parts + keep, (at ^ 1) * parts + keep),
+                (at * parts + 1 - keep, (at ^ 2) * parts + keep),
+            ]
+            onward.append((at * parts + 1 - keep, (at ^ 1) * parts + 1 - keep))
+        first = lax.ppermute(turned, ("island", "tensor"), pairs)
+        second = lax.ppermute(first, ("island", "tensor"), onward)
+        block = jax.ShapeDtypeStruct((half, routed_rows), BF16)
+        part_block = jax.ShapeDtypeStruct((half // 2, routed_rows), BF16)
+        chosen = pl.pallas_call(
+            choose_kernel,
+            in_specs=[SMEM] + [VMEM] * 2,
+            out_specs=VMEM,
+            out_shape=block,
+            compiler_params=params(4 + routed_rows // 48),
+            name="choose_features",
+        )(spot, turned, first)
+        moved = swap(chosen, "tensor", 1)
+        *chosen_halves, norms = pl.pallas_call(
+            choose_halves_kernel,
+            in_specs=[SMEM] + [VMEM] * 3 + [ANY],
+            out_specs=[VMEM] * 3,
+            out_shape=[part_block] * 2 + [jax.ShapeDtypeStruct(norms.shape, F32)],
+            compiler_params=params(4 + routed_rows // 48),
+            name="choose_halves",
+        )(spot, norms, first, second, moved)
+        features_of = [turned, first, second, moved]
+        features_of += [swap(v, "tensor", 1) for v in chosen_halves]
+    else:
+        every = lax.all_gather(turned, ("island", "tensor"))
+        features_of = [every[origin(island, d, islands) * parts + holder] for d in range(islands)]
     norms = lax.all_to_all(norms, AXES, split_axis=0, concat_axis=0, tiled=True)
-    messages_in = [messages[0]] + [swap(messages[d], "island", d) for d in range(1, islands)]
 
     *halves, notes = pl.pallas_call(
-        lambda *refs: average_kernel(islands, entries, 2, *refs),
-        in_specs=[SMEM] + [VMEM] * (4 + islands),
+        lambda *refs: average_kernel(islands, entries, 2, len(features_of), *refs),
+        in_specs=[SMEM] + [VMEM] * (2 + len(features_of) + islands),
         out_specs=[VMEM] * 3,
         out_shape=[jax.ShapeDtypeStruct((half // 2, columns), F32)] * 2
         + [jax.ShapeDtypeStruct((devices, 8, 128), F32)],
         scratch_shapes=[pltpu.VMEM((half, columns), F32), pltpu.VMEM((1, columns), F32)],
         compiler_params=params(8 + routed_rows // 48),
         name="average_block",
-    )(spot, norms, drift_sum, features_in, features_moved, *messages_in)
+    )(spot, norms, drift_sum, *features_of, *messages_in)
     notes = lax.all_to_all(notes, AXES, split_axis=0, concat_axis=0, tiled=True)
 
     parted = half // 2

time: 144 us -> 157 us (1.090)
  the two profiles are of different devices: /device:TPU:0 before, /device:TPU:21 now
where the time goes in v10:
time: 157 us; the launch traced here: 156 us
  waiting for transfers between devices  67.3 us (43%)
  starting transfers between devices  33.7 us (21%)
  Pallas kernels  31.8 us (20%)
  local copies, waits for them, and re-layouts  13.5 us (9%)
  other arithmetic  8.92 us (6%)
    ppermute x18, waiting for transfers between devices, swap(): lax.ppermute(value, axis, [(at, partner(at, step, size)) for at in range(...  49.8 us
    ppermute x18, starting transfers between devices, swap(): lax.ppermute(value, axis, [(at, partner(at, step, size)) for at in range(...  22.5 us
    unnamed x36, local copies, waits for them, and re-layouts  12.7 us
    ppermute x1, waiting for transfers between devices, body(): first = lax.ppermute(turned, ('island', 'tensor'), pairs)  10.8 us
    pallas_call x2, Pallas kernels, body(): pl.pallas_call(functools.partial(update_kernel, entries, list(values)), i...  8.69 us
    convert_element_type x6, other arithmetic, body(): v.astype(F32)  8.07 us
    pallas_call x1, Pallas kernels, body(): pl.pallas_call(lambda *refs: hidden_kernel(parts, islands, tails, *refs),...  6.71 us
    all_to_all x1, waiting for transfers between devices, body(): notes = lax.all_to_all(notes, AXES, split_axis=0, concat_axis=0, tiled=True)  6.71 us
  transfers between devices with their start and end apart: 22, of which 7 were waited for; matrix products, arithmetic and copies ran while one was open for 5% of the time, Pallas kernels for 12%

profile of v10, /device:TPU:21, one launch (start us, length us, event | category | flops | bytes accessed | tf_op | source)
XLA Modules:
  0.0 156.4 jit_solution(6168014693179345870)
XLA Ops:
  0.7 0.7 stack.79.refs_0_.spot
  1.3 4.2 %cut_drift.1 = (bf16[1024,384]{1,0:T(8,128)(2,1)}, bf16[1536,384]{1,0:T(8,128)(2,1)}, bf16[1536,384]{1,0:T(8,128)(2,1)}) custom-call(s32[6]{0:T(128)} %stack.79.refs_0_.spot, bf16[1,1,2048,768]{3,2,1,0:T(8,128)(2,1)} %refs_1_.4), custom_call_target="tpu_custom_call" | custom-call | tf_op jit(solution)/shard_map/cut_drift/pallas_call | solution.py:282
  5.6 1.3 collective-permute-start.4
  6.8 0.2 collective-permute-start.5
  7.1 3.6 %pick_slots.1 = (bf16[192,1024]{1,0:T(8,128)(2,1)}, bf16[192,1024]{1,0:T(8,128)(2,1)}, bf16[192,1024]{1,0:T(8,128)(2,1)}, bf16[192,1024]{1,0:T(8,128)(2,1)}) custom-call(s32[6]{0:T(128)} %stack.79.refs_0_.spot, s32[1,1,4,96]{3,2,1,0:T(4,128)} %refs_1_.3, s32[1,1,4]{2,1,0:T(1,128)} %refs_2_.2, f32[1,1,4,96]{3,2,1,0:T(4,128)} %refs_3_.1, ...), custom_call_target="tpu_custom_call" | custom-call | tf_op jit(solution)/shard_map/pick_slots/pallas_call | solution.py:266
  10.6 1.4 collective-permute-start
  12.0 0.1 collective-permute-start.1
  12.0 1.3 collective-permute-start.2
  13.3 1.1 copy-done.9
  14.5 1.0 copy-done.14
  15.5 0.1 own_parts.1
  15.6 11.2 %collective-permute-done.refs_1_ = bf16[192,1024]{1,0:T(8,128)(2,1)S(1)} collective-permute-done((bf16[192,1024]{1,0:T(8,128)(2,1)}, bf16[192,1024]{1,0:T(8,128)(2,1)S(1)}, u32[]{:S(2)}, u32[]{:S(2)}) %collective-permute-start) | collective-permute-done | bytes 393248 | tf_op jit(solution)/shard_map/ppermute | solution.py:35
  26.8 1.8 %collective-permute-done.1.refs_2_ = bf16[192,1024]{1,0:T(8,128)(2,1)S(1)} collective-permute-done((bf16[192,1024]{1,0:T(8,128)(2,1)}, bf16[192,1024]{1,0:T(8,128)(2,1)S(1)}, u32[]{:S(2)}, u32[]{:S(2)}) %collective-permute-start.1) | collective-permute-done | bytes 393248 | tf_op jit(solution)/shard_map/ppermute | solution.py:35
  28.6 17.9 %collective-permute-done.2.refs_3_ = bf16[192,1024]{1,0:T(8,128)(2,1)S(1)} collective-permute-done((bf16[192,1024]{1,0:T(8,128)(2,1)}, bf16[192,1024]{1,0:T(8,128)(2,1)S(1)}, u32[]{:S(2)}, u32[]{:S(2)}) %collective-permute-start.2) | collective-permute-done | bytes 393248 | tf_op jit(solution)/shard_map/ppermute | solution.py:35
  46.5 0.1 gather_slots.1.refs_0_.refs_3_
  46.7 2.5 %collective-permute-start.3 = (bf16[768,1024]{1,0:T(8,128)(2,1)S(1)}, bf16[768,1024]{1,0:T(8,128)(2,1)S(1)}, u32[]{:S(2)}, u32[]{:S(2)}) collective-permute-start(bf16[768,1024]{1,0:T(8,128)(2,1)S(1)} %gather_slots.1.refs_0_.refs_3_), channel_id=1, source_target_pairs={{0,1},{1,0},{2,3},{3,2},{4,5},{5,4},{6,7},{7,6},{8,9},{9,8},{10,11... | collective-permute-start | bytes 4718600 | tf_op jit(solution)/shard_map/ppermute | solution.py:35
  49.1 0.0 copy-start.6
  49.1 0.7 join_blocks.1
  49.8 0.0 copy-start.7
  49.9 0.3 collective-permute-start.6
  50.2 10.8 %collective-permute-done.6.other.one.refs_4_ = bf16[1024,384]{1,0:T(8,128)(2,1)S(1)} collective-permute-done((bf16[1024,384]{1,0:T(8,128)(2,1)S(1)}, bf16[1024,384]{1,0:T(8,128)(2,1)S(1)}, u32[]{:S(2)}, u32[]{:S(2)}) %collective-permute-start.6) | collective-permute-done | bytes 786464 | tf_op jit(solution)/shard_map/ppermute | solution.py:350
  61.0 0.6 choose_features.1
  61.6 0.5 collective-permute-start.8
  62.1 0.7 collective-permute-start.7
  62.8 6.7 %hidden_grads.1 = (bf16[384,384]{1,0:T(8,128)(2,1)S(1)}, bf16[896,384]{1,0:T(8,128)(2,1)}, bf16[896,384]{1,0:T(8,128)(2,1)}, bf16[384,384]{1,0:T(8,128)(2,1)}, f32[32,8,128]{2,1,0:T(8,128)S(1)}) custom-call(s32[6]{0:T(128)S(1)} %copy-done.17, bf16[1,1,2048,768]{3,2,1,0:T(8,128)(2,1)S(1)} %copy-done.5, bf16[1,1,768,2048]{3,2,1,0:T(8,128)(2,1)S(1)} %copy-done.6, ...), custom_call_target="tpu_custom_call" | custom-call | tf_op jit(solution)/shard_map/hidden_grads/pallas_call | solution.py:329
  69.6 0.3 collective-permute-start.11
  69.8 4.2 %collective-permute-start.12 = (bf16[896,384]{1,0:T(8,128)(2,1)}, bf16[896,384]{1,0:T(8,128)(2,1)S(1)}, u32[]{:S(2)}, u32[]{:S(2)}) collective-permute-start(bf16[896,384]{1,0:T(8,128)(2,1)} %get-tuple-element.47), channel_id=1, source_target_pairs={{0,16},{8,24},{16,0},{24,8},{1,17},{9,25},{17,1},{25,9},{2,18},{10... | collective-permute-start | bytes 2064392 | tf_op jit(solution)/shard_map/ppermute | solution.py:35
  74.0 1.7 %choose_halves.1 = (bf16[512,384]{1,0:T(8,128)(2,1)}, bf16[512,384]{1,0:T(8,128)(2,1)}, f32[32,8,128]{2,1,0:T(8,128)}) custom-call(s32[6]{0:T(128)S(1)} %copy-done.17, f32[32,8,128]{2,1,0:T(8,128)S(1)} %get-tuple-element.39.norms, bf16[1024,384]{1,0:T(8,128)(2,1)S(1)} %collective-permute-done.6.other.one.refs_4_, ...), custom_call_target="tpu_custom_call" | custom-call | tf_op jit(solution)/shard_map/choose_halves/pallas_call | solution.py:363
  75.7 0.9 copy-done.1
  76.6 5.2 %collective-permute-start.9 = (bf16[512,384]{1,0:T(8,128)(2,1)}, bf16[512,384]{1,0:T(8,128)(2,1)}, u32[]{:S(2)}, u32[]{:S(2)}) collective-permute-start(bf16[512,384]{1,0:T(8,128)(2,1)} %get-tuple-element.43), channel_id=1, source_target_pairs={{0,1},{1,0},{2,3},{3,2},{4,5},{5,4},{6,7},{7,6},{8,9},{9,8},{10,11... | collective-permute-start | bytes 1179656 | tf_op jit(solution)/shard_map/ppermute | solution.py:35
  81.8 0.0 collective-permute-start.10
  81.8 0.2 collective-permute-start.13
  82.0 5.4 %all-to-all-start = ((f32[32,8,128]{2,1,0:T(8,128)}), f32[32,8,128]{2,1,0:T(8,128)S(1)}, u32[]{:S(2)}, u32[]{:S(2)}) async-start(f32[32,8,128]{2,1,0:T(8,128)} %get-tuple-element.41), calls=%async_computation | async-start | bytes 262144 | tf_op jit(solution)/shard_map/all_to_all | solution.py:376
  87.4 11.4 %collective-permute-done.13.refs_12_ = bf16[384,384]{1,0:T(8,128)(2,1)} collective-permute-done((bf16[384,384]{1,0:T(8,128)(2,1)}, bf16[384,384]{1,0:T(8,128)(2,1)}, u32[]{:S(2)}, u32[]{:S(2)}) %collective-permute-start.13) | collective-permute-done | bytes 294944 | tf_op jit(solution)/shard_map/ppermute | solution.py:35
  98.7 0.8 copy-done.10
  99.6 0.8 copy-done.12
  100.5 1.1 copy-done.2
  101.6 1.1 copy-done.4
  102.7 1.4 copy-done.8
  104.1 1.1 copy-done.11
  105.2 1.1 copy-done.13
  106.3 1.0 copy-done.16
  107.3 5.4 %average_block.1 = (f32[512,384]{1,0:T(8,128)S(1)}, f32[512,384]{1,0:T(8,128)S(1)}, f32[32,8,128]{2,1,0:T(8,128)}) custom-call(s32[6]{0:T(128)S(1)} %copy-done.17, f32[32,8,128]{2,1,0:T(8,128)S(1)} %all-to-all-done.refs_1_, f32[1024,384]{1,0:T(8,128)S(1)} %copy-done.8, bf16[1024,384]{1,0:T(8,128)(2,1)S(1)} %get-tuple-element.40.one.refs_3_, ...), custom_call_target="tpu_custom_call" | custom-call | tf_op jit(solution)/shard_map/average_block/pallas_call | solution.py:378
  112.7 0.1 convert_element_type.27
  112.7 0.1 collective-permute-start.16
  112.8 0.8 convert_element_type.25
  113.6 0.3 collective-permute-start.14
  113.9 1.2 collective-permute-start.19
  115.1 1.5 collective-permute-start.18
  116.5 7.4 %collective-permute-done.16 = f16[512,384]{1,0:T(8,128)(2,1)} collective-permute-done((f16[512,384]{1,0:T(8,128)(2,1)S(1)}, f16[512,384]{1,0:T(8,128)(2,1)}, u32[]{:S(2)}, u32[]{:S(2)}) %collective-permute-start.16) | collective-permute-done | bytes 393248 | tf_op jit(solution)/shard_map/ppermute | solution.py:35
  123.9 0.3 collective-permute-start.17
  124.2 2.3 %collective-permute-start.15 = (f16[512,384]{1,0:T(8,128)(2,1)}, f16[512,384]{1,0:T(8,128)(2,1)}, u32[]{:S(2)}, u32[]{:S(2)}) collective-permute-start(f16[512,384]{1,0:T(8,128)(2,1)} %collective-permute-done.14), channel_id=1, source_target_pairs={{0,16},{8,24},{16,0},{24,8},{1,17},{9,25},{17,1},{25,9},{2,18},{10... | collective-permute-start | bytes 1179656 | tf_op jit(solution)/shard_map/ppermute | solution.py:35
  126.5 4.8 %all-to-all-start.1 = ((f32[32,8,128]{2,1,0:T(8,128)}), f32[32,8,128]{2,1,0:T(8,128)S(1)}, u32[]{:S(2)}, u32[]{:S(2)}) async-start(f32[32,8,128]{2,1,0:T(8,128)} %get-tuple-element.49), calls=%async_computation.1 | async-start | bytes 262144 | tf_op jit(solution)/shard_map/all_to_all | solution.py:388
  131.4 0.1 stack.72.place
  131.5 1.1 convert_element_type.31.refs_4_
  132.6 1.9 %convert_element_type.32.refs_5_ = f32[512,384]{1,0:T(8,128)} convert(f16[512,384]{1,0:T(8,128)(2,1)} %collective-permute-done.16) | non-fusion elementwise | flops 196608 | bytes 1179648 | tf_op jit(solution)/shard_map/convert_element_type | solution.py:431
  134.5 1.0 convert_element_type.30.refs_3_
  135.6 1.9 %convert_element_type.29.refs_2_ = f32[512,384]{1,0:T(8,128)} convert(f16[512,384]{1,0:T(8,128)(2,1)} %collective-permute-done.18) | non-fusion elementwise | flops 196608 | bytes 1179648 | tf_op jit(solution)/shard_map/convert_element_type | solution.py:431
  137.5 6.7 %all-to-all-done.1.notes = f32[32,8,128]{2,1,0:T(8,128)S(1)} async-done(((f32[32,8,128]{2,1,0:T(8,128)}), f32[32,8,128]{2,1,0:T(8,128)S(1)}, u32[]{:S(2)}, u32[]{:S(2)}) %all-to-all-start.1) | async-done | bytes 131104 | tf_op jit(solution)/shard_map/all_to_all | solution.py:388
  144.2 1.1 copy-done
  145.4 5.4 %update_pieces.2 = (f32[1,2048,768]{2,1,0:T(8,128)}, bf16[1,2048,768]{2,1,0:T(8,128)(2,1)}) custom-call(s32[12]{0:T(128)S(1)} %stack.72.place, f32[32,8,128]{2,1,0:T(8,128)S(1)} %all-to-all-done.1.notes, f32[1,2048,768]{2,1,0:T(8,128)} %momentum.3, f32[512,384]{1,0:T(8,128)S(1)} %get-tuple-element.50.refs_0_, f32[512,384]{1,0:T(8,128)S(1)} %get-tuple-element.51.refs_1_, ...), custom_call_target="tpu_custom_call" | custom-call | bytes 18874368 | tf_op jit(solution)/shard_map/update_pieces/pallas_call | solution.py:411
  150.8 1.0 convert_element_type.28.refs_1_
  151.9 1.0 convert_element_type.26.refs_0_
  152.9 3.2 %update_pieces.3 = (f32[1,2048,768]{2,1,0:T(8,128)}, bf16[1,2048,768]{2,1,0:T(8,128)(2,1)}) custom-call(s32[12]{0:T(128)S(1)} %stack.72.place, f32[32,8,128]{2,1,0:T(8,128)S(1)} %all-to-all-done.1.notes, f32[1,2048,768]{2,1,0:T(8,128)} %momentum.3, f32[512,384]{1,0:T(8,128)S(1)} %convert_element_type.26.refs_0_, ...), custom_call_target="tpu_custom_call", output_to_operand_aliasing={{0}: (5, {}), {1}: (6, {})} | custom-call | bytes 4718592 | tf_op jit(solution)/shard_map/update_pieces/pallas_call | solution.py:411
  (37 shorter events, 0.1 us)
Async XLA Ops:
  5.6 43.6 %collective-permute-start.4 = (bf16[1536,384]{1,0:T(8,128)(2,1)}, bf16[1536,384]{1,0:T(8,128)(2,1)S(1)}, u32[]{:S(2)}, u32[]{:S(2)}) collective-permute-start(bf16[1536,384]{1,0:T(8,128)(2,1)} %get-tuple-element.35), channel_id=1, source_target_pairs={{0,8},{8,0},{16,24},{24,16},{1,9},{9,1},{17,25},{25,17},{2,10},{10... | collective-permute-start | bytes 3538952 | tf_op jit(solution)/shard_map/ppermute | solution.py:35
  6.8 42.3 %collective-permute-start.5 = (bf16[1536,384]{1,0:T(8,128)(2,1)}, bf16[1536,384]{1,0:T(8,128)(2,1)S(1)}, u32[]{:S(2)}, u32[]{:S(2)}) collective-permute-start(bf16[1536,384]{1,0:T(8,128)(2,1)} %get-tuple-element.36), channel_id=1, source_target_pairs={{0,16},{8,24},{16,0},{24,8},{1,17},{9,25},{17,1},{25,9},{2,18},{10... | collective-permute-start | bytes 3538952 | tf_op jit(solution)/shard_map/ppermute | solution.py:35
  10.6 16.2 %collective-permute-start = (bf16[192,1024]{1,0:T(8,128)(2,1)}, bf16[192,1024]{1,0:T(8,128)(2,1)S(1)}, u32[]{:S(2)}, u32[]{:S(2)}) collective-permute-start(bf16[192,1024]{1,0:T(8,128)(2,1)} %get-tuple-element.31), channel_id=1, source_target_pairs={{0,2},{2,0},{4,6},{6,4},{1,3},{3,1},{5,7},{7,5},{8,10},{10,8},{12,... | collective-permute-start | bytes 1179656 | tf_op jit(solution)/shard_map/ppermute | solution.py:35
  12.0 16.6 %collective-permute-start.1 = (bf16[192,1024]{1,0:T(8,128)(2,1)}, bf16[192,1024]{1,0:T(8,128)(2,1)S(1)}, u32[]{:S(2)}, u32[]{:S(2)}) collective-permute-start(bf16[192,1024]{1,0:T(8,128)(2,1)} %get-tuple-element.32), channel_id=1, source_target_pairs={{0,4},{2,6},{4,0},{6,2},{1,5},{3,7},{5,1},{7,3},{8,12},{10,14},{12... | collective-permute-start | bytes 1179656 | tf_op jit(solution)/shard_map/ppermute | solution.py:35
  12.0 34.5 %collective-permute-start.2 = (bf16[192,1024]{1,0:T(8,128)(2,1)}, bf16[192,1024]{1,0:T(8,128)(2,1)S(1)}, u32[]{:S(2)}, u32[]{:S(2)}) collective-permute-start(bf16[192,1024]{1,0:T(8,128)(2,1)} %get-tuple-element.33), channel_id=1, source_target_pairs={{0,6},{2,4},{4,2},{6,0},{1,7},{3,5},{5,3},{7,1},{8,14},{10,12},{12... | collective-permute-start | bytes 1179656 | tf_op jit(solution)/shard_map/ppermute | solution.py:35
  13.3 1.1 copy-start.9
  14.5 1.0 copy-start.14
  46.7 14.3 %copy-start.17 = (s32[6]{0:T(128)S(1)}, s32[6]{0:T(128)}, u32[]{:S(2)}) copy-start(s32[6]{0:T(128)} %stack.79.refs_0_.spot) | copy-start | bytes 76
  46.7 16.1 %collective-permute-start.3 = (bf16[768,1024]{1,0:T(8,128)(2,1)S(1)}, bf16[768,1024]{1,0:T(8,128)(2,1)S(1)}, u32[]{:S(2)}, u32[]{:S(2)}) collective-permute-start(bf16[768,1024]{1,0:T(8,128)(2,1)S(1)} %gather_slots.1.refs_0_.refs_3_), channel_id=1, source_target_pairs={{0,1},{1,0},{2,3},{3,2},{4,5},{5,4},{6,7},{7,6},{8,9},{9,8},{10,11... | collective-permute-start | bytes 4718600 | tf_op jit(solution)/shard_map/ppermute | solution.py:35
  49.1 13.7 %copy-start.5 = (bf16[1,1,2048,768]{3,2,1,0:T(8,128)(2,1)S(1)}, bf16[1,1,2048,768]{3,2,1,0:T(8,128)(2,1)}, u32[]{:S(2)}) copy-start(bf16[1,1,2048,768]{3,2,1,0:T(8,128)(2,1)} %refs_1_.5) | copy-start | bytes 9437188
  49.1 13.7 %copy-start.6 = (bf16[1,1,768,2048]{3,2,1,0:T(8,128)(2,1)S(1)}, bf16[1,1,768,2048]{3,2,1,0:T(8,128)(2,1)}, u32[]{:S(2)}) copy-start(bf16[1,1,768,2048]{3,2,1,0:T(8,128)(2,1)} %refs_2_.3) | copy-start | bytes 9437188
  49.8 13.0 %copy-start.7 = (f32[1024,384]{1,0:T(8,128)}, f32[1024,384]{1,0:T(8,128)S(1)}, u32[]{:S(2)}) copy-start(f32[1024,384]{1,0:T(8,128)S(1)} %get-tuple-element.42.refs_2_) | copy-start | bytes 4718596
  49.9 11.1 %collective-permute-start.6 = (bf16[1024,384]{1,0:T(8,128)(2,1)S(1)}, bf16[1024,384]{1,0:T(8,128)(2,1)S(1)}, u32[]{:S(2)}, u32[]{:S(2)}) collective-permute-start(bf16[1024,384]{1,0:T(8,128)(2,1)S(1)} %get-tuple-element.40.one.refs_3_), channel_id=1, source_target_pairs={{0,8},{1,16},{8,0},{9,24},{17,25},{16,1},{25,17},{24,9},{2,10},{3,... | collective-permute-start | bytes 2359304 | tf_op jit(solution)/shard_map/ppermute | solution.py:350
  61.6 12.4 %collective-permute-start.8 = (bf16[1024,384]{1,0:T(8,128)(2,1)S(1)}, bf16[1024,384]{1,0:T(8,128)(2,1)S(1)}, u32[]{:S(2)}, u32[]{:S(2)}) collective-permute-start(bf16[1024,384]{1,0:T(8,128)(2,1)S(1)} %choose_features.1), channel_id=1, source_target_pairs={{0,1},{1,0},{2,3},{3,2},{4,5},{5,4},{6,7},{7,6},{8,9},{9,8},{10,11... | collective-permute-start | bytes 2359304 | tf_op jit(solution)/shard_map/ppermute | solution.py:35
  62.1 12.0 %collective-permute-start.7 = (bf16[1024,384]{1,0:T(8,128)(2,1)S(1)}, bf16[1024,384]{1,0:T(8,128)(2,1)S(1)}, u32[]{:S(2)}, u32[]{:S(2)}) collective-permute-start(bf16[1024,384]{1,0:T(8,128)(2,1)S(1)} %collective-permute-done.6.other.one.refs_4_), channel_id=1, source_target_pairs={{1,9},{9,1},{16,24},{24,16},{3,11},{11,3},{18,26},{26,18},{5,13},{... | collective-permute-start | bytes 2359304 | tf_op jit(solution)/shard_map/ppermute | solution.py:351
  69.5 7.1 %copy-start.15 = (bf16[384,384]{1,0:T(8,128)(2,1)}, bf16[384,384]{1,0:T(8,128)(2,1)S(1)}, u32[]{:S(2)}) copy-start(bf16[384,384]{1,0:T(8,128)(2,1)S(1)} %get-tuple-element.45.refs_9_) | copy-start | bytes 884740
  69.6 29.2 %collective-permute-start.11 = (bf16[896,384]{1,0:T(8,128)(2,1)}, bf16[896,384]{1,0:T(8,128)(2,1)S(1)}, u32[]{:S(2)}, u32[]{:S(2)}) collective-permute-start(bf16[896,384]{1,0:T(8,128)(2,1)} %get-tuple-element.46), channel_id=1, source_target_pairs={{0,8},{8,0},{16,24},{24,16},{1,9},{9,1},{17,25},{25,17},{2,10},{10... | collective-permute-start | bytes 2064392 | tf_op jit(solution)/shard_map/ppermute | solution.py:35
  69.8 29.8 %collective-permute-start.12 = (bf16[896,384]{1,0:T(8,128)(2,1)}, bf16[896,384]{1,0:T(8,128)(2,1)S(1)}, u32[]{:S(2)}, u32[]{:S(2)}) collective-permute-start(bf16[896,384]{1,0:T(8,128)(2,1)} %get-tuple-element.47), channel_id=1, source_target_pairs={{0,16},{8,24},{16,0},{24,8},{1,17},{9,25},{17,1},{25,9},{2,18},{10... | collective-permute-start | bytes 2064392 | tf_op jit(solution)/shard_map/ppermute | solution.py:35
  74.0 1.7 %copy-start.3 = (bf16[1024,384]{1,0:T(8,128)(2,1)}, bf16[1024,384]{1,0:T(8,128)(2,1)S(1)}, u32[]{:S(2)}) copy-start(bf16[1024,384]{1,0:T(8,128)(2,1)S(1)} %collective-permute-done.7.other.refs_5_) | copy-start | bytes 2359300
  75.7 0.9 copy-start.1
  76.6 23.8 %collective-permute-start.9 = (bf16[512,384]{1,0:T(8,128)(2,1)}, bf16[512,384]{1,0:T(8,128)(2,1)}, u32[]{:S(2)}, u32[]{:S(2)}) collective-permute-start(bf16[512,384]{1,0:T(8,128)(2,1)} %get-tuple-element.43), channel_id=1, source_target_pairs={{0,1},{1,0},{2,3},{3,2},{4,5},{5,4},{6,7},{7,6},{8,9},{9,8},{10,11... | collective-permute-start | bytes 1179656 | tf_op jit(solution)/shard_map/ppermute | solution.py:35
  81.8 18.7 %collective-permute-start.10 = (bf16[512,384]{1,0:T(8,128)(2,1)}, bf16[512,384]{1,0:T(8,128)(2,1)}, u32[]{:S(2)}, u32[]{:S(2)}) collective-permute-start(bf16[512,384]{1,0:T(8,128)(2,1)} %get-tuple-element.44), channel_id=1, source_target_pairs={{0,1},{1,0},{2,3},{3,2},{4,5},{5,4},{6,7},{7,6},{8,9},{9,8},{10,11... | collective-permute-start | bytes 1179656 | tf_op jit(solution)/shard_map/ppermute | solution.py:35
  81.8 16.9 %collective-permute-start.13 = (bf16[384,384]{1,0:T(8,128)(2,1)}, bf16[384,384]{1,0:T(8,128)(2,1)}, u32[]{:S(2)}, u32[]{:S(2)}) collective-permute-start(bf16[384,384]{1,0:T(8,128)(2,1)} %get-tuple-element.48), channel_id=1, source_target_pairs={{0,24},{8,16},{16,8},{24,0},{1,25},{9,17},{17,9},{25,1},{2,26},{10... | collective-permute-start | bytes 884744 | tf_op jit(solution)/shard_map/ppermute | solution.py:35
  82.0 18.5 %all-to-all-start = ((f32[32,8,128]{2,1,0:T(8,128)}), f32[32,8,128]{2,1,0:T(8,128)S(1)}, u32[]{:S(2)}, u32[]{:S(2)}) async-start(f32[32,8,128]{2,1,0:T(8,128)} %get-tuple-element.41), calls=%async_computation | async-start | bytes 262144 | tf_op jit(solution)/shard_map/all_to_all | solution.py:376
  98.7 0.8 copy-start.10
  99.6 0.9 copy-start.12
  100.5 1.1 copy-start.2
  101.6 1.1 copy-start.4
  102.7 1.4 copy-start.8
  104.1 1.1 copy-start.11
  105.2 1.1 copy-start.13
  106.3 1.0 copy-start.16
  112.7 11.2 %collective-permute-start.16 = (f16[512,384]{1,0:T(8,128)(2,1)S(1)}, f16[512,384]{1,0:T(8,128)(2,1)}, u32[]{:S(2)}, u32[]{:S(2)}) collective-permute-start(f16[512,384]{1,0:T(8,128)(2,1)S(1)} %convert_element_type.27), channel_id=1, source_target_pairs={{0,16},{8,24},{16,0},{24,8},{1,17},{9,25},{17,1},{25,9},{2,18},{10... | collective-permute-start | bytes 1179656 | tf_op jit(solution)/shard_map/ppermute | solution.py:35
  113.6 10.6 %collective-permute-start.14 = (f16[512,384]{1,0:T(8,128)(2,1)}, f16[512,384]{1,0:T(8,128)(2,1)}, u32[]{:S(2)}, u32[]{:S(2)}) collective-permute-start(f16[512,384]{1,0:T(8,128)(2,1)} %convert_element_type.25), channel_id=1, source_target_pairs={{0,8},{8,0},{16,24},{24,16},{1,9},{9,1},{17,25},{25,17},{2,10},{10... | collective-permute-start | bytes 1179656 | tf_op jit(solution)/shard_map/ppermute | solution.py:35
  113.9 20.7 %collective-permute-start.19 = (f16[512,384]{1,0:T(8,128)(2,1)S(1)}, f16[512,384]{1,0:T(8,128)(2,1)}, u32[]{:S(2)}, u32[]{:S(2)}) collective-permute-start(f16[512,384]{1,0:T(8,128)(2,1)S(1)} %convert_element_type.27), channel_id=1, source_target_pairs={{0,8},{8,0},{16,24},{24,16},{1,9},{9,1},{17,25},{25,17},{2,10},{10... | collective-permute-start | bytes 1179656 | tf_op jit(solution)/shard_map/ppermute | solution.py:35
  115.1 20.5 %collective-permute-start.18 = (f16[512,384]{1,0:T(8,128)(2,1)}, f16[512,384]{1,0:T(8,128)(2,1)}, u32[]{:S(2)}, u32[]{:S(2)}) collective-permute-start(f16[512,384]{1,0:T(8,128)(2,1)} %convert_element_type.25), channel_id=1, source_target_pairs={{0,16},{8,24},{16,0},{24,8},{1,17},{9,25},{17,1},{25,9},{2,18},{10... | collective-permute-start | bytes 1179656 | tf_op jit(solution)/shard_map/ppermute | solution.py:35
  123.9 26.9 %collective-permute-start.17 = (f16[512,384]{1,0:T(8,128)(2,1)}, f16[512,384]{1,0:T(8,128)(2,1)}, u32[]{:S(2)}, u32[]{:S(2)}) collective-permute-start(f16[512,384]{1,0:T(8,128)(2,1)} %collective-permute-done.16), channel_id=1, source_target_pairs={{0,8},{8,0},{16,24},{24,16},{1,9},{9,1},{17,25},{25,17},{2,10},{10... | collective-permute-start | bytes 1179656 | tf_op jit(solution)/shard_map/ppermute | solution.py:35
  124.2 27.7 %collective-permute-start.15 = (f16[512,384]{1,0:T(8,128)(2,1)}, f16[512,384]{1,0:T(8,128)(2,1)}, u32[]{:S(2)}, u32[]{:S(2)}) collective-permute-start(f16[512,384]{1,0:T(8,128)(2,1)} %collective-permute-done.14), channel_id=1, source_target_pairs={{0,16},{8,24},{16,0},{24,8},{1,17},{9,25},{17,1},{25,9},{2,18},{10... | collective-permute-start | bytes 1179656 | tf_op jit(solution)/shard_map/ppermute | solution.py:35
  126.5 17.7 %all-to-all-start.1 = ((f32[32,8,128]{2,1,0:T(8,128)}), f32[32,8,128]{2,1,0:T(8,128)S(1)}, u32[]{:S(2)}, u32[]{:S(2)}) async-start(f32[32,8,128]{2,1,0:T(8,128)} %get-tuple-element.49), calls=%async_computation.1 | async-start | bytes 262144 | tf_op jit(solution)/shard_map/all_to_all | solution.py:388
  144.2 1.1 copy-start

commit v11 on v8

--- a/solution.py
+++ b/solution.py
@@ -132,7 +132,7 @@
 
 def average_kernel(islands, entries, tiles, spot, norms, drift_sum, own, moved, *refs):
     messages = refs[:islands]
-    *halves, notes, total, square = refs[islands:]
+    scaled, notes, total, square = refs[islands:]
     rows = total.shape[0] // tiles
     slots = own.shape[2]
     group = norms.shape[0] // islands
@@ -165,12 +165,10 @@
     pl.when(spot[5] != 1)(lambda: compute(moved))
     peak = jnp.max(jnp.abs(total[...]))
     unit = jnp.maximum(peak, 1e-30) / 32768
-    for n, half in enumerate(halves):
-        size = half.shape[0]
-        value = total[n * size : (n + 1) * size, :] * (1 / unit)
-        spread_out = value * 8193.0
-        value = spread_out - (spread_out - value)
-        half[...] = jnp.where(jnp.abs(value) < 2.0**-13, 0.0, value)
+    value = total[...] * (1 / unit)
+    spread_out = value * 8193.0
+    value = spread_out - (spread_out - value)
+    scaled[...] = jnp.where(jnp.abs(value) < 2.0**-13, 0.0, value)
     sublane = lax.broadcasted_iota(jnp.int32, notes.shape, 1)
     notes[...] = jnp.where(sublane == 0, jnp.sum(square[...]), unit)
 
@@ -366,31 +364,29 @@
     norms = lax.all_to_all(norms, AXES, split_axis=0, concat_axis=0, tiled=True)
     messages_in = [messages[0]] + [swap(messages[d], "island", d) for d in range(1, islands)]
 
-    *halves, notes = pl.pallas_call(
+    scaled, notes = pl.pallas_call(
         lambda *refs: average_kernel(islands, entries, 2, *refs),
         in_specs=[SMEM] + [VMEM] * (4 + islands),
-        out_specs=[VMEM] * 3,
-        out_shape=[jax.ShapeDtypeStruct((half // 2, columns), F32)] * 2
-        + [jax.ShapeDtypeStruct((devices, 8, 128), F32)],
+        out_specs=[VMEM] * 2,
+        out_shape=[
+            jax.ShapeDtypeStruct((half, columns), F32),
+            jax.ShapeDtypeStruct((devices, 8, 128), F32),
+        ],
         scratch_shapes=[pltpu.VMEM((half, columns), F32), pltpu.VMEM((1, columns), F32)],
         compiler_params=params(8 + routed_rows // 48),
         name="average_block",
     )(spot, norms, drift_sum, features_in, features_moved, *messages_in)
     notes = lax.all_to_all(notes, AXES, split_axis=0, concat_axis=0, tiled=True)
 
-    parted = half // 2
-    sent = [v.astype(WIRE) for v in halves]
-    values = {(0, 0): halves[0], (0, parted): halves[1]}
-    last = {}
-    if islands == 4:
-        values[2, 0], values[1, parted] = swap(sent[0], "island", 2), swap(sent[1], "island", 1)
-        beside, below = swap(sent[0], "island", 1), swap(sent[1], "island", 2)
-        values[1, 0], values[2, parted] = beside, below
-        last[3, 0], last[3, parted] = swap(beside, "island", 2), swap(below, "island", 1)
-    else:
-        for d in range(1, islands):
-            for n in range(2):
-                last[d, n * parted] = swap(sent[n], "island", d)
+    sent = scaled.astype(WIRE)
+    values, last = {(0, 0): scaled}, {}
+    steps = [1, 2] if handed else range(1, islands)
+    for d in steps:
+        values[d, 0] = swap(sent, "island", d)
+    if handed:
+        nothing = jnp.minimum(notes[0, 1, 0], 0.0).astype(WIRE)
+        last[3, 0] = swap(values[1, 0][:handed] + nothing, "island", 2)
+        last[3, handed] = swap(values[2, 0][handed:] + nothing, "island", 1)
     place = []
     for d in range(islands):
         at = origin(island, d, islands)
@@ -399,6 +395,8 @@
     place = jnp.stack(place).astype(jnp.int32)
     outs = []
     for values, cost in ((values, 12), (last, 3)):
+        if not values:
+            continue
         outs = pl.pallas_call(
             functools.partial(update_kernel, entries, list(values)),
             in_specs=[SMEM, VMEM, ANY] + [VMEM] * len(values) + [ANY] * len(outs),
@@ -408,8 +406,8 @@
                 jax.ShapeDtypeStruct(momentum.shape, BF16),
             ],
             scratch_shapes=[
-                pltpu.VMEM((len(values), parted, columns), F32),
-                pltpu.VMEM((len(values), parted, columns), BF16),
+                pltpu.VMEM((len(values), *next(iter(values.values())).shape), F32),
+                pltpu.VMEM((len(values), *next(iter(values.values())).shape), BF16),
                 pltpu.SemaphoreType.DMA((len(values),)),
                 pltpu.SemaphoreType.DMA((len(values), 2)),
             ],

time: 144 us -> 141 us (0.979)
  blocking collectives: 21.3 us -> 40.7 us
  waiting for transfers between devices: 50.4 us -> 37.9 us
  starting transfers between devices: 30.2 us -> 24.5 us
  other arithmetic: 8.93 us -> 5.27 us
    all_to_all x0 -> x1, blocking collectives: none -> 19.4 us  [body(): notes = lax.all_to_all(notes, AXES, split_axis=0, concat_axis=0, tiled=True)]
    ppermute x15 -> x13, waiting for transfers between devices: 32.8 us -> 25 us  [swap(): lax.ppermute(value, axis, [(at, partner(at, step, size)) for at in range(...]
    all_to_all x1 -> x0, starting transfers between devices: 5.55 us -> none  [body(): notes = lax.all_to_all(notes, AXES, split_axis=0, concat_axis=0, tiled=True)]
    all_to_all x1 -> x0, waiting for transfers between devices: 4.78 us -> none  [body(): notes = lax.all_to_all(notes, AXES, split_axis=0, concat_axis=0, tiled=True)]
    convert_element_type x6 -> x4, other arithmetic: 8.08 us -> 3.44 us  [body(): v.astype(F32)]
    add x0 -> x2, other arithmetic: none -> 1.72 us  [the longest x1 0.86 us: body(): last[3, 0] = swap(values[1, 0][:handed] + nothing, 'island', 2)]
    ppermute x15 -> x13, starting transfers between devices: 18.1 us -> 17.9 us  [swap(): lax.ppermute(value, axis, [(at, partner(at, step, size)) for at in range(...]
  transfers between devices with their start and end apart: 20 -> 17, of which waited for: 9 -> 8; matrix products, arithmetic and copies ran while one was open for 6% -> 3% of each run, Pallas kernels for 11% -> 12%
where the time goes in v11:
time: 141 us
  blocking collectives  40.7 us (29%)
  waiting for transfers between devices  37.9 us (27%)
  Pallas kernels  28.5 us (20%)
  starting transfers between devices  24.5 us (17%)
  other arithmetic  5.27 us (4%)
  local copies, waits for them, and re-layouts  2.39 us (2%)
  between operations  1.69 us (1%)
    ppermute x13, waiting for transfers between devices, swap(): lax.ppermute(value, axis, [(at, partner(at, step, size)) for at in range(...  25 us
    all_to_all x1, blocking collectives, body(): norms = lax.all_to_all(norms, AXES, split_axis=0, concat_axis=0, tiled=True)  21.3 us
    all_to_all x1, blocking collectives, body(): notes = lax.all_to_all(notes, AXES, split_axis=0, concat_axis=0, tiled=True)  19.4 us
    ppermute x13, starting transfers between devices, swap(): lax.ppermute(value, axis, [(at, partner(at, step, size)) for at in range(...  17.9 us
    ppermute x3, waiting for transfers between devices, send_features(): return lax.ppermute(turned, ('island', 'tensor'), pairs)  12.9 us
    pallas_call x2, Pallas kernels, body(): pl.pallas_call(functools.partial(update_kernel, entries, list(values)), i...  9.31 us
    pallas_call x1, Pallas kernels, body(): pl.pallas_call(lambda *refs: hidden_kernel(parts, across, *refs), in_spec...  5.43 us
    ppermute x3, starting transfers between devices, send_features(): return lax.ppermute(turned, ('island', 'tensor'), pairs)  5.03 us
  transfers between devices with their start and end apart: 17, of which 8 were waited for; matrix products, arithmetic and copies ran while one was open for 3% of the time, Pallas kernels for 12%

profile of v11, /device:TPU:0, one launch (start us, length us, event | category | flops | bytes accessed | tf_op | source)
XLA Modules:
  0.0 140.8 jit_solution(17580215439377961851)
XLA Ops:
  0.7 0.6 stack.79.refs_0_
  1.3 3.6 %pick_slots.1 = (bf16[192,1024]{1,0:T(8,128)(2,1)}, bf16[192,1024]{1,0:T(8,128)(2,1)}, bf16[192,1024]{1,0:T(8,128)(2,1)}, bf16[192,1024]{1,0:T(8,128)(2,1)}) custom-call(s32[6]{0:T(128)} %stack.79.refs_0_, s32[1,1,4,96]{3,2,1,0:T(4,128)} %refs_1_.3, s32[1,1,4]{2,1,0:T(1,128)} %refs_2_.2, f32[1,1,4,96]{3,2,1,0:T(4,128)} %refs_3_.1, ...), custom_call_target="tpu_custom_call" | custom-call | tf_op jit(solution)/shard_map/pick_slots/pallas_call | solution.py:255
  4.9 0.0 copy-start.3
  4.9 3.1 %collective-permute-start = (bf16[192,1024]{1,0:T(8,128)(2,1)}, bf16[192,1024]{1,0:T(8,128)(2,1)S(1)}, u32[]{:S(2)}, u32[]{:S(2)}) collective-permute-start(bf16[192,1024]{1,0:T(8,128)(2,1)} %get-tuple-element.30), channel_id=1, source_target_pairs={{0,2},{2,0},{4,6},{6,4},{1,3},{3,1},{5,7},{7,5},{8,10},{10,8},{12,... | collective-permute-start | bytes 1179656 | tf_op jit(solution)/shard_map/ppermute | solution.py:35
  8.0 2.6 %collective-permute-start.1 = (bf16[192,1024]{1,0:T(8,128)(2,1)}, bf16[192,1024]{1,0:T(8,128)(2,1)S(1)}, u32[]{:S(2)}, u32[]{:S(2)}) collective-permute-start(bf16[192,1024]{1,0:T(8,128)(2,1)} %get-tuple-element.31), channel_id=1, source_target_pairs={{0,4},{2,6},{4,0},{6,2},{1,5},{3,7},{5,1},{7,3},{8,12},{10,14},{12... | collective-permute-start | bytes 1179656 | tf_op jit(solution)/shard_map/ppermute | solution.py:35
  10.6 0.0 collective-permute-start.2
  10.6 4.2 %cut_drift.1 = (bf16[1024,384]{1,0:T(8,128)(2,1)}, bf16[1536,384]{1,0:T(8,128)(2,1)}, bf16[1536,384]{1,0:T(8,128)(2,1)}) custom-call(s32[6]{0:T(128)} %stack.79.refs_0_, bf16[1,1,2048,768]{3,2,1,0:T(8,128)(2,1)} %refs_1_.4), custom_call_target="tpu_custom_call" | custom-call | tf_op jit(solution)/shard_map/cut_drift/pallas_call | solution.py:271
  14.8 1.8 %collective-permute-start.4 = (bf16[1536,384]{1,0:T(8,128)(2,1)}, bf16[1536,384]{1,0:T(8,128)(2,1)S(1)}, u32[]{:S(2)}, u32[]{:S(2)}) collective-permute-start(bf16[1536,384]{1,0:T(8,128)(2,1)} %get-tuple-element.36), channel_id=1, source_target_pairs={{0,8},{8,0},{16,24},{24,16},{1,9},{9,1},{17,25},{25,17},{2,10},{10... | collective-permute-start | bytes 3538952 | tf_op jit(solution)/shard_map/ppermute | solution.py:35
  16.5 1.5 %collective-permute-start.5 = (bf16[1536,384]{1,0:T(8,128)(2,1)}, bf16[1536,384]{1,0:T(8,128)(2,1)S(1)}, u32[]{:S(2)}, u32[]{:S(2)}) collective-permute-start(bf16[1536,384]{1,0:T(8,128)(2,1)} %get-tuple-element.37), channel_id=1, source_target_pairs={{0,16},{8,24},{16,0},{24,8},{1,17},{9,25},{17,1},{25,9},{2,18},{10... | collective-permute-start | bytes 3538952 | tf_op jit(solution)/shard_map/ppermute | solution.py:35
  18.1 0.0 copy-done.3
  18.1 1.1 copy-done.2
  19.2 0.1 own_parts.1
  19.3 5.7 %collective-permute-done.refs_1_ = bf16[192,1024]{1,0:T(8,128)(2,1)S(1)} collective-permute-done((bf16[192,1024]{1,0:T(8,128)(2,1)}, bf16[192,1024]{1,0:T(8,128)(2,1)S(1)}, u32[]{:S(2)}, u32[]{:S(2)}) %collective-permute-start) | collective-permute-done | bytes 393248 | tf_op jit(solution)/shard_map/ppermute | solution.py:35
  24.9 13.0 %collective-permute-done.1.refs_2_ = bf16[192,1024]{1,0:T(8,128)(2,1)S(1)} collective-permute-done((bf16[192,1024]{1,0:T(8,128)(2,1)}, bf16[192,1024]{1,0:T(8,128)(2,1)S(1)}, u32[]{:S(2)}, u32[]{:S(2)}) %collective-permute-start.1) | collective-permute-done | bytes 393248 | tf_op jit(solution)/shard_map/ppermute | solution.py:35
  38.0 0.0 collective-permute-done.2.refs_3_
  38.0 0.1 gather_slots.1.refs_3_.refs_0_
  38.1 0.0 copy-start
  38.1 0.0 copy-start.4
  38.1 0.1 collective-permute-start.3
  38.2 4.0 %collective-permute-done.4.refs_2_ = bf16[1536,384]{1,0:T(8,128)(2,1)S(1)} collective-permute-done((bf16[1536,384]{1,0:T(8,128)(2,1)}, bf16[1536,384]{1,0:T(8,128)(2,1)S(1)}, u32[]{:S(2)}, u32[]{:S(2)}) %collective-permute-start.4) | collective-permute-done | bytes 1179680 | tf_op jit(solution)/shard_map/ppermute | solution.py:35
  42.2 1.2 collective-permute-done.5.refs_3_
  43.4 0.7 join_blocks.1
  44.1 1.3 collective-permute-start.8
  45.4 1.3 collective-permute-start.7
  46.7 2.4 %collective-permute-start.6 = (bf16[1024,384]{1,0:T(8,128)(2,1)S(1)}, bf16[1024,384]{1,0:T(8,128)(2,1)S(1)}, u32[]{:S(2)}, u32[]{:S(2)}) collective-permute-start(bf16[1024,384]{1,0:T(8,128)(2,1)S(1)} %get-tuple-element.38.refs_3_), channel_id=1, source_target_pairs={{0,8},{8,0},{17,25},{25,17},{2,10},{10,2},{19,27},{27,19},{4,12},{... | collective-permute-start | bytes 2359304 | tf_op jit(solution)/shard_map/ppermute | solution.py:321
  49.1 0.0 collective-permute-done.3.refs_4_
  49.2 0.0 copy-done.1
  49.2 0.0 copy-done
  49.2 0.0 copy-done.4
  49.2 5.4 %hidden_grads.1 = (bf16[2,384,384]{2,1,0:T(8,128)(2,1)S(1)}, f32[32,8,128]{2,1,0:T(8,128)S(1)}) custom-call(s32[6]{0:T(128)S(1)} %copy-done.4, bf16[1,1,2048,768]{3,2,1,0:T(8,128)(2,1)S(1)} %copy-done, bf16[1,1,768,2048]{3,2,1,0:T(8,128)(2,1)S(1)} %copy-done.1, bf16[768,1024]{1,0:T(8,128)(2,1)S(1)} %gather_slots.1.refs_3_.refs_0_, ...), custom_call_target="tpu_custom_call" | custom-call | tf_op jit(solution)/shard_map/hidden_grads/pallas_call | solution.py:336
  54.6 12.3 %collective-permute-done.8.refs_6_ = bf16[1024,384]{1,0:T(8,128)(2,1)S(1)} collective-permute-done((bf16[1024,384]{1,0:T(8,128)(2,1)S(1)}, bf16[1024,384]{1,0:T(8,128)(2,1)S(1)}, u32[]{:S(2)}, u32[]{:S(2)}) %collective-permute-start.8) | collective-permute-done | bytes 786464 | tf_op jit(solution)/shard_map/ppermute | solution.py:321
  66.9 0.5 collective-permute-done.7.refs_5_
  67.5 0.0 collective-permute-done.6.refs_4_
  67.5 1.0 hand_on.1
  68.5 1.5 %collective-permute-start.9 = (bf16[4,1024,384]{2,1,0:T(8,128)(2,1)S(1)}, bf16[4,1024,384]{2,1,0:T(8,128)(2,1)S(1)}, u32[]{:S(2)}, u32[]{:S(2)}) collective-permute-start(bf16[4,1024,384]{2,1,0:T(8,128)(2,1)S(1)} %get-tuple-element.43.refs_3_), channel_id=1, source_target_pairs={{0,1},{8,9},{17,16},{25,24},{2,3},{10,11},{19,18},{27,26},{4,5},{1... | collective-permute-start | bytes 9437192 | tf_op jit(solution)/shard_map/ppermute | solution.py:330
  70.0 1.1 collective-permute-start.10
  71.0 0.0 collective-permute-start.11
  71.0 2.5 %collective-permute-start.12 = (bf16[384,384]{1,0:T(8,128)(2,1)S(1)}, bf16[384,384]{1,0:T(8,128)(2,1)S(1)}, u32[]{:S(2)}, u32[]{:S(2)}) collective-permute-start(bf16[384,384]{1,0:T(8,128)(2,1)S(1)} %get-tuple-element.47), channel_id=1, source_target_pairs={{0,24},{8,16},{16,8},{24,0},{1,25},{9,17},{17,9},{25,1},{2,26},{10... | collective-permute-start | bytes 884744 | tf_op jit(solution)/shard_map/ppermute | solution.py:35
  73.5 21.3 %all_to_all.10.refs_1_ = f32[32,8,128]{2,1,0:T(8,128)S(1)} all-to-all(f32[32,8,128]{2,1,0:T(8,128)S(1)} %get-tuple-element.41), channel_id=1, replica_groups=mesh['island'=4,'expert'=4,'tensor'=2] {'island','expert','tensor'}, dimensions={0} | all-to-all | bytes 262144 | tf_op jit(solution)/shard_map/all_to_all | solution.py:364
  94.8 0.0 collective-permute-done.12.refs_8_
  94.8 0.0 collective-permute-done.10.refs_6_
  94.8 0.0 collective-permute-done.11.refs_7_
  94.8 0.0 collective-permute-done.9.refs_4_
  94.8 4.1 %average_block.1 = (f32[1024,384]{1,0:T(8,128)S(1)}, f32[32,8,128]{2,1,0:T(8,128)S(1)}) custom-call(s32[6]{0:T(128)S(1)} %copy-done.4, f32[32,8,128]{2,1,0:T(8,128)S(1)} %all_to_all.10.refs_1_, f32[1024,384]{1,0:T(8,128)S(1)} %get-tuple-element.42.refs_2_, bf16[4,1024,384]{2,1,0:T(8,128)(2,1)S(1)} %get-tuple-element.43.refs_3_, ...), custom_call_target="tpu_custom_call" | custom-call | tf_op jit(solution)/shard_map/average_block/pallas_call | solution.py:367
  98.9 0.1 convert_element_type.22
  99.0 1.8 %collective-permute-start.15 = (f16[1024,384]{1,0:T(8,128)(2,1)S(1)}, f16[1024,384]{1,0:T(8,128)(2,1)S(1)}, u32[]{:S(2)}, u32[]{:S(2)}) collective-permute-start(f16[1024,384]{1,0:T(8,128)(2,1)S(1)} %convert_element_type.22), channel_id=1, source_target_pairs={{0,16},{8,24},{16,0},{24,8},{1,17},{9,25},{17,1},{25,9},{2,18},{10... | collective-permute-start | bytes 2359304 | tf_op jit(solution)/shard_map/ppermute | solution.py:35
  100.8 1.0 collective-permute-start.13
  101.9 19.4 %all_to_all.11.notes = f32[32,8,128]{2,1,0:T(8,128)S(1)} all-to-all(f32[32,8,128]{2,1,0:T(8,128)S(1)} %get-tuple-element.48), channel_id=1, replica_groups=mesh['island'=4,'expert'=4,'tensor'=2] {'island','expert','tensor'}, dimensions={0} | all-to-all | bytes 262144 | tf_op jit(solution)/shard_map/all_to_all | solution.py:379
  121.3 0.5 slice.13
  122.4 0.0 collective-permute-done.15
  122.4 0.9 slice_add_fusion
  123.3 1.2 collective-permute-start.16
  124.5 0.0 collective-permute-done.13
  124.5 0.9 slice_add_fusion.1
  125.4 1.3 collective-permute-start.14
  126.7 0.1 stack.72.place
  126.8 1.2 convert_element_type.28.refs_2_
  128.0 0.1 convert_element_type.27.refs_1_
  128.1 6.1 %update_pieces.2 = (f32[1,2048,768]{2,1,0:T(8,128)}, bf16[1,2048,768]{2,1,0:T(8,128)(2,1)}) custom-call(s32[12]{0:T(128)S(1)} %stack.72.place, f32[32,8,128]{2,1,0:T(8,128)S(1)} %all_to_all.11.notes, f32[1,2048,768]{2,1,0:T(8,128)} %momentum.3, f32[1024,384]{1,0:T(8,128)S(1)} %get-tuple-element.49.refs_0_, f32[1024,384]{1,0:T(8,128)S(1)} %convert_element_type.27.refs_1_, ...), custom_call_target="tpu_custom_call" | custom-call | bytes 18874368 | tf_op jit(solution)/shard_map/update_pieces/pallas_call | solution.py:400
  134.2 0.6 collective-permute-done.16
  134.8 1.0 convert_element_type.26.refs_1_
  135.8 0.5 collective-permute-done.14
  136.3 1.0 convert_element_type.25.refs_0_
  137.4 3.2 %update_pieces.3 = (f32[1,2048,768]{2,1,0:T(8,128)}, bf16[1,2048,768]{2,1,0:T(8,128)(2,1)}) custom-call(s32[12]{0:T(128)S(1)} %stack.72.place, f32[32,8,128]{2,1,0:T(8,128)S(1)} %all_to_all.11.notes, f32[1,2048,768]{2,1,0:T(8,128)} %momentum.3, f32[512,384]{1,0:T(8,128)S(1)} %convert_element_type.25.refs_0_, ...), custom_call_target="tpu_custom_call", output_to_operand_aliasing={{0}: (5, {}), {1}: (6, {})} | custom-call | bytes 4718592 | tf_op jit(solution)/shard_map/update_pieces/pallas_call | solution.py:400
  (2 shorter events, 0.0 us)
Async XLA Ops:
  4.9 13.2 %copy-start.3 = (bf16[192,1024]{1,0:T(8,128)(2,1)S(1)}, bf16[192,1024]{1,0:T(8,128)(2,1)}, u32[]{:S(2)}) copy-start(bf16[192,1024]{1,0:T(8,128)(2,1)} %get-tuple-element.27.slots) | copy-start | bytes 1179652
  4.9 20.1 %collective-permute-start = (bf16[192,1024]{1,0:T(8,128)(2,1)}, bf16[192,1024]{1,0:T(8,128)(2,1)S(1)}, u32[]{:S(2)}, u32[]{:S(2)}) collective-permute-start(bf16[192,1024]{1,0:T(8,128)(2,1)} %get-tuple-element.30), channel_id=1, source_target_pairs={{0,2},{2,0},{4,6},{6,4},{1,3},{3,1},{5,7},{7,5},{8,10},{10,8},{12,... | collective-permute-start | bytes 1179656 | tf_op jit(solution)/shard_map/ppermute | solution.py:35
  8.0 30.0 %collective-permute-start.1 = (bf16[192,1024]{1,0:T(8,128)(2,1)}, bf16[192,1024]{1,0:T(8,128)(2,1)S(1)}, u32[]{:S(2)}, u32[]{:S(2)}) collective-permute-start(bf16[192,1024]{1,0:T(8,128)(2,1)} %get-tuple-element.31), channel_id=1, source_target_pairs={{0,4},{2,6},{4,0},{6,2},{1,5},{3,7},{5,1},{7,3},{8,12},{10,14},{12... | collective-permute-start | bytes 1179656 | tf_op jit(solution)/shard_map/ppermute | solution.py:35
  10.6 27.4 %collective-permute-start.2 = (bf16[192,1024]{1,0:T(8,128)(2,1)}, bf16[192,1024]{1,0:T(8,128)(2,1)S(1)}, u32[]{:S(2)}, u32[]{:S(2)}) collective-permute-start(bf16[192,1024]{1,0:T(8,128)(2,1)} %get-tuple-element.32), channel_id=1, source_target_pairs={{0,6},{2,4},{4,2},{6,0},{1,7},{3,5},{5,3},{7,1},{8,14},{10,12},{12... | collective-permute-start | bytes 1179656 | tf_op jit(solution)/shard_map/ppermute | solution.py:35
  14.8 27.4 %collective-permute-start.4 = (bf16[1536,384]{1,0:T(8,128)(2,1)}, bf16[1536,384]{1,0:T(8,128)(2,1)S(1)}, u32[]{:S(2)}, u32[]{:S(2)}) collective-permute-start(bf16[1536,384]{1,0:T(8,128)(2,1)} %get-tuple-element.36), channel_id=1, source_target_pairs={{0,8},{8,0},{16,24},{24,16},{1,9},{9,1},{17,25},{25,17},{2,10},{10... | collective-permute-start | bytes 3538952 | tf_op jit(solution)/shard_map/ppermute | solution.py:35
  16.5 26.9 %collective-permute-start.5 = (bf16[1536,384]{1,0:T(8,128)(2,1)}, bf16[1536,384]{1,0:T(8,128)(2,1)S(1)}, u32[]{:S(2)}, u32[]{:S(2)}) collective-permute-start(bf16[1536,384]{1,0:T(8,128)(2,1)} %get-tuple-element.37), channel_id=1, source_target_pairs={{0,16},{8,24},{16,0},{24,8},{1,17},{9,25},{17,1},{25,9},{2,18},{10... | collective-permute-start | bytes 3538952 | tf_op jit(solution)/shard_map/ppermute | solution.py:35
  18.1 1.1 copy-start.2
  38.0 11.2 %copy-start.1 = (bf16[1,1,768,2048]{3,2,1,0:T(8,128)(2,1)S(1)}, bf16[1,1,768,2048]{3,2,1,0:T(8,128)(2,1)}, u32[]{:S(2)}) copy-start(bf16[1,1,768,2048]{3,2,1,0:T(8,128)(2,1)} %refs_2_.3) | copy-start | bytes 9437188
  38.1 11.1 %copy-start = (bf16[1,1,2048,768]{3,2,1,0:T(8,128)(2,1)S(1)}, bf16[1,1,2048,768]{3,2,1,0:T(8,128)(2,1)}, u32[]{:S(2)}) copy-start(bf16[1,1,2048,768]{3,2,1,0:T(8,128)(2,1)} %refs_1_.5) | copy-start | bytes 9437188
  38.1 11.1 %copy-start.4 = (s32[6]{0:T(128)S(1)}, s32[6]{0:T(128)}, u32[]{:S(2)}) copy-start(s32[6]{0:T(128)} %stack.79.refs_0_) | copy-start | bytes 76
  38.1 11.0 %collective-permute-start.3 = (bf16[768,1024]{1,0:T(8,128)(2,1)S(1)}, bf16[768,1024]{1,0:T(8,128)(2,1)S(1)}, u32[]{:S(2)}, u32[]{:S(2)}) collective-permute-start(bf16[768,1024]{1,0:T(8,128)(2,1)S(1)} %gather_slots.1.refs_3_.refs_0_), channel_id=1, source_target_pairs={{0,1},{1,0},{2,3},{3,2},{4,5},{5,4},{6,7},{7,6},{8,9},{9,8},{10,11... | collective-permute-start | bytes 4718600 | tf_op jit(solution)/shard_map/ppermute | solution.py:35
  44.1 22.8 %collective-permute-start.8 = (bf16[1024,384]{1,0:T(8,128)(2,1)S(1)}, bf16[1024,384]{1,0:T(8,128)(2,1)S(1)}, u32[]{:S(2)}, u32[]{:S(2)}) collective-permute-start(bf16[1024,384]{1,0:T(8,128)(2,1)S(1)} %get-tuple-element.38.refs_3_), channel_id=1, source_target_pairs={{1,25},{9,17},{16,8},{24,0},{3,27},{11,19},{18,10},{26,2},{5,29},{... | collective-permute-start | bytes 2359304 | tf_op jit(solution)/shard_map/ppermute | solution.py:321
  45.4 22.1 %collective-permute-start.7 = (bf16[1024,384]{1,0:T(8,128)(2,1)S(1)}, bf16[1024,384]{1,0:T(8,128)(2,1)S(1)}, u32[]{:S(2)}, u32[]{:S(2)}) collective-permute-start(bf16[1024,384]{1,0:T(8,128)(2,1)S(1)} %get-tuple-element.38.refs_3_), channel_id=1, source_target_pairs={{1,17},{9,25},{16,0},{24,8},{3,19},{11,27},{18,2},{26,10},{5,21},{... | collective-permute-start | bytes 2359304 | tf_op jit(solution)/shard_map/ppermute | solution.py:321
  46.7 20.8 %collective-permute-start.6 = (bf16[1024,384]{1,0:T(8,128)(2,1)S(1)}, bf16[1024,384]{1,0:T(8,128)(2,1)S(1)}, u32[]{:S(2)}, u32[]{:S(2)}) collective-permute-start(bf16[1024,384]{1,0:T(8,128)(2,1)S(1)} %get-tuple-element.38.refs_3_), channel_id=1, source_target_pairs={{0,8},{8,0},{17,25},{25,17},{2,10},{10,2},{19,27},{27,19},{4,12},{... | collective-permute-start | bytes 2359304 | tf_op jit(solution)/shard_map/ppermute | solution.py:321
  68.5 26.3 %collective-permute-start.9 = (bf16[4,1024,384]{2,1,0:T(8,128)(2,1)S(1)}, bf16[4,1024,384]{2,1,0:T(8,128)(2,1)S(1)}, u32[]{:S(2)}, u32[]{:S(2)}) collective-permute-start(bf16[4,1024,384]{2,1,0:T(8,128)(2,1)S(1)} %get-tuple-element.43.refs_3_), channel_id=1, source_target_pairs={{0,1},{8,9},{17,16},{25,24},{2,3},{10,11},{19,18},{27,26},{4,5},{1... | collective-permute-start | bytes 9437192 | tf_op jit(solution)/shard_map/ppermute | solution.py:330
  70.0 24.8 %collective-permute-start.10 = (bf16[896,384]{1,0:T(8,128)(2,1)S(1)}, bf16[896,384]{1,0:T(8,128)(2,1)S(1)}, u32[]{:S(2)}, u32[]{:S(2)}) collective-permute-start(bf16[896,384]{1,0:T(8,128)(2,1)S(1)} %get-tuple-element.45), channel_id=1, source_target_pairs={{0,8},{8,0},{16,24},{24,16},{1,9},{9,1},{17,25},{25,17},{2,10},{10... | collective-permute-start | bytes 2064392 | tf_op jit(solution)/shard_map/ppermute | solution.py:35
  71.0 23.8 %collective-permute-start.11 = (bf16[896,384]{1,0:T(8,128)(2,1)S(1)}, bf16[896,384]{1,0:T(8,128)(2,1)S(1)}, u32[]{:S(2)}, u32[]{:S(2)}) collective-permute-start(bf16[896,384]{1,0:T(8,128)(2,1)S(1)} %get-tuple-element.46), channel_id=1, source_target_pairs={{0,16},{8,24},{16,0},{24,8},{1,17},{9,25},{17,1},{25,9},{2,18},{10... | collective-permute-start | bytes 2064392 | tf_op jit(solution)/shard_map/ppermute | solution.py:35
  71.0 23.8 %collective-permute-start.12 = (bf16[384,384]{1,0:T(8,128)(2,1)S(1)}, bf16[384,384]{1,0:T(8,128)(2,1)S(1)}, u32[]{:S(2)}, u32[]{:S(2)}) collective-permute-start(bf16[384,384]{1,0:T(8,128)(2,1)S(1)} %get-tuple-element.47), channel_id=1, source_target_pairs={{0,24},{8,16},{16,8},{24,0},{1,25},{9,17},{17,9},{25,1},{2,26},{10... | collective-permute-start | bytes 884744 | tf_op jit(solution)/shard_map/ppermute | solution.py:35
  99.0 23.4 %collective-permute-start.15 = (f16[1024,384]{1,0:T(8,128)(2,1)S(1)}, f16[1024,384]{1,0:T(8,128)(2,1)S(1)}, u32[]{:S(2)}, u32[]{:S(2)}) collective-permute-start(f16[1024,384]{1,0:T(8,128)(2,1)S(1)} %convert_element_type.22), channel_id=1, source_target_pairs={{0,16},{8,24},{16,0},{24,8},{1,17},{9,25},{17,1},{25,9},{2,18},{10... | collective-permute-start | bytes 2359304 | tf_op jit(solution)/shard_map/ppermute | solution.py:35
  100.8 23.7 %collective-permute-start.13 = (f16[1024,384]{1,0:T(8,128)(2,1)S(1)}, f16[1024,384]{1,0:T(8,128)(2,1)S(1)}, u32[]{:S(2)}, u32[]{:S(2)}) collective-permute-start(f16[1024,384]{1,0:T(8,128)(2,1)S(1)} %convert_element_type.22), channel_id=1, source_target_pairs={{0,8},{8,0},{16,24},{24,16},{1,9},{9,1},{17,25},{25,17},{2,10},{10... | collective-permute-start | bytes 2359304 | tf_op jit(solution)/shard_map/ppermute | solution.py:35
  123.3 11.5 %collective-permute-start.16 = (f16[512,384]{1,0:T(8,128)(2,1)}, f16[512,384]{1,0:T(8,128)(2,1)}, u32[]{:S(2)}, u32[]{:S(2)}) collective-permute-start(f16[512,384]{1,0:T(8,128)(2,1)} %slice_add_fusion), channel_id=1, source_target_pairs={{0,8},{8,0},{16,24},{24,16},{1,9},{9,1},{17,25},{25,17},{2,10},{10... | collective-permute-start | bytes 1179656 | tf_op jit(solution)/shard_map/ppermute | solution.py:35
  125.4 11.0 %collective-permute-start.14 = (f16[512,384]{1,0:T(8,128)(2,1)}, f16[512,384]{1,0:T(8,128)(2,1)}, u32[]{:S(2)}, u32[]{:S(2)}) collective-permute-start(f16[512,384]{1,0:T(8,128)(2,1)} %slice_add_fusion.1), channel_id=1, source_target_pairs={{0,16},{8,24},{16,0},{24,8},{1,17},{9,25},{17,1},{25,9},{2,18},{10... | collective-permute-start | bytes 1179656 | tf_op jit(solution)/shard_map/ppermute | solution.py:35

commit v12 on v10

--- a/solution.py
+++ b/solution.py
@@ -138,9 +138,9 @@
 
 def average_kernel(islands, entries, tiles, count, spot, norms, drift_sum, *refs):
     features, messages = refs[:count], refs[count : count + islands]
-    *halves, notes, total, square = refs[count + islands :]
+    scaled, notes, total, square = refs[count + islands :]
     rows = total.shape[0] // tiles
-    slots = features[0].shape[1]
+    slots = features[0].shape[-1]
     group = norms.shape[0] // islands
     scales = []
     for d in range(islands):
@@ -163,38 +163,43 @@
             for d in range(islands):
                 size = total.shape[0] // len(blocks[d])
                 n, first = divmod(m * rows, size)
-                block = blocks[d][n][first : first + rows, :]
+                ref, *lead = blocks[d][n]
+                block = ref[(*lead, slice(first, first + rows), slice(None))]
                 average = average + scales[d] * dot(block, messages[d][:slots, :], ((1,), (0,)))
             total[part, :] = average
             squares = squares + jnp.sum(average * average, axis=0, keepdims=True)
         square[...] = squares
 
-    if count == islands:
-        compute([[ref] for ref in features])
+    if len(features[0].shape) == 2:
+        compute([[(ref,)] for ref in features])
     else:
-        turned, first, second, other, *others = features
-        pl.when(spot[5] == 1)(lambda: compute([[turned], [first], [other], others]))
-        pl.when(spot[5] != 1)(lambda: compute([[other], others, [first], [second]]))
+        pair, moved, *halves = features
+        held = [[(pair, 0)], [(pair, 1)]]
+        others = [[(moved,)], [(ref,) for ref in halves]]
+        pl.when(spot[5] == 1)(lambda: compute(held + others))
+        pl.when(spot[5] != 1)(lambda: compute(others + held))
     peak = jnp.max(jnp.abs(total[...]))
     unit = jnp.maximum(peak, 1e-30) / 32768
-    for n, half in enumerate(halves):
-        size = half.shape[0]
-        value = total[n * size : (n + 1) * size, :] * (1 / unit)
-        spread_out = value * 8193.0
-        value = spread_out - (spread_out - value)
-        half[...] = jnp.where(jnp.abs(value) < 2.0**-13, 0.0, value)
+    value = total[...] * (1 / unit)
+    spread_out = value * 8193.0
+    value = spread_out - (spread_out - value)
+    scaled[...] = jnp.where(jnp.abs(value) < 2.0**-13, 0.0, value)
     sublane = lax.broadcasted_iota(jnp.int32, notes.shape, 1)
     notes[...] = jnp.where(sublane == 0, jnp.sum(square[...]), unit)
 
 
-def choose_kernel(spot, one, other, out):
-    out[...] = jnp.where(spot[5] == 1, one[...], other[...])
-
-
-def choose_halves_kernel(spot, norms, one, other, earlier, top, bottom, passed):
+def choose_kernel(spot, norms, turned, first, chosen, passed):
+    chosen[...] = jnp.where(spot[5] == 1, turned[...], first[...])
+    passed[...] = first[...]
+
+
+def hold_kernel(spot, norms, turned, first, second, earlier, pair, top, bottom, passed):
+    holder = spot[5] == 1
     size = top.shape[0]
-    top[...] = jnp.where(spot[5] == 1, one[:size, :], other[:size, :])
-    bottom[...] = jnp.where(spot[5] == 1, one[size:, :], other[size:, :])
+    pair[0] = jnp.where(holder, turned[...], first[...])
+    pair[1] = jnp.where(holder, first[...], second[...])
+    top[...] = pair[1, :size, :]
+    bottom[...] = pair[1, size:, :]
     passed[...] = norms[...]
 
 
@@ -348,58 +353,60 @@
             ]
             onward.append((at * parts + 1 - keep, (at ^ 1) * parts + 1 - keep))
         first = lax.ppermute(turned, ("island", "tensor"), pairs)
-        second = lax.ppermute(first, ("island", "tensor"), onward)
         block = jax.ShapeDtypeStruct((half, routed_rows), BF16)
-        part_block = jax.ShapeDtypeStruct((half // 2, routed_rows), BF16)
-        chosen = pl.pallas_call(
+        half_block = jax.ShapeDtypeStruct((half // 2, routed_rows), BF16)
+        chosen, first = pl.pallas_call(
             choose_kernel,
-            in_specs=[SMEM] + [VMEM] * 2,
-            out_specs=VMEM,
-            out_shape=block,
+            in_specs=[SMEM, ANY] + [VMEM] * 2,
+            out_specs=[VMEM] * 2,
+            out_shape=[block] * 2,
             compiler_params=params(4 + routed_rows // 48),
             name="choose_features",
-        )(spot, turned, first)
+        )(spot, norms, turned, first)
+        second = lax.ppermute(first, ("island", "tensor"), onward)
         moved = swap(chosen, "tensor", 1)
-        *chosen_halves, norms = pl.pallas_call(
-            choose_halves_kernel,
-            in_specs=[SMEM] + [VMEM] * 3 + [ANY],
-            out_specs=[VMEM] * 3,
-            out_shape=[part_block] * 2 + [jax.ShapeDtypeStruct(norms.shape, F32)],
+        pair, *halves, norms = pl.pallas_call(
+            hold_kernel,
+            in_specs=[SMEM] + [VMEM] * 4 + [ANY],
+            out_specs=[VMEM] * 4,
+            out_shape=[
+                jax.ShapeDtypeStruct((2, half, routed_rows), BF16),
+                half_block,
+                half_block,
+                jax.ShapeDtypeStruct(norms.shape, F32),
+            ],
             compiler_params=params(4 + routed_rows // 48),
-            name="choose_halves",
-        )(spot, norms, first, second, moved)
-        features_of = [turned, first, second, moved]
-        features_of += [swap(v, "tensor", 1) for v in chosen_halves]
+            name="hold_features",
+        )(spot, norms, turned, first, second, moved)
+        features_of = [pair, moved] + [swap(v, "tensor", 1) for v in halves]
     else:
         every = lax.all_gather(turned, ("island", "tensor"))
         features_of = [every[origin(island, d, islands) * parts + holder] for d in range(islands)]
     norms = lax.all_to_all(norms, AXES, split_axis=0, concat_axis=0, tiled=True)
 
-    *halves, notes = pl.pallas_call(
+    scaled, notes = pl.pallas_call(
         lambda *refs: average_kernel(islands, entries, 2, len(features_of), *refs),
         in_specs=[SMEM] + [VMEM] * (2 + len(features_of) + islands),
-        out_specs=[VMEM] * 3,
-        out_shape=[jax.ShapeDtypeStruct((half // 2, columns), F32)] * 2
-        + [jax.ShapeDtypeStruct((devices, 8, 128), F32)],
+        out_specs=[VMEM] * 2,
+        out_shape=[
+            jax.ShapeDtypeStruct((half, columns), F32),
+            jax.ShapeDtypeStruct((devices, 8, 128), F32),
+        ],
         scratch_shapes=[pltpu.VMEM((half, columns), F32), pltpu.VMEM((1, columns), F32)],
         compiler_params=params(8 + routed_rows // 48),
         name="average_block",
     )(spot, norms, drift_sum, *features_of, *messages_in)
     notes = lax.all_to_all(notes, AXES, split_axis=0, concat_axis=0, tiled=True)
 
-    parted = half // 2
-    sent = [v.astype(WIRE) for v in halves]
-    values = {(0, 0): halves[0], (0, parted): halves[1]}
-    last = {}
-    if islands == 4:
-        values[2, 0], values[1, parted] = swap(sent[0], "island", 2), swap(sent[1], "island", 1)
-        beside, below = swap(sent[0], "island", 1), swap(sent[1], "island", 2)
-        values[1, 0], values[2, parted] = beside, below
-        last[3, 0], last[3, parted] = swap(beside, "island", 2), swap(below, "island", 1)
-    else:
-        for d in range(1, islands):
-            for n in range(2):
-                last[d, n * parted] = swap(sent[n], "island", d)
+    sent = scaled.astype(WIRE)
+    values, last = {(0, 0): scaled}, {}
+    steps = [1, 2] if handed else range(1, islands)
+    for d in steps:
+        values[d, 0] = swap(sent, "island", d)
+    if handed:
+        nothing = jnp.minimum(notes[0, 1, 0], 0.0).astype(WIRE)
+        last[3, 0] = swap(values[1, 0][:handed] + nothing, "island", 2)
+        last[3, handed] = swap(values[2, 0][handed:] + nothing, "island", 1)
     place = []
     for d in range(islands):
         at = origin(island, d, islands)
@@ -408,6 +415,8 @@
     place = jnp.stack(place).astype(jnp.int32)
     outs = []
     for values, cost in ((values, 12), (last, 3)):
+        if not values:
+            continue
         outs = pl.pallas_call(
             functools.partial(update_kernel, entries, list(values)),
             in_specs=[SMEM, VMEM, ANY] + [VMEM] * len(values) + [ANY] * len(outs),
@@ -417,8 +426,8 @@
                 jax.ShapeDtypeStruct(momentum.shape, BF16),
             ],
             scratch_shapes=[
-                pltpu.VMEM((len(values), parted, columns), F32),
-                pltpu.VMEM((len(values), parted, columns), BF16),
+                pltpu.VMEM((len(values), *next(iter(values.values())).shape), F32),
+                pltpu.VMEM((len(values), *next(iter(values.values())).shape), BF16),
                 pltpu.SemaphoreType.DMA((len(values),)),
                 pltpu.SemaphoreType.DMA((len(values), 2)),
             ],

time: 157 us -> 150 us (0.955)
  the two profiles are of different devices: /device:TPU:21 before, /device:TPU:0 now
where the time goes in v12:
time: 150 us; the launch traced here: 149 us
  starting transfers between devices  38.7 us (26%)
  waiting for transfers between devices  37.7 us (25%)
  Pallas kernels  31.8 us (21%)
  blocking collectives  20.8 us (14%)
  local copies, waits for them, and re-layouts  13.1 us (9%)
  other arithmetic  5.28 us (4%)
  between operations  1.64 us (1%)
    ppermute x16, starting transfers between devices, swap(): lax.ppermute(value, axis, [(at, partner(at, step, size)) for at in range(...  32.2 us
    ppermute x16, waiting for transfers between devices, swap(): lax.ppermute(value, axis, [(at, partner(at, step, size)) for at in range(...  30.7 us
    all_to_all x1, blocking collectives, body(): notes = lax.all_to_all(notes, AXES, split_axis=0, concat_axis=0, tiled=True)  20.8 us
    unnamed x32, local copies, waits for them, and re-layouts  11.8 us
    pallas_call x2, Pallas kernels, body(): pl.pallas_call(functools.partial(update_kernel, entries, list(values)), i...  9.31 us
    pallas_call x1, Pallas kernels, body(): pl.pallas_call(lambda *refs: hidden_kernel(parts, islands, tails, *refs),...  6.75 us
    all_to_all x1, starting transfers between devices, body(): norms = lax.all_to_all(norms, AXES, split_axis=0, concat_axis=0, tiled=True)  5.31 us
    ppermute x1, waiting for transfers between devices, body(): first = lax.ppermute(turned, ('island', 'tensor'), pairs)  4.62 us
  transfers between devices with their start and end apart: 19, of which 8 were waited for; matrix products, arithmetic and copies ran while one was open for 3% of the time, Pallas kernels for 13%

profile of v12, /device:TPU:0, one launch (start us, length us, event | category | flops | bytes accessed | tf_op | source)
XLA Modules:
  0.0 149.0 jit_solution(6639658573775706555)
XLA Ops:
  0.7 0.7 stack.79.refs_0_.spot
  1.3 3.5 %pick_slots.1 = (bf16[192,1024]{1,0:T(8,128)(2,1)}, bf16[192,1024]{1,0:T(8,128)(2,1)}, bf16[192,1024]{1,0:T(8,128)(2,1)}, bf16[192,1024]{1,0:T(8,128)(2,1)}) custom-call(s32[6]{0:T(128)} %stack.79.refs_0_.spot, s32[1,1,4,96]{3,2,1,0:T(4,128)} %refs_1_.3, s32[1,1,4]{2,1,0:T(1,128)} %refs_2_.2, f32[1,1,4,96]{3,2,1,0:T(4,128)} %refs_3_.1, ...), custom_call_target="tpu_custom_call" | custom-call | tf_op jit(solution)/shard_map/pick_slots/pallas_call | solution.py:271
  4.9 3.1 %collective-permute-start = (bf16[192,1024]{1,0:T(8,128)(2,1)}, bf16[192,1024]{1,0:T(8,128)(2,1)S(1)}, u32[]{:S(2)}, u32[]{:S(2)}) collective-permute-start(bf16[192,1024]{1,0:T(8,128)(2,1)} %get-tuple-element.33), channel_id=1, source_target_pairs={{0,2},{2,0},{4,6},{6,4},{1,3},{3,1},{5,7},{7,5},{8,10},{10,8},{12,... | collective-permute-start | bytes 1179656 | tf_op jit(solution)/shard_map/ppermute | solution.py:35
  8.0 2.6 %collective-permute-start.1 = (bf16[192,1024]{1,0:T(8,128)(2,1)}, bf16[192,1024]{1,0:T(8,128)(2,1)S(1)}, u32[]{:S(2)}, u32[]{:S(2)}) collective-permute-start(bf16[192,1024]{1,0:T(8,128)(2,1)} %get-tuple-element.34), channel_id=1, source_target_pairs={{0,4},{2,6},{4,0},{6,2},{1,5},{3,7},{5,1},{7,3},{8,12},{10,14},{12... | collective-permute-start | bytes 1179656 | tf_op jit(solution)/shard_map/ppermute | solution.py:35
  10.6 0.0 collective-permute-start.2
  10.6 4.3 %cut_drift.1 = (bf16[1024,384]{1,0:T(8,128)(2,1)}, bf16[1536,384]{1,0:T(8,128)(2,1)}, bf16[1536,384]{1,0:T(8,128)(2,1)}) custom-call(s32[6]{0:T(128)} %stack.79.refs_0_.spot, bf16[1,1,2048,768]{3,2,1,0:T(8,128)(2,1)} %refs_1_.4), custom_call_target="tpu_custom_call" | custom-call | tf_op jit(solution)/shard_map/cut_drift/pallas_call | solution.py:287
  14.9 1.6 %collective-permute-start.4 = (bf16[1536,384]{1,0:T(8,128)(2,1)}, bf16[1536,384]{1,0:T(8,128)(2,1)S(1)}, u32[]{:S(2)}, u32[]{:S(2)}) collective-permute-start(bf16[1536,384]{1,0:T(8,128)(2,1)} %get-tuple-element.37), channel_id=1, source_target_pairs={{0,8},{8,0},{16,24},{24,16},{1,9},{9,1},{17,25},{25,17},{2,10},{10... | collective-permute-start | bytes 3538952 | tf_op jit(solution)/shard_map/ppermute | solution.py:35
  16.6 1.5 %collective-permute-start.5 = (bf16[1536,384]{1,0:T(8,128)(2,1)}, bf16[1536,384]{1,0:T(8,128)(2,1)S(1)}, u32[]{:S(2)}, u32[]{:S(2)}) collective-permute-start(bf16[1536,384]{1,0:T(8,128)(2,1)} %get-tuple-element.38), channel_id=1, source_target_pairs={{0,16},{8,24},{16,0},{24,8},{1,17},{9,25},{17,1},{25,9},{2,18},{10... | collective-permute-start | bytes 3538952 | tf_op jit(solution)/shard_map/ppermute | solution.py:35
  18.1 1.1 copy-done.6
  19.2 0.1 own_parts.1
  19.3 5.6 %collective-permute-done.refs_1_ = bf16[192,1024]{1,0:T(8,128)(2,1)S(1)} collective-permute-done((bf16[192,1024]{1,0:T(8,128)(2,1)}, bf16[192,1024]{1,0:T(8,128)(2,1)S(1)}, u32[]{:S(2)}, u32[]{:S(2)}) %collective-permute-start) | collective-permute-done | bytes 393248 | tf_op jit(solution)/shard_map/ppermute | solution.py:35
  25.0 13.0 %collective-permute-done.1.refs_2_ = bf16[192,1024]{1,0:T(8,128)(2,1)S(1)} collective-permute-done((bf16[192,1024]{1,0:T(8,128)(2,1)}, bf16[192,1024]{1,0:T(8,128)(2,1)S(1)}, u32[]{:S(2)}, u32[]{:S(2)}) %collective-permute-start.1) | collective-permute-done | bytes 393248 | tf_op jit(solution)/shard_map/ppermute | solution.py:35
  38.0 0.0 collective-permute-done.2.refs_3_
  38.0 0.1 gather_slots.1.refs_0_.refs_3_
  38.1 0.1 collective-permute-start.3
  38.2 4.2 %collective-permute-done.4.refs_2_ = bf16[1536,384]{1,0:T(8,128)(2,1)S(1)} collective-permute-done((bf16[1536,384]{1,0:T(8,128)(2,1)}, bf16[1536,384]{1,0:T(8,128)(2,1)S(1)}, u32[]{:S(2)}, u32[]{:S(2)}) %collective-permute-start.4) | collective-permute-done | bytes 1179680 | tf_op jit(solution)/shard_map/ppermute | solution.py:35
  42.3 1.2 collective-permute-done.5.refs_3_
  43.5 0.7 join_blocks.1
  44.2 0.0 copy-start.2
  44.2 1.1 copy-done.2
  45.4 0.5 collective-permute-start.6
  45.9 0.1 copy-done
  46.0 6.7 %hidden_grads.1 = (bf16[384,384]{1,0:T(8,128)(2,1)S(1)}, bf16[896,384]{1,0:T(8,128)(2,1)}, bf16[896,384]{1,0:T(8,128)(2,1)}, bf16[384,384]{1,0:T(8,128)(2,1)}, f32[32,8,128]{2,1,0:T(8,128)S(1)}) custom-call(s32[6]{0:T(128)S(1)} %copy-done.15, bf16[1,1,2048,768]{3,2,1,0:T(8,128)(2,1)S(1)} %copy-done, bf16[1,1,768,2048]{3,2,1,0:T(8,128)(2,1)S(1)} %copy-done.1, ...), custom_call_target="tpu_custom_call" | custom-call | tf_op jit(solution)/shard_map/hidden_grads/pallas_call | solution.py:334
  52.8 4.6 %collective-permute-done.6.first = bf16[1024,384]{1,0:T(8,128)(2,1)S(1)} collective-permute-done((bf16[1024,384]{1,0:T(8,128)(2,1)S(1)}, bf16[1024,384]{1,0:T(8,128)(2,1)S(1)}, u32[]{:S(2)}, u32[]{:S(2)}) %collective-permute-start.6) | collective-permute-done | bytes 786464 | tf_op jit(solution)/shard_map/ppermute | solution.py:355
  57.4 0.7 choose_features.1
  58.1 0.1 collective-permute-start.8
  58.2 0.7 collective-permute-start.7
  58.9 0.6 collective-permute-start.11
  59.5 3.6 %collective-permute-start.12 = (bf16[896,384]{1,0:T(8,128)(2,1)}, bf16[896,384]{1,0:T(8,128)(2,1)S(1)}, u32[]{:S(2)}, u32[]{:S(2)}) collective-permute-start(bf16[896,384]{1,0:T(8,128)(2,1)} %get-tuple-element.52), channel_id=1, source_target_pairs={{0,16},{8,24},{16,0},{24,8},{1,17},{9,25},{17,1},{25,9},{2,18},{10... | collective-permute-start | bytes 2064392 | tf_op jit(solution)/shard_map/ppermute | solution.py:35
  63.1 1.8 %hold_features.1 = (bf16[2,1024,384]{2,1,0:T(8,128)(2,1)S(1)}, bf16[512,384]{1,0:T(8,128)(2,1)}, bf16[512,384]{1,0:T(8,128)(2,1)}, f32[32,8,128]{2,1,0:T(8,128)S(1)}) custom-call(s32[6]{0:T(128)S(1)} %copy-done.15, f32[32,8,128]{2,1,0:T(8,128)S(1)} %get-tuple-element.41.norms, bf16[1024,384]{1,0:T(8,128)(2,1)S(1)} %get-tuple-element.42.turned, ...), custom_call_target="tpu_custom_call" | custom-call | tf_op jit(solution)/shard_map/hold_features/pallas_call | solution.py:368
  64.9 1.1 copy-done.4
  66.0 15.5 %collective-permute-start.9 = (bf16[512,384]{1,0:T(8,128)(2,1)}, bf16[512,384]{1,0:T(8,128)(2,1)S(1)}, u32[]{:S(2)}, u32[]{:S(2)}) collective-permute-start(bf16[512,384]{1,0:T(8,128)(2,1)} %get-tuple-element.48), channel_id=1, source_target_pairs={{0,1},{1,0},{2,3},{3,2},{4,5},{5,4},{6,7},{7,6},{8,9},{9,8},{10,11... | collective-permute-start | bytes 1179656 | tf_op jit(solution)/shard_map/ppermute | solution.py:35
  81.5 0.8 collective-permute-start.13
  82.4 5.3 %all-to-all-start = ((f32[32,8,128]{2,1,0:T(8,128)}), f32[32,8,128]{2,1,0:T(8,128)S(1)}, u32[]{:S(2)}, u32[]{:S(2)}) async-start(f32[32,8,128]{2,1,0:T(8,128)} %copy-done.14), calls=%async_computation | async-start | bytes 262144 | tf_op jit(solution)/shard_map/all_to_all | solution.py:385
  87.7 4.9 %collective-permute-done.13.refs_10_ = bf16[384,384]{1,0:T(8,128)(2,1)} collective-permute-done((bf16[384,384]{1,0:T(8,128)(2,1)}, bf16[384,384]{1,0:T(8,128)(2,1)}, u32[]{:S(2)}, u32[]{:S(2)}) %collective-permute-start.13) | collective-permute-done | bytes 294944 | tf_op jit(solution)/shard_map/ppermute | solution.py:35
  92.6 0.9 copy-done.7
  93.4 2.4 %all-to-all-done.refs_1_ = f32[32,8,128]{2,1,0:T(8,128)S(1)} async-done(((f32[32,8,128]{2,1,0:T(8,128)}), f32[32,8,128]{2,1,0:T(8,128)S(1)}, u32[]{:S(2)}, u32[]{:S(2)}) %all-to-all-start) | async-done | bytes 131104 | tf_op jit(solution)/shard_map/all_to_all | solution.py:385
  95.9 0.0 collective-permute-done.9.refs_5_
  95.9 0.8 copy-done.10
  96.6 0.7 copy-done.12
  97.4 1.4 copy-done.3
  98.8 1.4 copy-done.5
  100.2 1.1 copy-done.8
  101.3 1.0 copy-done.11
  102.3 1.0 copy-done.13
  103.3 4.5 %average_block.1 = (f32[1024,384]{1,0:T(8,128)S(1)}, f32[32,8,128]{2,1,0:T(8,128)S(1)}) custom-call(s32[6]{0:T(128)S(1)} %copy-done.15, f32[32,8,128]{2,1,0:T(8,128)S(1)} %all-to-all-done.refs_1_, f32[1024,384]{1,0:T(8,128)S(1)} %copy-done.3, bf16[2,1024,384]{2,1,0:T(8,128)(2,1)S(1)} %copy-done.5, ...), custom_call_target="tpu_custom_call" | custom-call | tf_op jit(solution)/shard_map/average_block/pallas_call | solution.py:387
  107.8 0.1 convert_element_type.22
  107.9 0.9 collective-permute-start.16
  108.9 0.7 collective-permute-start.14
  109.6 20.8 %all_to_all.10.notes = f32[32,8,128]{2,1,0:T(8,128)S(1)} all-to-all(f32[32,8,128]{2,1,0:T(8,128)S(1)} %get-tuple-element.54), channel_id=1, replica_groups=mesh['island'=4,'expert'=4,'tensor'=2] {'island','expert','tensor'}, dimensions={0} | all-to-all | bytes 262144 | tf_op jit(solution)/shard_map/all_to_all | solution.py:399
  130.4 0.5 slice.13
  131.5 0.9 slice_add_fusion
  132.4 0.2 collective-permute-start.17
  132.6 0.8 slice_add_fusion.1
  133.4 0.9 collective-permute-start.15
  134.3 0.1 stack.72.place
  134.3 1.3 convert_element_type.28.refs_2_
  135.6 0.1 convert_element_type.27.refs_1_
  135.7 6.1 %update_pieces.2 = (f32[1,2048,768]{2,1,0:T(8,128)}, bf16[1,2048,768]{2,1,0:T(8,128)(2,1)}) custom-call(s32[12]{0:T(128)S(1)} %stack.72.place, f32[32,8,128]{2,1,0:T(8,128)S(1)} %all_to_all.10.notes, f32[1,2048,768]{2,1,0:T(8,128)} %momentum.3, f32[1024,384]{1,0:T(8,128)S(1)} %get-tuple-element.55.refs_0_, f32[1024,384]{1,0:T(8,128)S(1)} %convert_element_type.27.refs_1_, ...), custom_call_target="tpu_custom_call" | custom-call | bytes 18874368 | tf_op jit(solution)/shard_map/update_pieces/pallas_call | solution.py:420
  141.8 1.7 %collective-permute-done.17 = f16[512,384]{1,0:T(8,128)(2,1)} collective-permute-done((f16[512,384]{1,0:T(8,128)(2,1)}, f16[512,384]{1,0:T(8,128)(2,1)}, u32[]{:S(2)}, u32[]{:S(2)}) %collective-permute-start.17) | collective-permute-done | bytes 393248 | tf_op jit(solution)/shard_map/ppermute | solution.py:35
  143.5 1.0 convert_element_type.26.refs_1_
  144.5 0.0 collective-permute-done.15
  144.6 1.0 convert_element_type.25.refs_0_
  145.6 3.2 %update_pieces.3 = (f32[1,2048,768]{2,1,0:T(8,128)}, bf16[1,2048,768]{2,1,0:T(8,128)(2,1)}) custom-call(s32[12]{0:T(128)S(1)} %stack.72.place, f32[32,8,128]{2,1,0:T(8,128)S(1)} %all_to_all.10.notes, f32[1,2048,768]{2,1,0:T(8,128)} %momentum.3, f32[512,384]{1,0:T(8,128)S(1)} %convert_element_type.25.refs_0_, ...), custom_call_target="tpu_custom_call", output_to_operand_aliasing={{0}: (5, {}), {1}: (6, {})} | custom-call | bytes 4718592 | tf_op jit(solution)/shard_map/update_pieces/pallas_call | solution.py:420
  (28 shorter events, 0.1 us)
Async XLA Ops:
  4.9 20.1 %collective-permute-start = (bf16[192,1024]{1,0:T(8,128)(2,1)}, bf16[192,1024]{1,0:T(8,128)(2,1)S(1)}, u32[]{:S(2)}, u32[]{:S(2)}) collective-permute-start(bf16[192,1024]{1,0:T(8,128)(2,1)} %get-tuple-element.33), channel_id=1, source_target_pairs={{0,2},{2,0},{4,6},{6,4},{1,3},{3,1},{5,7},{7,5},{8,10},{10,8},{12,... | collective-permute-start | bytes 1179656 | tf_op jit(solution)/shard_map/ppermute | solution.py:35
  8.0 30.0 %collective-permute-start.1 = (bf16[192,1024]{1,0:T(8,128)(2,1)}, bf16[192,1024]{1,0:T(8,128)(2,1)S(1)}, u32[]{:S(2)}, u32[]{:S(2)}) collective-permute-start(bf16[192,1024]{1,0:T(8,128)(2,1)} %get-tuple-element.34), channel_id=1, source_target_pairs={{0,4},{2,6},{4,0},{6,2},{1,5},{3,7},{5,1},{7,3},{8,12},{10,14},{12... | collective-permute-start | bytes 1179656 | tf_op jit(solution)/shard_map/ppermute | solution.py:35
  10.6 7.5 %copy-start.9 = (bf16[192,1024]{1,0:T(8,128)(2,1)S(1)}, bf16[192,1024]{1,0:T(8,128)(2,1)}, u32[]{:S(2)}) copy-start(bf16[192,1024]{1,0:T(8,128)(2,1)} %get-tuple-element.30.slots) | copy-start | bytes 1179652
  10.6 27.4 %collective-permute-start.2 = (bf16[192,1024]{1,0:T(8,128)(2,1)}, bf16[192,1024]{1,0:T(8,128)(2,1)S(1)}, u32[]{:S(2)}, u32[]{:S(2)}) collective-permute-start(bf16[192,1024]{1,0:T(8,128)(2,1)} %get-tuple-element.35), channel_id=1, source_target_pairs={{0,6},{2,4},{4,2},{6,0},{1,7},{3,5},{5,3},{7,1},{8,14},{10,12},{12... | collective-permute-start | bytes 1179656 | tf_op jit(solution)/shard_map/ppermute | solution.py:35
  14.9 27.4 %collective-permute-start.4 = (bf16[1536,384]{1,0:T(8,128)(2,1)}, bf16[1536,384]{1,0:T(8,128)(2,1)S(1)}, u32[]{:S(2)}, u32[]{:S(2)}) collective-permute-start(bf16[1536,384]{1,0:T(8,128)(2,1)} %get-tuple-element.37), channel_id=1, source_target_pairs={{0,8},{8,0},{16,24},{24,16},{1,9},{9,1},{17,25},{25,17},{2,10},{10... | collective-permute-start | bytes 3538952 | tf_op jit(solution)/shard_map/ppermute | solution.py:35
  16.6 27.0 %collective-permute-start.5 = (bf16[1536,384]{1,0:T(8,128)(2,1)}, bf16[1536,384]{1,0:T(8,128)(2,1)S(1)}, u32[]{:S(2)}, u32[]{:S(2)}) collective-permute-start(bf16[1536,384]{1,0:T(8,128)(2,1)} %get-tuple-element.38), channel_id=1, source_target_pairs={{0,16},{8,24},{16,0},{24,8},{1,17},{9,25},{17,1},{25,9},{2,18},{10... | collective-permute-start | bytes 3538952 | tf_op jit(solution)/shard_map/ppermute | solution.py:35
  18.1 1.1 copy-start.6
  38.0 7.9 %copy-start.1 = (bf16[1,1,768,2048]{3,2,1,0:T(8,128)(2,1)S(1)}, bf16[1,1,768,2048]{3,2,1,0:T(8,128)(2,1)}, u32[]{:S(2)}) copy-start(bf16[1,1,768,2048]{3,2,1,0:T(8,128)(2,1)} %refs_2_.3) | copy-start | bytes 9437188
  38.1 7.8 %collective-permute-start.3 = (bf16[768,1024]{1,0:T(8,128)(2,1)S(1)}, bf16[768,1024]{1,0:T(8,128)(2,1)S(1)}, u32[]{:S(2)}, u32[]{:S(2)}) collective-permute-start(bf16[768,1024]{1,0:T(8,128)(2,1)S(1)} %gather_slots.1.refs_0_.refs_3_), channel_id=1, source_target_pairs={{0,1},{1,0},{2,3},{3,2},{4,5},{5,4},{6,7},{7,6},{8,9},{9,8},{10,11... | collective-permute-start | bytes 4718600 | tf_op jit(solution)/shard_map/ppermute | solution.py:35
  43.5 2.5 %copy-start = (bf16[1,1,2048,768]{3,2,1,0:T(8,128)(2,1)S(1)}, bf16[1,1,2048,768]{3,2,1,0:T(8,128)(2,1)}, u32[]{:S(2)}) copy-start(bf16[1,1,2048,768]{3,2,1,0:T(8,128)(2,1)} %refs_1_.5) | copy-start | bytes 9437188
  43.5 2.5 %copy-start.15 = (s32[6]{0:T(128)S(1)}, s32[6]{0:T(128)}, u32[]{:S(2)}) copy-start(s32[6]{0:T(128)} %stack.79.refs_0_.spot) | copy-start | bytes 76
  44.2 1.1 copy-start.2
  45.4 12.0 %collective-permute-start.6 = (bf16[1024,384]{1,0:T(8,128)(2,1)S(1)}, bf16[1024,384]{1,0:T(8,128)(2,1)S(1)}, u32[]{:S(2)}, u32[]{:S(2)}) collective-permute-start(bf16[1024,384]{1,0:T(8,128)(2,1)S(1)} %get-tuple-element.42.turned), channel_id=1, source_target_pairs={{0,8},{1,16},{8,0},{9,24},{17,25},{16,1},{25,17},{24,9},{2,10},{3,... | collective-permute-start | bytes 2359304 | tf_op jit(solution)/shard_map/ppermute | solution.py:355
  58.1 5.0 %collective-permute-start.8 = (bf16[1024,384]{1,0:T(8,128)(2,1)S(1)}, bf16[1024,384]{1,0:T(8,128)(2,1)S(1)}, u32[]{:S(2)}, u32[]{:S(2)}) collective-permute-start(bf16[1024,384]{1,0:T(8,128)(2,1)S(1)} %get-tuple-element.44), channel_id=1, source_target_pairs={{0,1},{1,0},{2,3},{3,2},{4,5},{5,4},{6,7},{7,6},{8,9},{9,8},{10,11... | collective-permute-start | bytes 2359304 | tf_op jit(solution)/shard_map/ppermute | solution.py:35
  58.2 5.0 %collective-permute-start.7 = (bf16[1024,384]{1,0:T(8,128)(2,1)S(1)}, bf16[1024,384]{1,0:T(8,128)(2,1)S(1)}, u32[]{:S(2)}, u32[]{:S(2)}) collective-permute-start(bf16[1024,384]{1,0:T(8,128)(2,1)S(1)} %get-tuple-element.43.first), channel_id=1, source_target_pairs={{1,9},{9,1},{16,24},{24,16},{3,11},{11,3},{18,26},{26,18},{5,13},{... | collective-permute-start | bytes 2359304 | tf_op jit(solution)/shard_map/ppermute | solution.py:366
  58.9 33.7 %collective-permute-start.11 = (bf16[896,384]{1,0:T(8,128)(2,1)}, bf16[896,384]{1,0:T(8,128)(2,1)S(1)}, u32[]{:S(2)}, u32[]{:S(2)}) collective-permute-start(bf16[896,384]{1,0:T(8,128)(2,1)} %get-tuple-element.51), channel_id=1, source_target_pairs={{0,8},{8,0},{16,24},{24,16},{1,9},{9,1},{17,25},{25,17},{2,10},{10... | collective-permute-start | bytes 2064392 | tf_op jit(solution)/shard_map/ppermute | solution.py:35
  59.5 33.1 %collective-permute-start.12 = (bf16[896,384]{1,0:T(8,128)(2,1)}, bf16[896,384]{1,0:T(8,128)(2,1)S(1)}, u32[]{:S(2)}, u32[]{:S(2)}) collective-permute-start(bf16[896,384]{1,0:T(8,128)(2,1)} %get-tuple-element.52), channel_id=1, source_target_pairs={{0,16},{8,24},{16,0},{24,8},{1,17},{9,25},{17,1},{25,9},{2,18},{10... | collective-permute-start | bytes 2064392 | tf_op jit(solution)/shard_map/ppermute | solution.py:35
  64.9 1.1 copy-start.4
  66.0 16.3 %copy-start.14 = (f32[32,8,128]{2,1,0:T(8,128)}, f32[32,8,128]{2,1,0:T(8,128)S(1)}, u32[]{:S(2)}) copy-start(f32[32,8,128]{2,1,0:T(8,128)S(1)} %get-tuple-element.45) | copy-start | bytes 393220
  66.0 29.8 %collective-permute-start.9 = (bf16[512,384]{1,0:T(8,128)(2,1)}, bf16[512,384]{1,0:T(8,128)(2,1)S(1)}, u32[]{:S(2)}, u32[]{:S(2)}) collective-permute-start(bf16[512,384]{1,0:T(8,128)(2,1)} %get-tuple-element.48), channel_id=1, source_target_pairs={{0,1},{1,0},{2,3},{3,2},{4,5},{5,4},{6,7},{7,6},{8,9},{9,8},{10,11... | collective-permute-start | bytes 1179656 | tf_op jit(solution)/shard_map/ppermute | solution.py:35
  81.5 15.1 %collective-permute-start.10 = (bf16[512,384]{1,0:T(8,128)(2,1)}, bf16[512,384]{1,0:T(8,128)(2,1)S(1)}, u32[]{:S(2)}, u32[]{:S(2)}) collective-permute-start(bf16[512,384]{1,0:T(8,128)(2,1)} %get-tuple-element.49), channel_id=1, source_target_pairs={{0,1},{1,0},{2,3},{3,2},{4,5},{5,4},{6,7},{7,6},{8,9},{9,8},{10,11... | collective-permute-start | bytes 1179656 | tf_op jit(solution)/shard_map/ppermute | solution.py:35
  81.5 11.0 %collective-permute-start.13 = (bf16[384,384]{1,0:T(8,128)(2,1)}, bf16[384,384]{1,0:T(8,128)(2,1)}, u32[]{:S(2)}, u32[]{:S(2)}) collective-permute-start(bf16[384,384]{1,0:T(8,128)(2,1)} %get-tuple-element.53), channel_id=1, source_target_pairs={{0,24},{8,16},{16,8},{24,0},{1,25},{9,17},{17,9},{25,1},{2,26},{10... | collective-permute-start | bytes 884744 | tf_op jit(solution)/shard_map/ppermute | solution.py:35
  82.4 13.5 %all-to-all-start = ((f32[32,8,128]{2,1,0:T(8,128)}), f32[32,8,128]{2,1,0:T(8,128)S(1)}, u32[]{:S(2)}, u32[]{:S(2)}) async-start(f32[32,8,128]{2,1,0:T(8,128)} %copy-done.14), calls=%async_computation | async-start | bytes 262144 | tf_op jit(solution)/shard_map/all_to_all | solution.py:385
  92.6 0.9 copy-start.7
  95.9 0.8 copy-start.10
  96.6 0.7 copy-start.12
  97.4 1.4 copy-start.3
  98.8 1.4 copy-start.5
  100.2 1.1 copy-start.8
  101.3 1.0 copy-start.11
  102.3 1.0 copy-start.13
  107.9 23.6 %collective-permute-start.16 = (f16[1024,384]{1,0:T(8,128)(2,1)S(1)}, f16[1024,384]{1,0:T(8,128)(2,1)S(1)}, u32[]{:S(2)}, u32[]{:S(2)}) collective-permute-start(f16[1024,384]{1,0:T(8,128)(2,1)S(1)} %convert_element_type.22), channel_id=1, source_target_pairs={{0,16},{8,24},{16,0},{24,8},{1,17},{9,25},{17,1},{25,9},{2,18},{10... | collective-permute-start | bytes 2359304 | tf_op jit(solution)/shard_map/ppermute | solution.py:35
  108.9 23.7 %collective-permute-start.14 = (f16[1024,384]{1,0:T(8,128)(2,1)S(1)}, f16[1024,384]{1,0:T(8,128)(2,1)S(1)}, u32[]{:S(2)}, u32[]{:S(2)}) collective-permute-start(f16[1024,384]{1,0:T(8,128)(2,1)S(1)} %convert_element_type.22), channel_id=1, source_target_pairs={{0,8},{8,0},{16,24},{24,16},{1,9},{9,1},{17,25},{25,17},{2,10},{10... | collective-permute-start | bytes 2359304 | tf_op jit(solution)/shard_map/ppermute | solution.py:35
  132.4 11.1 %collective-permute-start.17 = (f16[512,384]{1,0:T(8,128)(2,1)}, f16[512,384]{1,0:T(8,128)(2,1)}, u32[]{:S(2)}, u32[]{:S(2)}) collective-permute-start(f16[512,384]{1,0:T(8,128)(2,1)} %slice_add_fusion), channel_id=1, source_target_pairs={{0,8},{8,0},{16,24},{24,16},{1,9},{9,1},{17,25},{25,17},{2,10},{10... | collective-permute-start | bytes 1179656 | tf_op jit(solution)/shard_map/ppermute | solution.py:35
  133.4 11.2 %collective-permute-start.15 = (f16[512,384]{1,0:T(8,128)(2,1)}, f16[512,384]{1,0:T(8,128)(2,1)}, u32[]{:S(2)}, u32[]{:S(2)}) collective-permute-start(f16[512,384]{1,0:T(8,128)(2,1)} %slice_add_fusion.1), channel_id=1, source_target_pairs={{0,16},{8,24},{16,0},{24,8},{1,17},{9,25},{17,1},{25,9},{2,18},{10... | collective-permute-start | bytes 1179656 | tf_op jit(solution)/shard_map/ppermute | solution.py:35

commit v13 on v11

--- a/solution.py
+++ b/solution.py
@@ -71,18 +71,14 @@
         outs[d][slots:, :] = (chance * chosen).astype(BF16)
 
 
-def cut_kernel(islands, pieces, spot, drift, *refs):
-    *blocks, sems = refs
+def cut_kernel(islands, pieces, spot, drift, *blocks):
     rows, columns = blocks[0].shape
-    pairs = []
     for d, first, count_rows, target, at_row in pieces:
         at = partner(spot[3], d, islands)
-        top = pl.multiple_of(lax.div(at, spot[4]) * rows, rows) + first
+        top = pl.multiple_of(lax.div(at, spot[4]) * rows + first, 32)
         left = pl.multiple_of(lax.rem(at, spot[4]) * columns, columns)
-        source = drift.at[0, 0, pl.ds(top, count_rows), pl.ds(left, columns)]
-        pairs.append((source, blocks[target].at[pl.ds(at_row, count_rows)]))
-    for copy in copy_all(sems, pairs):
-        copy.wait()
+        source = drift[0, 0, pl.ds(top, count_rows), pl.ds(left, columns)]
+        blocks[target][at_row : at_row + count_rows, :] = source
 
 
 def gather_kernel(count, *refs):
@@ -192,29 +188,35 @@
     block_out[...] = block[...]
 
 
-def update_kernel(entries, pieces, place, notes, momentum, *refs):
+def update_kernel(entries, pieces, cuts, place, notes, momentum, *refs):
     values = refs[: len(pieces)]
     new_momentum, outer_step, moved, step, in_sems, sems = refs[-6:]
     rows, columns = values[0].shape
+    size = rows // cuts
+    parts = [(n, m) for n in range(len(pieces)) for m in range(cuts)]
     spots, loads = [], []
-    for n, (d, first) in enumerate(pieces):
-        top = pl.multiple_of(pl.multiple_of(place[3 * d], 32) + first, 32)
+    for i, (n, m) in enumerate(parts):
+        d, first = pieces[n]
+        top = pl.multiple_of(pl.multiple_of(place[3 * d], 32) + first + m * size, 32)
         left = pl.multiple_of(place[3 * d + 1], columns)
-        spots.append((0, pl.ds(top, rows), pl.ds(left, columns)))
-        loads.append(pltpu.make_async_copy(momentum.at[spots[n]], moved.at[n], in_sems.at[n]))
+        spots.append((0, pl.ds(top, size), pl.ds(left, columns)))
+        here = moved.at[n, pl.ds(m * size, size)]
+        loads.append(pltpu.make_async_copy(momentum.at[spots[i]], here, in_sems.at[i]))
         loads[-1].start()
     square = jnp.sum(notes[...], axis=0)[:1, :1]
     clip = jnp.minimum(1.0, 0.25 * math.sqrt(entries) / jnp.sqrt(square + 1e-06))
     stored = []
-    for n, (d, first) in enumerate(pieces):
-        unit = notes[pl.ds(place[3 * d + 2], 1)][0, 1:2, :1]
-        clipped = (clip * unit) * values[n][...]
-        loads[n].wait()
-        fresh = 0.9 * moved[n] + clipped
-        moved[n] = fresh
-        step[n] = (0.7 * (clipped + 0.9 * fresh)).astype(BF16)
-        for k, (here, out) in enumerate(((moved, new_momentum), (step, outer_step))):
-            stored.append(pltpu.make_async_copy(here.at[n], out.at[spots[n]], sems.at[n, k]))
+    for i, (n, m) in enumerate(parts):
+        unit = notes[pl.ds(place[3 * pieces[n][0] + 2], 1)][0, 1:2, :1]
+        here = slice(m * size, (m + 1) * size)
+        clipped = (clip * unit) * values[n][here, :]
+        loads[i].wait()
+        fresh = 0.9 * moved[n, here, :] + clipped
+        moved[n, here, :] = fresh
+        step[n, here, :] = (0.7 * (clipped + 0.9 * fresh)).astype(BF16)
+        for k, (held, out) in enumerate(((moved, new_momentum), (step, outer_step))):
+            held = held.at[n, pl.ds(m * size, size)]
+            stored.append(pltpu.make_async_copy(held, out.at[spots[i]], sems.at[i, k]))
             stored[-1].start()
     for copy in stored:
         copy.wait()
@@ -270,11 +272,10 @@
     )(spot, slot_token, slot_count, slot_prob, tokens, token_grads)
     blocks = pl.pallas_call(
         lambda *refs: cut_kernel(islands, pieces, *refs),
-        in_specs=[SMEM, ANY],
+        in_specs=[SMEM, VMEM],
         out_specs=[VMEM] * len(steps),
         out_shape=[jax.ShapeDtypeStruct((rows, columns), BF16) for rows in block_rows],
-        scratch_shapes=[pltpu.SemaphoreType.DMA((len(pieces),))],
-        compiler_params=params(56),
+        compiler_params=params(16),
         name="cut_drift",
     )(spot, drift)
     arrived = [picked[0]] + [swap(picked[d], "expert", d) for d in range(1, experts)]
@@ -394,11 +395,11 @@
         place += [(at // across) * half, (at % across) * columns, source]
     place = jnp.stack(place).astype(jnp.int32)
     outs = []
-    for values, cost in ((values, 12), (last, 3)):
+    for values, cost, cuts in ((values, 12, 2), (last, 3, 2)):
         if not values:
             continue
         outs = pl.pallas_call(
-            functools.partial(update_kernel, entries, list(values)),
+            functools.partial(update_kernel, entries, list(values), cuts),
             in_specs=[SMEM, VMEM, ANY] + [VMEM] * len(values) + [ANY] * len(outs),
             out_specs=[ANY, ANY],
             out_shape=[
@@ -408,8 +409,8 @@
             scratch_shapes=[
                 pltpu.VMEM((len(values), *next(iter(values.values())).shape), F32),
                 pltpu.VMEM((len(values), *next(iter(values.values())).shape), BF16),
-                pltpu.SemaphoreType.DMA((len(values),)),
-                pltpu.SemaphoreType.DMA((len(values), 2)),
+                pltpu.SemaphoreType.DMA((len(values) * cuts,)),
+                pltpu.SemaphoreType.DMA((len(values) * cuts, 2)),
             ],
             input_output_aliases={3 + len(values) + n: n for n in range(len(outs))},
             cost_estimate=pl.CostEstimate(

time: 141 us -> 141 us (level)
  Pallas kernels: 28.5 us -> 24.6 us
    pallas_call x1, Pallas kernels: 4.2 us -> 0.83 us  [body(): pl.pallas_call(lambda *refs: cut_kernel(islands, pieces, *refs), in_specs...]
  transfers between devices with their start and end apart: 17 -> 17, of which waited for: 8 -> 8; matrix products, arithmetic and copies ran while one was open for 3% -> 3% of each run, Pallas kernels for 12% -> 9%
where the time goes in v13:
time: 141 us; the launch traced here: 140 us
  blocking collectives  40.7 us (29%)
  waiting for transfers between devices  39.1 us (28%)
  Pallas kernels  24.6 us (17%)
  starting transfers between devices  24.5 us (17%)
  other arithmetic  5.36 us (4%)
  local copies, waits for them, and re-layouts  3.72 us (3%)
  between operations  1.68 us (1%)
    ppermute x13, waiting for transfers between devices, swap(): lax.ppermute(value, axis, [(at, partner(at, step, size)) for at in range(...  26.2 us
    all_to_all x1, blocking collectives, body(): norms = lax.all_to_all(norms, AXES, split_axis=0, concat_axis=0, tiled=True)  21.3 us
    all_to_all x1, blocking collectives, body(): notes = lax.all_to_all(notes, AXES, split_axis=0, concat_axis=0, tiled=True)  19.4 us
    ppermute x13, starting transfers between devices, swap(): lax.ppermute(value, axis, [(at, partner(at, step, size)) for at in range(...  17.9 us
    ppermute x3, waiting for transfers between devices, send_features(): return lax.ppermute(turned, ('island', 'tensor'), pairs)  12.9 us
    pallas_call x2, Pallas kernels, body(): pl.pallas_call(functools.partial(update_kernel, entries, list(values), cu...  8.83 us
    pallas_call x1, Pallas kernels, body(): pl.pallas_call(lambda *refs: hidden_kernel(parts, across, *refs), in_spec...  5.43 us
    ppermute x3, starting transfers between devices, send_features(): return lax.ppermute(turned, ('island', 'tensor'), pairs)  5.03 us
  transfers between devices with their start and end apart: 17, of which 8 were waited for; matrix products, arithmetic and copies ran while one was open for 3% of the time, Pallas kernels for 9%

profile of v13, /device:TPU:0, one launch (start us, length us, event | category | flops | bytes accessed | tf_op | source)
XLA Modules:
  0.0 139.6 jit_solution(585286316131904330)
XLA Ops:
  0.7 0.6 stack.79.refs_0_
  1.3 3.6 %pick_slots.1 = (bf16[192,1024]{1,0:T(8,128)(2,1)}, bf16[192,1024]{1,0:T(8,128)(2,1)}, bf16[192,1024]{1,0:T(8,128)(2,1)}, bf16[192,1024]{1,0:T(8,128)(2,1)}) custom-call(s32[6]{0:T(128)} %stack.79.refs_0_, s32[1,1,4,96]{3,2,1,0:T(4,128)} %refs_1_.3, s32[1,1,4]{2,1,0:T(1,128)} %refs_2_.2, f32[1,1,4,96]{3,2,1,0:T(4,128)} %refs_3_.1, ...), custom_call_target="tpu_custom_call" | custom-call | tf_op jit(solution)/shard_map/pick_slots/pallas_call | solution.py:257
  4.8 3.1 %collective-permute-start = (bf16[192,1024]{1,0:T(8,128)(2,1)}, bf16[192,1024]{1,0:T(8,128)(2,1)S(1)}, u32[]{:S(2)}, u32[]{:S(2)}) collective-permute-start(bf16[192,1024]{1,0:T(8,128)(2,1)} %get-tuple-element.30), channel_id=1, source_target_pairs={{0,2},{2,0},{4,6},{6,4},{1,3},{3,1},{5,7},{7,5},{8,10},{10,8},{12,... | collective-permute-start | bytes 1179656 | tf_op jit(solution)/shard_map/ppermute | solution.py:35
  7.9 2.6 %collective-permute-start.1 = (bf16[192,1024]{1,0:T(8,128)(2,1)}, bf16[192,1024]{1,0:T(8,128)(2,1)S(1)}, u32[]{:S(2)}, u32[]{:S(2)}) collective-permute-start(bf16[192,1024]{1,0:T(8,128)(2,1)} %get-tuple-element.31), channel_id=1, source_target_pairs={{0,4},{2,6},{4,0},{6,2},{1,5},{3,7},{5,1},{7,3},{8,12},{10,14},{12... | collective-permute-start | bytes 1179656 | tf_op jit(solution)/shard_map/ppermute | solution.py:35
  10.5 0.0 collective-permute-start.2
  10.5 1.9 %copy-done = bf16[1,1,2048,768]{3,2,1,0:T(8,128)(2,1)S(1)} copy-done((bf16[1,1,2048,768]{3,2,1,0:T(8,128)(2,1)S(1)}, bf16[1,1,2048,768]{3,2,1,0:T(8,128)(2,1)}, u32[]{:S(2)}) %copy-start) | copy-done | bytes 3145752
  12.4 0.6 copy-done.4
  13.0 0.8 cut_drift.1
  13.9 1.8 %collective-permute-start.4 = (bf16[1536,384]{1,0:T(8,128)(2,1)S(1)}, bf16[1536,384]{1,0:T(8,128)(2,1)S(1)}, u32[]{:S(2)}, u32[]{:S(2)}) collective-permute-start(bf16[1536,384]{1,0:T(8,128)(2,1)S(1)} %get-tuple-element.36), channel_id=1, source_target_pairs={{0,8},{8,0},{16,24},{24,16},{1,9},{9,1},{17,25},{25,17},{2,10},{10... | collective-permute-start | bytes 3538952 | tf_op jit(solution)/shard_map/ppermute | solution.py:35
  15.6 1.5 %collective-permute-start.5 = (bf16[1536,384]{1,0:T(8,128)(2,1)S(1)}, bf16[1536,384]{1,0:T(8,128)(2,1)S(1)}, u32[]{:S(2)}, u32[]{:S(2)}) collective-permute-start(bf16[1536,384]{1,0:T(8,128)(2,1)S(1)} %get-tuple-element.37), channel_id=1, source_target_pairs={{0,16},{8,24},{16,0},{24,8},{1,17},{9,25},{17,1},{25,9},{2,18},{10... | collective-permute-start | bytes 3538952 | tf_op jit(solution)/shard_map/ppermute | solution.py:35
  17.2 0.0 copy-done.3
  17.2 0.1 own_parts.1
  17.3 7.7 %collective-permute-done.refs_1_ = bf16[192,1024]{1,0:T(8,128)(2,1)S(1)} collective-permute-done((bf16[192,1024]{1,0:T(8,128)(2,1)}, bf16[192,1024]{1,0:T(8,128)(2,1)S(1)}, u32[]{:S(2)}, u32[]{:S(2)}) %collective-permute-start) | collective-permute-done | bytes 393248 | tf_op jit(solution)/shard_map/ppermute | solution.py:35
  24.9 13.0 %collective-permute-done.1.refs_2_ = bf16[192,1024]{1,0:T(8,128)(2,1)S(1)} collective-permute-done((bf16[192,1024]{1,0:T(8,128)(2,1)}, bf16[192,1024]{1,0:T(8,128)(2,1)S(1)}, u32[]{:S(2)}, u32[]{:S(2)}) %collective-permute-start.1) | collective-permute-done | bytes 393248 | tf_op jit(solution)/shard_map/ppermute | solution.py:35
  37.9 0.0 collective-permute-done.2.refs_3_
  37.9 0.1 gather_slots.1.refs_3_.refs_0_
  38.1 0.0 copy-start.1
  38.1 0.0 copy-start.5
  38.1 0.1 collective-permute-start.3
  38.2 2.9 %collective-permute-done.4.refs_2_ = bf16[1536,384]{1,0:T(8,128)(2,1)S(1)} collective-permute-done((bf16[1536,384]{1,0:T(8,128)(2,1)S(1)}, bf16[1536,384]{1,0:T(8,128)(2,1)S(1)}, u32[]{:S(2)}, u32[]{:S(2)}) %collective-permute-start.4) | collective-permute-done | bytes 1179680 | tf_op jit(solution)/shard_map/ppermute | solution.py:35
  41.1 1.2 collective-permute-done.5.refs_3_
  42.3 0.7 join_blocks.1
  43.0 1.3 collective-permute-start.8
  44.3 1.3 collective-permute-start.7
  45.6 2.4 %collective-permute-start.6 = (bf16[1024,384]{1,0:T(8,128)(2,1)S(1)}, bf16[1024,384]{1,0:T(8,128)(2,1)S(1)}, u32[]{:S(2)}, u32[]{:S(2)}) collective-permute-start(bf16[1024,384]{1,0:T(8,128)(2,1)S(1)} %get-tuple-element.38.refs_3_), channel_id=1, source_target_pairs={{0,8},{8,0},{17,25},{25,17},{2,10},{10,2},{19,27},{27,19},{4,12},{... | collective-permute-start | bytes 2359304 | tf_op jit(solution)/shard_map/ppermute | solution.py:322
  48.0 0.0 collective-permute-done.3.refs_4_
  48.0 0.0 copy-done.2
  48.0 0.0 copy-done.1
  48.1 0.0 copy-done.5
  48.1 5.4 %hidden_grads.1 = (bf16[2,384,384]{2,1,0:T(8,128)(2,1)S(1)}, f32[32,8,128]{2,1,0:T(8,128)S(1)}) custom-call(s32[6]{0:T(128)S(1)} %copy-done.5, bf16[1,1,2048,768]{3,2,1,0:T(8,128)(2,1)S(1)} %copy-done.1, bf16[1,1,768,2048]{3,2,1,0:T(8,128)(2,1)S(1)} %copy-done.2, bf16[768,1024]{1,0:T(8,128)(2,1)S(1)} %gather_slots.1.refs_3_.refs_0_, ...), custom_call_target="tpu_custom_call" | custom-call | tf_op jit(solution)/shard_map/hidden_grads/pallas_call | solution.py:337
  53.5 12.3 %collective-permute-done.8.refs_6_ = bf16[1024,384]{1,0:T(8,128)(2,1)S(1)} collective-permute-done((bf16[1024,384]{1,0:T(8,128)(2,1)S(1)}, bf16[1024,384]{1,0:T(8,128)(2,1)S(1)}, u32[]{:S(2)}, u32[]{:S(2)}) %collective-permute-start.8) | collective-permute-done | bytes 786464 | tf_op jit(solution)/shard_map/ppermute | solution.py:322
  65.8 0.5 collective-permute-done.7.refs_5_
  66.4 0.0 collective-permute-done.6.refs_4_
  66.4 1.0 hand_on.1
  67.4 1.5 %collective-permute-start.9 = (bf16[4,1024,384]{2,1,0:T(8,128)(2,1)S(1)}, bf16[4,1024,384]{2,1,0:T(8,128)(2,1)S(1)}, u32[]{:S(2)}, u32[]{:S(2)}) collective-permute-start(bf16[4,1024,384]{2,1,0:T(8,128)(2,1)S(1)} %get-tuple-element.43.refs_3_), channel_id=1, source_target_pairs={{0,1},{8,9},{17,16},{25,24},{2,3},{10,11},{19,18},{27,26},{4,5},{1... | collective-permute-start | bytes 9437192 | tf_op jit(solution)/shard_map/ppermute | solution.py:331
  68.9 1.1 collective-permute-start.10
  69.9 0.0 collective-permute-start.11
  69.9 2.5 %collective-permute-start.12 = (bf16[384,384]{1,0:T(8,128)(2,1)S(1)}, bf16[384,384]{1,0:T(8,128)(2,1)S(1)}, u32[]{:S(2)}, u32[]{:S(2)}) collective-permute-start(bf16[384,384]{1,0:T(8,128)(2,1)S(1)} %get-tuple-element.47), channel_id=1, source_target_pairs={{0,24},{8,16},{16,8},{24,0},{1,25},{9,17},{17,9},{25,1},{2,26},{10... | collective-permute-start | bytes 884744 | tf_op jit(solution)/shard_map/ppermute | solution.py:35
  72.4 21.3 %all_to_all.10.refs_1_ = f32[32,8,128]{2,1,0:T(8,128)S(1)} all-to-all(f32[32,8,128]{2,1,0:T(8,128)S(1)} %get-tuple-element.41), channel_id=1, replica_groups=mesh['island'=4,'expert'=4,'tensor'=2] {'island','expert','tensor'}, dimensions={0} | all-to-all | bytes 262144 | tf_op jit(solution)/shard_map/all_to_all | solution.py:365
  93.7 0.0 collective-permute-done.12.refs_8_
  93.7 0.0 collective-permute-done.10.refs_6_
  93.7 0.0 collective-permute-done.11.refs_7_
  93.7 0.0 collective-permute-done.9.refs_4_
  93.7 4.1 %average_block.1 = (f32[1024,384]{1,0:T(8,128)S(1)}, f32[32,8,128]{2,1,0:T(8,128)S(1)}) custom-call(s32[6]{0:T(128)S(1)} %copy-done.5, f32[32,8,128]{2,1,0:T(8,128)S(1)} %all_to_all.10.refs_1_, f32[1024,384]{1,0:T(8,128)S(1)} %get-tuple-element.42.refs_2_, bf16[4,1024,384]{2,1,0:T(8,128)(2,1)S(1)} %get-tuple-element.43.refs_3_, ...), custom_call_target="tpu_custom_call" | custom-call | tf_op jit(solution)/shard_map/average_block/pallas_call | solution.py:368
  97.8 0.1 convert_element_type.22
  97.9 1.8 %collective-permute-start.15 = (f16[1024,384]{1,0:T(8,128)(2,1)S(1)}, f16[1024,384]{1,0:T(8,128)(2,1)S(1)}, u32[]{:S(2)}, u32[]{:S(2)}) collective-permute-start(f16[1024,384]{1,0:T(8,128)(2,1)S(1)} %convert_element_type.22), channel_id=1, source_target_pairs={{0,16},{8,24},{16,0},{24,8},{1,17},{9,25},{17,1},{25,9},{2,18},{10... | collective-permute-start | bytes 2359304 | tf_op jit(solution)/shard_map/ppermute | solution.py:35
  99.7 1.0 collective-permute-start.13
  100.7 19.4 %all_to_all.11.notes = f32[32,8,128]{2,1,0:T(8,128)S(1)} all-to-all(f32[32,8,128]{2,1,0:T(8,128)S(1)} %get-tuple-element.48), channel_id=1, replica_groups=mesh['island'=4,'expert'=4,'tensor'=2] {'island','expert','tensor'}, dimensions={0} | all-to-all | bytes 262144 | tf_op jit(solution)/shard_map/all_to_all | solution.py:380
  120.2 0.5 slice.13
  121.3 0.0 collective-permute-done.15
  121.3 0.9 slice_add_fusion
  122.2 1.2 collective-permute-start.16
  123.4 0.0 collective-permute-done.13
  123.4 0.9 slice_add_fusion.1
  124.3 1.3 collective-permute-start.14
  125.6 0.1 stack.72.place
  125.7 1.3 convert_element_type.28.refs_2_
  127.0 0.1 convert_element_type.27.refs_1_
  127.1 5.7 %update_pieces.2 = (f32[1,2048,768]{2,1,0:T(8,128)}, bf16[1,2048,768]{2,1,0:T(8,128)(2,1)}) custom-call(s32[12]{0:T(128)S(1)} %stack.72.place, f32[32,8,128]{2,1,0:T(8,128)S(1)} %all_to_all.11.notes, f32[1,2048,768]{2,1,0:T(8,128)} %momentum.3, f32[1024,384]{1,0:T(8,128)S(1)} %get-tuple-element.49.refs_0_, f32[1024,384]{1,0:T(8,128)S(1)} %convert_element_type.27.refs_1_, ...), custom_call_target="tpu_custom_call" | custom-call | bytes 18874368 | tf_op jit(solution)/shard_map/update_pieces/pallas_call | solution.py:401
  132.8 0.8 collective-permute-done.16
  133.7 1.0 convert_element_type.26.refs_1_
  134.7 0.6 collective-permute-done.14
  135.3 1.0 convert_element_type.25.refs_0_
  136.3 3.1 %update_pieces.3 = (f32[1,2048,768]{2,1,0:T(8,128)}, bf16[1,2048,768]{2,1,0:T(8,128)(2,1)}) custom-call(s32[12]{0:T(128)S(1)} %stack.72.place, f32[32,8,128]{2,1,0:T(8,128)S(1)} %all_to_all.11.notes, f32[1,2048,768]{2,1,0:T(8,128)} %momentum.3, f32[512,384]{1,0:T(8,128)S(1)} %convert_element_type.25.refs_0_, ...), custom_call_target="tpu_custom_call", output_to_operand_aliasing={{0}: (5, {}), {1}: (6, {})} | custom-call | bytes 4718592 | tf_op jit(solution)/shard_map/update_pieces/pallas_call | solution.py:401
  (4 shorter events, 0.0 us)
Async XLA Ops:
  4.8 20.1 %collective-permute-start = (bf16[192,1024]{1,0:T(8,128)(2,1)}, bf16[192,1024]{1,0:T(8,128)(2,1)S(1)}, u32[]{:S(2)}, u32[]{:S(2)}) collective-permute-start(bf16[192,1024]{1,0:T(8,128)(2,1)} %get-tuple-element.30), channel_id=1, source_target_pairs={{0,2},{2,0},{4,6},{6,4},{1,3},{3,1},{5,7},{7,5},{8,10},{10,8},{12,... | collective-permute-start | bytes 1179656 | tf_op jit(solution)/shard_map/ppermute | solution.py:35
  7.9 30.0 %collective-permute-start.1 = (bf16[192,1024]{1,0:T(8,128)(2,1)}, bf16[192,1024]{1,0:T(8,128)(2,1)S(1)}, u32[]{:S(2)}, u32[]{:S(2)}) collective-permute-start(bf16[192,1024]{1,0:T(8,128)(2,1)} %get-tuple-element.31), channel_id=1, source_target_pairs={{0,4},{2,6},{4,0},{6,2},{1,5},{3,7},{5,1},{7,3},{8,12},{10,14},{12... | collective-permute-start | bytes 1179656 | tf_op jit(solution)/shard_map/ppermute | solution.py:35
  10.5 27.4 %collective-permute-start.2 = (bf16[192,1024]{1,0:T(8,128)(2,1)}, bf16[192,1024]{1,0:T(8,128)(2,1)S(1)}, u32[]{:S(2)}, u32[]{:S(2)}) collective-permute-start(bf16[192,1024]{1,0:T(8,128)(2,1)} %get-tuple-element.32), channel_id=1, source_target_pairs={{0,6},{2,4},{4,2},{6,0},{1,7},{3,5},{5,3},{7,1},{8,14},{10,12},{12... | collective-permute-start | bytes 1179656 | tf_op jit(solution)/shard_map/ppermute | solution.py:35
  10.5 1.9 %copy-start = (bf16[1,1,2048,768]{3,2,1,0:T(8,128)(2,1)S(1)}, bf16[1,1,2048,768]{3,2,1,0:T(8,128)(2,1)}, u32[]{:S(2)}) copy-start(bf16[1,1,2048,768]{3,2,1,0:T(8,128)(2,1)} %refs_1_.4) | copy-start | bytes 9437188
  12.4 0.6 copy-start.4
  13.0 4.1 %copy-start.3 = (bf16[192,1024]{1,0:T(8,128)(2,1)S(1)}, bf16[192,1024]{1,0:T(8,128)(2,1)}, u32[]{:S(2)}) copy-start(bf16[192,1024]{1,0:T(8,128)(2,1)} %get-tuple-element.27.slots) | copy-start | bytes 1179652
  13.9 27.2 %collective-permute-start.4 = (bf16[1536,384]{1,0:T(8,128)(2,1)S(1)}, bf16[1536,384]{1,0:T(8,128)(2,1)S(1)}, u32[]{:S(2)}, u32[]{:S(2)}) collective-permute-start(bf16[1536,384]{1,0:T(8,128)(2,1)S(1)} %get-tuple-element.36), channel_id=1, source_target_pairs={{0,8},{8,0},{16,24},{24,16},{1,9},{9,1},{17,25},{25,17},{2,10},{10... | collective-permute-start | bytes 3538952 | tf_op jit(solution)/shard_map/ppermute | solution.py:35
  15.6 26.7 %collective-permute-start.5 = (bf16[1536,384]{1,0:T(8,128)(2,1)S(1)}, bf16[1536,384]{1,0:T(8,128)(2,1)S(1)}, u32[]{:S(2)}, u32[]{:S(2)}) collective-permute-start(bf16[1536,384]{1,0:T(8,128)(2,1)S(1)} %get-tuple-element.37), channel_id=1, source_target_pairs={{0,16},{8,24},{16,0},{24,8},{1,17},{9,25},{17,1},{25,9},{2,18},{10... | collective-permute-start | bytes 3538952 | tf_op jit(solution)/shard_map/ppermute | solution.py:35
  37.9 10.1 %copy-start.2 = (bf16[1,1,768,2048]{3,2,1,0:T(8,128)(2,1)S(1)}, bf16[1,1,768,2048]{3,2,1,0:T(8,128)(2,1)}, u32[]{:S(2)}) copy-start(bf16[1,1,768,2048]{3,2,1,0:T(8,128)(2,1)} %refs_2_.3) | copy-start | bytes 9437188
  38.1 10.0 %copy-start.1 = (bf16[1,1,2048,768]{3,2,1,0:T(8,128)(2,1)S(1)}, bf16[1,1,2048,768]{3,2,1,0:T(8,128)(2,1)}, u32[]{:S(2)}) copy-start(bf16[1,1,2048,768]{3,2,1,0:T(8,128)(2,1)} %refs_1_.5) | copy-start | bytes 9437188
  38.1 10.0 %copy-start.5 = (s32[6]{0:T(128)S(1)}, s32[6]{0:T(128)}, u32[]{:S(2)}) copy-start(s32[6]{0:T(128)} %stack.79.refs_0_) | copy-start | bytes 76
  38.1 10.0 %collective-permute-start.3 = (bf16[768,1024]{1,0:T(8,128)(2,1)S(1)}, bf16[768,1024]{1,0:T(8,128)(2,1)S(1)}, u32[]{:S(2)}, u32[]{:S(2)}) collective-permute-start(bf16[768,1024]{1,0:T(8,128)(2,1)S(1)} %gather_slots.1.refs_3_.refs_0_), channel_id=1, source_target_pairs={{0,1},{1,0},{2,3},{3,2},{4,5},{5,4},{6,7},{7,6},{8,9},{9,8},{10,11... | collective-permute-start | bytes 4718600 | tf_op jit(solution)/shard_map/ppermute | solution.py:35
  43.0 22.9 %collective-permute-start.8 = (bf16[1024,384]{1,0:T(8,128)(2,1)S(1)}, bf16[1024,384]{1,0:T(8,128)(2,1)S(1)}, u32[]{:S(2)}, u32[]{:S(2)}) collective-permute-start(bf16[1024,384]{1,0:T(8,128)(2,1)S(1)} %get-tuple-element.38.refs_3_), channel_id=1, source_target_pairs={{1,25},{9,17},{16,8},{24,0},{3,27},{11,19},{18,10},{26,2},{5,29},{... | collective-permute-start | bytes 2359304 | tf_op jit(solution)/shard_map/ppermute | solution.py:322
  44.3 22.1 %collective-permute-start.7 = (bf16[1024,384]{1,0:T(8,128)(2,1)S(1)}, bf16[1024,384]{1,0:T(8,128)(2,1)S(1)}, u32[]{:S(2)}, u32[]{:S(2)}) collective-permute-start(bf16[1024,384]{1,0:T(8,128)(2,1)S(1)} %get-tuple-element.38.refs_3_), channel_id=1, source_target_pairs={{1,17},{9,25},{16,0},{24,8},{3,19},{11,27},{18,2},{26,10},{5,21},{... | collective-permute-start | bytes 2359304 | tf_op jit(solution)/shard_map/ppermute | solution.py:322
  45.6 20.8 %collective-permute-start.6 = (bf16[1024,384]{1,0:T(8,128)(2,1)S(1)}, bf16[1024,384]{1,0:T(8,128)(2,1)S(1)}, u32[]{:S(2)}, u32[]{:S(2)}) collective-permute-start(bf16[1024,384]{1,0:T(8,128)(2,1)S(1)} %get-tuple-element.38.refs_3_), channel_id=1, source_target_pairs={{0,8},{8,0},{17,25},{25,17},{2,10},{10,2},{19,27},{27,19},{4,12},{... | collective-permute-start | bytes 2359304 | tf_op jit(solution)/shard_map/ppermute | solution.py:322
  67.4 26.3 %collective-permute-start.9 = (bf16[4,1024,384]{2,1,0:T(8,128)(2,1)S(1)}, bf16[4,1024,384]{2,1,0:T(8,128)(2,1)S(1)}, u32[]{:S(2)}, u32[]{:S(2)}) collective-permute-start(bf16[4,1024,384]{2,1,0:T(8,128)(2,1)S(1)} %get-tuple-element.43.refs_3_), channel_id=1, source_target_pairs={{0,1},{8,9},{17,16},{25,24},{2,3},{10,11},{19,18},{27,26},{4,5},{1... | collective-permute-start | bytes 9437192 | tf_op jit(solution)/shard_map/ppermute | solution.py:331
  68.9 24.8 %collective-permute-start.10 = (bf16[896,384]{1,0:T(8,128)(2,1)S(1)}, bf16[896,384]{1,0:T(8,128)(2,1)S(1)}, u32[]{:S(2)}, u32[]{:S(2)}) collective-permute-start(bf16[896,384]{1,0:T(8,128)(2,1)S(1)} %get-tuple-element.45), channel_id=1, source_target_pairs={{0,8},{8,0},{16,24},{24,16},{1,9},{9,1},{17,25},{25,17},{2,10},{10... | collective-permute-start | bytes 2064392 | tf_op jit(solution)/shard_map/ppermute | solution.py:35
  69.9 23.8 %collective-permute-start.11 = (bf16[896,384]{1,0:T(8,128)(2,1)S(1)}, bf16[896,384]{1,0:T(8,128)(2,1)S(1)}, u32[]{:S(2)}, u32[]{:S(2)}) collective-permute-start(bf16[896,384]{1,0:T(8,128)(2,1)S(1)} %get-tuple-element.46), channel_id=1, source_target_pairs={{0,16},{8,24},{16,0},{24,8},{1,17},{9,25},{17,1},{25,9},{2,18},{10... | collective-permute-start | bytes 2064392 | tf_op jit(solution)/shard_map/ppermute | solution.py:35
  69.9 23.8 %collective-permute-start.12 = (bf16[384,384]{1,0:T(8,128)(2,1)S(1)}, bf16[384,384]{1,0:T(8,128)(2,1)S(1)}, u32[]{:S(2)}, u32[]{:S(2)}) collective-permute-start(bf16[384,384]{1,0:T(8,128)(2,1)S(1)} %get-tuple-element.47), channel_id=1, source_target_pairs={{0,24},{8,16},{16,8},{24,0},{1,25},{9,17},{17,9},{25,1},{2,26},{10... | collective-permute-start | bytes 884744 | tf_op jit(solution)/shard_map/ppermute | solution.py:35
  97.9 23.4 %collective-permute-start.15 = (f16[1024,384]{1,0:T(8,128)(2,1)S(1)}, f16[1024,384]{1,0:T(8,128)(2,1)S(1)}, u32[]{:S(2)}, u32[]{:S(2)}) collective-permute-start(f16[1024,384]{1,0:T(8,128)(2,1)S(1)} %convert_element_type.22), channel_id=1, source_target_pairs={{0,16},{8,24},{16,0},{24,8},{1,17},{9,25},{17,1},{25,9},{2,18},{10... | collective-permute-start | bytes 2359304 | tf_op jit(solution)/shard_map/ppermute | solution.py:35
  99.7 23.7 %collective-permute-start.13 = (f16[1024,384]{1,0:T(8,128)(2,1)S(1)}, f16[1024,384]{1,0:T(8,128)(2,1)S(1)}, u32[]{:S(2)}, u32[]{:S(2)}) collective-permute-start(f16[1024,384]{1,0:T(8,128)(2,1)S(1)} %convert_element_type.22), channel_id=1, source_target_pairs={{0,8},{8,0},{16,24},{24,16},{1,9},{9,1},{17,25},{25,17},{2,10},{10... | collective-permute-start | bytes 2359304 | tf_op jit(solution)/shard_map/ppermute | solution.py:35
  122.2 11.5 %collective-permute-start.16 = (f16[512,384]{1,0:T(8,128)(2,1)}, f16[512,384]{1,0:T(8,128)(2,1)}, u32[]{:S(2)}, u32[]{:S(2)}) collective-permute-start(f16[512,384]{1,0:T(8,128)(2,1)} %slice_add_fusion), channel_id=1, source_target_pairs={{0,8},{8,0},{16,24},{24,16},{1,9},{9,1},{17,25},{25,17},{2,10},{10... | collective-permute-start | bytes 1179656 | tf_op jit(solution)/shard_map/ppermute | solution.py:35
  124.3 11.0 %collective-permute-start.14 = (f16[512,384]{1,0:T(8,128)(2,1)}, f16[512,384]{1,0:T(8,128)(2,1)}, u32[]{:S(2)}, u32[]{:S(2)}) collective-permute-start(f16[512,384]{1,0:T(8,128)(2,1)} %slice_add_fusion.1), channel_id=1, source_target_pairs={{0,16},{8,24},{16,0},{24,8},{1,17},{9,25},{17,1},{25,9},{2,18},{10... | collective-permute-start | bytes 1179656 | tf_op jit(solution)/shard_map/ppermute | solution.py:35

commit v14 on v13

--- a/solution.py
+++ b/solution.py
@@ -71,14 +71,18 @@
         outs[d][slots:, :] = (chance * chosen).astype(BF16)
 
 
-def cut_kernel(islands, pieces, spot, drift, *blocks):
+def cut_kernel(islands, pieces, spot, drift, *refs):
+    *blocks, sems = refs
     rows, columns = blocks[0].shape
+    pairs = []
     for d, first, count_rows, target, at_row in pieces:
         at = partner(spot[3], d, islands)
         top = pl.multiple_of(lax.div(at, spot[4]) * rows + first, 32)
         left = pl.multiple_of(lax.rem(at, spot[4]) * columns, columns)
-        source = drift[0, 0, pl.ds(top, count_rows), pl.ds(left, columns)]
-        blocks[target][at_row : at_row + count_rows, :] = source
+        source = drift.at[0, 0, pl.ds(top, count_rows), pl.ds(left, columns)]
+        pairs.append((source, blocks[target].at[pl.ds(at_row, count_rows)]))
+    for copy in copy_all(sems, pairs):
+        copy.wait()
 
 
 def gather_kernel(count, *refs):
@@ -272,10 +276,11 @@
     )(spot, slot_token, slot_count, slot_prob, tokens, token_grads)
     blocks = pl.pallas_call(
         lambda *refs: cut_kernel(islands, pieces, *refs),
-        in_specs=[SMEM, VMEM],
+        in_specs=[SMEM, ANY],
         out_specs=[VMEM] * len(steps),
         out_shape=[jax.ShapeDtypeStruct((rows, columns), BF16) for rows in block_rows],
-        compiler_params=params(16),
+        scratch_shapes=[pltpu.SemaphoreType.DMA((len(pieces),))],
+        compiler_params=params(50),
         name="cut_drift",
     )(spot, drift)
     arrived = [picked[0]] + [swap(picked[d], "expert", d) for d in range(1, experts)]
@@ -385,9 +390,13 @@
     for d in steps:
         values[d, 0] = swap(sent, "island", d)
     if handed:
-        nothing = jnp.minimum(notes[0, 1, 0], 0.0).astype(WIRE)
-        last[3, 0] = swap(values[1, 0][:handed] + nothing, "island", 2)
-        last[3, handed] = swap(values[2, 0][handed:] + nothing, "island", 1)
+        nothing = jnp.where(notes[0, 1, 0] < 0, handed, 0)
+
+        def rows_of(value, first):
+            return lax.dynamic_slice(value, (first + nothing, 0), (handed, columns))
+
+        last[3, 0] = swap(rows_of(values[1, 0], 0), "island", 2)
+        last[3, handed] = swap(rows_of(values[2, 0], handed), "island", 1)
     place = []
     for d in range(islands):
         at = origin(island, d, islands)

time: 141 us -> 142 us (level)
  Pallas kernels: 24.6 us -> 26.2 us
    unnamed x12 -> x8, local copies, waits for them, and re-layouts: 2.52 us -> 0.63 us
    add x2 -> x0, other arithmetic: 1.75 us -> none  [the longest x1 0.88 us: body(): last[3, 0] = swap(values[1, 0][:handed] + nothing, 'island', 2)]
    dynamic_slice x0 -> x2, local copies, waits for them, and re-layouts: none -> 1.71 us  [rows_of(): return lax.dynamic_slice(value, (first + nothing, 0), (handed, columns))]
    pallas_call x1, Pallas kernels: 0.83 us -> 2.42 us  [body(): pl.pallas_call(lambda *refs: cut_kernel(islands, pieces, *refs), in_specs...]
  transfers between devices with their start and end apart: 17 -> 17, of which waited for: 8 -> 8; matrix products, arithmetic and copies ran while one was open for 3% -> 3% of each run, Pallas kernels for 9% -> 10%
where the time goes in v14:
time: 142 us; the launch traced here: 140 us
  blocking collectives  40.9 us (29%)
  waiting for transfers between devices  39.1 us (28%)
  Pallas kernels  26.2 us (18%)
  starting transfers between devices  24.4 us (17%)
  other arithmetic  4.47 us (3%)
  local copies, waits for them, and re-layouts  3.55 us (2%)
  between operations  1.66 us (1%)
    ppermute x13, waiting for transfers between devices, swap(): lax.ppermute(value, axis, [(at, partner(at, step, size)) for at in range(...  26.3 us
    all_to_all x1, blocking collectives, body(): norms = lax.all_to_all(norms, AXES, split_axis=0, concat_axis=0, tiled=True)  21.3 us
    all_to_all x1, blocking collectives, body(): notes = lax.all_to_all(notes, AXES, split_axis=0, concat_axis=0, tiled=True)  19.6 us
    ppermute x13, starting transfers between devices, swap(): lax.ppermute(value, axis, [(at, partner(at, step, size)) for at in range(...  17.9 us
    ppermute x3, waiting for transfers between devices, send_features(): return lax.ppermute(turned, ('island', 'tensor'), pairs)  12.9 us
    pallas_call x2, Pallas kernels, body(): pl.pallas_call(functools.partial(update_kernel, entries, list(values), cu...  8.83 us
    pallas_call x1, Pallas kernels, body(): pl.pallas_call(lambda *refs: hidden_kernel(parts, across, *refs), in_spec...  5.43 us
    ppermute x3, starting transfers between devices, send_features(): return lax.ppermute(turned, ('island', 'tensor'), pairs)  5.02 us
  transfers between devices with their start and end apart: 17, of which 8 were waited for; matrix products, arithmetic and copies ran while one was open for 3% of the time, Pallas kernels for 10%

profile of v14, /device:TPU:0, one launch (start us, length us, event | category | flops | bytes accessed | tf_op | source)
XLA Modules:
  0.0 140.3 jit_solution(3519415940214179290)
XLA Ops:
  0.7 0.6 stack.79.refs_0_
  1.3 3.6 %pick_slots.1 = (bf16[192,1024]{1,0:T(8,128)(2,1)}, bf16[192,1024]{1,0:T(8,128)(2,1)}, bf16[192,1024]{1,0:T(8,128)(2,1)}, bf16[192,1024]{1,0:T(8,128)(2,1)}) custom-call(s32[6]{0:T(128)} %stack.79.refs_0_, s32[1,1,4,96]{3,2,1,0:T(4,128)} %refs_1_.3, s32[1,1,4]{2,1,0:T(1,128)} %refs_2_.2, f32[1,1,4,96]{3,2,1,0:T(4,128)} %refs_3_.1, ...), custom_call_target="tpu_custom_call" | custom-call | tf_op jit(solution)/shard_map/pick_slots/pallas_call | solution.py:261
  4.8 0.0 copy-start.2
  4.9 3.1 %collective-permute-start = (bf16[192,1024]{1,0:T(8,128)(2,1)}, bf16[192,1024]{1,0:T(8,128)(2,1)S(1)}, u32[]{:S(2)}, u32[]{:S(2)}) collective-permute-start(bf16[192,1024]{1,0:T(8,128)(2,1)} %get-tuple-element.30), channel_id=1, source_target_pairs={{0,2},{2,0},{4,6},{6,4},{1,3},{3,1},{5,7},{7,5},{8,10},{10,8},{12,... | collective-permute-start | bytes 1179656 | tf_op jit(solution)/shard_map/ppermute | solution.py:35
  7.9 2.6 %collective-permute-start.1 = (bf16[192,1024]{1,0:T(8,128)(2,1)}, bf16[192,1024]{1,0:T(8,128)(2,1)S(1)}, u32[]{:S(2)}, u32[]{:S(2)}) collective-permute-start(bf16[192,1024]{1,0:T(8,128)(2,1)} %get-tuple-element.31), channel_id=1, source_target_pairs={{0,4},{2,6},{4,0},{6,2},{1,5},{3,7},{5,1},{7,3},{8,12},{10,14},{12... | collective-permute-start | bytes 1179656 | tf_op jit(solution)/shard_map/ppermute | solution.py:35
  10.5 0.0 collective-permute-start.2
  10.5 0.0 copy-start.3
  10.5 0.6 copy-done.3
  11.1 2.4 %cut_drift.1 = (bf16[1024,384]{1,0:T(8,128)(2,1)S(1)}, bf16[1536,384]{1,0:T(8,128)(2,1)S(1)}, bf16[1536,384]{1,0:T(8,128)(2,1)S(1)}) custom-call(s32[6]{0:T(128)S(1)} %copy-done.3, bf16[1,1,2048,768]{3,2,1,0:T(8,128)(2,1)} %refs_1_.4), custom_call_target="tpu_custom_call" | custom-call | tf_op jit(solution)/shard_map/cut_drift/pallas_call | solution.py:277
  13.6 1.8 %collective-permute-start.4 = (bf16[1536,384]{1,0:T(8,128)(2,1)S(1)}, bf16[1536,384]{1,0:T(8,128)(2,1)S(1)}, u32[]{:S(2)}, u32[]{:S(2)}) collective-permute-start(bf16[1536,384]{1,0:T(8,128)(2,1)S(1)} %get-tuple-element.36), channel_id=1, source_target_pairs={{0,8},{8,0},{16,24},{24,16},{1,9},{9,1},{17,25},{25,17},{2,10},{10... | collective-permute-start | bytes 3538952 | tf_op jit(solution)/shard_map/ppermute | solution.py:35
  15.4 1.5 %collective-permute-start.5 = (bf16[1536,384]{1,0:T(8,128)(2,1)S(1)}, bf16[1536,384]{1,0:T(8,128)(2,1)S(1)}, u32[]{:S(2)}, u32[]{:S(2)}) collective-permute-start(bf16[1536,384]{1,0:T(8,128)(2,1)S(1)} %get-tuple-element.37), channel_id=1, source_target_pairs={{0,16},{8,24},{16,0},{24,8},{1,17},{9,25},{17,1},{25,9},{2,18},{10... | collective-permute-start | bytes 3538952 | tf_op jit(solution)/shard_map/ppermute | solution.py:35
  16.9 0.0 copy-done.2
  16.9 0.1 own_parts.1
  17.0 8.0 %collective-permute-done.refs_1_ = bf16[192,1024]{1,0:T(8,128)(2,1)S(1)} collective-permute-done((bf16[192,1024]{1,0:T(8,128)(2,1)}, bf16[192,1024]{1,0:T(8,128)(2,1)S(1)}, u32[]{:S(2)}, u32[]{:S(2)}) %collective-permute-start) | collective-permute-done | bytes 393248 | tf_op jit(solution)/shard_map/ppermute | solution.py:35
  24.9 13.0 %collective-permute-done.1.refs_2_ = bf16[192,1024]{1,0:T(8,128)(2,1)S(1)} collective-permute-done((bf16[192,1024]{1,0:T(8,128)(2,1)}, bf16[192,1024]{1,0:T(8,128)(2,1)S(1)}, u32[]{:S(2)}, u32[]{:S(2)}) %collective-permute-start.1) | collective-permute-done | bytes 393248 | tf_op jit(solution)/shard_map/ppermute | solution.py:35
  38.0 0.0 collective-permute-done.2.refs_3_
  38.0 0.0 copy-start.1
  38.0 0.1 gather_slots.1.refs_3_.refs_0_
  38.1 0.0 copy-start
  38.1 0.1 collective-permute-start.3
  38.2 2.6 %collective-permute-done.4.refs_2_ = bf16[1536,384]{1,0:T(8,128)(2,1)S(1)} collective-permute-done((bf16[1536,384]{1,0:T(8,128)(2,1)S(1)}, bf16[1536,384]{1,0:T(8,128)(2,1)S(1)}, u32[]{:S(2)}, u32[]{:S(2)}) %collective-permute-start.4) | collective-permute-done | bytes 1179680 | tf_op jit(solution)/shard_map/ppermute | solution.py:35
  40.8 1.2 collective-permute-done.5.refs_3_
  42.0 0.7 join_blocks.1
  42.7 1.3 collective-permute-start.8
  44.0 1.3 collective-permute-start.7
  45.3 2.4 %collective-permute-start.6 = (bf16[1024,384]{1,0:T(8,128)(2,1)S(1)}, bf16[1024,384]{1,0:T(8,128)(2,1)S(1)}, u32[]{:S(2)}, u32[]{:S(2)}) collective-permute-start(bf16[1024,384]{1,0:T(8,128)(2,1)S(1)} %get-tuple-element.38.refs_3_), channel_id=1, source_target_pairs={{0,8},{8,0},{17,25},{25,17},{2,10},{10,2},{19,27},{27,19},{4,12},{... | collective-permute-start | bytes 2359304 | tf_op jit(solution)/shard_map/ppermute | solution.py:327
  47.7 0.0 collective-permute-done.3.refs_4_
  47.8 0.0 copy-done.1
  47.8 0.0 copy-done
  47.8 5.4 %hidden_grads.1 = (bf16[2,384,384]{2,1,0:T(8,128)(2,1)S(1)}, f32[32,8,128]{2,1,0:T(8,128)S(1)}) custom-call(s32[6]{0:T(128)S(1)} %copy-done.3, bf16[1,1,2048,768]{3,2,1,0:T(8,128)(2,1)S(1)} %copy-done, bf16[1,1,768,2048]{3,2,1,0:T(8,128)(2,1)S(1)} %copy-done.1, bf16[768,1024]{1,0:T(8,128)(2,1)S(1)} %gather_slots.1.refs_3_.refs_0_, ...), custom_call_target="tpu_custom_call" | custom-call | tf_op jit(solution)/shard_map/hidden_grads/pallas_call | solution.py:342
  53.2 12.3 %collective-permute-done.8.refs_6_ = bf16[1024,384]{1,0:T(8,128)(2,1)S(1)} collective-permute-done((bf16[1024,384]{1,0:T(8,128)(2,1)S(1)}, bf16[1024,384]{1,0:T(8,128)(2,1)S(1)}, u32[]{:S(2)}, u32[]{:S(2)}) %collective-permute-start.8) | collective-permute-done | bytes 786464 | tf_op jit(solution)/shard_map/ppermute | solution.py:327
  65.6 0.5 collective-permute-done.7.refs_5_
  66.1 0.0 collective-permute-done.6.refs_4_
  66.1 1.0 hand_on.1
  67.1 1.5 %collective-permute-start.9 = (bf16[4,1024,384]{2,1,0:T(8,128)(2,1)S(1)}, bf16[4,1024,384]{2,1,0:T(8,128)(2,1)S(1)}, u32[]{:S(2)}, u32[]{:S(2)}) collective-permute-start(bf16[4,1024,384]{2,1,0:T(8,128)(2,1)S(1)} %get-tuple-element.43.refs_3_), channel_id=1, source_target_pairs={{0,1},{8,9},{17,16},{25,24},{2,3},{10,11},{19,18},{27,26},{4,5},{1... | collective-permute-start | bytes 9437192 | tf_op jit(solution)/shard_map/ppermute | solution.py:336
  68.6 1.1 collective-permute-start.10
  69.6 0.0 collective-permute-start.11
  69.7 2.5 %collective-permute-start.12 = (bf16[384,384]{1,0:T(8,128)(2,1)S(1)}, bf16[384,384]{1,0:T(8,128)(2,1)S(1)}, u32[]{:S(2)}, u32[]{:S(2)}) collective-permute-start(bf16[384,384]{1,0:T(8,128)(2,1)S(1)} %get-tuple-element.47), channel_id=1, source_target_pairs={{0,24},{8,16},{16,8},{24,0},{1,25},{9,17},{17,9},{25,1},{2,26},{10... | collective-permute-start | bytes 884744 | tf_op jit(solution)/shard_map/ppermute | solution.py:35
  72.1 21.3 %all_to_all.10.refs_1_ = f32[32,8,128]{2,1,0:T(8,128)S(1)} all-to-all(f32[32,8,128]{2,1,0:T(8,128)S(1)} %get-tuple-element.41), channel_id=1, replica_groups=mesh['island'=4,'expert'=4,'tensor'=2] {'island','expert','tensor'}, dimensions={0} | all-to-all | bytes 262144 | tf_op jit(solution)/shard_map/all_to_all | solution.py:370
  93.4 0.0 collective-permute-done.12.refs_8_
  93.4 0.0 collective-permute-done.10.refs_6_
  93.4 0.0 collective-permute-done.11.refs_7_
  93.4 0.0 collective-permute-done.9.refs_4_
  93.4 4.1 %average_block.1 = (f32[1024,384]{1,0:T(8,128)S(1)}, f32[32,8,128]{2,1,0:T(8,128)S(1)}) custom-call(s32[6]{0:T(128)S(1)} %copy-done.3, f32[32,8,128]{2,1,0:T(8,128)S(1)} %all_to_all.10.refs_1_, f32[1024,384]{1,0:T(8,128)S(1)} %get-tuple-element.42.refs_2_, bf16[4,1024,384]{2,1,0:T(8,128)(2,1)S(1)} %get-tuple-element.43.refs_3_, ...), custom_call_target="tpu_custom_call" | custom-call | tf_op jit(solution)/shard_map/average_block/pallas_call | solution.py:373
  97.5 1.0 convert_element_type.16
  98.5 1.7 %collective-permute-start.15 = (f16[1024,384]{1,0:T(8,128)(2,1)}, f16[1024,384]{1,0:T(8,128)(2,1)S(1)}, u32[]{:S(2)}, u32[]{:S(2)}) collective-permute-start(f16[1024,384]{1,0:T(8,128)(2,1)} %convert_element_type.16), channel_id=1, source_target_pairs={{0,16},{8,24},{16,0},{24,8},{1,17},{9,25},{17,1},{25,9},{2,18},{10... | collective-permute-start | bytes 2359304 | tf_op jit(solution)/shard_map/ppermute | solution.py:35
  100.2 1.0 collective-permute-start.13
  101.3 19.6 %all_to_all.11.notes = f32[32,8,128]{2,1,0:T(8,128)S(1)} all-to-all(f32[32,8,128]{2,1,0:T(8,128)S(1)} %get-tuple-element.48), channel_id=1, replica_groups=mesh['island'=4,'expert'=4,'tensor'=2] {'island','expert','tensor'}, dimensions={0} | all-to-all | bytes 262144 | tf_op jit(solution)/shard_map/all_to_all | solution.py:385
  120.9 0.5 slice.4
  122.1 0.0 collective-permute-done.15
  122.1 0.8 constant_dynamic-slice_fusion
  122.9 1.2 collective-permute-start.16
  124.1 0.0 collective-permute-done.13
  124.1 0.9 constant_dynamic-slice_fusion.1
  125.0 1.3 collective-permute-start.14
  126.3 0.1 stack.72.place
  126.4 1.3 convert_element_type.20.refs_2_
  127.7 0.1 convert_element_type.19.refs_1_
  127.8 5.7 %update_pieces.2 = (f32[1,2048,768]{2,1,0:T(8,128)}, bf16[1,2048,768]{2,1,0:T(8,128)(2,1)}) custom-call(s32[12]{0:T(128)S(1)} %stack.72.place, f32[32,8,128]{2,1,0:T(8,128)S(1)} %all_to_all.11.notes, f32[1,2048,768]{2,1,0:T(8,128)} %momentum.3, f32[1024,384]{1,0:T(8,128)S(1)} %get-tuple-element.49.refs_0_, f32[1024,384]{1,0:T(8,128)S(1)} %convert_element_type.19.refs_1_, ...), custom_call_target="tpu_custom_call" | custom-call | bytes 18874368 | tf_op jit(solution)/shard_map/update_pieces/pallas_call | solution.py:410
  133.5 0.9 collective-permute-done.16
  134.4 1.0 convert_element_type.18.refs_1_
  135.4 0.5 collective-permute-done.14
  136.0 1.0 convert_element_type.17.refs_0_
  137.0 3.1 %update_pieces.3 = (f32[1,2048,768]{2,1,0:T(8,128)}, bf16[1,2048,768]{2,1,0:T(8,128)(2,1)}) custom-call(s32[12]{0:T(128)S(1)} %stack.72.place, f32[32,8,128]{2,1,0:T(8,128)S(1)} %all_to_all.11.notes, f32[1,2048,768]{2,1,0:T(8,128)} %momentum.3, f32[512,384]{1,0:T(8,128)S(1)} %convert_element_type.17.refs_0_, ...), custom_call_target="tpu_custom_call", output_to_operand_aliasing={{0}: (5, {}), {1}: (6, {})} | custom-call | bytes 4718592 | tf_op jit(solution)/shard_map/update_pieces/pallas_call | solution.py:410
Async XLA Ops:
  4.8 12.0 %copy-start.2 = (bf16[192,1024]{1,0:T(8,128)(2,1)S(1)}, bf16[192,1024]{1,0:T(8,128)(2,1)}, u32[]{:S(2)}) copy-start(bf16[192,1024]{1,0:T(8,128)(2,1)} %get-tuple-element.27.slots) | copy-start | bytes 1179652
  4.9 20.1 %collective-permute-start = (bf16[192,1024]{1,0:T(8,128)(2,1)}, bf16[192,1024]{1,0:T(8,128)(2,1)S(1)}, u32[]{:S(2)}, u32[]{:S(2)}) collective-permute-start(bf16[192,1024]{1,0:T(8,128)(2,1)} %get-tuple-element.30), channel_id=1, source_target_pairs={{0,2},{2,0},{4,6},{6,4},{1,3},{3,1},{5,7},{7,5},{8,10},{10,8},{12,... | collective-permute-start | bytes 1179656 | tf_op jit(solution)/shard_map/ppermute | solution.py:35
  7.9 30.0 %collective-permute-start.1 = (bf16[192,1024]{1,0:T(8,128)(2,1)}, bf16[192,1024]{1,0:T(8,128)(2,1)S(1)}, u32[]{:S(2)}, u32[]{:S(2)}) collective-permute-start(bf16[192,1024]{1,0:T(8,128)(2,1)} %get-tuple-element.31), channel_id=1, source_target_pairs={{0,4},{2,6},{4,0},{6,2},{1,5},{3,7},{5,1},{7,3},{8,12},{10,14},{12... | collective-permute-start | bytes 1179656 | tf_op jit(solution)/shard_map/ppermute | solution.py:35
  10.5 27.4 %collective-permute-start.2 = (bf16[192,1024]{1,0:T(8,128)(2,1)}, bf16[192,1024]{1,0:T(8,128)(2,1)S(1)}, u32[]{:S(2)}, u32[]{:S(2)}) collective-permute-start(bf16[192,1024]{1,0:T(8,128)(2,1)} %get-tuple-element.32), channel_id=1, source_target_pairs={{0,6},{2,4},{4,2},{6,0},{1,7},{3,5},{5,3},{7,1},{8,14},{10,12},{12... | collective-permute-start | bytes 1179656 | tf_op jit(solution)/shard_map/ppermute | solution.py:35
  10.5 0.6 copy-start.3
  13.6 27.2 %collective-permute-start.4 = (bf16[1536,384]{1,0:T(8,128)(2,1)S(1)}, bf16[1536,384]{1,0:T(8,128)(2,1)S(1)}, u32[]{:S(2)}, u32[]{:S(2)}) collective-permute-start(bf16[1536,384]{1,0:T(8,128)(2,1)S(1)} %get-tuple-element.36), channel_id=1, source_target_pairs={{0,8},{8,0},{16,24},{24,16},{1,9},{9,1},{17,25},{25,17},{2,10},{10... | collective-permute-start | bytes 3538952 | tf_op jit(solution)/shard_map/ppermute | solution.py:35
  15.4 26.7 %collective-permute-start.5 = (bf16[1536,384]{1,0:T(8,128)(2,1)S(1)}, bf16[1536,384]{1,0:T(8,128)(2,1)S(1)}, u32[]{:S(2)}, u32[]{:S(2)}) collective-permute-start(bf16[1536,384]{1,0:T(8,128)(2,1)S(1)} %get-tuple-element.37), channel_id=1, source_target_pairs={{0,16},{8,24},{16,0},{24,8},{1,17},{9,25},{17,1},{25,9},{2,18},{10... | collective-permute-start | bytes 3538952 | tf_op jit(solution)/shard_map/ppermute | solution.py:35
  38.0 9.8 %copy-start.1 = (bf16[1,1,768,2048]{3,2,1,0:T(8,128)(2,1)S(1)}, bf16[1,1,768,2048]{3,2,1,0:T(8,128)(2,1)}, u32[]{:S(2)}) copy-start(bf16[1,1,768,2048]{3,2,1,0:T(8,128)(2,1)} %refs_2_.3) | copy-start | bytes 9437188
  38.1 9.7 %copy-start = (bf16[1,1,2048,768]{3,2,1,0:T(8,128)(2,1)S(1)}, bf16[1,1,2048,768]{3,2,1,0:T(8,128)(2,1)}, u32[]{:S(2)}) copy-start(bf16[1,1,2048,768]{3,2,1,0:T(8,128)(2,1)} %refs_1_.5) | copy-start | bytes 9437188
  38.1 9.7 %collective-permute-start.3 = (bf16[768,1024]{1,0:T(8,128)(2,1)S(1)}, bf16[768,1024]{1,0:T(8,128)(2,1)S(1)}, u32[]{:S(2)}, u32[]{:S(2)}) collective-permute-start(bf16[768,1024]{1,0:T(8,128)(2,1)S(1)} %gather_slots.1.refs_3_.refs_0_), channel_id=1, source_target_pairs={{0,1},{1,0},{2,3},{3,2},{4,5},{5,4},{6,7},{7,6},{8,9},{9,8},{10,11... | collective-permute-start | bytes 4718600 | tf_op jit(solution)/shard_map/ppermute | solution.py:35
  42.7 22.9 %collective-permute-start.8 = (bf16[1024,384]{1,0:T(8,128)(2,1)S(1)}, bf16[1024,384]{1,0:T(8,128)(2,1)S(1)}, u32[]{:S(2)}, u32[]{:S(2)}) collective-permute-start(bf16[1024,384]{1,0:T(8,128)(2,1)S(1)} %get-tuple-element.38.refs_3_), channel_id=1, source_target_pairs={{1,25},{9,17},{16,8},{24,0},{3,27},{11,19},{18,10},{26,2},{5,29},{... | collective-permute-start | bytes 2359304 | tf_op jit(solution)/shard_map/ppermute | solution.py:327
  44.0 22.1 %collective-permute-start.7 = (bf16[1024,384]{1,0:T(8,128)(2,1)S(1)}, bf16[1024,384]{1,0:T(8,128)(2,1)S(1)}, u32[]{:S(2)}, u32[]{:S(2)}) collective-permute-start(bf16[1024,384]{1,0:T(8,128)(2,1)S(1)} %get-tuple-element.38.refs_3_), channel_id=1, source_target_pairs={{1,17},{9,25},{16,0},{24,8},{3,19},{11,27},{18,2},{26,10},{5,21},{... | collective-permute-start | bytes 2359304 | tf_op jit(solution)/shard_map/ppermute | solution.py:327
  45.3 20.8 %collective-permute-start.6 = (bf16[1024,384]{1,0:T(8,128)(2,1)S(1)}, bf16[1024,384]{1,0:T(8,128)(2,1)S(1)}, u32[]{:S(2)}, u32[]{:S(2)}) collective-permute-start(bf16[1024,384]{1,0:T(8,128)(2,1)S(1)} %get-tuple-element.38.refs_3_), channel_id=1, source_target_pairs={{0,8},{8,0},{17,25},{25,17},{2,10},{10,2},{19,27},{27,19},{4,12},{... | collective-permute-start | bytes 2359304 | tf_op jit(solution)/shard_map/ppermute | solution.py:327
  67.1 26.3 %collective-permute-start.9 = (bf16[4,1024,384]{2,1,0:T(8,128)(2,1)S(1)}, bf16[4,1024,384]{2,1,0:T(8,128)(2,1)S(1)}, u32[]{:S(2)}, u32[]{:S(2)}) collective-permute-start(bf16[4,1024,384]{2,1,0:T(8,128)(2,1)S(1)} %get-tuple-element.43.refs_3_), channel_id=1, source_target_pairs={{0,1},{8,9},{17,16},{25,24},{2,3},{10,11},{19,18},{27,26},{4,5},{1... | collective-permute-start | bytes 9437192 | tf_op jit(solution)/shard_map/ppermute | solution.py:336
  68.6 24.8 %collective-permute-start.10 = (bf16[896,384]{1,0:T(8,128)(2,1)S(1)}, bf16[896,384]{1,0:T(8,128)(2,1)S(1)}, u32[]{:S(2)}, u32[]{:S(2)}) collective-permute-start(bf16[896,384]{1,0:T(8,128)(2,1)S(1)} %get-tuple-element.45), channel_id=1, source_target_pairs={{0,8},{8,0},{16,24},{24,16},{1,9},{9,1},{17,25},{25,17},{2,10},{10... | collective-permute-start | bytes 2064392 | tf_op jit(solution)/shard_map/ppermute | solution.py:35
  69.6 23.8 %collective-permute-start.11 = (bf16[896,384]{1,0:T(8,128)(2,1)S(1)}, bf16[896,384]{1,0:T(8,128)(2,1)S(1)}, u32[]{:S(2)}, u32[]{:S(2)}) collective-permute-start(bf16[896,384]{1,0:T(8,128)(2,1)S(1)} %get-tuple-element.46), channel_id=1, source_target_pairs={{0,16},{8,24},{16,0},{24,8},{1,17},{9,25},{17,1},{25,9},{2,18},{10... | collective-permute-start | bytes 2064392 | tf_op jit(solution)/shard_map/ppermute | solution.py:35
  69.7 23.8 %collective-permute-start.12 = (bf16[384,384]{1,0:T(8,128)(2,1)S(1)}, bf16[384,384]{1,0:T(8,128)(2,1)S(1)}, u32[]{:S(2)}, u32[]{:S(2)}) collective-permute-start(bf16[384,384]{1,0:T(8,128)(2,1)S(1)} %get-tuple-element.47), channel_id=1, source_target_pairs={{0,24},{8,16},{16,8},{24,0},{1,25},{9,17},{17,9},{25,1},{2,26},{10... | collective-permute-start | bytes 884744 | tf_op jit(solution)/shard_map/ppermute | solution.py:35
  98.5 23.5 %collective-permute-start.15 = (f16[1024,384]{1,0:T(8,128)(2,1)}, f16[1024,384]{1,0:T(8,128)(2,1)S(1)}, u32[]{:S(2)}, u32[]{:S(2)}) collective-permute-start(f16[1024,384]{1,0:T(8,128)(2,1)} %convert_element_type.16), channel_id=1, source_target_pairs={{0,16},{8,24},{16,0},{24,8},{1,17},{9,25},{17,1},{25,9},{2,18},{10... | collective-permute-start | bytes 2359304 | tf_op jit(solution)/shard_map/ppermute | solution.py:35
  100.2 23.9 %collective-permute-start.13 = (f16[1024,384]{1,0:T(8,128)(2,1)}, f16[1024,384]{1,0:T(8,128)(2,1)S(1)}, u32[]{:S(2)}, u32[]{:S(2)}) collective-permute-start(f16[1024,384]{1,0:T(8,128)(2,1)} %convert_element_type.16), channel_id=1, source_target_pairs={{0,8},{8,0},{16,24},{24,16},{1,9},{9,1},{17,25},{25,17},{2,10},{10... | collective-permute-start | bytes 2359304 | tf_op jit(solution)/shard_map/ppermute | solution.py:35
  122.9 11.5 %collective-permute-start.16 = (f16[512,384]{1,0:T(8,128)(2,1)}, f16[512,384]{1,0:T(8,128)(2,1)}, u32[]{:S(2)}, u32[]{:S(2)}) collective-permute-start(f16[512,384]{1,0:T(8,128)(2,1)} %constant_dynamic-slice_fusion), channel_id=1, source_target_pairs={{0,8},{8,0},{16,24},{24,16},{1,9},{9,1},{17,25},{25,17},{2,10},{10... | collective-permute-start | bytes 1179656 | tf_op jit(solution)/shard_map/ppermute | solution.py:35
  125.0 11.0 %collective-permute-start.14 = (f16[512,384]{1,0:T(8,128)(2,1)}, f16[512,384]{1,0:T(8,128)(2,1)}, u32[]{:S(2)}, u32[]{:S(2)}) collective-permute-start(f16[512,384]{1,0:T(8,128)(2,1)} %constant_dynamic-slice_fusion.1), channel_id=1, source_target_pairs={{0,16},{8,24},{16,0},{24,8},{1,17},{9,25},{17,1},{25,9},{2,18},{10... | collective-permute-start | bytes 1179656 | tf_op jit(solution)/shard_map/ppermute | solution.py:35

commit v15 on v13

--- a/solution.py
+++ b/solution.py
@@ -82,19 +82,28 @@
 
 
 def gather_kernel(count, *refs):
-    arrived, joined = refs[:count], refs[count]
+    arrived, (inputs, grads) = refs[:count], refs[count:]
     slots = arrived[0].shape[0] // 2
     for n, piece in enumerate(arrived):
-        joined[n * slots : (n + 1) * slots, :] = piece[:slots, :]
-        joined[(count + n) * slots : (count + n + 1) * slots, :] = piece[slots:, :]
-
-
-def join_kernel(blocks, joined, *refs):
-    drifts, (turned, drift_sum) = refs[:blocks], refs[blocks : blocks + 2]
+        inputs[n * slots : (n + 1) * slots, :] = piece[:slots, :]
+        grads[n * slots : (n + 1) * slots, :] = piece[slots:, :]
+
+
+def join_kernel(parts, blocks, spot, *refs):
+    joined, drifts = refs[:parts], refs[parts : parts + blocks]
+    shares, (drift_sum, *relays) = refs[parts + blocks :][:parts], refs[parts + blocks :][parts:]
     rows = drift_sum.shape[0]
-    for n, ref in enumerate(refs[blocks + 2 :]):
+    for n, ref in enumerate(relays):
         ref[...] = drifts[1 + n][rows:, :]
-    turned[...] = joined[: joined.shape[0] // 2, :].T
+    size = shares[0].shape[0]
+    first = pl.multiple_of(spot[1] * size, size)
+
+    def take(share, source):
+        share[...] = source[:, pl.ds(first, size)].T
+
+    for r in range(parts):
+        for t in range(parts):
+            pl.when(partner(spot[5], r, parts) == t)(functools.partial(take, shares[r], joined[t]))
     added = drifts[0][...].astype(F32)
     for other in drifts[1:]:
         added = added + other[:rows, :].astype(F32)
@@ -102,8 +111,8 @@
 
 
 def hidden_kernel(parts, across, spot, gate, down, *refs):
-    joined, out, norms = refs[:parts], refs[parts], refs[-1]
-    rows, half = joined[0].shape[0] // 2, joined[0].shape[1]
+    inputs, grads, (out, norms) = refs[:parts], refs[parts : 2 * parts], refs[2 * parts :]
+    half = inputs[0].shape[1]
     columns = out.shape[2]
     starts = [pl.multiple_of(origin(spot[1], t, parts) * half, half) for t in range(parts)]
     hidden_gram = 0.0
@@ -113,24 +122,24 @@
         back = 0.0
         for t in range(parts):
             block = gate[0, 0, pl.ds(starts[t], half), first : first + columns]
-            value = value + dot(joined[t][:rows, :], block, ((1,), (0,)))
+            value = value + dot(inputs[t][...], block, ((1,), (0,)))
             block = down[0, 0, first : first + columns, pl.ds(starts[t], half)]
-            back = back + dot(joined[t][rows:, :], block, ((1,), (1,)))
+            back = back + dot(grads[t][...], block, ((1,), (1,)))
         rounded = (back * (value / (1.0 + jnp.exp(-value)))).astype(BF16)
         out[r] = rounded
         hidden_gram = hidden_gram + dot(rounded, rounded, ((1,), (1,)))
     input_gram = 0.0
     for t in range(parts):
-        features = joined[t][:rows, :]
+        features = inputs[t][...]
         input_gram = input_gram + dot(features, features, ((1,), (1,)))
     norms[...] = jnp.full(norms.shape, jnp.sum(hidden_gram * input_gram), F32)
 
 
-def average_kernel(islands, entries, tiles, spot, norms, drift_sum, own, moved, *refs):
-    messages = refs[:islands]
-    scaled, notes, total, square = refs[islands:]
-    rows = total.shape[0] // tiles
-    slots = own.shape[2]
+def average_kernel(islands, entries, parts, spot, norms, drift_sum, *refs):
+    features, messages = refs[:parts], refs[parts : parts + islands]
+    scaled, notes, total, square = refs[parts + islands :]
+    rows = total.shape[0] // parts
+    slots = features[0].shape[2]
     group = norms.shape[0] // islands
     scales = []
     for d in range(islands):
@@ -139,9 +148,9 @@
         scales.append(jnp.minimum(1.0, math.sqrt(entries) / jnp.sqrt(norm + 1e-06)) / islands)
     handed = [m for m in messages[:0:-1] if m.shape[0] > slots]
 
-    def compute(features):
+    def compute(at):
         squares = 0.0
-        for m in range(tiles):
+        for m in range(parts):
             part = slice(m * rows, (m + 1) * rows)
             average = drift_sum[part, :]
             if handed:
@@ -152,13 +161,13 @@
             average = average * (1.0 / islands)
             for d in range(islands):
                 factor = messages[d][:slots, :]
-                average = average + scales[d] * dot(features[d, part, :], factor, ((1,), (0,)))
+                average = average + scales[d] * dot(features[partner(at, m, parts)][d], factor, ((1,), (0,)))
             total[part, :] = average
             squares = squares + jnp.sum(average * average, axis=0, keepdims=True)
         square[...] = squares
 
-    pl.when(spot[5] == 1)(lambda: compute(own))
-    pl.when(spot[5] != 1)(lambda: compute(moved))
+    for at in range(parts):
+        pl.when(spot[1] == at)(functools.partial(compute, at))
     peak = jnp.max(jnp.abs(total[...]))
     unit = jnp.maximum(peak, 1e-30) / 32768
     value = total[...] * (1 / unit)
@@ -245,7 +254,7 @@
     routed_rows = experts * slots
     holder = island // across
     spot = jnp.stack(
-        [expert, part, island % across, island, jnp.int32(across), (part == holder).astype(jnp.int32)]
+        [expert, part, island % across, island, jnp.int32(across), part ^ holder]
     ).astype(jnp.int32)
 
     handed = half // 2 if islands == 4 else 0
@@ -291,52 +300,36 @@
         compiler_params=params(6),
         name="own_parts",
     )(arrived[0], drift_in[0])
-    joined = pl.pallas_call(
+    rows_block = jax.ShapeDtypeStruct((routed_rows, half), BF16)
+    inputs, grads = pl.pallas_call(
         lambda *refs: gather_kernel(experts, *refs),
         in_specs=[VMEM] * experts,
-        out_specs=VMEM,
-        out_shape=jax.ShapeDtypeStruct((2 * routed_rows, half), BF16),
+        out_specs=[VMEM] * 2,
+        out_shape=[rows_block] * 2,
         compiler_params=params(6 + routed_rows // 48),
         name="gather_slots",
     )(*arrived)
-    turned, drift_sum, *relays = pl.pallas_call(
-        lambda *refs: join_kernel(len(steps), *refs),
-        in_specs=[VMEM] * (1 + len(steps)),
-        out_specs=[VMEM] * (4 if handed else 2),
-        out_shape=[
-            jax.ShapeDtypeStruct((half, routed_rows), BF16),
-            jax.ShapeDtypeStruct((half, columns), F32),
-        ]
+
+    inputs_all = [inputs] + [swap(inputs, "tensor", t) for t in range(1, parts)]
+    grads_all = [grads] + [swap(grads, "tensor", t) for t in range(1, parts)]
+    share = jax.ShapeDtypeStruct((half // parts, routed_rows), BF16)
+    outputs = pl.pallas_call(
+        lambda *refs: join_kernel(parts, len(steps), *refs),
+        in_specs=[SMEM] + [VMEM] * (parts + len(steps)),
+        out_specs=[VMEM] * (parts + (3 if handed else 1)),
+        out_shape=[share] * parts
+        + [jax.ShapeDtypeStruct((half, columns), F32)]
         + [jax.ShapeDtypeStruct((handed, columns), BF16)] * (2 if handed else 0),
-        compiler_params=params(12 + routed_rows // 48),
+        compiler_params=params(14 + routed_rows // 48),
         name="join_blocks",
-    )(joined, *drift_in)
-
-    joined_all = [joined] + [swap(joined, "tensor", t) for t in range(1, parts)]
-
-    def send_features(d):
-        pairs = []
-        for at in range(islands):
-            to = partner(at, d, islands)
-            pairs.append((at * parts + to // across, to * parts + to // across))
-        return lax.ppermute(turned, ("island", "tensor"), pairs)
-
-    def spread(value):
-        result = value
-        for t in range(1, parts):
-            pairs = []
-            for at in range(islands):
-                keep = at // across
-                pairs.append((at * parts + keep, at * parts + partner(keep, t, parts)))
-            moved = lax.ppermute(value, ("island", "tensor"), pairs)
-            result = moved if t == 1 else result + moved
-        return result
-
-    features_in = [send_features(d) for d in range(1, islands)]
+    )(spot, *inputs_all, *drift_in)
+    shares, (drift_sum, *relays) = outputs[:parts], outputs[parts:]
+
+    features_in = [swap(shares[d // across], "island", d) for d in range(1, islands)]
 
     hidden_out, norms = pl.pallas_call(
         lambda *refs: hidden_kernel(parts, across, *refs),
-        in_specs=[SMEM] + [VMEM] * (2 + parts),
+        in_specs=[SMEM] + [VMEM] * (2 + 2 * parts),
         out_specs=[VMEM] * 2,
         out_shape=[
             jax.ShapeDtypeStruct((across, routed_rows, columns), BF16),
@@ -344,7 +337,7 @@
         ],
         compiler_params=params(16 + routed_rows // 48),
         name="hidden_grads",
-    )(spot, gate_weight, down_weight, *joined_all)
+    )(spot, gate_weight, down_weight, *inputs_all, *grads_all)
     tails = [2, 1] if handed else []
     message_rows = [
         routed_rows + (half - handed if d in tails else 0) for d in range(islands)
@@ -354,20 +347,20 @@
         in_specs=[SMEM] + [VMEM] * (2 + islands + len(relays)),
         out_specs=[VMEM] * (2 + islands),
         out_shape=[
-            jax.ShapeDtypeStruct((islands, half, routed_rows), BF16),
+            jax.ShapeDtypeStruct((islands, half // parts, routed_rows), BF16),
             jax.ShapeDtypeStruct(norms.shape, F32),
         ]
         + [jax.ShapeDtypeStruct((rows, columns), BF16) for rows in message_rows],
         compiler_params=params(6 + routed_rows // 48),
         name="hand_on",
-    )(spot, norms, hidden_out, turned, *features_in, *relays)
-    features_moved = spread(features_in)
+    )(spot, norms, hidden_out, shares[0], *features_in, *relays)
+    features_of = [features_in] + [swap(features_in, "tensor", t) for t in range(1, parts)]
     norms = lax.all_to_all(norms, AXES, split_axis=0, concat_axis=0, tiled=True)
     messages_in = [messages[0]] + [swap(messages[d], "island", d) for d in range(1, islands)]
 
     scaled, notes = pl.pallas_call(
-        lambda *refs: average_kernel(islands, entries, 2, *refs),
-        in_specs=[SMEM] + [VMEM] * (4 + islands),
+        lambda *refs: average_kernel(islands, entries, parts, *refs),
+        in_specs=[SMEM] + [VMEM] * (2 + parts + islands),
         out_specs=[VMEM] * 2,
         out_shape=[
             jax.ShapeDtypeStruct((half, columns), F32),
@@ -376,7 +369,7 @@
         scratch_shapes=[pltpu.VMEM((half, columns), F32), pltpu.VMEM((1, columns), F32)],
         compiler_params=params(8 + routed_rows // 48),
         name="average_block",
-    )(spot, norms, drift_sum, features_in, features_moved, *messages_in)
+    )(spot, norms, drift_sum, *features_of, *messages_in)
     notes = lax.all_to_all(notes, AXES, split_axis=0, concat_axis=0, tiled=True)
 
     sent = scaled.astype(WIRE)

time: 141 us -> 142 us (level)
  the two profiles are of different devices: /device:TPU:0 before, /device:TPU:8 now
where the time goes in v15:
time: 142 us; the launch traced here: 141 us
  waiting for transfers between devices  44.1 us (31%)
  blocking collectives  43.7 us (31%)
  Pallas kernels  25 us (18%)
  starting transfers between devices  17.6 us (12%)
  other arithmetic  5.31 us (4%)
  local copies, waits for them, and re-layouts  3.85 us (3%)
  between operations  1.64 us (1%)
    ppermute x18, waiting for transfers between devices, swap(): lax.ppermute(value, axis, [(at, partner(at, step, size)) for at in range(...  44.1 us
    all_to_all x1, blocking collectives, body(): norms = lax.all_to_all(norms, AXES, split_axis=0, concat_axis=0, tiled=True)  23.2 us
    all_to_all x1, blocking collectives, body(): notes = lax.all_to_all(notes, AXES, split_axis=0, concat_axis=0, tiled=True)  20.5 us
    ppermute x18, starting transfers between devices, swap(): lax.ppermute(value, axis, [(at, partner(at, step, size)) for at in range(...  17.6 us
    pallas_call x2, Pallas kernels, body(): pl.pallas_call(functools.partial(update_kernel, entries, list(values), cu...  8.83 us
    pallas_call x1, Pallas kernels, body(): pl.pallas_call(lambda *refs: hidden_kernel(parts, across, *refs), in_spec...  5.42 us
    pallas_call x1, Pallas kernels, body(): pl.pallas_call(lambda *refs: average_kernel(islands, entries, parts, *ref...  4.09 us
    pallas_call x1, Pallas kernels, body(): pl.pallas_call(lambda *refs: pick_kernel(experts, *refs), in_specs=[SMEM]...  3.57 us
  transfers between devices with their start and end apart: 18, of which 9 were waited for; matrix products, arithmetic and copies ran while one was open for 3% of the time, Pallas kernels for 9%

profile of v15, /device:TPU:8, one launch (start us, length us, event | category | flops | bytes accessed | tf_op | source)
XLA Modules:
  0.0 141.2 jit_solution(10286585525630972876)
XLA Ops:
  0.7 0.7 stack.75.refs_0_
  1.3 3.6 %pick_slots.1 = (bf16[192,1024]{1,0:T(8,128)(2,1)}, bf16[192,1024]{1,0:T(8,128)(2,1)}, bf16[192,1024]{1,0:T(8,128)(2,1)}, bf16[192,1024]{1,0:T(8,128)(2,1)}) custom-call(s32[6]{0:T(128)} %stack.75.refs_0_, s32[1,1,4,96]{3,2,1,0:T(4,128)} %refs_1_.3, s32[1,1,4]{2,1,0:T(1,128)} %refs_2_.2, f32[1,1,4,96]{3,2,1,0:T(4,128)} %refs_3_.1, ...), custom_call_target="tpu_custom_call" | custom-call | tf_op jit(solution)/shard_map/pick_slots/pallas_call | solution.py:266
  4.9 0.1 collective-permute-start
  5.0 3.0 %collective-permute-start.1 = (bf16[192,1024]{1,0:T(8,128)(2,1)}, bf16[192,1024]{1,0:T(8,128)(2,1)S(1)}, u32[]{:S(2)}, u32[]{:S(2)}) collective-permute-start(bf16[192,1024]{1,0:T(8,128)(2,1)} %get-tuple-element.34), channel_id=1, source_target_pairs={{0,4},{2,6},{4,0},{6,2},{1,5},{3,7},{5,1},{7,3},{8,12},{10,14},{12... | collective-permute-start | bytes 1179656 | tf_op jit(solution)/shard_map/ppermute | solution.py:35
  8.0 0.5 collective-permute-start.2
  8.5 1.9 %copy-done = bf16[1,1,2048,768]{3,2,1,0:T(8,128)(2,1)S(1)} copy-done((bf16[1,1,2048,768]{3,2,1,0:T(8,128)(2,1)S(1)}, bf16[1,1,2048,768]{3,2,1,0:T(8,128)(2,1)}, u32[]{:S(2)}) %copy-start) | copy-done | bytes 3145752
  10.4 0.7 copy-done.4
  11.0 0.8 cut_drift.1
  11.9 1.6 %collective-permute-start.5 = (bf16[1536,384]{1,0:T(8,128)(2,1)S(1)}, bf16[1536,384]{1,0:T(8,128)(2,1)S(1)}, u32[]{:S(2)}, u32[]{:S(2)}) collective-permute-start(bf16[1536,384]{1,0:T(8,128)(2,1)S(1)} %get-tuple-element.41), channel_id=1, source_target_pairs={{0,8},{8,0},{16,24},{24,16},{1,9},{9,1},{17,25},{25,17},{2,10},{10... | collective-permute-start | bytes 3538952 | tf_op jit(solution)/shard_map/ppermute | solution.py:35
  13.4 1.5 %collective-permute-start.6 = (bf16[1536,384]{1,0:T(8,128)(2,1)S(1)}, bf16[1536,384]{1,0:T(8,128)(2,1)S(1)}, u32[]{:S(2)}, u32[]{:S(2)}) collective-permute-start(bf16[1536,384]{1,0:T(8,128)(2,1)S(1)} %get-tuple-element.42), channel_id=1, source_target_pairs={{0,16},{8,24},{16,0},{24,8},{1,17},{9,25},{17,1},{25,9},{2,18},{10... | collective-permute-start | bytes 3538952 | tf_op jit(solution)/shard_map/ppermute | solution.py:35
  14.9 0.0 copy-done.3
  14.9 0.1 own_parts.1
  15.0 6.6 %collective-permute-done.refs_1_ = bf16[192,1024]{1,0:T(8,128)(2,1)S(1)} collective-permute-done((bf16[192,1024]{1,0:T(8,128)(2,1)}, bf16[192,1024]{1,0:T(8,128)(2,1)S(1)}, u32[]{:S(2)}, u32[]{:S(2)}) %collective-permute-start) | collective-permute-done | bytes 393248 | tf_op jit(solution)/shard_map/ppermute | solution.py:35
  21.6 13.1 %collective-permute-done.1.refs_2_ = bf16[192,1024]{1,0:T(8,128)(2,1)S(1)} collective-permute-done((bf16[192,1024]{1,0:T(8,128)(2,1)}, bf16[192,1024]{1,0:T(8,128)(2,1)S(1)}, u32[]{:S(2)}, u32[]{:S(2)}) %collective-permute-start.1) | collective-permute-done | bytes 393248 | tf_op jit(solution)/shard_map/ppermute | solution.py:35
  34.7 7.8 %collective-permute-done.2.refs_3_ = bf16[192,1024]{1,0:T(8,128)(2,1)S(1)} collective-permute-done((bf16[192,1024]{1,0:T(8,128)(2,1)}, bf16[192,1024]{1,0:T(8,128)(2,1)S(1)}, u32[]{:S(2)}, u32[]{:S(2)}) %collective-permute-start.2) | collective-permute-done | bytes 393248 | tf_op jit(solution)/shard_map/ppermute | solution.py:35
  42.5 0.1 gather_slots.1
  42.7 0.1 collective-permute-start.3
  42.7 0.5 collective-permute-start.4
  43.2 1.8 %collective-permute-done.3.refs_4_.refs_2_ = bf16[384,1024]{1,0:T(8,128)(2,1)S(1)} collective-permute-done((bf16[384,1024]{1,0:T(8,128)(2,1)S(1)}, bf16[384,1024]{1,0:T(8,128)(2,1)S(1)}, u32[]{:S(2)}, u32[]{:S(2)}) %collective-permute-start.3) | collective-permute-done | bytes 786464 | tf_op jit(solution)/shard_map/ppermute | solution.py:35
  45.0 0.0 collective-permute-done.5.refs_4_
  45.0 0.0 collective-permute-done.6.refs_5_
  45.0 0.0 copy-done.5
  45.0 0.0 copy-start.1
  45.0 1.2 join_blocks.1
  46.2 1.6 %collective-permute-start.7 = (bf16[512,384]{1,0:T(8,128)(2,1)S(1)}, bf16[512,384]{1,0:T(8,128)(2,1)S(1)}, u32[]{:S(2)}, u32[]{:S(2)}) collective-permute-start(bf16[512,384]{1,0:T(8,128)(2,1)S(1)} %get-tuple-element.43.refs_3_), channel_id=1, source_target_pairs={{0,8},{8,0},{16,24},{24,16},{1,9},{9,1},{17,25},{25,17},{2,10},{10... | collective-permute-start | bytes 1179656 | tf_op jit(solution)/shard_map/ppermute | solution.py:35
  47.8 1.5 %collective-permute-start.9 = (bf16[512,384]{1,0:T(8,128)(2,1)S(1)}, bf16[512,384]{1,0:T(8,128)(2,1)S(1)}, u32[]{:S(2)}, u32[]{:S(2)}) collective-permute-start(bf16[512,384]{1,0:T(8,128)(2,1)S(1)} %get-tuple-element.44), channel_id=1, source_target_pairs={{0,24},{8,16},{16,8},{24,0},{1,25},{9,17},{17,9},{25,1},{2,26},{10... | collective-permute-start | bytes 1179656 | tf_op jit(solution)/shard_map/ppermute | solution.py:35
  49.3 0.5 collective-permute-start.8
  49.8 0.0 collective-permute-done.4.refs_6_
  49.8 0.0 copy-done.2
  49.8 5.4 %hidden_grads.1 = (bf16[2,384,384]{2,1,0:T(8,128)(2,1)S(1)}, f32[32,8,128]{2,1,0:T(8,128)S(1)}) custom-call(s32[6]{0:T(128)S(1)} %copy-done.5, bf16[1,1,2048,768]{3,2,1,0:T(8,128)(2,1)S(1)} %copy-done.1, bf16[1,1,768,2048]{3,2,1,0:T(8,128)(2,1)S(1)} %copy-done.2, bf16[384,1024]{1,0:T(8,128)(2,1)S(1)} %get-tuple-element.36.refs_3_.refs_1_, ...), custom_call_target="tpu_custom_call" | custom-call | tf_op jit(solution)/shard_map/hidden_grads/pallas_call | solution.py:330
  55.2 3.0 %collective-permute-done.7.refs_4_ = bf16[512,384]{1,0:T(8,128)(2,1)S(1)} collective-permute-done((bf16[512,384]{1,0:T(8,128)(2,1)S(1)}, bf16[512,384]{1,0:T(8,128)(2,1)S(1)}, u32[]{:S(2)}, u32[]{:S(2)}) %collective-permute-start.7) | collective-permute-done | bytes 393248 | tf_op jit(solution)/shard_map/ppermute | solution.py:35
  58.3 8.7 %collective-permute-done.9.refs_6_ = bf16[512,384]{1,0:T(8,128)(2,1)S(1)} collective-permute-done((bf16[512,384]{1,0:T(8,128)(2,1)S(1)}, bf16[512,384]{1,0:T(8,128)(2,1)S(1)}, u32[]{:S(2)}, u32[]{:S(2)}) %collective-permute-start.9) | collective-permute-done | bytes 393248 | tf_op jit(solution)/shard_map/ppermute | solution.py:35
  66.9 1.4 collective-permute-done.8.refs_5_
  68.3 0.9 hand_on.1
  69.2 0.1 collective-permute-start.10
  69.2 1.6 %collective-permute-start.11 = (bf16[896,384]{1,0:T(8,128)(2,1)S(1)}, bf16[896,384]{1,0:T(8,128)(2,1)S(1)}, u32[]{:S(2)}, u32[]{:S(2)}) collective-permute-start(bf16[896,384]{1,0:T(8,128)(2,1)S(1)} %get-tuple-element.51), channel_id=1, source_target_pairs={{0,8},{8,0},{16,24},{24,16},{1,9},{9,1},{17,25},{25,17},{2,10},{10... | collective-permute-start | bytes 2064392 | tf_op jit(solution)/shard_map/ppermute | solution.py:35
  70.8 0.5 collective-permute-start.12
  71.3 1.5 %collective-permute-start.13 = (bf16[384,384]{1,0:T(8,128)(2,1)S(1)}, bf16[384,384]{1,0:T(8,128)(2,1)S(1)}, u32[]{:S(2)}, u32[]{:S(2)}) collective-permute-start(bf16[384,384]{1,0:T(8,128)(2,1)S(1)} %get-tuple-element.53), channel_id=1, source_target_pairs={{0,24},{8,16},{16,8},{24,0},{1,25},{9,17},{17,9},{25,1},{2,26},{10... | collective-permute-start | bytes 884744 | tf_op jit(solution)/shard_map/ppermute | solution.py:35
  72.8 23.2 %all_to_all.10.refs_1_ = f32[32,8,128]{2,1,0:T(8,128)S(1)} all-to-all(f32[32,8,128]{2,1,0:T(8,128)S(1)} %get-tuple-element.47), channel_id=1, replica_groups=mesh['island'=4,'expert'=4,'tensor'=2] {'island','expert','tensor'}, dimensions={0} | all-to-all | bytes 262144 | tf_op jit(solution)/shard_map/all_to_all | solution.py:358
  96.0 0.0 collective-permute-done.13.refs_8_
  96.0 0.0 collective-permute-done.11.refs_6_
  96.0 0.0 collective-permute-done.12.refs_7_
  96.0 0.0 collective-permute-done.10.refs_4_
  96.0 4.1 %average_block.1 = (f32[1024,384]{1,0:T(8,128)S(1)}, f32[32,8,128]{2,1,0:T(8,128)S(1)}) custom-call(s32[6]{0:T(128)S(1)} %copy-done.5, f32[32,8,128]{2,1,0:T(8,128)S(1)} %all_to_all.10.refs_1_, f32[1024,384]{1,0:T(8,128)S(1)} %get-tuple-element.48.refs_2_, bf16[4,512,384]{2,1,0:T(8,128)(2,1)S(1)} %get-tuple-element.49.refs_3_, ...), custom_call_target="tpu_custom_call" | custom-call | tf_op jit(solution)/shard_map/average_block/pallas_call | solution.py:361
  100.1 0.1 convert_element_type.21
  100.3 0.6 collective-permute-start.16
  100.8 1.1 collective-permute-start.14
  101.9 20.5 %all_to_all.11.notes = f32[32,8,128]{2,1,0:T(8,128)S(1)} all-to-all(f32[32,8,128]{2,1,0:T(8,128)S(1)} %get-tuple-element.54), channel_id=1, replica_groups=mesh['island'=4,'expert'=4,'tensor'=2] {'island','expert','tensor'}, dimensions={0} | all-to-all | bytes 262144 | tf_op jit(solution)/shard_map/all_to_all | solution.py:373
  122.4 0.5 slice.13
  123.6 0.0 collective-permute-done.16
  123.6 0.8 slice_add_fusion
  124.4 0.4 collective-permute-start.17
  124.8 0.0 collective-permute-done.14
  124.8 0.9 slice_add_fusion.1
  125.7 1.2 collective-permute-start.15
  126.9 0.1 stack.69.place
  126.9 1.3 convert_element_type.27.refs_2_
  128.2 0.1 convert_element_type.26.refs_1_
  128.3 5.7 %update_pieces.2 = (f32[1,2048,768]{2,1,0:T(8,128)}, bf16[1,2048,768]{2,1,0:T(8,128)(2,1)}) custom-call(s32[12]{0:T(128)S(1)} %stack.69.place, f32[32,8,128]{2,1,0:T(8,128)S(1)} %all_to_all.11.notes, f32[1,2048,768]{2,1,0:T(8,128)} %momentum.3, f32[1024,384]{1,0:T(8,128)S(1)} %get-tuple-element.55.refs_0_, f32[1024,384]{1,0:T(8,128)S(1)} %convert_element_type.26.refs_1_, ...), custom_call_target="tpu_custom_call" | custom-call | bytes 18874368 | tf_op jit(solution)/shard_map/update_pieces/pallas_call | solution.py:394
  134.1 1.4 %collective-permute-done.17 = f16[512,384]{1,0:T(8,128)(2,1)} collective-permute-done((f16[512,384]{1,0:T(8,128)(2,1)}, f16[512,384]{1,0:T(8,128)(2,1)}, u32[]{:S(2)}, u32[]{:S(2)}) %collective-permute-start.17) | collective-permute-done | bytes 393248 | tf_op jit(solution)/shard_map/ppermute | solution.py:35
  135.5 1.0 convert_element_type.25.refs_1_
  136.5 0.3 collective-permute-done.15
  136.9 1.0 convert_element_type.24.refs_0_
  137.9 3.1 %update_pieces.3 = (f32[1,2048,768]{2,1,0:T(8,128)}, bf16[1,2048,768]{2,1,0:T(8,128)(2,1)}) custom-call(s32[12]{0:T(128)S(1)} %stack.69.place, f32[32,8,128]{2,1,0:T(8,128)S(1)} %all_to_all.11.notes, f32[1,2048,768]{2,1,0:T(8,128)} %momentum.3, f32[512,384]{1,0:T(8,128)S(1)} %convert_element_type.24.refs_0_, ...), custom_call_target="tpu_custom_call", output_to_operand_aliasing={{0}: (5, {}), {1}: (6, {})} | custom-call | bytes 4718592 | tf_op jit(solution)/shard_map/update_pieces/pallas_call | solution.py:394
  (6 shorter events, 0.0 us)
Async XLA Ops:
  4.9 16.7 %collective-permute-start = (bf16[192,1024]{1,0:T(8,128)(2,1)}, bf16[192,1024]{1,0:T(8,128)(2,1)S(1)}, u32[]{:S(2)}, u32[]{:S(2)}) collective-permute-start(bf16[192,1024]{1,0:T(8,128)(2,1)} %get-tuple-element.33), channel_id=1, source_target_pairs={{0,2},{2,0},{4,6},{6,4},{1,3},{3,1},{5,7},{7,5},{8,10},{10,8},{12,... | collective-permute-start | bytes 1179656 | tf_op jit(solution)/shard_map/ppermute | solution.py:35
  5.0 29.8 %collective-permute-start.1 = (bf16[192,1024]{1,0:T(8,128)(2,1)}, bf16[192,1024]{1,0:T(8,128)(2,1)S(1)}, u32[]{:S(2)}, u32[]{:S(2)}) collective-permute-start(bf16[192,1024]{1,0:T(8,128)(2,1)} %get-tuple-element.34), channel_id=1, source_target_pairs={{0,4},{2,6},{4,0},{6,2},{1,5},{3,7},{5,1},{7,3},{8,12},{10,14},{12... | collective-permute-start | bytes 1179656 | tf_op jit(solution)/shard_map/ppermute | solution.py:35
  8.0 34.5 %collective-permute-start.2 = (bf16[192,1024]{1,0:T(8,128)(2,1)}, bf16[192,1024]{1,0:T(8,128)(2,1)S(1)}, u32[]{:S(2)}, u32[]{:S(2)}) collective-permute-start(bf16[192,1024]{1,0:T(8,128)(2,1)} %get-tuple-element.35), channel_id=1, source_target_pairs={{0,6},{2,4},{4,2},{6,0},{1,7},{3,5},{5,3},{7,1},{8,14},{10,12},{12... | collective-permute-start | bytes 1179656 | tf_op jit(solution)/shard_map/ppermute | solution.py:35
  8.5 1.9 %copy-start = (bf16[1,1,2048,768]{3,2,1,0:T(8,128)(2,1)S(1)}, bf16[1,1,2048,768]{3,2,1,0:T(8,128)(2,1)}, u32[]{:S(2)}) copy-start(bf16[1,1,2048,768]{3,2,1,0:T(8,128)(2,1)} %refs_1_.4) | copy-start | bytes 9437188
  10.3 0.7 copy-start.4
  11.0 3.9 %copy-start.3 = (bf16[192,1024]{1,0:T(8,128)(2,1)S(1)}, bf16[192,1024]{1,0:T(8,128)(2,1)}, u32[]{:S(2)}) copy-start(bf16[192,1024]{1,0:T(8,128)(2,1)} %get-tuple-element.30.slots) | copy-start | bytes 1179652
  11.9 33.2 %copy-start.5 = (s32[6]{0:T(128)S(1)}, s32[6]{0:T(128)}, u32[]{:S(2)}) copy-start(s32[6]{0:T(128)} %stack.75.refs_0_) | copy-start | bytes 76
  11.9 33.1 %collective-permute-start.5 = (bf16[1536,384]{1,0:T(8,128)(2,1)S(1)}, bf16[1536,384]{1,0:T(8,128)(2,1)S(1)}, u32[]{:S(2)}, u32[]{:S(2)}) collective-permute-start(bf16[1536,384]{1,0:T(8,128)(2,1)S(1)} %get-tuple-element.41), channel_id=1, source_target_pairs={{0,8},{8,0},{16,24},{24,16},{1,9},{9,1},{17,25},{25,17},{2,10},{10... | collective-permute-start | bytes 3538952 | tf_op jit(solution)/shard_map/ppermute | solution.py:35
  13.4 31.6 %collective-permute-start.6 = (bf16[1536,384]{1,0:T(8,128)(2,1)S(1)}, bf16[1536,384]{1,0:T(8,128)(2,1)S(1)}, u32[]{:S(2)}, u32[]{:S(2)}) collective-permute-start(bf16[1536,384]{1,0:T(8,128)(2,1)S(1)} %get-tuple-element.42), channel_id=1, source_target_pairs={{0,16},{8,24},{16,0},{24,8},{1,17},{9,25},{17,1},{25,9},{2,18},{10... | collective-permute-start | bytes 3538952 | tf_op jit(solution)/shard_map/ppermute | solution.py:35
  42.5 7.2 %copy-start.2 = (bf16[1,1,768,2048]{3,2,1,0:T(8,128)(2,1)S(1)}, bf16[1,1,768,2048]{3,2,1,0:T(8,128)(2,1)}, u32[]{:S(2)}) copy-start(bf16[1,1,768,2048]{3,2,1,0:T(8,128)(2,1)} %refs_2_.3) | copy-start | bytes 9437188
  42.7 2.4 %collective-permute-start.3 = (bf16[384,1024]{1,0:T(8,128)(2,1)S(1)}, bf16[384,1024]{1,0:T(8,128)(2,1)S(1)}, u32[]{:S(2)}, u32[]{:S(2)}) collective-permute-start(bf16[384,1024]{1,0:T(8,128)(2,1)S(1)} %get-tuple-element.36.refs_3_.refs_1_), channel_id=1, source_target_pairs={{0,1},{1,0},{2,3},{3,2},{4,5},{5,4},{6,7},{7,6},{8,9},{9,8},{10,11... | collective-permute-start | bytes 2359304 | tf_op jit(solution)/shard_map/ppermute | solution.py:35
  42.7 7.1 %collective-permute-start.4 = (bf16[384,1024]{1,0:T(8,128)(2,1)S(1)}, bf16[384,1024]{1,0:T(8,128)(2,1)S(1)}, u32[]{:S(2)}, u32[]{:S(2)}) collective-permute-start(bf16[384,1024]{1,0:T(8,128)(2,1)S(1)} %get-tuple-element.37.refs_5_), channel_id=1, source_target_pairs={{0,1},{1,0},{2,3},{3,2},{4,5},{5,4},{6,7},{7,6},{8,9},{9,8},{10,11... | collective-permute-start | bytes 2359304 | tf_op jit(solution)/shard_map/ppermute | solution.py:35
  45.0 4.8 %copy-start.1 = (bf16[1,1,2048,768]{3,2,1,0:T(8,128)(2,1)S(1)}, bf16[1,1,2048,768]{3,2,1,0:T(8,128)(2,1)}, u32[]{:S(2)}) copy-start(bf16[1,1,2048,768]{3,2,1,0:T(8,128)(2,1)} %refs_1_.5) | copy-start | bytes 9437188
  46.2 12.0 %collective-permute-start.7 = (bf16[512,384]{1,0:T(8,128)(2,1)S(1)}, bf16[512,384]{1,0:T(8,128)(2,1)S(1)}, u32[]{:S(2)}, u32[]{:S(2)}) collective-permute-start(bf16[512,384]{1,0:T(8,128)(2,1)S(1)} %get-tuple-element.43.refs_3_), channel_id=1, source_target_pairs={{0,8},{8,0},{16,24},{24,16},{1,9},{9,1},{17,25},{25,17},{2,10},{10... | collective-permute-start | bytes 1179656 | tf_op jit(solution)/shard_map/ppermute | solution.py:35
  47.8 19.2 %collective-permute-start.9 = (bf16[512,384]{1,0:T(8,128)(2,1)S(1)}, bf16[512,384]{1,0:T(8,128)(2,1)S(1)}, u32[]{:S(2)}, u32[]{:S(2)}) collective-permute-start(bf16[512,384]{1,0:T(8,128)(2,1)S(1)} %get-tuple-element.44), channel_id=1, source_target_pairs={{0,24},{8,16},{16,8},{24,0},{1,25},{9,17},{17,9},{25,1},{2,26},{10... | collective-permute-start | bytes 1179656 | tf_op jit(solution)/shard_map/ppermute | solution.py:35
  49.3 19.0 %collective-permute-start.8 = (bf16[512,384]{1,0:T(8,128)(2,1)S(1)}, bf16[512,384]{1,0:T(8,128)(2,1)S(1)}, u32[]{:S(2)}, u32[]{:S(2)}) collective-permute-start(bf16[512,384]{1,0:T(8,128)(2,1)S(1)} %get-tuple-element.44), channel_id=1, source_target_pairs={{0,16},{8,24},{16,0},{24,8},{1,17},{9,25},{17,1},{25,9},{2,18},{10... | collective-permute-start | bytes 1179656 | tf_op jit(solution)/shard_map/ppermute | solution.py:35
  69.2 26.9 %collective-permute-start.10 = (bf16[4,512,384]{2,1,0:T(8,128)(2,1)S(1)}, bf16[4,512,384]{2,1,0:T(8,128)(2,1)S(1)}, u32[]{:S(2)}, u32[]{:S(2)}) collective-permute-start(bf16[4,512,384]{2,1,0:T(8,128)(2,1)S(1)} %get-tuple-element.49.refs_3_), channel_id=1, source_target_pairs={{0,1},{1,0},{2,3},{3,2},{4,5},{5,4},{6,7},{7,6},{8,9},{9,8},{10,11... | collective-permute-start | bytes 4718600 | tf_op jit(solution)/shard_map/ppermute | solution.py:35
  69.2 26.8 %collective-permute-start.11 = (bf16[896,384]{1,0:T(8,128)(2,1)S(1)}, bf16[896,384]{1,0:T(8,128)(2,1)S(1)}, u32[]{:S(2)}, u32[]{:S(2)}) collective-permute-start(bf16[896,384]{1,0:T(8,128)(2,1)S(1)} %get-tuple-element.51), channel_id=1, source_target_pairs={{0,8},{8,0},{16,24},{24,16},{1,9},{9,1},{17,25},{25,17},{2,10},{10... | collective-permute-start | bytes 2064392 | tf_op jit(solution)/shard_map/ppermute | solution.py:35
  70.8 25.2 %collective-permute-start.12 = (bf16[896,384]{1,0:T(8,128)(2,1)S(1)}, bf16[896,384]{1,0:T(8,128)(2,1)S(1)}, u32[]{:S(2)}, u32[]{:S(2)}) collective-permute-start(bf16[896,384]{1,0:T(8,128)(2,1)S(1)} %get-tuple-element.52), channel_id=1, source_target_pairs={{0,16},{8,24},{16,0},{24,8},{1,17},{9,25},{17,1},{25,9},{2,18},{10... | collective-permute-start | bytes 2064392 | tf_op jit(solution)/shard_map/ppermute | solution.py:35
  71.3 24.7 %collective-permute-start.13 = (bf16[384,384]{1,0:T(8,128)(2,1)S(1)}, bf16[384,384]{1,0:T(8,128)(2,1)S(1)}, u32[]{:S(2)}, u32[]{:S(2)}) collective-permute-start(bf16[384,384]{1,0:T(8,128)(2,1)S(1)} %get-tuple-element.53), channel_id=1, source_target_pairs={{0,24},{8,16},{16,8},{24,0},{1,25},{9,17},{17,9},{25,1},{2,26},{10... | collective-permute-start | bytes 884744 | tf_op jit(solution)/shard_map/ppermute | solution.py:35
  100.3 23.3 %collective-permute-start.16 = (f16[1024,384]{1,0:T(8,128)(2,1)S(1)}, f16[1024,384]{1,0:T(8,128)(2,1)S(1)}, u32[]{:S(2)}, u32[]{:S(2)}) collective-permute-start(f16[1024,384]{1,0:T(8,128)(2,1)S(1)} %convert_element_type.21), channel_id=1, source_target_pairs={{0,16},{8,24},{16,0},{24,8},{1,17},{9,25},{17,1},{25,9},{2,18},{10... | collective-permute-start | bytes 2359304 | tf_op jit(solution)/shard_map/ppermute | solution.py:35
  100.8 24.0 %collective-permute-start.14 = (f16[1024,384]{1,0:T(8,128)(2,1)S(1)}, f16[1024,384]{1,0:T(8,128)(2,1)S(1)}, u32[]{:S(2)}, u32[]{:S(2)}) collective-permute-start(f16[1024,384]{1,0:T(8,128)(2,1)S(1)} %convert_element_type.21), channel_id=1, source_target_pairs={{0,8},{8,0},{16,24},{24,16},{1,9},{9,1},{17,25},{25,17},{2,10},{10... | collective-permute-start | bytes 2359304 | tf_op jit(solution)/shard_map/ppermute | solution.py:35
  124.4 11.1 %collective-permute-start.17 = (f16[512,384]{1,0:T(8,128)(2,1)}, f16[512,384]{1,0:T(8,128)(2,1)}, u32[]{:S(2)}, u32[]{:S(2)}) collective-permute-start(f16[512,384]{1,0:T(8,128)(2,1)} %slice_add_fusion), channel_id=1, source_target_pairs={{0,8},{8,0},{16,24},{24,16},{1,9},{9,1},{17,25},{25,17},{2,10},{10... | collective-permute-start | bytes 1179656 | tf_op jit(solution)/shard_map/ppermute | solution.py:35
  125.7 11.2 %collective-permute-start.15 = (f16[512,384]{1,0:T(8,128)(2,1)}, f16[512,384]{1,0:T(8,128)(2,1)}, u32[]{:S(2)}, u32[]{:S(2)}) collective-permute-start(f16[512,384]{1,0:T(8,128)(2,1)} %slice_add_fusion.1), channel_id=1, source_target_pairs={{0,16},{8,24},{16,0},{24,8},{1,17},{9,25},{17,1},{25,9},{2,18},{10... | collective-permute-start | bytes 1179656 | tf_op jit(solution)/shard_map/ppermute | solution.py:35

commit v16 on v14

--- a/solution.py
+++ b/solution.py
@@ -14,7 +14,6 @@
 AXES = ("island", "expert", "tensor")
 
 VMEM = pl.BlockSpec(memory_space=pltpu.VMEM)
-SMEM = pl.BlockSpec(memory_space=pltpu.SMEM)
 ANY = pl.BlockSpec(memory_space=pl.ANY)
 
 
@@ -33,6 +32,12 @@
 def swap(value, axis, step):
     size = lax.axis_size(axis)
     return lax.ppermute(value, axis, [(at, partner(at, step, size)) for at in range(size)])
+
+
+def position():
+    island, expert, part = (lax.axis_index(a) for a in AXES)
+    across = lax.axis_size("island") // lax.axis_size("tensor")
+    return expert, part, lax.rem(island, across), island, across, part == lax.div(island, across)
 
 
 def dot(a, b, contract):
@@ -46,7 +51,8 @@
     return copies
 
 
-def pick_kernel(experts, spot, *refs):
+def pick_kernel(experts, *refs):
+    spot = position()
     sources, outs = refs[:5], refs[5 : 5 + experts]
     table, count, weight, tokens, grads, sems = refs[5 + experts :]
     loads = copy_all(sems, list(zip(sources, refs[5 + experts : -1])))
@@ -71,7 +77,8 @@
         outs[d][slots:, :] = (chance * chosen).astype(BF16)
 
 
-def cut_kernel(islands, pieces, spot, drift, *refs):
+def cut_kernel(islands, pieces, drift, *refs):
+    spot = position()
     *blocks, sems = refs
     rows, columns = blocks[0].shape
     pairs = []
@@ -105,7 +112,8 @@
     drift_sum[...] = added
 
 
-def hidden_kernel(parts, across, spot, gate, down, *refs):
+def hidden_kernel(parts, across, gate, down, *refs):
+    spot = position()
     joined, out, norms = refs[:parts], refs[parts], refs[-1]
     rows, half = joined[0].shape[0] // 2, joined[0].shape[1]
     columns = out.shape[2]
@@ -130,7 +138,8 @@
     norms[...] = jnp.full(norms.shape, jnp.sum(hidden_gram * input_gram), F32)
 
 
-def average_kernel(islands, entries, tiles, spot, norms, drift_sum, own, moved, *refs):
+def average_kernel(islands, entries, tiles, norms, drift_sum, own, moved, *refs):
+    spot = position()
     messages = refs[:islands]
     scaled, notes, total, square = refs[islands:]
     rows = total.shape[0] // tiles
@@ -161,8 +170,8 @@
             squares = squares + jnp.sum(average * average, axis=0, keepdims=True)
         square[...] = squares
 
-    pl.when(spot[5] == 1)(lambda: compute(own))
-    pl.when(spot[5] != 1)(lambda: compute(moved))
+    pl.when(spot[5])(lambda: compute(own))
+    pl.when(jnp.logical_not(spot[5]))(lambda: compute(moved))
     peak = jnp.max(jnp.abs(total[...]))
     unit = jnp.maximum(peak, 1e-30) / 32768
     value = total[...] * (1 / unit)
@@ -173,7 +182,8 @@
     notes[...] = jnp.where(sublane == 0, jnp.sum(square[...]), unit)
 
 
-def hand_kernel(islands, tails, spot, norms, hidden, *refs):
+def hand_kernel(islands, tails, norms, hidden, *refs):
+    spot = position()
     features, relays = refs[:islands], refs[islands : islands + len(tails)]
     joined, passed, *messages = refs[islands + len(tails) :]
     across, slots, _ = hidden.shape
@@ -192,17 +202,21 @@
     block_out[...] = block[...]
 
 
-def update_kernel(entries, pieces, cuts, place, notes, momentum, *refs):
+def update_kernel(entries, pieces, cuts, notes, momentum, *refs):
     values = refs[: len(pieces)]
     new_momentum, outer_step, moved, step, in_sems, sems = refs[-6:]
+    expert, part, _, island, across, _ = position()
+    islands, experts, devices = (lax.axis_size(a) for a in AXES)
     rows, columns = values[0].shape
+    half = momentum.shape[1] // devices
     size = rows // cuts
     parts = [(n, m) for n in range(len(pieces)) for m in range(cuts)]
     spots, loads = [], []
     for i, (n, m) in enumerate(parts):
         d, first = pieces[n]
-        top = pl.multiple_of(pl.multiple_of(place[3 * d], 32) + first + m * size, 32)
-        left = pl.multiple_of(place[3 * d + 1], columns)
+        at = origin(island, d, islands)
+        top = pl.multiple_of(lax.div(at, across) * half + first + m * size, 32)
+        left = pl.multiple_of(lax.rem(at, across) * columns, columns)
         spots.append((0, pl.ds(top, size), pl.ds(left, columns)))
         here = moved.at[n, pl.ds(m * size, size)]
         loads.append(pltpu.make_async_copy(momentum.at[spots[i]], here, in_sems.at[i]))
@@ -211,7 +225,8 @@
     clip = jnp.minimum(1.0, 0.25 * math.sqrt(entries) / jnp.sqrt(square + 1e-06))
     stored = []
     for i, (n, m) in enumerate(parts):
-        unit = notes[pl.ds(place[3 * pieces[n][0] + 2], 1)][0, 1:2, :1]
+        at = (origin(island, pieces[n][0], islands) * experts + expert) * devices + part
+        unit = notes[pl.ds(at, 1)][0, 1:2, :1]
         here = slice(m * size, (m + 1) * size)
         clipped = (clip * unit) * values[n][here, :]
         loads[i].wait()
@@ -238,7 +253,6 @@
     momentum,
 ):
     islands, experts, parts = (lax.axis_size(a) for a in AXES)
-    island, expert, part = (lax.axis_index(a) for a in AXES)
     devices = islands * experts * parts
     features, hidden = gate_weight.shape[2:]
     half = features // parts
@@ -247,11 +261,7 @@
     entries = features * hidden * experts * parts
     slots = slot_token.shape[3]
     routed_rows = experts * slots
-    holder = island // across
-    spot = jnp.stack(
-        [expert, part, island % across, island, jnp.int32(across), (part == holder).astype(jnp.int32)]
-    ).astype(jnp.int32)
-
+    holder = lax.axis_index("island") // across
     handed = half // 2 if islands == 4 else 0
     steps = [0, 1, 2] if handed else list(range(islands))
     pieces = [(d, 0, half, n, 0) for n, d in enumerate(steps)]
@@ -260,7 +270,7 @@
     block_rows = [half + (handed if d else 0) for d in steps]
     picked = pl.pallas_call(
         lambda *refs: pick_kernel(experts, *refs),
-        in_specs=[SMEM] + [ANY] * 5,
+        in_specs=[ANY] * 5,
         out_specs=[VMEM] * experts,
         out_shape=[jax.ShapeDtypeStruct((2 * slots, half), BF16)] * experts,
         scratch_shapes=[
@@ -273,17 +283,17 @@
         ],
         compiler_params=params(56),
         name="pick_slots",
-    )(spot, slot_token, slot_count, slot_prob, tokens, token_grads)
+    )(slot_token, slot_count, slot_prob, tokens, token_grads)
     blocks = pl.pallas_call(
         lambda *refs: cut_kernel(islands, pieces, *refs),
-        in_specs=[SMEM, ANY],
+        in_specs=[ANY],
         out_specs=[VMEM] * len(steps),
         out_shape=[jax.ShapeDtypeStruct((rows, columns), BF16) for rows in block_rows],
         scratch_shapes=[pltpu.SemaphoreType.DMA((len(pieces),))],
         compiler_params=params(50),
         name="cut_drift",
-    )(spot, drift)
-    arrived = [picked[0]] + [swap(picked[d], "expert", d) for d in range(1, experts)]
+    )(drift)
+    arrived = [picked[0]] + [swap(picked[d], "expert", d) for d in range(experts - 1, 0, -1)]
     drift_in = [blocks[0]] + [swap(blocks[d], "island", d) for d in steps[1:]]
     arrived[0], drift_in[0] = pl.pallas_call(
         own_kernel,
@@ -341,7 +351,7 @@
 
     hidden_out, norms = pl.pallas_call(
         lambda *refs: hidden_kernel(parts, across, *refs),
-        in_specs=[SMEM] + [VMEM] * (2 + parts),
+        in_specs=[VMEM] * (2 + parts),
         out_specs=[VMEM] * 2,
         out_shape=[
             jax.ShapeDtypeStruct((across, routed_rows, columns), BF16),
@@ -349,14 +359,14 @@
         ],
         compiler_params=params(16 + routed_rows // 48),
         name="hidden_grads",
-    )(spot, gate_weight, down_weight, *joined_all)
+    )(gate_weight, down_weight, *joined_all)
     tails = [2, 1] if handed else []
     message_rows = [
         routed_rows + (half - handed if d in tails else 0) for d in range(islands)
     ]
     features_in, norms, *messages = pl.pallas_call(
         lambda *refs: hand_kernel(islands, tails, *refs),
-        in_specs=[SMEM] + [VMEM] * (2 + islands + len(relays)),
+        in_specs=[VMEM] * (2 + islands + len(relays)),
         out_specs=[VMEM] * (2 + islands),
         out_shape=[
             jax.ShapeDtypeStruct((islands, half, routed_rows), BF16),
@@ -365,14 +375,14 @@
         + [jax.ShapeDtypeStruct((rows, columns), BF16) for rows in message_rows],
         compiler_params=params(6 + routed_rows // 48),
         name="hand_on",
-    )(spot, norms, hidden_out, turned, *features_in, *relays)
+    )(norms, hidden_out, turned, *features_in, *relays)
     features_moved = spread(features_in)
     norms = lax.all_to_all(norms, AXES, split_axis=0, concat_axis=0, tiled=True)
     messages_in = [messages[0]] + [swap(messages[d], "island", d) for d in range(1, islands)]
 
     scaled, notes = pl.pallas_call(
         lambda *refs: average_kernel(islands, entries, 2, *refs),
-        in_specs=[SMEM] + [VMEM] * (4 + islands),
+        in_specs=[VMEM] * (4 + islands),
         out_specs=[VMEM] * 2,
         out_shape=[
             jax.ShapeDtypeStruct((half, columns), F32),
@@ -381,7 +391,7 @@
         scratch_shapes=[pltpu.VMEM((half, columns), F32), pltpu.VMEM((1, columns), F32)],
         compiler_params=params(8 + routed_rows // 48),
         name="average_block",
-    )(spot, norms, drift_sum, features_in, features_moved, *messages_in)
+    )(norms, drift_sum, features_in, features_moved, *messages_in)
     notes = lax.all_to_all(notes, AXES, split_axis=0, concat_axis=0, tiled=True)
 
     sent = scaled.astype(WIRE)
@@ -390,26 +400,16 @@
     for d in steps:
         values[d, 0] = swap(sent, "island", d)
     if handed:
-        nothing = jnp.where(notes[0, 1, 0] < 0, handed, 0)
-
-        def rows_of(value, first):
-            return lax.dynamic_slice(value, (first + nothing, 0), (handed, columns))
-
-        last[3, 0] = swap(rows_of(values[1, 0], 0), "island", 2)
-        last[3, handed] = swap(rows_of(values[2, 0], handed), "island", 1)
-    place = []
-    for d in range(islands):
-        at = origin(island, d, islands)
-        source = (at * experts + expert) * parts + part
-        place += [(at // across) * half, (at % across) * columns, source]
-    place = jnp.stack(place).astype(jnp.int32)
+        nothing = jnp.minimum(notes[0, 1, 0], 0.0).astype(WIRE)
+        last[3, 0] = swap(values[1, 0][:handed] + nothing, "island", 2)
+        last[3, handed] = swap(values[2, 0][handed:] + nothing, "island", 1)
     outs = []
     for values, cost, cuts in ((values, 12, 2), (last, 3, 2)):
         if not values:
             continue
         outs = pl.pallas_call(
             functools.partial(update_kernel, entries, list(values), cuts),
-            in_specs=[SMEM, VMEM, ANY] + [VMEM] * len(values) + [ANY] * len(outs),
+            in_specs=[VMEM, ANY] + [VMEM] * len(values) + [ANY] * len(outs),
             out_specs=[ANY, ANY],
             out_shape=[
                 jax.ShapeDtypeStruct(momentum.shape, F32),
@@ -421,13 +421,13 @@
                 pltpu.SemaphoreType.DMA((len(values) * cuts,)),
                 pltpu.SemaphoreType.DMA((len(values) * cuts, 2)),
             ],
-            input_output_aliases={3 + len(values) + n: n for n in range(len(outs))},
+            input_output_aliases={2 + len(values) + n: n for n in range(len(outs))},
             cost_estimate=pl.CostEstimate(
                 flops=0, bytes_accessed=cost * momentum.size, transcendentals=0
             ),
             compiler_params=params(50),
             name="update_pieces",
-        )(place, notes, momentum, *[v.astype(F32) for v in values.values()], *outs)
+        )(notes, momentum, *[v.astype(F32) for v in values.values()], *outs)
     return tuple(outs)
 
 

time: 142 us -> 136 us (0.958)
  Pallas kernels: 26.2 us -> 22.7 us
  waiting for transfers between devices: 39.1 us -> 42.4 us
  local copies, waits for them, and re-layouts: 3.55 us -> 0.53 us
  other arithmetic: 4.47 us -> 1.8 us
    ppermute x13, waiting for transfers between devices: 26.3 us -> 30.1 us  [swap(): lax.ppermute(value, axis, [(at, partner(at, step, size)) for at in range(...]
    convert_element_type x4, other arithmetic: 3.48 us -> 1.49 us  [body(): v.astype(F32)]
    dynamic_slice x2 -> x0, local copies, waits for them, and re-layouts: 1.71 us -> none  [rows_of(): return lax.dynamic_slice(value, (first + nothing, 0), (handed, columns))]
  transfers between devices with their start and end apart: 17 -> 17, of which waited for: 8 -> 6; matrix products, arithmetic and copies ran while one was open for 3% -> 2% of each run, Pallas kernels for 10% -> 10%
where the time goes in v16:
time: 136 us
  waiting for transfers between devices  42.4 us (31%)
  blocking collectives  41.6 us (31%)
  starting transfers between devices  24.8 us (18%)
  Pallas kernels  22.7 us (17%)
  other arithmetic  1.8 us (1%)
  between operations  1.67 us (1%)
    ppermute x13, waiting for transfers between devices, swap(): lax.ppermute(value, axis, [(at, partner(at, step, size)) for at in range(...  30.1 us
    all_to_all x1, blocking collectives, body(): norms = lax.all_to_all(norms, AXES, split_axis=0, concat_axis=0, tiled=True)  21.7 us
    all_to_all x1, blocking collectives, body(): notes = lax.all_to_all(notes, AXES, split_axis=0, concat_axis=0, tiled=True)  19.9 us
    ppermute x13, starting transfers between devices, swap(): lax.ppermute(value, axis, [(at, partner(at, step, size)) for at in range(...  17.1 us
    ppermute x3, waiting for transfers between devices, send_features(): return lax.ppermute(turned, ('island', 'tensor'), pairs)  12.3 us
    pallas_call x2, Pallas kernels, body(): pl.pallas_call(functools.partial(update_kernel, entries, list(values), cu...  8.31 us
    ppermute x3, starting transfers between devices, send_features(): return lax.ppermute(turned, ('island', 'tensor'), pairs)  6.25 us
    pallas_call x1, Pallas kernels, body(): pl.pallas_call(lambda *refs: hidden_kernel(parts, across, *refs), in_spec...  4.88 us
  transfers between devices with their start and end apart: 17, of which 6 were waited for; matrix products, arithmetic and copies ran while one was open for 2% of the time, Pallas kernels for 10%

profile of v16, /device:TPU:0, one launch (start us, length us, event | category | flops | bytes accessed | tf_op | source)
XLA Modules:
  0.0 135.6 jit_solution(18418702237327338466)
XLA Ops:
  0.6 2.9 %pick_slots.1 = (bf16[192,1024]{1,0:T(8,128)(2,1)}, bf16[192,1024]{1,0:T(8,128)(2,1)}, bf16[192,1024]{1,0:T(8,128)(2,1)}, bf16[192,1024]{1,0:T(8,128)(2,1)}) custom-call(s32[1,1,4,96]{3,2,1,0:T(4,128)} %refs_0_.3, s32[1,1,4]{2,1,0:T(1,128)} %refs_1_.2, f32[1,1,4,96]{3,2,1,0:T(4,128)} %refs_2_.1, bf16[1,256,1024]{2,1,0:T(8,128)(2,1)} %refs_3_.1, ...), custom_call_target="tpu_custom_call" | custom-call | tf_op jit(solution)/shard_map/pick_slots/pallas_call | solution.py:271
  3.5 0.0 copy-start.2
  3.5 5.1 %collective-permute-start = (bf16[192,1024]{1,0:T(8,128)(2,1)}, bf16[192,1024]{1,0:T(8,128)(2,1)S(1)}, u32[]{:S(2)}, u32[]{:S(2)}) collective-permute-start(bf16[192,1024]{1,0:T(8,128)(2,1)} %get-tuple-element.30), channel_id=1, source_target_pairs={{0,6},{2,4},{4,2},{6,0},{1,7},{3,5},{5,3},{7,1},{8,14},{10,12},{12... | collective-permute-start | bytes 1179656 | tf_op jit(solution)/shard_map/ppermute | solution.py:34
  8.7 0.0 collective-permute-start.1
  8.7 0.6 collective-permute-start.2
  9.3 1.9 %cut_drift.1 = (bf16[1024,384]{1,0:T(8,128)(2,1)S(1)}, bf16[1536,384]{1,0:T(8,128)(2,1)S(1)}, bf16[1536,384]{1,0:T(8,128)(2,1)S(1)}) custom-call(bf16[1,1,2048,768]{3,2,1,0:T(8,128)(2,1)} %refs_0_.4), custom_call_target="tpu_custom_call" | custom-call | tf_op jit(solution)/shard_map/cut_drift/pallas_call | solution.py:287
  11.2 1.7 %collective-permute-start.4 = (bf16[1536,384]{1,0:T(8,128)(2,1)S(1)}, bf16[1536,384]{1,0:T(8,128)(2,1)S(1)}, u32[]{:S(2)}, u32[]{:S(2)}) collective-permute-start(bf16[1536,384]{1,0:T(8,128)(2,1)S(1)} %get-tuple-element.36), channel_id=1, source_target_pairs={{0,8},{8,0},{16,24},{24,16},{1,9},{9,1},{17,25},{25,17},{2,10},{10... | collective-permute-start | bytes 3538952 | tf_op jit(solution)/shard_map/ppermute | solution.py:34
  12.9 1.5 %collective-permute-start.5 = (bf16[1536,384]{1,0:T(8,128)(2,1)S(1)}, bf16[1536,384]{1,0:T(8,128)(2,1)S(1)}, u32[]{:S(2)}, u32[]{:S(2)}) collective-permute-start(bf16[1536,384]{1,0:T(8,128)(2,1)S(1)} %get-tuple-element.37), channel_id=1, source_target_pairs={{0,16},{8,24},{16,0},{24,8},{1,17},{9,25},{17,1},{25,9},{2,18},{10... | collective-permute-start | bytes 3538952 | tf_op jit(solution)/shard_map/ppermute | solution.py:34
  14.4 0.0 copy-done.2
  14.4 0.1 own_parts.1
  14.5 4.5 %collective-permute-done.refs_1_ = bf16[192,1024]{1,0:T(8,128)(2,1)S(1)} collective-permute-done((bf16[192,1024]{1,0:T(8,128)(2,1)}, bf16[192,1024]{1,0:T(8,128)(2,1)S(1)}, u32[]{:S(2)}, u32[]{:S(2)}) %collective-permute-start) | collective-permute-done | bytes 393248 | tf_op jit(solution)/shard_map/ppermute | solution.py:34
  19.0 23.5 %collective-permute-done.1.refs_2_ = bf16[192,1024]{1,0:T(8,128)(2,1)S(1)} collective-permute-done((bf16[192,1024]{1,0:T(8,128)(2,1)}, bf16[192,1024]{1,0:T(8,128)(2,1)S(1)}, u32[]{:S(2)}, u32[]{:S(2)}) %collective-permute-start.1) | collective-permute-done | bytes 393248 | tf_op jit(solution)/shard_map/ppermute | solution.py:34
  42.4 0.0 collective-permute-done.2.refs_3_
  42.4 0.0 copy-start.1
  42.4 0.1 gather_slots.1.refs_2_.refs_0_
  42.5 0.0 copy-start
  42.5 0.1 collective-permute-start.3
  42.6 0.0 collective-permute-done.4.refs_2_
  42.6 0.0 collective-permute-done.5.refs_3_
  42.6 0.7 join_blocks.1
  43.3 1.6 %collective-permute-start.8 = (bf16[1024,384]{1,0:T(8,128)(2,1)S(1)}, bf16[1024,384]{1,0:T(8,128)(2,1)S(1)}, u32[]{:S(2)}, u32[]{:S(2)}) collective-permute-start(bf16[1024,384]{1,0:T(8,128)(2,1)S(1)} %get-tuple-element.38.refs_2_), channel_id=1, source_target_pairs={{1,25},{9,17},{16,8},{24,0},{3,27},{11,19},{18,10},{26,2},{5,29},{... | collective-permute-start | bytes 2359304 | tf_op jit(solution)/shard_map/ppermute | solution.py:337
  44.9 1.3 collective-permute-start.7
  46.2 3.4 %collective-permute-start.6 = (bf16[1024,384]{1,0:T(8,128)(2,1)S(1)}, bf16[1024,384]{1,0:T(8,128)(2,1)S(1)}, u32[]{:S(2)}, u32[]{:S(2)}) collective-permute-start(bf16[1024,384]{1,0:T(8,128)(2,1)S(1)} %get-tuple-element.38.refs_2_), channel_id=1, source_target_pairs={{0,8},{8,0},{17,25},{25,17},{2,10},{10,2},{19,27},{27,19},{4,12},{... | collective-permute-start | bytes 2359304 | tf_op jit(solution)/shard_map/ppermute | solution.py:337
  49.6 0.0 collective-permute-done.3.refs_3_
  49.6 0.0 copy-done.1
  49.6 0.0 copy-done
  49.6 4.9 %hidden_grads.1 = (bf16[2,384,384]{2,1,0:T(8,128)(2,1)S(1)}, f32[32,8,128]{2,1,0:T(8,128)S(1)}) custom-call(bf16[1,1,2048,768]{3,2,1,0:T(8,128)(2,1)S(1)} %copy-done, bf16[1,1,768,2048]{3,2,1,0:T(8,128)(2,1)S(1)} %copy-done.1, bf16[768,1024]{1,0:T(8,128)(2,1)S(1)} %gather_slots.1.refs_2_.refs_0_, bf16[768,1024]{1,0:T(8,128)(2,1)S(1)} %collective-permute-done.3.refs_3_), custom_call_target="tpu_custom_call" | custom-call | tf_op jit(solution)/shard_map/hidden_grads/pallas_call | solution.py:352
  54.5 10.3 %collective-permute-done.8.refs_5_ = bf16[1024,384]{1,0:T(8,128)(2,1)S(1)} collective-permute-done((bf16[1024,384]{1,0:T(8,128)(2,1)S(1)}, bf16[1024,384]{1,0:T(8,128)(2,1)S(1)}, u32[]{:S(2)}, u32[]{:S(2)}) %collective-permute-start.8) | collective-permute-done | bytes 786464 | tf_op jit(solution)/shard_map/ppermute | solution.py:337
  64.8 2.0 %collective-permute-done.7.refs_4_ = bf16[1024,384]{1,0:T(8,128)(2,1)S(1)} collective-permute-done((bf16[1024,384]{1,0:T(8,128)(2,1)S(1)}, bf16[1024,384]{1,0:T(8,128)(2,1)S(1)}, u32[]{:S(2)}, u32[]{:S(2)}) %collective-permute-start.7) | collective-permute-done | bytes 786464 | tf_op jit(solution)/shard_map/ppermute | solution.py:337
  66.8 0.0 collective-permute-done.6.refs_3_
  66.8 0.4 hand_on.1
  67.3 1.5 %collective-permute-start.9 = (bf16[4,1024,384]{2,1,0:T(8,128)(2,1)S(1)}, bf16[4,1024,384]{2,1,0:T(8,128)(2,1)S(1)}, u32[]{:S(2)}, u32[]{:S(2)}) collective-permute-start(bf16[4,1024,384]{2,1,0:T(8,128)(2,1)S(1)} %get-tuple-element.43.refs_2_), channel_id=1, source_target_pairs={{0,1},{8,9},{17,16},{25,24},{2,3},{10,11},{19,18},{27,26},{4,5},{1... | collective-permute-start | bytes 9437192 | tf_op jit(solution)/shard_map/ppermute | solution.py:346
  68.8 1.6 %collective-permute-start.10 = (bf16[896,384]{1,0:T(8,128)(2,1)S(1)}, bf16[896,384]{1,0:T(8,128)(2,1)S(1)}, u32[]{:S(2)}, u32[]{:S(2)}) collective-permute-start(bf16[896,384]{1,0:T(8,128)(2,1)S(1)} %get-tuple-element.45), channel_id=1, source_target_pairs={{0,8},{8,0},{16,24},{24,16},{1,9},{9,1},{17,25},{25,17},{2,10},{10... | collective-permute-start | bytes 2064392 | tf_op jit(solution)/shard_map/ppermute | solution.py:34
  70.3 0.0 collective-permute-start.11
  70.3 2.0 %collective-permute-start.12 = (bf16[384,384]{1,0:T(8,128)(2,1)S(1)}, bf16[384,384]{1,0:T(8,128)(2,1)S(1)}, u32[]{:S(2)}, u32[]{:S(2)}) collective-permute-start(bf16[384,384]{1,0:T(8,128)(2,1)S(1)} %get-tuple-element.47), channel_id=1, source_target_pairs={{0,24},{8,16},{16,8},{24,0},{1,25},{9,17},{17,9},{25,1},{2,26},{10... | collective-permute-start | bytes 884744 | tf_op jit(solution)/shard_map/ppermute | solution.py:34
  72.3 21.7 %all_to_all.10.refs_0_ = f32[32,8,128]{2,1,0:T(8,128)S(1)} all-to-all(f32[32,8,128]{2,1,0:T(8,128)S(1)} %get-tuple-element.41), channel_id=1, replica_groups=mesh['island'=4,'expert'=4,'tensor'=2] {'island','expert','tensor'}, dimensions={0} | all-to-all | bytes 262144 | tf_op jit(solution)/shard_map/all_to_all | solution.py:380
  94.0 0.0 collective-permute-done.12.refs_7_
  94.0 0.0 collective-permute-done.10.refs_5_
  94.0 0.0 collective-permute-done.11.refs_6_
  94.0 0.0 collective-permute-done.9.refs_3_
  94.0 3.5 %average_block.1 = (f32[1024,384]{1,0:T(8,128)S(1)}, f32[32,8,128]{2,1,0:T(8,128)S(1)}) custom-call(f32[32,8,128]{2,1,0:T(8,128)S(1)} %all_to_all.10.refs_0_, f32[1024,384]{1,0:T(8,128)S(1)} %get-tuple-element.42.refs_1_, bf16[4,1024,384]{2,1,0:T(8,128)(2,1)S(1)} %get-tuple-element.43.refs_2_, bf16[4,1024,384]{2,1,0:T(8,128)(2,1)S(1)} %collective-permute-done.9.refs_3_, ...), custom_call_target="tpu_custom_call" | custom-call | tf_op jit(solution)/shard_map/average_block/pallas_call | solution.py:383
  97.5 0.1 convert_element_type.21
  97.6 1.8 %collective-permute-start.15 = (f16[1024,384]{1,0:T(8,128)(2,1)S(1)}, f16[1024,384]{1,0:T(8,128)(2,1)S(1)}, u32[]{:S(2)}, u32[]{:S(2)}) collective-permute-start(f16[1024,384]{1,0:T(8,128)(2,1)S(1)} %convert_element_type.21), channel_id=1, source_target_pairs={{0,16},{8,24},{16,0},{24,8},{1,17},{9,25},{17,1},{25,9},{2,18},{10... | collective-permute-start | bytes 2359304 | tf_op jit(solution)/shard_map/ppermute | solution.py:34
  99.4 0.5 collective-permute-start.13
  100.0 19.9 %all_to_all.11.notes = f32[32,8,128]{2,1,0:T(8,128)S(1)} all-to-all(f32[32,8,128]{2,1,0:T(8,128)S(1)} %get-tuple-element.48), channel_id=1, replica_groups=mesh['island'=4,'expert'=4,'tensor'=2] {'island','expert','tensor'}, dimensions={0} | all-to-all | bytes 262144 | tf_op jit(solution)/shard_map/all_to_all | solution.py:395
  119.9 0.5 slice.13
  121.1 0.0 collective-permute-done.15
  121.1 0.1 slice_add_fusion
  121.2 0.7 collective-permute-start.16
  121.9 0.0 collective-permute-done.13
  121.9 0.1 slice_add_fusion.1
  122.0 1.4 %collective-permute-start.14 = (f16[512,384]{1,0:T(8,128)(2,1)S(1)}, f16[512,384]{1,0:T(8,128)(2,1)S(1)}, u32[]{:S(2)}, u32[]{:S(2)}) collective-permute-start(f16[512,384]{1,0:T(8,128)(2,1)S(1)} %slice_add_fusion.1), channel_id=1, source_target_pairs={{0,16},{8,24},{16,0},{24,8},{1,17},{9,25},{17,1},{25,9},{2,18},{10... | collective-permute-start | bytes 1179656 | tf_op jit(solution)/shard_map/ppermute | solution.py:34
  123.4 1.3 convert_element_type.27.refs_2_
  124.7 0.1 convert_element_type.26.refs_1_
  124.8 5.7 %update_pieces.2 = (f32[1,2048,768]{2,1,0:T(8,128)}, bf16[1,2048,768]{2,1,0:T(8,128)(2,1)}) custom-call(f32[32,8,128]{2,1,0:T(8,128)S(1)} %all_to_all.11.notes, f32[1,2048,768]{2,1,0:T(8,128)} %momentum.3, f32[1024,384]{1,0:T(8,128)S(1)} %get-tuple-element.49.refs_0_, f32[1024,384]{1,0:T(8,128)S(1)} %convert_element_type.26.refs_1_, ...), custom_call_target="tpu_custom_call" | custom-call | bytes 18874368 | tf_op jit(solution)/shard_map/update_pieces/pallas_call | solution.py:410
  130.6 1.8 %collective-permute-done.16 = f16[512,384]{1,0:T(8,128)(2,1)S(1)} collective-permute-done((f16[512,384]{1,0:T(8,128)(2,1)S(1)}, f16[512,384]{1,0:T(8,128)(2,1)S(1)}, u32[]{:S(2)}, u32[]{:S(2)}) %collective-permute-start.16) | collective-permute-done | bytes 393248 | tf_op jit(solution)/shard_map/ppermute | solution.py:34
  132.4 0.1 convert_element_type.25.refs_1_
  132.5 0.3 collective-permute-done.14
  132.8 0.1 convert_element_type.24.refs_0_
  132.8 2.6 %update_pieces.3 = (f32[1,2048,768]{2,1,0:T(8,128)}, bf16[1,2048,768]{2,1,0:T(8,128)(2,1)}) custom-call(f32[32,8,128]{2,1,0:T(8,128)S(1)} %all_to_all.11.notes, f32[1,2048,768]{2,1,0:T(8,128)} %momentum.3, f32[512,384]{1,0:T(8,128)S(1)} %convert_element_type.24.refs_0_, ...), custom_call_target="tpu_custom_call", output_to_operand_aliasing={{0}: (4, {}), {1}: (5, {})} | custom-call | bytes 4718592 | tf_op jit(solution)/shard_map/update_pieces/pallas_call | solution.py:410
Async XLA Ops:
  3.5 10.9 %copy-start.2 = (bf16[192,1024]{1,0:T(8,128)(2,1)S(1)}, bf16[192,1024]{1,0:T(8,128)(2,1)}, u32[]{:S(2)}) copy-start(bf16[192,1024]{1,0:T(8,128)(2,1)} %get-tuple-element.27.slots) | copy-start | bytes 1179652
  3.5 15.4 %collective-permute-start = (bf16[192,1024]{1,0:T(8,128)(2,1)}, bf16[192,1024]{1,0:T(8,128)(2,1)S(1)}, u32[]{:S(2)}, u32[]{:S(2)}) collective-permute-start(bf16[192,1024]{1,0:T(8,128)(2,1)} %get-tuple-element.30), channel_id=1, source_target_pairs={{0,6},{2,4},{4,2},{6,0},{1,7},{3,5},{5,3},{7,1},{8,14},{10,12},{12... | collective-permute-start | bytes 1179656 | tf_op jit(solution)/shard_map/ppermute | solution.py:34
  8.7 33.8 %collective-permute-start.1 = (bf16[192,1024]{1,0:T(8,128)(2,1)}, bf16[192,1024]{1,0:T(8,128)(2,1)S(1)}, u32[]{:S(2)}, u32[]{:S(2)}) collective-permute-start(bf16[192,1024]{1,0:T(8,128)(2,1)} %get-tuple-element.31), channel_id=1, source_target_pairs={{0,4},{2,6},{4,0},{6,2},{1,5},{3,7},{5,1},{7,3},{8,12},{10,14},{12... | collective-permute-start | bytes 1179656 | tf_op jit(solution)/shard_map/ppermute | solution.py:34
  8.7 33.8 %collective-permute-start.2 = (bf16[192,1024]{1,0:T(8,128)(2,1)}, bf16[192,1024]{1,0:T(8,128)(2,1)S(1)}, u32[]{:S(2)}, u32[]{:S(2)}) collective-permute-start(bf16[192,1024]{1,0:T(8,128)(2,1)} %get-tuple-element.32), channel_id=1, source_target_pairs={{0,2},{2,0},{4,6},{6,4},{1,3},{3,1},{5,7},{7,5},{8,10},{10,8},{12,... | collective-permute-start | bytes 1179656 | tf_op jit(solution)/shard_map/ppermute | solution.py:34
  11.2 31.4 %collective-permute-start.4 = (bf16[1536,384]{1,0:T(8,128)(2,1)S(1)}, bf16[1536,384]{1,0:T(8,128)(2,1)S(1)}, u32[]{:S(2)}, u32[]{:S(2)}) collective-permute-start(bf16[1536,384]{1,0:T(8,128)(2,1)S(1)} %get-tuple-element.36), channel_id=1, source_target_pairs={{0,8},{8,0},{16,24},{24,16},{1,9},{9,1},{17,25},{25,17},{2,10},{10... | collective-permute-start | bytes 3538952 | tf_op jit(solution)/shard_map/ppermute | solution.py:34
  12.9 29.8 %collective-permute-start.5 = (bf16[1536,384]{1,0:T(8,128)(2,1)S(1)}, bf16[1536,384]{1,0:T(8,128)(2,1)S(1)}, u32[]{:S(2)}, u32[]{:S(2)}) collective-permute-start(bf16[1536,384]{1,0:T(8,128)(2,1)S(1)} %get-tuple-element.37), channel_id=1, source_target_pairs={{0,16},{8,24},{16,0},{24,8},{1,17},{9,25},{17,1},{25,9},{2,18},{10... | collective-permute-start | bytes 3538952 | tf_op jit(solution)/shard_map/ppermute | solution.py:34
  42.4 7.2 %copy-start.1 = (bf16[1,1,768,2048]{3,2,1,0:T(8,128)(2,1)S(1)}, bf16[1,1,768,2048]{3,2,1,0:T(8,128)(2,1)}, u32[]{:S(2)}) copy-start(bf16[1,1,768,2048]{3,2,1,0:T(8,128)(2,1)} %refs_1_.3) | copy-start | bytes 9437188
  42.5 7.1 %copy-start = (bf16[1,1,2048,768]{3,2,1,0:T(8,128)(2,1)S(1)}, bf16[1,1,2048,768]{3,2,1,0:T(8,128)(2,1)}, u32[]{:S(2)}) copy-start(bf16[1,1,2048,768]{3,2,1,0:T(8,128)(2,1)} %refs_0_.5) | copy-start | bytes 9437188
  42.5 7.1 %collective-permute-start.3 = (bf16[768,1024]{1,0:T(8,128)(2,1)S(1)}, bf16[768,1024]{1,0:T(8,128)(2,1)S(1)}, u32[]{:S(2)}, u32[]{:S(2)}) collective-permute-start(bf16[768,1024]{1,0:T(8,128)(2,1)S(1)} %gather_slots.1.refs_2_.refs_0_), channel_id=1, source_target_pairs={{0,1},{1,0},{2,3},{3,2},{4,5},{5,4},{6,7},{7,6},{8,9},{9,8},{10,11... | collective-permute-start | bytes 4718600 | tf_op jit(solution)/shard_map/ppermute | solution.py:34
  43.3 21.5 %collective-permute-start.8 = (bf16[1024,384]{1,0:T(8,128)(2,1)S(1)}, bf16[1024,384]{1,0:T(8,128)(2,1)S(1)}, u32[]{:S(2)}, u32[]{:S(2)}) collective-permute-start(bf16[1024,384]{1,0:T(8,128)(2,1)S(1)} %get-tuple-element.38.refs_2_), channel_id=1, source_target_pairs={{1,25},{9,17},{16,8},{24,0},{3,27},{11,19},{18,10},{26,2},{5,29},{... | collective-permute-start | bytes 2359304 | tf_op jit(solution)/shard_map/ppermute | solution.py:337
  44.9 21.9 %collective-permute-start.7 = (bf16[1024,384]{1,0:T(8,128)(2,1)S(1)}, bf16[1024,384]{1,0:T(8,128)(2,1)S(1)}, u32[]{:S(2)}, u32[]{:S(2)}) collective-permute-start(bf16[1024,384]{1,0:T(8,128)(2,1)S(1)} %get-tuple-element.38.refs_2_), channel_id=1, source_target_pairs={{1,17},{9,25},{16,0},{24,8},{3,19},{11,27},{18,2},{26,10},{5,21},{... | collective-permute-start | bytes 2359304 | tf_op jit(solution)/shard_map/ppermute | solution.py:337
  46.2 20.6 %collective-permute-start.6 = (bf16[1024,384]{1,0:T(8,128)(2,1)S(1)}, bf16[1024,384]{1,0:T(8,128)(2,1)S(1)}, u32[]{:S(2)}, u32[]{:S(2)}) collective-permute-start(bf16[1024,384]{1,0:T(8,128)(2,1)S(1)} %get-tuple-element.38.refs_2_), channel_id=1, source_target_pairs={{0,8},{8,0},{17,25},{25,17},{2,10},{10,2},{19,27},{27,19},{4,12},{... | collective-permute-start | bytes 2359304 | tf_op jit(solution)/shard_map/ppermute | solution.py:337
  67.3 26.8 %collective-permute-start.9 = (bf16[4,1024,384]{2,1,0:T(8,128)(2,1)S(1)}, bf16[4,1024,384]{2,1,0:T(8,128)(2,1)S(1)}, u32[]{:S(2)}, u32[]{:S(2)}) collective-permute-start(bf16[4,1024,384]{2,1,0:T(8,128)(2,1)S(1)} %get-tuple-element.43.refs_2_), channel_id=1, source_target_pairs={{0,1},{8,9},{17,16},{25,24},{2,3},{10,11},{19,18},{27,26},{4,5},{1... | collective-permute-start | bytes 9437192 | tf_op jit(solution)/shard_map/ppermute | solution.py:346
  68.8 25.3 %collective-permute-start.10 = (bf16[896,384]{1,0:T(8,128)(2,1)S(1)}, bf16[896,384]{1,0:T(8,128)(2,1)S(1)}, u32[]{:S(2)}, u32[]{:S(2)}) collective-permute-start(bf16[896,384]{1,0:T(8,128)(2,1)S(1)} %get-tuple-element.45), channel_id=1, source_target_pairs={{0,8},{8,0},{16,24},{24,16},{1,9},{9,1},{17,25},{25,17},{2,10},{10... | collective-permute-start | bytes 2064392 | tf_op jit(solution)/shard_map/ppermute | solution.py:34
  70.3 23.7 %collective-permute-start.11 = (bf16[896,384]{1,0:T(8,128)(2,1)S(1)}, bf16[896,384]{1,0:T(8,128)(2,1)S(1)}, u32[]{:S(2)}, u32[]{:S(2)}) collective-permute-start(bf16[896,384]{1,0:T(8,128)(2,1)S(1)} %get-tuple-element.46), channel_id=1, source_target_pairs={{0,16},{8,24},{16,0},{24,8},{1,17},{9,25},{17,1},{25,9},{2,18},{10... | collective-permute-start | bytes 2064392 | tf_op jit(solution)/shard_map/ppermute | solution.py:34
  70.3 23.7 %collective-permute-start.12 = (bf16[384,384]{1,0:T(8,128)(2,1)S(1)}, bf16[384,384]{1,0:T(8,128)(2,1)S(1)}, u32[]{:S(2)}, u32[]{:S(2)}) collective-permute-start(bf16[384,384]{1,0:T(8,128)(2,1)S(1)} %get-tuple-element.47), channel_id=1, source_target_pairs={{0,24},{8,16},{16,8},{24,0},{1,25},{9,17},{17,9},{25,1},{2,26},{10... | collective-permute-start | bytes 884744 | tf_op jit(solution)/shard_map/ppermute | solution.py:34
  97.6 23.5 %collective-permute-start.15 = (f16[1024,384]{1,0:T(8,128)(2,1)S(1)}, f16[1024,384]{1,0:T(8,128)(2,1)S(1)}, u32[]{:S(2)}, u32[]{:S(2)}) collective-permute-start(f16[1024,384]{1,0:T(8,128)(2,1)S(1)} %convert_element_type.21), channel_id=1, source_target_pairs={{0,16},{8,24},{16,0},{24,8},{1,17},{9,25},{17,1},{25,9},{2,18},{10... | collective-permute-start | bytes 2359304 | tf_op jit(solution)/shard_map/ppermute | solution.py:34
  99.4 22.5 %collective-permute-start.13 = (f16[1024,384]{1,0:T(8,128)(2,1)S(1)}, f16[1024,384]{1,0:T(8,128)(2,1)S(1)}, u32[]{:S(2)}, u32[]{:S(2)}) collective-permute-start(f16[1024,384]{1,0:T(8,128)(2,1)S(1)} %convert_element_type.21), channel_id=1, source_target_pairs={{0,8},{8,0},{16,24},{24,16},{1,9},{9,1},{17,25},{25,17},{2,10},{10... | collective-permute-start | bytes 2359304 | tf_op jit(solution)/shard_map/ppermute | solution.py:34
  121.2 11.2 %collective-permute-start.16 = (f16[512,384]{1,0:T(8,128)(2,1)S(1)}, f16[512,384]{1,0:T(8,128)(2,1)S(1)}, u32[]{:S(2)}, u32[]{:S(2)}) collective-permute-start(f16[512,384]{1,0:T(8,128)(2,1)S(1)} %slice_add_fusion), channel_id=1, source_target_pairs={{0,8},{8,0},{16,24},{24,16},{1,9},{9,1},{17,25},{25,17},{2,10},{10... | collective-permute-start | bytes 1179656 | tf_op jit(solution)/shard_map/ppermute | solution.py:34
  122.0 10.7 %collective-permute-start.14 = (f16[512,384]{1,0:T(8,128)(2,1)S(1)}, f16[512,384]{1,0:T(8,128)(2,1)S(1)}, u32[]{:S(2)}, u32[]{:S(2)}) collective-permute-start(f16[512,384]{1,0:T(8,128)(2,1)S(1)} %slice_add_fusion.1), channel_id=1, source_target_pairs={{0,16},{8,24},{16,0},{24,8},{1,17},{9,25},{17,1},{25,9},{2,18},{10... | collective-permute-start | bytes 1179656 | tf_op jit(solution)/shard_map/ppermute | solution.py:34

commit v17 on v15

--- a/solution.py
+++ b/solution.py
@@ -14,7 +14,6 @@
 AXES = ("island", "expert", "tensor")
 
 VMEM = pl.BlockSpec(memory_space=pltpu.VMEM)
-SMEM = pl.BlockSpec(memory_space=pltpu.SMEM)
 ANY = pl.BlockSpec(memory_space=pl.ANY)
 
 
@@ -33,6 +32,12 @@
 def swap(value, axis, step):
     size = lax.axis_size(axis)
     return lax.ppermute(value, axis, [(at, partner(at, step, size)) for at in range(size)])
+
+
+def position():
+    island, expert, part = (lax.axis_index(a) for a in AXES)
+    across = lax.axis_size("island") // lax.axis_size("tensor")
+    return expert, part, lax.rem(island, across), island, across, part == lax.div(island, across)
 
 
 def dot(a, b, contract):
@@ -46,7 +51,8 @@
     return copies
 
 
-def pick_kernel(experts, spot, *refs):
+def pick_kernel(experts, *refs):
+    spot = position()
     sources, outs = refs[:5], refs[5 : 5 + experts]
     table, count, weight, tokens, grads, sems = refs[5 + experts :]
     loads = copy_all(sems, list(zip(sources, refs[5 + experts : -1])))
@@ -71,14 +77,19 @@
         outs[d][slots:, :] = (chance * chosen).astype(BF16)
 
 
-def cut_kernel(islands, pieces, spot, drift, *blocks):
+def cut_kernel(islands, pieces, drift, *refs):
+    spot = position()
+    *blocks, sems = refs
     rows, columns = blocks[0].shape
+    pairs = []
     for d, first, count_rows, target, at_row in pieces:
         at = partner(spot[3], d, islands)
         top = pl.multiple_of(lax.div(at, spot[4]) * rows + first, 32)
         left = pl.multiple_of(lax.rem(at, spot[4]) * columns, columns)
-        source = drift[0, 0, pl.ds(top, count_rows), pl.ds(left, columns)]
-        blocks[target][at_row : at_row + count_rows, :] = source
+        source = drift.at[0, 0, pl.ds(top, count_rows), pl.ds(left, columns)]
+        pairs.append((source, blocks[target].at[pl.ds(at_row, count_rows)]))
+    for copy in copy_all(sems, pairs):
+        copy.wait()
 
 
 def gather_kernel(count, *refs):
@@ -89,7 +100,9 @@
         grads[n * slots : (n + 1) * slots, :] = piece[slots:, :]
 
 
-def join_kernel(parts, blocks, spot, *refs):
+def join_kernel(parts, blocks, *refs):
+    spot = position()
+    away = spot[1] ^ lax.div(spot[3], spot[4])
     joined, drifts = refs[:parts], refs[parts : parts + blocks]
     shares, (drift_sum, *relays) = refs[parts + blocks :][:parts], refs[parts + blocks :][parts:]
     rows = drift_sum.shape[0]
@@ -103,17 +116,19 @@
 
     for r in range(parts):
         for t in range(parts):
-            pl.when(partner(spot[5], r, parts) == t)(functools.partial(take, shares[r], joined[t]))
+            pl.when(partner(away, r, parts) == t)(functools.partial(take, shares[r], joined[t]))
     added = drifts[0][...].astype(F32)
     for other in drifts[1:]:
         added = added + other[:rows, :].astype(F32)
     drift_sum[...] = added
 
 
-def hidden_kernel(parts, across, spot, gate, down, *refs):
-    inputs, grads, (out, norms) = refs[:parts], refs[parts : 2 * parts], refs[2 * parts :]
+def hidden_kernel(parts, islands, tails, gate, down, *refs):
+    spot = position()
+    inputs, grads, refs = refs[:parts], refs[parts : 2 * parts], refs[2 * parts :]
+    relays, (*messages, norms, hidden) = refs[: len(tails)], refs[len(tails) :]
+    across, slots, columns = hidden.shape
     half = inputs[0].shape[1]
-    columns = out.shape[2]
     starts = [pl.multiple_of(origin(spot[1], t, parts) * half, half) for t in range(parts)]
     hidden_gram = 0.0
     for r in range(across):
@@ -126,8 +141,13 @@
             block = down[0, 0, first : first + columns, pl.ds(starts[t], half)]
             back = back + dot(grads[t][...], block, ((1,), (1,)))
         rounded = (back * (value / (1.0 + jnp.exp(-value)))).astype(BF16)
-        out[r] = rounded
+        hidden[r] = rounded
         hidden_gram = hidden_gram + dot(rounded, rounded, ((1,), (1,)))
+    for d, message in enumerate(messages):
+        block = lax.rem(partner(spot[3], d, islands), across)
+        message[:slots, :] = hidden[pl.ds(block, 1)][0]
+        if d in tails:
+            message[slots:, :] = relays[tails.index(d)][...]
     input_gram = 0.0
     for t in range(parts):
         features = inputs[t][...]
@@ -135,12 +155,23 @@
     norms[...] = jnp.full(norms.shape, jnp.sum(hidden_gram * input_gram), F32)
 
 
-def average_kernel(islands, entries, parts, spot, norms, drift_sum, *refs):
-    features, messages = refs[:parts], refs[parts : parts + islands]
-    scaled, notes, total, square = refs[parts + islands :]
-    rows = total.shape[0] // parts
-    slots = features[0].shape[2]
+def average_kernel(islands, entries, norms, drift_sum, *refs):
+    spot = position()
+    mine, other, messages = refs[:islands], refs[islands : islands + 3], refs[islands + 3 : 2 * islands + 3]
+    scaled, notes, total, square = refs[2 * islands + 3 :]
+    rows, slots = mine[0].shape
     group = norms.shape[0] // islands
+
+    def moved(d):
+        if d == 0:
+            return other[0][...]
+        split = other[1].shape[0]
+        first, last = (d - 1) * rows, d * rows
+        above = other[1][first : min(last, split), :] if first < split else None
+        below = other[2][max(first - split, 0) : last - split, :] if last > split else None
+        found = [v for v in (above, below) if v is not None]
+        return found[0] if len(found) == 1 else jnp.concatenate(found)
+
     scales = []
     for d in range(islands):
         at = origin(spot[3], d, islands)
@@ -150,7 +181,7 @@
 
     def compute(at):
         squares = 0.0
-        for m in range(parts):
+        for m in range(2):
             part = slice(m * rows, (m + 1) * rows)
             average = drift_sum[part, :]
             if handed:
@@ -161,12 +192,12 @@
             average = average * (1.0 / islands)
             for d in range(islands):
                 factor = messages[d][:slots, :]
-                average = average + scales[d] * dot(features[partner(at, m, parts)][d], factor, ((1,), (0,)))
+                average = average + scales[d] * dot(mine[d][...] if m == at else moved(d), factor, ((1,), (0,)))
             total[part, :] = average
             squares = squares + jnp.sum(average * average, axis=0, keepdims=True)
         square[...] = squares
 
-    for at in range(parts):
+    for at in range(2):
         pl.when(spot[1] == at)(functools.partial(compute, at))
     peak = jnp.max(jnp.abs(total[...]))
     unit = jnp.maximum(peak, 1e-30) / 32768
@@ -178,18 +209,18 @@
     notes[...] = jnp.where(sublane == 0, jnp.sum(square[...]), unit)
 
 
-def hand_kernel(islands, tails, spot, norms, hidden, *refs):
-    features, relays = refs[:islands], refs[islands : islands + len(tails)]
-    joined, passed, *messages = refs[islands + len(tails) :]
-    across, slots, _ = hidden.shape
-    for n in range(islands):
-        joined[n] = features[n][...]
+def hand_kernel(count, norms, *refs):
+    shares, (_, top, bottom, passed) = refs[:count], refs[count:]
     passed[...] = norms[...]
-    for d, message in enumerate(messages):
-        block = lax.rem(partner(spot[3], d, islands), across)
-        message[:slots, :] = hidden[pl.ds(block, 1)][0]
-        if d in tails:
-            message[slots:, :] = relays[tails.index(d)][...]
+    size = shares[0].shape[0]
+    split = top.shape[0]
+    for n, share in enumerate(shares):
+        cut = min(max(split - n * size, 0), size)
+        if cut:
+            top[n * size : n * size + cut, :] = share[:cut, :]
+        if cut < size:
+            first = n * size + cut - split
+            bottom[first : first + size - cut, :] = share[cut:, :]
 
 
 def own_kernel(slots, block, slots_out, block_out):
@@ -197,17 +228,21 @@
     block_out[...] = block[...]
 
 
-def update_kernel(entries, pieces, cuts, place, notes, momentum, *refs):
+def update_kernel(entries, pieces, cuts, notes, momentum, *refs):
     values = refs[: len(pieces)]
     new_momentum, outer_step, moved, step, in_sems, sems = refs[-6:]
+    expert, part, _, island, across, _ = position()
+    islands, experts, devices = (lax.axis_size(a) for a in AXES)
     rows, columns = values[0].shape
+    half = momentum.shape[1] // devices
     size = rows // cuts
     parts = [(n, m) for n in range(len(pieces)) for m in range(cuts)]
     spots, loads = [], []
     for i, (n, m) in enumerate(parts):
         d, first = pieces[n]
-        top = pl.multiple_of(pl.multiple_of(place[3 * d], 32) + first + m * size, 32)
-        left = pl.multiple_of(place[3 * d + 1], columns)
+        at = origin(island, d, islands)
+        top = pl.multiple_of(lax.div(at, across) * half + first + m * size, 32)
+        left = pl.multiple_of(lax.rem(at, across) * columns, columns)
         spots.append((0, pl.ds(top, size), pl.ds(left, columns)))
         here = moved.at[n, pl.ds(m * size, size)]
         loads.append(pltpu.make_async_copy(momentum.at[spots[i]], here, in_sems.at[i]))
@@ -216,7 +251,8 @@
     clip = jnp.minimum(1.0, 0.25 * math.sqrt(entries) / jnp.sqrt(square + 1e-06))
     stored = []
     for i, (n, m) in enumerate(parts):
-        unit = notes[pl.ds(place[3 * pieces[n][0] + 2], 1)][0, 1:2, :1]
+        at = (origin(island, pieces[n][0], islands) * experts + expert) * devices + part
+        unit = notes[pl.ds(at, 1)][0, 1:2, :1]
         here = slice(m * size, (m + 1) * size)
         clipped = (clip * unit) * values[n][here, :]
         loads[i].wait()
@@ -243,7 +279,6 @@
     momentum,
 ):
     islands, experts, parts = (lax.axis_size(a) for a in AXES)
-    island, expert, part = (lax.axis_index(a) for a in AXES)
     devices = islands * experts * parts
     features, hidden = gate_weight.shape[2:]
     half = features // parts
@@ -252,11 +287,7 @@
     entries = features * hidden * experts * parts
     slots = slot_token.shape[3]
     routed_rows = experts * slots
-    holder = island // across
-    spot = jnp.stack(
-        [expert, part, island % across, island, jnp.int32(across), part ^ holder]
-    ).astype(jnp.int32)
-
+    holder = lax.axis_index("island") // across
     handed = half // 2 if islands == 4 else 0
     steps = [0, 1, 2] if handed else list(range(islands))
     pieces = [(d, 0, half, n, 0) for n, d in enumerate(steps)]
@@ -265,7 +296,7 @@
     block_rows = [half + (handed if d else 0) for d in steps]
     picked = pl.pallas_call(
         lambda *refs: pick_kernel(experts, *refs),
-        in_specs=[SMEM] + [ANY] * 5,
+        in_specs=[ANY] * 5,
         out_specs=[VMEM] * experts,
         out_shape=[jax.ShapeDtypeStruct((2 * slots, half), BF16)] * experts,
         scratch_shapes=[
@@ -278,16 +309,17 @@
         ],
         compiler_params=params(56),
         name="pick_slots",
-    )(spot, slot_token, slot_count, slot_prob, tokens, token_grads)
+    )(slot_token, slot_count, slot_prob, tokens, token_grads)
     blocks = pl.pallas_call(
         lambda *refs: cut_kernel(islands, pieces, *refs),
-        in_specs=[SMEM, VMEM],
+        in_specs=[ANY],
         out_specs=[VMEM] * len(steps),
         out_shape=[jax.ShapeDtypeStruct((rows, columns), BF16) for rows in block_rows],
-        compiler_params=params(16),
+        scratch_shapes=[pltpu.SemaphoreType.DMA((len(pieces),))],
+        compiler_params=params(50),
         name="cut_drift",
-    )(spot, drift)
-    arrived = [picked[0]] + [swap(picked[d], "expert", d) for d in range(1, experts)]
+    )(drift)
+    arrived = [picked[0]] + [swap(picked[d], "expert", d) for d in range(experts - 1, 0, -1)]
     drift_in = [blocks[0]] + [swap(blocks[d], "island", d) for d in steps[1:]]
     arrived[0], drift_in[0] = pl.pallas_call(
         own_kernel,
@@ -315,52 +347,49 @@
     share = jax.ShapeDtypeStruct((half // parts, routed_rows), BF16)
     outputs = pl.pallas_call(
         lambda *refs: join_kernel(parts, len(steps), *refs),
-        in_specs=[SMEM] + [VMEM] * (parts + len(steps)),
+        in_specs=[VMEM] * (parts + len(steps)),
         out_specs=[VMEM] * (parts + (3 if handed else 1)),
         out_shape=[share] * parts
         + [jax.ShapeDtypeStruct((half, columns), F32)]
         + [jax.ShapeDtypeStruct((handed, columns), BF16)] * (2 if handed else 0),
         compiler_params=params(14 + routed_rows // 48),
         name="join_blocks",
-    )(spot, *inputs_all, *drift_in)
+    )(*inputs_all, *drift_in)
     shares, (drift_sum, *relays) = outputs[:parts], outputs[parts:]
 
+    own_moved = swap(shares[0], "tensor", 1)
     features_in = [swap(shares[d // across], "island", d) for d in range(1, islands)]
 
-    hidden_out, norms = pl.pallas_call(
-        lambda *refs: hidden_kernel(parts, across, *refs),
-        in_specs=[SMEM] + [VMEM] * (2 + 2 * parts),
-        out_specs=[VMEM] * 2,
-        out_shape=[
-            jax.ShapeDtypeStruct((across, routed_rows, columns), BF16),
-            jax.ShapeDtypeStruct((devices, 8, 128), F32),
-        ],
-        compiler_params=params(16 + routed_rows // 48),
+    tails = [2, 1] if handed else []
+    message_rows = [routed_rows + (half - handed if d in tails else 0) for d in range(islands)]
+    *messages, norms = pl.pallas_call(
+        lambda *refs: hidden_kernel(parts, islands, tails, *refs),
+        in_specs=[VMEM] * (2 + 2 * parts + len(tails)),
+        out_specs=[VMEM] * (islands + 1),
+        out_shape=[jax.ShapeDtypeStruct((rows, columns), BF16) for rows in message_rows]
+        + [jax.ShapeDtypeStruct((devices, 8, 128), F32)],
+        scratch_shapes=[pltpu.VMEM((across, routed_rows, columns), BF16)],
+        compiler_params=params(18 + routed_rows // 48),
         name="hidden_grads",
-    )(spot, gate_weight, down_weight, *inputs_all, *grads_all)
-    tails = [2, 1] if handed else []
-    message_rows = [
-        routed_rows + (half - handed if d in tails else 0) for d in range(islands)
-    ]
-    features_in, norms, *messages = pl.pallas_call(
-        lambda *refs: hand_kernel(islands, tails, *refs),
-        in_specs=[SMEM] + [VMEM] * (2 + islands + len(relays)),
-        out_specs=[VMEM] * (2 + islands),
-        out_shape=[
-            jax.ShapeDtypeStruct((islands, half // parts, routed_rows), BF16),
-            jax.ShapeDtypeStruct(norms.shape, F32),
-        ]
-        + [jax.ShapeDtypeStruct((rows, columns), BF16) for rows in message_rows],
-        compiler_params=params(6 + routed_rows // 48),
+    )(gate_weight, down_weight, *inputs_all, *grads_all, *relays)
+    messages_in = [messages[0]] + [swap(messages[d], "island", d) for d in range(1, islands)]
+
+    middle = (islands - 1) * (half // parts) // 2
+    *halves, norms = pl.pallas_call(
+        lambda *refs: hand_kernel(islands - 1, *refs),
+        in_specs=[VMEM] * islands + [ANY],
+        out_specs=[VMEM] * 3,
+        out_shape=[jax.ShapeDtypeStruct((middle, routed_rows), BF16)] * 2
+        + [jax.ShapeDtypeStruct(norms.shape, F32)],
+        compiler_params=params(4 + routed_rows // 48),
         name="hand_on",
-    )(spot, norms, hidden_out, shares[0], *features_in, *relays)
-    features_of = [features_in] + [swap(features_in, "tensor", t) for t in range(1, parts)]
+    )(norms, *features_in, own_moved)
+    halves_moved = [swap(v, "tensor", 1) for v in halves]
     norms = lax.all_to_all(norms, AXES, split_axis=0, concat_axis=0, tiled=True)
-    messages_in = [messages[0]] + [swap(messages[d], "island", d) for d in range(1, islands)]
 
     scaled, notes = pl.pallas_call(
-        lambda *refs: average_kernel(islands, entries, parts, *refs),
-        in_specs=[SMEM] + [VMEM] * (2 + parts + islands),
+        lambda *refs: average_kernel(islands, entries, *refs),
+        in_specs=[VMEM] * (5 + 2 * islands),
         out_specs=[VMEM] * 2,
         out_shape=[
             jax.ShapeDtypeStruct((half, columns), F32),
@@ -369,7 +398,7 @@
         scratch_shapes=[pltpu.VMEM((half, columns), F32), pltpu.VMEM((1, columns), F32)],
         compiler_params=params(8 + routed_rows // 48),
         name="average_block",
-    )(spot, norms, drift_sum, *features_of, *messages_in)
+    )(norms, drift_sum, shares[0], *features_in, own_moved, *halves_moved, *messages_in)
     notes = lax.all_to_all(notes, AXES, split_axis=0, concat_axis=0, tiled=True)
 
     sent = scaled.astype(WIRE)
@@ -381,19 +410,13 @@
         nothing = jnp.minimum(notes[0, 1, 0], 0.0).astype(WIRE)
         last[3, 0] = swap(values[1, 0][:handed] + nothing, "island", 2)
         last[3, handed] = swap(values[2, 0][handed:] + nothing, "island", 1)
-    place = []
-    for d in range(islands):
-        at = origin(island, d, islands)
-        source = (at * experts + expert) * parts + part
-        place += [(at // across) * half, (at % across) * columns, source]
-    place = jnp.stack(place).astype(jnp.int32)
     outs = []
     for values, cost, cuts in ((values, 12, 2), (last, 3, 2)):
         if not values:
             continue
         outs = pl.pallas_call(
             functools.partial(update_kernel, entries, list(values), cuts),
-            in_specs=[SMEM, VMEM, ANY] + [VMEM] * len(values) + [ANY] * len(outs),
+            in_specs=[VMEM, ANY] + [VMEM] * len(values) + [ANY] * len(outs),
             out_specs=[ANY, ANY],
             out_shape=[
                 jax.ShapeDtypeStruct(momentum.shape, F32),
@@ -405,13 +428,13 @@
                 pltpu.SemaphoreType.DMA((len(values) * cuts,)),
                 pltpu.SemaphoreType.DMA((len(values) * cuts, 2)),
             ],
-            input_output_aliases={3 + len(values) + n: n for n in range(len(outs))},
+            input_output_aliases={2 + len(values) + n: n for n in range(len(outs))},
             cost_estimate=pl.CostEstimate(
                 flops=0, bytes_accessed=cost * momentum.size, transcendentals=0
             ),
             compiler_params=params(50),
             name="update_pieces",
-        )(place, notes, momentum, *[v.astype(F32) for v in values.values()], *outs)
+        )(notes, momentum, *[v.astype(F32) for v in values.values()], *outs)
     return tuple(outs)
 
 

time: 142 us -> 135 us (0.951)
  the two profiles are of different devices: /device:TPU:8 before, /device:TPU:0 now
where the time goes in v17:
time: 135 us
  waiting for transfers between devices  54.5 us (40%)
  starting transfers between devices  27.8 us (21%)
  Pallas kernels  26.4 us (20%)
  blocking collectives  19.2 us (14%)
  local copies, waits for them, and re-layouts  3.2 us (2%)
  other arithmetic  1.8 us (1%)
  between operations  1.62 us (1%)
    ppermute x20, waiting for transfers between devices, swap(): lax.ppermute(value, axis, [(at, partner(at, step, size)) for at in range(...  54.5 us
    ppermute x20, starting transfers between devices, swap(): lax.ppermute(value, axis, [(at, partner(at, step, size)) for at in range(...  24.3 us
    all_to_all x1, blocking collectives, body(): notes = lax.all_to_all(notes, AXES, split_axis=0, concat_axis=0, tiled=True)  19.2 us
    pallas_call x2, Pallas kernels, body(): pl.pallas_call(functools.partial(update_kernel, entries, list(values), cu...  8.31 us
    pallas_call x1, Pallas kernels, body(): pl.pallas_call(lambda *refs: hidden_kernel(parts, islands, tails, *refs),...  6.18 us
    pallas_call x1, Pallas kernels, body(): pl.pallas_call(lambda *refs: average_kernel(islands, entries, *refs), in_...  5.17 us
    all_to_all x1, starting transfers between devices, body(): norms = lax.all_to_all(norms, AXES, split_axis=0, concat_axis=0, tiled=True)  3.57 us
    pallas_call x1, Pallas kernels, body(): pl.pallas_call(lambda *refs: pick_kernel(experts, *refs), in_specs=[ANY]...  2.9 us
  transfers between devices with their start and end apart: 21, of which 9 were waited for; matrix products, arithmetic and copies ran while one was open for 2% of the time, Pallas kernels for 12%

profile of v17, /device:TPU:0, one launch (start us, length us, event | category | flops | bytes accessed | tf_op | source)
XLA Modules:
  0.0 134.6 jit_solution(885397037669021077)
XLA Ops:
  0.6 2.9 %pick_slots.1 = (bf16[192,1024]{1,0:T(8,128)(2,1)}, bf16[192,1024]{1,0:T(8,128)(2,1)}, bf16[192,1024]{1,0:T(8,128)(2,1)}, bf16[192,1024]{1,0:T(8,128)(2,1)}) custom-call(s32[1,1,4,96]{3,2,1,0:T(4,128)} %refs_0_.3, s32[1,1,4]{2,1,0:T(1,128)} %refs_1_.2, f32[1,1,4,96]{3,2,1,0:T(4,128)} %refs_2_.1, bf16[1,256,1024]{2,1,0:T(8,128)(2,1)} %refs_3_.1, ...), custom_call_target="tpu_custom_call" | custom-call | tf_op jit(solution)/shard_map/pick_slots/pallas_call | solution.py:297
  3.5 0.0 copy-start.2
  3.5 5.1 %collective-permute-start = (bf16[192,1024]{1,0:T(8,128)(2,1)}, bf16[192,1024]{1,0:T(8,128)(2,1)S(1)}, u32[]{:S(2)}, u32[]{:S(2)}) collective-permute-start(bf16[192,1024]{1,0:T(8,128)(2,1)} %get-tuple-element.33), channel_id=1, source_target_pairs={{0,6},{2,4},{4,2},{6,0},{1,7},{3,5},{5,3},{7,1},{8,14},{10,12},{12... | collective-permute-start | bytes 1179656 | tf_op jit(solution)/shard_map/ppermute | solution.py:34
  8.7 0.0 collective-permute-start.1
  8.7 0.6 collective-permute-start.2
  9.3 1.9 %cut_drift.1 = (bf16[1024,384]{1,0:T(8,128)(2,1)S(1)}, bf16[1536,384]{1,0:T(8,128)(2,1)S(1)}, bf16[1536,384]{1,0:T(8,128)(2,1)S(1)}) custom-call(bf16[1,1,2048,768]{3,2,1,0:T(8,128)(2,1)} %refs_0_.4), custom_call_target="tpu_custom_call" | custom-call | tf_op jit(solution)/shard_map/cut_drift/pallas_call | solution.py:313
  11.2 1.7 %collective-permute-start.5 = (bf16[1536,384]{1,0:T(8,128)(2,1)S(1)}, bf16[1536,384]{1,0:T(8,128)(2,1)S(1)}, u32[]{:S(2)}, u32[]{:S(2)}) collective-permute-start(bf16[1536,384]{1,0:T(8,128)(2,1)S(1)} %get-tuple-element.39), channel_id=1, source_target_pairs={{0,8},{8,0},{16,24},{24,16},{1,9},{9,1},{17,25},{25,17},{2,10},{10... | collective-permute-start | bytes 3538952 | tf_op jit(solution)/shard_map/ppermute | solution.py:34
  12.9 1.5 %collective-permute-start.6 = (bf16[1536,384]{1,0:T(8,128)(2,1)S(1)}, bf16[1536,384]{1,0:T(8,128)(2,1)S(1)}, u32[]{:S(2)}, u32[]{:S(2)}) collective-permute-start(bf16[1536,384]{1,0:T(8,128)(2,1)S(1)} %get-tuple-element.40), channel_id=1, source_target_pairs={{0,16},{8,24},{16,0},{24,8},{1,17},{9,25},{17,1},{25,9},{2,18},{10... | collective-permute-start | bytes 3538952 | tf_op jit(solution)/shard_map/ppermute | solution.py:34
  14.4 0.1 own_parts.1
  14.5 4.5 %collective-permute-done.refs_1_ = bf16[192,1024]{1,0:T(8,128)(2,1)S(1)} collective-permute-done((bf16[192,1024]{1,0:T(8,128)(2,1)}, bf16[192,1024]{1,0:T(8,128)(2,1)S(1)}, u32[]{:S(2)}, u32[]{:S(2)}) %collective-permute-start) | collective-permute-done | bytes 393248 | tf_op jit(solution)/shard_map/ppermute | solution.py:34
  19.0 23.5 %collective-permute-done.1.refs_2_ = bf16[192,1024]{1,0:T(8,128)(2,1)S(1)} collective-permute-done((bf16[192,1024]{1,0:T(8,128)(2,1)}, bf16[192,1024]{1,0:T(8,128)(2,1)S(1)}, u32[]{:S(2)}, u32[]{:S(2)}) %collective-permute-start.1) | collective-permute-done | bytes 393248 | tf_op jit(solution)/shard_map/ppermute | solution.py:34
  42.4 0.0 collective-permute-done.2.refs_3_
  42.4 0.1 gather_slots.1
  42.5 0.1 collective-permute-start.3
  42.6 0.5 collective-permute-start.4
  43.1 1.8 %collective-permute-done.3.refs_1_.refs_3_ = bf16[384,1024]{1,0:T(8,128)(2,1)S(1)} collective-permute-done((bf16[384,1024]{1,0:T(8,128)(2,1)S(1)}, bf16[384,1024]{1,0:T(8,128)(2,1)S(1)}, u32[]{:S(2)}, u32[]{:S(2)}) %collective-permute-start.3) | collective-permute-done | bytes 786464 | tf_op jit(solution)/shard_map/ppermute | solution.py:34
  44.9 0.0 collective-permute-done.5.refs_3_
  44.9 0.0 collective-permute-done.6.refs_4_
  44.9 0.6 join_blocks.1
  45.6 2.5 %collective-permute-start.9 = (bf16[512,384]{1,0:T(8,128)(2,1)S(1)}, bf16[512,384]{1,0:T(8,128)(2,1)S(1)}, u32[]{:S(2)}, u32[]{:S(2)}) collective-permute-start(bf16[512,384]{1,0:T(8,128)(2,1)S(1)} %get-tuple-element.45), channel_id=1, source_target_pairs={{0,24},{8,16},{16,8},{24,0},{1,25},{9,17},{17,9},{25,1},{2,26},{10... | collective-permute-start | bytes 1179656 | tf_op jit(solution)/shard_map/ppermute | solution.py:34
  48.1 0.5 collective-permute-start.8
  48.6 0.0 collective-permute-start.10
  48.6 0.5 collective-permute-start.7
  49.1 0.0 collective-permute-done.4.refs_5_
  49.1 6.2 %hidden_grads.1 = (bf16[384,384]{1,0:T(8,128)(2,1)S(1)}, bf16[896,384]{1,0:T(8,128)(2,1)}, bf16[896,384]{1,0:T(8,128)(2,1)}, bf16[384,384]{1,0:T(8,128)(2,1)}, f32[32,8,128]{2,1,0:T(8,128)S(1)}) custom-call(bf16[1,1,2048,768]{3,2,1,0:T(8,128)(2,1)S(1)} %copy-done, bf16[1,1,768,2048]{3,2,1,0:T(8,128)(2,1)S(1)} %copy-done.1, ...), custom_call_target="tpu_custom_call" | custom-call | tf_op jit(solution)/shard_map/hidden_grads/pallas_call | solution.py:365
  55.3 0.7 copy-done.5
  56.0 1.5 %collective-permute-start.13 = (bf16[896,384]{1,0:T(8,128)(2,1)}, bf16[896,384]{1,0:T(8,128)(2,1)}, u32[]{:S(2)}, u32[]{:S(2)}) collective-permute-start(bf16[896,384]{1,0:T(8,128)(2,1)} %get-tuple-element.51), channel_id=1, source_target_pairs={{0,8},{8,0},{16,24},{24,16},{1,9},{9,1},{17,25},{25,17},{2,10},{10... | collective-permute-start | bytes 2064392 | tf_op jit(solution)/shard_map/ppermute | solution.py:34
  57.5 1.0 collective-permute-done.9.refs_3_.refs_5_
  58.5 1.5 %collective-permute-start.14 = (bf16[896,384]{1,0:T(8,128)(2,1)}, bf16[896,384]{1,0:T(8,128)(2,1)}, u32[]{:S(2)}, u32[]{:S(2)}) collective-permute-start(bf16[896,384]{1,0:T(8,128)(2,1)} %get-tuple-element.52), channel_id=1, source_target_pairs={{0,16},{8,24},{16,0},{24,8},{1,17},{9,25},{17,1},{25,9},{2,18},{10... | collective-permute-start | bytes 2064392 | tf_op jit(solution)/shard_map/ppermute | solution.py:34
  60.0 6.2 %collective-permute-done.8.refs_2_.refs_4_ = bf16[512,384]{1,0:T(8,128)(2,1)S(1)} collective-permute-done((bf16[512,384]{1,0:T(8,128)(2,1)S(1)}, bf16[512,384]{1,0:T(8,128)(2,1)S(1)}, u32[]{:S(2)}, u32[]{:S(2)}) %collective-permute-start.8) | collective-permute-done | bytes 393248 | tf_op jit(solution)/shard_map/ppermute | solution.py:34
  66.2 0.0 collective-permute-done.10.refs_4_.refs_6_
  66.2 0.8 collective-permute-done.7.refs_1_.refs_3_
  67.0 1.2 hand_on.1
  68.2 0.0 collective-permute-start.11
  68.2 0.5 collective-permute-start.12
  68.7 1.7 %collective-permute-start.15 = (bf16[384,384]{1,0:T(8,128)(2,1)}, bf16[384,384]{1,0:T(8,128)(2,1)}, u32[]{:S(2)}, u32[]{:S(2)}) collective-permute-start(bf16[384,384]{1,0:T(8,128)(2,1)} %get-tuple-element.53), channel_id=1, source_target_pairs={{0,24},{8,16},{16,8},{24,0},{1,25},{9,17},{17,9},{25,1},{2,26},{10... | collective-permute-start | bytes 884744 | tf_op jit(solution)/shard_map/ppermute | solution.py:34
  70.3 3.6 %all-to-all-start = ((f32[32,8,128]{2,1,0:T(8,128)}), f32[32,8,128]{2,1,0:T(8,128)S(1)}, u32[]{:S(2)}, u32[]{:S(2)}) async-start(f32[32,8,128]{2,1,0:T(8,128)} %get-tuple-element.46), calls=%async_computation | async-start | bytes 262144 | tf_op jit(solution)/shard_map/all_to_all | solution.py:388
  73.9 14.7 %collective-permute-done.15.refs_12_ = bf16[384,384]{1,0:T(8,128)(2,1)} collective-permute-done((bf16[384,384]{1,0:T(8,128)(2,1)}, bf16[384,384]{1,0:T(8,128)(2,1)}, u32[]{:S(2)}, u32[]{:S(2)}) %collective-permute-start.15) | collective-permute-done | bytes 294944 | tf_op jit(solution)/shard_map/ppermute | solution.py:34
  88.6 0.0 all-to-all-done.refs_0_
  88.6 0.0 collective-permute-done.13.refs_10_
  88.6 0.0 collective-permute-done.14.refs_11_
  88.6 0.0 collective-permute-done.11.refs_7_
  88.6 0.0 collective-permute-done.12.refs_8_
  88.6 1.0 copy-done.4
  89.6 1.0 copy-done.6
  90.6 5.2 %average_block.1 = (f32[1024,384]{1,0:T(8,128)S(1)}, f32[32,8,128]{2,1,0:T(8,128)S(1)}) custom-call(f32[32,8,128]{2,1,0:T(8,128)S(1)} %all-to-all-done.refs_0_, f32[1024,384]{1,0:T(8,128)S(1)} %get-tuple-element.47.refs_1_, bf16[512,384]{1,0:T(8,128)(2,1)S(1)} %copy-done.4, bf16[512,384]{1,0:T(8,128)(2,1)S(1)} %collective-permute-done.7.refs_1_.refs_3_, ...), custom_call_target="tpu_custom_call" | custom-call | tf_op jit(solution)/shard_map/average_block/pallas_call | solution.py:390
  95.8 0.1 convert_element_type.21
  95.9 1.6 %collective-permute-start.18 = (f16[1024,384]{1,0:T(8,128)(2,1)S(1)}, f16[1024,384]{1,0:T(8,128)(2,1)S(1)}, u32[]{:S(2)}, u32[]{:S(2)}) collective-permute-start(f16[1024,384]{1,0:T(8,128)(2,1)S(1)} %convert_element_type.21), channel_id=1, source_target_pairs={{0,16},{8,24},{16,0},{24,8},{1,17},{9,25},{17,1},{25,9},{2,18},{10... | collective-permute-start | bytes 2359304 | tf_op jit(solution)/shard_map/ppermute | solution.py:34
  97.5 1.4 %collective-permute-start.16 = (f16[1024,384]{1,0:T(8,128)(2,1)S(1)}, f16[1024,384]{1,0:T(8,128)(2,1)S(1)}, u32[]{:S(2)}, u32[]{:S(2)}) collective-permute-start(f16[1024,384]{1,0:T(8,128)(2,1)S(1)} %convert_element_type.21), channel_id=1, source_target_pairs={{0,8},{8,0},{16,24},{24,16},{1,9},{9,1},{17,25},{25,17},{2,10},{10... | collective-permute-start | bytes 2359304 | tf_op jit(solution)/shard_map/ppermute | solution.py:34
  98.9 19.2 %all_to_all.10.notes = f32[32,8,128]{2,1,0:T(8,128)S(1)} all-to-all(f32[32,8,128]{2,1,0:T(8,128)S(1)} %get-tuple-element.54), channel_id=1, replica_groups=mesh['island'=4,'expert'=4,'tensor'=2] {'island','expert','tensor'}, dimensions={0} | all-to-all | bytes 262144 | tf_op jit(solution)/shard_map/all_to_all | solution.py:402
  118.1 0.5 slice.13
  119.3 0.0 collective-permute-done.18
  119.3 0.1 slice_add_fusion
  119.4 1.6 %collective-permute-start.19 = (f16[512,384]{1,0:T(8,128)(2,1)S(1)}, f16[512,384]{1,0:T(8,128)(2,1)S(1)}, u32[]{:S(2)}, u32[]{:S(2)}) collective-permute-start(f16[512,384]{1,0:T(8,128)(2,1)S(1)} %slice_add_fusion), channel_id=1, source_target_pairs={{0,8},{8,0},{16,24},{24,16},{1,9},{9,1},{17,25},{25,17},{2,10},{10... | collective-permute-start | bytes 1179656 | tf_op jit(solution)/shard_map/ppermute | solution.py:34
  121.0 0.1 slice_add_fusion.1
  121.1 1.4 %collective-permute-start.17 = (f16[512,384]{1,0:T(8,128)(2,1)S(1)}, f16[512,384]{1,0:T(8,128)(2,1)S(1)}, u32[]{:S(2)}, u32[]{:S(2)}) collective-permute-start(f16[512,384]{1,0:T(8,128)(2,1)S(1)} %slice_add_fusion.1), channel_id=1, source_target_pairs={{0,16},{8,24},{16,0},{24,8},{1,17},{9,25},{17,1},{25,9},{2,18},{10... | collective-permute-start | bytes 1179656 | tf_op jit(solution)/shard_map/ppermute | solution.py:34
  122.5 1.3 convert_element_type.27.refs_2_
  123.7 0.1 convert_element_type.26.refs_1_
  123.8 5.7 %update_pieces.2 = (f32[1,2048,768]{2,1,0:T(8,128)}, bf16[1,2048,768]{2,1,0:T(8,128)(2,1)}) custom-call(f32[32,8,128]{2,1,0:T(8,128)S(1)} %all_to_all.10.notes, f32[1,2048,768]{2,1,0:T(8,128)} %momentum.3, f32[1024,384]{1,0:T(8,128)S(1)} %get-tuple-element.55.refs_0_, f32[1024,384]{1,0:T(8,128)S(1)} %convert_element_type.26.refs_1_, ...), custom_call_target="tpu_custom_call" | custom-call | bytes 18874368 | tf_op jit(solution)/shard_map/update_pieces/pallas_call | solution.py:417
  129.6 1.0 collective-permute-done.19
  130.5 0.1 convert_element_type.25.refs_1_
  130.6 1.2 collective-permute-done.17
  131.8 0.1 convert_element_type.24.refs_0_
  131.9 2.6 %update_pieces.3 = (f32[1,2048,768]{2,1,0:T(8,128)}, bf16[1,2048,768]{2,1,0:T(8,128)(2,1)}) custom-call(f32[32,8,128]{2,1,0:T(8,128)S(1)} %all_to_all.10.notes, f32[1,2048,768]{2,1,0:T(8,128)} %momentum.3, f32[512,384]{1,0:T(8,128)S(1)} %convert_element_type.24.refs_0_, ...), custom_call_target="tpu_custom_call", output_to_operand_aliasing={{0}: (4, {}), {1}: (5, {})} | custom-call | bytes 4718592 | tf_op jit(solution)/shard_map/update_pieces/pallas_call | solution.py:417
  (11 shorter events, 0.0 us)
Async XLA Ops:
  3.5 10.9 %copy-start.2 = (bf16[192,1024]{1,0:T(8,128)(2,1)S(1)}, bf16[192,1024]{1,0:T(8,128)(2,1)}, u32[]{:S(2)}) copy-start(bf16[192,1024]{1,0:T(8,128)(2,1)} %get-tuple-element.30.slots) | copy-start | bytes 1179652
  3.5 15.4 %collective-permute-start = (bf16[192,1024]{1,0:T(8,128)(2,1)}, bf16[192,1024]{1,0:T(8,128)(2,1)S(1)}, u32[]{:S(2)}, u32[]{:S(2)}) collective-permute-start(bf16[192,1024]{1,0:T(8,128)(2,1)} %get-tuple-element.33), channel_id=1, source_target_pairs={{0,6},{2,4},{4,2},{6,0},{1,7},{3,5},{5,3},{7,1},{8,14},{10,12},{12... | collective-permute-start | bytes 1179656 | tf_op jit(solution)/shard_map/ppermute | solution.py:34
  8.7 33.8 %collective-permute-start.1 = (bf16[192,1024]{1,0:T(8,128)(2,1)}, bf16[192,1024]{1,0:T(8,128)(2,1)S(1)}, u32[]{:S(2)}, u32[]{:S(2)}) collective-permute-start(bf16[192,1024]{1,0:T(8,128)(2,1)} %get-tuple-element.34), channel_id=1, source_target_pairs={{0,4},{2,6},{4,0},{6,2},{1,5},{3,7},{5,1},{7,3},{8,12},{10,14},{12... | collective-permute-start | bytes 1179656 | tf_op jit(solution)/shard_map/ppermute | solution.py:34
  8.7 33.8 %collective-permute-start.2 = (bf16[192,1024]{1,0:T(8,128)(2,1)}, bf16[192,1024]{1,0:T(8,128)(2,1)S(1)}, u32[]{:S(2)}, u32[]{:S(2)}) collective-permute-start(bf16[192,1024]{1,0:T(8,128)(2,1)} %get-tuple-element.35), channel_id=1, source_target_pairs={{0,2},{2,0},{4,6},{6,4},{1,3},{3,1},{5,7},{7,5},{8,10},{10,8},{12,... | collective-permute-start | bytes 1179656 | tf_op jit(solution)/shard_map/ppermute | solution.py:34
  11.2 33.7 %collective-permute-start.5 = (bf16[1536,384]{1,0:T(8,128)(2,1)S(1)}, bf16[1536,384]{1,0:T(8,128)(2,1)S(1)}, u32[]{:S(2)}, u32[]{:S(2)}) collective-permute-start(bf16[1536,384]{1,0:T(8,128)(2,1)S(1)} %get-tuple-element.39), channel_id=1, source_target_pairs={{0,8},{8,0},{16,24},{24,16},{1,9},{9,1},{17,25},{25,17},{2,10},{10... | collective-permute-start | bytes 3538952 | tf_op jit(solution)/shard_map/ppermute | solution.py:34
  12.9 32.0 %collective-permute-start.6 = (bf16[1536,384]{1,0:T(8,128)(2,1)S(1)}, bf16[1536,384]{1,0:T(8,128)(2,1)S(1)}, u32[]{:S(2)}, u32[]{:S(2)}) collective-permute-start(bf16[1536,384]{1,0:T(8,128)(2,1)S(1)} %get-tuple-element.40), channel_id=1, source_target_pairs={{0,16},{8,24},{16,0},{24,8},{1,17},{9,25},{17,1},{25,9},{2,18},{10... | collective-permute-start | bytes 3538952 | tf_op jit(solution)/shard_map/ppermute | solution.py:34
  42.4 6.7 %copy-start = (bf16[1,1,2048,768]{3,2,1,0:T(8,128)(2,1)S(1)}, bf16[1,1,2048,768]{3,2,1,0:T(8,128)(2,1)}, u32[]{:S(2)}) copy-start(bf16[1,1,2048,768]{3,2,1,0:T(8,128)(2,1)} %refs_0_.5) | copy-start | bytes 9437188
  42.4 6.7 %copy-start.1 = (bf16[1,1,768,2048]{3,2,1,0:T(8,128)(2,1)S(1)}, bf16[1,1,768,2048]{3,2,1,0:T(8,128)(2,1)}, u32[]{:S(2)}) copy-start(bf16[1,1,768,2048]{3,2,1,0:T(8,128)(2,1)} %refs_1_.3) | copy-start | bytes 9437188
  42.5 2.4 %collective-permute-start.3 = (bf16[384,1024]{1,0:T(8,128)(2,1)S(1)}, bf16[384,1024]{1,0:T(8,128)(2,1)S(1)}, u32[]{:S(2)}, u32[]{:S(2)}) collective-permute-start(bf16[384,1024]{1,0:T(8,128)(2,1)S(1)} %get-tuple-element.36.refs_0_.refs_2_), channel_id=1, source_target_pairs={{0,1},{1,0},{2,3},{3,2},{4,5},{5,4},{6,7},{7,6},{8,9},{9,8},{10,11... | collective-permute-start | bytes 2359304 | tf_op jit(solution)/shard_map/ppermute | solution.py:34
  42.6 6.5 %collective-permute-start.4 = (bf16[384,1024]{1,0:T(8,128)(2,1)S(1)}, bf16[384,1024]{1,0:T(8,128)(2,1)S(1)}, u32[]{:S(2)}, u32[]{:S(2)}) collective-permute-start(bf16[384,1024]{1,0:T(8,128)(2,1)S(1)} %get-tuple-element.37.refs_4_), channel_id=1, source_target_pairs={{0,1},{1,0},{2,3},{3,2},{4,5},{5,4},{6,7},{7,6},{8,9},{9,8},{10,11... | collective-permute-start | bytes 2359304 | tf_op jit(solution)/shard_map/ppermute | solution.py:34
  45.5 9.8 %copy-start.3 = (bf16[512,384]{1,0:T(8,128)(2,1)}, bf16[512,384]{1,0:T(8,128)(2,1)S(1)}, u32[]{:S(2)}) copy-start(bf16[512,384]{1,0:T(8,128)(2,1)S(1)} %get-tuple-element.44.refs_2_) | copy-start | bytes 1179652
  45.6 13.0 %collective-permute-start.9 = (bf16[512,384]{1,0:T(8,128)(2,1)S(1)}, bf16[512,384]{1,0:T(8,128)(2,1)S(1)}, u32[]{:S(2)}, u32[]{:S(2)}) collective-permute-start(bf16[512,384]{1,0:T(8,128)(2,1)S(1)} %get-tuple-element.45), channel_id=1, source_target_pairs={{0,24},{8,16},{16,8},{24,0},{1,25},{9,17},{17,9},{25,1},{2,26},{10... | collective-permute-start | bytes 1179656 | tf_op jit(solution)/shard_map/ppermute | solution.py:34
  48.1 18.1 %collective-permute-start.8 = (bf16[512,384]{1,0:T(8,128)(2,1)S(1)}, bf16[512,384]{1,0:T(8,128)(2,1)S(1)}, u32[]{:S(2)}, u32[]{:S(2)}) collective-permute-start(bf16[512,384]{1,0:T(8,128)(2,1)S(1)} %get-tuple-element.45), channel_id=1, source_target_pairs={{0,16},{8,24},{16,0},{24,8},{1,17},{9,25},{17,1},{25,9},{2,18},{10... | collective-permute-start | bytes 1179656 | tf_op jit(solution)/shard_map/ppermute | solution.py:34
  48.6 17.6 %collective-permute-start.10 = (bf16[512,384]{1,0:T(8,128)(2,1)S(1)}, bf16[512,384]{1,0:T(8,128)(2,1)S(1)}, u32[]{:S(2)}, u32[]{:S(2)}) collective-permute-start(bf16[512,384]{1,0:T(8,128)(2,1)S(1)} %get-tuple-element.44.refs_2_), channel_id=1, source_target_pairs={{0,1},{1,0},{2,3},{3,2},{4,5},{5,4},{6,7},{7,6},{8,9},{9,8},{10,11... | collective-permute-start | bytes 1179656 | tf_op jit(solution)/shard_map/ppermute | solution.py:34
  48.6 18.4 %collective-permute-start.7 = (bf16[512,384]{1,0:T(8,128)(2,1)S(1)}, bf16[512,384]{1,0:T(8,128)(2,1)S(1)}, u32[]{:S(2)}, u32[]{:S(2)}) collective-permute-start(bf16[512,384]{1,0:T(8,128)(2,1)S(1)} %get-tuple-element.44.refs_2_), channel_id=1, source_target_pairs={{0,8},{8,0},{16,24},{24,16},{1,9},{9,1},{17,25},{25,17},{2,10},{10... | collective-permute-start | bytes 1179656 | tf_op jit(solution)/shard_map/ppermute | solution.py:34
  55.3 0.7 copy-start.5
  56.0 32.6 %collective-permute-start.13 = (bf16[896,384]{1,0:T(8,128)(2,1)}, bf16[896,384]{1,0:T(8,128)(2,1)}, u32[]{:S(2)}, u32[]{:S(2)}) collective-permute-start(bf16[896,384]{1,0:T(8,128)(2,1)} %get-tuple-element.51), channel_id=1, source_target_pairs={{0,8},{8,0},{16,24},{24,16},{1,9},{9,1},{17,25},{25,17},{2,10},{10... | collective-permute-start | bytes 2064392 | tf_op jit(solution)/shard_map/ppermute | solution.py:34
  58.5 30.1 %collective-permute-start.14 = (bf16[896,384]{1,0:T(8,128)(2,1)}, bf16[896,384]{1,0:T(8,128)(2,1)}, u32[]{:S(2)}, u32[]{:S(2)}) collective-permute-start(bf16[896,384]{1,0:T(8,128)(2,1)} %get-tuple-element.52), channel_id=1, source_target_pairs={{0,16},{8,24},{16,0},{24,8},{1,17},{9,25},{17,1},{25,9},{2,18},{10... | collective-permute-start | bytes 2064392 | tf_op jit(solution)/shard_map/ppermute | solution.py:34
  68.2 20.5 %collective-permute-start.11 = (bf16[768,384]{1,0:T(8,128)(2,1)}, bf16[768,384]{1,0:T(8,128)(2,1)}, u32[]{:S(2)}, u32[]{:S(2)}) collective-permute-start(bf16[768,384]{1,0:T(8,128)(2,1)} %get-tuple-element.48), channel_id=1, source_target_pairs={{0,1},{1,0},{2,3},{3,2},{4,5},{5,4},{6,7},{7,6},{8,9},{9,8},{10,11... | collective-permute-start | bytes 1769480 | tf_op jit(solution)/shard_map/ppermute | solution.py:34
  68.2 20.5 %collective-permute-start.12 = (bf16[768,384]{1,0:T(8,128)(2,1)}, bf16[768,384]{1,0:T(8,128)(2,1)}, u32[]{:S(2)}, u32[]{:S(2)}) collective-permute-start(bf16[768,384]{1,0:T(8,128)(2,1)} %get-tuple-element.49), channel_id=1, source_target_pairs={{0,1},{1,0},{2,3},{3,2},{4,5},{5,4},{6,7},{7,6},{8,9},{9,8},{10,11... | collective-permute-start | bytes 1769480 | tf_op jit(solution)/shard_map/ppermute | solution.py:34
  68.7 19.9 %collective-permute-start.15 = (bf16[384,384]{1,0:T(8,128)(2,1)}, bf16[384,384]{1,0:T(8,128)(2,1)}, u32[]{:S(2)}, u32[]{:S(2)}) collective-permute-start(bf16[384,384]{1,0:T(8,128)(2,1)} %get-tuple-element.53), channel_id=1, source_target_pairs={{0,24},{8,16},{16,8},{24,0},{1,25},{9,17},{17,9},{25,1},{2,26},{10... | collective-permute-start | bytes 884744 | tf_op jit(solution)/shard_map/ppermute | solution.py:34
  70.3 18.3 %all-to-all-start = ((f32[32,8,128]{2,1,0:T(8,128)}), f32[32,8,128]{2,1,0:T(8,128)S(1)}, u32[]{:S(2)}, u32[]{:S(2)}) async-start(f32[32,8,128]{2,1,0:T(8,128)} %get-tuple-element.46), calls=%async_computation | async-start | bytes 262144 | tf_op jit(solution)/shard_map/all_to_all | solution.py:388
  88.6 1.0 copy-start.4
  89.6 1.0 copy-start.6
  95.9 23.4 %collective-permute-start.18 = (f16[1024,384]{1,0:T(8,128)(2,1)S(1)}, f16[1024,384]{1,0:T(8,128)(2,1)S(1)}, u32[]{:S(2)}, u32[]{:S(2)}) collective-permute-start(f16[1024,384]{1,0:T(8,128)(2,1)S(1)} %convert_element_type.21), channel_id=1, source_target_pairs={{0,16},{8,24},{16,0},{24,8},{1,17},{9,25},{17,1},{25,9},{2,18},{10... | collective-permute-start | bytes 2359304 | tf_op jit(solution)/shard_map/ppermute | solution.py:34
  97.5 23.5 %collective-permute-start.16 = (f16[1024,384]{1,0:T(8,128)(2,1)S(1)}, f16[1024,384]{1,0:T(8,128)(2,1)S(1)}, u32[]{:S(2)}, u32[]{:S(2)}) collective-permute-start(f16[1024,384]{1,0:T(8,128)(2,1)S(1)} %convert_element_type.21), channel_id=1, source_target_pairs={{0,8},{8,0},{16,24},{24,16},{1,9},{9,1},{17,25},{25,17},{2,10},{10... | collective-permute-start | bytes 2359304 | tf_op jit(solution)/shard_map/ppermute | solution.py:34
  119.4 11.1 %collective-permute-start.19 = (f16[512,384]{1,0:T(8,128)(2,1)S(1)}, f16[512,384]{1,0:T(8,128)(2,1)S(1)}, u32[]{:S(2)}, u32[]{:S(2)}) collective-permute-start(f16[512,384]{1,0:T(8,128)(2,1)S(1)} %slice_add_fusion), channel_id=1, source_target_pairs={{0,8},{8,0},{16,24},{24,16},{1,9},{9,1},{17,25},{25,17},{2,10},{10... | collective-permute-start | bytes 1179656 | tf_op jit(solution)/shard_map/ppermute | solution.py:34
  121.1 10.7 %collective-permute-start.17 = (f16[512,384]{1,0:T(8,128)(2,1)S(1)}, f16[512,384]{1,0:T(8,128)(2,1)S(1)}, u32[]{:S(2)}, u32[]{:S(2)}) collective-permute-start(f16[512,384]{1,0:T(8,128)(2,1)S(1)} %slice_add_fusion.1), channel_id=1, source_target_pairs={{0,16},{8,24},{16,0},{24,8},{1,17},{9,25},{17,1},{25,9},{2,18},{10... | collective-permute-start | bytes 1179656 | tf_op jit(solution)/shard_map/ppermute | solution.py:34

commit v18 on v17

--- a/solution.py
+++ b/solution.py
@@ -158,19 +158,19 @@
 def average_kernel(islands, entries, norms, drift_sum, *refs):
     spot = position()
     mine, other, messages = refs[:islands], refs[islands : islands + 3], refs[islands + 3 : 2 * islands + 3]
-    scaled, notes, total, square = refs[2 * islands + 3 :]
-    rows, slots = mine[0].shape
+    scaled, notes, total, square, share, hidden, sems = refs[2 * islands + 3 :]
+    loads = copy_all(sems, [(mine[0], share), (messages[0], hidden)])
+    rows, slots = share.shape
     group = norms.shape[0] // islands
+    split = other[1].shape[0]
 
     def moved(d):
         if d == 0:
-            return other[0][...]
-        split = other[1].shape[0]
+            return [(0, rows, other[0], 0)]
         first, last = (d - 1) * rows, d * rows
-        above = other[1][first : min(last, split), :] if first < split else None
-        below = other[2][max(first - split, 0) : last - split, :] if last > split else None
-        found = [v for v in (above, below) if v is not None]
-        return found[0] if len(found) == 1 else jnp.concatenate(found)
+        cut = min(max(split - first, 0), rows)
+        found = [(0, cut, other[1], first), (cut, rows, other[2], first + cut - split)]
+        return [part for part in found if part[0] < part[1]]
 
     scales = []
     for d in range(islands):
@@ -180,7 +180,6 @@
     handed = [m for m in messages[:0:-1] if m.shape[0] > slots]
 
     def compute(at):
-        squares = 0.0
         for m in range(2):
             part = slice(m * rows, (m + 1) * rows)
             average = drift_sum[part, :]
@@ -190,12 +189,26 @@
                 first += slots
                 average = average + handed[n][first : first + rows, :].astype(F32)
             average = average * (1.0 / islands)
-            for d in range(islands):
-                factor = messages[d][:slots, :]
-                average = average + scales[d] * dot(mine[d][...] if m == at else moved(d), factor, ((1,), (0,)))
+            pieces = []
+            for d in [*range(1, islands), 0]:
+                if d == 0 and m == 0:
+                    for copy in loads:
+                        copy.wait()
+                factor = messages[d][:slots, :] if d else hidden[...]
+                places = moved(d)
+                if m == at:
+                    places = [(0, rows, mine[d] if d else share, 0)]
+                if len(places) > 1:
+                    pieces += [(place, scales[d], factor) for place in places]
+                    continue
+                block = places[0][2][places[0][3] : places[0][3] + rows, :]
+                average = average + scales[d] * dot(block, factor, ((1,), (0,)))
             total[part, :] = average
-            squares = squares + jnp.sum(average * average, axis=0, keepdims=True)
-        square[...] = squares
+            for (low, high, ref, first), scale, factor in pieces:
+                block = ref[first : first + high - low, :]
+                here = slice(m * rows + low, m * rows + high)
+                total[here, :] += scale * dot(block, factor, ((1,), (0,)))
+        square[...] = jnp.sum(total[...] * total[...], axis=0, keepdims=True)
 
     for at in range(2):
         pl.when(spot[1] == at)(functools.partial(compute, at))
@@ -389,13 +402,19 @@
 
     scaled, notes = pl.pallas_call(
         lambda *refs: average_kernel(islands, entries, *refs),
-        in_specs=[VMEM] * (5 + 2 * islands),
+        in_specs=[VMEM] * 2 + [ANY] + [VMEM] * (islands + 2) + [ANY] + [VMEM] * (islands - 1),
         out_specs=[VMEM] * 2,
         out_shape=[
             jax.ShapeDtypeStruct((half, columns), F32),
             jax.ShapeDtypeStruct((devices, 8, 128), F32),
         ],
-        scratch_shapes=[pltpu.VMEM((half, columns), F32), pltpu.VMEM((1, columns), F32)],
+        scratch_shapes=[
+            pltpu.VMEM((half, columns), F32),
+            pltpu.VMEM((1, columns), F32),
+            pltpu.VMEM((half // parts, routed_rows), BF16),
+            pltpu.VMEM((routed_rows, columns), BF16),
+            pltpu.SemaphoreType.DMA((2,)),
+        ],
         compiler_params=params(8 + routed_rows // 48),
         name="average_block",
     )(norms, drift_sum, shares[0], *features_in, own_moved, *halves_moved, *messages_in)

time: 135 us -> 135 us (level)
  no operation moved by 1% of the time
where the time goes in v18:
time: 135 us
  waiting for transfers between devices  54.5 us (40%)
  starting transfers between devices  27.8 us (21%)
  Pallas kernels  26.9 us (20%)
  blocking collectives  19.1 us (14%)
  local copies, waits for them, and re-layouts  3.2 us (2%)
  other arithmetic  1.8 us (1%)
  between operations  1.62 us (1%)
    ppermute x20, waiting for transfers between devices, swap(): lax.ppermute(value, axis, [(at, partner(at, step, size)) for at in range(...  54.5 us
    ppermute x20, starting transfers between devices, swap(): lax.ppermute(value, axis, [(at, partner(at, step, size)) for at in range(...  24.3 us
    all_to_all x1, blocking collectives, body(): notes = lax.all_to_all(notes, AXES, split_axis=0, concat_axis=0, tiled=True)  19.1 us
    pallas_call x2, Pallas kernels, body(): pl.pallas_call(functools.partial(update_kernel, entries, list(values), cu...  8.31 us
    pallas_call x1, Pallas kernels, body(): pl.pallas_call(lambda *refs: hidden_kernel(parts, islands, tails, *refs),...  6.18 us
    pallas_call x1, Pallas kernels, body(): pl.pallas_call(lambda *refs: average_kernel(islands, entries, *refs), in_...  5.66 us
    all_to_all x1, starting transfers between devices, body(): norms = lax.all_to_all(norms, AXES, split_axis=0, concat_axis=0, tiled=True)  3.57 us
    pallas_call x1, Pallas kernels, body(): pl.pallas_call(lambda *refs: pick_kernel(experts, *refs), in_specs=[ANY]...  2.9 us
  transfers between devices with their start and end apart: 21, of which 9 were waited for; matrix products, arithmetic and copies ran while one was open for 2% of the time, Pallas kernels for 12%

profile of v18, /device:TPU:0, one launch (start us, length us, event | category | flops | bytes accessed | tf_op | source)
XLA Modules:
  0.0 135.0 jit_solution(16408755986183135414)
XLA Ops:
  0.6 2.9 %pick_slots.1 = (bf16[192,1024]{1,0:T(8,128)(2,1)}, bf16[192,1024]{1,0:T(8,128)(2,1)}, bf16[192,1024]{1,0:T(8,128)(2,1)}, bf16[192,1024]{1,0:T(8,128)(2,1)}) custom-call(s32[1,1,4,96]{3,2,1,0:T(4,128)} %refs_0_.3, s32[1,1,4]{2,1,0:T(1,128)} %refs_1_.2, f32[1,1,4,96]{3,2,1,0:T(4,128)} %refs_2_.1, bf16[1,256,1024]{2,1,0:T(8,128)(2,1)} %refs_3_.1, ...), custom_call_target="tpu_custom_call" | custom-call | tf_op jit(solution)/shard_map/pick_slots/pallas_call | solution.py:310
  3.5 0.0 copy-start.2
  3.5 5.1 %collective-permute-start = (bf16[192,1024]{1,0:T(8,128)(2,1)}, bf16[192,1024]{1,0:T(8,128)(2,1)S(1)}, u32[]{:S(2)}, u32[]{:S(2)}) collective-permute-start(bf16[192,1024]{1,0:T(8,128)(2,1)} %get-tuple-element.33), channel_id=1, source_target_pairs={{0,6},{2,4},{4,2},{6,0},{1,7},{3,5},{5,3},{7,1},{8,14},{10,12},{12... | collective-permute-start | bytes 1179656 | tf_op jit(solution)/shard_map/ppermute | solution.py:34
  8.7 0.0 collective-permute-start.1
  8.7 0.6 collective-permute-start.2
  9.3 1.9 %cut_drift.1 = (bf16[1024,384]{1,0:T(8,128)(2,1)S(1)}, bf16[1536,384]{1,0:T(8,128)(2,1)S(1)}, bf16[1536,384]{1,0:T(8,128)(2,1)S(1)}) custom-call(bf16[1,1,2048,768]{3,2,1,0:T(8,128)(2,1)} %refs_0_.4), custom_call_target="tpu_custom_call" | custom-call | tf_op jit(solution)/shard_map/cut_drift/pallas_call | solution.py:326
  11.2 1.7 %collective-permute-start.5 = (bf16[1536,384]{1,0:T(8,128)(2,1)S(1)}, bf16[1536,384]{1,0:T(8,128)(2,1)S(1)}, u32[]{:S(2)}, u32[]{:S(2)}) collective-permute-start(bf16[1536,384]{1,0:T(8,128)(2,1)S(1)} %get-tuple-element.39), channel_id=1, source_target_pairs={{0,8},{8,0},{16,24},{24,16},{1,9},{9,1},{17,25},{25,17},{2,10},{10... | collective-permute-start | bytes 3538952 | tf_op jit(solution)/shard_map/ppermute | solution.py:34
  12.9 1.5 %collective-permute-start.6 = (bf16[1536,384]{1,0:T(8,128)(2,1)S(1)}, bf16[1536,384]{1,0:T(8,128)(2,1)S(1)}, u32[]{:S(2)}, u32[]{:S(2)}) collective-permute-start(bf16[1536,384]{1,0:T(8,128)(2,1)S(1)} %get-tuple-element.40), channel_id=1, source_target_pairs={{0,16},{8,24},{16,0},{24,8},{1,17},{9,25},{17,1},{25,9},{2,18},{10... | collective-permute-start | bytes 3538952 | tf_op jit(solution)/shard_map/ppermute | solution.py:34
  14.4 0.1 own_parts.1
  14.5 4.5 %collective-permute-done.refs_1_ = bf16[192,1024]{1,0:T(8,128)(2,1)S(1)} collective-permute-done((bf16[192,1024]{1,0:T(8,128)(2,1)}, bf16[192,1024]{1,0:T(8,128)(2,1)S(1)}, u32[]{:S(2)}, u32[]{:S(2)}) %collective-permute-start) | collective-permute-done | bytes 393248 | tf_op jit(solution)/shard_map/ppermute | solution.py:34
  19.0 23.5 %collective-permute-done.1.refs_2_ = bf16[192,1024]{1,0:T(8,128)(2,1)S(1)} collective-permute-done((bf16[192,1024]{1,0:T(8,128)(2,1)}, bf16[192,1024]{1,0:T(8,128)(2,1)S(1)}, u32[]{:S(2)}, u32[]{:S(2)}) %collective-permute-start.1) | collective-permute-done | bytes 393248 | tf_op jit(solution)/shard_map/ppermute | solution.py:34
  42.4 0.0 collective-permute-done.2.refs_3_
  42.4 0.1 gather_slots.1
  42.5 0.1 collective-permute-start.3
  42.6 0.5 collective-permute-start.4
  43.1 1.8 %collective-permute-done.3.refs_1_.refs_3_ = bf16[384,1024]{1,0:T(8,128)(2,1)S(1)} collective-permute-done((bf16[384,1024]{1,0:T(8,128)(2,1)S(1)}, bf16[384,1024]{1,0:T(8,128)(2,1)S(1)}, u32[]{:S(2)}, u32[]{:S(2)}) %collective-permute-start.3) | collective-permute-done | bytes 786464 | tf_op jit(solution)/shard_map/ppermute | solution.py:34
  44.9 0.0 collective-permute-done.5.refs_3_
  44.9 0.0 collective-permute-done.6.refs_4_
  44.9 0.6 join_blocks.1
  45.6 2.5 %collective-permute-start.9 = (bf16[512,384]{1,0:T(8,128)(2,1)S(1)}, bf16[512,384]{1,0:T(8,128)(2,1)S(1)}, u32[]{:S(2)}, u32[]{:S(2)}) collective-permute-start(bf16[512,384]{1,0:T(8,128)(2,1)S(1)} %get-tuple-element.45), channel_id=1, source_target_pairs={{0,24},{8,16},{16,8},{24,0},{1,25},{9,17},{17,9},{25,1},{2,26},{10... | collective-permute-start | bytes 1179656 | tf_op jit(solution)/shard_map/ppermute | solution.py:34
  48.1 0.5 collective-permute-start.8
  48.6 0.0 collective-permute-start.10
  48.6 0.5 collective-permute-start.7
  49.1 0.0 collective-permute-done.4.refs_5_
  49.1 6.2 %hidden_grads.1 = (bf16[384,384]{1,0:T(8,128)(2,1)S(1)}, bf16[896,384]{1,0:T(8,128)(2,1)}, bf16[896,384]{1,0:T(8,128)(2,1)}, bf16[384,384]{1,0:T(8,128)(2,1)}, f32[32,8,128]{2,1,0:T(8,128)S(1)}) custom-call(bf16[1,1,2048,768]{3,2,1,0:T(8,128)(2,1)S(1)} %copy-done, bf16[1,1,768,2048]{3,2,1,0:T(8,128)(2,1)S(1)} %copy-done.1, ...), custom_call_target="tpu_custom_call" | custom-call | tf_op jit(solution)/shard_map/hidden_grads/pallas_call | solution.py:378
  55.3 0.7 copy-done.5
  56.0 1.5 %collective-permute-start.13 = (bf16[896,384]{1,0:T(8,128)(2,1)}, bf16[896,384]{1,0:T(8,128)(2,1)}, u32[]{:S(2)}, u32[]{:S(2)}) collective-permute-start(bf16[896,384]{1,0:T(8,128)(2,1)} %get-tuple-element.51), channel_id=1, source_target_pairs={{0,8},{8,0},{16,24},{24,16},{1,9},{9,1},{17,25},{25,17},{2,10},{10... | collective-permute-start | bytes 2064392 | tf_op jit(solution)/shard_map/ppermute | solution.py:34
  57.5 1.0 collective-permute-done.9.refs_3_.refs_5_
  58.5 1.5 %collective-permute-start.14 = (bf16[896,384]{1,0:T(8,128)(2,1)}, bf16[896,384]{1,0:T(8,128)(2,1)}, u32[]{:S(2)}, u32[]{:S(2)}) collective-permute-start(bf16[896,384]{1,0:T(8,128)(2,1)} %get-tuple-element.52), channel_id=1, source_target_pairs={{0,16},{8,24},{16,0},{24,8},{1,17},{9,25},{17,1},{25,9},{2,18},{10... | collective-permute-start | bytes 2064392 | tf_op jit(solution)/shard_map/ppermute | solution.py:34
  60.0 6.2 %collective-permute-done.8.refs_2_.refs_4_ = bf16[512,384]{1,0:T(8,128)(2,1)S(1)} collective-permute-done((bf16[512,384]{1,0:T(8,128)(2,1)S(1)}, bf16[512,384]{1,0:T(8,128)(2,1)S(1)}, u32[]{:S(2)}, u32[]{:S(2)}) %collective-permute-start.8) | collective-permute-done | bytes 393248 | tf_op jit(solution)/shard_map/ppermute | solution.py:34
  66.2 0.0 collective-permute-done.10.refs_4_.refs_6_
  66.2 0.8 collective-permute-done.7.refs_1_.refs_3_
  67.0 1.2 hand_on.1
  68.2 0.0 collective-permute-start.11
  68.2 0.5 collective-permute-start.12
  68.7 1.7 %collective-permute-start.15 = (bf16[384,384]{1,0:T(8,128)(2,1)}, bf16[384,384]{1,0:T(8,128)(2,1)}, u32[]{:S(2)}, u32[]{:S(2)}) collective-permute-start(bf16[384,384]{1,0:T(8,128)(2,1)} %get-tuple-element.53), channel_id=1, source_target_pairs={{0,24},{8,16},{16,8},{24,0},{1,25},{9,17},{17,9},{25,1},{2,26},{10... | collective-permute-start | bytes 884744 | tf_op jit(solution)/shard_map/ppermute | solution.py:34
  70.3 3.6 %all-to-all-start = ((f32[32,8,128]{2,1,0:T(8,128)}), f32[32,8,128]{2,1,0:T(8,128)S(1)}, u32[]{:S(2)}, u32[]{:S(2)}) async-start(f32[32,8,128]{2,1,0:T(8,128)} %get-tuple-element.46), calls=%async_computation | async-start | bytes 262144 | tf_op jit(solution)/shard_map/all_to_all | solution.py:401
  73.9 14.7 %collective-permute-done.15.refs_12_ = bf16[384,384]{1,0:T(8,128)(2,1)} collective-permute-done((bf16[384,384]{1,0:T(8,128)(2,1)}, bf16[384,384]{1,0:T(8,128)(2,1)}, u32[]{:S(2)}, u32[]{:S(2)}) %collective-permute-start.15) | collective-permute-done | bytes 294944 | tf_op jit(solution)/shard_map/ppermute | solution.py:34
  88.6 0.0 all-to-all-done.refs_0_
  88.6 0.0 collective-permute-done.13.refs_10_
  88.6 0.0 collective-permute-done.14.refs_11_
  88.6 0.0 collective-permute-done.11.refs_7_
  88.6 0.0 collective-permute-done.12.refs_8_
  88.6 1.0 copy-done.4
  89.6 1.0 copy-done.6
  90.6 5.7 %average_block.1 = (f32[1024,384]{1,0:T(8,128)S(1)}, f32[32,8,128]{2,1,0:T(8,128)S(1)}) custom-call(f32[32,8,128]{2,1,0:T(8,128)S(1)} %all-to-all-done.refs_0_, f32[1024,384]{1,0:T(8,128)S(1)} %get-tuple-element.47.refs_1_, bf16[512,384]{1,0:T(8,128)(2,1)S(1)} %copy-done.4, bf16[512,384]{1,0:T(8,128)(2,1)S(1)} %collective-permute-done.7.refs_1_.refs_3_, ...), custom_call_target="tpu_custom_call" | custom-call | tf_op jit(solution)/shard_map/average_block/pallas_call | solution.py:403
  96.3 0.1 convert_element_type.21
  96.4 1.6 %collective-permute-start.18 = (f16[1024,384]{1,0:T(8,128)(2,1)S(1)}, f16[1024,384]{1,0:T(8,128)(2,1)S(1)}, u32[]{:S(2)}, u32[]{:S(2)}) collective-permute-start(f16[1024,384]{1,0:T(8,128)(2,1)S(1)} %convert_element_type.21), channel_id=1, source_target_pairs={{0,16},{8,24},{16,0},{24,8},{1,17},{9,25},{17,1},{25,9},{2,18},{10... | collective-permute-start | bytes 2359304 | tf_op jit(solution)/shard_map/ppermute | solution.py:34
  98.0 1.4 %collective-permute-start.16 = (f16[1024,384]{1,0:T(8,128)(2,1)S(1)}, f16[1024,384]{1,0:T(8,128)(2,1)S(1)}, u32[]{:S(2)}, u32[]{:S(2)}) collective-permute-start(f16[1024,384]{1,0:T(8,128)(2,1)S(1)} %convert_element_type.21), channel_id=1, source_target_pairs={{0,8},{8,0},{16,24},{24,16},{1,9},{9,1},{17,25},{25,17},{2,10},{10... | collective-permute-start | bytes 2359304 | tf_op jit(solution)/shard_map/ppermute | solution.py:34
  99.4 19.1 %all_to_all.10.notes = f32[32,8,128]{2,1,0:T(8,128)S(1)} all-to-all(f32[32,8,128]{2,1,0:T(8,128)S(1)} %get-tuple-element.54), channel_id=1, replica_groups=mesh['island'=4,'expert'=4,'tensor'=2] {'island','expert','tensor'}, dimensions={0} | all-to-all | bytes 262144 | tf_op jit(solution)/shard_map/all_to_all | solution.py:421
  118.5 0.5 slice.13
  119.7 0.1 slice_add_fusion
  119.8 1.6 %collective-permute-start.19 = (f16[512,384]{1,0:T(8,128)(2,1)S(1)}, f16[512,384]{1,0:T(8,128)(2,1)S(1)}, u32[]{:S(2)}, u32[]{:S(2)}) collective-permute-start(f16[512,384]{1,0:T(8,128)(2,1)S(1)} %slice_add_fusion), channel_id=1, source_target_pairs={{0,8},{8,0},{16,24},{24,16},{1,9},{9,1},{17,25},{25,17},{2,10},{10... | collective-permute-start | bytes 1179656 | tf_op jit(solution)/shard_map/ppermute | solution.py:34
  121.4 0.0 collective-permute-done.16
  121.4 0.1 slice_add_fusion.1
  121.5 1.4 %collective-permute-start.17 = (f16[512,384]{1,0:T(8,128)(2,1)S(1)}, f16[512,384]{1,0:T(8,128)(2,1)S(1)}, u32[]{:S(2)}, u32[]{:S(2)}) collective-permute-start(f16[512,384]{1,0:T(8,128)(2,1)S(1)} %slice_add_fusion.1), channel_id=1, source_target_pairs={{0,16},{8,24},{16,0},{24,8},{1,17},{9,25},{17,1},{25,9},{2,18},{10... | collective-permute-start | bytes 1179656 | tf_op jit(solution)/shard_map/ppermute | solution.py:34
  122.9 1.3 convert_element_type.27.refs_2_
  124.2 0.1 convert_element_type.26.refs_1_
  124.3 5.7 %update_pieces.2 = (f32[1,2048,768]{2,1,0:T(8,128)}, bf16[1,2048,768]{2,1,0:T(8,128)(2,1)}) custom-call(f32[32,8,128]{2,1,0:T(8,128)S(1)} %all_to_all.10.notes, f32[1,2048,768]{2,1,0:T(8,128)} %momentum.3, f32[1024,384]{1,0:T(8,128)S(1)} %get-tuple-element.55.refs_0_, f32[1024,384]{1,0:T(8,128)S(1)} %convert_element_type.26.refs_1_, ...), custom_call_target="tpu_custom_call" | custom-call | bytes 18874368 | tf_op jit(solution)/shard_map/update_pieces/pallas_call | solution.py:436
  130.0 1.0 collective-permute-done.19
  131.0 0.1 convert_element_type.25.refs_1_
  131.0 1.2 collective-permute-done.17
  132.2 0.1 convert_element_type.24.refs_0_
  132.3 2.6 %update_pieces.3 = (f32[1,2048,768]{2,1,0:T(8,128)}, bf16[1,2048,768]{2,1,0:T(8,128)(2,1)}) custom-call(f32[32,8,128]{2,1,0:T(8,128)S(1)} %all_to_all.10.notes, f32[1,2048,768]{2,1,0:T(8,128)} %momentum.3, f32[512,384]{1,0:T(8,128)S(1)} %convert_element_type.24.refs_0_, ...), custom_call_target="tpu_custom_call", output_to_operand_aliasing={{0}: (4, {}), {1}: (5, {})} | custom-call | bytes 4718592 | tf_op jit(solution)/shard_map/update_pieces/pallas_call | solution.py:436
  (11 shorter events, 0.0 us)
Async XLA Ops:
  3.5 10.9 %copy-start.2 = (bf16[192,1024]{1,0:T(8,128)(2,1)S(1)}, bf16[192,1024]{1,0:T(8,128)(2,1)}, u32[]{:S(2)}) copy-start(bf16[192,1024]{1,0:T(8,128)(2,1)} %get-tuple-element.30.slots) | copy-start | bytes 1179652
  3.5 15.4 %collective-permute-start = (bf16[192,1024]{1,0:T(8,128)(2,1)}, bf16[192,1024]{1,0:T(8,128)(2,1)S(1)}, u32[]{:S(2)}, u32[]{:S(2)}) collective-permute-start(bf16[192,1024]{1,0:T(8,128)(2,1)} %get-tuple-element.33), channel_id=1, source_target_pairs={{0,6},{2,4},{4,2},{6,0},{1,7},{3,5},{5,3},{7,1},{8,14},{10,12},{12... | collective-permute-start | bytes 1179656 | tf_op jit(solution)/shard_map/ppermute | solution.py:34
  8.7 33.8 %collective-permute-start.1 = (bf16[192,1024]{1,0:T(8,128)(2,1)}, bf16[192,1024]{1,0:T(8,128)(2,1)S(1)}, u32[]{:S(2)}, u32[]{:S(2)}) collective-permute-start(bf16[192,1024]{1,0:T(8,128)(2,1)} %get-tuple-element.34), channel_id=1, source_target_pairs={{0,4},{2,6},{4,0},{6,2},{1,5},{3,7},{5,1},{7,3},{8,12},{10,14},{12... | collective-permute-start | bytes 1179656 | tf_op jit(solution)/shard_map/ppermute | solution.py:34
  8.7 33.8 %collective-permute-start.2 = (bf16[192,1024]{1,0:T(8,128)(2,1)}, bf16[192,1024]{1,0:T(8,128)(2,1)S(1)}, u32[]{:S(2)}, u32[]{:S(2)}) collective-permute-start(bf16[192,1024]{1,0:T(8,128)(2,1)} %get-tuple-element.35), channel_id=1, source_target_pairs={{0,2},{2,0},{4,6},{6,4},{1,3},{3,1},{5,7},{7,5},{8,10},{10,8},{12,... | collective-permute-start | bytes 1179656 | tf_op jit(solution)/shard_map/ppermute | solution.py:34
  11.2 33.7 %collective-permute-start.5 = (bf16[1536,384]{1,0:T(8,128)(2,1)S(1)}, bf16[1536,384]{1,0:T(8,128)(2,1)S(1)}, u32[]{:S(2)}, u32[]{:S(2)}) collective-permute-start(bf16[1536,384]{1,0:T(8,128)(2,1)S(1)} %get-tuple-element.39), channel_id=1, source_target_pairs={{0,8},{8,0},{16,24},{24,16},{1,9},{9,1},{17,25},{25,17},{2,10},{10... | collective-permute-start | bytes 3538952 | tf_op jit(solution)/shard_map/ppermute | solution.py:34
  12.9 32.0 %collective-permute-start.6 = (bf16[1536,384]{1,0:T(8,128)(2,1)S(1)}, bf16[1536,384]{1,0:T(8,128)(2,1)S(1)}, u32[]{:S(2)}, u32[]{:S(2)}) collective-permute-start(bf16[1536,384]{1,0:T(8,128)(2,1)S(1)} %get-tuple-element.40), channel_id=1, source_target_pairs={{0,16},{8,24},{16,0},{24,8},{1,17},{9,25},{17,1},{25,9},{2,18},{10... | collective-permute-start | bytes 3538952 | tf_op jit(solution)/shard_map/ppermute | solution.py:34
  42.4 6.7 %copy-start = (bf16[1,1,2048,768]{3,2,1,0:T(8,128)(2,1)S(1)}, bf16[1,1,2048,768]{3,2,1,0:T(8,128)(2,1)}, u32[]{:S(2)}) copy-start(bf16[1,1,2048,768]{3,2,1,0:T(8,128)(2,1)} %refs_0_.5) | copy-start | bytes 9437188
  42.4 6.7 %copy-start.1 = (bf16[1,1,768,2048]{3,2,1,0:T(8,128)(2,1)S(1)}, bf16[1,1,768,2048]{3,2,1,0:T(8,128)(2,1)}, u32[]{:S(2)}) copy-start(bf16[1,1,768,2048]{3,2,1,0:T(8,128)(2,1)} %refs_1_.3) | copy-start | bytes 9437188
  42.5 2.4 %collective-permute-start.3 = (bf16[384,1024]{1,0:T(8,128)(2,1)S(1)}, bf16[384,1024]{1,0:T(8,128)(2,1)S(1)}, u32[]{:S(2)}, u32[]{:S(2)}) collective-permute-start(bf16[384,1024]{1,0:T(8,128)(2,1)S(1)} %get-tuple-element.36.refs_0_.refs_2_), channel_id=1, source_target_pairs={{0,1},{1,0},{2,3},{3,2},{4,5},{5,4},{6,7},{7,6},{8,9},{9,8},{10,11... | collective-permute-start | bytes 2359304 | tf_op jit(solution)/shard_map/ppermute | solution.py:34
  42.6 6.5 %collective-permute-start.4 = (bf16[384,1024]{1,0:T(8,128)(2,1)S(1)}, bf16[384,1024]{1,0:T(8,128)(2,1)S(1)}, u32[]{:S(2)}, u32[]{:S(2)}) collective-permute-start(bf16[384,1024]{1,0:T(8,128)(2,1)S(1)} %get-tuple-element.37.refs_4_), channel_id=1, source_target_pairs={{0,1},{1,0},{2,3},{3,2},{4,5},{5,4},{6,7},{7,6},{8,9},{9,8},{10,11... | collective-permute-start | bytes 2359304 | tf_op jit(solution)/shard_map/ppermute | solution.py:34
  45.5 9.8 %copy-start.3 = (bf16[512,384]{1,0:T(8,128)(2,1)}, bf16[512,384]{1,0:T(8,128)(2,1)S(1)}, u32[]{:S(2)}) copy-start(bf16[512,384]{1,0:T(8,128)(2,1)S(1)} %get-tuple-element.44.refs_2_) | copy-start | bytes 1179652
  45.6 13.0 %collective-permute-start.9 = (bf16[512,384]{1,0:T(8,128)(2,1)S(1)}, bf16[512,384]{1,0:T(8,128)(2,1)S(1)}, u32[]{:S(2)}, u32[]{:S(2)}) collective-permute-start(bf16[512,384]{1,0:T(8,128)(2,1)S(1)} %get-tuple-element.45), channel_id=1, source_target_pairs={{0,24},{8,16},{16,8},{24,0},{1,25},{9,17},{17,9},{25,1},{2,26},{10... | collective-permute-start | bytes 1179656 | tf_op jit(solution)/shard_map/ppermute | solution.py:34
  48.1 18.1 %collective-permute-start.8 = (bf16[512,384]{1,0:T(8,128)(2,1)S(1)}, bf16[512,384]{1,0:T(8,128)(2,1)S(1)}, u32[]{:S(2)}, u32[]{:S(2)}) collective-permute-start(bf16[512,384]{1,0:T(8,128)(2,1)S(1)} %get-tuple-element.45), channel_id=1, source_target_pairs={{0,16},{8,24},{16,0},{24,8},{1,17},{9,25},{17,1},{25,9},{2,18},{10... | collective-permute-start | bytes 1179656 | tf_op jit(solution)/shard_map/ppermute | solution.py:34
  48.6 17.6 %collective-permute-start.10 = (bf16[512,384]{1,0:T(8,128)(2,1)S(1)}, bf16[512,384]{1,0:T(8,128)(2,1)S(1)}, u32[]{:S(2)}, u32[]{:S(2)}) collective-permute-start(bf16[512,384]{1,0:T(8,128)(2,1)S(1)} %get-tuple-element.44.refs_2_), channel_id=1, source_target_pairs={{0,1},{1,0},{2,3},{3,2},{4,5},{5,4},{6,7},{7,6},{8,9},{9,8},{10,11... | collective-permute-start | bytes 1179656 | tf_op jit(solution)/shard_map/ppermute | solution.py:34
  48.6 18.4 %collective-permute-start.7 = (bf16[512,384]{1,0:T(8,128)(2,1)S(1)}, bf16[512,384]{1,0:T(8,128)(2,1)S(1)}, u32[]{:S(2)}, u32[]{:S(2)}) collective-permute-start(bf16[512,384]{1,0:T(8,128)(2,1)S(1)} %get-tuple-element.44.refs_2_), channel_id=1, source_target_pairs={{0,8},{8,0},{16,24},{24,16},{1,9},{9,1},{17,25},{25,17},{2,10},{10... | collective-permute-start | bytes 1179656 | tf_op jit(solution)/shard_map/ppermute | solution.py:34
  55.3 0.7 copy-start.5
  56.0 32.6 %collective-permute-start.13 = (bf16[896,384]{1,0:T(8,128)(2,1)}, bf16[896,384]{1,0:T(8,128)(2,1)}, u32[]{:S(2)}, u32[]{:S(2)}) collective-permute-start(bf16[896,384]{1,0:T(8,128)(2,1)} %get-tuple-element.51), channel_id=1, source_target_pairs={{0,8},{8,0},{16,24},{24,16},{1,9},{9,1},{17,25},{25,17},{2,10},{10... | collective-permute-start | bytes 2064392 | tf_op jit(solution)/shard_map/ppermute | solution.py:34
  58.5 30.1 %collective-permute-start.14 = (bf16[896,384]{1,0:T(8,128)(2,1)}, bf16[896,384]{1,0:T(8,128)(2,1)}, u32[]{:S(2)}, u32[]{:S(2)}) collective-permute-start(bf16[896,384]{1,0:T(8,128)(2,1)} %get-tuple-element.52), channel_id=1, source_target_pairs={{0,16},{8,24},{16,0},{24,8},{1,17},{9,25},{17,1},{25,9},{2,18},{10... | collective-permute-start | bytes 2064392 | tf_op jit(solution)/shard_map/ppermute | solution.py:34
  68.2 20.5 %collective-permute-start.11 = (bf16[768,384]{1,0:T(8,128)(2,1)}, bf16[768,384]{1,0:T(8,128)(2,1)}, u32[]{:S(2)}, u32[]{:S(2)}) collective-permute-start(bf16[768,384]{1,0:T(8,128)(2,1)} %get-tuple-element.48), channel_id=1, source_target_pairs={{0,1},{1,0},{2,3},{3,2},{4,5},{5,4},{6,7},{7,6},{8,9},{9,8},{10,11... | collective-permute-start | bytes 1769480 | tf_op jit(solution)/shard_map/ppermute | solution.py:34
  68.2 20.5 %collective-permute-start.12 = (bf16[768,384]{1,0:T(8,128)(2,1)}, bf16[768,384]{1,0:T(8,128)(2,1)}, u32[]{:S(2)}, u32[]{:S(2)}) collective-permute-start(bf16[768,384]{1,0:T(8,128)(2,1)} %get-tuple-element.49), channel_id=1, source_target_pairs={{0,1},{1,0},{2,3},{3,2},{4,5},{5,4},{6,7},{7,6},{8,9},{9,8},{10,11... | collective-permute-start | bytes 1769480 | tf_op jit(solution)/shard_map/ppermute | solution.py:34
  68.7 19.9 %collective-permute-start.15 = (bf16[384,384]{1,0:T(8,128)(2,1)}, bf16[384,384]{1,0:T(8,128)(2,1)}, u32[]{:S(2)}, u32[]{:S(2)}) collective-permute-start(bf16[384,384]{1,0:T(8,128)(2,1)} %get-tuple-element.53), channel_id=1, source_target_pairs={{0,24},{8,16},{16,8},{24,0},{1,25},{9,17},{17,9},{25,1},{2,26},{10... | collective-permute-start | bytes 884744 | tf_op jit(solution)/shard_map/ppermute | solution.py:34
  70.3 18.3 %all-to-all-start = ((f32[32,8,128]{2,1,0:T(8,128)}), f32[32,8,128]{2,1,0:T(8,128)S(1)}, u32[]{:S(2)}, u32[]{:S(2)}) async-start(f32[32,8,128]{2,1,0:T(8,128)} %get-tuple-element.46), calls=%async_computation | async-start | bytes 262144 | tf_op jit(solution)/shard_map/all_to_all | solution.py:401
  88.6 1.0 copy-start.4
  89.6 1.0 copy-start.6
  96.4 23.3 %collective-permute-start.18 = (f16[1024,384]{1,0:T(8,128)(2,1)S(1)}, f16[1024,384]{1,0:T(8,128)(2,1)S(1)}, u32[]{:S(2)}, u32[]{:S(2)}) collective-permute-start(f16[1024,384]{1,0:T(8,128)(2,1)S(1)} %convert_element_type.21), channel_id=1, source_target_pairs={{0,16},{8,24},{16,0},{24,8},{1,17},{9,25},{17,1},{25,9},{2,18},{10... | collective-permute-start | bytes 2359304 | tf_op jit(solution)/shard_map/ppermute | solution.py:34
  98.0 23.4 %collective-permute-start.16 = (f16[1024,384]{1,0:T(8,128)(2,1)S(1)}, f16[1024,384]{1,0:T(8,128)(2,1)S(1)}, u32[]{:S(2)}, u32[]{:S(2)}) collective-permute-start(f16[1024,384]{1,0:T(8,128)(2,1)S(1)} %convert_element_type.21), channel_id=1, source_target_pairs={{0,8},{8,0},{16,24},{24,16},{1,9},{9,1},{17,25},{25,17},{2,10},{10... | collective-permute-start | bytes 2359304 | tf_op jit(solution)/shard_map/ppermute | solution.py:34
  119.8 11.1 %collective-permute-start.19 = (f16[512,384]{1,0:T(8,128)(2,1)S(1)}, f16[512,384]{1,0:T(8,128)(2,1)S(1)}, u32[]{:S(2)}, u32[]{:S(2)}) collective-permute-start(f16[512,384]{1,0:T(8,128)(2,1)S(1)} %slice_add_fusion), channel_id=1, source_target_pairs={{0,8},{8,0},{16,24},{24,16},{1,9},{9,1},{17,25},{25,17},{2,10},{10... | collective-permute-start | bytes 1179656 | tf_op jit(solution)/shard_map/ppermute | solution.py:34
  121.5 10.7 %collective-permute-start.17 = (f16[512,384]{1,0:T(8,128)(2,1)S(1)}, f16[512,384]{1,0:T(8,128)(2,1)S(1)}, u32[]{:S(2)}, u32[]{:S(2)}) collective-permute-start(f16[512,384]{1,0:T(8,128)(2,1)S(1)} %slice_add_fusion.1), channel_id=1, source_target_pairs={{0,16},{8,24},{16,0},{24,8},{1,17},{9,25},{17,1},{25,9},{2,18},{10... | collective-permute-start | bytes 1179656 | tf_op jit(solution)/shard_map/ppermute | solution.py:34

commit v19 on v17

--- a/solution.py
+++ b/solution.py
@@ -210,8 +210,7 @@
 
 
 def hand_kernel(count, norms, *refs):
-    shares, (_, top, bottom, passed) = refs[:count], refs[count:]
-    passed[...] = norms[...]
+    shares, (_, top, bottom) = refs[:count], refs[count:]
     size = shares[0].shape[0]
     split = top.shape[0]
     for n, share in enumerate(shares):
@@ -375,17 +374,16 @@
     messages_in = [messages[0]] + [swap(messages[d], "island", d) for d in range(1, islands)]
 
     middle = (islands - 1) * (half // parts) // 2
-    *halves, norms = pl.pallas_call(
+    norms = lax.all_to_all(norms, AXES, split_axis=0, concat_axis=0, tiled=True)
+    halves = pl.pallas_call(
         lambda *refs: hand_kernel(islands - 1, *refs),
-        in_specs=[VMEM] * islands + [ANY],
-        out_specs=[VMEM] * 3,
-        out_shape=[jax.ShapeDtypeStruct((middle, routed_rows), BF16)] * 2
-        + [jax.ShapeDtypeStruct(norms.shape, F32)],
+        in_specs=[ANY] + [VMEM] * (islands - 1) + [ANY],
+        out_specs=[VMEM] * 2,
+        out_shape=[jax.ShapeDtypeStruct((middle, routed_rows), BF16)] * 2,
         compiler_params=params(4 + routed_rows // 48),
         name="hand_on",
     )(norms, *features_in, own_moved)
     halves_moved = [swap(v, "tensor", 1) for v in halves]
-    norms = lax.all_to_all(norms, AXES, split_axis=0, concat_axis=0, tiled=True)
 
     scaled, notes = pl.pallas_call(
         lambda *refs: average_kernel(islands, entries, *refs),

time: 135 us -> 134 us (level)
  local copies, waits for them, and re-layouts: 3.2 us -> 4.64 us
    ppermute x20, waiting for transfers between devices: 54.5 us -> 48.9 us  [swap(): lax.ppermute(value, axis, [(at, partner(at, step, size)) for at in range(...]
    all_to_all x1, waiting for transfers between devices: 0.03 us -> 4.88 us  [body(): norms = lax.all_to_all(norms, AXES, split_axis=0, concat_axis=0, tiled=True)]
    ppermute x20, starting transfers between devices: 24.3 us -> 22.6 us  [swap(): lax.ppermute(value, axis, [(at, partner(at, step, size)) for at in range(...]
    unnamed x14 -> x16, local copies, waits for them, and re-layouts: 2.68 us -> 4.12 us
  transfers between devices with their start and end apart: 21 -> 21, of which waited for: 9 -> 7; matrix products, arithmetic and copies ran while one was open for 2% -> 2% of each run, Pallas kernels for 12% -> 11%
where the time goes in v19:
time: 134 us
  waiting for transfers between devices  53.8 us (40%)
  starting transfers between devices  27.3 us (20%)
  Pallas kernels  25.5 us (19%)
  blocking collectives  19.2 us (14%)
  local copies, waits for them, and re-layouts  4.64 us (3%)
  other arithmetic  1.82 us (1%)
  between operations  1.61 us (1%)
    ppermute x20, waiting for transfers between devices, swap(): lax.ppermute(value, axis, [(at, partner(at, step, size)) for at in range(...  48.9 us
    ppermute x20, starting transfers between devices, swap(): lax.ppermute(value, axis, [(at, partner(at, step, size)) for at in range(...  22.6 us
    all_to_all x1, blocking collectives, body(): notes = lax.all_to_all(notes, AXES, split_axis=0, concat_axis=0, tiled=True)  19.2 us
    pallas_call x2, Pallas kernels, body(): pl.pallas_call(functools.partial(update_kernel, entries, list(values), cu...  8.31 us
    pallas_call x1, Pallas kernels, body(): pl.pallas_call(lambda *refs: hidden_kernel(parts, islands, tails, *refs),...  5.83 us
    all_to_all x1, waiting for transfers between devices, body(): norms = lax.all_to_all(norms, AXES, split_axis=0, concat_axis=0, tiled=True)  4.88 us
    pallas_call x1, Pallas kernels, body(): pl.pallas_call(lambda *refs: average_kernel(islands, entries, *refs), in_...  4.88 us
    all_to_all x1, starting transfers between devices, body(): norms = lax.all_to_all(norms, AXES, split_axis=0, concat_axis=0, tiled=True)  4.72 us
  transfers between devices with their start and end apart: 21, of which 7 were waited for; matrix products, arithmetic and copies ran while one was open for 2% of the time, Pallas kernels for 11%

profile of v19, /device:TPU:0, one launch (start us, length us, event | category | flops | bytes accessed | tf_op | source)
XLA Modules:
  0.0 133.9 jit_solution(1245551270542154161)
XLA Ops:
  0.6 2.9 %pick_slots.1 = (bf16[192,1024]{1,0:T(8,128)(2,1)}, bf16[192,1024]{1,0:T(8,128)(2,1)}, bf16[192,1024]{1,0:T(8,128)(2,1)}, bf16[192,1024]{1,0:T(8,128)(2,1)}) custom-call(s32[1,1,4,96]{3,2,1,0:T(4,128)} %refs_0_.3, s32[1,1,4]{2,1,0:T(1,128)} %refs_1_.2, f32[1,1,4,96]{3,2,1,0:T(4,128)} %refs_2_.1, bf16[1,256,1024]{2,1,0:T(8,128)(2,1)} %refs_3_.1, ...), custom_call_target="tpu_custom_call" | custom-call | tf_op jit(solution)/shard_map/pick_slots/pallas_call | solution.py:296
  3.5 0.0 copy-start.2
  3.5 5.1 %collective-permute-start = (bf16[192,1024]{1,0:T(8,128)(2,1)}, bf16[192,1024]{1,0:T(8,128)(2,1)S(1)}, u32[]{:S(2)}, u32[]{:S(2)}) collective-permute-start(bf16[192,1024]{1,0:T(8,128)(2,1)} %get-tuple-element.32), channel_id=1, source_target_pairs={{0,6},{2,4},{4,2},{6,0},{1,7},{3,5},{5,3},{7,1},{8,14},{10,12},{12... | collective-permute-start | bytes 1179656 | tf_op jit(solution)/shard_map/ppermute | solution.py:34
  8.7 0.0 collective-permute-start.1
  8.7 0.6 collective-permute-start.2
  9.3 1.9 %cut_drift.1 = (bf16[1024,384]{1,0:T(8,128)(2,1)S(1)}, bf16[1536,384]{1,0:T(8,128)(2,1)S(1)}, bf16[1536,384]{1,0:T(8,128)(2,1)S(1)}) custom-call(bf16[1,1,2048,768]{3,2,1,0:T(8,128)(2,1)} %refs_0_.4), custom_call_target="tpu_custom_call" | custom-call | tf_op jit(solution)/shard_map/cut_drift/pallas_call | solution.py:312
  11.2 1.7 %collective-permute-start.5 = (bf16[1536,384]{1,0:T(8,128)(2,1)S(1)}, bf16[1536,384]{1,0:T(8,128)(2,1)S(1)}, u32[]{:S(2)}, u32[]{:S(2)}) collective-permute-start(bf16[1536,384]{1,0:T(8,128)(2,1)S(1)} %get-tuple-element.38), channel_id=1, source_target_pairs={{0,8},{8,0},{16,24},{24,16},{1,9},{9,1},{17,25},{25,17},{2,10},{10... | collective-permute-start | bytes 3538952 | tf_op jit(solution)/shard_map/ppermute | solution.py:34
  12.9 1.5 %collective-permute-start.6 = (bf16[1536,384]{1,0:T(8,128)(2,1)S(1)}, bf16[1536,384]{1,0:T(8,128)(2,1)S(1)}, u32[]{:S(2)}, u32[]{:S(2)}) collective-permute-start(bf16[1536,384]{1,0:T(8,128)(2,1)S(1)} %get-tuple-element.39), channel_id=1, source_target_pairs={{0,16},{8,24},{16,0},{24,8},{1,17},{9,25},{17,1},{25,9},{2,18},{10... | collective-permute-start | bytes 3538952 | tf_op jit(solution)/shard_map/ppermute | solution.py:34
  14.4 0.1 own_parts.1
  14.5 4.5 %collective-permute-done.refs_1_ = bf16[192,1024]{1,0:T(8,128)(2,1)S(1)} collective-permute-done((bf16[192,1024]{1,0:T(8,128)(2,1)}, bf16[192,1024]{1,0:T(8,128)(2,1)S(1)}, u32[]{:S(2)}, u32[]{:S(2)}) %collective-permute-start) | collective-permute-done | bytes 393248 | tf_op jit(solution)/shard_map/ppermute | solution.py:34
  19.0 23.5 %collective-permute-done.1.refs_2_ = bf16[192,1024]{1,0:T(8,128)(2,1)S(1)} collective-permute-done((bf16[192,1024]{1,0:T(8,128)(2,1)}, bf16[192,1024]{1,0:T(8,128)(2,1)S(1)}, u32[]{:S(2)}, u32[]{:S(2)}) %collective-permute-start.1) | collective-permute-done | bytes 393248 | tf_op jit(solution)/shard_map/ppermute | solution.py:34
  42.4 0.0 collective-permute-done.2.refs_3_
  42.4 0.1 gather_slots.1
  42.5 0.1 collective-permute-start.3
  42.6 0.5 collective-permute-start.4
  43.1 1.8 %collective-permute-done.3.refs_1_.refs_3_ = bf16[384,1024]{1,0:T(8,128)(2,1)S(1)} collective-permute-done((bf16[384,1024]{1,0:T(8,128)(2,1)S(1)}, bf16[384,1024]{1,0:T(8,128)(2,1)S(1)}, u32[]{:S(2)}, u32[]{:S(2)}) %collective-permute-start.3) | collective-permute-done | bytes 786464 | tf_op jit(solution)/shard_map/ppermute | solution.py:34
  44.9 0.0 collective-permute-done.5.refs_3_
  44.9 0.0 collective-permute-done.6.refs_4_
  44.9 1.5 %join_blocks.1 = (bf16[512,384]{1,0:T(8,128)(2,1)}, bf16[512,384]{1,0:T(8,128)(2,1)}, f32[1024,384]{1,0:T(8,128)S(1)}, bf16[512,384]{1,0:T(8,128)(2,1)S(1)}, bf16[512,384]{1,0:T(8,128)(2,1)S(1)}) custom-call(bf16[384,1024]{1,0:T(8,128)(2,1)S(1)} %get-tuple-element.35.refs_0_.refs_2_, bf16[384,1024]{1,0:T(8,128)(2,1)S(1)} %collective-permute-done.3.refs_1_.refs_3_, ...), custom_call_target="tpu_custom_call" | custom-call | tf_op jit(solution)/shard_map/join_blocks/pallas_call | solution.py:347
  46.4 2.4 %collective-permute-start.9 = (bf16[512,384]{1,0:T(8,128)(2,1)}, bf16[512,384]{1,0:T(8,128)(2,1)S(1)}, u32[]{:S(2)}, u32[]{:S(2)}) collective-permute-start(bf16[512,384]{1,0:T(8,128)(2,1)} %get-tuple-element.45), channel_id=1, source_target_pairs={{0,24},{8,16},{16,8},{24,0},{1,25},{9,17},{17,9},{25,1},{2,26},{10... | collective-permute-start | bytes 1179656 | tf_op jit(solution)/shard_map/ppermute | solution.py:34
  48.8 0.5 collective-permute-start.8
  49.3 0.0 collective-permute-start.10
  49.3 0.5 collective-permute-start.7
  49.8 0.0 collective-permute-done.4.refs_5_
  49.9 5.8 %hidden_grads.1 = (bf16[384,384]{1,0:T(8,128)(2,1)S(1)}, bf16[896,384]{1,0:T(8,128)(2,1)S(1)}, bf16[896,384]{1,0:T(8,128)(2,1)S(1)}, bf16[384,384]{1,0:T(8,128)(2,1)S(1)}, f32[32,8,128]{2,1,0:T(8,128)}) custom-call(bf16[1,1,2048,768]{3,2,1,0:T(8,128)(2,1)S(1)} %copy-done, bf16[1,1,768,2048]{3,2,1,0:T(8,128)(2,1)S(1)} %copy-done.1, ...), custom_call_target="tpu_custom_call" | custom-call | tf_op jit(solution)/shard_map/hidden_grads/pallas_call | solution.py:364
  55.7 0.7 copy-done.3
  56.4 0.8 copy-done.5
  57.3 0.8 copy-done.6
  58.1 0.7 copy-done.7
  58.8 4.7 %all-to-all-start = ((f32[32,8,128]{2,1,0:T(8,128)}), f32[32,8,128]{2,1,0:T(8,128)S(1)}, u32[]{:S(2)}, u32[]{:S(2)}) async-start(f32[32,8,128]{2,1,0:T(8,128)} %get-tuple-element.42), calls=%async_computation | async-start | bytes 262144 | tf_op jit(solution)/shard_map/all_to_all | solution.py:377
  63.6 1.8 %collective-permute-start.13 = (bf16[896,384]{1,0:T(8,128)(2,1)}, bf16[896,384]{1,0:T(8,128)(2,1)}, u32[]{:S(2)}, u32[]{:S(2)}) collective-permute-start(bf16[896,384]{1,0:T(8,128)(2,1)} %copy-done.6), channel_id=1, source_target_pairs={{0,8},{8,0},{16,24},{24,16},{1,9},{9,1},{17,25},{25,17},{2,10},{10... | collective-permute-start | bytes 2064392 | tf_op jit(solution)/shard_map/ppermute | solution.py:34
  65.4 0.0 collective-permute-done.9.refs_3_.refs_5_
  65.4 1.5 %collective-permute-start.14 = (bf16[896,384]{1,0:T(8,128)(2,1)}, bf16[896,384]{1,0:T(8,128)(2,1)}, u32[]{:S(2)}, u32[]{:S(2)}) collective-permute-start(bf16[896,384]{1,0:T(8,128)(2,1)} %copy-done.5), channel_id=1, source_target_pairs={{0,16},{8,24},{16,0},{24,8},{1,17},{9,25},{17,1},{25,9},{2,18},{10... | collective-permute-start | bytes 2064392 | tf_op jit(solution)/shard_map/ppermute | solution.py:34
  66.9 4.9 %all-to-all-done.refs_0_ = f32[32,8,128]{2,1,0:T(8,128)S(1)} async-done(((f32[32,8,128]{2,1,0:T(8,128)}), f32[32,8,128]{2,1,0:T(8,128)S(1)}, u32[]{:S(2)}, u32[]{:S(2)}) %all-to-all-start) | async-done | bytes 131104 | tf_op jit(solution)/shard_map/all_to_all | solution.py:377
  71.8 0.0 collective-permute-done.8.refs_2_.refs_4_
  71.8 0.0 collective-permute-done.10.refs_4_.refs_6_
  71.8 0.0 collective-permute-done.7.refs_1_.refs_3_
  71.8 0.1 hand_on.1
  71.9 0.5 collective-permute-start.11
  72.4 0.1 collective-permute-start.12
  72.5 1.0 collective-permute-start.15
  73.4 16.7 %collective-permute-done.15.refs_12_ = bf16[384,384]{1,0:T(8,128)(2,1)S(1)} collective-permute-done((bf16[384,384]{1,0:T(8,128)(2,1)}, bf16[384,384]{1,0:T(8,128)(2,1)S(1)}, u32[]{:S(2)}, u32[]{:S(2)}) %collective-permute-start.15) | collective-permute-done | bytes 294944 | tf_op jit(solution)/shard_map/ppermute | solution.py:34
  90.1 0.0 collective-permute-done.13.refs_10_
  90.1 0.0 collective-permute-done.14.refs_11_
  90.2 1.0 copy-done.4
  91.1 4.9 %average_block.1 = (f32[1024,384]{1,0:T(8,128)S(1)}, f32[32,8,128]{2,1,0:T(8,128)S(1)}) custom-call(f32[32,8,128]{2,1,0:T(8,128)S(1)} %all-to-all-done.refs_0_, f32[1024,384]{1,0:T(8,128)S(1)} %get-tuple-element.43.refs_1_, bf16[512,384]{1,0:T(8,128)(2,1)} %get-tuple-element.44.refs_2_, bf16[512,384]{1,0:T(8,128)(2,1)S(1)} %collective-permute-done.7.refs_1_.refs_3_, ...), custom_call_target="tpu_custom_call" | custom-call | tf_op jit(solution)/shard_map/average_block/pallas_call | solution.py:388
  96.0 0.1 convert_element_type.21
  96.1 1.4 %collective-permute-start.18 = (f16[1024,384]{1,0:T(8,128)(2,1)S(1)}, f16[1024,384]{1,0:T(8,128)(2,1)S(1)}, u32[]{:S(2)}, u32[]{:S(2)}) collective-permute-start(f16[1024,384]{1,0:T(8,128)(2,1)S(1)} %convert_element_type.21), channel_id=1, source_target_pairs={{0,16},{8,24},{16,0},{24,8},{1,17},{9,25},{17,1},{25,9},{2,18},{10... | collective-permute-start | bytes 2359304 | tf_op jit(solution)/shard_map/ppermute | solution.py:34
  97.5 1.1 collective-permute-start.16
  98.6 19.2 %all_to_all.10.notes = f32[32,8,128]{2,1,0:T(8,128)S(1)} all-to-all(f32[32,8,128]{2,1,0:T(8,128)S(1)} %get-tuple-element.52), channel_id=1, replica_groups=mesh['island'=4,'expert'=4,'tensor'=2] {'island','expert','tensor'}, dimensions={0} | all-to-all | bytes 262144 | tf_op jit(solution)/shard_map/all_to_all | solution.py:400
  117.9 0.5 slice.13
  119.0 0.0 collective-permute-done.18
  119.0 0.1 slice_add_fusion
  119.1 1.0 collective-permute-start.19
  120.1 0.1 slice_add_fusion.1
  120.2 1.2 collective-permute-start.17
  121.4 1.3 convert_element_type.27.refs_2_
  122.7 0.1 convert_element_type.26.refs_1_
  122.8 5.7 %update_pieces.2 = (f32[1,2048,768]{2,1,0:T(8,128)}, bf16[1,2048,768]{2,1,0:T(8,128)(2,1)}) custom-call(f32[32,8,128]{2,1,0:T(8,128)S(1)} %all_to_all.10.notes, f32[1,2048,768]{2,1,0:T(8,128)} %momentum.3, f32[1024,384]{1,0:T(8,128)S(1)} %get-tuple-element.53.refs_0_, f32[1024,384]{1,0:T(8,128)S(1)} %convert_element_type.26.refs_1_, ...), custom_call_target="tpu_custom_call" | custom-call | bytes 18874368 | tf_op jit(solution)/shard_map/update_pieces/pallas_call | solution.py:415
  128.6 1.4 %collective-permute-done.19 = f16[512,384]{1,0:T(8,128)(2,1)S(1)} collective-permute-done((f16[512,384]{1,0:T(8,128)(2,1)S(1)}, f16[512,384]{1,0:T(8,128)(2,1)S(1)}, u32[]{:S(2)}, u32[]{:S(2)}) %collective-permute-start.19) | collective-permute-done | bytes 393248 | tf_op jit(solution)/shard_map/ppermute | solution.py:34
  130.0 0.1 convert_element_type.25.refs_1_
  130.0 1.1 collective-permute-done.17
  131.1 0.1 convert_element_type.24.refs_0_
  131.2 2.6 %update_pieces.3 = (f32[1,2048,768]{2,1,0:T(8,128)}, bf16[1,2048,768]{2,1,0:T(8,128)(2,1)}) custom-call(f32[32,8,128]{2,1,0:T(8,128)S(1)} %all_to_all.10.notes, f32[1,2048,768]{2,1,0:T(8,128)} %momentum.3, f32[512,384]{1,0:T(8,128)S(1)} %convert_element_type.24.refs_0_, ...), custom_call_target="tpu_custom_call", output_to_operand_aliasing={{0}: (4, {}), {1}: (5, {})} | custom-call | bytes 4718592 | tf_op jit(solution)/shard_map/update_pieces/pallas_call | solution.py:415
  (13 shorter events, 0.0 us)
Async XLA Ops:
  3.5 10.9 %copy-start.2 = (bf16[192,1024]{1,0:T(8,128)(2,1)S(1)}, bf16[192,1024]{1,0:T(8,128)(2,1)}, u32[]{:S(2)}) copy-start(bf16[192,1024]{1,0:T(8,128)(2,1)} %get-tuple-element.29.slots) | copy-start | bytes 1179652
  3.5 15.4 %collective-permute-start = (bf16[192,1024]{1,0:T(8,128)(2,1)}, bf16[192,1024]{1,0:T(8,128)(2,1)S(1)}, u32[]{:S(2)}, u32[]{:S(2)}) collective-permute-start(bf16[192,1024]{1,0:T(8,128)(2,1)} %get-tuple-element.32), channel_id=1, source_target_pairs={{0,6},{2,4},{4,2},{6,0},{1,7},{3,5},{5,3},{7,1},{8,14},{10,12},{12... | collective-permute-start | bytes 1179656 | tf_op jit(solution)/shard_map/ppermute | solution.py:34
  8.7 33.8 %collective-permute-start.1 = (bf16[192,1024]{1,0:T(8,128)(2,1)}, bf16[192,1024]{1,0:T(8,128)(2,1)S(1)}, u32[]{:S(2)}, u32[]{:S(2)}) collective-permute-start(bf16[192,1024]{1,0:T(8,128)(2,1)} %get-tuple-element.33), channel_id=1, source_target_pairs={{0,4},{2,6},{4,0},{6,2},{1,5},{3,7},{5,1},{7,3},{8,12},{10,14},{12... | collective-permute-start | bytes 1179656 | tf_op jit(solution)/shard_map/ppermute | solution.py:34
  8.7 33.8 %collective-permute-start.2 = (bf16[192,1024]{1,0:T(8,128)(2,1)}, bf16[192,1024]{1,0:T(8,128)(2,1)S(1)}, u32[]{:S(2)}, u32[]{:S(2)}) collective-permute-start(bf16[192,1024]{1,0:T(8,128)(2,1)} %get-tuple-element.34), channel_id=1, source_target_pairs={{0,2},{2,0},{4,6},{6,4},{1,3},{3,1},{5,7},{7,5},{8,10},{10,8},{12,... | collective-permute-start | bytes 1179656 | tf_op jit(solution)/shard_map/ppermute | solution.py:34
  11.2 33.7 %collective-permute-start.5 = (bf16[1536,384]{1,0:T(8,128)(2,1)S(1)}, bf16[1536,384]{1,0:T(8,128)(2,1)S(1)}, u32[]{:S(2)}, u32[]{:S(2)}) collective-permute-start(bf16[1536,384]{1,0:T(8,128)(2,1)S(1)} %get-tuple-element.38), channel_id=1, source_target_pairs={{0,8},{8,0},{16,24},{24,16},{1,9},{9,1},{17,25},{25,17},{2,10},{10... | collective-permute-start | bytes 3538952 | tf_op jit(solution)/shard_map/ppermute | solution.py:34
  12.9 32.0 %collective-permute-start.6 = (bf16[1536,384]{1,0:T(8,128)(2,1)S(1)}, bf16[1536,384]{1,0:T(8,128)(2,1)S(1)}, u32[]{:S(2)}, u32[]{:S(2)}) collective-permute-start(bf16[1536,384]{1,0:T(8,128)(2,1)S(1)} %get-tuple-element.39), channel_id=1, source_target_pairs={{0,16},{8,24},{16,0},{24,8},{1,17},{9,25},{17,1},{25,9},{2,18},{10... | collective-permute-start | bytes 3538952 | tf_op jit(solution)/shard_map/ppermute | solution.py:34
  42.4 7.4 %copy-start = (bf16[1,1,2048,768]{3,2,1,0:T(8,128)(2,1)S(1)}, bf16[1,1,2048,768]{3,2,1,0:T(8,128)(2,1)}, u32[]{:S(2)}) copy-start(bf16[1,1,2048,768]{3,2,1,0:T(8,128)(2,1)} %refs_0_.5) | copy-start | bytes 9437188
  42.4 7.4 %copy-start.1 = (bf16[1,1,768,2048]{3,2,1,0:T(8,128)(2,1)S(1)}, bf16[1,1,768,2048]{3,2,1,0:T(8,128)(2,1)}, u32[]{:S(2)}) copy-start(bf16[1,1,768,2048]{3,2,1,0:T(8,128)(2,1)} %refs_1_.3) | copy-start | bytes 9437188
  42.5 2.4 %collective-permute-start.3 = (bf16[384,1024]{1,0:T(8,128)(2,1)S(1)}, bf16[384,1024]{1,0:T(8,128)(2,1)S(1)}, u32[]{:S(2)}, u32[]{:S(2)}) collective-permute-start(bf16[384,1024]{1,0:T(8,128)(2,1)S(1)} %get-tuple-element.35.refs_0_.refs_2_), channel_id=1, source_target_pairs={{0,1},{1,0},{2,3},{3,2},{4,5},{5,4},{6,7},{7,6},{8,9},{9,8},{10,11... | collective-permute-start | bytes 2359304 | tf_op jit(solution)/shard_map/ppermute | solution.py:34
  42.6 7.2 %collective-permute-start.4 = (bf16[384,1024]{1,0:T(8,128)(2,1)S(1)}, bf16[384,1024]{1,0:T(8,128)(2,1)S(1)}, u32[]{:S(2)}, u32[]{:S(2)}) collective-permute-start(bf16[384,1024]{1,0:T(8,128)(2,1)S(1)} %get-tuple-element.36.refs_4_), channel_id=1, source_target_pairs={{0,1},{1,0},{2,3},{3,2},{4,5},{5,4},{6,7},{7,6},{8,9},{9,8},{10,11... | collective-permute-start | bytes 2359304 | tf_op jit(solution)/shard_map/ppermute | solution.py:34
  46.4 19.1 %collective-permute-start.9 = (bf16[512,384]{1,0:T(8,128)(2,1)}, bf16[512,384]{1,0:T(8,128)(2,1)S(1)}, u32[]{:S(2)}, u32[]{:S(2)}) collective-permute-start(bf16[512,384]{1,0:T(8,128)(2,1)} %get-tuple-element.45), channel_id=1, source_target_pairs={{0,24},{8,16},{16,8},{24,0},{1,25},{9,17},{17,9},{25,1},{2,26},{10... | collective-permute-start | bytes 1179656 | tf_op jit(solution)/shard_map/ppermute | solution.py:34
  48.8 23.0 %collective-permute-start.8 = (bf16[512,384]{1,0:T(8,128)(2,1)}, bf16[512,384]{1,0:T(8,128)(2,1)S(1)}, u32[]{:S(2)}, u32[]{:S(2)}) collective-permute-start(bf16[512,384]{1,0:T(8,128)(2,1)} %get-tuple-element.45), channel_id=1, source_target_pairs={{0,16},{8,24},{16,0},{24,8},{1,17},{9,25},{17,1},{25,9},{2,18},{10... | collective-permute-start | bytes 1179656 | tf_op jit(solution)/shard_map/ppermute | solution.py:34
  49.3 22.5 %collective-permute-start.10 = (bf16[512,384]{1,0:T(8,128)(2,1)}, bf16[512,384]{1,0:T(8,128)(2,1)S(1)}, u32[]{:S(2)}, u32[]{:S(2)}) collective-permute-start(bf16[512,384]{1,0:T(8,128)(2,1)} %get-tuple-element.44.refs_2_), channel_id=1, source_target_pairs={{0,1},{1,0},{2,3},{3,2},{4,5},{5,4},{6,7},{7,6},{8,9},{9,8},{10,11... | collective-permute-start | bytes 1179656 | tf_op jit(solution)/shard_map/ppermute | solution.py:34
  49.3 22.5 %collective-permute-start.7 = (bf16[512,384]{1,0:T(8,128)(2,1)}, bf16[512,384]{1,0:T(8,128)(2,1)S(1)}, u32[]{:S(2)}, u32[]{:S(2)}) collective-permute-start(bf16[512,384]{1,0:T(8,128)(2,1)} %get-tuple-element.44.refs_2_), channel_id=1, source_target_pairs={{0,8},{8,0},{16,24},{24,16},{1,9},{9,1},{17,25},{25,17},{2,10},{10... | collective-permute-start | bytes 1179656 | tf_op jit(solution)/shard_map/ppermute | solution.py:34
  55.7 0.7 copy-start.3
  56.4 0.8 copy-start.5
  57.3 0.8 copy-start.6
  58.1 0.7 copy-start.7
  58.8 12.9 %all-to-all-start = ((f32[32,8,128]{2,1,0:T(8,128)}), f32[32,8,128]{2,1,0:T(8,128)S(1)}, u32[]{:S(2)}, u32[]{:S(2)}) async-start(f32[32,8,128]{2,1,0:T(8,128)} %get-tuple-element.42), calls=%async_computation | async-start | bytes 262144 | tf_op jit(solution)/shard_map/all_to_all | solution.py:377
  63.6 26.5 %collective-permute-start.13 = (bf16[896,384]{1,0:T(8,128)(2,1)}, bf16[896,384]{1,0:T(8,128)(2,1)}, u32[]{:S(2)}, u32[]{:S(2)}) collective-permute-start(bf16[896,384]{1,0:T(8,128)(2,1)} %copy-done.6), channel_id=1, source_target_pairs={{0,8},{8,0},{16,24},{24,16},{1,9},{9,1},{17,25},{25,17},{2,10},{10... | collective-permute-start | bytes 2064392 | tf_op jit(solution)/shard_map/ppermute | solution.py:34
  65.4 24.7 %collective-permute-start.14 = (bf16[896,384]{1,0:T(8,128)(2,1)}, bf16[896,384]{1,0:T(8,128)(2,1)}, u32[]{:S(2)}, u32[]{:S(2)}) collective-permute-start(bf16[896,384]{1,0:T(8,128)(2,1)} %copy-done.5), channel_id=1, source_target_pairs={{0,16},{8,24},{16,0},{24,8},{1,17},{9,25},{17,1},{25,9},{2,18},{10... | collective-permute-start | bytes 2064392 | tf_op jit(solution)/shard_map/ppermute | solution.py:34
  71.9 18.2 %collective-permute-start.11 = (bf16[768,384]{1,0:T(8,128)(2,1)S(1)}, bf16[768,384]{1,0:T(8,128)(2,1)S(1)}, u32[]{:S(2)}, u32[]{:S(2)}) collective-permute-start(bf16[768,384]{1,0:T(8,128)(2,1)S(1)} %get-tuple-element.46), channel_id=1, source_target_pairs={{0,1},{1,0},{2,3},{3,2},{4,5},{5,4},{6,7},{7,6},{8,9},{9,8},{10,11... | collective-permute-start | bytes 1769480 | tf_op jit(solution)/shard_map/ppermute | solution.py:34
  72.4 17.8 %collective-permute-start.12 = (bf16[768,384]{1,0:T(8,128)(2,1)S(1)}, bf16[768,384]{1,0:T(8,128)(2,1)S(1)}, u32[]{:S(2)}, u32[]{:S(2)}) collective-permute-start(bf16[768,384]{1,0:T(8,128)(2,1)S(1)} %get-tuple-element.47), channel_id=1, source_target_pairs={{0,1},{1,0},{2,3},{3,2},{4,5},{5,4},{6,7},{7,6},{8,9},{9,8},{10,11... | collective-permute-start | bytes 1769480 | tf_op jit(solution)/shard_map/ppermute | solution.py:34
  72.5 17.7 %collective-permute-start.15 = (bf16[384,384]{1,0:T(8,128)(2,1)}, bf16[384,384]{1,0:T(8,128)(2,1)S(1)}, u32[]{:S(2)}, u32[]{:S(2)}) collective-permute-start(bf16[384,384]{1,0:T(8,128)(2,1)} %copy-done.7), channel_id=1, source_target_pairs={{0,24},{8,16},{16,8},{24,0},{1,25},{9,17},{17,9},{25,1},{2,26},{10... | collective-permute-start | bytes 884744 | tf_op jit(solution)/shard_map/ppermute | solution.py:34
  90.1 1.0 copy-start.4
  96.1 22.9 %collective-permute-start.18 = (f16[1024,384]{1,0:T(8,128)(2,1)S(1)}, f16[1024,384]{1,0:T(8,128)(2,1)S(1)}, u32[]{:S(2)}, u32[]{:S(2)}) collective-permute-start(f16[1024,384]{1,0:T(8,128)(2,1)S(1)} %convert_element_type.21), channel_id=1, source_target_pairs={{0,16},{8,24},{16,0},{24,8},{1,17},{9,25},{17,1},{25,9},{2,18},{10... | collective-permute-start | bytes 2359304 | tf_op jit(solution)/shard_map/ppermute | solution.py:34
  97.5 22.6 %collective-permute-start.16 = (f16[1024,384]{1,0:T(8,128)(2,1)S(1)}, f16[1024,384]{1,0:T(8,128)(2,1)S(1)}, u32[]{:S(2)}, u32[]{:S(2)}) collective-permute-start(f16[1024,384]{1,0:T(8,128)(2,1)S(1)} %convert_element_type.21), channel_id=1, source_target_pairs={{0,8},{8,0},{16,24},{24,16},{1,9},{9,1},{17,25},{25,17},{2,10},{10... | collective-permute-start | bytes 2359304 | tf_op jit(solution)/shard_map/ppermute | solution.py:34
  119.1 10.8 %collective-permute-start.19 = (f16[512,384]{1,0:T(8,128)(2,1)S(1)}, f16[512,384]{1,0:T(8,128)(2,1)S(1)}, u32[]{:S(2)}, u32[]{:S(2)}) collective-permute-start(f16[512,384]{1,0:T(8,128)(2,1)S(1)} %slice_add_fusion), channel_id=1, source_target_pairs={{0,8},{8,0},{16,24},{24,16},{1,9},{9,1},{17,25},{25,17},{2,10},{10... | collective-permute-start | bytes 1179656 | tf_op jit(solution)/shard_map/ppermute | solution.py:34
  120.2 10.9 %collective-permute-start.17 = (f16[512,384]{1,0:T(8,128)(2,1)S(1)}, f16[512,384]{1,0:T(8,128)(2,1)S(1)}, u32[]{:S(2)}, u32[]{:S(2)}) collective-permute-start(f16[512,384]{1,0:T(8,128)(2,1)S(1)} %slice_add_fusion.1), channel_id=1, source_target_pairs={{0,16},{8,24},{16,0},{24,8},{1,17},{9,25},{17,1},{25,9},{2,18},{10... | collective-permute-start | bytes 1179656 | tf_op jit(solution)/shard_map/ppermute | solution.py:34

commit v20 on v19

--- a/solution.py
+++ b/solution.py
@@ -220,6 +220,10 @@
         if cut < size:
             first = n * size + cut - split
             bottom[first : first + size - cut, :] = share[cut:, :]
+
+
+def pass_kernel(norms, share, passed):
+    passed[...] = norms[...]
 
 
 def own_kernel(slots, block, slots_out, block_out):
@@ -374,6 +378,14 @@
     messages_in = [messages[0]] + [swap(messages[d], "island", d) for d in range(1, islands)]
 
     middle = (islands - 1) * (half // parts) // 2
+    norms = pl.pallas_call(
+        pass_kernel,
+        in_specs=[VMEM, ANY],
+        out_specs=VMEM,
+        out_shape=jax.ShapeDtypeStruct(norms.shape, F32),
+        compiler_params=params(2),
+        name="pass_norms",
+    )(norms, features_in[0])
     norms = lax.all_to_all(norms, AXES, split_axis=0, concat_axis=0, tiled=True)
     halves = pl.pallas_call(
         lambda *refs: hand_kernel(islands - 1, *refs),

time: 134 us -> 135 us (level)
    ppermute x20, waiting for transfers between devices: 48.9 us -> 52.2 us  [swap(): lax.ppermute(value, axis, [(at, partner(at, step, size)) for at in range(...]
    all_to_all x1, waiting for transfers between devices: 4.88 us -> 2.36 us  [body(): norms = lax.all_to_all(norms, AXES, split_axis=0, concat_axis=0, tiled=True)]
  transfers between devices with their start and end apart: 21 -> 21, of which waited for: 7 -> 10; matrix products, arithmetic and copies ran while one was open for 2% -> 2% of each run, Pallas kernels for 11% -> 11%
where the time goes in v20:
time: 135 us; the launch traced here: 134 us
  waiting for transfers between devices  54.6 us (40%)
  starting transfers between devices  27.1 us (20%)
  Pallas kernels  25.5 us (19%)
  blocking collectives  19.1 us (14%)
  local copies, waits for them, and re-layouts  4.64 us (3%)
  other arithmetic  1.82 us (1%)
  between operations  1.61 us (1%)
    ppermute x20, waiting for transfers between devices, swap(): lax.ppermute(value, axis, [(at, partner(at, step, size)) for at in range(...  52.2 us
    ppermute x20, starting transfers between devices, swap(): lax.ppermute(value, axis, [(at, partner(at, step, size)) for at in range(...  22.4 us
    all_to_all x1, blocking collectives, body(): notes = lax.all_to_all(notes, AXES, split_axis=0, concat_axis=0, tiled=True)  19.1 us
    pallas_call x2, Pallas kernels, body(): pl.pallas_call(functools.partial(update_kernel, entries, list(values), cu...  8.31 us
    pallas_call x1, Pallas kernels, body(): pl.pallas_call(lambda *refs: hidden_kernel(parts, islands, tails, *refs),...  5.17 us
    pallas_call x1, Pallas kernels, body(): pl.pallas_call(lambda *refs: average_kernel(islands, entries, *refs), in_...  4.88 us
    all_to_all x1, starting transfers between devices, body(): norms = lax.all_to_all(norms, AXES, split_axis=0, concat_axis=0, tiled=True)  4.72 us
    unnamed x16, local copies, waits for them, and re-layouts  4.12 us
  transfers between devices with their start and end apart: 21, of which 10 were waited for; matrix products, arithmetic and copies ran while one was open for 2% of the time, Pallas kernels for 11%

profile of v20, /device:TPU:0, one launch (start us, length us, event | category | flops | bytes accessed | tf_op | source)
XLA Modules:
  0.0 134.3 jit_solution(1016264414483711670)
XLA Ops:
  0.6 2.9 %pick_slots.1 = (bf16[192,1024]{1,0:T(8,128)(2,1)}, bf16[192,1024]{1,0:T(8,128)(2,1)}, bf16[192,1024]{1,0:T(8,128)(2,1)}, bf16[192,1024]{1,0:T(8,128)(2,1)}) custom-call(s32[1,1,4,96]{3,2,1,0:T(4,128)} %refs_0_.3, s32[1,1,4]{2,1,0:T(1,128)} %refs_1_.2, f32[1,1,4,96]{3,2,1,0:T(4,128)} %refs_2_.1, bf16[1,256,1024]{2,1,0:T(8,128)(2,1)} %refs_3_.1, ...), custom_call_target="tpu_custom_call" | custom-call | tf_op jit(solution)/shard_map/pick_slots/pallas_call | solution.py:300
  3.5 0.0 copy-start.2
  3.5 5.1 %collective-permute-start = (bf16[192,1024]{1,0:T(8,128)(2,1)}, bf16[192,1024]{1,0:T(8,128)(2,1)S(1)}, u32[]{:S(2)}, u32[]{:S(2)}) collective-permute-start(bf16[192,1024]{1,0:T(8,128)(2,1)} %get-tuple-element.32), channel_id=1, source_target_pairs={{0,6},{2,4},{4,2},{6,0},{1,7},{3,5},{5,3},{7,1},{8,14},{10,12},{12... | collective-permute-start | bytes 1179656 | tf_op jit(solution)/shard_map/ppermute | solution.py:34
  8.7 0.0 collective-permute-start.1
  8.7 0.6 collective-permute-start.2
  9.3 1.9 %cut_drift.1 = (bf16[1024,384]{1,0:T(8,128)(2,1)S(1)}, bf16[1536,384]{1,0:T(8,128)(2,1)S(1)}, bf16[1536,384]{1,0:T(8,128)(2,1)S(1)}) custom-call(bf16[1,1,2048,768]{3,2,1,0:T(8,128)(2,1)} %refs_0_.4), custom_call_target="tpu_custom_call" | custom-call | tf_op jit(solution)/shard_map/cut_drift/pallas_call | solution.py:316
  11.2 1.7 %collective-permute-start.5 = (bf16[1536,384]{1,0:T(8,128)(2,1)S(1)}, bf16[1536,384]{1,0:T(8,128)(2,1)S(1)}, u32[]{:S(2)}, u32[]{:S(2)}) collective-permute-start(bf16[1536,384]{1,0:T(8,128)(2,1)S(1)} %get-tuple-element.38), channel_id=1, source_target_pairs={{0,8},{8,0},{16,24},{24,16},{1,9},{9,1},{17,25},{25,17},{2,10},{10... | collective-permute-start | bytes 3538952 | tf_op jit(solution)/shard_map/ppermute | solution.py:34
  12.9 1.5 %collective-permute-start.6 = (bf16[1536,384]{1,0:T(8,128)(2,1)S(1)}, bf16[1536,384]{1,0:T(8,128)(2,1)S(1)}, u32[]{:S(2)}, u32[]{:S(2)}) collective-permute-start(bf16[1536,384]{1,0:T(8,128)(2,1)S(1)} %get-tuple-element.39), channel_id=1, source_target_pairs={{0,16},{8,24},{16,0},{24,8},{1,17},{9,25},{17,1},{25,9},{2,18},{10... | collective-permute-start | bytes 3538952 | tf_op jit(solution)/shard_map/ppermute | solution.py:34
  14.4 0.1 own_parts.1
  14.5 4.5 %collective-permute-done.refs_1_ = bf16[192,1024]{1,0:T(8,128)(2,1)S(1)} collective-permute-done((bf16[192,1024]{1,0:T(8,128)(2,1)}, bf16[192,1024]{1,0:T(8,128)(2,1)S(1)}, u32[]{:S(2)}, u32[]{:S(2)}) %collective-permute-start) | collective-permute-done | bytes 393248 | tf_op jit(solution)/shard_map/ppermute | solution.py:34
  19.0 23.5 %collective-permute-done.1.refs_2_ = bf16[192,1024]{1,0:T(8,128)(2,1)S(1)} collective-permute-done((bf16[192,1024]{1,0:T(8,128)(2,1)}, bf16[192,1024]{1,0:T(8,128)(2,1)S(1)}, u32[]{:S(2)}, u32[]{:S(2)}) %collective-permute-start.1) | collective-permute-done | bytes 393248 | tf_op jit(solution)/shard_map/ppermute | solution.py:34
  42.4 0.0 collective-permute-done.2.refs_3_
  42.4 0.1 gather_slots.1
  42.5 0.1 collective-permute-start.3
  42.6 0.5 collective-permute-start.4
  43.1 1.8 %collective-permute-done.3.refs_1_.refs_3_ = bf16[384,1024]{1,0:T(8,128)(2,1)S(1)} collective-permute-done((bf16[384,1024]{1,0:T(8,128)(2,1)S(1)}, bf16[384,1024]{1,0:T(8,128)(2,1)S(1)}, u32[]{:S(2)}, u32[]{:S(2)}) %collective-permute-start.3) | collective-permute-done | bytes 786464 | tf_op jit(solution)/shard_map/ppermute | solution.py:34
  44.9 0.0 collective-permute-done.5.refs_3_
  44.9 1.5 %join_blocks.1 = (bf16[512,384]{1,0:T(8,128)(2,1)}, bf16[512,384]{1,0:T(8,128)(2,1)}, f32[1024,384]{1,0:T(8,128)S(1)}, bf16[512,384]{1,0:T(8,128)(2,1)S(1)}, bf16[512,384]{1,0:T(8,128)(2,1)S(1)}) custom-call(bf16[384,1024]{1,0:T(8,128)(2,1)S(1)} %get-tuple-element.35.refs_0_.refs_2_, bf16[384,1024]{1,0:T(8,128)(2,1)S(1)} %collective-permute-done.3.refs_1_.refs_3_, ...), custom_call_target="tpu_custom_call" | custom-call | tf_op jit(solution)/shard_map/join_blocks/pallas_call | solution.py:351
  46.4 1.5 %collective-permute-start.7 = (bf16[512,384]{1,0:T(8,128)(2,1)}, bf16[512,384]{1,0:T(8,128)(2,1)S(1)}, u32[]{:S(2)}, u32[]{:S(2)}) collective-permute-start(bf16[512,384]{1,0:T(8,128)(2,1)} %get-tuple-element.43.refs_2_), channel_id=1, source_target_pairs={{0,8},{8,0},{16,24},{24,16},{1,9},{9,1},{17,25},{25,17},{2,10},{10... | collective-permute-start | bytes 1179656 | tf_op jit(solution)/shard_map/ppermute | solution.py:34
  47.8 1.5 %collective-permute-start.9 = (bf16[512,384]{1,0:T(8,128)(2,1)}, bf16[512,384]{1,0:T(8,128)(2,1)S(1)}, u32[]{:S(2)}, u32[]{:S(2)}) collective-permute-start(bf16[512,384]{1,0:T(8,128)(2,1)} %get-tuple-element.45), channel_id=1, source_target_pairs={{0,24},{8,16},{16,8},{24,0},{1,25},{9,17},{17,9},{25,1},{2,26},{10... | collective-permute-start | bytes 1179656 | tf_op jit(solution)/shard_map/ppermute | solution.py:34
  49.3 0.5 collective-permute-start.8
  49.8 0.0 collective-permute-start.10
  49.9 5.2 %hidden_grads.1 = (bf16[384,384]{1,0:T(8,128)(2,1)S(1)}, bf16[896,384]{1,0:T(8,128)(2,1)S(1)}, bf16[896,384]{1,0:T(8,128)(2,1)S(1)}, bf16[384,384]{1,0:T(8,128)(2,1)S(1)}, f32[32,8,128]{2,1,0:T(8,128)S(1)}) custom-call(bf16[1,1,2048,768]{3,2,1,0:T(8,128)(2,1)S(1)} %copy-done, bf16[1,1,768,2048]{3,2,1,0:T(8,128)(2,1)S(1)} %copy-done.1, ...), custom_call_target="tpu_custom_call" | custom-call | tf_op jit(solution)/shard_map/hidden_grads/pallas_call | solution.py:368
  55.1 0.7 copy-done.3
  55.8 0.8 copy-done.5
  56.6 0.8 copy-done.6
  57.5 0.7 copy-done.7
  58.2 0.3 collective-permute-done.7.share.refs_1_.refs_3_
  58.5 0.7 pass_norms.1
  59.2 4.7 %all-to-all-start = ((f32[32,8,128]{2,1,0:T(8,128)}), f32[32,8,128]{2,1,0:T(8,128)S(1)}, u32[]{:S(2)}, u32[]{:S(2)}) async-start(f32[32,8,128]{2,1,0:T(8,128)} %pass_norms.1), calls=%async_computation | async-start | bytes 262144 | tf_op jit(solution)/shard_map/all_to_all | solution.py:389
  63.9 1.8 %collective-permute-start.13 = (bf16[896,384]{1,0:T(8,128)(2,1)}, bf16[896,384]{1,0:T(8,128)(2,1)}, u32[]{:S(2)}, u32[]{:S(2)}) collective-permute-start(bf16[896,384]{1,0:T(8,128)(2,1)} %copy-done.6), channel_id=1, source_target_pairs={{0,8},{8,0},{16,24},{24,16},{1,9},{9,1},{17,25},{25,17},{2,10},{10... | collective-permute-start | bytes 2064392 | tf_op jit(solution)/shard_map/ppermute | solution.py:34
  65.8 1.5 %collective-permute-start.14 = (bf16[896,384]{1,0:T(8,128)(2,1)}, bf16[896,384]{1,0:T(8,128)(2,1)}, u32[]{:S(2)}, u32[]{:S(2)}) collective-permute-start(bf16[896,384]{1,0:T(8,128)(2,1)} %copy-done.5), channel_id=1, source_target_pairs={{0,16},{8,24},{16,0},{24,8},{1,17},{9,25},{17,1},{25,9},{2,18},{10... | collective-permute-start | bytes 2064392 | tf_op jit(solution)/shard_map/ppermute | solution.py:34
  67.2 0.0 collective-permute-done.9.refs_3_.refs_5_
  67.2 2.5 %collective-permute-done.8.refs_2_.refs_4_ = bf16[512,384]{1,0:T(8,128)(2,1)S(1)} collective-permute-done((bf16[512,384]{1,0:T(8,128)(2,1)}, bf16[512,384]{1,0:T(8,128)(2,1)S(1)}, u32[]{:S(2)}, u32[]{:S(2)}) %collective-permute-start.8) | collective-permute-done | bytes 393248 | tf_op jit(solution)/shard_map/ppermute | solution.py:34
  69.7 0.0 collective-permute-done.10.refs_4_.refs_6_
  69.7 2.4 %all-to-all-done.refs_0_ = f32[32,8,128]{2,1,0:T(8,128)S(1)} async-done(((f32[32,8,128]{2,1,0:T(8,128)}), f32[32,8,128]{2,1,0:T(8,128)S(1)}, u32[]{:S(2)}, u32[]{:S(2)}) %all-to-all-start) | async-done | bytes 131104 | tf_op jit(solution)/shard_map/all_to_all | solution.py:389
  72.1 0.1 hand_on.1
  72.2 0.5 collective-permute-start.11
  72.7 0.1 collective-permute-start.12
  72.8 1.0 collective-permute-start.15
  73.8 16.8 %collective-permute-done.15.refs_12_ = bf16[384,384]{1,0:T(8,128)(2,1)S(1)} collective-permute-done((bf16[384,384]{1,0:T(8,128)(2,1)}, bf16[384,384]{1,0:T(8,128)(2,1)S(1)}, u32[]{:S(2)}, u32[]{:S(2)}) %collective-permute-start.15) | collective-permute-done | bytes 294944 | tf_op jit(solution)/shard_map/ppermute | solution.py:34
  90.5 0.0 collective-permute-done.13.refs_10_
  90.6 0.6 collective-permute-done.14.refs_11_
  91.2 0.0 collective-permute-done.12.refs_8_
  91.2 1.0 copy-done.4
  92.1 4.9 %average_block.1 = (f32[1024,384]{1,0:T(8,128)S(1)}, f32[32,8,128]{2,1,0:T(8,128)S(1)}) custom-call(f32[32,8,128]{2,1,0:T(8,128)S(1)} %all-to-all-done.refs_0_, f32[1024,384]{1,0:T(8,128)S(1)} %get-tuple-element.44.refs_1_, bf16[512,384]{1,0:T(8,128)(2,1)} %get-tuple-element.43.refs_2_, bf16[512,384]{1,0:T(8,128)(2,1)S(1)} %collective-permute-done.7.share.refs_1_.refs_3_, ...), custom_call_target="tpu_custom_call" | custom-call | tf_op jit(solution)/shard_map/average_block/pallas_call | solution.py:400
  97.0 0.1 convert_element_type.21
  97.1 0.6 collective-permute-start.18
  97.7 1.4 %collective-permute-start.16 = (f16[1024,384]{1,0:T(8,128)(2,1)S(1)}, f16[1024,384]{1,0:T(8,128)(2,1)S(1)}, u32[]{:S(2)}, u32[]{:S(2)}) collective-permute-start(f16[1024,384]{1,0:T(8,128)(2,1)S(1)} %convert_element_type.21), channel_id=1, source_target_pairs={{0,8},{8,0},{16,24},{24,16},{1,9},{9,1},{17,25},{25,17},{2,10},{10... | collective-permute-start | bytes 2359304 | tf_op jit(solution)/shard_map/ppermute | solution.py:34
  99.2 19.1 %all_to_all.10.notes = f32[32,8,128]{2,1,0:T(8,128)S(1)} all-to-all(f32[32,8,128]{2,1,0:T(8,128)S(1)} %get-tuple-element.52), channel_id=1, replica_groups=mesh['island'=4,'expert'=4,'tensor'=2] {'island','expert','tensor'}, dimensions={0} | all-to-all | bytes 262144 | tf_op jit(solution)/shard_map/all_to_all | solution.py:412
  118.3 0.5 slice.13
  119.4 0.0 collective-permute-done.18
  119.4 0.1 slice_add_fusion
  119.5 1.0 collective-permute-start.19
  120.6 0.1 slice_add_fusion.1
  120.7 1.4 %collective-permute-start.17 = (f16[512,384]{1,0:T(8,128)(2,1)S(1)}, f16[512,384]{1,0:T(8,128)(2,1)S(1)}, u32[]{:S(2)}, u32[]{:S(2)}) collective-permute-start(f16[512,384]{1,0:T(8,128)(2,1)S(1)} %slice_add_fusion.1), channel_id=1, source_target_pairs={{0,16},{8,24},{16,0},{24,8},{1,17},{9,25},{17,1},{25,9},{2,18},{10... | collective-permute-start | bytes 1179656 | tf_op jit(solution)/shard_map/ppermute | solution.py:34
  122.1 1.3 convert_element_type.27.refs_2_
  123.4 0.1 convert_element_type.26.refs_1_
  123.5 5.7 %update_pieces.2 = (f32[1,2048,768]{2,1,0:T(8,128)}, bf16[1,2048,768]{2,1,0:T(8,128)(2,1)}) custom-call(f32[32,8,128]{2,1,0:T(8,128)S(1)} %all_to_all.10.notes, f32[1,2048,768]{2,1,0:T(8,128)} %momentum.3, f32[1024,384]{1,0:T(8,128)S(1)} %get-tuple-element.53.refs_0_, f32[1024,384]{1,0:T(8,128)S(1)} %convert_element_type.26.refs_1_, ...), custom_call_target="tpu_custom_call" | custom-call | bytes 18874368 | tf_op jit(solution)/shard_map/update_pieces/pallas_call | solution.py:427
  129.2 1.1 collective-permute-done.19
  130.4 0.1 convert_element_type.25.refs_1_
  130.4 1.1 collective-permute-done.17
  131.5 0.1 convert_element_type.24.refs_0_
  131.6 2.6 %update_pieces.3 = (f32[1,2048,768]{2,1,0:T(8,128)}, bf16[1,2048,768]{2,1,0:T(8,128)(2,1)}) custom-call(f32[32,8,128]{2,1,0:T(8,128)S(1)} %all_to_all.10.notes, f32[1,2048,768]{2,1,0:T(8,128)} %momentum.3, f32[512,384]{1,0:T(8,128)S(1)} %convert_element_type.24.refs_0_, ...), custom_call_target="tpu_custom_call", output_to_operand_aliasing={{0}: (4, {}), {1}: (5, {})} | custom-call | bytes 4718592 | tf_op jit(solution)/shard_map/update_pieces/pallas_call | solution.py:427
  (14 shorter events, 0.0 us)
Async XLA Ops:
  3.5 10.9 %copy-start.2 = (bf16[192,1024]{1,0:T(8,128)(2,1)S(1)}, bf16[192,1024]{1,0:T(8,128)(2,1)}, u32[]{:S(2)}) copy-start(bf16[192,1024]{1,0:T(8,128)(2,1)} %get-tuple-element.29.slots) | copy-start | bytes 1179652
  3.5 15.4 %collective-permute-start = (bf16[192,1024]{1,0:T(8,128)(2,1)}, bf16[192,1024]{1,0:T(8,128)(2,1)S(1)}, u32[]{:S(2)}, u32[]{:S(2)}) collective-permute-start(bf16[192,1024]{1,0:T(8,128)(2,1)} %get-tuple-element.32), channel_id=1, source_target_pairs={{0,6},{2,4},{4,2},{6,0},{1,7},{3,5},{5,3},{7,1},{8,14},{10,12},{12... | collective-permute-start | bytes 1179656 | tf_op jit(solution)/shard_map/ppermute | solution.py:34
  8.7 33.8 %collective-permute-start.1 = (bf16[192,1024]{1,0:T(8,128)(2,1)}, bf16[192,1024]{1,0:T(8,128)(2,1)S(1)}, u32[]{:S(2)}, u32[]{:S(2)}) collective-permute-start(bf16[192,1024]{1,0:T(8,128)(2,1)} %get-tuple-element.33), channel_id=1, source_target_pairs={{0,4},{2,6},{4,0},{6,2},{1,5},{3,7},{5,1},{7,3},{8,12},{10,14},{12... | collective-permute-start | bytes 1179656 | tf_op jit(solution)/shard_map/ppermute | solution.py:34
  8.7 33.8 %collective-permute-start.2 = (bf16[192,1024]{1,0:T(8,128)(2,1)}, bf16[192,1024]{1,0:T(8,128)(2,1)S(1)}, u32[]{:S(2)}, u32[]{:S(2)}) collective-permute-start(bf16[192,1024]{1,0:T(8,128)(2,1)} %get-tuple-element.34), channel_id=1, source_target_pairs={{0,2},{2,0},{4,6},{6,4},{1,3},{3,1},{5,7},{7,5},{8,10},{10,8},{12,... | collective-permute-start | bytes 1179656 | tf_op jit(solution)/shard_map/ppermute | solution.py:34
  11.2 33.7 %collective-permute-start.5 = (bf16[1536,384]{1,0:T(8,128)(2,1)S(1)}, bf16[1536,384]{1,0:T(8,128)(2,1)S(1)}, u32[]{:S(2)}, u32[]{:S(2)}) collective-permute-start(bf16[1536,384]{1,0:T(8,128)(2,1)S(1)} %get-tuple-element.38), channel_id=1, source_target_pairs={{0,8},{8,0},{16,24},{24,16},{1,9},{9,1},{17,25},{25,17},{2,10},{10... | collective-permute-start | bytes 3538952 | tf_op jit(solution)/shard_map/ppermute | solution.py:34
  12.9 32.0 %collective-permute-start.6 = (bf16[1536,384]{1,0:T(8,128)(2,1)S(1)}, bf16[1536,384]{1,0:T(8,128)(2,1)S(1)}, u32[]{:S(2)}, u32[]{:S(2)}) collective-permute-start(bf16[1536,384]{1,0:T(8,128)(2,1)S(1)} %get-tuple-element.39), channel_id=1, source_target_pairs={{0,16},{8,24},{16,0},{24,8},{1,17},{9,25},{17,1},{25,9},{2,18},{10... | collective-permute-start | bytes 3538952 | tf_op jit(solution)/shard_map/ppermute | solution.py:34
  42.4 7.4 %copy-start = (bf16[1,1,2048,768]{3,2,1,0:T(8,128)(2,1)S(1)}, bf16[1,1,2048,768]{3,2,1,0:T(8,128)(2,1)}, u32[]{:S(2)}) copy-start(bf16[1,1,2048,768]{3,2,1,0:T(8,128)(2,1)} %refs_0_.5) | copy-start | bytes 9437188
  42.4 7.4 %copy-start.1 = (bf16[1,1,768,2048]{3,2,1,0:T(8,128)(2,1)S(1)}, bf16[1,1,768,2048]{3,2,1,0:T(8,128)(2,1)}, u32[]{:S(2)}) copy-start(bf16[1,1,768,2048]{3,2,1,0:T(8,128)(2,1)} %refs_1_.3) | copy-start | bytes 9437188
  42.5 2.4 %collective-permute-start.3 = (bf16[384,1024]{1,0:T(8,128)(2,1)S(1)}, bf16[384,1024]{1,0:T(8,128)(2,1)S(1)}, u32[]{:S(2)}, u32[]{:S(2)}) collective-permute-start(bf16[384,1024]{1,0:T(8,128)(2,1)S(1)} %get-tuple-element.35.refs_0_.refs_2_), channel_id=1, source_target_pairs={{0,1},{1,0},{2,3},{3,2},{4,5},{5,4},{6,7},{7,6},{8,9},{9,8},{10,11... | collective-permute-start | bytes 2359304 | tf_op jit(solution)/shard_map/ppermute | solution.py:34
  42.6 7.2 %collective-permute-start.4 = (bf16[384,1024]{1,0:T(8,128)(2,1)S(1)}, bf16[384,1024]{1,0:T(8,128)(2,1)S(1)}, u32[]{:S(2)}, u32[]{:S(2)}) collective-permute-start(bf16[384,1024]{1,0:T(8,128)(2,1)S(1)} %get-tuple-element.36.refs_4_), channel_id=1, source_target_pairs={{0,1},{1,0},{2,3},{3,2},{4,5},{5,4},{6,7},{7,6},{8,9},{9,8},{10,11... | collective-permute-start | bytes 2359304 | tf_op jit(solution)/shard_map/ppermute | solution.py:34
  46.4 12.2 %collective-permute-start.7 = (bf16[512,384]{1,0:T(8,128)(2,1)}, bf16[512,384]{1,0:T(8,128)(2,1)S(1)}, u32[]{:S(2)}, u32[]{:S(2)}) collective-permute-start(bf16[512,384]{1,0:T(8,128)(2,1)} %get-tuple-element.43.refs_2_), channel_id=1, source_target_pairs={{0,8},{8,0},{16,24},{24,16},{1,9},{9,1},{17,25},{25,17},{2,10},{10... | collective-permute-start | bytes 1179656 | tf_op jit(solution)/shard_map/ppermute | solution.py:34
  47.8 19.4 %collective-permute-start.9 = (bf16[512,384]{1,0:T(8,128)(2,1)}, bf16[512,384]{1,0:T(8,128)(2,1)S(1)}, u32[]{:S(2)}, u32[]{:S(2)}) collective-permute-start(bf16[512,384]{1,0:T(8,128)(2,1)} %get-tuple-element.45), channel_id=1, source_target_pairs={{0,24},{8,16},{16,8},{24,0},{1,25},{9,17},{17,9},{25,1},{2,26},{10... | collective-permute-start | bytes 1179656 | tf_op jit(solution)/shard_map/ppermute | solution.py:34
  49.3 20.4 %collective-permute-start.8 = (bf16[512,384]{1,0:T(8,128)(2,1)}, bf16[512,384]{1,0:T(8,128)(2,1)S(1)}, u32[]{:S(2)}, u32[]{:S(2)}) collective-permute-start(bf16[512,384]{1,0:T(8,128)(2,1)} %get-tuple-element.45), channel_id=1, source_target_pairs={{0,16},{8,24},{16,0},{24,8},{1,17},{9,25},{17,1},{25,9},{2,18},{10... | collective-permute-start | bytes 1179656 | tf_op jit(solution)/shard_map/ppermute | solution.py:34
  49.8 19.9 %collective-permute-start.10 = (bf16[512,384]{1,0:T(8,128)(2,1)}, bf16[512,384]{1,0:T(8,128)(2,1)S(1)}, u32[]{:S(2)}, u32[]{:S(2)}) collective-permute-start(bf16[512,384]{1,0:T(8,128)(2,1)} %get-tuple-element.43.refs_2_), channel_id=1, source_target_pairs={{0,1},{1,0},{2,3},{3,2},{4,5},{5,4},{6,7},{7,6},{8,9},{9,8},{10,11... | collective-permute-start | bytes 1179656 | tf_op jit(solution)/shard_map/ppermute | solution.py:34
  55.0 0.7 copy-start.3
  55.8 0.8 copy-start.5
  56.6 0.8 copy-start.6
  57.5 0.7 copy-start.7
  59.2 12.9 %all-to-all-start = ((f32[32,8,128]{2,1,0:T(8,128)}), f32[32,8,128]{2,1,0:T(8,128)S(1)}, u32[]{:S(2)}, u32[]{:S(2)}) async-start(f32[32,8,128]{2,1,0:T(8,128)} %pass_norms.1), calls=%async_computation | async-start | bytes 262144 | tf_op jit(solution)/shard_map/all_to_all | solution.py:389
  63.9 26.6 %collective-permute-start.13 = (bf16[896,384]{1,0:T(8,128)(2,1)}, bf16[896,384]{1,0:T(8,128)(2,1)}, u32[]{:S(2)}, u32[]{:S(2)}) collective-permute-start(bf16[896,384]{1,0:T(8,128)(2,1)} %copy-done.6), channel_id=1, source_target_pairs={{0,8},{8,0},{16,24},{24,16},{1,9},{9,1},{17,25},{25,17},{2,10},{10... | collective-permute-start | bytes 2064392 | tf_op jit(solution)/shard_map/ppermute | solution.py:34
  65.8 25.4 %collective-permute-start.14 = (bf16[896,384]{1,0:T(8,128)(2,1)}, bf16[896,384]{1,0:T(8,128)(2,1)}, u32[]{:S(2)}, u32[]{:S(2)}) collective-permute-start(bf16[896,384]{1,0:T(8,128)(2,1)} %copy-done.5), channel_id=1, source_target_pairs={{0,16},{8,24},{16,0},{24,8},{1,17},{9,25},{17,1},{25,9},{2,18},{10... | collective-permute-start | bytes 2064392 | tf_op jit(solution)/shard_map/ppermute | solution.py:34
  72.2 18.9 %collective-permute-start.11 = (bf16[768,384]{1,0:T(8,128)(2,1)S(1)}, bf16[768,384]{1,0:T(8,128)(2,1)S(1)}, u32[]{:S(2)}, u32[]{:S(2)}) collective-permute-start(bf16[768,384]{1,0:T(8,128)(2,1)S(1)} %get-tuple-element.46), channel_id=1, source_target_pairs={{0,1},{1,0},{2,3},{3,2},{4,5},{5,4},{6,7},{7,6},{8,9},{9,8},{10,11... | collective-permute-start | bytes 1769480 | tf_op jit(solution)/shard_map/ppermute | solution.py:34
  72.7 18.5 %collective-permute-start.12 = (bf16[768,384]{1,0:T(8,128)(2,1)S(1)}, bf16[768,384]{1,0:T(8,128)(2,1)S(1)}, u32[]{:S(2)}, u32[]{:S(2)}) collective-permute-start(bf16[768,384]{1,0:T(8,128)(2,1)S(1)} %get-tuple-element.47), channel_id=1, source_target_pairs={{0,1},{1,0},{2,3},{3,2},{4,5},{5,4},{6,7},{7,6},{8,9},{9,8},{10,11... | collective-permute-start | bytes 1769480 | tf_op jit(solution)/shard_map/ppermute | solution.py:34
  72.8 17.8 %collective-permute-start.15 = (bf16[384,384]{1,0:T(8,128)(2,1)}, bf16[384,384]{1,0:T(8,128)(2,1)S(1)}, u32[]{:S(2)}, u32[]{:S(2)}) collective-permute-start(bf16[384,384]{1,0:T(8,128)(2,1)} %copy-done.7), channel_id=1, source_target_pairs={{0,24},{8,16},{16,8},{24,0},{1,25},{9,17},{17,9},{25,1},{2,26},{10... | collective-permute-start | bytes 884744 | tf_op jit(solution)/shard_map/ppermute | solution.py:34
  91.2 1.0 copy-start.4
  97.1 22.3 %collective-permute-start.18 = (f16[1024,384]{1,0:T(8,128)(2,1)S(1)}, f16[1024,384]{1,0:T(8,128)(2,1)S(1)}, u32[]{:S(2)}, u32[]{:S(2)}) collective-permute-start(f16[1024,384]{1,0:T(8,128)(2,1)S(1)} %convert_element_type.21), channel_id=1, source_target_pairs={{0,16},{8,24},{16,0},{24,8},{1,17},{9,25},{17,1},{25,9},{2,18},{10... | collective-permute-start | bytes 2359304 | tf_op jit(solution)/shard_map/ppermute | solution.py:34
  97.7 22.8 %collective-permute-start.16 = (f16[1024,384]{1,0:T(8,128)(2,1)S(1)}, f16[1024,384]{1,0:T(8,128)(2,1)S(1)}, u32[]{:S(2)}, u32[]{:S(2)}) collective-permute-start(f16[1024,384]{1,0:T(8,128)(2,1)S(1)} %convert_element_type.21), channel_id=1, source_target_pairs={{0,8},{8,0},{16,24},{24,16},{1,9},{9,1},{17,25},{25,17},{2,10},{10... | collective-permute-start | bytes 2359304 | tf_op jit(solution)/shard_map/ppermute | solution.py:34
  119.5 10.8 %collective-permute-start.19 = (f16[512,384]{1,0:T(8,128)(2,1)S(1)}, f16[512,384]{1,0:T(8,128)(2,1)S(1)}, u32[]{:S(2)}, u32[]{:S(2)}) collective-permute-start(f16[512,384]{1,0:T(8,128)(2,1)S(1)} %slice_add_fusion), channel_id=1, source_target_pairs={{0,8},{8,0},{16,24},{24,16},{1,9},{9,1},{17,25},{25,17},{2,10},{10... | collective-permute-start | bytes 1179656 | tf_op jit(solution)/shard_map/ppermute | solution.py:34
  120.7 10.9 %collective-permute-start.17 = (f16[512,384]{1,0:T(8,128)(2,1)S(1)}, f16[512,384]{1,0:T(8,128)(2,1)S(1)}, u32[]{:S(2)}, u32[]{:S(2)}) collective-permute-start(f16[512,384]{1,0:T(8,128)(2,1)S(1)} %slice_add_fusion.1), channel_id=1, source_target_pairs={{0,16},{8,24},{16,0},{24,8},{1,17},{9,25},{17,1},{25,9},{2,18},{10... | collective-permute-start | bytes 1179656 | tf_op jit(solution)/shard_map/ppermute | solution.py:34

commit v21 on v19

--- a/solution.py
+++ b/solution.py
@@ -409,7 +409,7 @@
         last[3, 0] = swap(values[1, 0][:handed] + nothing, "island", 2)
         last[3, handed] = swap(values[2, 0][handed:] + nothing, "island", 1)
     outs = []
-    for values, cost, cuts in ((values, 12, 2), (last, 3, 2)):
+    for values, cost, cuts in ((values, 12, 4), (last, 3, 4)):
         if not values:
             continue
         outs = pl.pallas_call(

time: 134 us -> 134 us (level)
  no operation moved by 1% of the time
where the time goes in v21:
time: 134 us
  waiting for transfers between devices  53.8 us (40%)
  starting transfers between devices  27.3 us (20%)
  Pallas kernels  25.5 us (19%)
  blocking collectives  19.2 us (14%)
  local copies, waits for them, and re-layouts  4.64 us (3%)
  other arithmetic  1.82 us (1%)
  between operations  1.61 us (1%)
    ppermute x20, waiting for transfers between devices, swap(): lax.ppermute(value, axis, [(at, partner(at, step, size)) for at in range(...  48.9 us
    ppermute x20, starting transfers between devices, swap(): lax.ppermute(value, axis, [(at, partner(at, step, size)) for at in range(...  22.6 us
    all_to_all x1, blocking collectives, body(): notes = lax.all_to_all(notes, AXES, split_axis=0, concat_axis=0, tiled=True)  19.2 us
    pallas_call x2, Pallas kernels, body(): pl.pallas_call(functools.partial(update_kernel, entries, list(values), cu...  8.3 us
    pallas_call x1, Pallas kernels, body(): pl.pallas_call(lambda *refs: hidden_kernel(parts, islands, tails, *refs),...  5.83 us
    all_to_all x1, waiting for transfers between devices, body(): norms = lax.all_to_all(norms, AXES, split_axis=0, concat_axis=0, tiled=True)  4.88 us
    pallas_call x1, Pallas kernels, body(): pl.pallas_call(lambda *refs: average_kernel(islands, entries, *refs), in_...  4.88 us
    all_to_all x1, starting transfers between devices, body(): norms = lax.all_to_all(norms, AXES, split_axis=0, concat_axis=0, tiled=True)  4.72 us
  transfers between devices with their start and end apart: 21, of which 7 were waited for; matrix products, arithmetic and copies ran while one was open for 2% of the time, Pallas kernels for 11%

profile of v21, /device:TPU:0, one launch (start us, length us, event | category | flops | bytes accessed | tf_op | source)
XLA Modules:
  0.0 133.9 jit_solution(16087954425714933893)
XLA Ops:
  0.6 2.9 %pick_slots.1 = (bf16[192,1024]{1,0:T(8,128)(2,1)}, bf16[192,1024]{1,0:T(8,128)(2,1)}, bf16[192,1024]{1,0:T(8,128)(2,1)}, bf16[192,1024]{1,0:T(8,128)(2,1)}) custom-call(s32[1,1,4,96]{3,2,1,0:T(4,128)} %refs_0_.3, s32[1,1,4]{2,1,0:T(1,128)} %refs_1_.2, f32[1,1,4,96]{3,2,1,0:T(4,128)} %refs_2_.1, bf16[1,256,1024]{2,1,0:T(8,128)(2,1)} %refs_3_.1, ...), custom_call_target="tpu_custom_call" | custom-call | tf_op jit(solution)/shard_map/pick_slots/pallas_call | solution.py:296
  3.5 0.0 copy-start.2
  3.5 5.1 %collective-permute-start = (bf16[192,1024]{1,0:T(8,128)(2,1)}, bf16[192,1024]{1,0:T(8,128)(2,1)S(1)}, u32[]{:S(2)}, u32[]{:S(2)}) collective-permute-start(bf16[192,1024]{1,0:T(8,128)(2,1)} %get-tuple-element.32), channel_id=1, source_target_pairs={{0,6},{2,4},{4,2},{6,0},{1,7},{3,5},{5,3},{7,1},{8,14},{10,12},{12... | collective-permute-start | bytes 1179656 | tf_op jit(solution)/shard_map/ppermute | solution.py:34
  8.7 0.0 collective-permute-start.1
  8.7 0.6 collective-permute-start.2
  9.3 1.9 %cut_drift.1 = (bf16[1024,384]{1,0:T(8,128)(2,1)S(1)}, bf16[1536,384]{1,0:T(8,128)(2,1)S(1)}, bf16[1536,384]{1,0:T(8,128)(2,1)S(1)}) custom-call(bf16[1,1,2048,768]{3,2,1,0:T(8,128)(2,1)} %refs_0_.4), custom_call_target="tpu_custom_call" | custom-call | tf_op jit(solution)/shard_map/cut_drift/pallas_call | solution.py:312
  11.2 1.7 %collective-permute-start.5 = (bf16[1536,384]{1,0:T(8,128)(2,1)S(1)}, bf16[1536,384]{1,0:T(8,128)(2,1)S(1)}, u32[]{:S(2)}, u32[]{:S(2)}) collective-permute-start(bf16[1536,384]{1,0:T(8,128)(2,1)S(1)} %get-tuple-element.38), channel_id=1, source_target_pairs={{0,8},{8,0},{16,24},{24,16},{1,9},{9,1},{17,25},{25,17},{2,10},{10... | collective-permute-start | bytes 3538952 | tf_op jit(solution)/shard_map/ppermute | solution.py:34
  12.9 1.5 %collective-permute-start.6 = (bf16[1536,384]{1,0:T(8,128)(2,1)S(1)}, bf16[1536,384]{1,0:T(8,128)(2,1)S(1)}, u32[]{:S(2)}, u32[]{:S(2)}) collective-permute-start(bf16[1536,384]{1,0:T(8,128)(2,1)S(1)} %get-tuple-element.39), channel_id=1, source_target_pairs={{0,16},{8,24},{16,0},{24,8},{1,17},{9,25},{17,1},{25,9},{2,18},{10... | collective-permute-start | bytes 3538952 | tf_op jit(solution)/shard_map/ppermute | solution.py:34
  14.4 0.1 own_parts.1
  14.5 4.5 %collective-permute-done.refs_1_ = bf16[192,1024]{1,0:T(8,128)(2,1)S(1)} collective-permute-done((bf16[192,1024]{1,0:T(8,128)(2,1)}, bf16[192,1024]{1,0:T(8,128)(2,1)S(1)}, u32[]{:S(2)}, u32[]{:S(2)}) %collective-permute-start) | collective-permute-done | bytes 393248 | tf_op jit(solution)/shard_map/ppermute | solution.py:34
  19.0 23.5 %collective-permute-done.1.refs_2_ = bf16[192,1024]{1,0:T(8,128)(2,1)S(1)} collective-permute-done((bf16[192,1024]{1,0:T(8,128)(2,1)}, bf16[192,1024]{1,0:T(8,128)(2,1)S(1)}, u32[]{:S(2)}, u32[]{:S(2)}) %collective-permute-start.1) | collective-permute-done | bytes 393248 | tf_op jit(solution)/shard_map/ppermute | solution.py:34
  42.4 0.0 collective-permute-done.2.refs_3_
  42.4 0.1 gather_slots.1
  42.5 0.1 collective-permute-start.3
  42.6 0.5 collective-permute-start.4
  43.1 1.8 %collective-permute-done.3.refs_1_.refs_3_ = bf16[384,1024]{1,0:T(8,128)(2,1)S(1)} collective-permute-done((bf16[384,1024]{1,0:T(8,128)(2,1)S(1)}, bf16[384,1024]{1,0:T(8,128)(2,1)S(1)}, u32[]{:S(2)}, u32[]{:S(2)}) %collective-permute-start.3) | collective-permute-done | bytes 786464 | tf_op jit(solution)/shard_map/ppermute | solution.py:34
  44.9 0.0 collective-permute-done.5.refs_3_
  44.9 0.0 collective-permute-done.6.refs_4_
  44.9 1.5 %join_blocks.1 = (bf16[512,384]{1,0:T(8,128)(2,1)}, bf16[512,384]{1,0:T(8,128)(2,1)}, f32[1024,384]{1,0:T(8,128)S(1)}, bf16[512,384]{1,0:T(8,128)(2,1)S(1)}, bf16[512,384]{1,0:T(8,128)(2,1)S(1)}) custom-call(bf16[384,1024]{1,0:T(8,128)(2,1)S(1)} %get-tuple-element.35.refs_0_.refs_2_, bf16[384,1024]{1,0:T(8,128)(2,1)S(1)} %collective-permute-done.3.refs_1_.refs_3_, ...), custom_call_target="tpu_custom_call" | custom-call | tf_op jit(solution)/shard_map/join_blocks/pallas_call | solution.py:347
  46.4 2.4 %collective-permute-start.9 = (bf16[512,384]{1,0:T(8,128)(2,1)}, bf16[512,384]{1,0:T(8,128)(2,1)S(1)}, u32[]{:S(2)}, u32[]{:S(2)}) collective-permute-start(bf16[512,384]{1,0:T(8,128)(2,1)} %get-tuple-element.45), channel_id=1, source_target_pairs={{0,24},{8,16},{16,8},{24,0},{1,25},{9,17},{17,9},{25,1},{2,26},{10... | collective-permute-start | bytes 1179656 | tf_op jit(solution)/shard_map/ppermute | solution.py:34
  48.8 0.5 collective-permute-start.8
  49.3 0.0 collective-permute-start.10
  49.3 0.5 collective-permute-start.7
  49.8 0.0 collective-permute-done.4.refs_5_
  49.9 5.8 %hidden_grads.1 = (bf16[384,384]{1,0:T(8,128)(2,1)S(1)}, bf16[896,384]{1,0:T(8,128)(2,1)S(1)}, bf16[896,384]{1,0:T(8,128)(2,1)S(1)}, bf16[384,384]{1,0:T(8,128)(2,1)S(1)}, f32[32,8,128]{2,1,0:T(8,128)}) custom-call(bf16[1,1,2048,768]{3,2,1,0:T(8,128)(2,1)S(1)} %copy-done, bf16[1,1,768,2048]{3,2,1,0:T(8,128)(2,1)S(1)} %copy-done.1, ...), custom_call_target="tpu_custom_call" | custom-call | tf_op jit(solution)/shard_map/hidden_grads/pallas_call | solution.py:364
  55.7 0.7 copy-done.3
  56.4 0.8 copy-done.5
  57.3 0.8 copy-done.6
  58.1 0.7 copy-done.7
  58.8 4.7 %all-to-all-start = ((f32[32,8,128]{2,1,0:T(8,128)}), f32[32,8,128]{2,1,0:T(8,128)S(1)}, u32[]{:S(2)}, u32[]{:S(2)}) async-start(f32[32,8,128]{2,1,0:T(8,128)} %get-tuple-element.42), calls=%async_computation | async-start | bytes 262144 | tf_op jit(solution)/shard_map/all_to_all | solution.py:377
  63.6 1.8 %collective-permute-start.13 = (bf16[896,384]{1,0:T(8,128)(2,1)}, bf16[896,384]{1,0:T(8,128)(2,1)}, u32[]{:S(2)}, u32[]{:S(2)}) collective-permute-start(bf16[896,384]{1,0:T(8,128)(2,1)} %copy-done.6), channel_id=1, source_target_pairs={{0,8},{8,0},{16,24},{24,16},{1,9},{9,1},{17,25},{25,17},{2,10},{10... | collective-permute-start | bytes 2064392 | tf_op jit(solution)/shard_map/ppermute | solution.py:34
  65.4 0.0 collective-permute-done.9.refs_3_.refs_5_
  65.4 1.5 %collective-permute-start.14 = (bf16[896,384]{1,0:T(8,128)(2,1)}, bf16[896,384]{1,0:T(8,128)(2,1)}, u32[]{:S(2)}, u32[]{:S(2)}) collective-permute-start(bf16[896,384]{1,0:T(8,128)(2,1)} %copy-done.5), channel_id=1, source_target_pairs={{0,16},{8,24},{16,0},{24,8},{1,17},{9,25},{17,1},{25,9},{2,18},{10... | collective-permute-start | bytes 2064392 | tf_op jit(solution)/shard_map/ppermute | solution.py:34
  66.9 4.9 %all-to-all-done.refs_0_ = f32[32,8,128]{2,1,0:T(8,128)S(1)} async-done(((f32[32,8,128]{2,1,0:T(8,128)}), f32[32,8,128]{2,1,0:T(8,128)S(1)}, u32[]{:S(2)}, u32[]{:S(2)}) %all-to-all-start) | async-done | bytes 131104 | tf_op jit(solution)/shard_map/all_to_all | solution.py:377
  71.8 0.0 collective-permute-done.8.refs_2_.refs_4_
  71.8 0.0 collective-permute-done.10.refs_4_.refs_6_
  71.8 0.0 collective-permute-done.7.refs_1_.refs_3_
  71.8 0.1 hand_on.1
  71.9 0.5 collective-permute-start.11
  72.4 0.1 collective-permute-start.12
  72.5 1.0 collective-permute-start.15
  73.4 16.7 %collective-permute-done.15.refs_12_ = bf16[384,384]{1,0:T(8,128)(2,1)S(1)} collective-permute-done((bf16[384,384]{1,0:T(8,128)(2,1)}, bf16[384,384]{1,0:T(8,128)(2,1)S(1)}, u32[]{:S(2)}, u32[]{:S(2)}) %collective-permute-start.15) | collective-permute-done | bytes 294944 | tf_op jit(solution)/shard_map/ppermute | solution.py:34
  90.1 0.0 collective-permute-done.13.refs_10_
  90.1 0.0 collective-permute-done.14.refs_11_
  90.2 1.0 copy-done.4
  91.1 4.9 %average_block.1 = (f32[1024,384]{1,0:T(8,128)S(1)}, f32[32,8,128]{2,1,0:T(8,128)S(1)}) custom-call(f32[32,8,128]{2,1,0:T(8,128)S(1)} %all-to-all-done.refs_0_, f32[1024,384]{1,0:T(8,128)S(1)} %get-tuple-element.43.refs_1_, bf16[512,384]{1,0:T(8,128)(2,1)} %get-tuple-element.44.refs_2_, bf16[512,384]{1,0:T(8,128)(2,1)S(1)} %collective-permute-done.7.refs_1_.refs_3_, ...), custom_call_target="tpu_custom_call" | custom-call | tf_op jit(solution)/shard_map/average_block/pallas_call | solution.py:388
  96.0 0.1 convert_element_type.21
  96.1 1.4 %collective-permute-start.18 = (f16[1024,384]{1,0:T(8,128)(2,1)S(1)}, f16[1024,384]{1,0:T(8,128)(2,1)S(1)}, u32[]{:S(2)}, u32[]{:S(2)}) collective-permute-start(f16[1024,384]{1,0:T(8,128)(2,1)S(1)} %convert_element_type.21), channel_id=1, source_target_pairs={{0,16},{8,24},{16,0},{24,8},{1,17},{9,25},{17,1},{25,9},{2,18},{10... | collective-permute-start | bytes 2359304 | tf_op jit(solution)/shard_map/ppermute | solution.py:34
  97.5 1.1 collective-permute-start.16
  98.6 19.2 %all_to_all.10.notes = f32[32,8,128]{2,1,0:T(8,128)S(1)} all-to-all(f32[32,8,128]{2,1,0:T(8,128)S(1)} %get-tuple-element.52), channel_id=1, replica_groups=mesh['island'=4,'expert'=4,'tensor'=2] {'island','expert','tensor'}, dimensions={0} | all-to-all | bytes 262144 | tf_op jit(solution)/shard_map/all_to_all | solution.py:400
  117.9 0.5 slice.13
  119.0 0.0 collective-permute-done.18
  119.0 0.1 slice_add_fusion
  119.1 1.0 collective-permute-start.19
  120.1 0.1 slice_add_fusion.1
  120.2 1.2 collective-permute-start.17
  121.4 1.3 convert_element_type.27.refs_2_
  122.7 0.1 convert_element_type.26.refs_1_
  122.8 5.7 %update_pieces.2 = (f32[1,2048,768]{2,1,0:T(8,128)}, bf16[1,2048,768]{2,1,0:T(8,128)(2,1)}) custom-call(f32[32,8,128]{2,1,0:T(8,128)S(1)} %all_to_all.10.notes, f32[1,2048,768]{2,1,0:T(8,128)} %momentum.3, f32[1024,384]{1,0:T(8,128)S(1)} %get-tuple-element.53.refs_0_, f32[1024,384]{1,0:T(8,128)S(1)} %convert_element_type.26.refs_1_, ...), custom_call_target="tpu_custom_call" | custom-call | bytes 18874368 | tf_op jit(solution)/shard_map/update_pieces/pallas_call | solution.py:415
  128.6 1.4 %collective-permute-done.19 = f16[512,384]{1,0:T(8,128)(2,1)S(1)} collective-permute-done((f16[512,384]{1,0:T(8,128)(2,1)S(1)}, f16[512,384]{1,0:T(8,128)(2,1)S(1)}, u32[]{:S(2)}, u32[]{:S(2)}) %collective-permute-start.19) | collective-permute-done | bytes 393248 | tf_op jit(solution)/shard_map/ppermute | solution.py:34
  130.0 0.1 convert_element_type.25.refs_1_
  130.0 1.1 collective-permute-done.17
  131.1 0.1 convert_element_type.24.refs_0_
  131.2 2.6 %update_pieces.3 = (f32[1,2048,768]{2,1,0:T(8,128)}, bf16[1,2048,768]{2,1,0:T(8,128)(2,1)}) custom-call(f32[32,8,128]{2,1,0:T(8,128)S(1)} %all_to_all.10.notes, f32[1,2048,768]{2,1,0:T(8,128)} %momentum.3, f32[512,384]{1,0:T(8,128)S(1)} %convert_element_type.24.refs_0_, ...), custom_call_target="tpu_custom_call", output_to_operand_aliasing={{0}: (4, {}), {1}: (5, {})} | custom-call | bytes 4718592 | tf_op jit(solution)/shard_map/update_pieces/pallas_call | solution.py:415
  (13 shorter events, 0.0 us)
Async XLA Ops:
  3.5 10.9 %copy-start.2 = (bf16[192,1024]{1,0:T(8,128)(2,1)S(1)}, bf16[192,1024]{1,0:T(8,128)(2,1)}, u32[]{:S(2)}) copy-start(bf16[192,1024]{1,0:T(8,128)(2,1)} %get-tuple-element.29.slots) | copy-start | bytes 1179652
  3.5 15.4 %collective-permute-start = (bf16[192,1024]{1,0:T(8,128)(2,1)}, bf16[192,1024]{1,0:T(8,128)(2,1)S(1)}, u32[]{:S(2)}, u32[]{:S(2)}) collective-permute-start(bf16[192,1024]{1,0:T(8,128)(2,1)} %get-tuple-element.32), channel_id=1, source_target_pairs={{0,6},{2,4},{4,2},{6,0},{1,7},{3,5},{5,3},{7,1},{8,14},{10,12},{12... | collective-permute-start | bytes 1179656 | tf_op jit(solution)/shard_map/ppermute | solution.py:34
  8.7 33.8 %collective-permute-start.1 = (bf16[192,1024]{1,0:T(8,128)(2,1)}, bf16[192,1024]{1,0:T(8,128)(2,1)S(1)}, u32[]{:S(2)}, u32[]{:S(2)}) collective-permute-start(bf16[192,1024]{1,0:T(8,128)(2,1)} %get-tuple-element.33), channel_id=1, source_target_pairs={{0,4},{2,6},{4,0},{6,2},{1,5},{3,7},{5,1},{7,3},{8,12},{10,14},{12... | collective-permute-start | bytes 1179656 | tf_op jit(solution)/shard_map/ppermute | solution.py:34
  8.7 33.8 %collective-permute-start.2 = (bf16[192,1024]{1,0:T(8,128)(2,1)}, bf16[192,1024]{1,0:T(8,128)(2,1)S(1)}, u32[]{:S(2)}, u32[]{:S(2)}) collective-permute-start(bf16[192,1024]{1,0:T(8,128)(2,1)} %get-tuple-element.34), channel_id=1, source_target_pairs={{0,2},{2,0},{4,6},{6,4},{1,3},{3,1},{5,7},{7,5},{8,10},{10,8},{12,... | collective-permute-start | bytes 1179656 | tf_op jit(solution)/shard_map/ppermute | solution.py:34
  11.2 33.7 %collective-permute-start.5 = (bf16[1536,384]{1,0:T(8,128)(2,1)S(1)}, bf16[1536,384]{1,0:T(8,128)(2,1)S(1)}, u32[]{:S(2)}, u32[]{:S(2)}) collective-permute-start(bf16[1536,384]{1,0:T(8,128)(2,1)S(1)} %get-tuple-element.38), channel_id=1, source_target_pairs={{0,8},{8,0},{16,24},{24,16},{1,9},{9,1},{17,25},{25,17},{2,10},{10... | collective-permute-start | bytes 3538952 | tf_op jit(solution)/shard_map/ppermute | solution.py:34
  12.9 32.0 %collective-permute-start.6 = (bf16[1536,384]{1,0:T(8,128)(2,1)S(1)}, bf16[1536,384]{1,0:T(8,128)(2,1)S(1)}, u32[]{:S(2)}, u32[]{:S(2)}) collective-permute-start(bf16[1536,384]{1,0:T(8,128)(2,1)S(1)} %get-tuple-element.39), channel_id=1, source_target_pairs={{0,16},{8,24},{16,0},{24,8},{1,17},{9,25},{17,1},{25,9},{2,18},{10... | collective-permute-start | bytes 3538952 | tf_op jit(solution)/shard_map/ppermute | solution.py:34
  42.4 7.4 %copy-start = (bf16[1,1,2048,768]{3,2,1,0:T(8,128)(2,1)S(1)}, bf16[1,1,2048,768]{3,2,1,0:T(8,128)(2,1)}, u32[]{:S(2)}) copy-start(bf16[1,1,2048,768]{3,2,1,0:T(8,128)(2,1)} %refs_0_.5) | copy-start | bytes 9437188
  42.4 7.4 %copy-start.1 = (bf16[1,1,768,2048]{3,2,1,0:T(8,128)(2,1)S(1)}, bf16[1,1,768,2048]{3,2,1,0:T(8,128)(2,1)}, u32[]{:S(2)}) copy-start(bf16[1,1,768,2048]{3,2,1,0:T(8,128)(2,1)} %refs_1_.3) | copy-start | bytes 9437188
  42.5 2.4 %collective-permute-start.3 = (bf16[384,1024]{1,0:T(8,128)(2,1)S(1)}, bf16[384,1024]{1,0:T(8,128)(2,1)S(1)}, u32[]{:S(2)}, u32[]{:S(2)}) collective-permute-start(bf16[384,1024]{1,0:T(8,128)(2,1)S(1)} %get-tuple-element.35.refs_0_.refs_2_), channel_id=1, source_target_pairs={{0,1},{1,0},{2,3},{3,2},{4,5},{5,4},{6,7},{7,6},{8,9},{9,8},{10,11... | collective-permute-start | bytes 2359304 | tf_op jit(solution)/shard_map/ppermute | solution.py:34
  42.6 7.2 %collective-permute-start.4 = (bf16[384,1024]{1,0:T(8,128)(2,1)S(1)}, bf16[384,1024]{1,0:T(8,128)(2,1)S(1)}, u32[]{:S(2)}, u32[]{:S(2)}) collective-permute-start(bf16[384,1024]{1,0:T(8,128)(2,1)S(1)} %get-tuple-element.36.refs_4_), channel_id=1, source_target_pairs={{0,1},{1,0},{2,3},{3,2},{4,5},{5,4},{6,7},{7,6},{8,9},{9,8},{10,11... | collective-permute-start | bytes 2359304 | tf_op jit(solution)/shard_map/ppermute | solution.py:34
  46.4 19.1 %collective-permute-start.9 = (bf16[512,384]{1,0:T(8,128)(2,1)}, bf16[512,384]{1,0:T(8,128)(2,1)S(1)}, u32[]{:S(2)}, u32[]{:S(2)}) collective-permute-start(bf16[512,384]{1,0:T(8,128)(2,1)} %get-tuple-element.45), channel_id=1, source_target_pairs={{0,24},{8,16},{16,8},{24,0},{1,25},{9,17},{17,9},{25,1},{2,26},{10... | collective-permute-start | bytes 1179656 | tf_op jit(solution)/shard_map/ppermute | solution.py:34
  48.8 23.0 %collective-permute-start.8 = (bf16[512,384]{1,0:T(8,128)(2,1)}, bf16[512,384]{1,0:T(8,128)(2,1)S(1)}, u32[]{:S(2)}, u32[]{:S(2)}) collective-permute-start(bf16[512,384]{1,0:T(8,128)(2,1)} %get-tuple-element.45), channel_id=1, source_target_pairs={{0,16},{8,24},{16,0},{24,8},{1,17},{9,25},{17,1},{25,9},{2,18},{10... | collective-permute-start | bytes 1179656 | tf_op jit(solution)/shard_map/ppermute | solution.py:34
  49.3 22.5 %collective-permute-start.10 = (bf16[512,384]{1,0:T(8,128)(2,1)}, bf16[512,384]{1,0:T(8,128)(2,1)S(1)}, u32[]{:S(2)}, u32[]{:S(2)}) collective-permute-start(bf16[512,384]{1,0:T(8,128)(2,1)} %get-tuple-element.44.refs_2_), channel_id=1, source_target_pairs={{0,1},{1,0},{2,3},{3,2},{4,5},{5,4},{6,7},{7,6},{8,9},{9,8},{10,11... | collective-permute-start | bytes 1179656 | tf_op jit(solution)/shard_map/ppermute | solution.py:34
  49.3 22.5 %collective-permute-start.7 = (bf16[512,384]{1,0:T(8,128)(2,1)}, bf16[512,384]{1,0:T(8,128)(2,1)S(1)}, u32[]{:S(2)}, u32[]{:S(2)}) collective-permute-start(bf16[512,384]{1,0:T(8,128)(2,1)} %get-tuple-element.44.refs_2_), channel_id=1, source_target_pairs={{0,8},{8,0},{16,24},{24,16},{1,9},{9,1},{17,25},{25,17},{2,10},{10... | collective-permute-start | bytes 1179656 | tf_op jit(solution)/shard_map/ppermute | solution.py:34
  55.7 0.7 copy-start.3
  56.4 0.8 copy-start.5
  57.3 0.8 copy-start.6
  58.1 0.7 copy-start.7
  58.8 12.9 %all-to-all-start = ((f32[32,8,128]{2,1,0:T(8,128)}), f32[32,8,128]{2,1,0:T(8,128)S(1)}, u32[]{:S(2)}, u32[]{:S(2)}) async-start(f32[32,8,128]{2,1,0:T(8,128)} %get-tuple-element.42), calls=%async_computation | async-start | bytes 262144 | tf_op jit(solution)/shard_map/all_to_all | solution.py:377
  63.6 26.5 %collective-permute-start.13 = (bf16[896,384]{1,0:T(8,128)(2,1)}, bf16[896,384]{1,0:T(8,128)(2,1)}, u32[]{:S(2)}, u32[]{:S(2)}) collective-permute-start(bf16[896,384]{1,0:T(8,128)(2,1)} %copy-done.6), channel_id=1, source_target_pairs={{0,8},{8,0},{16,24},{24,16},{1,9},{9,1},{17,25},{25,17},{2,10},{10... | collective-permute-start | bytes 2064392 | tf_op jit(solution)/shard_map/ppermute | solution.py:34
  65.4 24.7 %collective-permute-start.14 = (bf16[896,384]{1,0:T(8,128)(2,1)}, bf16[896,384]{1,0:T(8,128)(2,1)}, u32[]{:S(2)}, u32[]{:S(2)}) collective-permute-start(bf16[896,384]{1,0:T(8,128)(2,1)} %copy-done.5), channel_id=1, source_target_pairs={{0,16},{8,24},{16,0},{24,8},{1,17},{9,25},{17,1},{25,9},{2,18},{10... | collective-permute-start | bytes 2064392 | tf_op jit(solution)/shard_map/ppermute | solution.py:34
  71.9 18.2 %collective-permute-start.11 = (bf16[768,384]{1,0:T(8,128)(2,1)S(1)}, bf16[768,384]{1,0:T(8,128)(2,1)S(1)}, u32[]{:S(2)}, u32[]{:S(2)}) collective-permute-start(bf16[768,384]{1,0:T(8,128)(2,1)S(1)} %get-tuple-element.46), channel_id=1, source_target_pairs={{0,1},{1,0},{2,3},{3,2},{4,5},{5,4},{6,7},{7,6},{8,9},{9,8},{10,11... | collective-permute-start | bytes 1769480 | tf_op jit(solution)/shard_map/ppermute | solution.py:34
  72.4 17.8 %collective-permute-start.12 = (bf16[768,384]{1,0:T(8,128)(2,1)S(1)}, bf16[768,384]{1,0:T(8,128)(2,1)S(1)}, u32[]{:S(2)}, u32[]{:S(2)}) collective-permute-start(bf16[768,384]{1,0:T(8,128)(2,1)S(1)} %get-tuple-element.47), channel_id=1, source_target_pairs={{0,1},{1,0},{2,3},{3,2},{4,5},{5,4},{6,7},{7,6},{8,9},{9,8},{10,11... | collective-permute-start | bytes 1769480 | tf_op jit(solution)/shard_map/ppermute | solution.py:34
  72.5 17.7 %collective-permute-start.15 = (bf16[384,384]{1,0:T(8,128)(2,1)}, bf16[384,384]{1,0:T(8,128)(2,1)S(1)}, u32[]{:S(2)}, u32[]{:S(2)}) collective-permute-start(bf16[384,384]{1,0:T(8,128)(2,1)} %copy-done.7), channel_id=1, source_target_pairs={{0,24},{8,16},{16,8},{24,0},{1,25},{9,17},{17,9},{25,1},{2,26},{10... | collective-permute-start | bytes 884744 | tf_op jit(solution)/shard_map/ppermute | solution.py:34
  90.1 1.0 copy-start.4
  96.1 22.9 %collective-permute-start.18 = (f16[1024,384]{1,0:T(8,128)(2,1)S(1)}, f16[1024,384]{1,0:T(8,128)(2,1)S(1)}, u32[]{:S(2)}, u32[]{:S(2)}) collective-permute-start(f16[1024,384]{1,0:T(8,128)(2,1)S(1)} %convert_element_type.21), channel_id=1, source_target_pairs={{0,16},{8,24},{16,0},{24,8},{1,17},{9,25},{17,1},{25,9},{2,18},{10... | collective-permute-start | bytes 2359304 | tf_op jit(solution)/shard_map/ppermute | solution.py:34
  97.5 22.6 %collective-permute-start.16 = (f16[1024,384]{1,0:T(8,128)(2,1)S(1)}, f16[1024,384]{1,0:T(8,128)(2,1)S(1)}, u32[]{:S(2)}, u32[]{:S(2)}) collective-permute-start(f16[1024,384]{1,0:T(8,128)(2,1)S(1)} %convert_element_type.21), channel_id=1, source_target_pairs={{0,8},{8,0},{16,24},{24,16},{1,9},{9,1},{17,25},{25,17},{2,10},{10... | collective-permute-start | bytes 2359304 | tf_op jit(solution)/shard_map/ppermute | solution.py:34
  119.1 10.8 %collective-permute-start.19 = (f16[512,384]{1,0:T(8,128)(2,1)S(1)}, f16[512,384]{1,0:T(8,128)(2,1)S(1)}, u32[]{:S(2)}, u32[]{:S(2)}) collective-permute-start(f16[512,384]{1,0:T(8,128)(2,1)S(1)} %slice_add_fusion), channel_id=1, source_target_pairs={{0,8},{8,0},{16,24},{24,16},{1,9},{9,1},{17,25},{25,17},{2,10},{10... | collective-permute-start | bytes 1179656 | tf_op jit(solution)/shard_map/ppermute | solution.py:34
  120.2 10.9 %collective-permute-start.17 = (f16[512,384]{1,0:T(8,128)(2,1)S(1)}, f16[512,384]{1,0:T(8,128)(2,1)S(1)}, u32[]{:S(2)}, u32[]{:S(2)}) collective-permute-start(f16[512,384]{1,0:T(8,128)(2,1)S(1)} %slice_add_fusion.1), channel_id=1, source_target_pairs={{0,16},{8,24},{16,0},{24,8},{1,17},{9,25},{17,1},{25,9},{2,18},{10... | collective-permute-start | bytes 1179656 | tf_op jit(solution)/shard_map/ppermute | solution.py:34
